TPU v7x, 32 devices: a whole 2x2x4 slice. The times are simulated.
32 devices in a mesh: groups: 2 (over y), dp: 4 (over z), mp: 2 (over x), pair: 2 (over core).
Axes of the slice: x: 2, y: 2, z: 4, core: 2. Of those that a mesh axis runs over, the one named last changes fastest.
Arguments:
- hidden_input: bfloat16 [12288, 2048], P(('groups', 'dp', 'pair'), 'mp'), parts along dimension 0, may hold values from -6 to 6
- key_weight_frozen: bfloat16 [2048, 1024], P(None, 'mp'), may hold values from -0.125 to 0.125
- adapter_down: bfloat16 [16, 2048, 64], P(('groups', 'dp'), 'mp'), parts along dimension 0, may hold values from -0.125 to 0.125
- adapter_up: bfloat16 [16, 64, 1024], P(('groups', 'dp'), None, 'mp'), parts along dimension 0, may hold values from -0.75 to 0.75
- output_cotangent: bfloat16 [12288, 1024], P(('groups', 'dp', 'pair'), 'mp'), parts along dimension 0, may hold values from -0.119628906 to 0.119628906
- block_owner_index: int32 [192], P(('groups', 'dp', 'pair')), parts along dimension 0, may hold values from 0 to 3, as said below
- send_site_table: int32 [8, 2, 4], P(('groups', 'dp')), parts along dimension 0, may hold values from 0 to 1
Outputs:
- key_projection_output: bfloat16 [12288, 1024], P(('groups', 'dp', 'pair'), 'mp'), parts along dimension 0
- input_gradient: bfloat16 [12288, 2048], P(('groups', 'dp', 'pair'), 'mp'), parts along dimension 0
- down_gradient: float32 [16, 2048, 64], P(('groups', 'dp'), 'mp'), parts along dimension 0
- up_gradient: float32 [16, 64, 1024], P(('groups', 'dp'), None, 'mp'), parts along dimension 0
There are 2 independent parts, one for each index of `groups`. A program takes and returns all parts, laid end to end along the dimension named above; an argument that names none is the same for every part. Nothing has to cross between parts.
Inputs may be any that keep to these rules, and one draw needn't show every extreme that they name: `block_owner_index`: within the 12 blocks of one device equal values stand in consecutive runs, and exactly 4 different values occur.
All inputs are finite; a program needn't handle non-finite values.
Results may differ from a plain program's by a relative error of at most 0.014.
Values may be sent and summed in bfloat16 or wider, within the bound.
No kernel may reach another device: no remote copies, remote signals or barrier semaphores. Data moves between devices by JAX's collectives and lax.ppermute only.
A program may use at most 64 MiB of HBM per device.

v0:
```python
import jax
import jax.numpy as jnp
from jax import lax
from jax.sharding import PartitionSpec as P

adapter_scale = 2.0


def shards(
    hidden_input,
    key_weight_frozen,
    adapter_down,
    adapter_up,
    output_cotangent,
    block_owner_index,
    send_site_table,
):
    tok_rows, feat_loc = hidden_input.shape
    key_loc = key_weight_frozen.shape[1]
    owner_count = lax.axis_size("dp")
    block_count = block_owner_index.shape[0]
    block_rows = tok_rows // block_count
    local_site_count = adapter_down.shape[0]
    top_precision = lax.Precision.HIGHEST
    my_pair = lax.axis_index("pair")
    wanted = lax.dynamic_index_in_dim(send_site_table[0], my_pair, 0, keepdims=False)
    site_ids = jnp.arange(local_site_count, dtype=jnp.int32)
    site_selector = (wanted[:, None] == site_ids[None, :]).astype(jnp.bfloat16)
    outgoing_down = jnp.einsum(
        "qu,uyh->qyh", site_selector, adapter_down, preferred_element_type=jnp.float32
    ).astype(jnp.bfloat16)
    outgoing_up = jnp.einsum(
        "ly,yfz->lfz", site_selector, adapter_up, preferred_element_type=jnp.float32
    ).astype(jnp.bfloat16)
    recv_a, recv_b = (
        lax.all_to_all(outgoing_down, "dp", split_axis=0, concat_axis=0, tiled=True),
        lax.all_to_all(outgoing_up, "dp", split_axis=0, concat_axis=0, tiled=True),
    )
    owner_ids = jnp.arange(owner_count, dtype=jnp.int32)
    owner_hot = (block_owner_index[:, None] == owner_ids[None, :]).astype(jnp.bfloat16)
    blk_a = jnp.einsum("bo,odr->bdr", owner_hot, recv_a, preferred_element_type=jnp.float32).astype(
        jnp.bfloat16
    )
    block_up_map = jnp.einsum(
        "bo,orc->brc", owner_hot, recv_b, preferred_element_type=jnp.float32
    ).astype(jnp.bfloat16)
    x_blk = hidden_input.reshape(block_count, block_rows, feat_loc)
    grad_blk = output_cotangent.reshape(block_count, block_rows, key_loc)
    u_part = jnp.einsum("btd,bdr->btr", x_blk, blk_a, preferred_element_type=jnp.float32)
    h_part = jnp.einsum("btc,brc->btr", grad_blk, block_up_map, preferred_element_type=jnp.float32)
    u_sum, h_sum = (
        lax.psum(u_part.astype(jnp.bfloat16), "mp").astype(jnp.float32),
        lax.psum(h_part.astype(jnp.bfloat16), "mp").astype(jnp.float32),
    )
    update_reduced = u_sum.astype(jnp.bfloat16)
    h_low = h_sum.astype(jnp.bfloat16)
    frozen_output = jnp.dot(
        lax.all_gather(hidden_input, "mp", axis=1, tiled=True),
        key_weight_frozen,
        preferred_element_type=jnp.float32,
    )
    adapter_output = jnp.einsum(
        "njh,nhq->njq", update_reduced, block_up_map, preferred_element_type=jnp.float32
    ).reshape(tok_rows, key_loc)
    final_output = (frozen_output + adapter_scale * adapter_output).astype(jnp.bfloat16)
    back_part = lax.dot_general(
        output_cotangent,
        key_weight_frozen,
        (((1,), (1,)), ((), ())),
        preferred_element_type=jnp.float32,
    )
    backward_sum = lax.psum_scatter(
        back_part.astype(jnp.bfloat16), "mp", scatter_dimension=1, tiled=True
    ).astype(jnp.float32)
    adapter_backward = jnp.einsum(
        "osp,omp->osm", h_low, blk_a, preferred_element_type=jnp.float32
    ).reshape(tok_rows, feat_loc)
    input_gradient = (backward_sum + adapter_scale * adapter_backward).astype(jnp.bfloat16)
    part_a = jnp.einsum("btd,btr->bdr", x_blk, h_low, preferred_element_type=jnp.float32)
    part_b = jnp.einsum(
        "btr,btc->brc", update_reduced, grad_blk, preferred_element_type=jnp.float32
    )
    owner_float = owner_hot.astype(jnp.float32)
    slot_a = jnp.einsum("bo,bdr->odr", owner_float, part_a, precision=top_precision)
    slot_b = jnp.einsum("bo,brc->orc", owner_float, part_b, precision=top_precision)
    back_a, back_b = (
        lax.all_to_all(
            slot_a.astype(jnp.bfloat16), "dp", split_axis=0, concat_axis=0, tiled=True
        ).astype(slot_a.dtype),
        lax.all_to_all(
            slot_b.astype(jnp.bfloat16), "dp", split_axis=0, concat_axis=0, tiled=True
        ).astype(slot_b.dtype),
    )
    picker_float = site_selector.astype(jnp.float32)
    local_a = jnp.einsum("os,odr->sdr", picker_float, back_a, precision=top_precision)
    local_b = jnp.einsum("os,orc->src", picker_float, back_b, precision=top_precision)
    down_gradient, up_gradient = (
        lax.psum(local_a.astype(jnp.bfloat16), "pair").astype(jnp.float32),
        lax.psum(local_b.astype(jnp.bfloat16), "pair").astype(jnp.float32),
    )
    return (
        final_output,
        input_gradient,
        adapter_scale * down_gradient,
        adapter_scale * up_gradient,
    )


def solution(mesh):
    in_specs = (
        P(("groups", "dp", "pair"), "mp"),
        P(None, "mp"),
        P(("groups", "dp"), "mp", None),
        P(("groups", "dp"), None, "mp"),
        P(("groups", "dp", "pair"), "mp"),
        P(("groups", "dp", "pair")),
        P(("groups", "dp"), None, None),
    )
    out_specs = (
        P(("groups", "dp", "pair"), "mp"),
        P(("groups", "dp", "pair"), "mp"),
        P(("groups", "dp"), "mp", None),
        P(("groups", "dp"), None, "mp"),
    )
    return jax.shard_map(shards, mesh=mesh, in_specs=in_specs, out_specs=out_specs, check_vma=False)
```

profile of v0, /device:TPU:0, one launch (start us, length us, event | category | flops | bytes accessed | tf_op | source)
XLA Modules:
  0.0 230.8 jit_solution(16409355309920937932)
XLA Ops:
  8.0 1.3 convolution_convert_fusion.3
  10.0 6.3 %all-to-all-start.1 = ((bf16[4,64,512]{2,1,0:T(8,128)(2,1)}), bf16[4,64,512]{2,1,0:T(8,128)(2,1)S(1)}, u32[]{:S(2)}, u32[]{:S(2)}) async-start(bf16[4,64,512]{2,1,0:T(8,128)(2,1)} %copy.36), calls=%async_computation.1 | async-start | bytes 524288 | tf_op jit(solution)/shard_map/all_to_all | solution.py:37
  16.4 1.5 convolution_convert_fusion.1
  18.8 6.5 %all-to-all-done.1 = bf16[4,64,512]{2,1,0:T(8,128)(2,1)S(1)} async-done(((bf16[4,64,512]{2,1,0:T(8,128)(2,1)}), bf16[4,64,512]{2,1,0:T(8,128)(2,1)S(1)}, u32[]{:S(2)}, u32[]{:S(2)}) %all-to-all-start.1) | async-done | bytes 262176 | tf_op jit(solution)/shard_map/all_to_all | solution.py:37
  25.3 4.1 %all-to-all-start = ((bf16[4,1024,64]{1,2,0:T(8,128)(2,1)}), bf16[4,1024,64]{1,2,0:T(8,128)(2,1)}, u32[]{:S(2)}, u32[]{:S(2)}) async-start(bf16[4,1024,64]{1,2,0:T(8,128)(2,1)} %copy.32), calls=%async_computation | async-start | bytes 1048576 | tf_op jit(solution)/shard_map/all_to_all | solution.py:36
  30.0 2.4 %fusion.13 = bf16[12,64,64]{1,2,0:T(8,128)(2,1)} fusion(bf16[12,64,512]{2,1,0:T(8,128)(2,1)} %bitcast.47, bf16[12,64,512]{2,0,1:T(8,128)(2,1)S(1)} %fusion.17), kind=kOutput, calls=%fused_computation.23 | convolution fusion | flops 50380800 | bytes 1671168 | tf_op jit(solution)/shard_map/btc,brc->btr/dot_general | solution.py:50
  32.4 10.2 %all-to-all-done = bf16[4,1024,64]{1,2,0:T(8,128)(2,1)} async-done(((bf16[4,1024,64]{1,2,0:T(8,128)(2,1)}), bf16[4,1024,64]{1,2,0:T(8,128)(2,1)}, u32[]{:S(2)}, u32[]{:S(2)}) %all-to-all-start) | async-done | bytes 524320 | tf_op jit(solution)/shard_map/all_to_all | solution.py:36
  42.6 2.0 fusion.14
  44.6 1.4 copy-done.1
  46.0 1.8 fusion.12
  47.8 25.2 %all-reduce.7.cloned.1.call-done = (bf16[12,64,64]{1,2,0:T(8,128)(2,1)}, bf16[12,64,64]{1,2,0:T(8,128)(2,1)}) async-done(((bf16[12,64,64]{1,2,0:T(8,128)(2,1)}, bf16[12,64,64]{1,2,0:T(8,128)(2,1)}), (bf16[12,64,64]{1,2,0:T(8,128)(2,1)}, bf16[12,64,64]{1,2,0:T(8,128)(2,1)})) %all-reduce.7.cloned.1.call-update) | async-done | bytes 196624 | tf_op jit(solution)/shard_map/psum | solution.py:52
  73.0 1.6 fusion.35
  74.6 1.7 fusion.9
  77.0 4.6 %all-to-all-start.3 = ((bf16[4,64,512]{2,1,0:T(8,128)(2,1)}), bf16[4,64,512]{2,1,0:T(8,128)(2,1)}, u32[]{:S(2)}, u32[]{:S(2)}) async-start(bf16[4,64,512]{2,1,0:T(8,128)(2,1)} %copy.45), calls=%async_computation.4 | async-start | bytes 524288 | tf_op jit(solution)/shard_map/all_to_all | solution.py:90
  81.6 2.0 convolution_bitcast_fusion
  83.6 3.3 %fusion.6 = bf16[4,1024,64]{1,0,2:T(4,128)(2,1)S(1)} fusion(f32[12,1024,64]{1,2,0:T(8,128)S(1)} %convolution_bitcast_fusion, s32[12]{0:T(128)S(1)} %copy-done.6), kind=kOutput, calls=%fused_computation.14 | convolution fusion | flops 38010928 | bytes 3670064 | tf_op jit(solution)/shard_map/bo,bdr->odr/dot_general | solution.py:84
  87.8 2.8 %all-to-all-done.3 = bf16[4,64,512]{2,1,0:T(8,128)(2,1)} async-done(((bf16[4,64,512]{2,1,0:T(8,128)(2,1)}), bf16[4,64,512]{2,1,0:T(8,128)(2,1)}, u32[]{:S(2)}, u32[]{:S(2)}) %all-to-all-start.3) | async-done | bytes 262176 | tf_op jit(solution)/shard_map/all_to_all | solution.py:90
  90.6 4.1 %all-to-all-start.2 = ((bf16[4,1024,64]{1,2,0:T(8,128)(2,1)}), bf16[4,1024,64]{1,2,0:T(8,128)(2,1)}, u32[]{:S(2)}, u32[]{:S(2)}) async-start(bf16[4,1024,64]{1,2,0:T(8,128)(2,1)} %copy.42), calls=%async_computation.3 | async-start | bytes 1048576 | tf_op jit(solution)/shard_map/all_to_all | solution.py:87
  94.8 1.9 convolution_convert_fusion.6
  96.7 11.3 %all-to-all-done.2 = bf16[4,1024,64]{1,2,0:T(8,128)(2,1)} async-done(((bf16[4,1024,64]{1,2,0:T(8,128)(2,1)}), bf16[4,1024,64]{1,2,0:T(8,128)(2,1)}, u32[]{:S(2)}, u32[]{:S(2)}) %all-to-all-start.2) | async-done | bytes 524320 | tf_op jit(solution)/shard_map/all_to_all | solution.py:87
  108.0 2.2 convolution_convert_fusion.2
  111.2 4.6 %convolution_convert_fusion = bf16[768,2048]{1,0:T(8,128)(2,1)} fusion(bf16[768,512]{1,0:T(8,128)(2,1)} %param.11, bf16[2048,512]{1,0:T(8,128)(2,1)S(1)} %copy-done), kind=kOutput, calls=%fused_computation.2 | convolution fusion | flops 1612185600 | bytes 6029312 | tf_op jit(solution)/shard_map/dot_general | solution.py:66
  116.8 2.3 convolution_multiply_fusion.1
  119.1 3.9 %convolution_multiply_fusion = f32[12,64,1024]{2,1,0:T(8,128)} fusion(bf16[12,64,64]{1,2,0:T(8,128)(2,1)S(1)} %copy-done.4, bf16[12,1024,64]{1,0,2:T(8,128)(2,1)S(1)} %copy-done.2), kind=kOutput, calls=%fused_computation.9 | convolution fusion | flops 101449728 | bytes 4816896 | tf_op jit(solution)/shard_map/osp,omp->osm/dot_general | solution.py:75
  123.0 4.0 %all-reduce.5.cloned.1.call-done = (bf16[2,1024,64]{1,0,2:T(2,128)(2,1)}, bf16[2,64,512]{2,0,1:T(2,128)(2,1)}) async-done(((bf16[2,1024,64]{1,0,2:T(2,128)(2,1)}, bf16[2,64,512]{2,0,1:T(2,128)(2,1)}), (bf16[2,1024,64]{1,0,2:T(2,128)(2,1)}, bf16[2,64,512]{2,0,1:T(2,128)(2,1)})) %all-reduce.5.cloned.1.call-update) | async-done | bytes 393232 | tf_op jit(solution)/shard_map/psum | solution.py:98
  127.1 1.2 convert_multiply_fusion
  128.2 1.0 copy.47
  129.2 1.0 convert_multiply_fusion.1
  131.0 43.8 %all-gather.2.cloned.1.call-done = bf16[768,2048]{1,0:T(8,128)(2,1)} async-done(((bf16[768,1024]{1,0:T(8,128)(2,1)}), bf16[768,2048]{1,0:T(8,128)(2,1)}) %all-gather.2.cloned.1.call-update) | async-done | bytes 3145744 | tf_op jit(solution)/shard_map/all_gather | solution.py:58
  174.7 5.0 %fusion.5 = bf16[768,512]{1,0:T(8,128)(2,1)} fusion(f32[12,64,512]{2,1,0:T(8,128)} %convolution_multiply_fusion.1, bf16[768,2048]{1,0:T(8,128)(2,1)} %all-gather.2.cloned.1.call-done, bf16[2048,512]{1,0:T(8,128)(2,1)S(1)} %copy-done), kind=kOutput, calls=%fused_computation.11 | convolution fusion | flops 1611399168 | bytes 7602176 | tf_op jit(solution)/shard_map/dot_general | solution.py:57
  179.8 40.4 %reduce-scatter.2.cloned.1.call-done = bf16[768,1024]{1,0:T(8,128)(2,1)} async-done(((bf16[768,2048]{1,0:T(8,128)(2,1)}), bf16[768,1024]{1,0:T(8,128)(2,1)}) %reduce-scatter.2.cloned.1.call-update) | async-done | bytes 1572880 | tf_op jit(solution)/shard_map/reduce_scatter | solution.py:72
  220.2 4.1 %fusion.2 = bf16[768,1024]{1,0:T(8,128)(2,1)} fusion(f32[12,64,1024]{2,1,0:T(8,128)} %convolution_multiply_fusion, bf16[768,1024]{1,0:T(8,128)(2,1)} %reduce-scatter.2.cloned.1.call-done), kind=kLoop, calls=%fused_computation.4 | loop fusion | flops 2359296 | bytes 6291456 | tf_op jit(solution)/shard_map/convert_element_type | solution.py:78
  (28 shorter events, 7.5 us)
Async XLA Ops:
  7.2 104.0 %copy-start = (bf16[2048,512]{1,0:T(8,128)(2,1)S(1)}, bf16[2048,512]{1,0:T(8,128)(2,1)}, u32[]{:S(2)}) copy-start(bf16[2048,512]{1,0:T(8,128)(2,1)} %param.8) | copy-start | bytes 6291460
  9.3 20.2 %copy-start.6 = (s32[12]{0:T(128)S(1)}, s32[12]{0:T(128)}, u32[]{:S(2)}) copy-start(s32[12]{0:T(128)} %param.12) | copy-start | bytes 148
  10.0 15.2 %all-to-all-start.1 = ((bf16[4,64,512]{2,1,0:T(8,128)(2,1)}), bf16[4,64,512]{2,1,0:T(8,128)(2,1)S(1)}, u32[]{:S(2)}, u32[]{:S(2)}) async-start(bf16[4,64,512]{2,1,0:T(8,128)(2,1)} %copy.36), calls=%async_computation.1 | async-start | bytes 524288 | tf_op jit(solution)/shard_map/all_to_all | solution.py:37
  25.3 17.3 %all-to-all-start = ((bf16[4,1024,64]{1,2,0:T(8,128)(2,1)}), bf16[4,1024,64]{1,2,0:T(8,128)(2,1)}, u32[]{:S(2)}, u32[]{:S(2)}) async-start(bf16[4,1024,64]{1,2,0:T(8,128)(2,1)} %copy.32), calls=%async_computation | async-start | bytes 1048576 | tf_op jit(solution)/shard_map/all_to_all | solution.py:36
  29.4 43.6 %all-reduce.7.cloned.1.call-start = ((), (), s32[]{:S(2)}) async-start(), calls=%async_computation.8 | async-start | bytes 786432 | tf_op jit(solution)/shard_map/psum | solution.py:52
  42.6 3.3 %copy-start.3 = (bf16[768,1024]{1,0:T(8,128)(2,1)S(1)}, bf16[768,1024]{1,0:T(8,128)(2,1)}, u32[]{:S(2)}) copy-start(bf16[768,1024]{1,0:T(8,128)(2,1)} %param.7) | copy-start | bytes 4718596
  44.6 1.4 copy-start.1
  74.6 7.0 %copy-start.4 = (bf16[12,64,64]{1,2,0:T(8,128)(2,1)S(1)}, bf16[12,64,64]{1,2,0:T(8,128)(2,1)}, u32[]{:S(2)}) copy-start(bf16[12,64,64]{1,2,0:T(8,128)(2,1)} %get-tuple-element.19) | copy-start | bytes 294916
  77.0 13.6 %all-to-all-start.3 = ((bf16[4,64,512]{2,1,0:T(8,128)(2,1)}), bf16[4,64,512]{2,1,0:T(8,128)(2,1)}, u32[]{:S(2)}, u32[]{:S(2)}) async-start(bf16[4,64,512]{2,1,0:T(8,128)(2,1)} %copy.45), calls=%async_computation.4 | async-start | bytes 524288 | tf_op jit(solution)/shard_map/all_to_all | solution.py:90
  90.6 17.3 %all-to-all-start.2 = ((bf16[4,1024,64]{1,2,0:T(8,128)(2,1)}), bf16[4,1024,64]{1,2,0:T(8,128)(2,1)}, u32[]{:S(2)}, u32[]{:S(2)}) async-start(bf16[4,1024,64]{1,2,0:T(8,128)(2,1)} %copy.42), calls=%async_computation.3 | async-start | bytes 1048576 | tf_op jit(solution)/shard_map/all_to_all | solution.py:87
  94.8 32.3 %all-reduce.5.cloned.1.call-start = ((), (), s32[]{:S(2)}) async-start(), calls=%async_computation.7 | async-start | bytes 786432 | tf_op jit(solution)/shard_map/psum | solution.py:98
  110.2 64.5 %all-gather.2.cloned.1.call-start = ((), (), s32[]{:S(2)}) async-start(), calls=%async_computation.5 | async-start | bytes 4718592 | tf_op jit(solution)/shard_map/all_gather | solution.py:58
  111.0 109.2 %reduce-scatter.2.cloned.1.call-start = ((), (), s32[]{:S(2)}) async-start(), calls=%async_computation.6 | async-start | bytes 4718592 | tf_op jit(solution)/shard_map/reduce_scatter | solution.py:72
  115.8 0.9 copy-start.5
  116.8 2.3 copy-start.2
Sparse Core Ops, SparseCore 0:
  47.9 25.0 all-reduce.6
  110.4 16.6 all-reduce.4
  128.6 46.0 all-gather.1
  176.8 43.3 reduce-scatter.1
where the time goes:
time: 232 us; the launch traced here: 231 us
  waiting for transfers between devices  145 us (62%)
  matrix products  38 us (16%)
  starting transfers between devices  19.5 us (8%)
  between operations  13.9 us (6%)
  local copies, waits for them, and re-layouts  8.24 us (4%)
  other arithmetic  6.26 us (3%)
    all_gather x1, waiting for transfers between devices, shards(): lax.all_gather(hidden_input, 'mp', axis=1, tiled=True)  43.8 us
    reduce_scatter x1, waiting for transfers between devices, shards(): lax.psum_scatter(back_part.astype(jnp.bfloat16), 'mp', scatter_dimension=...  40.4 us
    psum x1, waiting for transfers between devices, shards(): lax.psum(u_part.astype(jnp.bfloat16), 'mp').astype(jnp.float32)  25.2 us
    all_to_all x1, waiting for transfers between devices, shards(): lax.all_to_all(slot_a.astype(jnp.bfloat16), 'dp', split_axis=0, concat_ax...  11.3 us
    all_to_all x1, waiting for transfers between devices, shards(): lax.all_to_all(outgoing_down, 'dp', split_axis=0, concat_axis=0, tiled=True)  10.2 us
    all_to_all x1, waiting for transfers between devices, shards(): lax.all_to_all(outgoing_up, 'dp', split_axis=0, concat_axis=0, tiled=True)  6.48 us
    all_to_all x1, starting transfers between devices, shards(): lax.all_to_all(outgoing_up, 'dp', split_axis=0, concat_axis=0, tiled=True)  6.32 us
    dot_general x1, matrix products, shards(): jnp.dot(lax.all_gather(hidden_input, 'mp', axis=1, tiled=True), key_weigh...  5.03 us
  transfers between devices with their start and end apart: 8, of which 8 were waited for; matrix products, arithmetic and copies ran while one was open for 14% of the time, Pallas kernels for 0%

commit v1 on v0

v1 whole, which is shorter than its diff:
```python
import jax
import jax.numpy as jnp
from jax import lax
from jax.sharding import PartitionSpec as P

SCALE = 2.0
F32 = jnp.float32
BF16 = jnp.bfloat16


def shift(value, axis, by):
    size = lax.axis_size(axis)
    return lax.ppermute(value, axis, [(i, (i + by) % size) for i in range(size)])


def after(value, *others):
    return lax.optimization_barrier((value, *others))[0]


def nn(a, b):
    return lax.dot_general(a, b, (((1,), (0,)), ((), ())), preferred_element_type=F32)


def nt(a, b):
    return lax.dot_general(a, b, (((1,), (1,)), ((), ())), preferred_element_type=F32)


def tn(a, b):
    return lax.dot_general(a, b, (((0,), (0,)), ((), ())), preferred_element_type=F32)


def shards(x, w, down, up, gy, owner, table):
    tok, feat = x.shape
    cols = w.shape[1]
    rank = up.shape[1]
    sites = up.shape[0]
    n_dp, n_mp, n_pair = (lax.axis_size(a) for a in ("dp", "mp", "pair"))
    me_dp, me_mp, me_pair = (lax.axis_index(a) for a in ("dp", "mp", "pair"))

    part = feat // n_pair
    w_own = lax.dynamic_slice(w, (me_mp * feat, 0), (feat, cols))
    w_sent = []
    for s in range(1, n_mp):
        row = ((me_mp + s) % n_mp) * feat + me_pair * part
        w_sent.append(shift(lax.dynamic_slice(w, (row, 0), (part, cols)), "mp", s))

    wanted = lax.dynamic_index_in_dim(table[0], me_pair, 0, keepdims=False)
    maps = jnp.concatenate([down.transpose(0, 2, 1), up], axis=2)
    slots = []
    for s in range(n_dp):
        chosen = lax.dynamic_index_in_dim(maps, wanted[(me_dp + s) % n_dp], 0, keepdims=False)
        slots.append(shift(chosen, "dp", s) if s else chosen)

    w_rows = [w_own]
    for piece in w_sent:
        pieces = jnp.zeros((n_pair, part, cols), BF16)
        for q in range(n_pair):
            got = shift(piece, "pair", q) if q else piece
            pieces = lax.dynamic_update_slice(pieces, got[None], ((me_pair - q) % n_pair, 0, 0))
        w_rows.append(pieces.reshape(feat, cols))

    gy_all = [gy] + [shift(after(gy, *w_sent), "mp", s) for s in range(1, n_mp)]

    y_own = nn(x, w_own)
    y_got = [shift(nn(x, w_rows[s]).astype(BF16), "mp", n_mp - s) for s in range(1, n_mp)]

    adapters = jnp.concatenate(slots, axis=0)
    a_down, a_up = adapters[:, :feat], adapters[:, feat:]
    source = (me_dp - jnp.arange(n_dp, dtype=jnp.int32)) % n_dp
    hit = (owner[:, None] == source[None, :]).astype(BF16)
    hit = jnp.broadcast_to(
        hit[:, None, :, None], (owner.shape[0], tok // owner.shape[0], n_dp, rank)
    ).reshape(tok, n_dp * rank)
    u_part = (nt(x, a_down) * hit).astype(BF16)
    h_part = (nt(gy, a_up) * hit).astype(BF16)
    fold = lambda v: v.reshape(tok, n_dp, rank).sum(1).astype(BF16)
    uh_part = jnp.concatenate([fold(u_part), fold(h_part)], axis=1)
    uh = uh_part.astype(F32)
    for s in range(1, n_mp):
        uh = uh + shift(uh_part, "mp", s).astype(F32)
    uh = uh.astype(BF16)
    u_wide = jnp.tile(uh[:, :rank], (1, n_dp)) * hit
    h_wide = jnp.tile(uh[:, rank:], (1, n_dp)) * hit

    grads = jnp.concatenate([tn(h_wide, x), tn(u_wide, gy)], axis=1).astype(BF16)
    total = jnp.zeros((sites, rank, feat + cols), F32)
    mine = jnp.arange(sites, dtype=jnp.int32)
    for s in range(n_dp):
        sent = grads[s * rank:(s + 1) * rank]
        got = shift(sent, "dp", n_dp - s) if s else sent
        use = (mine == wanted[(me_dp + s) % n_dp]).astype(F32)
        total = total + use[:, None, None] * got.astype(F32)[None]
    total_part = total.astype(BF16)
    total = total_part.astype(F32)
    for q in range(1, n_pair):
        total = total + shift(total_part, "pair", q).astype(F32)
    total = SCALE * total
    down_grad = total[:, :, :feat].transpose(0, 2, 1)
    up_grad = total[:, :, feat:]

    back = SCALE * nn(h_wide, a_down)
    for g, rows in zip(gy_all, w_rows):
        back = back + nt(g, rows)
    y = y_own + SCALE * nn(u_wide, a_up)
    for got in y_got:
        y = y + got.astype(F32)
    return y.astype(BF16), back.astype(BF16), down_grad, up_grad


def solution(mesh):
    rows = P(("groups", "dp", "pair"), "mp")
    in_specs = (
        rows,
        P(None, "mp"),
        P(("groups", "dp"), "mp", None),
        P(("groups", "dp"), None, "mp"),
        rows,
        P(("groups", "dp", "pair")),
        P(("groups", "dp"), None, None),
    )
    out_specs = (rows, rows, P(("groups", "dp"), "mp", None), P(("groups", "dp"), None, "mp"))
    return jax.shard_map(shards, mesh=mesh, in_specs=in_specs, out_specs=out_specs, check_vma=False)
```

time: 232 us -> 99.7 us (0.43)
  waiting for transfers between devices: 145 us -> 37.5 us
  matrix products: 38 us -> 16.2 us
  between operations: 13.9 us -> 8.33 us
  local copies, waits for them, and re-layouts: 8.24 us -> 12.5 us
  starting transfers between devices: 19.5 us -> 16.8 us
    all_gather x1 -> x0, waiting for transfers between devices: 43.8 us -> none  [shards(): lax.all_gather(hidden_input, 'mp', axis=1, tiled=True)]
    reduce_scatter x1 -> x0, waiting for transfers between devices: 40.4 us -> none  [shards(): lax.psum_scatter(back_part.astype(jnp.bfloat16), 'mp', scatter_dimension=...]
    ppermute x0 -> x12, waiting for transfers between devices: none -> 37.5 us  [shift(): lax.ppermute(value, axis, [(i, (i + by) % size) for i in range(size)])]
    all_to_all x4 -> x0, waiting for transfers between devices: 30.7 us -> none  [the longest x1 11.3 us: shards(): lax.all_to_all(slot_a.astype(jnp.bfloat16), 'dp', split_axis=0, concat_ax...]
    psum x2 -> x0, waiting for transfers between devices: 29.2 us -> none  [the longest x1 25.2 us: shards(): lax.psum(u_part.astype(jnp.bfloat16), 'mp').astype(jnp.float32)]
    dot_general x16 -> x10, matrix products: 38 us -> 16.2 us  [the longest x4 8.73 us: nt(): lax.dot_general(a, b, (((1,), (1,)), ((), ())), preferred_element_type=F32)]
    all_to_all x4 -> x0, starting transfers between devices: 19.2 us -> none  [the longest x1 6.32 us: shards(): lax.all_to_all(outgoing_up, 'dp', split_axis=0, concat_axis=0, tiled=True)]
    ppermute x0 -> x12, starting transfers between devices: none -> 16.8 us  [shift(): lax.ppermute(value, axis, [(i, (i + by) % size) for i in range(size)])]
  transfers between devices with their start and end apart: 8 -> 12, of which waited for: 8 -> 6; matrix products, arithmetic and copies ran while one was open for 14% -> 32% of each run, Pallas kernels for 0% -> 0%
where the time goes in v1:
time: 99.7 us; the launch traced here: 99 us
  waiting for transfers between devices  37.5 us (38%)
  starting transfers between devices  16.8 us (17%)
  matrix products  16.2 us (16%)
  local copies, waits for them, and re-layouts  12.5 us (13%)
  between operations  8.33 us (8%)
  other arithmetic  7.67 us (8%)
    ppermute x12, waiting for transfers between devices, shift(): lax.ppermute(value, axis, [(i, (i + by) % size) for i in range(size)])  37.5 us
    ppermute x12, starting transfers between devices, shift(): lax.ppermute(value, axis, [(i, (i + by) % size) for i in range(size)])  16.8 us
    dot_general x4, matrix products, nt(): lax.dot_general(a, b, (((1,), (1,)), ((), ())), preferred_element_type=F32)  8.73 us
    dot_general x4, matrix products, nn(): lax.dot_general(a, b, (((1,), (0,)), ((), ())), preferred_element_type=F32)  5.18 us
    unnamed x25, local copies, waits for them, and re-layouts  2.88 us
    another operation x2, local copies, waits for them, and re-layouts, shards(): u_wide = jnp.tile(uh[:, :rank], (1, n_dp)) * hit  2.83 us
    convert_element_type x2, other arithmetic, shards(): use = (mine == wanted[(me_dp + s) % n_dp]).astype(F32)  2.45 us
    dot_general x2, matrix products, tn(): lax.dot_general(a, b, (((0,), (0,)), ((), ())), preferred_element_type=F32)  2.32 us
  transfers between devices with their start and end apart: 12, of which 6 were waited for; matrix products, arithmetic and copies ran while one was open for 32% of the time, Pallas kernels for 0%

profile of v1, /device:TPU:0, one launch (start us, length us, event | category | flops | bytes accessed | tf_op | source)
XLA Modules:
  0.0 99.0 jit_solution(2360900276333577099)
XLA Ops:
  0.7 1.6 %copy-done = bf16[2048,512]{1,0:T(8,128)(2,1)S(1)} copy-done((bf16[2048,512]{1,0:T(8,128)(2,1)S(1)}, bf16[2048,512]{1,0:T(8,128)(2,1)}, u32[]{:S(2)}) %copy-start) | copy-done | bytes 2097176
  3.1 2.9 %collective-permute-start.4 = (bf16[512,512]{1,0:T(8,128)(2,1)}, bf16[512,512]{1,0:T(8,128)(2,1)}, u32[]{:S(2)}, u32[]{:S(2)}) collective-permute-start(bf16[512,512]{1,0:T(8,128)(2,1)} %constant_dynamic-slice_fusion), channel_id=1, source_target_pairs={{0,2},{2,0},{1,3},{3,1},{4,6},{6,4},{5,7},{7,5},{8,10},{10,8},{9,1... | collective-permute-start | bytes 1572872 | tf_op jit(solution)/shard_map/ppermute | solution.py:13
  6.0 1.5 %constant_dynamic-slice_fusion.4 = (s32[1,1,1]{2,1,0:T(1,128)}, s32[1,1,1]{2,1,0:T(1,128)}, s32[1,1,1]{2,1,0:T(1,128)}, s32[1,1,1]{2,1,0:T(1,128)}) fusion(s32[1,2,4]{2,1,0:T(2,128)} %param.13, s32[]{:T(128)S(6)} %select_n.106, s32[]{:T(128)S(6)} %select_n.109, s32[]{:T(128)S(6)} %select_n.113, s32[]{:T(128)S(6)} %select_n.121, s32[]{:T(128)S(6)} %select_n.117), kind=kLoop, calls=%fused_computation.69 | loop fusion | bytes 52 | tf_op jit(solution)/shard_map/dynamic_slice | solution.py:51
  14.8 2.0 %fusion.19 = (bf16[64,1536]{1,0:T(8,128)(2,1)S(1)}, bf16[64,1536]{1,0:T(8,128)(2,1)}, bf16[64,1536]{1,0:T(8,128)(2,1)}, bf16[64,1536]{1,0:T(8,128)(2,1)}) fusion(s32[]{:T(128)S(6)} %select_n.110, bf16[2,64,1024]{2,1,0:T(8,128)(2,1)} %bitcast.66, bf16[2,64,512]{2,1,0:T(8,128)(2,1)} %param.10, s32[]{:T(128)S(6)} %select_n.114, s32[]{:T(128)S(6)} %select_n.118, ...), kind=kLoop, calls=%fused_computation.48 | loop fusion | flops 1572864 | bytes 1179664 | tf_op jit(solution)/shard_map/jit(dynamic_index_in_dim)/squeeze | solution.py:51
  16.9 1.5 %collective-permute-start = (bf16[64,1536]{1,0:T(8,128)(2,1)}, bf16[64,1536]{1,0:T(8,128)(2,1)}, u32[]{:S(2)}, u32[]{:S(2)}) collective-permute-start(bf16[64,1536]{1,0:T(8,128)(2,1)} %get-tuple-element.23), channel_id=1, source_target_pairs={{0,4},{4,8},{8,12},{12,0},{1,5},{5,9},{9,13},{13,1},{2,6},{6,10},{... | collective-permute-start | bytes 589832 | tf_op jit(solution)/shard_map/ppermute | solution.py:13
  18.4 2.6 %collective-permute-start.1 = (bf16[64,1536]{1,0:T(8,128)(2,1)}, bf16[64,1536]{1,0:T(8,128)(2,1)}, u32[]{:S(2)}, u32[]{:S(2)}) collective-permute-start(bf16[64,1536]{1,0:T(8,128)(2,1)} %get-tuple-element.24), channel_id=1, source_target_pairs={{0,8},{4,12},{8,0},{12,4},{1,9},{5,13},{9,1},{13,5},{2,10},{6,14},... | collective-permute-start | bytes 589832 | tf_op jit(solution)/shard_map/ppermute | solution.py:13
  21.1 1.5 %collective-permute-start.2 = (bf16[64,1536]{1,0:T(8,128)(2,1)}, bf16[64,1536]{1,0:T(8,128)(2,1)}, u32[]{:S(2)}, u32[]{:S(2)}) collective-permute-start(bf16[64,1536]{1,0:T(8,128)(2,1)} %get-tuple-element.25), channel_id=1, source_target_pairs={{0,12},{4,0},{8,4},{12,8},{1,13},{5,1},{9,5},{13,9},{2,14},{6,2},{... | collective-permute-start | bytes 589832 | tf_op jit(solution)/shard_map/ppermute | solution.py:13
  23.6 3.9 %fusion.9 = f32[1024,768]{0,1:T(8,128)} fusion(bf16[768,512]{1,0:T(8,128)(2,1)} %param.11, bf16[2048,512]{1,0:T(8,128)(2,1)S(1)} %copy-done, s32[]{:T(128)S(6)} %select_n.104), kind=kOutput, calls=%fused_computation.19 | convolution fusion | flops 805306368 | bytes 4980740 | tf_op jit(solution)/shard_map/dot_general | solution.py:25
  27.5 2.2 %fusion.11 = f32[512,768]{1,0:T(8,128)} fusion(bf16[768,1024]{1,0:T(8,128)(2,1)S(1)} %copy-done.6, bf16[2048,512]{1,0:T(8,128)(2,1)S(1)} %copy-done, s32[]{:T(128)S(6)} %select_n.104), kind=kOutput, calls=%fused_computation.21 | convolution fusion | flops 805306368 | bytes 4194308 | tf_op jit(solution)/shard_map/dot_general | solution.py:21
  29.7 4.3 %collective-permute-done.1 = bf16[64,1536]{1,0:T(8,128)(2,1)} collective-permute-done((bf16[64,1536]{1,0:T(8,128)(2,1)}, bf16[64,1536]{1,0:T(8,128)(2,1)}, u32[]{:S(2)}, u32[]{:S(2)}) %collective-permute-start.1) | collective-permute-done | bytes 196640 | tf_op jit(solution)/shard_map/ppermute | solution.py:13
  34.0 1.2 %pad_maximum_fusion = bf16[256,1536]{1,0:T(8,128)(2,1)S(1)} fusion(bf16[64,1536]{1,0:T(8,128)(2,1)} %collective-permute-done.2, bf16[64,1536]{1,0:T(8,128)(2,1)} %collective-permute-done.1, bf16[64,1536]{1,0:T(8,128)(2,1)} %collective-permute-done, bf16[64,1536]{1,0:T(8,128)(2,1)S(1)} %get-tuple-element.22), kind=kLoop, calls=%fused_computation.26 | loop fusion | flops 3145728 | bytes 1572864 | tf_op jit(solution)/shard_map/concatenate | solution.py:67
  35.2 1.4 %fusion.7 = bf16[768,256]{0,1:T(8,128)(2,1)} fusion(bf16[768,1024]{1,0:T(8,128)(2,1)S(1)} %copy-done.6, bf16[768,256]{0,1:T(8,128)(2,1)S(1)} %copy.18, bf16[256,1536]{1,0:T(8,128)(2,1)S(1)} %pad_maximum_fusion), kind=kOutput, calls=%fused_computation.13 | convolution fusion | flops 403243008 | bytes 2883584 | tf_op jit(solution)/shard_map/dot_general | solution.py:25
  36.6 1.3 %fusion.8 = bf16[768,256]{0,1:T(8,128)(2,1)S(1)} fusion(bf16[768,512]{1,0:T(8,128)(2,1)S(1)} %copy-done.9, bf16[768,256]{0,1:T(8,128)(2,1)S(1)} %copy.18, bf16[64,1536]{1,0:T(8,128)(2,1)} %collective-permute-done.2, bf16[64,1536]{1,0:T(8,128)(2,1)} %collective-permute-done.1, bf16[64,1536]{1,0:T(8,128)(2,1)} %collective-permute-done, ...), kind=kOutput, calls=%fused_computation.14 | convolution fusion | flops 202964992 | bytes 2359296 | tf_op jit(solution)/shard_map/dot_general | solution.py:25
  38.0 1.1 %reduce_sum.24 = bf16[768,64]{0,1:T(8,128)(2,1)S(1)} reduce(bf16[768,4,64]{0,2,1:T(8,128)(2,1)} %bitcast.65, bf16[]{:T(256)} %constant.165.clone.1), dimensions={1}, to_apply=%region_0.1 | reduce | flops 147456 | bytes 491522 | tf_op jit(solution)/shard_map/reduce_sum | solution.py:76
  39.6 1.3 %compare_convert_fusion.3 = (f32[2]{0:T(128)S(1)}, f32[2]{0:T(128)S(1)}) fusion(s32[]{:T(128)} %bitcast.4, s32[]{:T(128)} %bitcast.2), kind=kLoop, calls=%fused_computation.75 | loop fusion | flops 8 | bytes 24 | tf_op jit(solution)/shard_map/convert_element_type | solution.py:91
  40.9 1.2 %compare_convert_fusion.1 = (f32[2]{0:T(128)S(1)}, f32[2]{0:T(128)S(1)}) fusion(s32[]{:T(128)} %bitcast.8, s32[]{:T(128)} %bitcast.6), kind=kLoop, calls=%fused_computation.73 | loop fusion | flops 8 | bytes 24 | tf_op jit(solution)/shard_map/convert_element_type | solution.py:91
  42.1 3.7 %collective-permute-done.3 = bf16[768,128]{0,1:T(8,128)(2,1)S(1)} collective-permute-done((bf16[768,128]{0,1:T(8,128)(2,1)S(1)}, bf16[768,128]{0,1:T(8,128)(2,1)S(1)}, u32[]{:S(2)}, u32[]{:S(2)}) %collective-permute-start.3) | collective-permute-done | bytes 196640 | tf_op jit(solution)/shard_map/ppermute | solution.py:13
  46.7 1.7 %tile.8 = bf16[768,4,64]{0,2,1:T(8,128)(2,1)} broadcast(bf16[768,64]{0,1:T(8,128)(2,1)} %get-tuple-element.27), dimensions={0,2} | broadcast | bytes 491520 | tf_op jit(solution)/shard_map/tile | solution.py:82
  48.4 1.2 %copy.19 = bf16[768,256]{1,0:T(8,128)(2,1)S(1)} copy(bf16[768,256]{0,1:T(8,128)(2,1)} %bitcast.64) | data formatting | bytes 786432 | tf_op jit(solution)/shard_map/tile | solution.py:82
  49.6 1.7 %convolution_convert_fusion.2 = bf16[256,512]{1,0:T(8,128)(2,1)S(1)} fusion(bf16[768,512]{1,0:T(8,128)(2,1)} %param.11, bf16[768,256]{1,0:T(8,128)(2,1)S(1)} %copy.19, bf16[768,256]{1,0:T(8,128)(2,1)S(1)} %reshape.104), kind=kOutput, calls=%fused_computation.15 | convolution fusion | flops 201654272 | bytes 1835008 | tf_op jit(solution)/shard_map/dot_general | solution.py:29
  52.1 4.7 %collective-permute-start.8 = (bf16[64,1536]{1,0:T(8,128)(2,1)S(1)}, bf16[64,1536]{1,0:T(8,128)(2,1)S(1)}, u32[]{:S(2)}, u32[]{:S(2)}) collective-permute-start(bf16[64,1536]{1,0:T(8,128)(2,1)S(1)} %get-tuple-element.19), channel_id=1, source_target_pairs={{0,12},{4,0},{8,4},{12,8},{1,13},{5,1},{9,5},{13,9},{2,14},{6,2},{... | collective-permute-start | bytes 589832 | tf_op jit(solution)/shard_map/ppermute | solution.py:13
  57.0 1.4 %collective-permute-start.9 = (bf16[64,1536]{1,0:T(8,128)(2,1)S(1)}, bf16[64,1536]{1,0:T(8,128)(2,1)S(1)}, u32[]{:S(2)}, u32[]{:S(2)}) collective-permute-start(bf16[64,1536]{1,0:T(8,128)(2,1)S(1)} %get-tuple-element.21), channel_id=1, source_target_pairs={{0,8},{4,12},{8,0},{12,4},{1,9},{5,13},{9,1},{13,5},{2,10},{6,14},... | collective-permute-start | bytes 589832 | tf_op jit(solution)/shard_map/ppermute | solution.py:13
  59.7 1.1 %bitcast_dynamic-update-slice_fusion.1 = bf16[2,512,512]{2,1,0:T(8,128)(2,1)S(1)} fusion(bf16[2,512,512]{2,1,0:T(8,128)(2,1)S(1)} %broadcast_in_dim.9, s32[]{:T(128)S(6)} %select_n.127, bf16[512,512]{1,0:T(8,128)(2,1)} %collective-permute-done.4), kind=kLoop, calls=%fused_computation.35 | loop fusion | bytes 1048580 | tf_op jit(solution)/shard_map/dynamic_update_slice | solution.py:59
  60.8 3.2 %collective-permute-done.8 = bf16[64,1536]{1,0:T(8,128)(2,1)S(1)} collective-permute-done((bf16[64,1536]{1,0:T(8,128)(2,1)S(1)}, bf16[64,1536]{1,0:T(8,128)(2,1)S(1)}, u32[]{:S(2)}, u32[]{:S(2)}) %collective-permute-start.8) | collective-permute-done | bytes 196640 | tf_op jit(solution)/shard_map/ppermute | solution.py:13
  64.0 3.5 %collective-permute-done.10 = bf16[64,1536]{1,0:T(8,128)(2,1)S(1)} collective-permute-done((bf16[64,1536]{1,0:T(8,128)(2,1)S(1)}, bf16[64,1536]{1,0:T(8,128)(2,1)S(1)}, u32[]{:S(2)}, u32[]{:S(2)}) %collective-permute-start.10) | collective-permute-done | bytes 196640 | tf_op jit(solution)/shard_map/ppermute | solution.py:13
  67.6 7.4 %collective-permute-done.9 = bf16[64,1536]{1,0:T(8,128)(2,1)S(1)} collective-permute-done((bf16[64,1536]{1,0:T(8,128)(2,1)S(1)}, bf16[64,1536]{1,0:T(8,128)(2,1)S(1)}, u32[]{:S(2)}, u32[]{:S(2)}) %collective-permute-start.9) | collective-permute-done | bytes 196640 | tf_op jit(solution)/shard_map/ppermute | solution.py:13
  75.4 1.0 %fusion.4 = bf16[768,512]{0,1:T(8,128)(2,1)S(1)} fusion(bf16[1024,512]{1,0:T(8,128)(2,1)S(1)} %bitcast.60, bf16[768,1024]{1,0:T(8,128)(2,1)S(1)} %copy-done.7), kind=kOutput, calls=%fused_computation.8 | convolution fusion | flops 805699584 | bytes 3407872 | tf_op jit(solution)/shard_map/dot_general | solution.py:21
  78.2 0.8 slice_bitcast_fusion
  79.0 2.2 %fusion.1 = bf16[768,1024]{1,0:T(8,128)(2,1)} fusion(f32[1024,768]{0,1:T(8,128)S(1)} %copy-done.1, f32[768,1024]{1,0:T(8,128)S(1)} %fusion.13, bf16[768,512]{1,0:T(8,128)(2,1)S(1)} %collective-permute-done.7, bf16[1024,512]{1,0:T(8,128)(2,1)S(1)} %bitcast.61), kind=kOutput, calls=%fused_computation.2 | convolution fusion | flops 808452096 | bytes 9699328 | tf_op jit(solution)/shard_map/dot_general | solution.py:25
  81.2 15.3 %collective-permute-done.6 = bf16[768,512]{0,1:T(8,128)(2,1)S(1)} collective-permute-done((bf16[768,512]{0,1:T(8,128)(2,1)S(1)}, bf16[768,512]{0,1:T(8,128)(2,1)S(1)}, u32[]{:S(2)}, u32[]{:S(2)}) %collective-permute-start.6) | collective-permute-done | bytes 786464 | tf_op jit(solution)/shard_map/ppermute | solution.py:13
  96.5 1.4 %fusion.3 = bf16[768,512]{0,1:T(8,128)(2,1)S(1)} fusion(f32[512,768]{1,0:T(8,128)S(1)} %copy-done.8, bf16[768,512]{0,1:T(8,128)(2,1)S(1)} %collective-permute-done.6, bf16[768,256]{1,0:T(8,128)(2,1)S(1)} %copy-done.5, bf16[768,256]{1,0:T(8,128)(2,1)S(1)} %reshape.104, bf16[64,1536]{1,0:T(8,128)(2,1)} %collective-permute-done.2, ...), kind=kOutput, calls=%fused_computation.5 | convolution fusion | flops 204537856 | bytes 4718592 | tf_op jit(solution)/shard_map/dot_general | solution.py:21
  97.8 1.2 %copy.23 = bf16[768,512]{1,0:T(8,128)(2,1)} copy(bf16[768,512]{0,1:T(8,128)(2,1)S(1)} %fusion.3) | data formatting | bytes 1572864
  (58 shorter events, 7.9 us)
Async XLA Ops:
  0.6 1.6 %copy-start = (bf16[2048,512]{1,0:T(8,128)(2,1)S(1)}, bf16[2048,512]{1,0:T(8,128)(2,1)}, u32[]{:S(2)}) copy-start(bf16[2048,512]{1,0:T(8,128)(2,1)} %param.8) | copy-start | bytes 6291460
  0.6 21.9 %copy-start.11 = (s32[12]{0:T(128)S(1)}, s32[12]{0:T(128)}, u32[]{:S(2)}) copy-start(s32[12]{0:T(128)} %param.12) | copy-start | bytes 148
  3.1 55.9 %collective-permute-start.4 = (bf16[512,512]{1,0:T(8,128)(2,1)}, bf16[512,512]{1,0:T(8,128)(2,1)}, u32[]{:S(2)}, u32[]{:S(2)}) collective-permute-start(bf16[512,512]{1,0:T(8,128)(2,1)} %constant_dynamic-slice_fusion), channel_id=1, source_target_pairs={{0,2},{2,0},{1,3},{3,1},{4,6},{6,4},{5,7},{7,5},{8,10},{10,8},{9,1... | collective-permute-start | bytes 1572872 | tf_op jit(solution)/shard_map/ppermute | solution.py:13
  16.9 12.8 %collective-permute-start = (bf16[64,1536]{1,0:T(8,128)(2,1)}, bf16[64,1536]{1,0:T(8,128)(2,1)}, u32[]{:S(2)}, u32[]{:S(2)}) collective-permute-start(bf16[64,1536]{1,0:T(8,128)(2,1)} %get-tuple-element.23), channel_id=1, source_target_pairs={{0,4},{4,8},{8,12},{12,0},{1,5},{5,9},{9,13},{13,1},{2,6},{6,10},{... | collective-permute-start | bytes 589832 | tf_op jit(solution)/shard_map/ppermute | solution.py:13
  18.4 15.6 %collective-permute-start.1 = (bf16[64,1536]{1,0:T(8,128)(2,1)}, bf16[64,1536]{1,0:T(8,128)(2,1)}, u32[]{:S(2)}, u32[]{:S(2)}) collective-permute-start(bf16[64,1536]{1,0:T(8,128)(2,1)} %get-tuple-element.24), channel_id=1, source_target_pairs={{0,8},{4,12},{8,0},{12,4},{1,9},{5,13},{9,1},{13,5},{2,10},{6,14},... | collective-permute-start | bytes 589832 | tf_op jit(solution)/shard_map/ppermute | solution.py:13
  21.1 12.9 %collective-permute-start.2 = (bf16[64,1536]{1,0:T(8,128)(2,1)}, bf16[64,1536]{1,0:T(8,128)(2,1)}, u32[]{:S(2)}, u32[]{:S(2)}) collective-permute-start(bf16[64,1536]{1,0:T(8,128)(2,1)} %get-tuple-element.25), channel_id=1, source_target_pairs={{0,12},{4,0},{8,4},{12,8},{1,13},{5,1},{9,5},{13,9},{2,14},{6,2},{... | collective-permute-start | bytes 589832 | tf_op jit(solution)/shard_map/ppermute | solution.py:13
  23.6 3.9 %copy-start.6 = (bf16[768,1024]{1,0:T(8,128)(2,1)S(1)}, bf16[768,1024]{1,0:T(8,128)(2,1)}, u32[]{:S(2)}) copy-start(bf16[768,1024]{1,0:T(8,128)(2,1)} %param.7) | copy-start | bytes 4718596
  35.1 2.7 %copy-start.2 = (bf16[256,1536]{1,0:T(8,128)(2,1)}, bf16[256,1536]{1,0:T(8,128)(2,1)S(1)}, u32[]{:S(2)}) copy-start(bf16[256,1536]{1,0:T(8,128)(2,1)S(1)} %pad_maximum_fusion) | copy-start | bytes 2359300
  35.1 1.4 %copy-start.9 = (bf16[768,512]{1,0:T(8,128)(2,1)S(1)}, bf16[768,512]{1,0:T(8,128)(2,1)}, u32[]{:S(2)}) copy-start(bf16[768,512]{1,0:T(8,128)(2,1)} %param.11) | copy-start | bytes 2359300
  39.0 6.8 %collective-permute-start.3 = (bf16[768,128]{0,1:T(8,128)(2,1)S(1)}, bf16[768,128]{0,1:T(8,128)(2,1)S(1)}, u32[]{:S(2)}, u32[]{:S(2)}) collective-permute-start(bf16[768,128]{0,1:T(8,128)(2,1)S(1)} %pad_maximum_fusion.3), channel_id=1, source_target_pairs={{0,2},{2,0},{1,3},{3,1},{4,6},{6,4},{5,7},{7,5},{8,10},{10,8},{9,1... | collective-permute-start | bytes 589832 | tf_op jit(solution)/shard_map/ppermute | solution.py:13
  49.6 2.4 %copy-start.4 = (bf16[768,256]{1,0:T(8,128)(2,1)}, bf16[768,256]{1,0:T(8,128)(2,1)S(1)}, u32[]{:S(2)}) copy-start(bf16[768,256]{1,0:T(8,128)(2,1)S(1)} %copy.19) | copy-start | bytes 1179652
  49.6 1.8 %copy-start.7 = (bf16[768,1024]{1,0:T(8,128)(2,1)S(1)}, bf16[768,1024]{1,0:T(8,128)(2,1)}, u32[]{:S(2)}) copy-start(bf16[768,1024]{1,0:T(8,128)(2,1)} %param.7) | copy-start | bytes 4718596
  52.0 6.4 %copy-start.3 = (bf16[256,1536]{1,0:T(8,128)(2,1)S(1)}, bf16[256,1536]{1,0:T(8,128)(2,1)}, u32[]{:S(2)}) copy-start(bf16[256,1536]{1,0:T(8,128)(2,1)} %copy-done.2) | copy-start | bytes 2359300
  52.1 11.9 %collective-permute-start.8 = (bf16[64,1536]{1,0:T(8,128)(2,1)S(1)}, bf16[64,1536]{1,0:T(8,128)(2,1)S(1)}, u32[]{:S(2)}, u32[]{:S(2)}) collective-permute-start(bf16[64,1536]{1,0:T(8,128)(2,1)S(1)} %get-tuple-element.19), channel_id=1, source_target_pairs={{0,12},{4,0},{8,4},{12,8},{1,13},{5,1},{9,5},{13,9},{2,14},{6,2},{... | collective-permute-start | bytes 589832 | tf_op jit(solution)/shard_map/ppermute | solution.py:13
  56.8 10.7 %collective-permute-start.10 = (bf16[64,1536]{1,0:T(8,128)(2,1)S(1)}, bf16[64,1536]{1,0:T(8,128)(2,1)S(1)}, u32[]{:S(2)}, u32[]{:S(2)}) collective-permute-start(bf16[64,1536]{1,0:T(8,128)(2,1)S(1)} %get-tuple-element.20), channel_id=1, source_target_pairs={{0,4},{4,8},{8,12},{12,0},{1,5},{5,9},{9,13},{13,1},{2,6},{6,10},{... | collective-permute-start | bytes 589832 | tf_op jit(solution)/shard_map/ppermute | solution.py:13
  57.0 2.0 %copy-start.10 = (bf16[768,512]{1,0:T(8,128)(2,1)S(1)}, bf16[768,512]{1,0:T(8,128)(2,1)}, u32[]{:S(2)}) copy-start(bf16[768,512]{1,0:T(8,128)(2,1)} %param.11) | copy-start | bytes 2359300
  57.0 18.0 %collective-permute-start.9 = (bf16[64,1536]{1,0:T(8,128)(2,1)S(1)}, bf16[64,1536]{1,0:T(8,128)(2,1)S(1)}, u32[]{:S(2)}, u32[]{:S(2)}) collective-permute-start(bf16[64,1536]{1,0:T(8,128)(2,1)S(1)} %get-tuple-element.21), channel_id=1, source_target_pairs={{0,8},{4,12},{8,0},{12,4},{1,9},{5,13},{9,1},{13,5},{2,10},{6,14},... | collective-permute-start | bytes 589832 | tf_op jit(solution)/shard_map/ppermute | solution.py:13
  59.0 20.0 %collective-permute-start.7 = (bf16[768,512]{1,0:T(8,128)(2,1)S(1)}, bf16[768,512]{1,0:T(8,128)(2,1)S(1)}, u32[]{:S(2)}, u32[]{:S(2)}) collective-permute-start(bf16[768,512]{1,0:T(8,128)(2,1)S(1)} %copy-done.10), channel_id=1, source_target_pairs={{0,2},{2,0},{1,3},{3,1},{4,6},{6,4},{5,7},{7,5},{8,10},{10,8},{9,1... | collective-permute-start | bytes 2359304 | tf_op jit(solution)/shard_map/ppermute | solution.py:13
  59.6 15.8 %collective-permute-start.5 = (bf16[512,512]{1,0:T(8,128)(2,1)}, bf16[512,512]{1,0:T(8,128)(2,1)S(1)}, u32[]{:S(2)}, u32[]{:S(2)}) collective-permute-start(bf16[512,512]{1,0:T(8,128)(2,1)} %collective-permute-done.4), channel_id=1, source_target_pairs={{0,1},{1,0},{2,3},{3,2},{4,5},{5,4},{6,7},{7,6},{8,9},{9,8},{10,11... | collective-permute-start | bytes 1572872 | tf_op jit(solution)/shard_map/ppermute | solution.py:13
  75.3 1.8 %collective-permute-start.11 = (bf16[2,64,1536]{2,1,0:T(8,128)(2,1)S(1)}, bf16[2,64,1536]{2,1,0:T(8,128)(2,1)S(1)}, u32[]{:S(2)}, u32[]{:S(2)}) collective-permute-start(bf16[2,64,1536]{2,1,0:T(8,128)(2,1)S(1)} %add_convert_fusion), channel_id=1, source_target_pairs={{0,1},{1,0},{2,3},{3,2},{4,5},{5,4},{6,7},{7,6},{8,9},{9,8},{10,11... | collective-permute-start | bytes 1179656 | tf_op jit(solution)/shard_map/ppermute | solution.py:13
  76.5 2.5 %copy-start.1 = (f32[1024,768]{0,1:T(8,128)S(1)}, f32[1024,768]{0,1:T(8,128)}, u32[]{:S(2)}) copy-start(f32[1024,768]{0,1:T(8,128)} %fusion.9) | copy-start | bytes 9437188
  76.5 20.0 %collective-permute-start.6 = (bf16[768,512]{0,1:T(8,128)(2,1)S(1)}, bf16[768,512]{0,1:T(8,128)(2,1)S(1)}, u32[]{:S(2)}, u32[]{:S(2)}) collective-permute-start(bf16[768,512]{0,1:T(8,128)(2,1)S(1)} %fusion.4), channel_id=1, source_target_pairs={{0,2},{2,0},{1,3},{3,1},{4,6},{6,4},{5,7},{7,5},{8,10},{10,8},{9,1... | collective-permute-start | bytes 2359304 | tf_op jit(solution)/shard_map/ppermute | solution.py:13
  79.0 17.5 %copy-start.5 = (bf16[768,256]{1,0:T(8,128)(2,1)S(1)}, bf16[768,256]{1,0:T(8,128)(2,1)}, u32[]{:S(2)}) copy-start(bf16[768,256]{1,0:T(8,128)(2,1)} %copy-done.4) | copy-start | bytes 1179652
  79.0 17.5 %copy-start.8 = (f32[512,768]{1,0:T(8,128)S(1)}, f32[512,768]{1,0:T(8,128)}, u32[]{:S(2)}) copy-start(f32[512,768]{1,0:T(8,128)} %fusion.11) | copy-start | bytes 4718596

commit v2 on v1

v2 whole, which is shorter than its diff:
```python
import functools

import jax
import jax.numpy as jnp
from jax import lax
from jax.experimental import pallas as pl
from jax.experimental.pallas import tpu as pltpu
from jax.sharding import PartitionSpec as P

SCALE = 2.0
F32 = jnp.float32
BF16 = jnp.bfloat16
SMEM = pl.BlockSpec(memory_space=pltpu.SMEM)
VMEM = pl.BlockSpec(memory_space=pltpu.VMEM)
HBM = pl.BlockSpec(memory_space=pl.ANY)


def params():
    return pltpu.CompilerParams(vmem_limit_bytes=48 * 1024 * 1024)


def cost():
    return pl.CostEstimate(flops=1, bytes_accessed=1, transcendentals=0)


def shape(*dims, dtype=BF16):
    return jax.ShapeDtypeStruct(dims, dtype)


def shift(value, axis, by):
    size = lax.axis_size(axis)
    return lax.ppermute(value, axis, [(i, (i + by) % size) for i in range(size)])


def after(value, *others):
    return lax.optimization_barrier((value, *others))[0]


def nn(a, b):
    return lax.dot_general(a, b, (((1,), (0,)), ((), ())), preferred_element_type=F32)


def nt(a, b):
    return lax.dot_general(a, b, (((1,), (1,)), ((), ())), preferred_element_type=F32)


def tn(a, b):
    return lax.dot_general(a, b, (((0,), (0,)), ((), ())), preferred_element_type=F32)


def wanted_site(table, n_dp, s):
    return table[0, lax.axis_index("pair"), lax.rem(lax.axis_index("dp") + s, n_dp)]


def pack_kernel(n_dp, n_mp, n_pair, table, down, up, w, *refs):
    ups, downs, pieces, sem = refs[:n_dp], refs[n_dp:2 * n_dp], refs[2 * n_dp:-1], refs[-1]
    feat = w.shape[0] // n_mp
    part = feat // n_pair
    copies = []
    for s in range(1, n_mp):
        row = lax.rem(lax.axis_index("mp") + s, n_mp) * feat + lax.axis_index("pair") * part
        row = pl.multiple_of(row, part)
        copies.append(pltpu.make_async_copy(w.at[pl.ds(row, part)], pieces[s - 1], sem.at[s - 1]))
    for s in range(n_dp):
        site = wanted_site(table, n_dp, s)
        copies.append(pltpu.make_async_copy(up.at[site], ups[s], sem.at[n_mp - 1 + s]))
        copies.append(pltpu.make_async_copy(down.at[site], downs[s], sem.at[n_mp - 1 + n_dp + s]))
    for copy in copies:
        copy.start()
    for copy in copies:
        copy.wait()


def slot_of(owner, b, n_dp):
    return lax.rem(lax.axis_index("dp") - owner[b] + n_dp, n_dp)


def reduce_kernel(n_dp, owner, act, *refs):
    maps, out, wide = refs[:n_dp], refs[n_dp], refs[n_dp + 1]
    rank = maps[0].shape[0]
    blocks = owner.shape[0]
    rows = act.shape[0] // blocks
    for s in range(n_dp):
        wide[s * rank:(s + 1) * rank, :] = maps[s][...]
    full = nt(act[...], wide[...])
    lane_slot = lax.broadcasted_iota(jnp.int32, (rows, n_dp * rank), 1) // rank
    folded = []
    for b in range(blocks):
        kept = jnp.where(lane_slot == slot_of(owner, b, n_dp), full[b * rows:(b + 1) * rows], 0.0)
        total = kept[:, :rank]
        for s in range(1, n_dp):
            total = total + kept[:, s * rank:(s + 1) * rank]
        folded.append(total)
    for j in range(blocks // 2):
        pair = jnp.concatenate([folded[2 * j], folded[2 * j + 1]], axis=1)
        out[j * rows:(j + 1) * rows, :] = pair.astype(BF16)


def grad_kernel(n_dp, n_part, owner, act, *refs):
    parts, grads, wide = refs[:n_part], refs[n_part:n_part + n_dp], refs[n_part + n_dp]
    rank = wide.shape[1] // n_dp
    blocks = owner.shape[0]
    rows = act.shape[0] // blocks
    total = parts[0][...].astype(F32)
    for part in parts[1:]:
        total = total + part[...].astype(F32)
    lane_slot = lax.broadcasted_iota(jnp.int32, (rows, n_dp * rank), 1) // rank
    for b in range(blocks):
        one = total[(b // 2) * rows:(b // 2 + 1) * rows, (b % 2) * rank:(b % 2 + 1) * rank]
        spread = jnp.concatenate([one] * n_dp, axis=1)
        kept = jnp.where(lane_slot == slot_of(owner, b, n_dp), spread, 0.0)
        wide[b * rows:(b + 1) * rows, :] = kept.astype(BF16)
    full = tn(wide[...], act[...])
    for s in range(n_dp):
        grads[s][...] = full[s * rank:(s + 1) * rank].astype(BF16)


def send_kernel(n_pair, feat, n_mp, x, *refs):
    n_other = n_mp - 1
    pieces, outs, rows = refs[:n_other * n_pair], refs[n_other * n_pair:n_other * n_pair + n_other], refs[-n_other:]
    part = feat // n_pair

    @pl.when(pl.program_id(0) == 0)
    def _():
        for s in range(n_other):
            for q in range(n_pair):
                at = lax.rem(lax.axis_index("pair") + n_pair - q, n_pair) * part
                rows[s][pl.ds(pl.multiple_of(at, part), part), :] = pieces[s * n_pair + q][...]

    for s in range(n_other):
        outs[s][...] = nn(x[...], rows[s][...]).astype(BF16)


def back_kernel(n_dp, n_mp, *refs):
    w, gys, rows, wide, downs, out, own, maps = (
        refs[0], refs[1:1 + n_mp], refs[1 + n_mp:2 * n_mp], refs[2 * n_mp],
        refs[2 * n_mp + 1:-3], refs[-3], refs[-2], refs[-1],
    )
    rank, feat = downs[0].shape

    @pl.when(pl.program_id(0) == 0)
    def _():
        own[...] = w[pl.ds(pl.multiple_of(lax.axis_index("mp") * feat, feat), feat), :]
        for s in range(n_dp):
            maps[s * rank:(s + 1) * rank, :] = downs[s][...]

    total = nt(gys[0][...], own[...]) + SCALE * nn(wide[...], maps[...])
    for gy, row in zip(gys[1:], rows):
        total = total + nt(gy[...], row[...])
    out[...] = total.astype(BF16)


def own_kernel(n_dp, w, x, wide, *refs):
    ups, out, maps = refs[:n_dp], refs[n_dp], refs[n_dp + 1]
    rank = ups[0].shape[0]
    feat = x.shape[1]

    @pl.when(pl.program_id(0) == 0)
    def _():
        for s in range(n_dp):
            maps[s * rank:(s + 1) * rank, :] = ups[s][...]

    own = w[pl.ds(pl.multiple_of(lax.axis_index("mp") * feat, feat), feat), :]
    out[...] = nn(x[...], own) + SCALE * nn(wide[...], maps[...])


def add_kernel(*refs):
    total = refs[0][...]
    for ref in refs[1:-1]:
        total = total + ref[...].astype(F32)
    refs[-1][...] = total.astype(BF16)


def site_kernel(n_dp, feat, table, *refs):
    downs, ups, out = refs[:n_dp], refs[n_dp:2 * n_dp], refs[-1]
    for site in range(out.shape[0]):
        for grads, lo, hi in ((downs, 0, feat), (ups, feat, out.shape[2])):
            total = jnp.zeros((out.shape[1], hi - lo), F32)
            for s in range(n_dp):
                use = wanted_site(table, n_dp, s) == site
                total = total + jnp.where(use, grads[s][...].astype(F32), 0.0)
            out[site, :, lo:hi] = total.astype(BF16)


def last_kernel(feat, *refs):
    parts, down, up = refs[:-2], refs[-2], refs[-1]
    total = parts[0][...].astype(F32)
    for part in parts[1:]:
        total = total + part[...].astype(F32)
    total = SCALE * total
    down[...] = total[:, :, :feat]
    up[...] = total[:, :, feat:]


def shards(x, w, down, up, gy, owner, table):
    tok, feat = x.shape
    cols = w.shape[1]
    sites, rank = up.shape[:2]
    n_dp, n_mp, n_pair = (lax.axis_size(a) for a in ("dp", "mp", "pair"))
    down = down.transpose(0, 2, 1)
    part = feat // n_pair
    tile = tok // 3
    row_block = lambda width: pl.BlockSpec((tile, width), lambda i: (i, 0))
    whole = lambda *dims: pl.BlockSpec(dims, lambda i: (0,) * len(dims))

    gys = [gy] + [shift(gy, "mp", s) for s in range(1, n_mp)]

    packed = pl.pallas_call(
        functools.partial(pack_kernel, n_dp, n_mp, n_pair),
        out_shape=[shape(rank, cols)] * n_dp + [shape(rank, feat)] * n_dp + [shape(part, cols)] * (n_mp - 1),
        in_specs=[SMEM, HBM, HBM, HBM],
        out_specs=[HBM] * (2 * n_dp + n_mp - 1),
        scratch_shapes=[pltpu.SemaphoreType.DMA((n_mp - 1 + 2 * n_dp,))],
        compiler_params=params(), cost_estimate=cost(), name="pack",
    )(table, down, up, w)
    pieces = [shift(packed[2 * n_dp + s - 1], "mp", s) for s in range(1, n_mp)]
    ups = [packed[0]] + [shift(packed[s], "dp", s) for s in range(1, n_dp)]
    downs = [packed[n_dp]] + [shift(packed[n_dp + s], "dp", s) for s in range(1, n_dp)]

    def low_rank(act, maps, name):
        mine = pl.pallas_call(
            functools.partial(reduce_kernel, n_dp),
            out_shape=shape(tok // 2, 2 * rank),
            in_specs=[SMEM] + [VMEM] * (1 + n_dp), out_specs=VMEM,
            scratch_shapes=[pltpu.VMEM((n_dp * rank, act.shape[1]), BF16)],
            compiler_params=params(), cost_estimate=cost(), name=name + "_part",
        )(owner, act, *maps)
        return [mine] + [shift(mine, "mp", s) for s in range(1, n_mp)]

    def gradient(act, parts, name):
        *grads, wide = pl.pallas_call(
            functools.partial(grad_kernel, n_dp, n_mp),
            out_shape=[shape(rank, act.shape[1])] * n_dp + [shape(tok, n_dp * rank)],
            in_specs=[SMEM] + [VMEM] * (1 + n_mp), out_specs=[VMEM] * (n_dp + 1),
            compiler_params=params(), cost_estimate=cost(), name=name + "_grad",
        )(owner, act, *parts)
        return [grads[0]] + [shift(grads[s], "dp", n_dp - s) for s in range(1, n_dp)], wide

    h_parts = low_rank(gy, ups, "h")
    down_back, h_wide = gradient(x, h_parts, "down")
    u_parts = low_rank(x, downs, "u")
    up_back, u_wide = gradient(gy, u_parts, "up")

    parts = []
    for piece in pieces:
        parts += [piece] + [shift(piece, "pair", q) for q in range(1, n_pair)]
    sent = pl.pallas_call(
        functools.partial(send_kernel, n_pair, feat, n_mp),
        grid=(3,),
        out_shape=[shape(tok, cols)] * (n_mp - 1) + [shape(feat, cols)] * (n_mp - 1),
        in_specs=[row_block(feat)] + [whole(part, cols)] * len(parts),
        out_specs=[row_block(cols)] * (n_mp - 1) + [whole(feat, cols)] * (n_mp - 1),
        compiler_params=params(), cost_estimate=cost(), name="y_send",
    )(x, *parts)
    w_rows = sent[n_mp - 1:]
    y_got = [shift(sent[s - 1], "mp", n_mp - s) for s in range(1, n_mp)]

    y_own = pl.pallas_call(
        functools.partial(own_kernel, n_dp),
        grid=(3,),
        out_shape=shape(tok, cols, dtype=F32),
        in_specs=[whole(*w.shape), row_block(feat), row_block(n_dp * rank)] + [whole(rank, cols)] * n_dp,
        out_specs=row_block(cols),
        scratch_shapes=[pltpu.VMEM((n_dp * rank, cols), BF16)],
        compiler_params=params(), cost_estimate=cost(), name="y_own",
    )(w, x, u_wide, *ups)

    back = pl.pallas_call(
        functools.partial(back_kernel, n_dp, n_mp),
        grid=(3,),
        out_shape=shape(tok, feat),
        in_specs=[whole(*w.shape)] + [row_block(cols)] * n_mp + [whole(feat, cols)] * (n_mp - 1)
        + [row_block(n_dp * rank)] + [whole(rank, feat)] * n_dp,
        out_specs=row_block(feat),
        scratch_shapes=[pltpu.VMEM((feat, cols), BF16), pltpu.VMEM((n_dp * rank, feat), BF16)],
        compiler_params=params(), cost_estimate=cost(), name="back",
    )(w, *gys, *w_rows, h_wide, *downs)

    summed = pl.pallas_call(
        functools.partial(site_kernel, n_dp, feat),
        out_shape=shape(sites, rank, feat + cols),
        in_specs=[SMEM] + [VMEM] * (2 * n_dp), out_specs=VMEM,
        compiler_params=params(), cost_estimate=cost(), name="sites",
    )(table, *down_back, *up_back)
    both = [summed] + [shift(summed, "pair", q) for q in range(1, n_pair)]
    down_grad, up_grad = pl.pallas_call(
        functools.partial(last_kernel, feat),
        out_shape=[shape(sites, rank, feat, dtype=F32), shape(sites, rank, cols, dtype=F32)],
        in_specs=[VMEM] * n_pair, out_specs=[VMEM] * 2,
        compiler_params=params(), cost_estimate=cost(), name="gradients",
    )(*both)

    y = pl.pallas_call(
        add_kernel,
        grid=(3,),
        out_shape=shape(tok, cols),
        in_specs=[row_block(cols)] * n_mp, out_specs=row_block(cols),
        compiler_params=params(), cost_estimate=cost(), name="y_add",
    )(y_own, *y_got)
    return y, back, down_grad.transpose(0, 2, 1), up_grad


def solution(mesh):
    rows = P(("groups", "dp", "pair"), "mp")
    in_specs = (
        rows,
        P(None, "mp"),
        P(("groups", "dp"), "mp", None),
        P(("groups", "dp"), None, "mp"),
        rows,
        P(("groups", "dp", "pair")),
        P(("groups", "dp"), None, None),
    )
    out_specs = (rows, rows, P(("groups", "dp"), "mp", None), P(("groups", "dp"), None, "mp"))
    return jax.shard_map(shards, mesh=mesh, in_specs=in_specs, out_specs=out_specs, check_vma=False)
```

time: 99.7 us -> 102 us (1.023)
  waiting for transfers between devices: 37.5 us -> 58.7 us
  Pallas kernels: 0 us -> 16.5 us
  matrix products: 16.2 us -> 0 us
  local copies, waits for them, and re-layouts: 12.5 us -> 4.26 us
  other arithmetic: 7.67 us -> 0 us
  between operations: 8.33 us -> 0.77 us
  starting transfers between devices: 16.8 us -> 22.1 us
    ppermute x12 -> x19, waiting for transfers between devices: 37.5 us -> 58.7 us  [shift(): lax.ppermute(value, axis, [(i, (i + by) % size) for i in range(size)])]
    pallas_call x0 -> x11, Pallas kernels: none -> 16.5 us  [the longest x1 3.49 us: shards(): pl.pallas_call(functools.partial(back_kernel, n_dp, n_mp), grid=(3,), out...]
    dot_general x10 -> x0, matrix products: 16.2 us -> none  [the longest x4 8.73 us: nt(): lax.dot_general(a, b, (((1,), (1,)), ((), ())), preferred_element_type=F32)]
    ppermute x12 -> x19, starting transfers between devices: 16.8 us -> 22.1 us  [shift(): lax.ppermute(value, axis, [(i, (i + by) % size) for i in range(size)])]
    another operation x4 -> x0, local copies, waits for them, and re-layouts: 3.02 us -> none  [the longest x2 2.83 us: shards(): u_wide = jnp.tile(uh[:, :rank], (1, n_dp)) * hit]
    convert_element_type x9 -> x0, other arithmetic: 2.99 us -> none  [the longest x2 2.45 us: shards(): use = (mine == wanted[(me_dp + s) % n_dp]).astype(F32)]
    dynamic_slice x2 -> x0, local copies, waits for them, and re-layouts: 2.31 us -> none  [the longest x1 1.49 us: shards(): wanted[(me_dp + s) % n_dp]]
    squeeze x1 -> x0, other arithmetic: 2.04 us -> none  [shards(): lax.dynamic_index_in_dim(maps, wanted[(me_dp + s) % n_dp], 0, keepdims=Fa...]
  transfers between devices with their start and end apart: 12 -> 19, of which waited for: 6 -> 11; matrix products, arithmetic and copies ran while one was open for 32% -> 0% of each run, Pallas kernels for 0% -> 13%
where the time goes in v2:
time: 102 us
  waiting for transfers between devices  58.7 us (58%)
  starting transfers between devices  22.1 us (22%)
  Pallas kernels  16.5 us (16%)
  local copies, waits for them, and re-layouts  4.26 us (4%)
    ppermute x19, waiting for transfers between devices, shift(): lax.ppermute(value, axis, [(i, (i + by) % size) for i in range(size)])  58.7 us
    ppermute x19, starting transfers between devices, shift(): lax.ppermute(value, axis, [(i, (i + by) % size) for i in range(size)])  22.1 us
    unnamed x16, local copies, waits for them, and re-layouts  4.26 us
    pallas_call x1, Pallas kernels, shards(): pl.pallas_call(functools.partial(back_kernel, n_dp, n_mp), grid=(3,), out...  3.49 us
    pallas_call x2, Pallas kernels, gradient(): pl.pallas_call(functools.partial(grad_kernel, n_dp, n_mp), out_shape=[sha...  2.43 us
    pallas_call x2, Pallas kernels, low_rank(): pl.pallas_call(functools.partial(reduce_kernel, n_dp), out_shape=shape(to...  2.36 us
  transfers between devices with their start and end apart: 19, of which 11 were waited for; matrix products, arithmetic and copies ran while one was open for 0% of the time, Pallas kernels for 13%

profile of v2, /device:TPU:0, one launch (start us, length us, event | category | flops | bytes accessed | tf_op | source)
XLA Modules:
  0.0 102.3 jit_solution(2999610434421578819)
XLA Ops:
  0.7 1.7 %copy-done.1 = bf16[2048,512]{1,0:T(8,128)(2,1)S(1)} copy-done((bf16[2048,512]{1,0:T(8,128)(2,1)S(1)}, bf16[2048,512]{1,0:T(8,128)(2,1)}, u32[]{:S(2)}) %copy-start.1) | copy-done | bytes 2097176
  2.4 0.9 copy-done.4
  3.3 0.9 copy-done.5
  4.9 1.9 %pack.1 = (bf16[64,512]{1,0:T(8,128)(2,1)S(1)}, bf16[64,512]{1,0:T(8,128)(2,1)S(1)}, bf16[64,512]{1,0:T(8,128)(2,1)S(1)}, bf16[64,512]{1,0:T(8,128)(2,1)S(1)}, b...) custom-call(s32[1,2,4]{2,1,0:T(2,128)S(1)} %copy-done.7, ...), custom_call_target="tpu_custom_call" | custom-call | flops 1 | bytes 1 | tf_op jit(solution)/shard_map/pack/pallas_call | solution.py:208
  6.8 3.0 %collective-permute-start.7 = (bf16[512,512]{1,0:T(8,128)(2,1)S(1)}, bf16[512,512]{1,0:T(8,128)(2,1)S(1)}, u32[]{:S(2)}, u32[]{:S(2)}) collective-permute-start(bf16[512,512]{1,0:T(8,128)(2,1)S(1)} %get-tuple-element.36), channel_id=1, source_target_pairs={{0,2},{2,0},{1,3},{3,1},{4,6},{6,4},{5,7},{7,5},{8,10},{10,8},{9,1... | collective-permute-start | bytes 1572872 | tf_op jit(solution)/shard_map/ppermute | solution.py:32
  9.8 11.9 %collective-permute-done.7.refs_0_ = bf16[512,512]{1,0:T(8,128)(2,1)S(1)} collective-permute-done((bf16[512,512]{1,0:T(8,128)(2,1)S(1)}, bf16[512,512]{1,0:T(8,128)(2,1)S(1)}, u32[]{:S(2)}, u32[]{:S(2)}) %collective-permute-start.7) | collective-permute-done | bytes 524320 | tf_op jit(solution)/shard_map/ppermute | solution.py:32
  21.7 1.8 %collective-permute-start.4 = (bf16[64,512]{1,0:T(8,128)(2,1)S(1)}, bf16[64,512]{1,0:T(8,128)(2,1)S(1)}, u32[]{:S(2)}, u32[]{:S(2)}) collective-permute-start(bf16[64,512]{1,0:T(8,128)(2,1)S(1)} %get-tuple-element.33), channel_id=1, source_target_pairs={{0,4},{4,8},{8,12},{12,0},{1,5},{5,9},{9,13},{13,1},{2,6},{6,10},{... | collective-permute-start | bytes 196616 | tf_op jit(solution)/shard_map/ppermute | solution.py:32
  23.5 2.6 %collective-permute-start.5 = (bf16[64,512]{1,0:T(8,128)(2,1)S(1)}, bf16[64,512]{1,0:T(8,128)(2,1)S(1)}, u32[]{:S(2)}, u32[]{:S(2)}) collective-permute-start(bf16[64,512]{1,0:T(8,128)(2,1)S(1)} %get-tuple-element.34), channel_id=1, source_target_pairs={{0,8},{4,12},{8,0},{12,4},{1,9},{5,13},{9,1},{13,5},{2,10},{6,14},... | collective-permute-start | bytes 196616 | tf_op jit(solution)/shard_map/ppermute | solution.py:32
  26.1 1.3 %collective-permute-start.6 = (bf16[64,512]{1,0:T(8,128)(2,1)S(1)}, bf16[64,512]{1,0:T(8,128)(2,1)S(1)}, u32[]{:S(2)}, u32[]{:S(2)}) collective-permute-start(bf16[64,512]{1,0:T(8,128)(2,1)S(1)} %get-tuple-element.35), channel_id=1, source_target_pairs={{0,12},{4,0},{8,4},{12,8},{1,13},{5,1},{9,5},{13,9},{2,14},{6,2},{... | collective-permute-start | bytes 196616 | tf_op jit(solution)/shard_map/ppermute | solution.py:32
  28.4 1.0 collective-permute-start.1
  29.4 1.8 %collective-permute-done.5.refs_2_ = bf16[64,512]{1,0:T(8,128)(2,1)S(1)} collective-permute-done((bf16[64,512]{1,0:T(8,128)(2,1)S(1)}, bf16[64,512]{1,0:T(8,128)(2,1)S(1)}, u32[]{:S(2)}, u32[]{:S(2)}) %collective-permute-start.5) | collective-permute-done | bytes 65568 | tf_op jit(solution)/shard_map/ppermute | solution.py:32
  31.2 3.3 %collective-permute-start.2 = (bf16[64,1024]{1,0:T(8,128)(2,1)S(1)}, bf16[64,1024]{1,0:T(8,128)(2,1)S(1)}, u32[]{:S(2)}, u32[]{:S(2)}) collective-permute-start(bf16[64,1024]{1,0:T(8,128)(2,1)S(1)} %get-tuple-element.30), channel_id=1, source_target_pairs={{0,12},{4,0},{8,4},{12,8},{1,13},{5,1},{9,5},{13,9},{2,14},{6,2},{... | collective-permute-start | bytes 393224 | tf_op jit(solution)/shard_map/ppermute | solution.py:32
  34.5 1.5 %collective-permute-start.10 = (bf16[768,512]{1,0:T(8,128)(2,1)S(1)}, bf16[768,512]{1,0:T(8,128)(2,1)S(1)}, u32[]{:S(2)}, u32[]{:S(2)}) collective-permute-start(bf16[768,512]{1,0:T(8,128)(2,1)S(1)} %copy-done.3), channel_id=1, source_target_pairs={{0,2},{2,0},{1,3},{3,1},{4,6},{6,4},{5,7},{7,5},{8,10},{10,8},{9,1... | collective-permute-start | bytes 2359304 | tf_op jit(solution)/shard_map/ppermute | solution.py:32
  36.1 1.4 %y_send.1 = (bf16[768,512]{1,0:T(8,128)(2,1)S(1)}, bf16[1024,512]{1,0:T(8,128)(2,1)S(1)}) custom-call(bf16[768,1024]{1,0:T(8,128)(2,1)S(1)} %copy-done, bf16[512,512]{1,0:T(8,128)(2,1)S(1)} %collective-permute-done.7.refs_0_, bf16[512,512]{1,0:T(8,128)(2,1)S(1)} %collective-permute-done.8.refs_1_), custom_call_target="tpu_custom_call" | custom-call | flops 1 | bytes 1 | tf_op jit(solution)/shard_map/y_send/pallas_call | solution.py:247
  38.1 1.1 %h_part.1.refs_0_ = bf16[384,128]{1,0:T(8,128)(2,1)S(1)} custom-call(s32[12]{0:T(128)S(1)} %copy-done.6, bf16[768,512]{1,0:T(8,128)(2,1)S(1)} %copy-done.3, bf16[64,512]{1,0:T(8,128)(2,1)S(1)} %get-tuple-element.32.refs_0_, bf16[64,512]{1,0:T(8,128)(2,1)S(1)} %collective-permute-done.4.refs_1_, bf16[64,512]{1,0:T(8,128)(2,1)S(1)} %collective-permute-done.5.refs_2_, ...), custom_call_target="tpu_custom_call" | custom-call | flops 1 | bytes 1 | tf_op jit(solution)/shard_map/h_part/pallas_call | solution.py:221
  39.2 1.6 %collective-permute-start.11 = (bf16[384,128]{1,0:T(8,128)(2,1)S(1)}, bf16[384,128]{1,0:T(8,128)(2,1)S(1)}, u32[]{:S(2)}, u32[]{:S(2)}) collective-permute-start(bf16[384,128]{1,0:T(8,128)(2,1)S(1)} %h_part.1.refs_0_), channel_id=1, source_target_pairs={{0,2},{2,0},{1,3},{3,1},{4,6},{6,4},{5,7},{7,5},{8,10},{10,8},{9,1... | collective-permute-start | bytes 294920 | tf_op jit(solution)/shard_map/ppermute | solution.py:32
  41.0 1.3 %u_part.1.refs_0_ = bf16[384,128]{1,0:T(8,128)(2,1)S(1)} custom-call(s32[12]{0:T(128)S(1)} %copy-done.6, bf16[768,1024]{1,0:T(8,128)(2,1)S(1)} %copy-done, bf16[64,1024]{1,0:T(8,128)(2,1)S(1)} %get-tuple-element.27.refs_0_.refs_5_, bf16[64,1024]{1,0:T(8,128)(2,1)S(1)} %collective-permute-done.refs_1_.refs_6_, ...), custom_call_target="tpu_custom_call" | custom-call | flops 1 | bytes 1 | tf_op jit(solution)/shard_map/u_part/pallas_call | solution.py:221
  42.3 1.6 %collective-permute-start.3 = (bf16[384,128]{1,0:T(8,128)(2,1)S(1)}, bf16[384,128]{1,0:T(8,128)(2,1)S(1)}, u32[]{:S(2)}, u32[]{:S(2)}) collective-permute-start(bf16[384,128]{1,0:T(8,128)(2,1)S(1)} %u_part.1.refs_0_), channel_id=1, source_target_pairs={{0,2},{2,0},{1,3},{3,1},{4,6},{6,4},{5,7},{7,5},{8,10},{10,8},{9,1... | collective-permute-start | bytes 294920 | tf_op jit(solution)/shard_map/ppermute | solution.py:32
  43.9 28.7 %collective-permute-done.11.refs_1_ = bf16[384,128]{1,0:T(8,128)(2,1)S(1)} collective-permute-done((bf16[384,128]{1,0:T(8,128)(2,1)S(1)}, bf16[384,128]{1,0:T(8,128)(2,1)S(1)}, u32[]{:S(2)}, u32[]{:S(2)}) %collective-permute-start.11) | collective-permute-done | bytes 98336 | tf_op jit(solution)/shard_map/ppermute | solution.py:32
  72.6 1.3 %down_grad.1 = (bf16[64,1024]{1,0:T(8,128)(2,1)S(1)}, bf16[64,1024]{1,0:T(8,128)(2,1)S(1)}, bf16[64,1024]{1,0:T(8,128)(2,1)S(1)}, bf16[64,1024]{1,0:T(8,128)(2,1)S(1)}, bf16[768,256]{1,0:T(8,128)(2,1)S(1)}) custom-call(s32[12]{0:T(128)S(1)} %copy-done.6, bf16[768,1024]{1,0:T(8,128)(2,1)S(1)} %copy-done, bf16[384,128]{1,0:T(8,128)(2,1)S(1)} %h_part.1.refs_0_, ...), custom_call_target="tpu_custom_call" | custom-call | flops 1 | bytes 1 | tf_op jit(solution)/shard_map/down_grad/pallas_call | solution.py:231
  74.3 0.9 collective-permute-start.13
  75.2 0.8 collective-permute-start.14
  76.0 1.1 %up_grad.1 = (bf16[64,512]{1,0:T(8,128)(2,1)S(1)}, bf16[64,512]{1,0:T(8,128)(2,1)S(1)}, bf16[64,512]{1,0:T(8,128)(2,1)S(1)}, bf16[64,512]{1,0:T(8,128)(2,1)S(1)}, bf16[768,256]{1,0:T(8,128)(2,1)S(1)}) custom-call(s32[12]{0:T(128)S(1)} %copy-done.6, bf16[768,512]{1,0:T(8,128)(2,1)S(1)} %copy-done.3, bf16[384,128]{1,0:T(8,128)(2,1)S(1)} %u_part.1.refs_0_, ...), custom_call_target="tpu_custom_call" | custom-call | flops 1 | bytes 1 | tf_op jit(solution)/shard_map/up_grad/pallas_call | solution.py:231
  77.1 3.9 %collective-permute-done.12.refs_1_ = bf16[64,1024]{1,0:T(8,128)(2,1)S(1)} collective-permute-done((bf16[64,1024]{1,0:T(8,128)(2,1)S(1)}, bf16[64,1024]{1,0:T(8,128)(2,1)S(1)}, u32[]{:S(2)}, u32[]{:S(2)}) %collective-permute-start.12) | collective-permute-done | bytes 131104 | tf_op jit(solution)/shard_map/ppermute | solution.py:32
  81.4 6.2 %collective-permute-done.13.refs_2_ = bf16[64,1024]{1,0:T(8,128)(2,1)S(1)} collective-permute-done((bf16[64,1024]{1,0:T(8,128)(2,1)S(1)}, bf16[64,1024]{1,0:T(8,128)(2,1)S(1)}, u32[]{:S(2)}, u32[]{:S(2)}) %collective-permute-start.13) | collective-permute-done | bytes 131104 | tf_op jit(solution)/shard_map/ppermute | solution.py:32
  88.4 4.3 %collective-permute-done.16.refs_6_ = bf16[64,512]{1,0:T(8,128)(2,1)S(1)} collective-permute-done((bf16[64,512]{1,0:T(8,128)(2,1)S(1)}, bf16[64,512]{1,0:T(8,128)(2,1)S(1)}, u32[]{:S(2)}, u32[]{:S(2)}) %collective-permute-start.16) | collective-permute-done | bytes 65568 | tf_op jit(solution)/shard_map/ppermute | solution.py:32
  92.7 1.0 collective-permute-done.17.refs_7_
  93.7 0.9 sites.1.refs_0_
  94.6 1.6 %y_own.1.refs_0_ = f32[768,512]{1,0:T(8,128)S(1)} custom-call(bf16[2048,512]{1,0:T(8,128)(2,1)S(1)} %copy-done.2, bf16[768,1024]{1,0:T(8,128)(2,1)S(1)} %copy-done, bf16[768,256]{1,0:T(8,128)(2,1)S(1)} %get-tuple-element.31.wide, bf16[64,512]{1,0:T(8,128)(2,1)S(1)} %get-tuple-element.32.refs_0_, bf16[64,512]{1,0:T(8,128)(2,1)S(1)} %collective-permute-done.4.refs_1_, ...), custom_call_target="tpu_custom_call" | custom-call | flops 1 | bytes 1 | tf_op jit(solution)/shard_map/y_own/pallas_call | solution.py:258
  96.3 0.9 gradients.1
  97.3 3.5 %back.1 = bf16[768,1024]{1,0:T(8,128)(2,1)} custom-call(bf16[2048,512]{1,0:T(8,128)(2,1)S(1)} %copy-done.2, bf16[768,512]{1,0:T(8,128)(2,1)S(1)} %copy-done.3, bf16[768,512]{1,0:T(8,128)(2,1)S(1)} %collective-permute-done.10.refs_2_, bf16[1024,512]{1,0:T(8,128)(2,1)S(1)} %get-tuple-element.38.refs_3_, bf16[768,256]{1,0:T(8,128)(2,1)S(1)} %get-tuple-element.39.refs_4_, ...), custom_call_target="tpu_custom_call" | custom-call | flops 1 | bytes 1 | tf_op jit(solution)/shard_map/back/pallas_call | solution.py:268
  100.8 1.5 %y_add.1 = bf16[768,512]{1,0:T(8,128)(2,1)} custom-call(f32[768,512]{1,0:T(8,128)S(1)} %y_own.1.refs_0_, bf16[768,512]{1,0:T(8,128)(2,1)S(1)} %collective-permute-done.9.refs_1_), custom_call_target="tpu_custom_call" | custom-call | flops 1 | bytes 1 | tf_op jit(solution)/shard_map/y_add/pallas_call | solution.py:293
  (33 shorter events, 4.3 us)
Async XLA Ops:
  0.6 35.4 %copy-start = (bf16[768,1024]{1,0:T(8,128)(2,1)S(1)}, bf16[768,1024]{1,0:T(8,128)(2,1)}, u32[]{:S(2)}) copy-start(bf16[768,1024]{1,0:T(8,128)(2,1)} %act.7) | copy-start | bytes 4718596
  0.6 1.7 %copy-start.1 = (bf16[2048,512]{1,0:T(8,128)(2,1)S(1)}, bf16[2048,512]{1,0:T(8,128)(2,1)}, u32[]{:S(2)}) copy-start(bf16[2048,512]{1,0:T(8,128)(2,1)} %refs_0_.1) | copy-start | bytes 6291460
  2.4 0.9 copy-start.4
  3.3 0.9 copy-start.5
  4.2 0.7 copy-start.7
  4.9 29.7 %copy-start.3 = (bf16[768,512]{1,0:T(8,128)(2,1)S(1)}, bf16[768,512]{1,0:T(8,128)(2,1)}, u32[]{:S(2)}) copy-start(bf16[768,512]{1,0:T(8,128)(2,1)} %refs_1_.1) | copy-start | bytes 2359300
  6.8 31.3 %copy-start.6 = (s32[12]{0:T(128)S(1)}, s32[12]{0:T(128)}, u32[]{:S(2)}) copy-start(s32[12]{0:T(128)} %owner.7) | copy-start | bytes 148
  6.8 14.9 %collective-permute-start.7 = (bf16[512,512]{1,0:T(8,128)(2,1)S(1)}, bf16[512,512]{1,0:T(8,128)(2,1)S(1)}, u32[]{:S(2)}, u32[]{:S(2)}) collective-permute-start(bf16[512,512]{1,0:T(8,128)(2,1)S(1)} %get-tuple-element.36), channel_id=1, source_target_pairs={{0,2},{2,0},{1,3},{3,1},{4,6},{6,4},{5,7},{7,5},{8,10},{10,8},{9,1... | collective-permute-start | bytes 1572872 | tf_op jit(solution)/shard_map/ppermute | solution.py:32
  21.7 12.8 %collective-permute-start.8 = (bf16[512,512]{1,0:T(8,128)(2,1)S(1)}, bf16[512,512]{1,0:T(8,128)(2,1)S(1)}, u32[]{:S(2)}, u32[]{:S(2)}) collective-permute-start(bf16[512,512]{1,0:T(8,128)(2,1)S(1)} %collective-permute-done.7.refs_0_), channel_id=1, source_target_pairs={{0,1},{1,0},{2,3},{3,2},{4,5},{5,4},{6,7},{7,6},{8,9},{9,8},{10,11... | collective-permute-start | bytes 1572872 | tf_op jit(solution)/shard_map/ppermute | solution.py:32
  21.7 6.7 %collective-permute-start.4 = (bf16[64,512]{1,0:T(8,128)(2,1)S(1)}, bf16[64,512]{1,0:T(8,128)(2,1)S(1)}, u32[]{:S(2)}, u32[]{:S(2)}) collective-permute-start(bf16[64,512]{1,0:T(8,128)(2,1)S(1)} %get-tuple-element.33), channel_id=1, source_target_pairs={{0,4},{4,8},{8,12},{12,0},{1,5},{5,9},{9,13},{13,1},{2,6},{6,10},{... | collective-permute-start | bytes 196616 | tf_op jit(solution)/shard_map/ppermute | solution.py:32
  23.5 7.7 %collective-permute-start.5 = (bf16[64,512]{1,0:T(8,128)(2,1)S(1)}, bf16[64,512]{1,0:T(8,128)(2,1)S(1)}, u32[]{:S(2)}, u32[]{:S(2)}) collective-permute-start(bf16[64,512]{1,0:T(8,128)(2,1)S(1)} %get-tuple-element.34), channel_id=1, source_target_pairs={{0,8},{4,12},{8,0},{12,4},{1,9},{5,13},{9,1},{13,5},{2,10},{6,14},... | collective-permute-start | bytes 196616 | tf_op jit(solution)/shard_map/ppermute | solution.py:32
  26.1 11.4 %collective-permute-start.6 = (bf16[64,512]{1,0:T(8,128)(2,1)S(1)}, bf16[64,512]{1,0:T(8,128)(2,1)S(1)}, u32[]{:S(2)}, u32[]{:S(2)}) collective-permute-start(bf16[64,512]{1,0:T(8,128)(2,1)S(1)} %get-tuple-element.35), channel_id=1, source_target_pairs={{0,12},{4,0},{8,4},{12,8},{1,13},{5,1},{9,5},{13,9},{2,14},{6,2},{... | collective-permute-start | bytes 196616 | tf_op jit(solution)/shard_map/ppermute | solution.py:32
  27.5 11.7 %collective-permute-start = (bf16[64,1024]{1,0:T(8,128)(2,1)S(1)}, bf16[64,1024]{1,0:T(8,128)(2,1)S(1)}, u32[]{:S(2)}, u32[]{:S(2)}) collective-permute-start(bf16[64,1024]{1,0:T(8,128)(2,1)S(1)} %get-tuple-element.28), channel_id=1, source_target_pairs={{0,4},{4,8},{8,12},{12,0},{1,5},{5,9},{9,13},{13,1},{2,6},{6,10},{... | collective-permute-start | bytes 393224 | tf_op jit(solution)/shard_map/ppermute | solution.py:32
  28.4 12.6 %collective-permute-start.1 = (bf16[64,1024]{1,0:T(8,128)(2,1)S(1)}, bf16[64,1024]{1,0:T(8,128)(2,1)S(1)}, u32[]{:S(2)}, u32[]{:S(2)}) collective-permute-start(bf16[64,1024]{1,0:T(8,128)(2,1)S(1)} %get-tuple-element.29), channel_id=1, source_target_pairs={{0,8},{4,12},{8,0},{12,4},{1,9},{5,13},{9,1},{13,5},{2,10},{6,14},... | collective-permute-start | bytes 393224 | tf_op jit(solution)/shard_map/ppermute | solution.py:32
  31.2 9.8 %collective-permute-start.2 = (bf16[64,1024]{1,0:T(8,128)(2,1)S(1)}, bf16[64,1024]{1,0:T(8,128)(2,1)S(1)}, u32[]{:S(2)}, u32[]{:S(2)}) collective-permute-start(bf16[64,1024]{1,0:T(8,128)(2,1)S(1)} %get-tuple-element.30), channel_id=1, source_target_pairs={{0,12},{4,0},{8,4},{12,8},{1,13},{5,1},{9,5},{13,9},{2,14},{6,2},{... | collective-permute-start | bytes 393224 | tf_op jit(solution)/shard_map/ppermute | solution.py:32
  34.5 62.7 %collective-permute-start.10 = (bf16[768,512]{1,0:T(8,128)(2,1)S(1)}, bf16[768,512]{1,0:T(8,128)(2,1)S(1)}, u32[]{:S(2)}, u32[]{:S(2)}) collective-permute-start(bf16[768,512]{1,0:T(8,128)(2,1)S(1)} %copy-done.3), channel_id=1, source_target_pairs={{0,2},{2,0},{1,3},{3,1},{4,6},{6,4},{5,7},{7,5},{8,10},{10,8},{9,1... | collective-permute-start | bytes 2359304 | tf_op jit(solution)/shard_map/ppermute | solution.py:32
  37.5 63.3 %collective-permute-start.9 = (bf16[768,512]{1,0:T(8,128)(2,1)S(1)}, bf16[768,512]{1,0:T(8,128)(2,1)S(1)}, u32[]{:S(2)}, u32[]{:S(2)}) collective-permute-start(bf16[768,512]{1,0:T(8,128)(2,1)S(1)} %get-tuple-element.37), channel_id=1, source_target_pairs={{0,2},{2,0},{1,3},{3,1},{4,6},{6,4},{5,7},{7,5},{8,10},{10,8},{9,1... | collective-permute-start | bytes 2359304 | tf_op jit(solution)/shard_map/ppermute | solution.py:32
  39.2 33.4 %collective-permute-start.11 = (bf16[384,128]{1,0:T(8,128)(2,1)S(1)}, bf16[384,128]{1,0:T(8,128)(2,1)S(1)}, u32[]{:S(2)}, u32[]{:S(2)}) collective-permute-start(bf16[384,128]{1,0:T(8,128)(2,1)S(1)} %h_part.1.refs_0_), channel_id=1, source_target_pairs={{0,2},{2,0},{1,3},{3,1},{4,6},{6,4},{5,7},{7,5},{8,10},{10,8},{9,1... | collective-permute-start | bytes 294920 | tf_op jit(solution)/shard_map/ppermute | solution.py:32
  42.3 52.3 %copy-start.2 = (bf16[2048,512]{1,0:T(8,128)(2,1)S(1)}, bf16[2048,512]{1,0:T(8,128)(2,1)}, u32[]{:S(2)}) copy-start(bf16[2048,512]{1,0:T(8,128)(2,1)} %refs_0_.1) | copy-start | bytes 6291460
  42.3 32.9 %collective-permute-start.3 = (bf16[384,128]{1,0:T(8,128)(2,1)S(1)}, bf16[384,128]{1,0:T(8,128)(2,1)S(1)}, u32[]{:S(2)}, u32[]{:S(2)}) collective-permute-start(bf16[384,128]{1,0:T(8,128)(2,1)S(1)} %u_part.1.refs_0_), channel_id=1, source_target_pairs={{0,2},{2,0},{1,3},{3,1},{4,6},{6,4},{5,7},{7,5},{8,10},{10,8},{9,1... | collective-permute-start | bytes 294920 | tf_op jit(solution)/shard_map/ppermute | solution.py:32
  73.9 7.1 %collective-permute-start.12 = (bf16[64,1024]{1,0:T(8,128)(2,1)S(1)}, bf16[64,1024]{1,0:T(8,128)(2,1)S(1)}, u32[]{:S(2)}, u32[]{:S(2)}) collective-permute-start(bf16[64,1024]{1,0:T(8,128)(2,1)S(1)} %get-tuple-element.41), channel_id=1, source_target_pairs={{0,12},{4,0},{8,4},{12,8},{1,13},{5,1},{9,5},{13,9},{2,14},{6,2},{... | collective-permute-start | bytes 393224 | tf_op jit(solution)/shard_map/ppermute | solution.py:32
  74.3 13.2 %collective-permute-start.13 = (bf16[64,1024]{1,0:T(8,128)(2,1)S(1)}, bf16[64,1024]{1,0:T(8,128)(2,1)S(1)}, u32[]{:S(2)}, u32[]{:S(2)}) collective-permute-start(bf16[64,1024]{1,0:T(8,128)(2,1)S(1)} %get-tuple-element.42), channel_id=1, source_target_pairs={{0,8},{4,12},{8,0},{12,4},{1,9},{5,13},{9,1},{13,5},{2,10},{6,14},... | collective-permute-start | bytes 393224 | tf_op jit(solution)/shard_map/ppermute | solution.py:32
  75.2 12.4 %collective-permute-start.14 = (bf16[64,1024]{1,0:T(8,128)(2,1)S(1)}, bf16[64,1024]{1,0:T(8,128)(2,1)S(1)}, u32[]{:S(2)}, u32[]{:S(2)}) collective-permute-start(bf16[64,1024]{1,0:T(8,128)(2,1)S(1)} %get-tuple-element.43), channel_id=1, source_target_pairs={{0,4},{4,8},{8,12},{12,0},{1,5},{5,9},{9,13},{13,1},{2,6},{6,10},{... | collective-permute-start | bytes 393224 | tf_op jit(solution)/shard_map/ppermute | solution.py:32
  81.1 7.3 %collective-permute-start.15 = (bf16[64,512]{1,0:T(8,128)(2,1)S(1)}, bf16[64,512]{1,0:T(8,128)(2,1)S(1)}, u32[]{:S(2)}, u32[]{:S(2)}) collective-permute-start(bf16[64,512]{1,0:T(8,128)(2,1)S(1)} %get-tuple-element.45), channel_id=1, source_target_pairs={{0,12},{4,0},{8,4},{12,8},{1,13},{5,1},{9,5},{13,9},{2,14},{6,2},{... | collective-permute-start | bytes 196616 | tf_op jit(solution)/shard_map/ppermute | solution.py:32
  87.6 5.2 %collective-permute-start.16 = (bf16[64,512]{1,0:T(8,128)(2,1)S(1)}, bf16[64,512]{1,0:T(8,128)(2,1)S(1)}, u32[]{:S(2)}, u32[]{:S(2)}) collective-permute-start(bf16[64,512]{1,0:T(8,128)(2,1)S(1)} %get-tuple-element.46), channel_id=1, source_target_pairs={{0,8},{4,12},{8,0},{12,4},{1,9},{5,13},{9,1},{13,5},{2,10},{6,14},... | collective-permute-start | bytes 196616 | tf_op jit(solution)/shard_map/ppermute | solution.py:32
  87.6 6.1 %collective-permute-start.17 = (bf16[64,512]{1,0:T(8,128)(2,1)S(1)}, bf16[64,512]{1,0:T(8,128)(2,1)S(1)}, u32[]{:S(2)}, u32[]{:S(2)}) collective-permute-start(bf16[64,512]{1,0:T(8,128)(2,1)S(1)} %get-tuple-element.47), channel_id=1, source_target_pairs={{0,4},{4,8},{8,12},{12,0},{1,5},{5,9},{9,13},{13,1},{2,6},{6,10},{... | collective-permute-start | bytes 196616 | tf_op jit(solution)/shard_map/ppermute | solution.py:32
  94.6 1.8 %collective-permute-start.18 = (bf16[2,64,1536]{2,1,0:T(8,128)(2,1)S(1)}, bf16[2,64,1536]{2,1,0:T(8,128)(2,1)S(1)}, u32[]{:S(2)}, u32[]{:S(2)}) collective-permute-start(bf16[2,64,1536]{2,1,0:T(8,128)(2,1)S(1)} %sites.1.refs_0_), channel_id=1, source_target_pairs={{0,1},{1,0},{2,3},{3,2},{4,5},{5,4},{6,7},{7,6},{8,9},{9,8},{10,11... | collective-permute-start | bytes 1179656 | tf_op jit(solution)/shard_map/ppermute | solution.py:32

commit v3 on v1

v3 whole, which is shorter than its diff:
```python
import functools

import jax
import jax.numpy as jnp
from jax import lax
from jax.experimental import pallas as pl
from jax.experimental.pallas import tpu as pltpu
from jax.sharding import PartitionSpec as P

SCALE = 2.0
TILES = 3
UHCOST = 1
F32 = jnp.float32
BF16 = jnp.bfloat16
SMEM = pl.BlockSpec(memory_space=pltpu.SMEM)
VMEM = pl.BlockSpec(memory_space=pltpu.VMEM)
ANY = pl.BlockSpec(memory_space=pl.ANY)


def shape(*dims, dtype=BF16):
    return jax.ShapeDtypeStruct(dims, dtype)


def call(kernel, name, out_shape, in_specs, out_specs, scratch=(), grid=(), flops=1):
    return pl.pallas_call(
        kernel, name=name, out_shape=out_shape, grid=grid, in_specs=in_specs, out_specs=out_specs,
        scratch_shapes=scratch,
        compiler_params=pltpu.CompilerParams(vmem_limit_bytes=64 * 1024 * 1024),
        cost_estimate=pl.CostEstimate(flops=flops, bytes_accessed=1, transcendentals=0),
    )


def shift(value, axis, by):
    size = lax.axis_size(axis)
    return lax.ppermute(value, axis, [(i, (i + by) % size) for i in range(size)])


def after(value, *others):
    return lax.optimization_barrier((value, *others))[0]


def nn(a, b):
    return lax.dot_general(a, b, (((1,), (0,)), ((), ())), preferred_element_type=F32)


def nt(a, b):
    return lax.dot_general(a, b, (((1,), (1,)), ((), ())), preferred_element_type=F32)


def tn(a, b):
    return lax.dot_general(a, b, (((0,), (0,)), ((), ())), preferred_element_type=F32)


def run(copies):
    for copy in copies:
        copy.start()
    for copy in copies:
        copy.wait()


def wanted_site(table, n_dp, s):
    return table[0, lax.axis_index("pair"), lax.rem(lax.axis_index("dp") + s, n_dp)]


def slot_of(owner, b, n_dp):
    return lax.rem(lax.axis_index("dp") - owner[b] + n_dp, n_dp)


def first_kernel(n_mp, n_share, w, *refs):
    pieces, sem = refs[:-1], refs[-1]
    feat = w.shape[0] // n_mp
    part = feat // n_share
    place = lax.axis_index("groups") * lax.axis_size("pair") + lax.axis_index("pair")
    copies = []
    for s in range(1, n_mp):
        row = pl.multiple_of(lax.rem(lax.axis_index("mp") + s, n_mp) * feat + place * part, part)
        copies.append(pltpu.make_async_copy(w.at[pl.ds(row, part)], pieces[s - 1], sem.at[s - 1]))
    run(copies)


def pack_kernel(n_dp, table, down, up, _, *refs):
    maps, sem = refs[:n_dp], refs[-1]
    feat, cols = down.shape[2], up.shape[2]
    copies = []
    for s in range(n_dp):
        site = wanted_site(table, n_dp, s)
        copies.append(pltpu.make_async_copy(down.at[site], maps[s].at[:, pl.ds(0, feat)], sem.at[s]))
        copies.append(pltpu.make_async_copy(up.at[site], maps[s].at[:, pl.ds(feat, cols)], sem.at[n_dp + s]))
    run(copies)


def reduce_kernel(n_dp, owner, x, gy, *refs):
    maps, out, wide = refs[:n_dp], refs[n_dp], refs[n_dp + 1]
    rank = maps[0].shape[0]
    feat = x.shape[1]
    blocks = owner.shape[0]
    rows = x.shape[0] // blocks
    for s in range(n_dp):
        wide[s * rank:(s + 1) * rank, :] = maps[s][...]
    lane_slot = lax.broadcasted_iota(jnp.int32, (rows, n_dp * rank), 1) // rank
    full = nt(x[...], wide[:, :feat]), nt(gy[...], wide[:, feat:])
    for b in range(blocks):
        mine = lane_slot == slot_of(owner, b, n_dp)
        halves = []
        for one in full:
            kept = jnp.where(mine, one[b * rows:(b + 1) * rows], 0.0)
            total = kept[:, :rank]
            for s in range(1, n_dp):
                total = total + kept[:, s * rank:(s + 1) * rank]
            halves.append(total)
        out[b * rows:(b + 1) * rows, :] = jnp.concatenate(halves, axis=1).astype(BF16)


def send_kernel(n_groups, n_pair, feat, n_mp, _, x, *refs):
    n_other, n_share = n_mp - 1, n_groups * n_pair
    pieces, outs, rows = refs[:n_other * n_share], refs[-2 * n_other:-n_other], refs[-n_other:]
    part = feat // n_share

    @pl.when(pl.program_id(0) == 0)
    def _():
        for s in range(n_other):
            for k in range(n_share):
                group = lax.rem(lax.axis_index("groups") + n_groups - k // n_pair, n_groups)
                core = lax.rem(lax.axis_index("pair") + n_pair - k % n_pair, n_pair)
                at = pl.multiple_of((group * n_pair + core) * part, part)
                rows[s][pl.ds(at, part), :] = pieces[s * n_share + k][...]

    for s in range(n_other):
        outs[s][...] = nn(x[...], rows[s][...]).astype(BF16)


def grad_kernel(n_dp, n_mp, owner, _, x, gy, *refs):
    parts, grads, u_wide, h_wide = refs[:n_mp], refs[n_mp:n_mp + n_dp], refs[-2], refs[-1]
    rank = u_wide.shape[1] // n_dp
    feat = x.shape[1]
    blocks = owner.shape[0]
    rows = x.shape[0] // blocks
    total = parts[0][...].astype(F32)
    for part in parts[1:]:
        total = total + part[...].astype(F32)
    lane_slot = lax.broadcasted_iota(jnp.int32, (rows, n_dp * rank), 1) // rank
    for b in range(blocks):
        mine = lane_slot == slot_of(owner, b, n_dp)
        for k, wide in enumerate((u_wide, h_wide)):
            one = total[b * rows:(b + 1) * rows, k * rank:(k + 1) * rank]
            spread = jnp.concatenate([one] * n_dp, axis=1)
            wide[b * rows:(b + 1) * rows, :] = jnp.where(mine, spread, 0.0).astype(BF16)
    for wide, act, lo in ((h_wide, x, 0), (u_wide, gy, feat)):
        full = tn(wide[...], act[...])
        for s in range(n_dp):
            grads[s][:, lo:lo + full.shape[1]] = full[s * rank:(s + 1) * rank].astype(BF16)


def back_kernel(n_dp, n_mp, w, gy, wide, *refs):
    n_other = n_mp - 1
    gots, rows = refs[:n_other], refs[n_other:2 * n_other]
    maps, out, own, downs = refs[2 * n_other:-3], refs[-3], refs[-2], refs[-1]
    rank = maps[0].shape[0]
    feat = out.shape[1]

    @pl.when(pl.program_id(0) == 0)
    def _():
        own[...] = w[pl.ds(pl.multiple_of(lax.axis_index("mp") * feat, feat), feat), :]
        for s in range(n_dp):
            downs[s * rank:(s + 1) * rank, :] = maps[s][:, :feat]

    total = nt(gy[...], own[...]) + SCALE * nn(wide[...], downs[...])
    for got, row in zip(gots, rows):
        total = total + nt(got[...], row[...])
    out[...] = total.astype(BF16)


def own_kernel(n_dp, w, x, wide, *refs):
    maps, out, ups = refs[:n_dp], refs[n_dp], refs[n_dp + 1]
    rank = maps[0].shape[0]
    feat = x.shape[1]

    @pl.when(pl.program_id(0) == 0)
    def _():
        for s in range(n_dp):
            ups[s * rank:(s + 1) * rank, :] = maps[s][:, feat:]

    own = w[pl.ds(pl.multiple_of(lax.axis_index("mp") * feat, feat), feat), :]
    out[...] = nn(x[...], own) + SCALE * nn(wide[...], ups[...])


def add_kernel(*refs):
    total = refs[0][...]
    for ref in refs[1:-1]:
        total = total + ref[...].astype(F32)
    refs[-1][...] = total.astype(BF16)


def site_kernel(n_dp, table, _, *refs):
    grads, out = refs[:n_dp], refs[-1]
    for site in range(out.shape[0]):
        total = jnp.zeros(out.shape[1:], F32)
        for s in range(n_dp):
            use = wanted_site(table, n_dp, s) == site
            total = total + jnp.where(use, grads[s][...].astype(F32), 0.0)
        out[site] = total.astype(BF16)


def last_kernel(feat, *refs):
    parts, down, up = refs[:-2], refs[-2], refs[-1]
    total = parts[0][...].astype(F32)
    for part in parts[1:]:
        total = total + part[...].astype(F32)
    total = SCALE * total
    down[...] = total[:, :, :feat]
    up[...] = total[:, :, feat:]


def shards(x, w, down, up, gy, owner, table):
    tok, feat = x.shape
    cols = w.shape[1]
    sites, rank = up.shape[:2]
    n_groups, n_dp, n_mp, n_pair = (lax.axis_size(a) for a in ("groups", "dp", "mp", "pair"))
    n_other, n_share = n_mp - 1, n_groups * n_pair
    down = down.transpose(0, 2, 1)
    part = feat // n_share
    both = feat + cols
    tile = tok // TILES
    row_block = lambda width: pl.BlockSpec((tile, width), lambda i: (i, 0))
    whole = lambda *dims: pl.BlockSpec(dims, lambda i: (0,) * len(dims))

    pieces = call(
        functools.partial(first_kernel, n_mp, n_share), "first",
        [shape(part, cols)] * n_other, [ANY], [ANY] * n_other, [pltpu.SemaphoreType.DMA((n_other,))],
    )(w)
    maps = call(
        functools.partial(pack_kernel, n_dp), "pack",
        [shape(rank, both)] * n_dp, [SMEM, ANY, ANY, ANY], [ANY] * n_dp,
        [pltpu.SemaphoreType.DMA((2 * n_dp,))],
    )(table, down, up, pieces[0])
    maps = [maps[0]] + [shift(maps[s], "dp", s) for s in range(1, n_dp)]
    pieces = [shift(pieces[s - 1], "mp", s) for s in range(1, n_mp)]
    gy_got = [shift(after(gy, maps[0], *pieces), "mp", s) for s in range(1, n_mp)]
    pieces = [after(piece, maps[0]) for piece in pieces]
    parts = []
    for piece in pieces:
        for j in range(n_groups):
            one = shift(piece, "groups", j) if j else piece
            parts += [shift(one, "pair", q) if q else one for q in range(n_pair)]

    uh = call(
        functools.partial(reduce_kernel, n_dp), "uh",
        shape(tok, 2 * rank), [SMEM] + [VMEM] * (2 + n_dp), VMEM,
        [pltpu.VMEM((n_dp * rank, both), BF16)], flops=UHCOST,
    )(owner, x, gy, *maps)
    uhs = [uh] + [shift(uh, "mp", s) for s in range(1, n_mp)]

    *grads, u_wide, h_wide = call(
        functools.partial(grad_kernel, n_dp, n_mp), "grads",
        [shape(rank, both)] * n_dp + [shape(tok, n_dp * rank)] * 2,
        [SMEM, ANY] + [VMEM] * (2 + n_mp), [VMEM] * (n_dp + 2),
    )(owner, gy_got[0], x, gy, *uhs)
    grads = [grads[0]] + [shift(grads[s], "dp", n_dp - s) for s in range(1, n_dp)]

    sent = call(
        functools.partial(send_kernel, n_groups, n_pair, feat, n_mp), "y_send",
        [shape(tok, cols)] * n_other + [shape(feat, cols)] * n_other,
        [ANY, row_block(feat)] + [whole(part, cols)] * len(parts),
        [row_block(cols)] * n_other + [whole(feat, cols)] * n_other,
        grid=(TILES,),
    )(u_wide, x, *parts)
    w_rows = sent[n_other:]
    y_got = [shift(sent[s - 1], "mp", n_mp - s) for s in range(1, n_mp)]

    y_own = call(
        functools.partial(own_kernel, n_dp), "y_own",
        shape(tok, cols, dtype=F32),
        [whole(*w.shape), row_block(feat), row_block(n_dp * rank)] + [whole(rank, both)] * n_dp,
        row_block(cols), [pltpu.VMEM((n_dp * rank, cols), BF16)], grid=(TILES,),
    )(w, x, u_wide, *maps)

    back = call(
        functools.partial(back_kernel, n_dp, n_mp), "back",
        shape(tok, feat),
        [whole(*w.shape), row_block(cols), row_block(n_dp * rank)] + [row_block(cols)] * n_other
        + [whole(feat, cols)] * n_other + [whole(rank, both)] * n_dp,
        row_block(feat), [pltpu.VMEM((feat, cols), BF16), pltpu.VMEM((n_dp * rank, feat), BF16)], grid=(TILES,),
    )(w, gy, h_wide, *gy_got, *w_rows, *maps)

    summed = call(
        functools.partial(site_kernel, n_dp), "sites",
        shape(sites, rank, both), [SMEM, ANY] + [VMEM] * n_dp, VMEM,
    )(table, back, *grads)
    halves = [summed] + [shift(summed, "pair", q) for q in range(1, n_pair)]
    down_grad, up_grad = call(
        functools.partial(last_kernel, feat), "gradients",
        [shape(sites, rank, feat, dtype=F32), shape(sites, rank, cols, dtype=F32)],
        [VMEM] * n_pair, [VMEM] * 2,
    )(*halves)

    y = call(
        add_kernel, "y_add", shape(tok, cols), [row_block(cols)] * n_mp, row_block(cols), grid=(TILES,),
    )(y_own, *y_got)
    return y, back, down_grad.transpose(0, 2, 1), up_grad


def solution(mesh):
    rows = P(("groups", "dp", "pair"), "mp")
    in_specs = (
        rows,
        P(None, "mp"),
        P(("groups", "dp"), "mp", None),
        P(("groups", "dp"), None, "mp"),
        rows,
        P(("groups", "dp", "pair")),
        P(("groups", "dp"), None, None),
    )
    out_specs = (rows, rows, P(("groups", "dp"), "mp", None), P(("groups", "dp"), None, "mp"))
    return jax.shard_map(shards, mesh=mesh, in_specs=in_specs, out_specs=out_specs, check_vma=False)
```

time: 99.7 us -> 113 us (1.13)
  Pallas kernels: 0 us -> 65.4 us
  matrix products: 16.2 us -> 0 us
  local copies, waits for them, and re-layouts: 12.5 us -> 0 us
  waiting for transfers between devices: 37.5 us -> 26.4 us
  other arithmetic: 7.67 us -> 0 us
  between operations: 8.33 us -> 0.67 us
  starting transfers between devices: 16.8 us -> 20.4 us
    pallas_call x0 -> x10, Pallas kernels: none -> 65.4 us  [the longest x1 25.7 us: shards(): call(functools.partial(pack_kernel, n_dp), 'pack', [shape(rank, both)] *...]
    dot_general x10 -> x0, matrix products: 16.2 us -> none  [the longest x4 8.73 us: nt(): lax.dot_general(a, b, (((1,), (1,)), ((), ())), preferred_element_type=F32)]
    ppermute x12 -> x14, waiting for transfers between devices: 37.5 us -> 26.4 us  [shift(): lax.ppermute(value, axis, [(i, (i + by) % size) for i in range(size)])]
    ppermute x12 -> x14, starting transfers between devices: 16.8 us -> 20.4 us  [shift(): lax.ppermute(value, axis, [(i, (i + by) % size) for i in range(size)])]
    another operation x4 -> x0, local copies, waits for them, and re-layouts: 3.02 us -> none  [the longest x2 2.83 us: shards(): u_wide = jnp.tile(uh[:, :rank], (1, n_dp)) * hit]
    convert_element_type x9 -> x0, other arithmetic: 2.99 us -> none  [the longest x2 2.45 us: shards(): use = (mine == wanted[(me_dp + s) % n_dp]).astype(F32)]
    unnamed x25 -> x0, local copies, waits for them, and re-layouts: 2.88 us -> none
    dynamic_slice x2 -> x0, local copies, waits for them, and re-layouts: 2.31 us -> none  [the longest x1 1.49 us: shards(): wanted[(me_dp + s) % n_dp]]
  transfers between devices with their start and end apart: 12 -> 14, of which waited for: 6 -> 4; matrix products, arithmetic and copies ran while one was open for 32% -> 0% of each run, Pallas kernels for 0% -> 43%
where the time goes in v3:
time: 113 us
  Pallas kernels  65.4 us (58%)
  waiting for transfers between devices  26.4 us (23%)
  starting transfers between devices  20.4 us (18%)
    ppermute x14, waiting for transfers between devices, shift(): lax.ppermute(value, axis, [(i, (i + by) % size) for i in range(size)])  26.4 us
    pallas_call x1, Pallas kernels, shards(): call(functools.partial(pack_kernel, n_dp), 'pack', [shape(rank, both)] *...  25.7 us
    ppermute x14, starting transfers between devices, shift(): lax.ppermute(value, axis, [(i, (i + by) % size) for i in range(size)])  20.4 us
    pallas_call x1, Pallas kernels, shards(): call(functools.partial(first_kernel, n_mp, n_share), 'first', [shape(part...  9.07 us
    pallas_call x1, Pallas kernels, shards(): call(functools.partial(back_kernel, n_dp, n_mp), 'back', shape(tok, feat)...  6.23 us
    pallas_call x1, Pallas kernels, shards(): call(functools.partial(own_kernel, n_dp), 'y_own', shape(tok, cols, dtype...  5.08 us
    pallas_call x1, Pallas kernels, shards(): call(functools.partial(send_kernel, n_groups, n_pair, feat, n_mp), 'y_sen...  4.32 us
    pallas_call x1, Pallas kernels, shards(): call(functools.partial(grad_kernel, n_dp, n_mp), 'grads', [shape(rank, bo...  3.68 us
  transfers between devices with their start and end apart: 14, of which 4 were waited for; matrix products, arithmetic and copies ran while one was open for 0% of the time, Pallas kernels for 43%

profile of v3, /device:TPU:0, one launch (start us, length us, event | category | flops | bytes accessed | tf_op | source)
XLA Modules:
  0.0 112.8 jit_solution(8332578917401137008)
XLA Ops:
  0.6 9.1 %first.1._ = bf16[256,512]{1,0:T(8,128)(2,1)} custom-call(bf16[2048,512]{1,0:T(8,128)(2,1)} %w.5), custom_call_target="tpu_custom_call" | custom-call | flops 1 | bytes 1 | tf_op jit(solution)/shard_map/first/pallas_call | solution.py:227
  9.7 3.0 %collective-permute-start = (bf16[256,512]{1,0:T(8,128)(2,1)}, bf16[256,512]{1,0:T(8,128)(2,1)}, u32[]{:S(2)}, u32[]{:S(2)}) collective-permute-start(bf16[256,512]{1,0:T(8,128)(2,1)} %first.1._), channel_id=1, source_target_pairs={{0,2},{2,0},{1,3},{3,1},{4,6},{6,4},{5,7},{7,5},{8,10},{10,8},{9,1... | collective-permute-start | bytes 786440 | tf_op jit(solution)/shard_map/ppermute | solution.py:35
  12.7 25.7 %pack.1 = (bf16[64,1536]{1,0:T(8,128)(2,1)}, bf16[64,1536]{1,0:T(8,128)(2,1)}, bf16[64,1536]{1,0:T(8,128)(2,1)}, bf16[64,1536]{1,0:T(8,128)(2,1)}) custom-call(s32[1,2,4]{2,1,0:T(2,128)} %table.3, bf16[2,64,1024]{2,1,0:T(8,128)(2,1)} %bitcast.2, bf16[2,64,512]{2,1,0:T(8,128)(2,1)} %up.1, bf16[256,512]{1,0:T(8,128)(2,1)} %first.1._), custom_call_target="tpu_custom_call" | custom-call | flops 1 | bytes 1 | tf_op jit(solution)/shard_map/pack/pallas_call | solution.py:231
  38.4 0.0 collective-permute-done.refs_0_
  38.4 0.1 collective-permute-start.1
  38.5 2.0 %collective-permute-start.7 = (bf16[256,512]{1,0:T(8,128)(2,1)}, bf16[256,512]{1,0:T(8,128)(2,1)}, u32[]{:S(2)}, u32[]{:S(2)}) collective-permute-start(bf16[256,512]{1,0:T(8,128)(2,1)} %collective-permute-done.refs_0_), channel_id=1, source_target_pairs={{0,16},{16,0},{1,17},{17,1},{2,18},{18,2},{3,19},{19,3},{4,20},{20... | collective-permute-start | bytes 786440 | tf_op jit(solution)/shard_map/ppermute | solution.py:35
  40.5 1.6 %collective-permute-start.2 = (bf16[64,1536]{1,0:T(8,128)(2,1)}, bf16[64,1536]{1,0:T(8,128)(2,1)}, u32[]{:S(2)}, u32[]{:S(2)}) collective-permute-start(bf16[64,1536]{1,0:T(8,128)(2,1)} %get-tuple-element.22), channel_id=1, source_target_pairs={{0,4},{4,8},{8,12},{12,0},{1,5},{5,9},{9,13},{13,1},{2,6},{6,10},{... | collective-permute-start | bytes 589832 | tf_op jit(solution)/shard_map/ppermute | solution.py:35
  42.1 2.6 %collective-permute-start.3 = (bf16[64,1536]{1,0:T(8,128)(2,1)}, bf16[64,1536]{1,0:T(8,128)(2,1)}, u32[]{:S(2)}, u32[]{:S(2)}) collective-permute-start(bf16[64,1536]{1,0:T(8,128)(2,1)} %get-tuple-element.23), channel_id=1, source_target_pairs={{0,8},{4,12},{8,0},{12,4},{1,9},{5,13},{9,1},{13,5},{2,10},{6,14},... | collective-permute-start | bytes 589832 | tf_op jit(solution)/shard_map/ppermute | solution.py:35
  44.7 1.3 %collective-permute-start.4 = (bf16[64,1536]{1,0:T(8,128)(2,1)}, bf16[64,1536]{1,0:T(8,128)(2,1)}, u32[]{:S(2)}, u32[]{:S(2)}) collective-permute-start(bf16[64,1536]{1,0:T(8,128)(2,1)} %get-tuple-element.24), channel_id=1, source_target_pairs={{0,12},{4,0},{8,4},{12,8},{1,13},{5,1},{9,5},{13,9},{2,14},{6,2},{... | collective-permute-start | bytes 589832 | tf_op jit(solution)/shard_map/ppermute | solution.py:35
  46.1 4.5 %collective-permute-done.2.refs_1_.refs_3_ = bf16[64,1536]{1,0:T(8,128)(2,1)} collective-permute-done((bf16[64,1536]{1,0:T(8,128)(2,1)}, bf16[64,1536]{1,0:T(8,128)(2,1)}, u32[]{:S(2)}, u32[]{:S(2)}) %collective-permute-start.2) | collective-permute-done | bytes 196640 | tf_op jit(solution)/shard_map/ppermute | solution.py:35
  50.6 0.0 collective-permute-start.6
  50.6 0.0 collective-permute-done.7.refs_2_
  50.6 0.5 collective-permute-start.8
  51.1 5.9 %collective-permute-done.3.refs_2_.refs_4_ = bf16[64,1536]{1,0:T(8,128)(2,1)} collective-permute-done((bf16[64,1536]{1,0:T(8,128)(2,1)}, bf16[64,1536]{1,0:T(8,128)(2,1)}, u32[]{:S(2)}, u32[]{:S(2)}) %collective-permute-start.3) | collective-permute-done | bytes 196640 | tf_op jit(solution)/shard_map/ppermute | solution.py:35
  57.0 3.7 %uh.1.refs_0_ = bf16[768,128]{1,0:T(8,128)(2,1)} custom-call(s32[12]{0:T(128)} %owner.3, bf16[768,1024]{1,0:T(8,128)(2,1)} %x.7, bf16[768,512]{1,0:T(8,128)(2,1)} %gy.5, bf16[64,1536]{1,0:T(8,128)(2,1)} %get-tuple-element.20.refs_0_.refs_2_, bf16[64,1536]{1,0:T(8,128)(2,1)} %collective-permute-done.2.refs_1_.refs_3_, ...), custom_call_target="tpu_custom_call" | custom-call | flops 1 | bytes 1 | tf_op jit(solution)/shard_map/uh/pallas_call | solution.py:246
  60.7 1.5 %collective-permute-start.5 = (bf16[768,128]{1,0:T(8,128)(2,1)}, bf16[768,128]{1,0:T(8,128)(2,1)}, u32[]{:S(2)}, u32[]{:S(2)}) collective-permute-start(bf16[768,128]{1,0:T(8,128)(2,1)} %uh.1.refs_0_), channel_id=1, source_target_pairs={{0,2},{2,0},{1,3},{3,1},{4,6},{6,4},{5,7},{7,5},{8,10},{10,8},{9,1... | collective-permute-start | bytes 589832 | tf_op jit(solution)/shard_map/ppermute | solution.py:35
  62.2 5.6 %collective-permute-done.5.refs_1_ = bf16[768,128]{1,0:T(8,128)(2,1)} collective-permute-done((bf16[768,128]{1,0:T(8,128)(2,1)}, bf16[768,128]{1,0:T(8,128)(2,1)}, u32[]{:S(2)}, u32[]{:S(2)}) %collective-permute-start.5) | collective-permute-done | bytes 196640 | tf_op jit(solution)/shard_map/ppermute | solution.py:35
  67.8 3.7 %grads.1 = (bf16[64,1536]{1,0:T(8,128)(2,1)}, bf16[64,1536]{1,0:T(8,128)(2,1)}, bf16[64,1536]{1,0:T(8,128)(2,1)}, bf16[64,1536]{1,0:T(8,128)(2,1)}, bf16[768,256]{1,0:T(8,128)(2,1)}, /*index=5*/bf16[768,256]{1,0:T(8,128)(2,1)}) custom-call(s32[12]{0:T(128)} %owner.3, bf16[768,512]{1,0:T(8,128)(2,1)} %collective-permute-done.1._.refs_0_, ...), custom_call_target="tpu_custom_call" | custom-call | flops 1 | bytes 1 | tf_op jit(solution)/shard_map/grads/pallas_call | solution.py:253
  71.5 4.3 %y_send.1 = (bf16[768,512]{1,0:T(8,128)(2,1)}, bf16[1024,512]{1,0:T(8,128)(2,1)}) custom-call(bf16[768,256]{1,0:T(8,128)(2,1)} %get-tuple-element.25.wide._, bf16[768,1024]{1,0:T(8,128)(2,1)} %x.7, bf16[256,512]{1,0:T(8,128)(2,1)} %collective-permute-done.refs_0_, bf16[256,512]{1,0:T(8,128)(2,1)} %collective-permute-done.6.refs_1_, ...), custom_call_target="tpu_custom_call" | custom-call | flops 1 | bytes 1 | tf_op jit(solution)/shard_map/y_send/pallas_call | solution.py:260
  75.8 1.5 %collective-permute-start.9 = (bf16[768,512]{1,0:T(8,128)(2,1)}, bf16[768,512]{1,0:T(8,128)(2,1)}, u32[]{:S(2)}, u32[]{:S(2)}) collective-permute-start(bf16[768,512]{1,0:T(8,128)(2,1)} %get-tuple-element.27), channel_id=1, source_target_pairs={{0,2},{2,0},{1,3},{3,1},{4,6},{6,4},{5,7},{7,5},{8,10},{10,8},{9,1... | collective-permute-start | bytes 2359304 | tf_op jit(solution)/shard_map/ppermute | solution.py:35
  77.3 4.7 %collective-permute-start.10 = (bf16[64,1536]{1,0:T(8,128)(2,1)}, bf16[64,1536]{1,0:T(8,128)(2,1)}, u32[]{:S(2)}, u32[]{:S(2)}) collective-permute-start(bf16[64,1536]{1,0:T(8,128)(2,1)} %get-tuple-element.31), channel_id=1, source_target_pairs={{0,12},{4,0},{8,4},{12,8},{1,13},{5,1},{9,5},{13,9},{2,14},{6,2},{... | collective-permute-start | bytes 589832 | tf_op jit(solution)/shard_map/ppermute | solution.py:35
  82.0 1.5 %collective-permute-start.11 = (bf16[64,1536]{1,0:T(8,128)(2,1)}, bf16[64,1536]{1,0:T(8,128)(2,1)}, u32[]{:S(2)}, u32[]{:S(2)}) collective-permute-start(bf16[64,1536]{1,0:T(8,128)(2,1)} %get-tuple-element.32), channel_id=1, source_target_pairs={{0,8},{4,12},{8,0},{12,4},{1,9},{5,13},{9,1},{13,5},{2,10},{6,14},... | collective-permute-start | bytes 589832 | tf_op jit(solution)/shard_map/ppermute | solution.py:35
  83.5 6.2 %back.1._ = bf16[768,1024]{1,0:T(8,128)(2,1)} custom-call(bf16[2048,512]{1,0:T(8,128)(2,1)} %w.5, bf16[768,512]{1,0:T(8,128)(2,1)} %gy.5, bf16[768,256]{1,0:T(8,128)(2,1)} %get-tuple-element.28.wide, bf16[768,512]{1,0:T(8,128)(2,1)} %collective-permute-done.1._.refs_0_, bf16[1024,512]{1,0:T(8,128)(2,1)} %get-tuple-element.29.refs_1_, ...), custom_call_target="tpu_custom_call" | custom-call | flops 1 | bytes 1 | tf_op jit(solution)/shard_map/back/pallas_call | solution.py:277
  89.7 0.0 collective-permute-done.10.refs_1_
  89.7 10.4 %collective-permute-done.11.refs_2_ = bf16[64,1536]{1,0:T(8,128)(2,1)} collective-permute-done((bf16[64,1536]{1,0:T(8,128)(2,1)}, bf16[64,1536]{1,0:T(8,128)(2,1)}, u32[]{:S(2)}, u32[]{:S(2)}) %collective-permute-start.11) | collective-permute-done | bytes 196640 | tf_op jit(solution)/shard_map/ppermute | solution.py:35
  100.1 0.0 collective-permute-done.12.refs_3_
  100.1 2.3 %sites.1.refs_0_ = bf16[2,64,1536]{2,1,0:T(8,128)(2,1)} custom-call(s32[1,2,4]{2,1,0:T(2,128)} %table.3, bf16[768,1024]{1,0:T(8,128)(2,1)} %back.1._, bf16[64,1536]{1,0:T(8,128)(2,1)} %get-tuple-element.30.refs_0_, bf16[64,1536]{1,0:T(8,128)(2,1)} %collective-permute-done.10.refs_1_, bf16[64,1536]{1,0:T(8,128)(2,1)} %collective-permute-done.11.refs_2_, ...), custom_call_target="tpu_custom_call" | custom-call | flops 1 | bytes 1 | tf_op jit(solution)/shard_map/sites/pallas_call | solution.py:285
  102.4 0.0 collective-permute-start.13
  102.4 5.1 %y_own.1.refs_0_ = f32[768,512]{1,0:T(8,128)} custom-call(bf16[2048,512]{1,0:T(8,128)(2,1)} %w.5, bf16[768,1024]{1,0:T(8,128)(2,1)} %x.7, bf16[768,256]{1,0:T(8,128)(2,1)} %get-tuple-element.25.wide._, bf16[64,1536]{1,0:T(8,128)(2,1)} %get-tuple-element.20.refs_0_.refs_2_, bf16[64,1536]{1,0:T(8,128)(2,1)} %collective-permute-done.2.refs_1_.refs_3_, ...), custom_call_target="tpu_custom_call" | custom-call | flops 1 | bytes 1 | tf_op jit(solution)/shard_map/y_own/pallas_call | solution.py:270
  107.5 0.0 collective-permute-done.13.refs_1_
  107.5 2.1 %gradients.1 = (f32[2,64,1024]{2,1,0:T(8,128)}, f32[2,64,512]{2,1,0:T(8,128)}) custom-call(bf16[2,64,1536]{2,1,0:T(8,128)(2,1)} %sites.1.refs_0_, bf16[2,64,1536]{2,1,0:T(8,128)(2,1)} %collective-permute-done.13.refs_1_), custom_call_target="tpu_custom_call" | custom-call | flops 1 | bytes 1 | tf_op jit(solution)/shard_map/gradients/pallas_call | solution.py:290
  109.6 3.3 %y_add.1 = bf16[768,512]{1,0:T(8,128)(2,1)} custom-call(f32[768,512]{1,0:T(8,128)} %y_own.1.refs_0_, bf16[768,512]{1,0:T(8,128)(2,1)} %collective-permute-done.9.refs_1_), custom_call_target="tpu_custom_call" | custom-call | flops 1 | bytes 1 | tf_op jit(solution)/shard_map/y_add/pallas_call | solution.py:296
  (6 shorter events, 0.0 us)
Async XLA Ops:
  9.7 28.7 %collective-permute-start = (bf16[256,512]{1,0:T(8,128)(2,1)}, bf16[256,512]{1,0:T(8,128)(2,1)}, u32[]{:S(2)}, u32[]{:S(2)}) collective-permute-start(bf16[256,512]{1,0:T(8,128)(2,1)} %first.1._), channel_id=1, source_target_pairs={{0,2},{2,0},{1,3},{3,1},{4,6},{6,4},{5,7},{7,5},{8,10},{10,8},{9,1... | collective-permute-start | bytes 786440 | tf_op jit(solution)/shard_map/ppermute | solution.py:35
  38.4 29.3 %collective-permute-start.1 = (bf16[768,512]{1,0:T(8,128)(2,1)}, bf16[768,512]{1,0:T(8,128)(2,1)}, u32[]{:S(2)}, u32[]{:S(2)}) collective-permute-start(bf16[768,512]{1,0:T(8,128)(2,1)} %gy.5), channel_id=1, source_target_pairs={{0,2},{2,0},{1,3},{3,1},{4,6},{6,4},{5,7},{7,5},{8,10},{10,8},{9,1... | collective-permute-start | bytes 2359304 | tf_op jit(solution)/shard_map/ppermute | solution.py:35
  38.5 12.1 %collective-permute-start.7 = (bf16[256,512]{1,0:T(8,128)(2,1)}, bf16[256,512]{1,0:T(8,128)(2,1)}, u32[]{:S(2)}, u32[]{:S(2)}) collective-permute-start(bf16[256,512]{1,0:T(8,128)(2,1)} %collective-permute-done.refs_0_), channel_id=1, source_target_pairs={{0,16},{16,0},{1,17},{17,1},{2,18},{18,2},{3,19},{19,3},{4,20},{20... | collective-permute-start | bytes 786440 | tf_op jit(solution)/shard_map/ppermute | solution.py:35
  40.5 10.0 %collective-permute-start.2 = (bf16[64,1536]{1,0:T(8,128)(2,1)}, bf16[64,1536]{1,0:T(8,128)(2,1)}, u32[]{:S(2)}, u32[]{:S(2)}) collective-permute-start(bf16[64,1536]{1,0:T(8,128)(2,1)} %get-tuple-element.22), channel_id=1, source_target_pairs={{0,4},{4,8},{8,12},{12,0},{1,5},{5,9},{9,13},{13,1},{2,6},{6,10},{... | collective-permute-start | bytes 589832 | tf_op jit(solution)/shard_map/ppermute | solution.py:35
  42.1 14.9 %collective-permute-start.3 = (bf16[64,1536]{1,0:T(8,128)(2,1)}, bf16[64,1536]{1,0:T(8,128)(2,1)}, u32[]{:S(2)}, u32[]{:S(2)}) collective-permute-start(bf16[64,1536]{1,0:T(8,128)(2,1)} %get-tuple-element.23), channel_id=1, source_target_pairs={{0,8},{4,12},{8,0},{12,4},{1,9},{5,13},{9,1},{13,5},{2,10},{6,14},... | collective-permute-start | bytes 589832 | tf_op jit(solution)/shard_map/ppermute | solution.py:35
  44.7 12.3 %collective-permute-start.4 = (bf16[64,1536]{1,0:T(8,128)(2,1)}, bf16[64,1536]{1,0:T(8,128)(2,1)}, u32[]{:S(2)}, u32[]{:S(2)}) collective-permute-start(bf16[64,1536]{1,0:T(8,128)(2,1)} %get-tuple-element.24), channel_id=1, source_target_pairs={{0,12},{4,0},{8,4},{12,8},{1,13},{5,1},{9,5},{13,9},{2,14},{6,2},{... | collective-permute-start | bytes 589832 | tf_op jit(solution)/shard_map/ppermute | solution.py:35
  50.6 20.9 %collective-permute-start.6 = (bf16[256,512]{1,0:T(8,128)(2,1)}, bf16[256,512]{1,0:T(8,128)(2,1)}, u32[]{:S(2)}, u32[]{:S(2)}) collective-permute-start(bf16[256,512]{1,0:T(8,128)(2,1)} %collective-permute-done.refs_0_), channel_id=1, source_target_pairs={{0,1},{1,0},{2,3},{3,2},{4,5},{5,4},{6,7},{7,6},{8,9},{9,8},{10,11... | collective-permute-start | bytes 786440 | tf_op jit(solution)/shard_map/ppermute | solution.py:35
  50.6 20.9 %collective-permute-start.8 = (bf16[256,512]{1,0:T(8,128)(2,1)}, bf16[256,512]{1,0:T(8,128)(2,1)}, u32[]{:S(2)}, u32[]{:S(2)}) collective-permute-start(bf16[256,512]{1,0:T(8,128)(2,1)} %collective-permute-done.7.refs_2_), channel_id=1, source_target_pairs={{0,1},{1,0},{2,3},{3,2},{4,5},{5,4},{6,7},{7,6},{8,9},{9,8},{10,11... | collective-permute-start | bytes 786440 | tf_op jit(solution)/shard_map/ppermute | solution.py:35
  60.7 7.0 %collective-permute-start.5 = (bf16[768,128]{1,0:T(8,128)(2,1)}, bf16[768,128]{1,0:T(8,128)(2,1)}, u32[]{:S(2)}, u32[]{:S(2)}) collective-permute-start(bf16[768,128]{1,0:T(8,128)(2,1)} %uh.1.refs_0_), channel_id=1, source_target_pairs={{0,2},{2,0},{1,3},{3,1},{4,6},{6,4},{5,7},{7,5},{8,10},{10,8},{9,1... | collective-permute-start | bytes 589832 | tf_op jit(solution)/shard_map/ppermute | solution.py:35
  75.8 33.8 %collective-permute-start.9 = (bf16[768,512]{1,0:T(8,128)(2,1)}, bf16[768,512]{1,0:T(8,128)(2,1)}, u32[]{:S(2)}, u32[]{:S(2)}) collective-permute-start(bf16[768,512]{1,0:T(8,128)(2,1)} %get-tuple-element.27), channel_id=1, source_target_pairs={{0,2},{2,0},{1,3},{3,1},{4,6},{6,4},{5,7},{7,5},{8,10},{10,8},{9,1... | collective-permute-start | bytes 2359304 | tf_op jit(solution)/shard_map/ppermute | solution.py:35
  77.3 12.5 %collective-permute-start.10 = (bf16[64,1536]{1,0:T(8,128)(2,1)}, bf16[64,1536]{1,0:T(8,128)(2,1)}, u32[]{:S(2)}, u32[]{:S(2)}) collective-permute-start(bf16[64,1536]{1,0:T(8,128)(2,1)} %get-tuple-element.31), channel_id=1, source_target_pairs={{0,12},{4,0},{8,4},{12,8},{1,13},{5,1},{9,5},{13,9},{2,14},{6,2},{... | collective-permute-start | bytes 589832 | tf_op jit(solution)/shard_map/ppermute | solution.py:35
  82.0 18.2 %collective-permute-start.11 = (bf16[64,1536]{1,0:T(8,128)(2,1)}, bf16[64,1536]{1,0:T(8,128)(2,1)}, u32[]{:S(2)}, u32[]{:S(2)}) collective-permute-start(bf16[64,1536]{1,0:T(8,128)(2,1)} %get-tuple-element.32), channel_id=1, source_target_pairs={{0,8},{4,12},{8,0},{12,4},{1,9},{5,13},{9,1},{13,5},{2,10},{6,14},... | collective-permute-start | bytes 589832 | tf_op jit(solution)/shard_map/ppermute | solution.py:35
  83.5 16.6 %collective-permute-start.12 = (bf16[64,1536]{1,0:T(8,128)(2,1)}, bf16[64,1536]{1,0:T(8,128)(2,1)}, u32[]{:S(2)}, u32[]{:S(2)}) collective-permute-start(bf16[64,1536]{1,0:T(8,128)(2,1)} %get-tuple-element.33), channel_id=1, source_target_pairs={{0,4},{4,8},{8,12},{12,0},{1,5},{5,9},{9,13},{13,1},{2,6},{6,10},{... | collective-permute-start | bytes 589832 | tf_op jit(solution)/shard_map/ppermute | solution.py:35
  102.4 5.1 %collective-permute-start.13 = (bf16[2,64,1536]{2,1,0:T(8,128)(2,1)}, bf16[2,64,1536]{2,1,0:T(8,128)(2,1)}, u32[]{:S(2)}, u32[]{:S(2)}) collective-permute-start(bf16[2,64,1536]{2,1,0:T(8,128)(2,1)} %sites.1.refs_0_), channel_id=1, source_target_pairs={{0,1},{1,0},{2,3},{3,2},{4,5},{5,4},{6,7},{7,6},{8,9},{9,8},{10,11... | collective-permute-start | bytes 1179656 | tf_op jit(solution)/shard_map/ppermute | solution.py:35

commit v4 on v2

v4 whole, which is shorter than its diff:
```python
import functools

import jax
import jax.numpy as jnp
from jax import lax
from jax.experimental import pallas as pl
from jax.experimental.pallas import tpu as pltpu
from jax.sharding import PartitionSpec as P

SCALE = 2.0
TILES = 3
GRAD_COST = 15_000_000_000
F32 = jnp.float32
BF16 = jnp.bfloat16
SMEM = pl.BlockSpec(memory_space=pltpu.SMEM)
VMEM = pl.BlockSpec(memory_space=pltpu.VMEM)
ANY = pl.BlockSpec(memory_space=pl.ANY)


def shape(*dims, dtype=BF16):
    return jax.ShapeDtypeStruct(dims, dtype)


def call(kernel, name, out_shape, in_specs, out_specs, scratch=(), grid=(), mib=32, flops=1):
    return pl.pallas_call(
        kernel, name=name, out_shape=out_shape, grid=grid, in_specs=in_specs, out_specs=out_specs,
        scratch_shapes=scratch,
        compiler_params=pltpu.CompilerParams(vmem_limit_bytes=mib * 1024 * 1024),
        cost_estimate=pl.CostEstimate(flops=flops, bytes_accessed=1, transcendentals=0),
    )


def shift(value, axis, by):
    size = lax.axis_size(axis)
    return lax.ppermute(value, axis, [(i, (i + by) % size) for i in range(size)])


def after(value, *others):
    return lax.optimization_barrier((value, *others))[0]


def nn(a, b):
    return lax.dot_general(a, b, (((1,), (0,)), ((), ())), preferred_element_type=F32)


def nt(a, b):
    return lax.dot_general(a, b, (((1,), (1,)), ((), ())), preferred_element_type=F32)


def tn(a, b):
    return lax.dot_general(a, b, (((0,), (0,)), ((), ())), preferred_element_type=F32)


def run(copies):
    for copy in copies:
        copy.start()
    for copy in copies:
        copy.wait()


def wanted_site(table, n_dp, s):
    return table[0, lax.axis_index("pair"), lax.rem(lax.axis_index("dp") + s, n_dp)]


def slot_of(owner, b, n_dp):
    return lax.rem(lax.axis_index("dp") - owner[b] + n_dp, n_dp)


def pack_kernel(n_dp, n_mp, n_pair, table, down, up, w, *refs):
    ups, downs, pieces, sem = refs[:n_dp], refs[n_dp:2 * n_dp], refs[2 * n_dp:-1], refs[-1]
    feat = w.shape[0] // n_mp
    part = feat // n_pair
    copies = []
    for s in range(n_dp):
        site = wanted_site(table, n_dp, s)
        copies.append(pltpu.make_async_copy(up.at[site], ups[s], sem.at[s]))
        copies.append(pltpu.make_async_copy(down.at[site], downs[s], sem.at[n_dp + s]))
    for s in range(1, n_mp):
        row = lax.rem(lax.axis_index("mp") + s, n_mp) * feat + lax.axis_index("pair") * part
        row = pl.multiple_of(row, part)
        copies.append(pltpu.make_async_copy(w.at[pl.ds(row, part)], pieces[s - 1], sem.at[2 * n_dp + s - 1]))
    run(copies)


def reduce_kernel(n_dp, owner, act, _, *refs):
    maps, out, wide = refs[:n_dp], refs[n_dp], refs[n_dp + 1]
    rank = maps[0].shape[0]
    blocks = owner.shape[0]
    rows = act.shape[0] // blocks
    for s in range(n_dp):
        wide[s * rank:(s + 1) * rank, :] = maps[s][...]
    full = nt(act[...], wide[...])
    lane_slot = lax.broadcasted_iota(jnp.int32, (rows, n_dp * rank), 1) // rank
    folded = []
    for b in range(blocks):
        kept = jnp.where(lane_slot == slot_of(owner, b, n_dp), full[b * rows:(b + 1) * rows], 0.0)
        total = kept[:, :rank]
        for s in range(1, n_dp):
            total = total + kept[:, s * rank:(s + 1) * rank]
        folded.append(total)
    for j in range(blocks // 2):
        pair = jnp.concatenate([folded[2 * j], folded[2 * j + 1]], axis=1)
        out[j * rows:(j + 1) * rows, :] = pair.astype(BF16)


def grad_kernel(n_dp, n_part, n_behind, owner, act, *refs):
    refs = refs[n_behind:]
    parts, grads, wide = refs[:n_part], refs[n_part:n_part + n_dp], refs[n_part + n_dp]
    rank = wide.shape[1] // n_dp
    blocks = owner.shape[0]
    rows = act.shape[0] // blocks
    total = parts[0][...].astype(F32)
    for part in parts[1:]:
        total = total + part[...].astype(F32)
    lane_slot = lax.broadcasted_iota(jnp.int32, (rows, n_dp * rank), 1) // rank
    for b in range(blocks):
        one = total[(b // 2) * rows:(b // 2 + 1) * rows, (b % 2) * rank:(b % 2 + 1) * rank]
        spread = jnp.concatenate([one] * n_dp, axis=1)
        kept = jnp.where(lane_slot == slot_of(owner, b, n_dp), spread, 0.0)
        wide[b * rows:(b + 1) * rows, :] = kept.astype(BF16)
    full = tn(wide[...], act[...])
    for s in range(n_dp):
        grads[s][...] = full[s * rank:(s + 1) * rank].astype(BF16)


def send_kernel(n_pair, feat, n_mp, _, __, x, *refs):
    n_other = n_mp - 1
    pieces, outs, rows = refs[:n_other * n_pair], refs[n_other * n_pair:n_other * n_pair + n_other], refs[-n_other:]
    part = feat // n_pair

    @pl.when(pl.program_id(0) == 0)
    def _():
        for s in range(n_other):
            for q in range(n_pair):
                at = lax.rem(lax.axis_index("pair") + n_pair - q, n_pair) * part
                rows[s][pl.ds(pl.multiple_of(at, part), part), :] = pieces[s * n_pair + q][...]

    for s in range(n_other):
        outs[s][...] = nn(x[...], rows[s][...]).astype(BF16)


def back_kernel(n_dp, n_mp, _, *refs):
    w, gys, rows, wide, downs, out, own, maps = (
        refs[0], refs[1:1 + n_mp], refs[1 + n_mp:2 * n_mp], refs[2 * n_mp],
        refs[2 * n_mp + 1:-3], refs[-3], refs[-2], refs[-1],
    )
    rank, feat = downs[0].shape

    @pl.when(pl.program_id(0) == 0)
    def _():
        own[...] = w[pl.ds(pl.multiple_of(lax.axis_index("mp") * feat, feat), feat), :]
        for s in range(n_dp):
            maps[s * rank:(s + 1) * rank, :] = downs[s][...]

    total = nt(gys[0][...], own[...]) + SCALE * nn(wide[...], maps[...])
    for gy, row in zip(gys[1:], rows):
        total = total + nt(gy[...], row[...])
    out[...] = total.astype(BF16)


def own_kernel(n_dp, w, x, wide, *refs):
    ups, out, maps = refs[:n_dp], refs[n_dp], refs[n_dp + 1]
    rank = ups[0].shape[0]
    feat = x.shape[1]

    @pl.when(pl.program_id(0) == 0)
    def _():
        for s in range(n_dp):
            maps[s * rank:(s + 1) * rank, :] = ups[s][...]

    own = w[pl.ds(pl.multiple_of(lax.axis_index("mp") * feat, feat), feat), :]
    out[...] = nn(x[...], own) + SCALE * nn(wide[...], maps[...])


def add_kernel(*refs):
    total = refs[0][...]
    for ref in refs[1:-1]:
        total = total + ref[...].astype(F32)
    refs[-1][...] = total.astype(BF16)


def site_kernel(n_dp, feat, table, *refs):
    downs, ups, out = refs[:n_dp], refs[n_dp:2 * n_dp], refs[-1]
    for site in range(out.shape[0]):
        for grads, lo, hi in ((downs, 0, feat), (ups, feat, out.shape[2])):
            total = jnp.zeros((out.shape[1], hi - lo), F32)
            for s in range(n_dp):
                use = wanted_site(table, n_dp, s) == site
                total = total + jnp.where(use, grads[s][...].astype(F32), 0.0)
            out[site, :, lo:hi] = total.astype(BF16)


def last_kernel(feat, *refs):
    parts, down, up = refs[:-2], refs[-2], refs[-1]
    total = parts[0][...].astype(F32)
    for part in parts[1:]:
        total = total + part[...].astype(F32)
    total = SCALE * total
    down[...] = total[:, :, :feat]
    up[...] = total[:, :, feat:]


def shards(x, w, down, up, gy, owner, table):
    tok, feat = x.shape
    cols = w.shape[1]
    sites, rank = up.shape[:2]
    n_dp, n_mp, n_pair = (lax.axis_size(a) for a in ("dp", "mp", "pair"))
    n_other = n_mp - 1
    down = down.transpose(0, 2, 1)
    part = feat // n_pair
    tile = tok // TILES
    row_block = lambda width: pl.BlockSpec((tile, width), lambda i: (i, 0))
    whole = lambda *dims: pl.BlockSpec(dims, lambda i: (0,) * len(dims))

    packed = call(
        functools.partial(pack_kernel, n_dp, n_mp, n_pair), "pack",
        [shape(rank, cols)] * n_dp + [shape(rank, feat)] * n_dp + [shape(part, cols)] * n_other,
        [SMEM, ANY, ANY, ANY], [VMEM] * (2 * n_dp + n_other),
        [pltpu.SemaphoreType.DMA((2 * n_dp + n_other,))], mib=64,
    )(table, down, up, w)
    pieces = [shift(packed[2 * n_dp + s - 1], "mp", s) for s in range(1, n_mp)]
    ups = [packed[0]] + [shift(packed[s], "dp", s) for s in range(1, n_dp)]
    downs = [packed[n_dp]] + [shift(packed[n_dp + s], "dp", s) for s in range(1, n_dp)]

    def low_rank(act, maps, behind, name):
        mine = call(
            functools.partial(reduce_kernel, n_dp), name + "_part",
            shape(tok // 2, 2 * rank), [SMEM, VMEM, ANY] + [VMEM] * n_dp, VMEM,
            [pltpu.VMEM((n_dp * rank, act.shape[1]), BF16)],
        )(owner, act, behind, *maps)
        return [mine] + [shift(mine, "mp", s) for s in range(1, n_mp)]

    def gradient(act, parts, behind, name, flops):
        *grads, wide = call(
            functools.partial(grad_kernel, n_dp, n_mp, len(behind)), name + "_grad",
            [shape(rank, act.shape[1])] * n_dp + [shape(tok, n_dp * rank)],
            [SMEM, VMEM] + [ANY] * len(behind) + [VMEM] * n_mp, [VMEM] * (n_dp + 1), flops=flops,
        )(owner, act, *behind, *parts)
        return [grads[0]] + [shift(grads[s], "dp", n_dp - s) for s in range(1, n_dp)], wide

    h_parts = low_rank(gy, ups, packed[0], "h")
    gy_got = [shift(after(gy, h_parts[0], *pieces), "mp", s) for s in range(1, n_mp)]
    down_back, h_wide = gradient(x, h_parts, downs[1:], "down", GRAD_COST)
    u_parts = low_rank(x, downs, h_wide, "u")

    parts = []
    for piece in pieces:
        parts += [piece] + [shift(after(piece, h_parts[0]), "pair", q) for q in range(1, n_pair)]
    sent = call(
        functools.partial(send_kernel, n_pair, feat, n_mp), "y_send",
        [shape(tok, cols)] * n_other + [shape(feat, cols)] * n_other,
        [ANY, ANY, row_block(feat)] + [whole(part, cols)] * len(parts),
        [row_block(cols)] * n_other + [whole(feat, cols)] * n_other,
        grid=(TILES,),
    )(u_parts[0], down_back[1], x, *parts)
    w_rows = sent[n_other:]
    y_got = [shift(sent[s - 1], "mp", n_mp - s) for s in range(1, n_mp)]
    up_back, u_wide = gradient(gy, u_parts, down_back[2:] + gy_got, "up", GRAD_COST)

    y_own = call(
        functools.partial(own_kernel, n_dp), "y_own",
        shape(tok, cols, dtype=F32),
        [whole(*w.shape), row_block(feat), row_block(n_dp * rank)] + [whole(rank, cols)] * n_dp,
        row_block(cols), [pltpu.VMEM((n_dp * rank, cols), BF16)], grid=(TILES,),
    )(w, x, u_wide, *ups)

    back = call(
        functools.partial(back_kernel, n_dp, n_mp), "back",
        shape(tok, feat),
        [ANY, whole(*w.shape)] + [row_block(cols)] * n_mp + [whole(feat, cols)] * n_other
        + [row_block(n_dp * rank)] + [whole(rank, feat)] * n_dp,
        row_block(feat), [pltpu.VMEM((feat, cols), BF16), pltpu.VMEM((n_dp * rank, feat), BF16)], grid=(TILES,),
    )(u_wide, w, gy, *gy_got, *w_rows, h_wide, *downs)

    summed = call(
        functools.partial(site_kernel, n_dp, feat), "sites",
        shape(sites, rank, feat + cols), [SMEM] + [VMEM] * (2 * n_dp), VMEM,
    )(table, *down_back, *up_back)
    both = [summed] + [shift(summed, "pair", q) for q in range(1, n_pair)]
    down_grad, up_grad = call(
        functools.partial(last_kernel, feat), "gradients",
        [shape(sites, rank, feat, dtype=F32), shape(sites, rank, cols, dtype=F32)],
        [VMEM] * n_pair, [VMEM] * 2,
    )(*both)

    y = call(
        add_kernel, "y_add", shape(tok, cols), [row_block(cols)] * n_mp, row_block(cols), grid=(TILES,),
    )(y_own, *y_got)
    return y, back, down_grad.transpose(0, 2, 1), up_grad


def solution(mesh):
    rows = P(("groups", "dp", "pair"), "mp")
    in_specs = (
        rows,
        P(None, "mp"),
        P(("groups", "dp"), "mp", None),
        P(("groups", "dp"), None, "mp"),
        rows,
        P(("groups", "dp", "pair")),
        P(("groups", "dp"), None, None),
    )
    out_specs = (rows, rows, P(("groups", "dp"), "mp", None), P(("groups", "dp"), None, "mp"))
    return jax.shard_map(shards, mesh=mesh, in_specs=in_specs, out_specs=out_specs, check_vma=False)
```

time: 102 us -> 71 us (0.70)
  waiting for transfers between devices: 58.7 us -> 16.9 us
  starting transfers between devices: 22.1 us -> 29.6 us
  Pallas kernels: 16.5 us -> 20.5 us
  local copies, waits for them, and re-layouts: 4.26 us -> 2.93 us
    ppermute x19, waiting for transfers between devices: 58.7 us -> 16.9 us  [shift(): lax.ppermute(value, axis, [(i, (i + by) % size) for i in range(size)])]
    ppermute x19, starting transfers between devices: 22.1 us -> 29.6 us  [shift(): lax.ppermute(value, axis, [(i, (i + by) % size) for i in range(size)])]
    pallas_call x11, Pallas kernels: 16.5 us -> 20.5 us  [the longest x1 4.71 us: shards(): call(functools.partial(back_kernel, n_dp, n_mp), 'back', shape(tok, feat)...]
    unnamed x16 -> x18, local copies, waits for them, and re-layouts: 4.26 us -> 2.93 us
  transfers between devices with their start and end apart: 19 -> 19, of which waited for: 11 -> 9; matrix products, arithmetic and copies ran while one was open for 0% -> 0% of each run, Pallas kernels for 13% -> 22%
where the time goes in v4:
time: 71 us; the launch traced here: 70.7 us
  starting transfers between devices  29.6 us (42%)
  Pallas kernels  20.5 us (29%)
  waiting for transfers between devices  16.9 us (24%)
  local copies, waits for them, and re-layouts  2.93 us (4%)
  between operations  0.78 us (1%)
    ppermute x19, starting transfers between devices, shift(): lax.ppermute(value, axis, [(i, (i + by) % size) for i in range(size)])  29.6 us
    ppermute x19, waiting for transfers between devices, shift(): lax.ppermute(value, axis, [(i, (i + by) % size) for i in range(size)])  16.9 us
    pallas_call x1, Pallas kernels, shards(): call(functools.partial(back_kernel, n_dp, n_mp), 'back', shape(tok, feat)...  4.71 us
    pallas_call x1, Pallas kernels, shards(): call(functools.partial(pack_kernel, n_dp, n_mp, n_pair), 'pack', [shape(r...  3.23 us
    pallas_call x2, Pallas kernels, gradient(): call(functools.partial(grad_kernel, n_dp, n_mp, len(behind)), name + '_gr...  3.18 us
    pallas_call x2, Pallas kernels, low_rank(): call(functools.partial(reduce_kernel, n_dp), name + '_part', shape(tok //...  3.01 us
    unnamed x18, local copies, waits for them, and re-layouts  2.93 us
    pallas_call x1, Pallas kernels, shards(): call(functools.partial(own_kernel, n_dp), 'y_own', shape(tok, cols, dtype...  1.58 us
  transfers between devices with their start and end apart: 19, of which 9 were waited for; matrix products, arithmetic and copies ran while one was open for 0% of the time, Pallas kernels for 22%

profile of v4, /device:TPU:0, one launch (start us, length us, event | category | flops | bytes accessed | tf_op | source)
XLA Modules:
  0.0 70.7 jit_solution(6717731822937270729)
XLA Ops:
  0.6 3.2 %pack.1 = (bf16[64,512]{1,0:T(8,128)(2,1)}, bf16[64,512]{1,0:T(8,128)(2,1)}, bf16[64,512]{1,0:T(8,128)(2,1)}, bf16[64,512]{1,0:T(8,128)(2,1)}, bf16[64,1024]{1,0...) custom-call(s32[1,2,4]{2,1,0:T(2,128)} %table.3, ...), custom_call_target="tpu_custom_call" | custom-call | flops 1 | bytes 1 | tf_op jit(solution)/shard_map/pack/pallas_call | solution.py:215
  3.9 3.0 %collective-permute-start.9 = (bf16[512,512]{1,0:T(8,128)(2,1)}, bf16[512,512]{1,0:T(8,128)(2,1)S(1)}, u32[]{:S(2)}, u32[]{:S(2)}) collective-permute-start(bf16[512,512]{1,0:T(8,128)(2,1)} %get-tuple-element.38), channel_id=1, source_target_pairs={{0,2},{2,0},{1,3},{3,1},{4,6},{6,4},{5,7},{7,5},{8,10},{10,8},{9,1... | collective-permute-start | bytes 1572872 | tf_op jit(solution)/shard_map/ppermute | solution.py:35
  6.9 1.6 %collective-permute-start.3 = (bf16[64,512]{1,0:T(8,128)(2,1)}, bf16[64,512]{1,0:T(8,128)(2,1)S(1)}, u32[]{:S(2)}, u32[]{:S(2)}) collective-permute-start(bf16[64,512]{1,0:T(8,128)(2,1)} %get-tuple-element.33), channel_id=1, source_target_pairs={{0,4},{4,8},{8,12},{12,0},{1,5},{5,9},{9,13},{13,1},{2,6},{6,10},{... | collective-permute-start | bytes 196616 | tf_op jit(solution)/shard_map/ppermute | solution.py:35
  8.5 2.5 %collective-permute-start.4 = (bf16[64,512]{1,0:T(8,128)(2,1)}, bf16[64,512]{1,0:T(8,128)(2,1)S(1)}, u32[]{:S(2)}, u32[]{:S(2)}) collective-permute-start(bf16[64,512]{1,0:T(8,128)(2,1)} %get-tuple-element.34), channel_id=1, source_target_pairs={{0,8},{4,12},{8,0},{12,4},{1,9},{5,13},{9,1},{13,5},{2,10},{6,14},... | collective-permute-start | bytes 196616 | tf_op jit(solution)/shard_map/ppermute | solution.py:35
  11.0 1.3 %collective-permute-start.5 = (bf16[64,512]{1,0:T(8,128)(2,1)}, bf16[64,512]{1,0:T(8,128)(2,1)S(1)}, u32[]{:S(2)}, u32[]{:S(2)}) collective-permute-start(bf16[64,512]{1,0:T(8,128)(2,1)} %get-tuple-element.35), channel_id=1, source_target_pairs={{0,12},{4,0},{8,4},{12,8},{1,13},{5,1},{9,5},{13,9},{2,14},{6,2},{... | collective-permute-start | bytes 196616 | tf_op jit(solution)/shard_map/ppermute | solution.py:35
  13.1 0.9 %collective-permute-done.3.refs_1_ = bf16[64,512]{1,0:T(8,128)(2,1)S(1)} collective-permute-done((bf16[64,512]{1,0:T(8,128)(2,1)}, bf16[64,512]{1,0:T(8,128)(2,1)S(1)}, u32[]{:S(2)}, u32[]{:S(2)}) %collective-permute-start.3) | collective-permute-done | bytes 65568 | tf_op jit(solution)/shard_map/ppermute | solution.py:35
  13.9 1.1 %collective-permute-start.1 = (bf16[64,1024]{1,0:T(8,128)(2,1)}, bf16[64,1024]{1,0:T(8,128)(2,1)S(1)}, u32[]{:S(2)}, u32[]{:S(2)}) collective-permute-start(bf16[64,1024]{1,0:T(8,128)(2,1)} %get-tuple-element.30), channel_id=1, source_target_pairs={{0,8},{4,12},{8,0},{12,4},{1,9},{5,13},{9,1},{13,5},{2,10},{6,14},... | collective-permute-start | bytes 393224 | tf_op jit(solution)/shard_map/ppermute | solution.py:35
  15.1 1.2 %collective-permute-done.4.refs_2_ = bf16[64,512]{1,0:T(8,128)(2,1)S(1)} collective-permute-done((bf16[64,512]{1,0:T(8,128)(2,1)}, bf16[64,512]{1,0:T(8,128)(2,1)S(1)}, u32[]{:S(2)}, u32[]{:S(2)}) %collective-permute-start.4) | collective-permute-done | bytes 65568 | tf_op jit(solution)/shard_map/ppermute | solution.py:35
  16.3 3.2 %collective-permute-start.2 = (bf16[64,1024]{1,0:T(8,128)(2,1)}, bf16[64,1024]{1,0:T(8,128)(2,1)S(1)}, u32[]{:S(2)}, u32[]{:S(2)}) collective-permute-start(bf16[64,1024]{1,0:T(8,128)(2,1)} %get-tuple-element.31), channel_id=1, source_target_pairs={{0,12},{4,0},{8,4},{12,8},{1,13},{5,1},{9,5},{13,9},{2,14},{6,2},{... | collective-permute-start | bytes 393224 | tf_op jit(solution)/shard_map/ppermute | solution.py:35
  21.0 1.7 %h_part.1.refs_3_ = bf16[384,128]{1,0:T(8,128)(2,1)S(1)} custom-call(s32[12]{0:T(128)S(1)} %copy-done.7, bf16[768,512]{1,0:T(8,128)(2,1)} %refs_1_.1, bf16[64,512]{1,0:T(8,128)(2,1)S(1)} %copy-done.3, bf16[64,512]{1,0:T(8,128)(2,1)S(1)} %copy-done.3, bf16[64,512]{1,0:T(8,128)(2,1)S(1)} %collective-permute-done.3.refs_1_, ...), custom_call_target="tpu_custom_call" | custom-call | flops 1 | bytes 1 | tf_op jit(solution)/shard_map/h_part/pallas_call | solution.py:226
  23.3 1.6 %collective-permute-start.10 = (bf16[768,512]{1,0:T(8,128)(2,1)}, bf16[768,512]{1,0:T(8,128)(2,1)S(1)}, u32[]{:S(2)}, u32[]{:S(2)}) collective-permute-start(bf16[768,512]{1,0:T(8,128)(2,1)} %refs_1_.1), channel_id=1, source_target_pairs={{0,2},{2,0},{1,3},{3,1},{4,6},{6,4},{5,7},{7,5},{8,10},{10,8},{9,1... | collective-permute-start | bytes 2359304 | tf_op jit(solution)/shard_map/ppermute | solution.py:35
  24.9 1.0 %collective-permute-done.1.refs_1_.refs_2_.refs_7_ = bf16[64,1024]{1,0:T(8,128)(2,1)S(1)} collective-permute-done((bf16[64,1024]{1,0:T(8,128)(2,1)}, bf16[64,1024]{1,0:T(8,128)(2,1)S(1)}, u32[]{:S(2)}, u32[]{:S(2)}) %collective-permute-start.1) | collective-permute-done | bytes 131104 | tf_op jit(solution)/shard_map/ppermute | solution.py:35
  25.9 2.3 %collective-permute-done.6.refs_4_ = bf16[384,128]{1,0:T(8,128)(2,1)S(1)} collective-permute-done((bf16[384,128]{1,0:T(8,128)(2,1)S(1)}, bf16[384,128]{1,0:T(8,128)(2,1)S(1)}, u32[]{:S(2)}, u32[]{:S(2)}) %collective-permute-start.6) | collective-permute-done | bytes 98336 | tf_op jit(solution)/shard_map/ppermute | solution.py:35
  28.1 1.4 %copy-done.1 = bf16[768,1024]{1,0:T(8,128)(2,1)S(1)} copy-done((bf16[768,1024]{1,0:T(8,128)(2,1)S(1)}, bf16[768,1024]{1,0:T(8,128)(2,1)}, u32[]{:S(2)}) %copy-start.1) | copy-done | bytes 1572888
  29.6 1.3 %down_grad.1 = (bf16[64,1024]{1,0:T(8,128)(2,1)S(1)}, bf16[64,1024]{1,0:T(8,128)(2,1)S(1)}, bf16[64,1024]{1,0:T(8,128)(2,1)S(1)}, bf16[64,1024]{1,0:T(8,128)(2,1)S(1)}, bf16[768,256]{1,0:T(8,128)(2,1)S(1)}) custom-call(s32[12]{0:T(128)S(1)} %copy-done.7, bf16[768,1024]{1,0:T(8,128)(2,1)S(1)} %copy-done.1, ...), custom_call_target="tpu_custom_call" | custom-call | flops 15000000512 | bytes 1 | tf_op jit(solution)/shard_map/down_grad/pallas_call | solution.py:234
  30.9 1.8 %collective-permute-start.12 = (bf16[64,1024]{1,0:T(8,128)(2,1)S(1)}, bf16[64,1024]{1,0:T(8,128)(2,1)S(1)}, u32[]{:S(2)}, u32[]{:S(2)}) collective-permute-start(bf16[64,1024]{1,0:T(8,128)(2,1)S(1)} %get-tuple-element.43), channel_id=1, source_target_pairs={{0,12},{4,0},{8,4},{12,8},{1,13},{5,1},{9,5},{13,9},{2,14},{6,2},{... | collective-permute-start | bytes 393224 | tf_op jit(solution)/shard_map/ppermute | solution.py:35
  32.7 4.1 %collective-permute-start.7 = (bf16[64,1024]{1,0:T(8,128)(2,1)S(1)}, bf16[64,1024]{1,0:T(8,128)(2,1)S(1)}, u32[]{:S(2)}, u32[]{:S(2)}) collective-permute-start(bf16[64,1024]{1,0:T(8,128)(2,1)S(1)} %get-tuple-element.36), channel_id=1, source_target_pairs={{0,8},{4,12},{8,0},{12,4},{1,9},{5,13},{9,1},{13,5},{2,10},{6,14},... | collective-permute-start | bytes 393224 | tf_op jit(solution)/shard_map/ppermute | solution.py:35
  36.8 1.3 %u_part.1.refs_3_._ = bf16[384,128]{1,0:T(8,128)(2,1)S(1)} custom-call(s32[12]{0:T(128)S(1)} %copy-done.7, bf16[768,1024]{1,0:T(8,128)(2,1)S(1)} %copy-done.2, bf16[768,256]{1,0:T(8,128)(2,1)S(1)} %get-tuple-element.40._.refs_4_, bf16[64,1024]{1,0:T(8,128)(2,1)S(1)} %copy-done.5, bf16[64,1024]{1,0:T(8,128)(2,1)S(1)} %collective-permute-done.refs_0_.refs_1_.refs_6_, ...), custom_call_target="tpu_custom_call" | custom-call | flops 1 | bytes 1 | tf_op jit(solution)/shard_map/u_part/pallas_call | solution.py:226
  38.1 2.6 %collective-permute-done.12.__.refs_1_ = bf16[64,1024]{1,0:T(8,128)(2,1)S(1)} collective-permute-done((bf16[64,1024]{1,0:T(8,128)(2,1)S(1)}, bf16[64,1024]{1,0:T(8,128)(2,1)S(1)}, u32[]{:S(2)}, u32[]{:S(2)}) %collective-permute-start.12) | collective-permute-done | bytes 131104 | tf_op jit(solution)/shard_map/ppermute | solution.py:35
  40.7 1.4 %y_send.1 = (bf16[768,512]{1,0:T(8,128)(2,1)S(1)}, bf16[1024,512]{1,0:T(8,128)(2,1)S(1)}) custom-call(bf16[384,128]{1,0:T(8,128)(2,1)S(1)} %u_part.1.refs_3_._, bf16[64,1024]{1,0:T(8,128)(2,1)S(1)} %collective-permute-done.12.__.refs_1_, bf16[768,1024]{1,0:T(8,128)(2,1)S(1)} %copy-done.2, bf16[512,512]{1,0:T(8,128)(2,1)S(1)} %collective-permute-done.9.refs_0_, ...), custom_call_target="tpu_custom_call" | custom-call | flops 1 | bytes 1 | tf_op jit(solution)/shard_map/y_send/pallas_call | solution.py:249
  42.1 2.1 %collective-permute-start.14 = (bf16[768,512]{1,0:T(8,128)(2,1)S(1)}, bf16[768,512]{1,0:T(8,128)(2,1)S(1)}, u32[]{:S(2)}, u32[]{:S(2)}) collective-permute-start(bf16[768,512]{1,0:T(8,128)(2,1)S(1)} %get-tuple-element.45), channel_id=1, source_target_pairs={{0,2},{2,0},{1,3},{3,1},{4,6},{6,4},{5,7},{7,5},{8,10},{10,8},{9,1... | collective-permute-start | bytes 2359304 | tf_op jit(solution)/shard_map/ppermute | solution.py:35
  44.2 2.9 %collective-permute-done.11.refs_4_ = bf16[384,128]{1,0:T(8,128)(2,1)S(1)} collective-permute-done((bf16[384,128]{1,0:T(8,128)(2,1)S(1)}, bf16[384,128]{1,0:T(8,128)(2,1)S(1)}, u32[]{:S(2)}, u32[]{:S(2)}) %collective-permute-start.11) | collective-permute-done | bytes 98336 | tf_op jit(solution)/shard_map/ppermute | solution.py:35
  47.1 1.8 %up_grad.1 = (bf16[64,512]{1,0:T(8,128)(2,1)S(1)}, bf16[64,512]{1,0:T(8,128)(2,1)S(1)}, bf16[64,512]{1,0:T(8,128)(2,1)S(1)}, bf16[64,512]{1,0:T(8,128)(2,1)S(1)}, bf16[768,256]{1,0:T(8,128)(2,1)S(1)}) custom-call(s32[12]{0:T(128)S(1)} %copy-done.8, bf16[768,512]{1,0:T(8,128)(2,1)} %refs_1_.1, bf16[64,1024]{1,0:T(8,128)(2,1)S(1)} %collective-permute-done.7.refs_0_.refs_2_, ...), custom_call_target="tpu_custom_call" | custom-call | flops 15000000512 | bytes 1 | tf_op jit(solution)/shard_map/up_grad/pallas_call | solution.py:234
  49.7 5.2 %collective-permute-start.16 = (bf16[64,512]{1,0:T(8,128)(2,1)S(1)}, bf16[64,512]{1,0:T(8,128)(2,1)S(1)}, u32[]{:S(2)}, u32[]{:S(2)}) collective-permute-start(bf16[64,512]{1,0:T(8,128)(2,1)S(1)} %get-tuple-element.50), channel_id=1, source_target_pairs={{0,8},{4,12},{8,0},{12,4},{1,9},{5,13},{9,1},{13,5},{2,10},{6,14},... | collective-permute-start | bytes 196616 | tf_op jit(solution)/shard_map/ppermute | solution.py:35
  54.9 1.1 %collective-permute-done.15.refs_5_ = bf16[64,512]{1,0:T(8,128)(2,1)S(1)} collective-permute-done((bf16[64,512]{1,0:T(8,128)(2,1)S(1)}, bf16[64,512]{1,0:T(8,128)(2,1)S(1)}, u32[]{:S(2)}, u32[]{:S(2)}) %collective-permute-start.15) | collective-permute-done | bytes 65568 | tf_op jit(solution)/shard_map/ppermute | solution.py:35
  56.0 3.3 %collective-permute-done.16.refs_6_ = bf16[64,512]{1,0:T(8,128)(2,1)S(1)} collective-permute-done((bf16[64,512]{1,0:T(8,128)(2,1)S(1)}, bf16[64,512]{1,0:T(8,128)(2,1)S(1)}, u32[]{:S(2)}, u32[]{:S(2)}) %collective-permute-start.16) | collective-permute-done | bytes 65568 | tf_op jit(solution)/shard_map/ppermute | solution.py:35
  59.2 1.7 %collective-permute-done.17.refs_7_ = bf16[64,512]{1,0:T(8,128)(2,1)S(1)} collective-permute-done((bf16[64,512]{1,0:T(8,128)(2,1)S(1)}, bf16[64,512]{1,0:T(8,128)(2,1)S(1)}, u32[]{:S(2)}, u32[]{:S(2)}) %collective-permute-start.17) | collective-permute-done | bytes 65568 | tf_op jit(solution)/shard_map/ppermute | solution.py:35
  61.0 0.9 %sites.1.refs_0_ = bf16[2,64,1536]{2,1,0:T(8,128)(2,1)S(1)} custom-call(s32[1,2,4]{2,1,0:T(2,128)S(1)} %copy-done.6, bf16[64,1024]{1,0:T(8,128)(2,1)S(1)} %get-tuple-element.47.refs_0_, bf16[64,1024]{1,0:T(8,128)(2,1)S(1)} %collective-permute-done.12.__.refs_1_, bf16[64,1024]{1,0:T(8,128)(2,1)S(1)} %collective-permute-done.7.refs_0_.refs_2_, ...), custom_call_target="tpu_custom_call" | custom-call | flops 1 | bytes 1 | tf_op jit(solution)/shard_map/sites/pallas_call | solution.py:275
  61.9 1.6 %y_own.1.refs_0_ = f32[768,512]{1,0:T(8,128)S(1)} custom-call(bf16[2048,512]{1,0:T(8,128)(2,1)S(1)} %copy-done, bf16[768,1024]{1,0:T(8,128)(2,1)S(1)} %copy-done.2, bf16[768,256]{1,0:T(8,128)(2,1)S(1)} %get-tuple-element.42.wide._, bf16[64,512]{1,0:T(8,128)(2,1)S(1)} %copy-done.4, bf16[64,512]{1,0:T(8,128)(2,1)S(1)} %collective-permute-done.3.refs_1_, ...), custom_call_target="tpu_custom_call" | custom-call | flops 1 | bytes 1 | tf_op jit(solution)/shard_map/y_own/pallas_call | solution.py:260
  63.5 4.7 %back.1 = bf16[768,1024]{1,0:T(8,128)(2,1)} custom-call(bf16[768,256]{1,0:T(8,128)(2,1)S(1)} %get-tuple-element.42.wide._, bf16[2048,512]{1,0:T(8,128)(2,1)S(1)} %copy-done, bf16[768,512]{1,0:T(8,128)(2,1)} %refs_1_.1, bf16[768,512]{1,0:T(8,128)(2,1)S(1)} %collective-permute-done.10.refs_2_, bf16[1024,512]{1,0:T(8,128)(2,1)S(1)} %get-tuple-element.46.refs_3_, ...), custom_call_target="tpu_custom_call" | custom-call | flops 1 | bytes 1 | tf_op jit(solution)/shard_map/back/pallas_call | solution.py:267
  68.2 0.9 %gradients.1 = (f32[2,64,1024]{2,1,0:T(8,128)}, f32[2,64,512]{2,1,0:T(8,128)}) custom-call(bf16[2,64,1536]{2,1,0:T(8,128)(2,1)S(1)} %sites.1.refs_0_, bf16[2,64,1536]{2,1,0:T(8,128)(2,1)S(1)} %collective-permute-done.18.refs_1_), custom_call_target="tpu_custom_call" | custom-call | flops 1 | bytes 1 | tf_op jit(solution)/shard_map/gradients/pallas_call | solution.py:280
  69.2 1.5 %y_add.1 = bf16[768,512]{1,0:T(8,128)(2,1)} custom-call(f32[768,512]{1,0:T(8,128)S(1)} %y_own.1.refs_0_, bf16[768,512]{1,0:T(8,128)(2,1)S(1)} %collective-permute-done.14.refs_1_), custom_call_target="tpu_custom_call" | custom-call | flops 1 | bytes 1 | tf_op jit(solution)/shard_map/y_add/pallas_call | solution.py:286
  (35 shorter events, 3.6 us)
Async XLA Ops:
  3.9 19.4 %collective-permute-start.9 = (bf16[512,512]{1,0:T(8,128)(2,1)}, bf16[512,512]{1,0:T(8,128)(2,1)S(1)}, u32[]{:S(2)}, u32[]{:S(2)}) collective-permute-start(bf16[512,512]{1,0:T(8,128)(2,1)} %get-tuple-element.38), channel_id=1, source_target_pairs={{0,2},{2,0},{1,3},{3,1},{4,6},{6,4},{5,7},{7,5},{8,10},{10,8},{9,1... | collective-permute-start | bytes 1572872 | tf_op jit(solution)/shard_map/ppermute | solution.py:35
  6.9 7.1 %collective-permute-start.3 = (bf16[64,512]{1,0:T(8,128)(2,1)}, bf16[64,512]{1,0:T(8,128)(2,1)S(1)}, u32[]{:S(2)}, u32[]{:S(2)}) collective-permute-start(bf16[64,512]{1,0:T(8,128)(2,1)} %get-tuple-element.33), channel_id=1, source_target_pairs={{0,4},{4,8},{8,12},{12,0},{1,5},{5,9},{9,13},{13,1},{2,6},{6,10},{... | collective-permute-start | bytes 196616 | tf_op jit(solution)/shard_map/ppermute | solution.py:35
  8.5 7.8 %collective-permute-start.4 = (bf16[64,512]{1,0:T(8,128)(2,1)}, bf16[64,512]{1,0:T(8,128)(2,1)S(1)}, u32[]{:S(2)}, u32[]{:S(2)}) collective-permute-start(bf16[64,512]{1,0:T(8,128)(2,1)} %get-tuple-element.34), channel_id=1, source_target_pairs={{0,8},{4,12},{8,0},{12,4},{1,9},{5,13},{9,1},{13,5},{2,10},{6,14},... | collective-permute-start | bytes 196616 | tf_op jit(solution)/shard_map/ppermute | solution.py:35
  11.0 8.4 %collective-permute-start.5 = (bf16[64,512]{1,0:T(8,128)(2,1)}, bf16[64,512]{1,0:T(8,128)(2,1)S(1)}, u32[]{:S(2)}, u32[]{:S(2)}) collective-permute-start(bf16[64,512]{1,0:T(8,128)(2,1)} %get-tuple-element.35), channel_id=1, source_target_pairs={{0,12},{4,0},{8,4},{12,8},{1,13},{5,1},{9,5},{13,9},{2,14},{6,2},{... | collective-permute-start | bytes 196616 | tf_op jit(solution)/shard_map/ppermute | solution.py:35
  12.4 10.9 %collective-permute-start = (bf16[64,1024]{1,0:T(8,128)(2,1)}, bf16[64,1024]{1,0:T(8,128)(2,1)S(1)}, u32[]{:S(2)}, u32[]{:S(2)}) collective-permute-start(bf16[64,1024]{1,0:T(8,128)(2,1)} %get-tuple-element.29), channel_id=1, source_target_pairs={{0,4},{4,8},{8,12},{12,0},{1,5},{5,9},{9,13},{13,1},{2,6},{6,10},{... | collective-permute-start | bytes 393224 | tf_op jit(solution)/shard_map/ppermute | solution.py:35
  13.9 11.9 %collective-permute-start.1 = (bf16[64,1024]{1,0:T(8,128)(2,1)}, bf16[64,1024]{1,0:T(8,128)(2,1)S(1)}, u32[]{:S(2)}, u32[]{:S(2)}) collective-permute-start(bf16[64,1024]{1,0:T(8,128)(2,1)} %get-tuple-element.30), channel_id=1, source_target_pairs={{0,8},{4,12},{8,0},{12,4},{1,9},{5,13},{9,1},{13,5},{2,10},{6,14},... | collective-permute-start | bytes 393224 | tf_op jit(solution)/shard_map/ppermute | solution.py:35
  16.3 9.6 %collective-permute-start.2 = (bf16[64,1024]{1,0:T(8,128)(2,1)}, bf16[64,1024]{1,0:T(8,128)(2,1)S(1)}, u32[]{:S(2)}, u32[]{:S(2)}) collective-permute-start(bf16[64,1024]{1,0:T(8,128)(2,1)} %get-tuple-element.31), channel_id=1, source_target_pairs={{0,12},{4,0},{8,4},{12,8},{1,13},{5,1},{9,5},{13,9},{2,14},{6,2},{... | collective-permute-start | bytes 393224 | tf_op jit(solution)/shard_map/ppermute | solution.py:35
  19.5 0.8 %copy-start.3 = (bf16[64,512]{1,0:T(8,128)(2,1)S(1)}, bf16[64,512]{1,0:T(8,128)(2,1)}, u32[]{:S(2)}) copy-start(bf16[64,512]{1,0:T(8,128)(2,1)} %get-tuple-element.32._.refs_0_) | copy-start | bytes 196612
  20.3 0.7 copy-start.7
  21.0 15.8 %copy-start.5 = (bf16[64,1024]{1,0:T(8,128)(2,1)S(1)}, bf16[64,1024]{1,0:T(8,128)(2,1)}, u32[]{:S(2)}) copy-start(bf16[64,1024]{1,0:T(8,128)(2,1)} %get-tuple-element.41.refs_0_.refs_5_) | copy-start | bytes 393220
  22.7 5.5 %collective-permute-start.6 = (bf16[384,128]{1,0:T(8,128)(2,1)S(1)}, bf16[384,128]{1,0:T(8,128)(2,1)S(1)}, u32[]{:S(2)}, u32[]{:S(2)}) collective-permute-start(bf16[384,128]{1,0:T(8,128)(2,1)S(1)} %h_part.1.refs_3_), channel_id=1, source_target_pairs={{0,2},{2,0},{1,3},{3,1},{4,6},{6,4},{5,7},{7,5},{8,10},{10,8},{9,1... | collective-permute-start | bytes 294920 | tf_op jit(solution)/shard_map/ppermute | solution.py:35
  23.3 17.4 %collective-permute-start.13 = (bf16[512,512]{1,0:T(8,128)(2,1)S(1)}, bf16[512,512]{1,0:T(8,128)(2,1)S(1)}, u32[]{:S(2)}, u32[]{:S(2)}) collective-permute-start(bf16[512,512]{1,0:T(8,128)(2,1)S(1)} %collective-permute-done.9.refs_0_), channel_id=1, source_target_pairs={{0,1},{1,0},{2,3},{3,2},{4,5},{5,4},{6,7},{7,6},{8,9},{9,8},{10,11... | collective-permute-start | bytes 1572872 | tf_op jit(solution)/shard_map/ppermute | solution.py:35
  23.3 23.8 %collective-permute-start.10 = (bf16[768,512]{1,0:T(8,128)(2,1)}, bf16[768,512]{1,0:T(8,128)(2,1)S(1)}, u32[]{:S(2)}, u32[]{:S(2)}) collective-permute-start(bf16[768,512]{1,0:T(8,128)(2,1)} %refs_1_.1), channel_id=1, source_target_pairs={{0,2},{2,0},{1,3},{3,1},{4,6},{6,4},{5,7},{7,5},{8,10},{10,8},{9,1... | collective-permute-start | bytes 2359304 | tf_op jit(solution)/shard_map/ppermute | solution.py:35
  28.1 1.4 %copy-start.1 = (bf16[768,1024]{1,0:T(8,128)(2,1)S(1)}, bf16[768,1024]{1,0:T(8,128)(2,1)}, u32[]{:S(2)}) copy-start(bf16[768,1024]{1,0:T(8,128)(2,1)} %x.3) | copy-start | bytes 4718596
  29.6 7.3 %copy-start.2 = (bf16[768,1024]{1,0:T(8,128)(2,1)S(1)}, bf16[768,1024]{1,0:T(8,128)(2,1)}, u32[]{:S(2)}) copy-start(bf16[768,1024]{1,0:T(8,128)(2,1)} %x.3) | copy-start | bytes 4718596
  30.9 9.8 %collective-permute-start.12 = (bf16[64,1024]{1,0:T(8,128)(2,1)S(1)}, bf16[64,1024]{1,0:T(8,128)(2,1)S(1)}, u32[]{:S(2)}, u32[]{:S(2)}) collective-permute-start(bf16[64,1024]{1,0:T(8,128)(2,1)S(1)} %get-tuple-element.43), channel_id=1, source_target_pairs={{0,12},{4,0},{8,4},{12,8},{1,13},{5,1},{9,5},{13,9},{2,14},{6,2},{... | collective-permute-start | bytes 393224 | tf_op jit(solution)/shard_map/ppermute | solution.py:35
  32.7 14.4 %collective-permute-start.7 = (bf16[64,1024]{1,0:T(8,128)(2,1)S(1)}, bf16[64,1024]{1,0:T(8,128)(2,1)S(1)}, u32[]{:S(2)}, u32[]{:S(2)}) collective-permute-start(bf16[64,1024]{1,0:T(8,128)(2,1)S(1)} %get-tuple-element.36), channel_id=1, source_target_pairs={{0,8},{4,12},{8,0},{12,4},{1,9},{5,13},{9,1},{13,5},{2,10},{6,14},... | collective-permute-start | bytes 393224 | tf_op jit(solution)/shard_map/ppermute | solution.py:35
  36.8 10.3 %collective-permute-start.8 = (bf16[64,1024]{1,0:T(8,128)(2,1)S(1)}, bf16[64,1024]{1,0:T(8,128)(2,1)S(1)}, u32[]{:S(2)}, u32[]{:S(2)}) collective-permute-start(bf16[64,1024]{1,0:T(8,128)(2,1)S(1)} %get-tuple-element.37), channel_id=1, source_target_pairs={{0,4},{4,8},{8,12},{12,0},{1,5},{5,9},{9,13},{13,1},{2,6},{6,10},{... | collective-permute-start | bytes 393224 | tf_op jit(solution)/shard_map/ppermute | solution.py:35
  38.1 9.0 %copy-start.8 = (s32[12]{0:T(128)S(1)}, s32[12]{0:T(128)}, u32[]{:S(2)}) copy-start(s32[12]{0:T(128)} %owner.7) | copy-start | bytes 148
  40.7 6.4 %collective-permute-start.11 = (bf16[384,128]{1,0:T(8,128)(2,1)S(1)}, bf16[384,128]{1,0:T(8,128)(2,1)S(1)}, u32[]{:S(2)}, u32[]{:S(2)}) collective-permute-start(bf16[384,128]{1,0:T(8,128)(2,1)S(1)} %u_part.1.refs_3_._), channel_id=1, source_target_pairs={{0,2},{2,0},{1,3},{3,1},{4,6},{6,4},{5,7},{7,5},{8,10},{10,8},{9,1... | collective-permute-start | bytes 294920 | tf_op jit(solution)/shard_map/ppermute | solution.py:35
  42.1 18.8 %copy-start.6 = (s32[1,2,4]{2,1,0:T(2,128)S(1)}, s32[1,2,4]{2,1,0:T(2,128)}, u32[]{:S(2)}) copy-start(s32[1,2,4]{2,1,0:T(2,128)} %table.3) | copy-start | bytes 100
  42.1 19.8 %copy-start.4 = (bf16[64,512]{1,0:T(8,128)(2,1)S(1)}, bf16[64,512]{1,0:T(8,128)(2,1)}, u32[]{:S(2)}) copy-start(bf16[64,512]{1,0:T(8,128)(2,1)} %get-tuple-element.32._.refs_0_) | copy-start | bytes 196612
  42.1 27.1 %collective-permute-start.14 = (bf16[768,512]{1,0:T(8,128)(2,1)S(1)}, bf16[768,512]{1,0:T(8,128)(2,1)S(1)}, u32[]{:S(2)}, u32[]{:S(2)}) collective-permute-start(bf16[768,512]{1,0:T(8,128)(2,1)S(1)} %get-tuple-element.45), channel_id=1, source_target_pairs={{0,2},{2,0},{1,3},{3,1},{4,6},{6,4},{5,7},{7,5},{8,10},{10,8},{9,1... | collective-permute-start | bytes 2359304 | tf_op jit(solution)/shard_map/ppermute | solution.py:35
  47.1 14.8 %copy-start = (bf16[2048,512]{1,0:T(8,128)(2,1)S(1)}, bf16[2048,512]{1,0:T(8,128)(2,1)}, u32[]{:S(2)}) copy-start(bf16[2048,512]{1,0:T(8,128)(2,1)} %refs_0_.1) | copy-start | bytes 6291460
  49.0 7.0 %collective-permute-start.15 = (bf16[64,512]{1,0:T(8,128)(2,1)S(1)}, bf16[64,512]{1,0:T(8,128)(2,1)S(1)}, u32[]{:S(2)}, u32[]{:S(2)}) collective-permute-start(bf16[64,512]{1,0:T(8,128)(2,1)S(1)} %get-tuple-element.49), channel_id=1, source_target_pairs={{0,12},{4,0},{8,4},{12,8},{1,13},{5,1},{9,5},{13,9},{2,14},{6,2},{... | collective-permute-start | bytes 196616 | tf_op jit(solution)/shard_map/ppermute | solution.py:35
  49.7 9.6 %collective-permute-start.16 = (bf16[64,512]{1,0:T(8,128)(2,1)S(1)}, bf16[64,512]{1,0:T(8,128)(2,1)S(1)}, u32[]{:S(2)}, u32[]{:S(2)}) collective-permute-start(bf16[64,512]{1,0:T(8,128)(2,1)S(1)} %get-tuple-element.50), channel_id=1, source_target_pairs={{0,8},{4,12},{8,0},{12,4},{1,9},{5,13},{9,1},{13,5},{2,10},{6,14},... | collective-permute-start | bytes 196616 | tf_op jit(solution)/shard_map/ppermute | solution.py:35
  54.9 6.1 %collective-permute-start.17 = (bf16[64,512]{1,0:T(8,128)(2,1)S(1)}, bf16[64,512]{1,0:T(8,128)(2,1)S(1)}, u32[]{:S(2)}, u32[]{:S(2)}) collective-permute-start(bf16[64,512]{1,0:T(8,128)(2,1)S(1)} %get-tuple-element.51), channel_id=1, source_target_pairs={{0,4},{4,8},{8,12},{12,0},{1,5},{5,9},{9,13},{13,1},{2,6},{6,10},{... | collective-permute-start | bytes 196616 | tf_op jit(solution)/shard_map/ppermute | solution.py:35
  61.8 6.4 %collective-permute-start.18 = (bf16[2,64,1536]{2,1,0:T(8,128)(2,1)S(1)}, bf16[2,64,1536]{2,1,0:T(8,128)(2,1)S(1)}, u32[]{:S(2)}, u32[]{:S(2)}) collective-permute-start(bf16[2,64,1536]{2,1,0:T(8,128)(2,1)S(1)} %sites.1.refs_0_), channel_id=1, source_target_pairs={{0,1},{1,0},{2,3},{3,2},{4,5},{5,4},{6,7},{7,6},{8,9},{9,8},{10,11... | collective-permute-start | bytes 1179656 | tf_op jit(solution)/shard_map/ppermute | solution.py:35

commit v5 on v3

--- a/solution.py
+++ b/solution.py
@@ -9,7 +9,7 @@
 
 SCALE = 2.0
 TILES = 3
-UHCOST = 1
+LONG = 7000000000
 F32 = jnp.float32
 BF16 = jnp.bfloat16
 SMEM = pl.BlockSpec(memory_space=pltpu.SMEM)
@@ -21,11 +21,11 @@
     return jax.ShapeDtypeStruct(dims, dtype)
 
 
-def call(kernel, name, out_shape, in_specs, out_specs, scratch=(), grid=(), flops=1):
+def call(kernel, name, out_shape, in_specs, out_specs, scratch=(), grid=(), mib=32, flops=1):
     return pl.pallas_call(
         kernel, name=name, out_shape=out_shape, grid=grid, in_specs=in_specs, out_specs=out_specs,
         scratch_shapes=scratch,
-        compiler_params=pltpu.CompilerParams(vmem_limit_bytes=64 * 1024 * 1024),
+        compiler_params=pltpu.CompilerParams(vmem_limit_bytes=mib * 1024 * 1024),
         cost_estimate=pl.CostEstimate(flops=flops, bytes_accessed=1, transcendentals=0),
     )
 
@@ -66,30 +66,23 @@
     return lax.rem(lax.axis_index("dp") - owner[b] + n_dp, n_dp)
 
 
-def first_kernel(n_mp, n_share, w, *refs):
-    pieces, sem = refs[:-1], refs[-1]
-    feat = w.shape[0] // n_mp
+def pack_kernel(n_dp, n_mp, n_share, table, down, up, w, *refs):
+    maps, pieces, sem = refs[:n_dp], refs[n_dp:-1], refs[-1]
+    feat, cols = down.shape[2], up.shape[2]
     part = feat // n_share
     place = lax.axis_index("groups") * lax.axis_size("pair") + lax.axis_index("pair")
-    copies = []
-    for s in range(1, n_mp):
-        row = pl.multiple_of(lax.rem(lax.axis_index("mp") + s, n_mp) * feat + place * part, part)
-        copies.append(pltpu.make_async_copy(w.at[pl.ds(row, part)], pieces[s - 1], sem.at[s - 1]))
-    run(copies)
-
-
-def pack_kernel(n_dp, table, down, up, _, *refs):
-    maps, sem = refs[:n_dp], refs[-1]
-    feat, cols = down.shape[2], up.shape[2]
     copies = []
     for s in range(n_dp):
         site = wanted_site(table, n_dp, s)
         copies.append(pltpu.make_async_copy(down.at[site], maps[s].at[:, pl.ds(0, feat)], sem.at[s]))
         copies.append(pltpu.make_async_copy(up.at[site], maps[s].at[:, pl.ds(feat, cols)], sem.at[n_dp + s]))
+    for s in range(1, n_mp):
+        row = pl.multiple_of(lax.rem(lax.axis_index("mp") + s, n_mp) * feat + place * part, part)
+        copies.append(pltpu.make_async_copy(w.at[pl.ds(row, part)], pieces[s - 1], sem.at[2 * n_dp + s - 1]))
     run(copies)
 
 
-def reduce_kernel(n_dp, owner, x, gy, *refs):
+def reduce_kernel(n_dp, owner, _, x, gy, *refs):
     maps, out, wide = refs[:n_dp], refs[n_dp], refs[n_dp + 1]
     rank = maps[0].shape[0]
     feat = x.shape[1]
@@ -129,7 +122,7 @@
         outs[s][...] = nn(x[...], rows[s][...]).astype(BF16)
 
 
-def grad_kernel(n_dp, n_mp, owner, _, x, gy, *refs):
+def grad_kernel(n_dp, n_mp, owner, x, gy, *refs):
     parts, grads, u_wide, h_wide = refs[:n_mp], refs[n_mp:n_mp + n_dp], refs[-2], refs[-1]
     rank = u_wide.shape[1] // n_dp
     feat = x.shape[1]
@@ -191,7 +184,7 @@
     refs[-1][...] = total.astype(BF16)
 
 
-def site_kernel(n_dp, table, _, *refs):
+def site_kernel(n_dp, table, _, __, *refs):
     grads, out = refs[:n_dp], refs[-1]
     for site in range(out.shape[0]):
         total = jnp.zeros(out.shape[1:], F32)
@@ -224,38 +217,35 @@
     row_block = lambda width: pl.BlockSpec((tile, width), lambda i: (i, 0))
     whole = lambda *dims: pl.BlockSpec(dims, lambda i: (0,) * len(dims))
 
-    pieces = call(
-        functools.partial(first_kernel, n_mp, n_share), "first",
-        [shape(part, cols)] * n_other, [ANY], [ANY] * n_other, [pltpu.SemaphoreType.DMA((n_other,))],
-    )(w)
-    maps = call(
-        functools.partial(pack_kernel, n_dp), "pack",
-        [shape(rank, both)] * n_dp, [SMEM, ANY, ANY, ANY], [ANY] * n_dp,
-        [pltpu.SemaphoreType.DMA((2 * n_dp,))],
-    )(table, down, up, pieces[0])
-    maps = [maps[0]] + [shift(maps[s], "dp", s) for s in range(1, n_dp)]
-    pieces = [shift(pieces[s - 1], "mp", s) for s in range(1, n_mp)]
-    gy_got = [shift(after(gy, maps[0], *pieces), "mp", s) for s in range(1, n_mp)]
-    pieces = [after(piece, maps[0]) for piece in pieces]
+    packed = call(
+        functools.partial(pack_kernel, n_dp, n_mp, n_share), "pack",
+        [shape(rank, both)] * n_dp + [shape(part, cols)] * n_other,
+        [SMEM, ANY, ANY, ANY], [VMEM] * (n_dp + n_other),
+        [pltpu.SemaphoreType.DMA((2 * n_dp + n_other,))], mib=60,
+    )(table, down, up, w)
+    gy_got = [shift(gy, "mp", s) for s in range(1, n_mp)]
+    maps = [packed[0]] + [shift(packed[s], "dp", s) for s in range(1, n_dp)]
+    pieces = [shift(packed[n_dp + s - 1], "mp", s) for s in range(1, n_mp)]
+
+    uh = call(
+        functools.partial(reduce_kernel, n_dp), "uh",
+        shape(tok, 2 * rank), [SMEM, ANY] + [VMEM] * (2 + n_dp), VMEM,
+        [pltpu.VMEM((n_dp * rank, both), BF16)],
+    )(owner, gy_got[0], x, gy, *maps)
+    uhs = [uh] + [shift(uh, "mp", s) for s in range(1, n_mp)]
+
+    *grads, u_wide, h_wide = call(
+        functools.partial(grad_kernel, n_dp, n_mp), "grads",
+        [shape(rank, both)] * n_dp + [shape(tok, n_dp * rank)] * 2,
+        [SMEM] + [VMEM] * (2 + n_mp), [VMEM] * (n_dp + 2),
+    )(owner, x, gy, *uhs)
+    grads = [grads[0]] + [shift(grads[s], "dp", n_dp - s) for s in range(1, n_dp)]
+
     parts = []
     for piece in pieces:
         for j in range(n_groups):
-            one = shift(piece, "groups", j) if j else piece
-            parts += [shift(one, "pair", q) if q else one for q in range(n_pair)]
-
-    uh = call(
-        functools.partial(reduce_kernel, n_dp), "uh",
-        shape(tok, 2 * rank), [SMEM] + [VMEM] * (2 + n_dp), VMEM,
-        [pltpu.VMEM((n_dp * rank, both), BF16)], flops=UHCOST,
-    )(owner, x, gy, *maps)
-    uhs = [uh] + [shift(uh, "mp", s) for s in range(1, n_mp)]
-
-    *grads, u_wide, h_wide = call(
-        functools.partial(grad_kernel, n_dp, n_mp), "grads",
-        [shape(rank, both)] * n_dp + [shape(tok, n_dp * rank)] * 2,
-        [SMEM, ANY] + [VMEM] * (2 + n_mp), [VMEM] * (n_dp + 2),
-    )(owner, gy_got[0], x, gy, *uhs)
-    grads = [grads[0]] + [shift(grads[s], "dp", n_dp - s) for s in range(1, n_dp)]
+            one = shift(after(piece, uh), "groups", j) if j else piece
+            parts += [shift(after(one, h_wide), "pair", q) if q else one for q in range(n_pair)]
 
     sent = call(
         functools.partial(send_kernel, n_groups, n_pair, feat, n_mp), "y_send",
@@ -271,7 +261,7 @@
         functools.partial(own_kernel, n_dp), "y_own",
         shape(tok, cols, dtype=F32),
         [whole(*w.shape), row_block(feat), row_block(n_dp * rank)] + [whole(rank, both)] * n_dp,
-        row_block(cols), [pltpu.VMEM((n_dp * rank, cols), BF16)], grid=(TILES,),
+        row_block(cols), [pltpu.VMEM((n_dp * rank, cols), BF16)], grid=(TILES,), flops=LONG,
     )(w, x, u_wide, *maps)
 
     back = call(
@@ -284,8 +274,8 @@
 
     summed = call(
         functools.partial(site_kernel, n_dp), "sites",
-        shape(sites, rank, both), [SMEM, ANY] + [VMEM] * n_dp, VMEM,
-    )(table, back, *grads)
+        shape(sites, rank, both), [SMEM, ANY, ANY] + [VMEM] * n_dp, VMEM,
+    )(table, back, y_own, *grads)
     halves = [summed] + [shift(summed, "pair", q) for q in range(1, n_pair)]
     down_grad, up_grad = call(
         functools.partial(last_kernel, feat), "gradients",

time: 113 us -> 67.5 us (0.60)
  Pallas kernels: 65.4 us -> 16.1 us
  local copies, waits for them, and re-layouts: 0 us -> 2.36 us
    pallas_call x2 -> x1, Pallas kernels: 34.8 us -> 3.04 us  [shards(): call(functools.partial(pack_kernel, n_dp, n_mp, n_share), 'pack', [shape(...]
    pallas_call x1, Pallas kernels: 5.08 us -> 1.57 us  [shards(): call(functools.partial(own_kernel, n_dp), 'y_own', shape(tok, cols, dtype...]
    pallas_call x1, Pallas kernels: 4.32 us -> 1.44 us  [shards(): call(functools.partial(send_kernel, n_groups, n_pair, feat, n_mp), 'y_sen...]
    pallas_call x1, Pallas kernels: 6.23 us -> 3.51 us  [shards(): call(functools.partial(back_kernel, n_dp, n_mp), 'back', shape(tok, feat)...]
    unnamed x0 -> x16, local copies, waits for them, and re-layouts: none -> 2.36 us
    pallas_call x1, Pallas kernels: 3.68 us -> 1.55 us  [shards(): call(functools.partial(grad_kernel, n_dp, n_mp), 'grads', [shape(rank, bo...]
    pallas_call x1, Pallas kernels: 3.67 us -> 1.7 us  [shards(): call(functools.partial(reduce_kernel, n_dp), 'uh', shape(tok, 2 * rank),...]
    pallas_call x1, Pallas kernels: 3.26 us -> 1.5 us  [shards(): call(add_kernel, 'y_add', shape(tok, cols), [row_block(cols)] * n_mp, row...]
  transfers between devices with their start and end apart: 14 -> 14, of which waited for: 4 -> 6; matrix products, arithmetic and copies ran while one was open for 0% -> 0% of each run, Pallas kernels for 43% -> 22%
where the time goes in v5:
time: 67.5 us; the launch traced here: 67.3 us
  waiting for transfers between devices  27.2 us (40%)
  starting transfers between devices  20.8 us (31%)
  Pallas kernels  16.1 us (24%)
  local copies, waits for them, and re-layouts  2.36 us (3%)
  between operations  0.79 us (1%)
    ppermute x14, waiting for transfers between devices, shift(): lax.ppermute(value, axis, [(i, (i + by) % size) for i in range(size)])  27.2 us
    ppermute x14, starting transfers between devices, shift(): lax.ppermute(value, axis, [(i, (i + by) % size) for i in range(size)])  20.8 us
    pallas_call x1, Pallas kernels, shards(): call(functools.partial(back_kernel, n_dp, n_mp), 'back', shape(tok, feat)...  3.51 us
    pallas_call x1, Pallas kernels, shards(): call(functools.partial(pack_kernel, n_dp, n_mp, n_share), 'pack', [shape(...  3.04 us
    unnamed x16, local copies, waits for them, and re-layouts  2.36 us
    pallas_call x1, Pallas kernels, shards(): call(functools.partial(reduce_kernel, n_dp), 'uh', shape(tok, 2 * rank),...  1.7 us
    pallas_call x1, Pallas kernels, shards(): call(functools.partial(own_kernel, n_dp), 'y_own', shape(tok, cols, dtype...  1.57 us
    pallas_call x1, Pallas kernels, shards(): call(functools.partial(grad_kernel, n_dp, n_mp), 'grads', [shape(rank, bo...  1.55 us
  transfers between devices with their start and end apart: 14, of which 6 were waited for; matrix products, arithmetic and copies ran while one was open for 0% of the time, Pallas kernels for 22%

profile of v5, /device:TPU:0, one launch (start us, length us, event | category | flops | bytes accessed | tf_op | source)
XLA Modules:
  0.0 67.3 jit_solution(937695197642407281)
XLA Ops:
  0.7 3.0 %collective-permute-start = (bf16[768,512]{1,0:T(8,128)(2,1)}, bf16[768,512]{1,0:T(8,128)(2,1)S(1)}, u32[]{:S(2)}, u32[]{:S(2)}) collective-permute-start(bf16[768,512]{1,0:T(8,128)(2,1)} %gy.5), channel_id=1, source_target_pairs={{0,2},{2,0},{1,3},{3,1},{4,6},{6,4},{5,7},{7,5},{8,10},{10,8},{9,1... | collective-permute-start | bytes 2359304 | tf_op jit(solution)/shard_map/ppermute | solution.py:35
  3.7 3.0 %pack.1 = (bf16[64,1536]{1,0:T(8,128)(2,1)}, bf16[64,1536]{1,0:T(8,128)(2,1)}, bf16[64,1536]{1,0:T(8,128)(2,1)}, bf16[64,1536]{1,0:T(8,128)(2,1)}, bf16[256,512]{1,0:T(8,128)(2,1)}) custom-call(s32[1,2,4]{2,1,0:T(2,128)} %table.3, bf16[2,64,1024]{2,1,0:T(8,128)(2,1)} %bitcast.2, bf16[2,64,512]{2,1,0:T(8,128)(2,1)} %up.1, bf16[2048,512]{1,0:T(8,128)(2,1)} %w.5), custom_call_target="tpu_custom_call" | custom-call | flops 1 | bytes 1 | tf_op jit(solution)/shard_map/pack/pallas_call | solution.py:220
  6.7 0.2 collective-permute-start.5
  6.9 2.1 %collective-permute-start.1 = (bf16[64,1536]{1,0:T(8,128)(2,1)}, bf16[64,1536]{1,0:T(8,128)(2,1)S(1)}, u32[]{:S(2)}, u32[]{:S(2)}) collective-permute-start(bf16[64,1536]{1,0:T(8,128)(2,1)} %get-tuple-element.23), channel_id=1, source_target_pairs={{0,4},{4,8},{8,12},{12,0},{1,5},{5,9},{9,13},{13,1},{2,6},{6,10},{... | collective-permute-start | bytes 589832 | tf_op jit(solution)/shard_map/ppermute | solution.py:35
  9.0 2.6 %collective-permute-start.2 = (bf16[64,1536]{1,0:T(8,128)(2,1)}, bf16[64,1536]{1,0:T(8,128)(2,1)S(1)}, u32[]{:S(2)}, u32[]{:S(2)}) collective-permute-start(bf16[64,1536]{1,0:T(8,128)(2,1)} %get-tuple-element.24), channel_id=1, source_target_pairs={{0,8},{4,12},{8,0},{12,4},{1,9},{5,13},{9,1},{13,5},{2,10},{6,14},... | collective-permute-start | bytes 589832 | tf_op jit(solution)/shard_map/ppermute | solution.py:35
  11.6 1.3 %collective-permute-start.3 = (bf16[64,1536]{1,0:T(8,128)(2,1)}, bf16[64,1536]{1,0:T(8,128)(2,1)S(1)}, u32[]{:S(2)}, u32[]{:S(2)}) collective-permute-start(bf16[64,1536]{1,0:T(8,128)(2,1)} %get-tuple-element.25), channel_id=1, source_target_pairs={{0,12},{4,0},{8,4},{12,8},{1,13},{5,1},{9,5},{13,9},{2,14},{6,2},{... | collective-permute-start | bytes 589832 | tf_op jit(solution)/shard_map/ppermute | solution.py:35
  13.0 4.2 %collective-permute-done.1.refs_1_.refs_3_ = bf16[64,1536]{1,0:T(8,128)(2,1)S(1)} collective-permute-done((bf16[64,1536]{1,0:T(8,128)(2,1)}, bf16[64,1536]{1,0:T(8,128)(2,1)S(1)}, u32[]{:S(2)}, u32[]{:S(2)}) %collective-permute-start.1) | collective-permute-done | bytes 196640 | tf_op jit(solution)/shard_map/ppermute | solution.py:35
  17.2 7.0 %collective-permute-done.2.refs_2_.refs_4_ = bf16[64,1536]{1,0:T(8,128)(2,1)S(1)} collective-permute-done((bf16[64,1536]{1,0:T(8,128)(2,1)}, bf16[64,1536]{1,0:T(8,128)(2,1)S(1)}, u32[]{:S(2)}, u32[]{:S(2)}) %collective-permute-start.2) | collective-permute-done | bytes 196640 | tf_op jit(solution)/shard_map/ppermute | solution.py:35
  24.2 0.0 copy-start.4
  24.2 0.9 %copy-done.4 = bf16[64,1536]{1,0:T(8,128)(2,1)S(1)} copy-done((bf16[64,1536]{1,0:T(8,128)(2,1)S(1)}, bf16[64,1536]{1,0:T(8,128)(2,1)}, u32[]{:S(2)}) %copy-start.4) | copy-done | bytes 196632
  25.1 1.7 %uh.1.refs_0_ = bf16[768,128]{1,0:T(8,128)(2,1)S(1)} custom-call(s32[12]{0:T(128)S(1)} %copy-done.7, bf16[768,512]{1,0:T(8,128)(2,1)S(1)} %collective-permute-done._.refs_0_, bf16[768,1024]{1,0:T(8,128)(2,1)S(1)} %copy-done, bf16[768,512]{1,0:T(8,128)(2,1)S(1)} %copy-done.2, bf16[64,1536]{1,0:T(8,128)(2,1)S(1)} %copy-done.4, ...), custom_call_target="tpu_custom_call" | custom-call | flops 1 | bytes 1 | tf_op jit(solution)/shard_map/uh/pallas_call | solution.py:230
  26.8 0.3 collective-permute-done.5.refs_0_
  27.0 1.8 %collective-permute-start.7 = (bf16[256,512]{1,0:T(8,128)(2,1)S(1)}, bf16[256,512]{1,0:T(8,128)(2,1)S(1)}, u32[]{:S(2)}, u32[]{:S(2)}) collective-permute-start(bf16[256,512]{1,0:T(8,128)(2,1)S(1)} %collective-permute-done.5.refs_0_), channel_id=1, source_target_pairs={{0,16},{16,0},{1,17},{17,1},{2,18},{18,2},{3,19},{19,3},{4,20},{20... | collective-permute-start | bytes 786440 | tf_op jit(solution)/shard_map/ppermute | solution.py:35
  28.8 1.5 %collective-permute-start.4 = (bf16[768,128]{1,0:T(8,128)(2,1)S(1)}, bf16[768,128]{1,0:T(8,128)(2,1)S(1)}, u32[]{:S(2)}, u32[]{:S(2)}) collective-permute-start(bf16[768,128]{1,0:T(8,128)(2,1)S(1)} %uh.1.refs_0_), channel_id=1, source_target_pairs={{0,2},{2,0},{1,3},{3,1},{4,6},{6,4},{5,7},{7,5},{8,10},{10,8},{9,1... | collective-permute-start | bytes 589832 | tf_op jit(solution)/shard_map/ppermute | solution.py:35
  30.3 4.5 %collective-permute-done.4.refs_1_ = bf16[768,128]{1,0:T(8,128)(2,1)S(1)} collective-permute-done((bf16[768,128]{1,0:T(8,128)(2,1)S(1)}, bf16[768,128]{1,0:T(8,128)(2,1)S(1)}, u32[]{:S(2)}, u32[]{:S(2)}) %collective-permute-start.4) | collective-permute-done | bytes 196640 | tf_op jit(solution)/shard_map/ppermute | solution.py:35
  34.8 1.6 %grads.1 = (bf16[64,1536]{1,0:T(8,128)(2,1)S(1)}, bf16[64,1536]{1,0:T(8,128)(2,1)S(1)}, bf16[64,1536]{1,0:T(8,128)(2,1)S(1)}, bf16[64,1536]{1,0:T(8,128)(2,1)S(1...) custom-call(s32[12]{0:T(128)S(1)} %copy-done.7, bf16[768,1024]{1,0:T(8,128)(2,1)S(1)} %copy-done, ...), custom_call_target="tpu_custom_call" | custom-call | flops 1 | bytes 1 | tf_op jit(solution)/shard_map/grads/pallas_call | solution.py:237
  36.4 0.1 collective-permute-start.6
  36.5 0.5 collective-permute-start.8
  37.0 5.0 %collective-permute-start.10 = (bf16[64,1536]{1,0:T(8,128)(2,1)S(1)}, bf16[64,1536]{1,0:T(8,128)(2,1)S(1)}, u32[]{:S(2)}, u32[]{:S(2)}) collective-permute-start(bf16[64,1536]{1,0:T(8,128)(2,1)S(1)} %get-tuple-element.35), channel_id=1, source_target_pairs={{0,12},{4,0},{8,4},{12,8},{1,13},{5,1},{9,5},{13,9},{2,14},{6,2},{... | collective-permute-start | bytes 589832 | tf_op jit(solution)/shard_map/ppermute | solution.py:35
  42.0 1.3 %collective-permute-start.11 = (bf16[64,1536]{1,0:T(8,128)(2,1)S(1)}, bf16[64,1536]{1,0:T(8,128)(2,1)S(1)}, u32[]{:S(2)}, u32[]{:S(2)}) collective-permute-start(bf16[64,1536]{1,0:T(8,128)(2,1)S(1)} %get-tuple-element.36), channel_id=1, source_target_pairs={{0,8},{4,12},{8,0},{12,4},{1,9},{5,13},{9,1},{13,5},{2,10},{6,14},... | collective-permute-start | bytes 589832 | tf_op jit(solution)/shard_map/ppermute | solution.py:35
  43.2 1.4 %y_send.1 = (bf16[768,512]{1,0:T(8,128)(2,1)S(1)}, bf16[1024,512]{1,0:T(8,128)(2,1)S(1)}) custom-call(bf16[768,256]{1,0:T(8,128)(2,1)S(1)} %get-tuple-element.26.wide._, bf16[768,1024]{1,0:T(8,128)(2,1)S(1)} %copy-done, bf16[256,512]{1,0:T(8,128)(2,1)S(1)} %collective-permute-done.5.refs_0_, bf16[256,512]{1,0:T(8,128)(2,1)S(1)} %collective-permute-done.6.refs_1_, ...), custom_call_target="tpu_custom_call" | custom-call | flops 1 | bytes 1 | tf_op jit(solution)/shard_map/y_send/pallas_call | solution.py:250
  44.7 1.4 %collective-permute-start.9 = (bf16[768,512]{1,0:T(8,128)(2,1)S(1)}, bf16[768,512]{1,0:T(8,128)(2,1)S(1)}, u32[]{:S(2)}, u32[]{:S(2)}) collective-permute-start(bf16[768,512]{1,0:T(8,128)(2,1)S(1)} %get-tuple-element.32), channel_id=1, source_target_pairs={{0,2},{2,0},{1,3},{3,1},{4,6},{6,4},{5,7},{7,5},{8,10},{10,8},{9,1... | collective-permute-start | bytes 2359304 | tf_op jit(solution)/shard_map/ppermute | solution.py:35
  46.1 1.6 %y_own.1.refs_0_.__ = f32[768,512]{1,0:T(8,128)S(1)} custom-call(bf16[2048,512]{1,0:T(8,128)(2,1)S(1)} %copy-done.1, bf16[768,1024]{1,0:T(8,128)(2,1)S(1)} %copy-done, bf16[768,256]{1,0:T(8,128)(2,1)S(1)} %get-tuple-element.26.wide._, bf16[64,1536]{1,0:T(8,128)(2,1)S(1)} %copy-done.5, bf16[64,1536]{1,0:T(8,128)(2,1)S(1)} %collective-permute-done.1.refs_1_.refs_3_, ...), custom_call_target="tpu_custom_call" | custom-call | flops 7000000000 | bytes 1 | tf_op jit(solution)/shard_map/y_own/pallas_call | solution.py:260
  47.7 0.0 copy-start.6
  47.7 3.5 %back.1._ = bf16[768,1024]{1,0:T(8,128)(2,1)} custom-call(bf16[2048,512]{1,0:T(8,128)(2,1)S(1)} %copy-done.1, bf16[768,512]{1,0:T(8,128)(2,1)S(1)} %copy-done.2, bf16[768,256]{1,0:T(8,128)(2,1)S(1)} %get-tuple-element.28.wide, bf16[768,512]{1,0:T(8,128)(2,1)S(1)} %collective-permute-done._.refs_0_, bf16[1024,512]{1,0:T(8,128)(2,1)S(1)} %get-tuple-element.33.refs_1_, ...), custom_call_target="tpu_custom_call" | custom-call | flops 1 | bytes 1 | tf_op jit(solution)/shard_map/back/pallas_call | solution.py:267
  51.2 9.5 %collective-permute-done.11.refs_2_ = bf16[64,1536]{1,0:T(8,128)(2,1)S(1)} collective-permute-done((bf16[64,1536]{1,0:T(8,128)(2,1)S(1)}, bf16[64,1536]{1,0:T(8,128)(2,1)S(1)}, u32[]{:S(2)}, u32[]{:S(2)}) %collective-permute-start.11) | collective-permute-done | bytes 196640 | tf_op jit(solution)/shard_map/ppermute | solution.py:35
  60.7 1.4 %copy-done.3 = bf16[768,1024]{1,0:T(8,128)(2,1)S(1)} copy-done((bf16[768,1024]{1,0:T(8,128)(2,1)S(1)}, bf16[768,1024]{1,0:T(8,128)(2,1)}, u32[]{:S(2)}) %copy-start.3) | copy-done | bytes 1572888
  62.1 0.9 %sites.1.refs_0_ = bf16[2,64,1536]{2,1,0:T(8,128)(2,1)S(1)} custom-call(s32[1,2,4]{2,1,0:T(2,128)S(1)} %copy-done.6, bf16[768,1024]{1,0:T(8,128)(2,1)S(1)} %copy-done.3, f32[768,512]{1,0:T(8,128)S(1)} %y_own.1.refs_0_.__, bf16[64,1536]{1,0:T(8,128)(2,1)S(1)} %get-tuple-element.34.refs_0_, bf16[64,1536]{1,0:T(8,128)(2,1)S(1)} %collective-permute-done.10.refs_1_, ...), custom_call_target="tpu_custom_call" | custom-call | flops 1 | bytes 1 | tf_op jit(solution)/shard_map/sites/pallas_call | solution.py:275
  63.0 0.1 collective-permute-start.13
  63.1 1.7 %collective-permute-done.13.refs_1_ = bf16[2,64,1536]{2,1,0:T(8,128)(2,1)S(1)} collective-permute-done((bf16[2,64,1536]{2,1,0:T(8,128)(2,1)S(1)}, bf16[2,64,1536]{2,1,0:T(8,128)(2,1)S(1)}, u32[]{:S(2)}, u32[]{:S(2)}) %collective-permute-start.13) | collective-permute-done | bytes 393248 | tf_op jit(solution)/shard_map/ppermute | solution.py:35
  64.8 0.9 %gradients.1 = (f32[2,64,1024]{2,1,0:T(8,128)}, f32[2,64,512]{2,1,0:T(8,128)}) custom-call(bf16[2,64,1536]{2,1,0:T(8,128)(2,1)S(1)} %sites.1.refs_0_, bf16[2,64,1536]{2,1,0:T(8,128)(2,1)S(1)} %collective-permute-done.13.refs_1_), custom_call_target="tpu_custom_call" | custom-call | flops 1 | bytes 1 | tf_op jit(solution)/shard_map/gradients/pallas_call | solution.py:280
  65.8 1.5 %y_add.1 = bf16[768,512]{1,0:T(8,128)(2,1)} custom-call(f32[768,512]{1,0:T(8,128)S(1)} %y_own.1.refs_0_.__, bf16[768,512]{1,0:T(8,128)(2,1)S(1)} %collective-permute-done.9.refs_1_), custom_call_target="tpu_custom_call" | custom-call | flops 1 | bytes 1 | tf_op jit(solution)/shard_map/y_add/pallas_call | solution.py:286
  (21 shorter events, 0.1 us)
Async XLA Ops:
  0.6 23.5 %copy-start.2 = (bf16[768,512]{1,0:T(8,128)(2,1)S(1)}, bf16[768,512]{1,0:T(8,128)(2,1)}, u32[]{:S(2)}) copy-start(bf16[768,512]{1,0:T(8,128)(2,1)} %gy.5) | copy-start | bytes 2359300
  0.6 23.5 %copy-start = (bf16[768,1024]{1,0:T(8,128)(2,1)S(1)}, bf16[768,1024]{1,0:T(8,128)(2,1)}, u32[]{:S(2)}) copy-start(bf16[768,1024]{1,0:T(8,128)(2,1)} %x.7) | copy-start | bytes 4718596
  0.7 23.5 %copy-start.7 = (s32[12]{0:T(128)S(1)}, s32[12]{0:T(128)}, u32[]{:S(2)}) copy-start(s32[12]{0:T(128)} %owner.3) | copy-start | bytes 148
  0.7 23.5 %collective-permute-start = (bf16[768,512]{1,0:T(8,128)(2,1)}, bf16[768,512]{1,0:T(8,128)(2,1)S(1)}, u32[]{:S(2)}, u32[]{:S(2)}) collective-permute-start(bf16[768,512]{1,0:T(8,128)(2,1)} %gy.5), channel_id=1, source_target_pairs={{0,2},{2,0},{1,3},{3,1},{4,6},{6,4},{5,7},{7,5},{8,10},{10,8},{9,1... | collective-permute-start | bytes 2359304 | tf_op jit(solution)/shard_map/ppermute | solution.py:35
  6.7 20.3 %collective-permute-start.5 = (bf16[256,512]{1,0:T(8,128)(2,1)}, bf16[256,512]{1,0:T(8,128)(2,1)S(1)}, u32[]{:S(2)}, u32[]{:S(2)}) collective-permute-start(bf16[256,512]{1,0:T(8,128)(2,1)} %get-tuple-element.27), channel_id=1, source_target_pairs={{0,2},{2,0},{1,3},{3,1},{4,6},{6,4},{5,7},{7,5},{8,10},{10,8},{9,1... | collective-permute-start | bytes 786440 | tf_op jit(solution)/shard_map/ppermute | solution.py:35
  6.9 10.2 %collective-permute-start.1 = (bf16[64,1536]{1,0:T(8,128)(2,1)}, bf16[64,1536]{1,0:T(8,128)(2,1)S(1)}, u32[]{:S(2)}, u32[]{:S(2)}) collective-permute-start(bf16[64,1536]{1,0:T(8,128)(2,1)} %get-tuple-element.23), channel_id=1, source_target_pairs={{0,4},{4,8},{8,12},{12,0},{1,5},{5,9},{9,13},{13,1},{2,6},{6,10},{... | collective-permute-start | bytes 589832 | tf_op jit(solution)/shard_map/ppermute | solution.py:35
  9.0 15.1 %collective-permute-start.2 = (bf16[64,1536]{1,0:T(8,128)(2,1)}, bf16[64,1536]{1,0:T(8,128)(2,1)S(1)}, u32[]{:S(2)}, u32[]{:S(2)}) collective-permute-start(bf16[64,1536]{1,0:T(8,128)(2,1)} %get-tuple-element.24), channel_id=1, source_target_pairs={{0,8},{4,12},{8,0},{12,4},{1,9},{5,13},{9,1},{13,5},{2,10},{6,14},... | collective-permute-start | bytes 589832 | tf_op jit(solution)/shard_map/ppermute | solution.py:35
  11.6 12.5 %collective-permute-start.3 = (bf16[64,1536]{1,0:T(8,128)(2,1)}, bf16[64,1536]{1,0:T(8,128)(2,1)S(1)}, u32[]{:S(2)}, u32[]{:S(2)}) collective-permute-start(bf16[64,1536]{1,0:T(8,128)(2,1)} %get-tuple-element.25), channel_id=1, source_target_pairs={{0,12},{4,0},{8,4},{12,8},{1,13},{5,1},{9,5},{13,9},{2,14},{6,2},{... | collective-permute-start | bytes 589832 | tf_op jit(solution)/shard_map/ppermute | solution.py:35
  24.2 0.9 %copy-start.4 = (bf16[64,1536]{1,0:T(8,128)(2,1)S(1)}, bf16[64,1536]{1,0:T(8,128)(2,1)}, u32[]{:S(2)}) copy-start(bf16[64,1536]{1,0:T(8,128)(2,1)} %get-tuple-element.22.refs_0_.refs_2_) | copy-start | bytes 589828
  27.0 9.5 %collective-permute-start.7 = (bf16[256,512]{1,0:T(8,128)(2,1)S(1)}, bf16[256,512]{1,0:T(8,128)(2,1)S(1)}, u32[]{:S(2)}, u32[]{:S(2)}) collective-permute-start(bf16[256,512]{1,0:T(8,128)(2,1)S(1)} %collective-permute-done.5.refs_0_), channel_id=1, source_target_pairs={{0,16},{16,0},{1,17},{17,1},{2,18},{18,2},{3,19},{19,3},{4,20},{20... | collective-permute-start | bytes 786440 | tf_op jit(solution)/shard_map/ppermute | solution.py:35
  28.8 6.0 %collective-permute-start.4 = (bf16[768,128]{1,0:T(8,128)(2,1)S(1)}, bf16[768,128]{1,0:T(8,128)(2,1)S(1)}, u32[]{:S(2)}, u32[]{:S(2)}) collective-permute-start(bf16[768,128]{1,0:T(8,128)(2,1)S(1)} %uh.1.refs_0_), channel_id=1, source_target_pairs={{0,2},{2,0},{1,3},{3,1},{4,6},{6,4},{5,7},{7,5},{8,10},{10,8},{9,1... | collective-permute-start | bytes 589832 | tf_op jit(solution)/shard_map/ppermute | solution.py:35
  36.4 9.7 %copy-start.1 = (bf16[2048,512]{1,0:T(8,128)(2,1)S(1)}, bf16[2048,512]{1,0:T(8,128)(2,1)}, u32[]{:S(2)}) copy-start(bf16[2048,512]{1,0:T(8,128)(2,1)} %w.5) | copy-start | bytes 6291460
  36.4 9.7 %copy-start.5 = (bf16[64,1536]{1,0:T(8,128)(2,1)S(1)}, bf16[64,1536]{1,0:T(8,128)(2,1)}, u32[]{:S(2)}) copy-start(bf16[64,1536]{1,0:T(8,128)(2,1)} %get-tuple-element.22.refs_0_.refs_2_) | copy-start | bytes 589828
  36.4 6.8 %collective-permute-start.6 = (bf16[256,512]{1,0:T(8,128)(2,1)S(1)}, bf16[256,512]{1,0:T(8,128)(2,1)S(1)}, u32[]{:S(2)}, u32[]{:S(2)}) collective-permute-start(bf16[256,512]{1,0:T(8,128)(2,1)S(1)} %collective-permute-done.5.refs_0_), channel_id=1, source_target_pairs={{0,1},{1,0},{2,3},{3,2},{4,5},{5,4},{6,7},{7,6},{8,9},{9,8},{10,11... | collective-permute-start | bytes 786440 | tf_op jit(solution)/shard_map/ppermute | solution.py:35
  36.5 6.7 %collective-permute-start.8 = (bf16[256,512]{1,0:T(8,128)(2,1)S(1)}, bf16[256,512]{1,0:T(8,128)(2,1)S(1)}, u32[]{:S(2)}, u32[]{:S(2)}) collective-permute-start(bf16[256,512]{1,0:T(8,128)(2,1)S(1)} %collective-permute-done.7.refs_2_), channel_id=1, source_target_pairs={{0,1},{1,0},{2,3},{3,2},{4,5},{5,4},{6,7},{7,6},{8,9},{9,8},{10,11... | collective-permute-start | bytes 786440 | tf_op jit(solution)/shard_map/ppermute | solution.py:35
  37.0 14.2 %collective-permute-start.10 = (bf16[64,1536]{1,0:T(8,128)(2,1)S(1)}, bf16[64,1536]{1,0:T(8,128)(2,1)S(1)}, u32[]{:S(2)}, u32[]{:S(2)}) collective-permute-start(bf16[64,1536]{1,0:T(8,128)(2,1)S(1)} %get-tuple-element.35), channel_id=1, source_target_pairs={{0,12},{4,0},{8,4},{12,8},{1,13},{5,1},{9,5},{13,9},{2,14},{6,2},{... | collective-permute-start | bytes 589832 | tf_op jit(solution)/shard_map/ppermute | solution.py:35
  42.0 18.8 %collective-permute-start.11 = (bf16[64,1536]{1,0:T(8,128)(2,1)S(1)}, bf16[64,1536]{1,0:T(8,128)(2,1)S(1)}, u32[]{:S(2)}, u32[]{:S(2)}) collective-permute-start(bf16[64,1536]{1,0:T(8,128)(2,1)S(1)} %get-tuple-element.36), channel_id=1, source_target_pairs={{0,8},{4,12},{8,0},{12,4},{1,9},{5,13},{9,1},{13,5},{2,10},{6,14},... | collective-permute-start | bytes 589832 | tf_op jit(solution)/shard_map/ppermute | solution.py:35
  43.2 17.5 %collective-permute-start.12 = (bf16[64,1536]{1,0:T(8,128)(2,1)S(1)}, bf16[64,1536]{1,0:T(8,128)(2,1)S(1)}, u32[]{:S(2)}, u32[]{:S(2)}) collective-permute-start(bf16[64,1536]{1,0:T(8,128)(2,1)S(1)} %get-tuple-element.37), channel_id=1, source_target_pairs={{0,4},{4,8},{8,12},{12,0},{1,5},{5,9},{9,13},{13,1},{2,6},{6,10},{... | collective-permute-start | bytes 589832 | tf_op jit(solution)/shard_map/ppermute | solution.py:35
  44.7 21.1 %collective-permute-start.9 = (bf16[768,512]{1,0:T(8,128)(2,1)S(1)}, bf16[768,512]{1,0:T(8,128)(2,1)S(1)}, u32[]{:S(2)}, u32[]{:S(2)}) collective-permute-start(bf16[768,512]{1,0:T(8,128)(2,1)S(1)} %get-tuple-element.32), channel_id=1, source_target_pairs={{0,2},{2,0},{1,3},{3,1},{4,6},{6,4},{5,7},{7,5},{8,10},{10,8},{9,1... | collective-permute-start | bytes 2359304 | tf_op jit(solution)/shard_map/ppermute | solution.py:35
  47.7 13.0 %copy-start.6 = (s32[1,2,4]{2,1,0:T(2,128)S(1)}, s32[1,2,4]{2,1,0:T(2,128)}, u32[]{:S(2)}) copy-start(s32[1,2,4]{2,1,0:T(2,128)} %table.3) | copy-start | bytes 100
  60.7 1.4 %copy-start.3 = (bf16[768,1024]{1,0:T(8,128)(2,1)S(1)}, bf16[768,1024]{1,0:T(8,128)(2,1)}, u32[]{:S(2)}) copy-start(bf16[768,1024]{1,0:T(8,128)(2,1)} %back.1._) | copy-start | bytes 4718596
  63.0 1.8 %collective-permute-start.13 = (bf16[2,64,1536]{2,1,0:T(8,128)(2,1)S(1)}, bf16[2,64,1536]{2,1,0:T(8,128)(2,1)S(1)}, u32[]{:S(2)}, u32[]{:S(2)}) collective-permute-start(bf16[2,64,1536]{2,1,0:T(8,128)(2,1)S(1)} %sites.1.refs_0_), channel_id=1, source_target_pairs={{0,1},{1,0},{2,3},{3,2},{4,5},{5,4},{6,7},{7,6},{8,9},{9,8},{10,11... | collective-permute-start | bytes 1179656 | tf_op jit(solution)/shard_map/ppermute | solution.py:35

commit v6 on v4

--- a/solution.py
+++ b/solution.py
@@ -67,28 +67,35 @@
 
 
 def pack_kernel(n_dp, n_mp, n_pair, table, down, up, w, *refs):
-    ups, downs, pieces, sem = refs[:n_dp], refs[n_dp:2 * n_dp], refs[2 * n_dp:-1], refs[-1]
+    away = n_dp - 1
+    ups, downs, pieces, sem = refs[:away], refs[away:2 * away], refs[2 * away:-1], refs[-1]
     feat = w.shape[0] // n_mp
     part = feat // n_pair
     copies = []
-    for s in range(n_dp):
-        site = wanted_site(table, n_dp, s)
+    for s in range(away):
+        site = wanted_site(table, n_dp, s + 1)
         copies.append(pltpu.make_async_copy(up.at[site], ups[s], sem.at[s]))
-        copies.append(pltpu.make_async_copy(down.at[site], downs[s], sem.at[n_dp + s]))
+        copies.append(pltpu.make_async_copy(down.at[site], downs[s], sem.at[away + s]))
     for s in range(1, n_mp):
         row = lax.rem(lax.axis_index("mp") + s, n_mp) * feat + lax.axis_index("pair") * part
         row = pl.multiple_of(row, part)
-        copies.append(pltpu.make_async_copy(w.at[pl.ds(row, part)], pieces[s - 1], sem.at[2 * n_dp + s - 1]))
+        copies.append(pltpu.make_async_copy(w.at[pl.ds(row, part)], pieces[s - 1], sem.at[2 * away + s - 1]))
     run(copies)
 
 
-def reduce_kernel(n_dp, owner, act, _, *refs):
-    maps, out, wide = refs[:n_dp], refs[n_dp], refs[n_dp + 1]
-    rank = maps[0].shape[0]
+def gather_maps(n_dp, table, own, gots, wide):
+    rank = own.shape[1]
+    wide[:rank, :] = own[wanted_site(table, n_dp, 0)]
+    for s in range(1, n_dp):
+        wide[s * rank:(s + 1) * rank, :] = gots[s - 1][...]
+
+
+def reduce_kernel(n_dp, owner, table, act, _, own, *refs):
+    gots, out, wide = refs[:n_dp - 1], refs[n_dp - 1], refs[n_dp]
+    rank = own.shape[1]
     blocks = owner.shape[0]
     rows = act.shape[0] // blocks
-    for s in range(n_dp):
-        wide[s * rank:(s + 1) * rank, :] = maps[s][...]
+    gather_maps(n_dp, table, own, gots, wide)
     full = nt(act[...], wide[...])
     lane_slot = lax.broadcasted_iota(jnp.int32, (rows, n_dp * rank), 1) // rank
     folded = []
@@ -139,18 +146,18 @@
         outs[s][...] = nn(x[...], rows[s][...]).astype(BF16)
 
 
-def back_kernel(n_dp, n_mp, _, *refs):
-    w, gys, rows, wide, downs, out, own, maps = (
-        refs[0], refs[1:1 + n_mp], refs[1 + n_mp:2 * n_mp], refs[2 * n_mp],
-        refs[2 * n_mp + 1:-3], refs[-3], refs[-2], refs[-1],
+def back_kernel(n_dp, n_mp, table, _, *refs):
+    w, gys, rows, wide, own_down, downs, out, token, own, maps = (
+        refs[0], refs[1:1 + n_mp], refs[1 + n_mp:2 * n_mp], refs[2 * n_mp], refs[2 * n_mp + 1],
+        refs[2 * n_mp + 2:-4], refs[-4], refs[-3], refs[-2], refs[-1],
     )
-    rank, feat = downs[0].shape
+    feat = out.shape[1]
 
     @pl.when(pl.program_id(0) == 0)
     def _():
+        token[...] = jnp.zeros_like(token)
         own[...] = w[pl.ds(pl.multiple_of(lax.axis_index("mp") * feat, feat), feat), :]
-        for s in range(n_dp):
-            maps[s * rank:(s + 1) * rank, :] = downs[s][...]
+        gather_maps(n_dp, table, own_down, downs, maps)
 
     total = nt(gys[0][...], own[...]) + SCALE * nn(wide[...], maps[...])
     for gy, row in zip(gys[1:], rows):
@@ -158,15 +165,18 @@
     out[...] = total.astype(BF16)
 
 
-def own_kernel(n_dp, w, x, wide, *refs):
-    ups, out, maps = refs[:n_dp], refs[n_dp], refs[n_dp + 1]
-    rank = ups[0].shape[0]
+def own_kernel(n_dp, table, w, x, wide, own_up, *refs):
+    ups, out, picks, maps = refs[:n_dp - 1], refs[n_dp - 1], refs[n_dp], refs[n_dp + 1]
     feat = x.shape[1]
 
     @pl.when(pl.program_id(0) == 0)
     def _():
+        gather_maps(n_dp, table, own_up, ups, maps)
+        row = lax.broadcasted_iota(jnp.int32, picks.shape, 0)
+        total = jnp.zeros(picks.shape, jnp.int32)
         for s in range(n_dp):
-            maps[s * rank:(s + 1) * rank, :] = ups[s][...]
+            total = jnp.where(row == s, wanted_site(table, n_dp, s), total)
+        picks[...] = total
 
     own = w[pl.ds(pl.multiple_of(lax.axis_index("mp") * feat, feat), feat), :]
     out[...] = nn(x[...], own) + SCALE * nn(wide[...], maps[...])
@@ -179,13 +189,13 @@
     refs[-1][...] = total.astype(BF16)
 
 
-def site_kernel(n_dp, feat, table, *refs):
+def site_kernel(n_dp, feat, picks, _, *refs):
     downs, ups, out = refs[:n_dp], refs[n_dp:2 * n_dp], refs[-1]
     for site in range(out.shape[0]):
         for grads, lo, hi in ((downs, 0, feat), (ups, feat, out.shape[2])):
             total = jnp.zeros((out.shape[1], hi - lo), F32)
             for s in range(n_dp):
-                use = wanted_site(table, n_dp, s) == site
+                use = picks[s:s + 1, :1] == site
                 total = total + jnp.where(use, grads[s][...].astype(F32), 0.0)
             out[site, :, lo:hi] = total.astype(BF16)
 
@@ -212,22 +222,23 @@
     row_block = lambda width: pl.BlockSpec((tile, width), lambda i: (i, 0))
     whole = lambda *dims: pl.BlockSpec(dims, lambda i: (0,) * len(dims))
 
+    away = n_dp - 1
     packed = call(
         functools.partial(pack_kernel, n_dp, n_mp, n_pair), "pack",
-        [shape(rank, cols)] * n_dp + [shape(rank, feat)] * n_dp + [shape(part, cols)] * n_other,
-        [SMEM, ANY, ANY, ANY], [VMEM] * (2 * n_dp + n_other),
-        [pltpu.SemaphoreType.DMA((2 * n_dp + n_other,))], mib=64,
+        [shape(rank, cols)] * away + [shape(rank, feat)] * away + [shape(part, cols)] * n_other,
+        [SMEM, ANY, ANY, ANY], [VMEM] * (2 * away + n_other),
+        [pltpu.SemaphoreType.DMA((2 * away + n_other,))], mib=60,
     )(table, down, up, w)
-    pieces = [shift(packed[2 * n_dp + s - 1], "mp", s) for s in range(1, n_mp)]
-    ups = [packed[0]] + [shift(packed[s], "dp", s) for s in range(1, n_dp)]
-    downs = [packed[n_dp]] + [shift(packed[n_dp + s], "dp", s) for s in range(1, n_dp)]
-
-    def low_rank(act, maps, behind, name):
+    pieces = [shift(packed[2 * away + s - 1], "mp", s) for s in range(1, n_mp)]
+    ups = [shift(packed[s - 1], "dp", s) for s in range(1, n_dp)]
+    downs = [shift(after(packed[away + s - 1], ups[1 % away]), "dp", s) for s in range(1, n_dp)]
+
+    def low_rank(act, own, maps, behind, name):
         mine = call(
             functools.partial(reduce_kernel, n_dp), name + "_part",
-            shape(tok // 2, 2 * rank), [SMEM, VMEM, ANY] + [VMEM] * n_dp, VMEM,
+            shape(tok // 2, 2 * rank), [SMEM, SMEM, VMEM, ANY] + [VMEM] * n_dp, VMEM,
             [pltpu.VMEM((n_dp * rank, act.shape[1]), BF16)],
-        )(owner, act, behind, *maps)
+        )(owner, table, act, behind, own, *maps)
         return [mine] + [shift(mine, "mp", s) for s in range(1, n_mp)]
 
     def gradient(act, parts, behind, name, flops):
@@ -238,14 +249,14 @@
         )(owner, act, *behind, *parts)
         return [grads[0]] + [shift(grads[s], "dp", n_dp - s) for s in range(1, n_dp)], wide
 
-    h_parts = low_rank(gy, ups, packed[0], "h")
-    gy_got = [shift(after(gy, h_parts[0], *pieces), "mp", s) for s in range(1, n_mp)]
-    down_back, h_wide = gradient(x, h_parts, downs[1:], "down", GRAD_COST)
-    u_parts = low_rank(x, downs, h_wide, "u")
+    h_parts = low_rank(gy, up, ups, ups[0], "h")
+    gy_got = [shift(after(gy, *pieces), "mp", s) for s in range(1, n_mp)]
+    down_back, h_wide = gradient(x, h_parts, downs, "down", GRAD_COST)
+    u_parts = low_rank(x, down, downs, h_wide, "u")
 
     parts = []
     for piece in pieces:
-        parts += [piece] + [shift(after(piece, h_parts[0]), "pair", q) for q in range(1, n_pair)]
+        parts += [piece] + [shift(after(piece, h_wide), "pair", q) for q in range(1, n_pair)]
     sent = call(
         functools.partial(send_kernel, n_pair, feat, n_mp), "y_send",
         [shape(tok, cols)] * n_other + [shape(feat, cols)] * n_other,
@@ -257,25 +268,28 @@
     y_got = [shift(sent[s - 1], "mp", n_mp - s) for s in range(1, n_mp)]
     up_back, u_wide = gradient(gy, u_parts, down_back[2:] + gy_got, "up", GRAD_COST)
 
-    y_own = call(
+    y_own, picks = call(
         functools.partial(own_kernel, n_dp), "y_own",
-        shape(tok, cols, dtype=F32),
-        [whole(*w.shape), row_block(feat), row_block(n_dp * rank)] + [whole(rank, cols)] * n_dp,
-        row_block(cols), [pltpu.VMEM((n_dp * rank, cols), BF16)], grid=(TILES,),
-    )(w, x, u_wide, *ups)
-
-    back = call(
+        [shape(tok, cols, dtype=F32), shape(-(-n_dp // 8) * 8, 128, dtype=jnp.int32)],
+        [SMEM, whole(*w.shape), row_block(feat), row_block(n_dp * rank), whole(*up.shape)]
+        + [whole(rank, cols)] * away,
+        [row_block(cols), whole(-(-n_dp // 8) * 8, 128)],
+        [pltpu.VMEM((n_dp * rank, cols), BF16)], grid=(TILES,),
+    )(table, w, x, u_wide, up, *ups)
+
+    back, token = call(
         functools.partial(back_kernel, n_dp, n_mp), "back",
-        shape(tok, feat),
-        [ANY, whole(*w.shape)] + [row_block(cols)] * n_mp + [whole(feat, cols)] * n_other
-        + [row_block(n_dp * rank)] + [whole(rank, feat)] * n_dp,
-        row_block(feat), [pltpu.VMEM((feat, cols), BF16), pltpu.VMEM((n_dp * rank, feat), BF16)], grid=(TILES,),
-    )(u_wide, w, gy, *gy_got, *w_rows, h_wide, *downs)
+        [shape(tok, feat), shape(8, 128, dtype=F32)],
+        [SMEM, ANY, whole(*w.shape)] + [row_block(cols)] * n_mp + [whole(feat, cols)] * n_other
+        + [row_block(n_dp * rank), whole(*down.shape)] + [whole(rank, feat)] * away,
+        [row_block(feat), whole(8, 128)],
+        [pltpu.VMEM((feat, cols), BF16), pltpu.VMEM((n_dp * rank, feat), BF16)], grid=(TILES,),
+    )(table, u_wide, w, gy, *gy_got, *w_rows, h_wide, down, *downs)
 
     summed = call(
         functools.partial(site_kernel, n_dp, feat), "sites",
-        shape(sites, rank, feat + cols), [SMEM] + [VMEM] * (2 * n_dp), VMEM,
-    )(table, *down_back, *up_back)
+        shape(sites, rank, feat + cols), [VMEM, ANY] + [VMEM] * (2 * n_dp), VMEM,
+    )(picks, token, *down_back, *up_back)
     both = [summed] + [shift(summed, "pair", q) for q in range(1, n_pair)]
     down_grad, up_grad = call(
         functools.partial(last_kernel, feat), "gradients",

time: 71 us -> 60.7 us (0.85)
  waiting for transfers between devices: 16.9 us -> 12 us
  local copies, waits for them, and re-layouts: 2.93 us -> 0.03 us
  Pallas kernels: 20.5 us -> 18.7 us
    ppermute x19, waiting for transfers between devices: 16.9 us -> 12 us  [shift(): lax.ppermute(value, axis, [(i, (i + by) % size) for i in range(size)])]
    unnamed x18 -> x14, local copies, waits for them, and re-layouts: 2.93 us -> 0.03 us
    pallas_call x2, Pallas kernels: 3.18 us -> 2.45 us  [gradient(): call(functools.partial(grad_kernel, n_dp, n_mp, len(behind)), name + '_gr...]
  transfers between devices with their start and end apart: 19 -> 19, of which waited for: 9 -> 5; matrix products, arithmetic and copies ran while one was open for 0% -> 0% of each run, Pallas kernels for 22% -> 23%
where the time goes in v6:
time: 60.7 us; the launch traced here: 60.6 us
  starting transfers between devices  29 us (48%)
  Pallas kernels  18.7 us (31%)
  waiting for transfers between devices  12 us (20%)
  between operations  0.81 us (1%)
    ppermute x19, starting transfers between devices, shift(): lax.ppermute(value, axis, [(i, (i + by) % size) for i in range(size)])  29 us
    ppermute x19, waiting for transfers between devices, shift(): lax.ppermute(value, axis, [(i, (i + by) % size) for i in range(size)])  12 us
    pallas_call x1, Pallas kernels, shards(): call(functools.partial(back_kernel, n_dp, n_mp), 'back', [shape(tok, feat...  4.11 us
    pallas_call x1, Pallas kernels, shards(): call(functools.partial(pack_kernel, n_dp, n_mp, n_pair), 'pack', [shape(r...  3.23 us
    pallas_call x2, Pallas kernels, gradient(): call(functools.partial(grad_kernel, n_dp, n_mp, len(behind)), name + '_gr...  2.45 us
    pallas_call x2, Pallas kernels, low_rank(): call(functools.partial(reduce_kernel, n_dp), name + '_part', shape(tok //...  2.43 us
    pallas_call x1, Pallas kernels, shards(): call(functools.partial(own_kernel, n_dp), 'y_own', [shape(tok, cols, dtyp...  2.14 us
    pallas_call x1, Pallas kernels, shards(): call(add_kernel, 'y_add', shape(tok, cols), [row_block(cols)] * n_mp, row...  1.52 us
  transfers between devices with their start and end apart: 19, of which 5 were waited for; matrix products, arithmetic and copies ran while one was open for 0% of the time, Pallas kernels for 23%

profile of v6, /device:TPU:0, one launch (start us, length us, event | category | flops | bytes accessed | tf_op | source)
XLA Modules:
  0.0 60.6 jit_solution(4205000561058664181)
XLA Ops:
  0.7 3.2 %pack.1 = (bf16[64,512]{1,0:T(8,128)(2,1)}, bf16[64,512]{1,0:T(8,128)(2,1)}, bf16[64,512]{1,0:T(8,128)(2,1)}, bf16[64,1024]{1,0:T(8,128)(2,1)}, bf16[64,1024]{1,...) custom-call(s32[1,2,4]{2,1,0:T(2,128)} %table.9, bf16[2,64,1024]{2,1,0:T(8,128)(2,1)} %bitcast.2, ...), custom_call_target="tpu_custom_call" | custom-call | flops 1 | bytes 1 | tf_op jit(solution)/shard_map/pack/pallas_call | solution.py:226
  3.9 3.0 %collective-permute-start.9 = (bf16[512,512]{1,0:T(8,128)(2,1)}, bf16[512,512]{1,0:T(8,128)(2,1)S(1)}, u32[]{:S(2)}, u32[]{:S(2)}) collective-permute-start(bf16[512,512]{1,0:T(8,128)(2,1)} %get-tuple-element.45), channel_id=1, source_target_pairs={{0,2},{2,0},{1,3},{3,1},{4,6},{6,4},{5,7},{7,5},{8,10},{10,8},{9,1... | collective-permute-start | bytes 1572872 | tf_op jit(solution)/shard_map/ppermute | solution.py:35
  6.9 2.6 %collective-permute-start = (bf16[64,512]{1,0:T(8,128)(2,1)}, bf16[64,512]{1,0:T(8,128)(2,1)S(1)}, u32[]{:S(2)}, u32[]{:S(2)}) collective-permute-start(bf16[64,512]{1,0:T(8,128)(2,1)} %get-tuple-element.35), channel_id=1, source_target_pairs={{0,8},{4,12},{8,0},{12,4},{1,9},{5,13},{9,1},{13,5},{2,10},{6,14},... | collective-permute-start | bytes 196616 | tf_op jit(solution)/shard_map/ppermute | solution.py:35
  9.5 1.6 %collective-permute-start.4 = (bf16[64,512]{1,0:T(8,128)(2,1)}, bf16[64,512]{1,0:T(8,128)(2,1)S(1)}, u32[]{:S(2)}, u32[]{:S(2)}) collective-permute-start(bf16[64,512]{1,0:T(8,128)(2,1)} %get-tuple-element.41), channel_id=1, source_target_pairs={{0,4},{4,8},{8,12},{12,0},{1,5},{5,9},{9,13},{13,1},{2,6},{6,10},{... | collective-permute-start | bytes 196616 | tf_op jit(solution)/shard_map/ppermute | solution.py:35
  11.1 2.2 %collective-permute-start.5 = (bf16[64,512]{1,0:T(8,128)(2,1)}, bf16[64,512]{1,0:T(8,128)(2,1)S(1)}, u32[]{:S(2)}, u32[]{:S(2)}) collective-permute-start(bf16[64,512]{1,0:T(8,128)(2,1)} %get-tuple-element.42), channel_id=1, source_target_pairs={{0,12},{4,0},{8,4},{12,8},{1,13},{5,1},{9,5},{13,9},{2,14},{6,2},{... | collective-permute-start | bytes 196616 | tf_op jit(solution)/shard_map/ppermute | solution.py:35
  13.3 1.2 %collective-permute-start.1 = (bf16[64,1024]{1,0:T(8,128)(2,1)}, bf16[64,1024]{1,0:T(8,128)(2,1)S(1)}, u32[]{:S(2)}, u32[]{:S(2)}) collective-permute-start(bf16[64,1024]{1,0:T(8,128)(2,1)} %get-tuple-element.36), channel_id=1, source_target_pairs={{0,4},{4,8},{8,12},{12,0},{1,5},{5,9},{9,13},{13,1},{2,6},{6,10},{... | collective-permute-start | bytes 393224 | tf_op jit(solution)/shard_map/ppermute | solution.py:35
  14.6 3.7 %collective-permute-start.2 = (bf16[64,1024]{1,0:T(8,128)(2,1)}, bf16[64,1024]{1,0:T(8,128)(2,1)S(1)}, u32[]{:S(2)}, u32[]{:S(2)}) collective-permute-start(bf16[64,1024]{1,0:T(8,128)(2,1)} %get-tuple-element.38), channel_id=1, source_target_pairs={{0,8},{4,12},{8,0},{12,4},{1,9},{5,13},{9,1},{13,5},{2,10},{6,14},... | collective-permute-start | bytes 393224 | tf_op jit(solution)/shard_map/ppermute | solution.py:35
  18.2 0.3 collective-permute-start.3
  18.5 1.1 %h_part.1.refs_3_ = bf16[384,128]{1,0:T(8,128)(2,1)S(1)} custom-call(s32[12]{0:T(128)S(1)} %copy-done.6, s32[1,2,4]{2,1,0:T(2,128)S(1)} %copy-done.5, bf16[768,512]{1,0:T(8,128)(2,1)S(1)} %copy-done.2, bf16[64,512]{1,0:T(8,128)(2,1)S(1)} %collective-permute-done.4._.refs_0_, bf16[2,64,512]{2,1,0:T(8,128)(2,1)S(1)} %copy-done.4, ...), custom_call_target="tpu_custom_call" | custom-call | flops 1 | bytes 1 | tf_op jit(solution)/shard_map/h_part/pallas_call | solution.py:237
  19.7 0.6 collective-permute-start.6
  20.3 1.5 %collective-permute-start.10 = (bf16[768,512]{1,0:T(8,128)(2,1)S(1)}, bf16[768,512]{1,0:T(8,128)(2,1)S(1)}, u32[]{:S(2)}, u32[]{:S(2)}) collective-permute-start(bf16[768,512]{1,0:T(8,128)(2,1)S(1)} %copy-done.2), channel_id=1, source_target_pairs={{0,2},{2,0},{1,3},{3,1},{4,6},{6,4},{5,7},{7,5},{8,10},{10,8},{9,1... | collective-permute-start | bytes 2359304 | tf_op jit(solution)/shard_map/ppermute | solution.py:35
  21.8 3.7 %collective-permute-done.6.refs_4_ = bf16[384,128]{1,0:T(8,128)(2,1)S(1)} collective-permute-done((bf16[384,128]{1,0:T(8,128)(2,1)S(1)}, bf16[384,128]{1,0:T(8,128)(2,1)S(1)}, u32[]{:S(2)}, u32[]{:S(2)}) %collective-permute-start.6) | collective-permute-done | bytes 98336 | tf_op jit(solution)/shard_map/ppermute | solution.py:35
  25.5 1.3 %down_grad.1 = (bf16[64,1024]{1,0:T(8,128)(2,1)S(1)}, bf16[64,1024]{1,0:T(8,128)(2,1)S(1)}, bf16[64,1024]{1,0:T(8,128)(2,1)S(1)}, bf16[64,1024]{1,0:T(8,128)(2,1)S(1)}, bf16[768,256]{1,0:T(8,128)(2,1)S(1)}) custom-call(s32[12]{0:T(128)S(1)} %copy-done.6, bf16[768,1024]{1,0:T(8,128)(2,1)S(1)} %copy-done.1, ...), custom_call_target="tpu_custom_call" | custom-call | flops 15000000512 | bytes 1 | tf_op jit(solution)/shard_map/down_grad/pallas_call | solution.py:245
  26.9 5.1 %collective-permute-start.12 = (bf16[64,1024]{1,0:T(8,128)(2,1)S(1)}, bf16[64,1024]{1,0:T(8,128)(2,1)S(1)}, u32[]{:S(2)}, u32[]{:S(2)}) collective-permute-start(bf16[64,1024]{1,0:T(8,128)(2,1)S(1)} %get-tuple-element.50), channel_id=1, source_target_pairs={{0,12},{4,0},{8,4},{12,8},{1,13},{5,1},{9,5},{13,9},{2,14},{6,2},{... | collective-permute-start | bytes 393224 | tf_op jit(solution)/shard_map/ppermute | solution.py:35
  32.0 0.7 %collective-permute-start.8 = (bf16[64,1024]{1,0:T(8,128)(2,1)S(1)}, bf16[64,1024]{1,0:T(8,128)(2,1)S(1)}, u32[]{:S(2)}, u32[]{:S(2)}) collective-permute-start(bf16[64,1024]{1,0:T(8,128)(2,1)S(1)} %get-tuple-element.44), channel_id=1, source_target_pairs={{0,4},{4,8},{8,12},{12,0},{1,5},{5,9},{9,13},{13,1},{2,6},{6,10},{... | collective-permute-start | bytes 393224 | tf_op jit(solution)/shard_map/ppermute | solution.py:35
  32.7 1.3 %u_part.1.refs_3_._ = bf16[384,128]{1,0:T(8,128)(2,1)S(1)} custom-call(s32[12]{0:T(128)S(1)} %copy-done.6, s32[1,2,4]{2,1,0:T(2,128)S(1)} %copy-done.5, bf16[768,1024]{1,0:T(8,128)(2,1)S(1)} %copy-done.1, bf16[768,256]{1,0:T(8,128)(2,1)S(1)} %get-tuple-element.47._.refs_4_, bf16[2,64,1024]{2,1,0:T(8,128)(2,1)S(1)} %bitcast.3, ...), custom_call_target="tpu_custom_call" | custom-call | flops 1 | bytes 1 | tf_op jit(solution)/shard_map/u_part/pallas_call | solution.py:237
  34.0 1.9 %collective-permute-done.12.__.refs_1_ = bf16[64,1024]{1,0:T(8,128)(2,1)S(1)} collective-permute-done((bf16[64,1024]{1,0:T(8,128)(2,1)S(1)}, bf16[64,1024]{1,0:T(8,128)(2,1)S(1)}, u32[]{:S(2)}, u32[]{:S(2)}) %collective-permute-start.12) | collective-permute-done | bytes 131104 | tf_op jit(solution)/shard_map/ppermute | solution.py:35
  35.9 0.5 collective-permute-start.11
  36.4 1.4 %y_send.1 = (bf16[768,512]{1,0:T(8,128)(2,1)S(1)}, bf16[1024,512]{1,0:T(8,128)(2,1)S(1)}) custom-call(bf16[384,128]{1,0:T(8,128)(2,1)S(1)} %u_part.1.refs_3_._, bf16[64,1024]{1,0:T(8,128)(2,1)S(1)} %collective-permute-done.12.__.refs_1_, bf16[768,1024]{1,0:T(8,128)(2,1)S(1)} %copy-done.1, bf16[512,512]{1,0:T(8,128)(2,1)S(1)} %collective-permute-done.9.refs_0_, ...), custom_call_target="tpu_custom_call" | custom-call | flops 1 | bytes 1 | tf_op jit(solution)/shard_map/y_send/pallas_call | solution.py:260
  37.9 1.6 %collective-permute-start.14 = (bf16[768,512]{1,0:T(8,128)(2,1)S(1)}, bf16[768,512]{1,0:T(8,128)(2,1)S(1)}, u32[]{:S(2)}, u32[]{:S(2)}) collective-permute-start(bf16[768,512]{1,0:T(8,128)(2,1)S(1)} %get-tuple-element.52), channel_id=1, source_target_pairs={{0,2},{2,0},{1,3},{3,1},{4,6},{6,4},{5,7},{7,5},{8,10},{10,8},{9,1... | collective-permute-start | bytes 2359304 | tf_op jit(solution)/shard_map/ppermute | solution.py:35
  39.4 2.6 %collective-permute-done.11.refs_4_ = bf16[384,128]{1,0:T(8,128)(2,1)S(1)} collective-permute-done((bf16[384,128]{1,0:T(8,128)(2,1)S(1)}, bf16[384,128]{1,0:T(8,128)(2,1)S(1)}, u32[]{:S(2)}, u32[]{:S(2)}) %collective-permute-start.11) | collective-permute-done | bytes 98336 | tf_op jit(solution)/shard_map/ppermute | solution.py:35
  42.0 2.0 %collective-permute-done.7.refs_0_.refs_2_ = bf16[64,1024]{1,0:T(8,128)(2,1)S(1)} collective-permute-done((bf16[64,1024]{1,0:T(8,128)(2,1)S(1)}, bf16[64,1024]{1,0:T(8,128)(2,1)S(1)}, u32[]{:S(2)}, u32[]{:S(2)}) %collective-permute-start.7) | collective-permute-done | bytes 131104 | tf_op jit(solution)/shard_map/ppermute | solution.py:35
  44.1 1.1 %up_grad.1 = (bf16[64,512]{1,0:T(8,128)(2,1)S(1)}, bf16[64,512]{1,0:T(8,128)(2,1)S(1)}, bf16[64,512]{1,0:T(8,128)(2,1)S(1)}, bf16[64,512]{1,0:T(8,128)(2,1)S(1)}, bf16[768,256]{1,0:T(8,128)(2,1)S(1)}) custom-call(s32[12]{0:T(128)S(1)} %copy-done.6, bf16[768,512]{1,0:T(8,128)(2,1)S(1)} %copy-done.2, ...), custom_call_target="tpu_custom_call" | custom-call | flops 15000000512 | bytes 1 | tf_op jit(solution)/shard_map/up_grad/pallas_call | solution.py:245
  45.2 1.9 %collective-permute-start.15 = (bf16[64,512]{1,0:T(8,128)(2,1)S(1)}, bf16[64,512]{1,0:T(8,128)(2,1)S(1)}, u32[]{:S(2)}, u32[]{:S(2)}) collective-permute-start(bf16[64,512]{1,0:T(8,128)(2,1)S(1)} %get-tuple-element.59), channel_id=1, source_target_pairs={{0,12},{4,0},{8,4},{12,8},{1,13},{5,1},{9,5},{13,9},{2,14},{6,2},{... | collective-permute-start | bytes 196616 | tf_op jit(solution)/shard_map/ppermute | solution.py:35
  47.1 0.5 collective-permute-start.16
  47.6 1.9 %collective-permute-start.17 = (bf16[64,512]{1,0:T(8,128)(2,1)S(1)}, bf16[64,512]{1,0:T(8,128)(2,1)S(1)}, u32[]{:S(2)}, u32[]{:S(2)}) collective-permute-start(bf16[64,512]{1,0:T(8,128)(2,1)S(1)} %get-tuple-element.61), channel_id=1, source_target_pairs={{0,4},{4,8},{8,12},{12,0},{1,5},{5,9},{9,13},{13,1},{2,6},{6,10},{... | collective-permute-start | bytes 196616 | tf_op jit(solution)/shard_map/ppermute | solution.py:35
  49.5 2.1 %y_own.1 = (f32[768,512]{1,0:T(8,128)S(1)}, s32[8,128]{1,0:T(8,128)S(1)}) custom-call(s32[1,2,4]{2,1,0:T(2,128)S(1)} %copy-done.5, bf16[2048,512]{1,0:T(8,128)(2,1)S(1)} %copy-done, bf16[768,1024]{1,0:T(8,128)(2,1)S(1)} %copy-done.1, bf16[768,256]{1,0:T(8,128)(2,1)S(1)} %get-tuple-element.48.wide._, bf16[2,64,512]{2,1,0:T(8,128)(2,1)S(1)} %copy-done.4, ...), custom_call_target="tpu_custom_call" | custom-call | flops 1 | bytes 1 | tf_op jit(solution)/shard_map/y_own/pallas_call | solution.py:271
  51.7 4.1 %back.1 = (bf16[768,1024]{1,0:T(8,128)(2,1)}, f32[8,128]{1,0:T(8,128)S(1)}) custom-call(s32[1,2,4]{2,1,0:T(2,128)S(1)} %copy-done.5, bf16[768,256]{1,0:T(8,128)(2,1)S(1)} %get-tuple-element.48.wide._, bf16[2048,512]{1,0:T(8,128)(2,1)S(1)} %copy-done, bf16[768,512]{1,0:T(8,128)(2,1)S(1)} %copy-done.2, bf16[768,512]{1,0:T(8,128)(2,1)S(1)} %collective-permute-done.10.refs_2_, ...), custom_call_target="tpu_custom_call" | custom-call | flops 1 | bytes 1 | tf_op jit(solution)/shard_map/back/pallas_call | solution.py:280
  55.8 0.5 sites.1.refs_0_
  56.4 1.7 %collective-permute-done.18.refs_1_ = bf16[2,64,1536]{2,1,0:T(8,128)(2,1)S(1)} collective-permute-done((bf16[2,64,1536]{2,1,0:T(8,128)(2,1)S(1)}, bf16[2,64,1536]{2,1,0:T(8,128)(2,1)S(1)}, u32[]{:S(2)}, u32[]{:S(2)}) %collective-permute-start.18) | collective-permute-done | bytes 393248 | tf_op jit(solution)/shard_map/ppermute | solution.py:35
  58.1 0.9 %gradients.1 = (f32[2,64,1024]{2,1,0:T(8,128)}, f32[2,64,512]{2,1,0:T(8,128)}) custom-call(bf16[2,64,1536]{2,1,0:T(8,128)(2,1)S(1)} %sites.1.refs_0_, bf16[2,64,1536]{2,1,0:T(8,128)(2,1)S(1)} %collective-permute-done.18.refs_1_), custom_call_target="tpu_custom_call" | custom-call | flops 1 | bytes 1 | tf_op jit(solution)/shard_map/gradients/pallas_call | solution.py:294
  59.0 1.5 %y_add.1 = bf16[768,512]{1,0:T(8,128)(2,1)} custom-call(f32[768,512]{1,0:T(8,128)S(1)} %get-tuple-element.49.refs_0_, bf16[768,512]{1,0:T(8,128)(2,1)S(1)} %collective-permute-done.14.refs_1_), custom_call_target="tpu_custom_call" | custom-call | flops 1 | bytes 1 | tf_op jit(solution)/shard_map/y_add/pallas_call | solution.py:300
  (31 shorter events, 0.2 us)
Async XLA Ops:
  0.6 17.9 %copy-start.5 = (s32[1,2,4]{2,1,0:T(2,128)S(1)}, s32[1,2,4]{2,1,0:T(2,128)}, u32[]{:S(2)}) copy-start(s32[1,2,4]{2,1,0:T(2,128)} %table.9) | copy-start | bytes 100
  0.6 17.9 %copy-start.4 = (bf16[2,64,512]{2,1,0:T(8,128)(2,1)S(1)}, bf16[2,64,512]{2,1,0:T(8,128)(2,1)}, u32[]{:S(2)}) copy-start(bf16[2,64,512]{2,1,0:T(8,128)(2,1)} %own_up.1) | copy-start | bytes 393220
  0.7 17.9 %copy-start.6 = (s32[12]{0:T(128)S(1)}, s32[12]{0:T(128)}, u32[]{:S(2)}) copy-start(s32[12]{0:T(128)} %owner.7) | copy-start | bytes 148
  0.7 17.9 %copy-start.2 = (bf16[768,512]{1,0:T(8,128)(2,1)S(1)}, bf16[768,512]{1,0:T(8,128)(2,1)}, u32[]{:S(2)}) copy-start(bf16[768,512]{1,0:T(8,128)(2,1)} %refs_1_.1) | copy-start | bytes 2359300
  0.7 24.8 %copy-start.1 = (bf16[768,1024]{1,0:T(8,128)(2,1)S(1)}, bf16[768,1024]{1,0:T(8,128)(2,1)}, u32[]{:S(2)}) copy-start(bf16[768,1024]{1,0:T(8,128)(2,1)} %x.3) | copy-start | bytes 4718596
  3.9 16.3 %collective-permute-start.9 = (bf16[512,512]{1,0:T(8,128)(2,1)}, bf16[512,512]{1,0:T(8,128)(2,1)S(1)}, u32[]{:S(2)}, u32[]{:S(2)}) collective-permute-start(bf16[512,512]{1,0:T(8,128)(2,1)} %get-tuple-element.45), channel_id=1, source_target_pairs={{0,2},{2,0},{1,3},{3,1},{4,6},{6,4},{5,7},{7,5},{8,10},{10,8},{9,1... | collective-permute-start | bytes 1572872 | tf_op jit(solution)/shard_map/ppermute | solution.py:35
  6.9 6.4 %collective-permute-start = (bf16[64,512]{1,0:T(8,128)(2,1)}, bf16[64,512]{1,0:T(8,128)(2,1)S(1)}, u32[]{:S(2)}, u32[]{:S(2)}) collective-permute-start(bf16[64,512]{1,0:T(8,128)(2,1)} %get-tuple-element.35), channel_id=1, source_target_pairs={{0,8},{4,12},{8,0},{12,4},{1,9},{5,13},{9,1},{13,5},{2,10},{6,14},... | collective-permute-start | bytes 196616 | tf_op jit(solution)/shard_map/ppermute | solution.py:35
  9.5 8.7 %collective-permute-start.4 = (bf16[64,512]{1,0:T(8,128)(2,1)}, bf16[64,512]{1,0:T(8,128)(2,1)S(1)}, u32[]{:S(2)}, u32[]{:S(2)}) collective-permute-start(bf16[64,512]{1,0:T(8,128)(2,1)} %get-tuple-element.41), channel_id=1, source_target_pairs={{0,4},{4,8},{8,12},{12,0},{1,5},{5,9},{9,13},{13,1},{2,6},{6,10},{... | collective-permute-start | bytes 196616 | tf_op jit(solution)/shard_map/ppermute | solution.py:35
  11.1 7.4 %collective-permute-start.5 = (bf16[64,512]{1,0:T(8,128)(2,1)}, bf16[64,512]{1,0:T(8,128)(2,1)S(1)}, u32[]{:S(2)}, u32[]{:S(2)}) collective-permute-start(bf16[64,512]{1,0:T(8,128)(2,1)} %get-tuple-element.42), channel_id=1, source_target_pairs={{0,12},{4,0},{8,4},{12,8},{1,13},{5,1},{9,5},{13,9},{2,14},{6,2},{... | collective-permute-start | bytes 196616 | tf_op jit(solution)/shard_map/ppermute | solution.py:35
  13.3 12.1 %collective-permute-start.1 = (bf16[64,1024]{1,0:T(8,128)(2,1)}, bf16[64,1024]{1,0:T(8,128)(2,1)S(1)}, u32[]{:S(2)}, u32[]{:S(2)}) collective-permute-start(bf16[64,1024]{1,0:T(8,128)(2,1)} %get-tuple-element.36), channel_id=1, source_target_pairs={{0,4},{4,8},{8,12},{12,0},{1,5},{5,9},{9,13},{13,1},{2,6},{6,10},{... | collective-permute-start | bytes 393224 | tf_op jit(solution)/shard_map/ppermute | solution.py:35
  14.6 10.9 %collective-permute-start.2 = (bf16[64,1024]{1,0:T(8,128)(2,1)}, bf16[64,1024]{1,0:T(8,128)(2,1)S(1)}, u32[]{:S(2)}, u32[]{:S(2)}) collective-permute-start(bf16[64,1024]{1,0:T(8,128)(2,1)} %get-tuple-element.38), channel_id=1, source_target_pairs={{0,8},{4,12},{8,0},{12,4},{1,9},{5,13},{9,1},{13,5},{2,10},{6,14},... | collective-permute-start | bytes 393224 | tf_op jit(solution)/shard_map/ppermute | solution.py:35
  18.2 7.2 %collective-permute-start.3 = (bf16[64,1024]{1,0:T(8,128)(2,1)}, bf16[64,1024]{1,0:T(8,128)(2,1)S(1)}, u32[]{:S(2)}, u32[]{:S(2)}) collective-permute-start(bf16[64,1024]{1,0:T(8,128)(2,1)} %get-tuple-element.40), channel_id=1, source_target_pairs={{0,12},{4,0},{8,4},{12,8},{1,13},{5,1},{9,5},{13,9},{2,14},{6,2},{... | collective-permute-start | bytes 393224 | tf_op jit(solution)/shard_map/ppermute | solution.py:35
  19.6 13.0 %copy-start.3 = (bf16[2,1024,64]{1,2,0:T(8,128)(2,1)S(1)}, bf16[2,1024,64]{1,2,0:T(8,128)(2,1)}, u32[]{:S(2)}) copy-start(bf16[2,1024,64]{1,2,0:T(8,128)(2,1)} %param.9) | copy-start | bytes 786436
  19.7 5.8 %collective-permute-start.6 = (bf16[384,128]{1,0:T(8,128)(2,1)S(1)}, bf16[384,128]{1,0:T(8,128)(2,1)S(1)}, u32[]{:S(2)}, u32[]{:S(2)}) collective-permute-start(bf16[384,128]{1,0:T(8,128)(2,1)S(1)} %h_part.1.refs_3_), channel_id=1, source_target_pairs={{0,2},{2,0},{1,3},{3,1},{4,6},{6,4},{5,7},{7,5},{8,10},{10,8},{9,1... | collective-permute-start | bytes 294920 | tf_op jit(solution)/shard_map/ppermute | solution.py:35
  20.3 23.8 %collective-permute-start.10 = (bf16[768,512]{1,0:T(8,128)(2,1)S(1)}, bf16[768,512]{1,0:T(8,128)(2,1)S(1)}, u32[]{:S(2)}, u32[]{:S(2)}) collective-permute-start(bf16[768,512]{1,0:T(8,128)(2,1)S(1)} %copy-done.2), channel_id=1, source_target_pairs={{0,2},{2,0},{1,3},{3,1},{4,6},{6,4},{5,7},{7,5},{8,10},{10,8},{9,1... | collective-permute-start | bytes 2359304 | tf_op jit(solution)/shard_map/ppermute | solution.py:35
  26.8 9.6 %collective-permute-start.13 = (bf16[512,512]{1,0:T(8,128)(2,1)S(1)}, bf16[512,512]{1,0:T(8,128)(2,1)S(1)}, u32[]{:S(2)}, u32[]{:S(2)}) collective-permute-start(bf16[512,512]{1,0:T(8,128)(2,1)S(1)} %collective-permute-done.9.refs_0_), channel_id=1, source_target_pairs={{0,1},{1,0},{2,3},{3,2},{4,5},{5,4},{6,7},{7,6},{8,9},{9,8},{10,11... | collective-permute-start | bytes 1572872 | tf_op jit(solution)/shard_map/ppermute | solution.py:35
  26.9 9.0 %collective-permute-start.12 = (bf16[64,1024]{1,0:T(8,128)(2,1)S(1)}, bf16[64,1024]{1,0:T(8,128)(2,1)S(1)}, u32[]{:S(2)}, u32[]{:S(2)}) collective-permute-start(bf16[64,1024]{1,0:T(8,128)(2,1)S(1)} %get-tuple-element.50), channel_id=1, source_target_pairs={{0,12},{4,0},{8,4},{12,8},{1,13},{5,1},{9,5},{13,9},{2,14},{6,2},{... | collective-permute-start | bytes 393224 | tf_op jit(solution)/shard_map/ppermute | solution.py:35
  32.0 12.1 %collective-permute-start.7 = (bf16[64,1024]{1,0:T(8,128)(2,1)S(1)}, bf16[64,1024]{1,0:T(8,128)(2,1)S(1)}, u32[]{:S(2)}, u32[]{:S(2)}) collective-permute-start(bf16[64,1024]{1,0:T(8,128)(2,1)S(1)} %get-tuple-element.43), channel_id=1, source_target_pairs={{0,8},{4,12},{8,0},{12,4},{1,9},{5,13},{9,1},{13,5},{2,10},{6,14},... | collective-permute-start | bytes 393224 | tf_op jit(solution)/shard_map/ppermute | solution.py:35
  32.0 12.1 %collective-permute-start.8 = (bf16[64,1024]{1,0:T(8,128)(2,1)S(1)}, bf16[64,1024]{1,0:T(8,128)(2,1)S(1)}, u32[]{:S(2)}, u32[]{:S(2)}) collective-permute-start(bf16[64,1024]{1,0:T(8,128)(2,1)S(1)} %get-tuple-element.44), channel_id=1, source_target_pairs={{0,4},{4,8},{8,12},{12,0},{1,5},{5,9},{9,13},{13,1},{2,6},{6,10},{... | collective-permute-start | bytes 393224 | tf_op jit(solution)/shard_map/ppermute | solution.py:35
  35.9 6.1 %collective-permute-start.11 = (bf16[384,128]{1,0:T(8,128)(2,1)S(1)}, bf16[384,128]{1,0:T(8,128)(2,1)S(1)}, u32[]{:S(2)}, u32[]{:S(2)}) collective-permute-start(bf16[384,128]{1,0:T(8,128)(2,1)S(1)} %u_part.1.refs_3_._), channel_id=1, source_target_pairs={{0,2},{2,0},{1,3},{3,1},{4,6},{6,4},{5,7},{7,5},{8,10},{10,8},{9,1... | collective-permute-start | bytes 294920 | tf_op jit(solution)/shard_map/ppermute | solution.py:35
  37.9 11.7 %copy-start = (bf16[2048,512]{1,0:T(8,128)(2,1)S(1)}, bf16[2048,512]{1,0:T(8,128)(2,1)}, u32[]{:S(2)}) copy-start(bf16[2048,512]{1,0:T(8,128)(2,1)} %refs_0_.1) | copy-start | bytes 6291460
  37.9 21.2 %collective-permute-start.14 = (bf16[768,512]{1,0:T(8,128)(2,1)S(1)}, bf16[768,512]{1,0:T(8,128)(2,1)S(1)}, u32[]{:S(2)}, u32[]{:S(2)}) collective-permute-start(bf16[768,512]{1,0:T(8,128)(2,1)S(1)} %get-tuple-element.52), channel_id=1, source_target_pairs={{0,2},{2,0},{1,3},{3,1},{4,6},{6,4},{5,7},{7,5},{8,10},{10,8},{9,1... | collective-permute-start | bytes 2359304 | tf_op jit(solution)/shard_map/ppermute | solution.py:35
  45.2 10.6 %collective-permute-start.15 = (bf16[64,512]{1,0:T(8,128)(2,1)S(1)}, bf16[64,512]{1,0:T(8,128)(2,1)S(1)}, u32[]{:S(2)}, u32[]{:S(2)}) collective-permute-start(bf16[64,512]{1,0:T(8,128)(2,1)S(1)} %get-tuple-element.59), channel_id=1, source_target_pairs={{0,12},{4,0},{8,4},{12,8},{1,13},{5,1},{9,5},{13,9},{2,14},{6,2},{... | collective-permute-start | bytes 196616 | tf_op jit(solution)/shard_map/ppermute | solution.py:35
  47.1 8.7 %collective-permute-start.16 = (bf16[64,512]{1,0:T(8,128)(2,1)S(1)}, bf16[64,512]{1,0:T(8,128)(2,1)S(1)}, u32[]{:S(2)}, u32[]{:S(2)}) collective-permute-start(bf16[64,512]{1,0:T(8,128)(2,1)S(1)} %get-tuple-element.60), channel_id=1, source_target_pairs={{0,8},{4,12},{8,0},{12,4},{1,9},{5,13},{9,1},{13,5},{2,10},{6,14},... | collective-permute-start | bytes 196616 | tf_op jit(solution)/shard_map/ppermute | solution.py:35
  47.6 8.2 %collective-permute-start.17 = (bf16[64,512]{1,0:T(8,128)(2,1)S(1)}, bf16[64,512]{1,0:T(8,128)(2,1)S(1)}, u32[]{:S(2)}, u32[]{:S(2)}) collective-permute-start(bf16[64,512]{1,0:T(8,128)(2,1)S(1)} %get-tuple-element.61), channel_id=1, source_target_pairs={{0,4},{4,8},{8,12},{12,0},{1,5},{5,9},{9,13},{13,1},{2,6},{6,10},{... | collective-permute-start | bytes 196616 | tf_op jit(solution)/shard_map/ppermute | solution.py:35
  56.3 1.8 %collective-permute-start.18 = (bf16[2,64,1536]{2,1,0:T(8,128)(2,1)S(1)}, bf16[2,64,1536]{2,1,0:T(8,128)(2,1)S(1)}, u32[]{:S(2)}, u32[]{:S(2)}) collective-permute-start(bf16[2,64,1536]{2,1,0:T(8,128)(2,1)S(1)} %sites.1.refs_0_), channel_id=1, source_target_pairs={{0,1},{1,0},{2,3},{3,2},{4,5},{5,4},{6,7},{7,6},{8,9},{9,8},{10,11... | collective-permute-start | bytes 1179656 | tf_op jit(solution)/shard_map/ppermute | solution.py:35

commit v7 on v6

--- a/solution.py
+++ b/solution.py
@@ -146,50 +146,47 @@
         outs[s][...] = nn(x[...], rows[s][...]).astype(BF16)
 
 
-def back_kernel(n_dp, n_mp, table, _, *refs):
-    w, gys, rows, wide, own_down, downs, out, token, own, maps = (
-        refs[0], refs[1:1 + n_mp], refs[1 + n_mp:2 * n_mp], refs[2 * n_mp], refs[2 * n_mp + 1],
-        refs[2 * n_mp + 2:-4], refs[-4], refs[-3], refs[-2], refs[-1],
-    )
+def back_kernel(n_dp, n_mp, table, w, gy, wide, own_down, *refs):
+    n_other = n_mp - 1
+    gots, rows = refs[:n_other], refs[n_other:2 * n_other]
+    downs, out, picks, own, maps = refs[2 * n_other:-4], refs[-4], refs[-3], refs[-2], refs[-1]
     feat = out.shape[1]
 
     @pl.when(pl.program_id(0) == 0)
     def _():
-        token[...] = jnp.zeros_like(token)
         own[...] = w[pl.ds(pl.multiple_of(lax.axis_index("mp") * feat, feat), feat), :]
         gather_maps(n_dp, table, own_down, downs, maps)
-
-    total = nt(gys[0][...], own[...]) + SCALE * nn(wide[...], maps[...])
-    for gy, row in zip(gys[1:], rows):
-        total = total + nt(gy[...], row[...])
+        row = lax.broadcasted_iota(jnp.int32, picks.shape, 0)
+        sites = jnp.zeros(picks.shape, jnp.int32)
+        for s in range(n_dp):
+            sites = jnp.where(row == s, wanted_site(table, n_dp, s), sites)
+        picks[...] = sites
+
+    total = nt(gy[...], own[...]) + SCALE * nn(wide[...], maps[...])
+    for got, row in zip(gots, rows):
+        total = total + nt(got[...], row[...])
     out[...] = total.astype(BF16)
 
 
-def own_kernel(n_dp, table, w, x, wide, own_up, *refs):
-    ups, out, picks, maps = refs[:n_dp - 1], refs[n_dp - 1], refs[n_dp], refs[n_dp + 1]
+def base_kernel(_, w, x, out):
     feat = x.shape[1]
+    out[...] = nn(x[...], w[pl.ds(pl.multiple_of(lax.axis_index("mp") * feat, feat), feat), :])
+
+
+def add_kernel(n_dp, table, base, wide, own_up, *refs):
+    ups, gots, out, maps = refs[:n_dp - 1], refs[n_dp - 1:-2], refs[-2], refs[-1]
 
     @pl.when(pl.program_id(0) == 0)
     def _():
         gather_maps(n_dp, table, own_up, ups, maps)
-        row = lax.broadcasted_iota(jnp.int32, picks.shape, 0)
-        total = jnp.zeros(picks.shape, jnp.int32)
-        for s in range(n_dp):
-            total = jnp.where(row == s, wanted_site(table, n_dp, s), total)
-        picks[...] = total
-
-    own = w[pl.ds(pl.multiple_of(lax.axis_index("mp") * feat, feat), feat), :]
-    out[...] = nn(x[...], own) + SCALE * nn(wide[...], maps[...])
-
-
-def add_kernel(*refs):
-    total = refs[0][...]
-    for ref in refs[1:-1]:
-        total = total + ref[...].astype(F32)
-    refs[-1][...] = total.astype(BF16)
-
-
-def site_kernel(n_dp, feat, picks, _, *refs):
+
+    total = base[...] + SCALE * nn(wide[...], maps[...])
+    for got in gots:
+        total = total + got[...].astype(F32)
+    out[...] = total.astype(BF16)
+
+
+def site_kernel(n_dp, feat, picks, *refs):
     downs, ups, out = refs[:n_dp], refs[n_dp:2 * n_dp], refs[-1]
     for site in range(out.shape[0]):
         for grads, lo, hi in ((downs, 0, feat), (ups, feat, out.shape[2])):
@@ -251,7 +248,11 @@
 
     h_parts = low_rank(gy, up, ups, ups[0], "h")
     gy_got = [shift(after(gy, *pieces), "mp", s) for s in range(1, n_mp)]
-    down_back, h_wide = gradient(x, h_parts, downs, "down", GRAD_COST)
+    base = call(
+        base_kernel, "base", shape(tok, cols, dtype=F32),
+        [ANY, whole(*w.shape), row_block(feat)], row_block(cols), grid=(TILES,),
+    )(h_parts[1 % n_mp], w, x)
+    down_back, h_wide = gradient(x, h_parts, [base] + downs, "down", GRAD_COST)
     u_parts = low_rank(x, down, downs, h_wide, "u")
 
     parts = []
@@ -266,30 +267,20 @@
     )(u_parts[0], down_back[1], x, *parts)
     w_rows = sent[n_other:]
     y_got = [shift(sent[s - 1], "mp", n_mp - s) for s in range(1, n_mp)]
-    up_back, u_wide = gradient(gy, u_parts, down_back[2:] + gy_got, "up", GRAD_COST)
-
-    y_own, picks = call(
-        functools.partial(own_kernel, n_dp), "y_own",
-        [shape(tok, cols, dtype=F32), shape(-(-n_dp // 8) * 8, 128, dtype=jnp.int32)],
-        [SMEM, whole(*w.shape), row_block(feat), row_block(n_dp * rank), whole(*up.shape)]
-        + [whole(rank, cols)] * away,
-        [row_block(cols), whole(-(-n_dp // 8) * 8, 128)],
-        [pltpu.VMEM((n_dp * rank, cols), BF16)], grid=(TILES,),
-    )(table, w, x, u_wide, up, *ups)
-
-    back, token = call(
+    back, picks = call(
         functools.partial(back_kernel, n_dp, n_mp), "back",
-        [shape(tok, feat), shape(8, 128, dtype=F32)],
-        [SMEM, ANY, whole(*w.shape)] + [row_block(cols)] * n_mp + [whole(feat, cols)] * n_other
-        + [row_block(n_dp * rank), whole(*down.shape)] + [whole(rank, feat)] * away,
-        [row_block(feat), whole(8, 128)],
+        [shape(tok, feat), shape(-(-n_dp // 8) * 8, 128, dtype=jnp.int32)],
+        [SMEM, whole(*w.shape), row_block(cols), row_block(n_dp * rank), whole(*down.shape)]
+        + [row_block(cols)] * n_other + [whole(feat, cols)] * n_other + [whole(rank, feat)] * away,
+        [row_block(feat), whole(-(-n_dp // 8) * 8, 128)],
         [pltpu.VMEM((feat, cols), BF16), pltpu.VMEM((n_dp * rank, feat), BF16)], grid=(TILES,),
-    )(table, u_wide, w, gy, *gy_got, *w_rows, h_wide, down, *downs)
+    )(table, w, gy, h_wide, down, *gy_got, *w_rows, *downs)
+    up_back, u_wide = gradient(gy, u_parts, [picks] + down_back[2:], "up", GRAD_COST)
 
     summed = call(
         functools.partial(site_kernel, n_dp, feat), "sites",
-        shape(sites, rank, feat + cols), [VMEM, ANY] + [VMEM] * (2 * n_dp), VMEM,
-    )(picks, token, *down_back, *up_back)
+        shape(sites, rank, feat + cols), [VMEM] + [VMEM] * (2 * n_dp), VMEM,
+    )(picks, *down_back, *up_back)
     both = [summed] + [shift(summed, "pair", q) for q in range(1, n_pair)]
     down_grad, up_grad = call(
         functools.partial(last_kernel, feat), "gradients",
@@ -298,8 +289,11 @@
     )(*both)
 
     y = call(
-        add_kernel, "y_add", shape(tok, cols), [row_block(cols)] * n_mp, row_block(cols), grid=(TILES,),
-    )(y_own, *y_got)
+        functools.partial(add_kernel, n_dp), "y_add", shape(tok, cols),
+        [SMEM, row_block(cols), row_block(n_dp * rank), whole(*up.shape)] + [whole(rank, cols)] * away
+        + [row_block(cols)] * n_other,
+        row_block(cols), [pltpu.VMEM((n_dp * rank, cols), BF16)], grid=(TILES,),
+    )(table, base, u_wide, up, *ups, *y_got)
     return y, back, down_grad.transpose(0, 2, 1), up_grad
 
 

time: 60.7 us -> 68 us (1.12)
  waiting for transfers between devices: 12 us -> 20 us
  starting transfers between devices: 29 us -> 25.1 us
  Pallas kernels: 18.7 us -> 20.9 us
  local copies, waits for them, and re-layouts: 0.03 us -> 0.93 us
    ppermute x19, waiting for transfers between devices: 12 us -> 20 us  [shift(): lax.ppermute(value, axis, [(i, (i + by) % size) for i in range(size)])]
    ppermute x19, starting transfers between devices: 29 us -> 25.1 us  [shift(): lax.ppermute(value, axis, [(i, (i + by) % size) for i in range(size)])]
    unnamed x14, local copies, waits for them, and re-layouts: 0.03 us -> 0.93 us
  transfers between devices with their start and end apart: 19 -> 19, of which waited for: 5 -> 7; matrix products, arithmetic and copies ran while one was open for 0% -> 0% of each run, Pallas kernels for 23% -> 22%
where the time goes in v7:
time: 68 us; the launch traced here: 67.7 us
  starting transfers between devices  25.1 us (37%)
  Pallas kernels  20.9 us (31%)
  waiting for transfers between devices  20 us (29%)
  local copies, waits for them, and re-layouts  0.93 us (1%)
  between operations  0.8 us (1%)
    ppermute x19, starting transfers between devices, shift(): lax.ppermute(value, axis, [(i, (i + by) % size) for i in range(size)])  25.1 us
    ppermute x19, waiting for transfers between devices, shift(): lax.ppermute(value, axis, [(i, (i + by) % size) for i in range(size)])  20 us
    pallas_call x1, Pallas kernels, shards(): call(functools.partial(back_kernel, n_dp, n_mp), 'back', [shape(tok, feat...  4.73 us
    pallas_call x1, Pallas kernels, shards(): call(functools.partial(pack_kernel, n_dp, n_mp, n_pair), 'pack', [shape(r...  3.46 us
    pallas_call x2, Pallas kernels, gradient(): call(functools.partial(grad_kernel, n_dp, n_mp, len(behind)), name + '_gr...  3.04 us
    pallas_call x2, Pallas kernels, low_rank(): call(functools.partial(reduce_kernel, n_dp), name + '_part', shape(tok //...  3.01 us
    pallas_call x1, Pallas kernels, shards(): call(functools.partial(add_kernel, n_dp), 'y_add', shape(tok, cols), [SME...  2.48 us
    pallas_call x1, Pallas kernels, shards(): call(functools.partial(send_kernel, n_pair, feat, n_mp), 'y_send', [shape...  1.42 us
  transfers between devices with their start and end apart: 19, of which 7 were waited for; matrix products, arithmetic and copies ran while one was open for 0% of the time, Pallas kernels for 22%

profile of v7, /device:TPU:0, one launch (start us, length us, event | category | flops | bytes accessed | tf_op | source)
XLA Modules:
  0.0 67.7 jit_solution(2226396386131890441)
XLA Ops:
  0.7 3.5 %pack.1 = (bf16[64,512]{1,0:T(8,128)(2,1)}, bf16[64,512]{1,0:T(8,128)(2,1)}, bf16[64,512]{1,0:T(8,128)(2,1)}, bf16[64,1024]{1,0:T(8,128)(2,1)}, bf16[64,1024]{1,...) custom-call(s32[1,2,4]{2,1,0:T(2,128)} %table.9, bf16[2,64,1024]{2,1,0:T(8,128)(2,1)} %bitcast.2, ...), custom_call_target="tpu_custom_call" | custom-call | flops 1 | bytes 1 | tf_op jit(solution)/shard_map/pack/pallas_call | solution.py:223
  4.1 3.0 %collective-permute-start.7 = (bf16[512,512]{1,0:T(8,128)(2,1)}, bf16[512,512]{1,0:T(8,128)(2,1)S(1)}, u32[]{:S(2)}, u32[]{:S(2)}) collective-permute-start(bf16[512,512]{1,0:T(8,128)(2,1)} %get-tuple-element.42), channel_id=1, source_target_pairs={{0,2},{2,0},{1,3},{3,1},{4,6},{6,4},{5,7},{7,5},{8,10},{10,8},{9,1... | collective-permute-start | bytes 1572872 | tf_op jit(solution)/shard_map/ppermute | solution.py:35
  7.1 2.6 %collective-permute-start.1 = (bf16[64,512]{1,0:T(8,128)(2,1)}, bf16[64,512]{1,0:T(8,128)(2,1)S(1)}, u32[]{:S(2)}, u32[]{:S(2)}) collective-permute-start(bf16[64,512]{1,0:T(8,128)(2,1)} %get-tuple-element.33), channel_id=1, source_target_pairs={{0,8},{4,12},{8,0},{12,4},{1,9},{5,13},{9,1},{13,5},{2,10},{6,14},... | collective-permute-start | bytes 196616 | tf_op jit(solution)/shard_map/ppermute | solution.py:35
  9.7 1.6 %collective-permute-start = (bf16[64,512]{1,0:T(8,128)(2,1)}, bf16[64,512]{1,0:T(8,128)(2,1)S(1)}, u32[]{:S(2)}, u32[]{:S(2)}) collective-permute-start(bf16[64,512]{1,0:T(8,128)(2,1)} %get-tuple-element.32), channel_id=1, source_target_pairs={{0,4},{4,8},{8,12},{12,0},{1,5},{5,9},{9,13},{13,1},{2,6},{6,10},{... | collective-permute-start | bytes 196616 | tf_op jit(solution)/shard_map/ppermute | solution.py:35
  11.3 2.2 %collective-permute-start.2 = (bf16[64,512]{1,0:T(8,128)(2,1)}, bf16[64,512]{1,0:T(8,128)(2,1)S(1)}, u32[]{:S(2)}, u32[]{:S(2)}) collective-permute-start(bf16[64,512]{1,0:T(8,128)(2,1)} %get-tuple-element.34), channel_id=1, source_target_pairs={{0,12},{4,0},{8,4},{12,8},{1,13},{5,1},{9,5},{13,9},{2,14},{6,2},{... | collective-permute-start | bytes 196616 | tf_op jit(solution)/shard_map/ppermute | solution.py:35
  13.6 1.2 %collective-permute-start.4 = (bf16[64,1024]{1,0:T(8,128)(2,1)}, bf16[64,1024]{1,0:T(8,128)(2,1)S(1)}, u32[]{:S(2)}, u32[]{:S(2)}) collective-permute-start(bf16[64,1024]{1,0:T(8,128)(2,1)} %get-tuple-element.36), channel_id=1, source_target_pairs={{0,4},{4,8},{8,12},{12,0},{1,5},{5,9},{9,13},{13,1},{2,6},{6,10},{... | collective-permute-start | bytes 393224 | tf_op jit(solution)/shard_map/ppermute | solution.py:35
  14.8 3.7 %collective-permute-start.5 = (bf16[64,1024]{1,0:T(8,128)(2,1)}, bf16[64,1024]{1,0:T(8,128)(2,1)S(1)}, u32[]{:S(2)}, u32[]{:S(2)}) collective-permute-start(bf16[64,1024]{1,0:T(8,128)(2,1)} %get-tuple-element.38), channel_id=1, source_target_pairs={{0,8},{4,12},{8,0},{12,4},{1,9},{5,13},{9,1},{13,5},{2,10},{6,14},... | collective-permute-start | bytes 393224 | tf_op jit(solution)/shard_map/ppermute | solution.py:35
  18.8 0.9 %copy-done.3 = bf16[2,64,512]{2,1,0:T(8,128)(2,1)S(1)} copy-done((bf16[2,64,512]{2,1,0:T(8,128)(2,1)S(1)}, bf16[2,64,512]{2,1,0:T(8,128)(2,1)}, u32[]{:S(2)}) %copy-start.3) | copy-done | bytes 131096
  19.6 1.7 %h_part.1.refs_4_ = bf16[384,128]{1,0:T(8,128)(2,1)S(1)} custom-call(s32[12]{0:T(128)S(1)} %copy-done.6, s32[1,2,4]{2,1,0:T(2,128)S(1)} %copy-done.5, bf16[768,512]{1,0:T(8,128)(2,1)} %act.7, bf16[64,512]{1,0:T(8,128)(2,1)S(1)} %collective-permute-done._.refs_0_, bf16[2,64,512]{2,1,0:T(8,128)(2,1)S(1)} %copy-done.3, ...), custom_call_target="tpu_custom_call" | custom-call | flops 1 | bytes 1 | tf_op jit(solution)/shard_map/h_part/pallas_call | solution.py:234
  21.3 0.6 collective-permute-start.3
  22.0 4.1 %collective-permute-done.3._.refs_5_ = bf16[384,128]{1,0:T(8,128)(2,1)S(1)} collective-permute-done((bf16[384,128]{1,0:T(8,128)(2,1)S(1)}, bf16[384,128]{1,0:T(8,128)(2,1)S(1)}, u32[]{:S(2)}, u32[]{:S(2)}) %collective-permute-start.3) | collective-permute-done | bytes 98336 | tf_op jit(solution)/shard_map/ppermute | solution.py:35
  26.0 1.3 %base.1.refs_0_ = f32[768,512]{1,0:T(8,128)S(1)} custom-call(bf16[384,128]{1,0:T(8,128)(2,1)S(1)} %collective-permute-done.3._.refs_5_, bf16[2048,512]{1,0:T(8,128)(2,1)S(1)} %copy-done, bf16[768,1024]{1,0:T(8,128)(2,1)S(1)} %copy-done.1), custom_call_target="tpu_custom_call" | custom-call | flops 1 | bytes 1 | tf_op jit(solution)/shard_map/base/pallas_call | solution.py:251
  27.4 0.6 collective-permute-start.8
  28.0 1.3 %down_grad.1 = (bf16[64,1024]{1,0:T(8,128)(2,1)S(1)}, bf16[64,1024]{1,0:T(8,128)(2,1)S(1)}, bf16[64,1024]{1,0:T(8,128)(2,1)S(1)}, bf16[64,1024]{1,0:T(8,128)(2,1)S(1)}, bf16[768,256]{1,0:T(8,128)(2,1)S(1)}) custom-call(s32[12]{0:T(128)S(1)} %copy-done.6, bf16[768,1024]{1,0:T(8,128)(2,1)S(1)} %copy-done.1, f32[768,512]{1,0:T(8,128)S(1)} %base.1.refs_0_, ...), custom_call_target="tpu_custom_call" | custom-call | flops 15000000512 | bytes 1 | tf_op jit(solution)/shard_map/down_grad/pallas_call | solution.py:242
  29.4 2.8 %collective-permute-start.9 = (bf16[64,1024]{1,0:T(8,128)(2,1)S(1)}, bf16[64,1024]{1,0:T(8,128)(2,1)S(1)}, u32[]{:S(2)}, u32[]{:S(2)}) collective-permute-start(bf16[64,1024]{1,0:T(8,128)(2,1)S(1)} %get-tuple-element.44), channel_id=1, source_target_pairs={{0,12},{4,0},{8,4},{12,8},{1,13},{5,1},{9,5},{13,9},{2,14},{6,2},{... | collective-permute-start | bytes 393224 | tf_op jit(solution)/shard_map/ppermute | solution.py:35
  32.2 0.7 %collective-permute-start.11 = (bf16[64,1024]{1,0:T(8,128)(2,1)S(1)}, bf16[64,1024]{1,0:T(8,128)(2,1)S(1)}, u32[]{:S(2)}, u32[]{:S(2)}) collective-permute-start(bf16[64,1024]{1,0:T(8,128)(2,1)S(1)} %get-tuple-element.48), channel_id=1, source_target_pairs={{0,8},{4,12},{8,0},{12,4},{1,9},{5,13},{9,1},{13,5},{2,10},{6,14},... | collective-permute-start | bytes 393224 | tf_op jit(solution)/shard_map/ppermute | solution.py:35
  32.9 1.3 %u_part.1._.refs_3_ = bf16[384,128]{1,0:T(8,128)(2,1)S(1)} custom-call(s32[12]{0:T(128)S(1)} %copy-done.6, s32[1,2,4]{2,1,0:T(2,128)S(1)} %copy-done.5, bf16[768,1024]{1,0:T(8,128)(2,1)S(1)} %copy-done.1, bf16[768,256]{1,0:T(8,128)(2,1)S(1)} %get-tuple-element.41._.wide, bf16[2,64,1024]{2,1,0:T(8,128)(2,1)S(1)} %bitcast.3, ...), custom_call_target="tpu_custom_call" | custom-call | flops 1 | bytes 1 | tf_op jit(solution)/shard_map/u_part/pallas_call | solution.py:234
  34.2 1.9 %collective-permute-done.9.__.refs_1_ = bf16[64,1024]{1,0:T(8,128)(2,1)S(1)} collective-permute-done((bf16[64,1024]{1,0:T(8,128)(2,1)S(1)}, bf16[64,1024]{1,0:T(8,128)(2,1)S(1)}, u32[]{:S(2)}, u32[]{:S(2)}) %collective-permute-start.9) | collective-permute-done | bytes 131104 | tf_op jit(solution)/shard_map/ppermute | solution.py:35
  36.1 0.9 %collective-permute-start.13 = (bf16[384,128]{1,0:T(8,128)(2,1)S(1)}, bf16[384,128]{1,0:T(8,128)(2,1)S(1)}, u32[]{:S(2)}, u32[]{:S(2)}) collective-permute-start(bf16[384,128]{1,0:T(8,128)(2,1)S(1)} %u_part.1._.refs_3_), channel_id=1, source_target_pairs={{0,2},{2,0},{1,3},{3,1},{4,6},{6,4},{5,7},{7,5},{8,10},{10,8},{9,1... | collective-permute-start | bytes 294920 | tf_op jit(solution)/shard_map/ppermute | solution.py:35
  37.0 1.4 %y_send.1 = (bf16[768,512]{1,0:T(8,128)(2,1)S(1)}, bf16[1024,512]{1,0:T(8,128)(2,1)S(1)}) custom-call(bf16[384,128]{1,0:T(8,128)(2,1)S(1)} %u_part.1._.refs_3_, bf16[64,1024]{1,0:T(8,128)(2,1)S(1)} %collective-permute-done.9.__.refs_1_, bf16[768,1024]{1,0:T(8,128)(2,1)S(1)} %copy-done.1, bf16[512,512]{1,0:T(8,128)(2,1)S(1)} %collective-permute-done.7.refs_0_, ...), custom_call_target="tpu_custom_call" | custom-call | flops 1 | bytes 1 | tf_op jit(solution)/shard_map/y_send/pallas_call | solution.py:261
  38.5 1.2 %collective-permute-start.14 = (bf16[768,512]{1,0:T(8,128)(2,1)S(1)}, bf16[768,512]{1,0:T(8,128)(2,1)S(1)}, u32[]{:S(2)}, u32[]{:S(2)}) collective-permute-start(bf16[768,512]{1,0:T(8,128)(2,1)S(1)} %get-tuple-element.51), channel_id=1, source_target_pairs={{0,2},{2,0},{1,3},{3,1},{4,6},{6,4},{5,7},{7,5},{8,10},{10,8},{9,1... | collective-permute-start | bytes 2359304 | tf_op jit(solution)/shard_map/ppermute | solution.py:35
  39.7 8.2 %collective-permute-done.8.refs_0_ = bf16[768,512]{1,0:T(8,128)(2,1)S(1)} collective-permute-done((bf16[768,512]{1,0:T(8,128)(2,1)}, bf16[768,512]{1,0:T(8,128)(2,1)S(1)}, u32[]{:S(2)}, u32[]{:S(2)}) %collective-permute-start.8) | collective-permute-done | bytes 786464 | tf_op jit(solution)/shard_map/ppermute | solution.py:35
  47.8 4.7 %back.1 = (bf16[768,1024]{1,0:T(8,128)(2,1)}, s32[8,128]{1,0:T(8,128)S(1)}) custom-call(s32[1,2,4]{2,1,0:T(2,128)S(1)} %copy-done.5, bf16[2048,512]{1,0:T(8,128)(2,1)S(1)} %copy-done, bf16[768,512]{1,0:T(8,128)(2,1)} %act.7, bf16[768,256]{1,0:T(8,128)(2,1)S(1)} %get-tuple-element.41._.wide, bf16[2,64,1024]{2,1,0:T(8,128)(2,1)S(1)} %bitcast.4, ...), custom_call_target="tpu_custom_call" | custom-call | flops 1 | bytes 1 | tf_op jit(solution)/shard_map/back/pallas_call | solution.py:270
  52.6 1.7 %up_grad.1 = (bf16[64,512]{1,0:T(8,128)(2,1)S(1)}, bf16[64,512]{1,0:T(8,128)(2,1)S(1)}, bf16[64,512]{1,0:T(8,128)(2,1)S(1)}, bf16[64,512]{1,0:T(8,128)(2,1)S(1)}, bf16[768,256]{1,0:T(8,128)(2,1)S(1)}) custom-call(s32[12]{0:T(128)S(1)} %copy-done.6, bf16[768,512]{1,0:T(8,128)(2,1)} %act.7, s32[8,128]{1,0:T(8,128)S(1)} %get-tuple-element.47.refs_0_.picks, ...), custom_call_target="tpu_custom_call" | custom-call | flops 15000000512 | bytes 1 | tf_op jit(solution)/shard_map/up_grad/pallas_call | solution.py:242
  54.3 1.1 %collective-permute-start.15 = (bf16[64,512]{1,0:T(8,128)(2,1)S(1)}, bf16[64,512]{1,0:T(8,128)(2,1)S(1)}, u32[]{:S(2)}, u32[]{:S(2)}) collective-permute-start(bf16[64,512]{1,0:T(8,128)(2,1)S(1)} %get-tuple-element.55), channel_id=1, source_target_pairs={{0,12},{4,0},{8,4},{12,8},{1,13},{5,1},{9,5},{13,9},{2,14},{6,2},{... | collective-permute-start | bytes 196616 | tf_op jit(solution)/shard_map/ppermute | solution.py:35
  56.0 1.9 %collective-permute-start.17 = (bf16[64,512]{1,0:T(8,128)(2,1)S(1)}, bf16[64,512]{1,0:T(8,128)(2,1)S(1)}, u32[]{:S(2)}, u32[]{:S(2)}) collective-permute-start(bf16[64,512]{1,0:T(8,128)(2,1)S(1)} %get-tuple-element.57), channel_id=1, source_target_pairs={{0,4},{4,8},{8,12},{12,0},{1,5},{5,9},{9,13},{13,1},{2,6},{6,10},{... | collective-permute-start | bytes 196616 | tf_op jit(solution)/shard_map/ppermute | solution.py:35
  57.9 0.7 %collective-permute-done.15.refs_5_ = bf16[64,512]{1,0:T(8,128)(2,1)S(1)} collective-permute-done((bf16[64,512]{1,0:T(8,128)(2,1)S(1)}, bf16[64,512]{1,0:T(8,128)(2,1)S(1)}, u32[]{:S(2)}, u32[]{:S(2)}) %collective-permute-start.15) | collective-permute-done | bytes 65568 | tf_op jit(solution)/shard_map/ppermute | solution.py:35
  58.6 2.7 %collective-permute-done.16.refs_6_ = bf16[64,512]{1,0:T(8,128)(2,1)S(1)} collective-permute-done((bf16[64,512]{1,0:T(8,128)(2,1)S(1)}, bf16[64,512]{1,0:T(8,128)(2,1)S(1)}, u32[]{:S(2)}, u32[]{:S(2)}) %collective-permute-start.16) | collective-permute-done | bytes 65568 | tf_op jit(solution)/shard_map/ppermute | solution.py:35
  61.3 0.7 %collective-permute-done.17.refs_7_ = bf16[64,512]{1,0:T(8,128)(2,1)S(1)} collective-permute-done((bf16[64,512]{1,0:T(8,128)(2,1)S(1)}, bf16[64,512]{1,0:T(8,128)(2,1)S(1)}, u32[]{:S(2)}, u32[]{:S(2)}) %collective-permute-start.17) | collective-permute-done | bytes 65568 | tf_op jit(solution)/shard_map/ppermute | solution.py:35
  62.6 1.7 %collective-permute-done.18.refs_1_ = bf16[2,64,1536]{2,1,0:T(8,128)(2,1)S(1)} collective-permute-done((bf16[2,64,1536]{2,1,0:T(8,128)(2,1)S(1)}, bf16[2,64,1536]{2,1,0:T(8,128)(2,1)S(1)}, u32[]{:S(2)}, u32[]{:S(2)}) %collective-permute-start.18) | collective-permute-done | bytes 393248 | tf_op jit(solution)/shard_map/ppermute | solution.py:35
  64.3 0.9 %gradients.1 = (f32[2,64,1024]{2,1,0:T(8,128)}, f32[2,64,512]{2,1,0:T(8,128)}) custom-call(bf16[2,64,1536]{2,1,0:T(8,128)(2,1)S(1)} %sites.1.refs_0_, bf16[2,64,1536]{2,1,0:T(8,128)(2,1)S(1)} %collective-permute-done.18.refs_1_), custom_call_target="tpu_custom_call" | custom-call | flops 1 | bytes 1 | tf_op jit(solution)/shard_map/gradients/pallas_call | solution.py:285
  65.3 2.5 %y_add.1 = bf16[768,512]{1,0:T(8,128)(2,1)} custom-call(s32[1,2,4]{2,1,0:T(2,128)S(1)} %copy-done.5, f32[768,512]{1,0:T(8,128)S(1)} %base.1.refs_0_, bf16[768,256]{1,0:T(8,128)(2,1)S(1)} %get-tuple-element.50.wide, bf16[2,64,512]{2,1,0:T(8,128)(2,1)S(1)} %copy-done.4, bf16[64,512]{1,0:T(8,128)(2,1)S(1)} %collective-permute-done._.refs_0_, ...), custom_call_target="tpu_custom_call" | custom-call | flops 1 | bytes 1 | tf_op jit(solution)/shard_map/y_add/pallas_call | solution.py:291
  (31 shorter events, 1.5 us)
Async XLA Ops:
  0.6 18.1 %copy-start.5 = (s32[1,2,4]{2,1,0:T(2,128)S(1)}, s32[1,2,4]{2,1,0:T(2,128)}, u32[]{:S(2)}) copy-start(s32[1,2,4]{2,1,0:T(2,128)} %table.9) | copy-start | bytes 100
  0.6 18.1 %copy-start.6 = (s32[12]{0:T(128)S(1)}, s32[12]{0:T(128)}, u32[]{:S(2)}) copy-start(s32[12]{0:T(128)} %owner.7) | copy-start | bytes 148
  0.7 25.4 %copy-start = (bf16[2048,512]{1,0:T(8,128)(2,1)S(1)}, bf16[2048,512]{1,0:T(8,128)(2,1)}, u32[]{:S(2)}) copy-start(bf16[2048,512]{1,0:T(8,128)(2,1)} %w.5) | copy-start | bytes 6291460
  0.7 25.4 %copy-start.1 = (bf16[768,1024]{1,0:T(8,128)(2,1)S(1)}, bf16[768,1024]{1,0:T(8,128)(2,1)}, u32[]{:S(2)}) copy-start(bf16[768,1024]{1,0:T(8,128)(2,1)} %x.3) | copy-start | bytes 4718596
  4.1 23.2 %collective-permute-start.7 = (bf16[512,512]{1,0:T(8,128)(2,1)}, bf16[512,512]{1,0:T(8,128)(2,1)S(1)}, u32[]{:S(2)}, u32[]{:S(2)}) collective-permute-start(bf16[512,512]{1,0:T(8,128)(2,1)} %get-tuple-element.42), channel_id=1, source_target_pairs={{0,2},{2,0},{1,3},{3,1},{4,6},{6,4},{5,7},{7,5},{8,10},{10,8},{9,1... | collective-permute-start | bytes 1572872 | tf_op jit(solution)/shard_map/ppermute | solution.py:35
  7.1 6.4 %collective-permute-start.1 = (bf16[64,512]{1,0:T(8,128)(2,1)}, bf16[64,512]{1,0:T(8,128)(2,1)S(1)}, u32[]{:S(2)}, u32[]{:S(2)}) collective-permute-start(bf16[64,512]{1,0:T(8,128)(2,1)} %get-tuple-element.33), channel_id=1, source_target_pairs={{0,8},{4,12},{8,0},{12,4},{1,9},{5,13},{9,1},{13,5},{2,10},{6,14},... | collective-permute-start | bytes 196616 | tf_op jit(solution)/shard_map/ppermute | solution.py:35
  9.7 8.7 %collective-permute-start = (bf16[64,512]{1,0:T(8,128)(2,1)}, bf16[64,512]{1,0:T(8,128)(2,1)S(1)}, u32[]{:S(2)}, u32[]{:S(2)}) collective-permute-start(bf16[64,512]{1,0:T(8,128)(2,1)} %get-tuple-element.32), channel_id=1, source_target_pairs={{0,4},{4,8},{8,12},{12,0},{1,5},{5,9},{9,13},{13,1},{2,6},{6,10},{... | collective-permute-start | bytes 196616 | tf_op jit(solution)/shard_map/ppermute | solution.py:35
  11.3 7.4 %collective-permute-start.2 = (bf16[64,512]{1,0:T(8,128)(2,1)}, bf16[64,512]{1,0:T(8,128)(2,1)S(1)}, u32[]{:S(2)}, u32[]{:S(2)}) collective-permute-start(bf16[64,512]{1,0:T(8,128)(2,1)} %get-tuple-element.34), channel_id=1, source_target_pairs={{0,12},{4,0},{8,4},{12,8},{1,13},{5,1},{9,5},{13,9},{2,14},{6,2},{... | collective-permute-start | bytes 196616 | tf_op jit(solution)/shard_map/ppermute | solution.py:35
  13.6 14.4 %collective-permute-start.4 = (bf16[64,1024]{1,0:T(8,128)(2,1)}, bf16[64,1024]{1,0:T(8,128)(2,1)S(1)}, u32[]{:S(2)}, u32[]{:S(2)}) collective-permute-start(bf16[64,1024]{1,0:T(8,128)(2,1)} %get-tuple-element.36), channel_id=1, source_target_pairs={{0,4},{4,8},{8,12},{12,0},{1,5},{5,9},{9,13},{13,1},{2,6},{6,10},{... | collective-permute-start | bytes 393224 | tf_op jit(solution)/shard_map/ppermute | solution.py:35
  14.8 13.2 %collective-permute-start.5 = (bf16[64,1024]{1,0:T(8,128)(2,1)}, bf16[64,1024]{1,0:T(8,128)(2,1)S(1)}, u32[]{:S(2)}, u32[]{:S(2)}) collective-permute-start(bf16[64,1024]{1,0:T(8,128)(2,1)} %get-tuple-element.38), channel_id=1, source_target_pairs={{0,8},{4,12},{8,0},{12,4},{1,9},{5,13},{9,1},{13,5},{2,10},{6,14},... | collective-permute-start | bytes 393224 | tf_op jit(solution)/shard_map/ppermute | solution.py:35
  18.5 9.6 %collective-permute-start.6 = (bf16[64,1024]{1,0:T(8,128)(2,1)}, bf16[64,1024]{1,0:T(8,128)(2,1)S(1)}, u32[]{:S(2)}, u32[]{:S(2)}) collective-permute-start(bf16[64,1024]{1,0:T(8,128)(2,1)} %get-tuple-element.40), channel_id=1, source_target_pairs={{0,12},{4,0},{8,4},{12,8},{1,13},{5,1},{9,5},{13,9},{2,14},{6,2},{... | collective-permute-start | bytes 393224 | tf_op jit(solution)/shard_map/ppermute | solution.py:35
  18.7 0.9 %copy-start.3 = (bf16[2,64,512]{2,1,0:T(8,128)(2,1)S(1)}, bf16[2,64,512]{2,1,0:T(8,128)(2,1)}, u32[]{:S(2)}) copy-start(bf16[2,64,512]{2,1,0:T(8,128)(2,1)} %own_up.1) | copy-start | bytes 393220
  21.3 4.7 %collective-permute-start.3 = (bf16[384,128]{1,0:T(8,128)(2,1)S(1)}, bf16[384,128]{1,0:T(8,128)(2,1)S(1)}, u32[]{:S(2)}, u32[]{:S(2)}) collective-permute-start(bf16[384,128]{1,0:T(8,128)(2,1)S(1)} %h_part.1.refs_4_), channel_id=1, source_target_pairs={{0,2},{2,0},{1,3},{3,1},{4,6},{6,4},{5,7},{7,5},{8,10},{10,8},{9,1... | collective-permute-start | bytes 294920 | tf_op jit(solution)/shard_map/ppermute | solution.py:35
  27.4 5.5 %copy-start.2 = (bf16[2,1024,64]{1,2,0:T(8,128)(2,1)S(1)}, bf16[2,1024,64]{1,2,0:T(8,128)(2,1)}, u32[]{:S(2)}) copy-start(bf16[2,1024,64]{1,2,0:T(8,128)(2,1)} %param.9) | copy-start | bytes 786436
  27.4 20.4 %collective-permute-start.8 = (bf16[768,512]{1,0:T(8,128)(2,1)}, bf16[768,512]{1,0:T(8,128)(2,1)S(1)}, u32[]{:S(2)}, u32[]{:S(2)}) collective-permute-start(bf16[768,512]{1,0:T(8,128)(2,1)} %act.7), channel_id=1, source_target_pairs={{0,2},{2,0},{1,3},{3,1},{4,6},{6,4},{5,7},{7,5},{8,10},{10,8},{9,1... | collective-permute-start | bytes 2359304 | tf_op jit(solution)/shard_map/ppermute | solution.py:35
  29.4 7.7 %collective-permute-start.10 = (bf16[512,512]{1,0:T(8,128)(2,1)S(1)}, bf16[512,512]{1,0:T(8,128)(2,1)S(1)}, u32[]{:S(2)}, u32[]{:S(2)}) collective-permute-start(bf16[512,512]{1,0:T(8,128)(2,1)S(1)} %collective-permute-done.7.refs_0_), channel_id=1, source_target_pairs={{0,1},{1,0},{2,3},{3,2},{4,5},{5,4},{6,7},{7,6},{8,9},{9,8},{10,11... | collective-permute-start | bytes 1572872 | tf_op jit(solution)/shard_map/ppermute | solution.py:35
  29.4 6.7 %collective-permute-start.9 = (bf16[64,1024]{1,0:T(8,128)(2,1)S(1)}, bf16[64,1024]{1,0:T(8,128)(2,1)S(1)}, u32[]{:S(2)}, u32[]{:S(2)}) collective-permute-start(bf16[64,1024]{1,0:T(8,128)(2,1)S(1)} %get-tuple-element.44), channel_id=1, source_target_pairs={{0,12},{4,0},{8,4},{12,8},{1,13},{5,1},{9,5},{13,9},{2,14},{6,2},{... | collective-permute-start | bytes 393224 | tf_op jit(solution)/shard_map/ppermute | solution.py:35
  32.2 20.3 %collective-permute-start.11 = (bf16[64,1024]{1,0:T(8,128)(2,1)S(1)}, bf16[64,1024]{1,0:T(8,128)(2,1)S(1)}, u32[]{:S(2)}, u32[]{:S(2)}) collective-permute-start(bf16[64,1024]{1,0:T(8,128)(2,1)S(1)} %get-tuple-element.48), channel_id=1, source_target_pairs={{0,8},{4,12},{8,0},{12,4},{1,9},{5,13},{9,1},{13,5},{2,10},{6,14},... | collective-permute-start | bytes 393224 | tf_op jit(solution)/shard_map/ppermute | solution.py:35
  32.9 19.7 %collective-permute-start.12 = (bf16[64,1024]{1,0:T(8,128)(2,1)S(1)}, bf16[64,1024]{1,0:T(8,128)(2,1)S(1)}, u32[]{:S(2)}, u32[]{:S(2)}) collective-permute-start(bf16[64,1024]{1,0:T(8,128)(2,1)S(1)} %get-tuple-element.49), channel_id=1, source_target_pairs={{0,4},{4,8},{8,12},{12,0},{1,5},{5,9},{9,13},{13,1},{2,6},{6,10},{... | collective-permute-start | bytes 393224 | tf_op jit(solution)/shard_map/ppermute | solution.py:35
  36.1 16.4 %collective-permute-start.13 = (bf16[384,128]{1,0:T(8,128)(2,1)S(1)}, bf16[384,128]{1,0:T(8,128)(2,1)S(1)}, u32[]{:S(2)}, u32[]{:S(2)}) collective-permute-start(bf16[384,128]{1,0:T(8,128)(2,1)S(1)} %u_part.1._.refs_3_), channel_id=1, source_target_pairs={{0,2},{2,0},{1,3},{3,1},{4,6},{6,4},{5,7},{7,5},{8,10},{10,8},{9,1... | collective-permute-start | bytes 294920 | tf_op jit(solution)/shard_map/ppermute | solution.py:35
  38.5 26.8 %collective-permute-start.14 = (bf16[768,512]{1,0:T(8,128)(2,1)S(1)}, bf16[768,512]{1,0:T(8,128)(2,1)S(1)}, u32[]{:S(2)}, u32[]{:S(2)}) collective-permute-start(bf16[768,512]{1,0:T(8,128)(2,1)S(1)} %get-tuple-element.51), channel_id=1, source_target_pairs={{0,2},{2,0},{1,3},{3,1},{4,6},{6,4},{5,7},{7,5},{8,10},{10,8},{9,1... | collective-permute-start | bytes 2359304 | tf_op jit(solution)/shard_map/ppermute | solution.py:35
  54.3 11.0 %copy-start.4 = (bf16[2,64,512]{2,1,0:T(8,128)(2,1)S(1)}, bf16[2,64,512]{2,1,0:T(8,128)(2,1)}, u32[]{:S(2)}) copy-start(bf16[2,64,512]{2,1,0:T(8,128)(2,1)} %own_up.1) | copy-start | bytes 393220
  54.3 4.3 %collective-permute-start.15 = (bf16[64,512]{1,0:T(8,128)(2,1)S(1)}, bf16[64,512]{1,0:T(8,128)(2,1)S(1)}, u32[]{:S(2)}, u32[]{:S(2)}) collective-permute-start(bf16[64,512]{1,0:T(8,128)(2,1)S(1)} %get-tuple-element.55), channel_id=1, source_target_pairs={{0,12},{4,0},{8,4},{12,8},{1,13},{5,1},{9,5},{13,9},{2,14},{6,2},{... | collective-permute-start | bytes 196616 | tf_op jit(solution)/shard_map/ppermute | solution.py:35
  55.4 5.9 %collective-permute-start.16 = (bf16[64,512]{1,0:T(8,128)(2,1)S(1)}, bf16[64,512]{1,0:T(8,128)(2,1)S(1)}, u32[]{:S(2)}, u32[]{:S(2)}) collective-permute-start(bf16[64,512]{1,0:T(8,128)(2,1)S(1)} %get-tuple-element.56), channel_id=1, source_target_pairs={{0,8},{4,12},{8,0},{12,4},{1,9},{5,13},{9,1},{13,5},{2,10},{6,14},... | collective-permute-start | bytes 196616 | tf_op jit(solution)/shard_map/ppermute | solution.py:35
  56.0 6.1 %collective-permute-start.17 = (bf16[64,512]{1,0:T(8,128)(2,1)S(1)}, bf16[64,512]{1,0:T(8,128)(2,1)S(1)}, u32[]{:S(2)}, u32[]{:S(2)}) collective-permute-start(bf16[64,512]{1,0:T(8,128)(2,1)S(1)} %get-tuple-element.57), channel_id=1, source_target_pairs={{0,4},{4,8},{8,12},{12,0},{1,5},{5,9},{9,13},{13,1},{2,6},{6,10},{... | collective-permute-start | bytes 196616 | tf_op jit(solution)/shard_map/ppermute | solution.py:35
  62.5 1.8 %collective-permute-start.18 = (bf16[2,64,1536]{2,1,0:T(8,128)(2,1)S(1)}, bf16[2,64,1536]{2,1,0:T(8,128)(2,1)S(1)}, u32[]{:S(2)}, u32[]{:S(2)}) collective-permute-start(bf16[2,64,1536]{2,1,0:T(8,128)(2,1)S(1)} %sites.1.refs_0_), channel_id=1, source_target_pairs={{0,1},{1,0},{2,3},{3,2},{4,5},{5,4},{6,7},{7,6},{8,9},{9,8},{10,11... | collective-permute-start | bytes 1179656 | tf_op jit(solution)/shard_map/ppermute | solution.py:35

commit v8 on v6

--- a/solution.py
+++ b/solution.py
@@ -146,8 +146,8 @@
         outs[s][...] = nn(x[...], rows[s][...]).astype(BF16)
 
 
-def back_kernel(n_dp, n_mp, table, _, *refs):
-    w, gys, rows, wide, own_down, downs, out, token, own, maps = (
+def back_kernel(n_dp, n_mp, table, *refs):
+    w, gys, rows, wide, own_down, downs, out, picks, own, maps = (
         refs[0], refs[1:1 + n_mp], refs[1 + n_mp:2 * n_mp], refs[2 * n_mp], refs[2 * n_mp + 1],
         refs[2 * n_mp + 2:-4], refs[-4], refs[-3], refs[-2], refs[-1],
     )
@@ -155,7 +155,11 @@
 
     @pl.when(pl.program_id(0) == 0)
     def _():
-        token[...] = jnp.zeros_like(token)
+        row = lax.broadcasted_iota(jnp.int32, picks.shape, 0)
+        sites = jnp.zeros(picks.shape, jnp.int32)
+        for s in range(n_dp):
+            sites = jnp.where(row == s, wanted_site(table, n_dp, s), sites)
+        picks[...] = sites
         own[...] = w[pl.ds(pl.multiple_of(lax.axis_index("mp") * feat, feat), feat), :]
         gather_maps(n_dp, table, own_down, downs, maps)
 
@@ -166,17 +170,12 @@
 
 
 def own_kernel(n_dp, table, w, x, wide, own_up, *refs):
-    ups, out, picks, maps = refs[:n_dp - 1], refs[n_dp - 1], refs[n_dp], refs[n_dp + 1]
+    ups, out, maps = refs[:n_dp - 1], refs[n_dp - 1], refs[n_dp]
     feat = x.shape[1]
 
     @pl.when(pl.program_id(0) == 0)
     def _():
         gather_maps(n_dp, table, own_up, ups, maps)
-        row = lax.broadcasted_iota(jnp.int32, picks.shape, 0)
-        total = jnp.zeros(picks.shape, jnp.int32)
-        for s in range(n_dp):
-            total = jnp.where(row == s, wanted_site(table, n_dp, s), total)
-        picks[...] = total
 
     own = w[pl.ds(pl.multiple_of(lax.axis_index("mp") * feat, feat), feat), :]
     out[...] = nn(x[...], own) + SCALE * nn(wide[...], maps[...])
@@ -266,30 +265,27 @@
     )(u_parts[0], down_back[1], x, *parts)
     w_rows = sent[n_other:]
     y_got = [shift(sent[s - 1], "mp", n_mp - s) for s in range(1, n_mp)]
-    up_back, u_wide = gradient(gy, u_parts, down_back[2:] + gy_got, "up", GRAD_COST)
-
-    y_own, picks = call(
-        functools.partial(own_kernel, n_dp), "y_own",
-        [shape(tok, cols, dtype=F32), shape(-(-n_dp // 8) * 8, 128, dtype=jnp.int32)],
+    back, picks = call(
+        functools.partial(back_kernel, n_dp, n_mp), "back",
+        [shape(tok, feat), shape(-(-n_dp // 8) * 8, 128, dtype=jnp.int32)],
+        [SMEM, whole(*w.shape)] + [row_block(cols)] * n_mp + [whole(feat, cols)] * n_other
+        + [row_block(n_dp * rank), whole(*down.shape)] + [whole(rank, feat)] * away,
+        [row_block(feat), whole(-(-n_dp // 8) * 8, 128)],
+        [pltpu.VMEM((feat, cols), BF16), pltpu.VMEM((n_dp * rank, feat), BF16)], grid=(TILES,),
+    )(table, w, gy, *gy_got, *w_rows, h_wide, down, *downs)
+    up_back, u_wide = gradient(gy, u_parts, [picks] + down_back[2:] + gy_got, "up", GRAD_COST)
+
+    y_own = call(
+        functools.partial(own_kernel, n_dp), "y_own", shape(tok, cols, dtype=F32),
         [SMEM, whole(*w.shape), row_block(feat), row_block(n_dp * rank), whole(*up.shape)]
         + [whole(rank, cols)] * away,
-        [row_block(cols), whole(-(-n_dp // 8) * 8, 128)],
-        [pltpu.VMEM((n_dp * rank, cols), BF16)], grid=(TILES,),
+        row_block(cols), [pltpu.VMEM((n_dp * rank, cols), BF16)], grid=(TILES,),
     )(table, w, x, u_wide, up, *ups)
-
-    back, token = call(
-        functools.partial(back_kernel, n_dp, n_mp), "back",
-        [shape(tok, feat), shape(8, 128, dtype=F32)],
-        [SMEM, ANY, whole(*w.shape)] + [row_block(cols)] * n_mp + [whole(feat, cols)] * n_other
-        + [row_block(n_dp * rank), whole(*down.shape)] + [whole(rank, feat)] * away,
-        [row_block(feat), whole(8, 128)],
-        [pltpu.VMEM((feat, cols), BF16), pltpu.VMEM((n_dp * rank, feat), BF16)], grid=(TILES,),
-    )(table, u_wide, w, gy, *gy_got, *w_rows, h_wide, down, *downs)
 
     summed = call(
         functools.partial(site_kernel, n_dp, feat), "sites",
         shape(sites, rank, feat + cols), [VMEM, ANY] + [VMEM] * (2 * n_dp), VMEM,
-    )(picks, token, *down_back, *up_back)
+    )(picks, y_own, *down_back, *up_back)
     both = [summed] + [shift(summed, "pair", q) for q in range(1, n_pair)]
     down_grad, up_grad = call(
         functools.partial(last_kernel, feat), "gradients",

time: 60.7 us -> 60.1 us (level)
  waiting for transfers between devices: 12 us -> 10.2 us
  starting transfers between devices: 29 us -> 30.2 us
    ppermute x19, waiting for transfers between devices: 12 us -> 10.2 us  [shift(): lax.ppermute(value, axis, [(i, (i + by) % size) for i in range(size)])]
    ppermute x19, starting transfers between devices: 29 us -> 30.2 us  [shift(): lax.ppermute(value, axis, [(i, (i + by) % size) for i in range(size)])]
where the time goes in v8:
time: 60.1 us; the launch traced here: 60 us
  starting transfers between devices  30.2 us (50%)
  Pallas kernels  18.7 us (31%)
  waiting for transfers between devices  10.2 us (17%)
  between operations  0.81 us (1%)
    ppermute x19, starting transfers between devices, shift(): lax.ppermute(value, axis, [(i, (i + by) % size) for i in range(size)])  30.2 us
    ppermute x19, waiting for transfers between devices, shift(): lax.ppermute(value, axis, [(i, (i + by) % size) for i in range(size)])  10.2 us
    pallas_call x1, Pallas kernels, shards(): call(functools.partial(back_kernel, n_dp, n_mp), 'back', [shape(tok, feat...  4.09 us
    pallas_call x1, Pallas kernels, shards(): call(functools.partial(pack_kernel, n_dp, n_mp, n_pair), 'pack', [shape(r...  3.23 us
    pallas_call x2, Pallas kernels, gradient(): call(functools.partial(grad_kernel, n_dp, n_mp, len(behind)), name + '_gr...  2.45 us
    pallas_call x2, Pallas kernels, low_rank(): call(functools.partial(reduce_kernel, n_dp), name + '_part', shape(tok //...  2.43 us
    pallas_call x1, Pallas kernels, shards(): call(functools.partial(own_kernel, n_dp), 'y_own', shape(tok, cols, dtype...  2.18 us
    pallas_call x1, Pallas kernels, shards(): call(add_kernel, 'y_add', shape(tok, cols), [row_block(cols)] * n_mp, row...  1.5 us
  transfers between devices with their start and end apart: 19, of which 5 were waited for; matrix products, arithmetic and copies ran while one was open for 0% of the time, Pallas kernels for 23%

profile of v8, /device:TPU:0, one launch (start us, length us, event | category | flops | bytes accessed | tf_op | source)
XLA Modules:
  0.0 60.0 jit_solution(991704882397848853)
XLA Ops:
  0.7 3.2 %pack.1 = (bf16[64,512]{1,0:T(8,128)(2,1)}, bf16[64,512]{1,0:T(8,128)(2,1)}, bf16[64,512]{1,0:T(8,128)(2,1)}, bf16[64,1024]{1,0:T(8,128)(2,1)}, bf16[64,1024]{1,...) custom-call(s32[1,2,4]{2,1,0:T(2,128)} %table.9, bf16[2,64,1024]{2,1,0:T(8,128)(2,1)} %bitcast.2, ...), custom_call_target="tpu_custom_call" | custom-call | flops 1 | bytes 1 | tf_op jit(solution)/shard_map/pack/pallas_call | solution.py:225
  3.9 3.0 %collective-permute-start = (bf16[512,512]{1,0:T(8,128)(2,1)}, bf16[512,512]{1,0:T(8,128)(2,1)S(1)}, u32[]{:S(2)}, u32[]{:S(2)}) collective-permute-start(bf16[512,512]{1,0:T(8,128)(2,1)} %get-tuple-element.32), channel_id=1, source_target_pairs={{0,2},{2,0},{1,3},{3,1},{4,6},{6,4},{5,7},{7,5},{8,10},{10,8},{9,1... | collective-permute-start | bytes 1572872 | tf_op jit(solution)/shard_map/ppermute | solution.py:35
  6.9 2.6 %collective-permute-start.2 = (bf16[64,512]{1,0:T(8,128)(2,1)}, bf16[64,512]{1,0:T(8,128)(2,1)S(1)}, u32[]{:S(2)}, u32[]{:S(2)}) collective-permute-start(bf16[64,512]{1,0:T(8,128)(2,1)} %get-tuple-element.35), channel_id=1, source_target_pairs={{0,8},{4,12},{8,0},{12,4},{1,9},{5,13},{9,1},{13,5},{2,10},{6,14},... | collective-permute-start | bytes 196616 | tf_op jit(solution)/shard_map/ppermute | solution.py:35
  9.5 1.6 %collective-permute-start.6 = (bf16[64,512]{1,0:T(8,128)(2,1)}, bf16[64,512]{1,0:T(8,128)(2,1)S(1)}, u32[]{:S(2)}, u32[]{:S(2)}) collective-permute-start(bf16[64,512]{1,0:T(8,128)(2,1)} %get-tuple-element.41), channel_id=1, source_target_pairs={{0,4},{4,8},{8,12},{12,0},{1,5},{5,9},{9,13},{13,1},{2,6},{6,10},{... | collective-permute-start | bytes 196616 | tf_op jit(solution)/shard_map/ppermute | solution.py:35
  11.1 2.2 %collective-permute-start.7 = (bf16[64,512]{1,0:T(8,128)(2,1)}, bf16[64,512]{1,0:T(8,128)(2,1)S(1)}, u32[]{:S(2)}, u32[]{:S(2)}) collective-permute-start(bf16[64,512]{1,0:T(8,128)(2,1)} %get-tuple-element.42), channel_id=1, source_target_pairs={{0,12},{4,0},{8,4},{12,8},{1,13},{5,1},{9,5},{13,9},{2,14},{6,2},{... | collective-permute-start | bytes 196616 | tf_op jit(solution)/shard_map/ppermute | solution.py:35
  13.3 1.2 %collective-permute-start.3 = (bf16[64,1024]{1,0:T(8,128)(2,1)}, bf16[64,1024]{1,0:T(8,128)(2,1)S(1)}, u32[]{:S(2)}, u32[]{:S(2)}) collective-permute-start(bf16[64,1024]{1,0:T(8,128)(2,1)} %get-tuple-element.36), channel_id=1, source_target_pairs={{0,4},{4,8},{8,12},{12,0},{1,5},{5,9},{9,13},{13,1},{2,6},{6,10},{... | collective-permute-start | bytes 393224 | tf_op jit(solution)/shard_map/ppermute | solution.py:35
  14.6 3.7 %collective-permute-start.4 = (bf16[64,1024]{1,0:T(8,128)(2,1)}, bf16[64,1024]{1,0:T(8,128)(2,1)S(1)}, u32[]{:S(2)}, u32[]{:S(2)}) collective-permute-start(bf16[64,1024]{1,0:T(8,128)(2,1)} %get-tuple-element.38), channel_id=1, source_target_pairs={{0,8},{4,12},{8,0},{12,4},{1,9},{5,13},{9,1},{13,5},{2,10},{6,14},... | collective-permute-start | bytes 393224 | tf_op jit(solution)/shard_map/ppermute | solution.py:35
  18.2 0.3 collective-permute-start.5
  18.5 1.1 %h_part.1.refs_3_ = bf16[384,128]{1,0:T(8,128)(2,1)S(1)} custom-call(s32[12]{0:T(128)S(1)} %copy-done.6, s32[1,2,4]{2,1,0:T(2,128)S(1)} %copy-done.5, bf16[768,512]{1,0:T(8,128)(2,1)S(1)} %copy-done.2, bf16[64,512]{1,0:T(8,128)(2,1)S(1)} %collective-permute-done.6._.refs_0_, bf16[2,64,512]{2,1,0:T(8,128)(2,1)S(1)} %copy-done.4, ...), custom_call_target="tpu_custom_call" | custom-call | flops 1 | bytes 1 | tf_op jit(solution)/shard_map/h_part/pallas_call | solution.py:236
  19.7 0.6 collective-permute-start.8
  20.3 1.5 %collective-permute-start.1 = (bf16[768,512]{1,0:T(8,128)(2,1)S(1)}, bf16[768,512]{1,0:T(8,128)(2,1)S(1)}, u32[]{:S(2)}, u32[]{:S(2)}) collective-permute-start(bf16[768,512]{1,0:T(8,128)(2,1)S(1)} %copy-done.2), channel_id=1, source_target_pairs={{0,2},{2,0},{1,3},{3,1},{4,6},{6,4},{5,7},{7,5},{8,10},{10,8},{9,1... | collective-permute-start | bytes 2359304 | tf_op jit(solution)/shard_map/ppermute | solution.py:35
  21.8 3.7 %collective-permute-done.8.refs_4_ = bf16[384,128]{1,0:T(8,128)(2,1)S(1)} collective-permute-done((bf16[384,128]{1,0:T(8,128)(2,1)S(1)}, bf16[384,128]{1,0:T(8,128)(2,1)S(1)}, u32[]{:S(2)}, u32[]{:S(2)}) %collective-permute-start.8) | collective-permute-done | bytes 98336 | tf_op jit(solution)/shard_map/ppermute | solution.py:35
  25.5 1.3 %down_grad.1 = (bf16[64,1024]{1,0:T(8,128)(2,1)S(1)}, bf16[64,1024]{1,0:T(8,128)(2,1)S(1)}, bf16[64,1024]{1,0:T(8,128)(2,1)S(1)}, bf16[64,1024]{1,0:T(8,128)(2,1)S(1)}, bf16[768,256]{1,0:T(8,128)(2,1)S(1)}) custom-call(s32[12]{0:T(128)S(1)} %copy-done.6, bf16[768,1024]{1,0:T(8,128)(2,1)S(1)} %copy-done.1, ...), custom_call_target="tpu_custom_call" | custom-call | flops 15000000512 | bytes 1 | tf_op jit(solution)/shard_map/down_grad/pallas_call | solution.py:244
  26.8 0.1 collective-permute-start.10
  26.9 5.1 %collective-permute-start.9 = (bf16[64,1024]{1,0:T(8,128)(2,1)S(1)}, bf16[64,1024]{1,0:T(8,128)(2,1)S(1)}, u32[]{:S(2)}, u32[]{:S(2)}) collective-permute-start(bf16[64,1024]{1,0:T(8,128)(2,1)S(1)} %get-tuple-element.44), channel_id=1, source_target_pairs={{0,12},{4,0},{8,4},{12,8},{1,13},{5,1},{9,5},{13,9},{2,14},{6,2},{... | collective-permute-start | bytes 393224 | tf_op jit(solution)/shard_map/ppermute | solution.py:35
  32.0 0.7 %collective-permute-start.12 = (bf16[64,1024]{1,0:T(8,128)(2,1)S(1)}, bf16[64,1024]{1,0:T(8,128)(2,1)S(1)}, u32[]{:S(2)}, u32[]{:S(2)}) collective-permute-start(bf16[64,1024]{1,0:T(8,128)(2,1)S(1)} %get-tuple-element.49), channel_id=1, source_target_pairs={{0,4},{4,8},{8,12},{12,0},{1,5},{5,9},{9,13},{13,1},{2,6},{6,10},{... | collective-permute-start | bytes 393224 | tf_op jit(solution)/shard_map/ppermute | solution.py:35
  32.7 1.3 %u_part.1._.refs_4_ = bf16[384,128]{1,0:T(8,128)(2,1)S(1)} custom-call(s32[12]{0:T(128)S(1)} %copy-done.6, s32[1,2,4]{2,1,0:T(2,128)S(1)} %copy-done.5, bf16[768,1024]{1,0:T(8,128)(2,1)S(1)} %copy-done.1, bf16[768,256]{1,0:T(8,128)(2,1)S(1)} %get-tuple-element.43._.refs_4_, bf16[2,64,1024]{2,1,0:T(8,128)(2,1)S(1)} %bitcast.3, ...), custom_call_target="tpu_custom_call" | custom-call | flops 1 | bytes 1 | tf_op jit(solution)/shard_map/u_part/pallas_call | solution.py:236
  34.0 1.9 %collective-permute-done.9.__.refs_1_ = bf16[64,1024]{1,0:T(8,128)(2,1)S(1)} collective-permute-done((bf16[64,1024]{1,0:T(8,128)(2,1)S(1)}, bf16[64,1024]{1,0:T(8,128)(2,1)S(1)}, u32[]{:S(2)}, u32[]{:S(2)}) %collective-permute-start.9) | collective-permute-done | bytes 131104 | tf_op jit(solution)/shard_map/ppermute | solution.py:35
  35.9 0.5 collective-permute-start.13
  36.4 1.4 %y_send.1 = (bf16[768,512]{1,0:T(8,128)(2,1)S(1)}, bf16[1024,512]{1,0:T(8,128)(2,1)S(1)}) custom-call(bf16[384,128]{1,0:T(8,128)(2,1)S(1)} %u_part.1._.refs_4_, bf16[64,1024]{1,0:T(8,128)(2,1)S(1)} %collective-permute-done.9.__.refs_1_, bf16[768,1024]{1,0:T(8,128)(2,1)S(1)} %copy-done.1, bf16[512,512]{1,0:T(8,128)(2,1)S(1)} %collective-permute-done.refs_0_, ...), custom_call_target="tpu_custom_call" | custom-call | flops 1 | bytes 1 | tf_op jit(solution)/shard_map/y_send/pallas_call | solution.py:259
  37.9 1.6 %collective-permute-start.14 = (bf16[768,512]{1,0:T(8,128)(2,1)S(1)}, bf16[768,512]{1,0:T(8,128)(2,1)S(1)}, u32[]{:S(2)}, u32[]{:S(2)}) collective-permute-start(bf16[768,512]{1,0:T(8,128)(2,1)S(1)} %get-tuple-element.51), channel_id=1, source_target_pairs={{0,2},{2,0},{1,3},{3,1},{4,6},{6,4},{5,7},{7,5},{8,10},{10,8},{9,1... | collective-permute-start | bytes 2359304 | tf_op jit(solution)/shard_map/ppermute | solution.py:35
  39.4 0.5 collective-permute-done.1.refs_2_.refs_3_
  39.9 4.1 %back.1 = (bf16[768,1024]{1,0:T(8,128)(2,1)}, s32[8,128]{1,0:T(8,128)S(1)}) custom-call(s32[1,2,4]{2,1,0:T(2,128)S(1)} %copy-done.5, bf16[2048,512]{1,0:T(8,128)(2,1)S(1)} %copy-done, bf16[768,512]{1,0:T(8,128)(2,1)S(1)} %copy-done.2, bf16[768,512]{1,0:T(8,128)(2,1)S(1)} %collective-permute-done.1.refs_2_.refs_3_, ...), custom_call_target="tpu_custom_call" | custom-call | flops 1 | bytes 1 | tf_op jit(solution)/shard_map/back/pallas_call | solution.py:268
  44.1 1.1 %up_grad.1 = (bf16[64,512]{1,0:T(8,128)(2,1)S(1)}, bf16[64,512]{1,0:T(8,128)(2,1)S(1)}, bf16[64,512]{1,0:T(8,128)(2,1)S(1)}, bf16[64,512]{1,0:T(8,128)(2,1)S(1)}, bf16[768,256]{1,0:T(8,128)(2,1)S(1)}) custom-call(s32[12]{0:T(128)S(1)} %copy-done.6, bf16[768,512]{1,0:T(8,128)(2,1)S(1)} %copy-done.2, s32[8,128]{1,0:T(8,128)S(1)} %get-tuple-element.47.refs_0_.picks, ...), custom_call_target="tpu_custom_call" | custom-call | flops 15000000512 | bytes 1 | tf_op jit(solution)/shard_map/up_grad/pallas_call | solution.py:244
  45.2 3.9 %collective-permute-start.15 = (bf16[64,512]{1,0:T(8,128)(2,1)S(1)}, bf16[64,512]{1,0:T(8,128)(2,1)S(1)}, u32[]{:S(2)}, u32[]{:S(2)}) collective-permute-start(bf16[64,512]{1,0:T(8,128)(2,1)S(1)} %get-tuple-element.55), channel_id=1, source_target_pairs={{0,12},{4,0},{8,4},{12,8},{1,13},{5,1},{9,5},{13,9},{2,14},{6,2},{... | collective-permute-start | bytes 196616 | tf_op jit(solution)/shard_map/ppermute | solution.py:35
  49.1 1.7 %collective-permute-start.17 = (bf16[64,512]{1,0:T(8,128)(2,1)S(1)}, bf16[64,512]{1,0:T(8,128)(2,1)S(1)}, u32[]{:S(2)}, u32[]{:S(2)}) collective-permute-start(bf16[64,512]{1,0:T(8,128)(2,1)S(1)} %get-tuple-element.57), channel_id=1, source_target_pairs={{0,4},{4,8},{8,12},{12,0},{1,5},{5,9},{9,13},{13,1},{2,6},{6,10},{... | collective-permute-start | bytes 196616 | tf_op jit(solution)/shard_map/ppermute | solution.py:35
  50.8 2.2 %y_own.1.refs_0_._ = f32[768,512]{1,0:T(8,128)S(1)} custom-call(s32[1,2,4]{2,1,0:T(2,128)S(1)} %copy-done.5, bf16[2048,512]{1,0:T(8,128)(2,1)S(1)} %copy-done, bf16[768,1024]{1,0:T(8,128)(2,1)S(1)} %copy-done.1, bf16[768,256]{1,0:T(8,128)(2,1)S(1)} %get-tuple-element.50.wide, bf16[2,64,512]{2,1,0:T(8,128)(2,1)S(1)} %copy-done.4, ...), custom_call_target="tpu_custom_call" | custom-call | flops 1 | bytes 1 | tf_op jit(solution)/shard_map/y_own/pallas_call | solution.py:278
  53.0 2.3 %collective-permute-done.16.refs_6_ = bf16[64,512]{1,0:T(8,128)(2,1)S(1)} collective-permute-done((bf16[64,512]{1,0:T(8,128)(2,1)S(1)}, bf16[64,512]{1,0:T(8,128)(2,1)S(1)}, u32[]{:S(2)}, u32[]{:S(2)}) %collective-permute-start.16) | collective-permute-done | bytes 65568 | tf_op jit(solution)/shard_map/ppermute | solution.py:35
  55.2 0.5 sites.1.refs_0_
  55.8 1.7 %collective-permute-done.18.refs_1_ = bf16[2,64,1536]{2,1,0:T(8,128)(2,1)S(1)} collective-permute-done((bf16[2,64,1536]{2,1,0:T(8,128)(2,1)S(1)}, bf16[2,64,1536]{2,1,0:T(8,128)(2,1)S(1)}, u32[]{:S(2)}, u32[]{:S(2)}) %collective-permute-start.18) | collective-permute-done | bytes 393248 | tf_op jit(solution)/shard_map/ppermute | solution.py:35
  57.5 0.9 %gradients.1 = (f32[2,64,1024]{2,1,0:T(8,128)}, f32[2,64,512]{2,1,0:T(8,128)}) custom-call(bf16[2,64,1536]{2,1,0:T(8,128)(2,1)S(1)} %sites.1.refs_0_, bf16[2,64,1536]{2,1,0:T(8,128)(2,1)S(1)} %collective-permute-done.18.refs_1_), custom_call_target="tpu_custom_call" | custom-call | flops 1 | bytes 1 | tf_op jit(solution)/shard_map/gradients/pallas_call | solution.py:290
  58.5 1.5 %y_add.1 = bf16[768,512]{1,0:T(8,128)(2,1)} custom-call(f32[768,512]{1,0:T(8,128)S(1)} %y_own.1.refs_0_._, bf16[768,512]{1,0:T(8,128)(2,1)S(1)} %collective-permute-done.14.refs_1_), custom_call_target="tpu_custom_call" | custom-call | flops 1 | bytes 1 | tf_op jit(solution)/shard_map/y_add/pallas_call | solution.py:296
  (31 shorter events, 0.2 us)
Async XLA Ops:
  0.6 17.9 %copy-start.4 = (bf16[2,64,512]{2,1,0:T(8,128)(2,1)S(1)}, bf16[2,64,512]{2,1,0:T(8,128)(2,1)}, u32[]{:S(2)}) copy-start(bf16[2,64,512]{2,1,0:T(8,128)(2,1)} %own_up.1) | copy-start | bytes 393220
  0.6 17.9 %copy-start.5 = (s32[1,2,4]{2,1,0:T(2,128)S(1)}, s32[1,2,4]{2,1,0:T(2,128)}, u32[]{:S(2)}) copy-start(s32[1,2,4]{2,1,0:T(2,128)} %table.9) | copy-start | bytes 100
  0.7 17.9 %copy-start.2 = (bf16[768,512]{1,0:T(8,128)(2,1)S(1)}, bf16[768,512]{1,0:T(8,128)(2,1)}, u32[]{:S(2)}) copy-start(bf16[768,512]{1,0:T(8,128)(2,1)} %act.7) | copy-start | bytes 2359300
  0.7 17.9 %copy-start.6 = (s32[12]{0:T(128)S(1)}, s32[12]{0:T(128)}, u32[]{:S(2)}) copy-start(s32[12]{0:T(128)} %owner.7) | copy-start | bytes 148
  0.7 24.8 %copy-start.1 = (bf16[768,1024]{1,0:T(8,128)(2,1)S(1)}, bf16[768,1024]{1,0:T(8,128)(2,1)}, u32[]{:S(2)}) copy-start(bf16[768,1024]{1,0:T(8,128)(2,1)} %x.3) | copy-start | bytes 4718596
  3.9 16.3 %collective-permute-start = (bf16[512,512]{1,0:T(8,128)(2,1)}, bf16[512,512]{1,0:T(8,128)(2,1)S(1)}, u32[]{:S(2)}, u32[]{:S(2)}) collective-permute-start(bf16[512,512]{1,0:T(8,128)(2,1)} %get-tuple-element.32), channel_id=1, source_target_pairs={{0,2},{2,0},{1,3},{3,1},{4,6},{6,4},{5,7},{7,5},{8,10},{10,8},{9,1... | collective-permute-start | bytes 1572872 | tf_op jit(solution)/shard_map/ppermute | solution.py:35
  6.9 6.4 %collective-permute-start.2 = (bf16[64,512]{1,0:T(8,128)(2,1)}, bf16[64,512]{1,0:T(8,128)(2,1)S(1)}, u32[]{:S(2)}, u32[]{:S(2)}) collective-permute-start(bf16[64,512]{1,0:T(8,128)(2,1)} %get-tuple-element.35), channel_id=1, source_target_pairs={{0,8},{4,12},{8,0},{12,4},{1,9},{5,13},{9,1},{13,5},{2,10},{6,14},... | collective-permute-start | bytes 196616 | tf_op jit(solution)/shard_map/ppermute | solution.py:35
  9.5 8.7 %collective-permute-start.6 = (bf16[64,512]{1,0:T(8,128)(2,1)}, bf16[64,512]{1,0:T(8,128)(2,1)S(1)}, u32[]{:S(2)}, u32[]{:S(2)}) collective-permute-start(bf16[64,512]{1,0:T(8,128)(2,1)} %get-tuple-element.41), channel_id=1, source_target_pairs={{0,4},{4,8},{8,12},{12,0},{1,5},{5,9},{9,13},{13,1},{2,6},{6,10},{... | collective-permute-start | bytes 196616 | tf_op jit(solution)/shard_map/ppermute | solution.py:35
  11.1 7.4 %collective-permute-start.7 = (bf16[64,512]{1,0:T(8,128)(2,1)}, bf16[64,512]{1,0:T(8,128)(2,1)S(1)}, u32[]{:S(2)}, u32[]{:S(2)}) collective-permute-start(bf16[64,512]{1,0:T(8,128)(2,1)} %get-tuple-element.42), channel_id=1, source_target_pairs={{0,12},{4,0},{8,4},{12,8},{1,13},{5,1},{9,5},{13,9},{2,14},{6,2},{... | collective-permute-start | bytes 196616 | tf_op jit(solution)/shard_map/ppermute | solution.py:35
  13.3 12.1 %collective-permute-start.3 = (bf16[64,1024]{1,0:T(8,128)(2,1)}, bf16[64,1024]{1,0:T(8,128)(2,1)S(1)}, u32[]{:S(2)}, u32[]{:S(2)}) collective-permute-start(bf16[64,1024]{1,0:T(8,128)(2,1)} %get-tuple-element.36), channel_id=1, source_target_pairs={{0,4},{4,8},{8,12},{12,0},{1,5},{5,9},{9,13},{13,1},{2,6},{6,10},{... | collective-permute-start | bytes 393224 | tf_op jit(solution)/shard_map/ppermute | solution.py:35
  14.6 10.9 %collective-permute-start.4 = (bf16[64,1024]{1,0:T(8,128)(2,1)}, bf16[64,1024]{1,0:T(8,128)(2,1)S(1)}, u32[]{:S(2)}, u32[]{:S(2)}) collective-permute-start(bf16[64,1024]{1,0:T(8,128)(2,1)} %get-tuple-element.38), channel_id=1, source_target_pairs={{0,8},{4,12},{8,0},{12,4},{1,9},{5,13},{9,1},{13,5},{2,10},{6,14},... | collective-permute-start | bytes 393224 | tf_op jit(solution)/shard_map/ppermute | solution.py:35
  18.2 7.2 %collective-permute-start.5 = (bf16[64,1024]{1,0:T(8,128)(2,1)}, bf16[64,1024]{1,0:T(8,128)(2,1)S(1)}, u32[]{:S(2)}, u32[]{:S(2)}) collective-permute-start(bf16[64,1024]{1,0:T(8,128)(2,1)} %get-tuple-element.40), channel_id=1, source_target_pairs={{0,12},{4,0},{8,4},{12,8},{1,13},{5,1},{9,5},{13,9},{2,14},{6,2},{... | collective-permute-start | bytes 393224 | tf_op jit(solution)/shard_map/ppermute | solution.py:35
  19.6 13.0 %copy-start.3 = (bf16[2,1024,64]{1,2,0:T(8,128)(2,1)S(1)}, bf16[2,1024,64]{1,2,0:T(8,128)(2,1)}, u32[]{:S(2)}) copy-start(bf16[2,1024,64]{1,2,0:T(8,128)(2,1)} %param.9) | copy-start | bytes 786436
  19.7 5.8 %collective-permute-start.8 = (bf16[384,128]{1,0:T(8,128)(2,1)S(1)}, bf16[384,128]{1,0:T(8,128)(2,1)S(1)}, u32[]{:S(2)}, u32[]{:S(2)}) collective-permute-start(bf16[384,128]{1,0:T(8,128)(2,1)S(1)} %h_part.1.refs_3_), channel_id=1, source_target_pairs={{0,2},{2,0},{1,3},{3,1},{4,6},{6,4},{5,7},{7,5},{8,10},{10,8},{9,1... | collective-permute-start | bytes 294920 | tf_op jit(solution)/shard_map/ppermute | solution.py:35
  20.3 19.7 %collective-permute-start.1 = (bf16[768,512]{1,0:T(8,128)(2,1)S(1)}, bf16[768,512]{1,0:T(8,128)(2,1)S(1)}, u32[]{:S(2)}, u32[]{:S(2)}) collective-permute-start(bf16[768,512]{1,0:T(8,128)(2,1)S(1)} %copy-done.2), channel_id=1, source_target_pairs={{0,2},{2,0},{1,3},{3,1},{4,6},{6,4},{5,7},{7,5},{8,10},{10,8},{9,1... | collective-permute-start | bytes 2359304 | tf_op jit(solution)/shard_map/ppermute | solution.py:35
  26.8 9.6 %collective-permute-start.10 = (bf16[512,512]{1,0:T(8,128)(2,1)S(1)}, bf16[512,512]{1,0:T(8,128)(2,1)S(1)}, u32[]{:S(2)}, u32[]{:S(2)}) collective-permute-start(bf16[512,512]{1,0:T(8,128)(2,1)S(1)} %collective-permute-done.refs_0_), channel_id=1, source_target_pairs={{0,1},{1,0},{2,3},{3,2},{4,5},{5,4},{6,7},{7,6},{8,9},{9,8},{10,11... | collective-permute-start | bytes 1572872 | tf_op jit(solution)/shard_map/ppermute | solution.py:35
  26.9 9.0 %collective-permute-start.9 = (bf16[64,1024]{1,0:T(8,128)(2,1)S(1)}, bf16[64,1024]{1,0:T(8,128)(2,1)S(1)}, u32[]{:S(2)}, u32[]{:S(2)}) collective-permute-start(bf16[64,1024]{1,0:T(8,128)(2,1)S(1)} %get-tuple-element.44), channel_id=1, source_target_pairs={{0,12},{4,0},{8,4},{12,8},{1,13},{5,1},{9,5},{13,9},{2,14},{6,2},{... | collective-permute-start | bytes 393224 | tf_op jit(solution)/shard_map/ppermute | solution.py:35
  32.0 12.1 %collective-permute-start.11 = (bf16[64,1024]{1,0:T(8,128)(2,1)S(1)}, bf16[64,1024]{1,0:T(8,128)(2,1)S(1)}, u32[]{:S(2)}, u32[]{:S(2)}) collective-permute-start(bf16[64,1024]{1,0:T(8,128)(2,1)S(1)} %get-tuple-element.48), channel_id=1, source_target_pairs={{0,8},{4,12},{8,0},{12,4},{1,9},{5,13},{9,1},{13,5},{2,10},{6,14},... | collective-permute-start | bytes 393224 | tf_op jit(solution)/shard_map/ppermute | solution.py:35
  32.0 12.1 %collective-permute-start.12 = (bf16[64,1024]{1,0:T(8,128)(2,1)S(1)}, bf16[64,1024]{1,0:T(8,128)(2,1)S(1)}, u32[]{:S(2)}, u32[]{:S(2)}) collective-permute-start(bf16[64,1024]{1,0:T(8,128)(2,1)S(1)} %get-tuple-element.49), channel_id=1, source_target_pairs={{0,4},{4,8},{8,12},{12,0},{1,5},{5,9},{9,13},{13,1},{2,6},{6,10},{... | collective-permute-start | bytes 393224 | tf_op jit(solution)/shard_map/ppermute | solution.py:35
  34.0 6.0 %copy-start = (bf16[2048,512]{1,0:T(8,128)(2,1)S(1)}, bf16[2048,512]{1,0:T(8,128)(2,1)}, u32[]{:S(2)}) copy-start(bf16[2048,512]{1,0:T(8,128)(2,1)} %w.3) | copy-start | bytes 6291460
  35.9 8.1 %collective-permute-start.13 = (bf16[384,128]{1,0:T(8,128)(2,1)S(1)}, bf16[384,128]{1,0:T(8,128)(2,1)S(1)}, u32[]{:S(2)}, u32[]{:S(2)}) collective-permute-start(bf16[384,128]{1,0:T(8,128)(2,1)S(1)} %u_part.1._.refs_4_), channel_id=1, source_target_pairs={{0,2},{2,0},{1,3},{3,1},{4,6},{6,4},{5,7},{7,5},{8,10},{10,8},{9,1... | collective-permute-start | bytes 294920 | tf_op jit(solution)/shard_map/ppermute | solution.py:35
  37.9 20.6 %collective-permute-start.14 = (bf16[768,512]{1,0:T(8,128)(2,1)S(1)}, bf16[768,512]{1,0:T(8,128)(2,1)S(1)}, u32[]{:S(2)}, u32[]{:S(2)}) collective-permute-start(bf16[768,512]{1,0:T(8,128)(2,1)S(1)} %get-tuple-element.51), channel_id=1, source_target_pairs={{0,2},{2,0},{1,3},{3,1},{4,6},{6,4},{5,7},{7,5},{8,10},{10,8},{9,1... | collective-permute-start | bytes 2359304 | tf_op jit(solution)/shard_map/ppermute | solution.py:35
  45.2 7.7 %collective-permute-start.15 = (bf16[64,512]{1,0:T(8,128)(2,1)S(1)}, bf16[64,512]{1,0:T(8,128)(2,1)S(1)}, u32[]{:S(2)}, u32[]{:S(2)}) collective-permute-start(bf16[64,512]{1,0:T(8,128)(2,1)S(1)} %get-tuple-element.55), channel_id=1, source_target_pairs={{0,12},{4,0},{8,4},{12,8},{1,13},{5,1},{9,5},{13,9},{2,14},{6,2},{... | collective-permute-start | bytes 196616 | tf_op jit(solution)/shard_map/ppermute | solution.py:35
  49.1 6.2 %collective-permute-start.16 = (bf16[64,512]{1,0:T(8,128)(2,1)S(1)}, bf16[64,512]{1,0:T(8,128)(2,1)S(1)}, u32[]{:S(2)}, u32[]{:S(2)}) collective-permute-start(bf16[64,512]{1,0:T(8,128)(2,1)S(1)} %get-tuple-element.56), channel_id=1, source_target_pairs={{0,8},{4,12},{8,0},{12,4},{1,9},{5,13},{9,1},{13,5},{2,10},{6,14},... | collective-permute-start | bytes 196616 | tf_op jit(solution)/shard_map/ppermute | solution.py:35
  49.1 6.2 %collective-permute-start.17 = (bf16[64,512]{1,0:T(8,128)(2,1)S(1)}, bf16[64,512]{1,0:T(8,128)(2,1)S(1)}, u32[]{:S(2)}, u32[]{:S(2)}) collective-permute-start(bf16[64,512]{1,0:T(8,128)(2,1)S(1)} %get-tuple-element.57), channel_id=1, source_target_pairs={{0,4},{4,8},{8,12},{12,0},{1,5},{5,9},{9,13},{13,1},{2,6},{6,10},{... | collective-permute-start | bytes 196616 | tf_op jit(solution)/shard_map/ppermute | solution.py:35
  55.7 1.8 %collective-permute-start.18 = (bf16[2,64,1536]{2,1,0:T(8,128)(2,1)S(1)}, bf16[2,64,1536]{2,1,0:T(8,128)(2,1)S(1)}, u32[]{:S(2)}, u32[]{:S(2)}) collective-permute-start(bf16[2,64,1536]{2,1,0:T(8,128)(2,1)S(1)} %sites.1.refs_0_), channel_id=1, source_target_pairs={{0,1},{1,0},{2,3},{3,2},{4,5},{5,4},{6,7},{7,6},{8,9},{9,8},{10,11... | collective-permute-start | bytes 1179656 | tf_op jit(solution)/shard_map/ppermute | solution.py:35

commit v9 on v8

--- a/solution.py
+++ b/solution.py
@@ -58,8 +58,10 @@
         copy.wait()
 
 
-def wanted_site(table, n_dp, s):
-    return table[0, lax.axis_index("pair"), lax.rem(lax.axis_index("dp") + s, n_dp)]
+def wanted_site(table, n_dp, s, q=0):
+    n_pair = lax.axis_size("pair")
+    core = lax.rem(lax.axis_index("pair") + n_pair - q, n_pair)
+    return table[0, core, lax.rem(lax.axis_index("dp") + s, n_dp)]
 
 
 def slot_of(owner, b, n_dp):
@@ -157,8 +159,8 @@
     def _():
         row = lax.broadcasted_iota(jnp.int32, picks.shape, 0)
         sites = jnp.zeros(picks.shape, jnp.int32)
-        for s in range(n_dp):
-            sites = jnp.where(row == s, wanted_site(table, n_dp, s), sites)
+        for k in range(n_dp * lax.axis_size("pair")):
+            sites = jnp.where(row == k, wanted_site(table, n_dp, k % n_dp, k // n_dp), sites)
         picks[...] = sites
         own[...] = w[pl.ds(pl.multiple_of(lax.axis_index("mp") * feat, feat), feat), :]
         gather_maps(n_dp, table, own_down, downs, maps)
@@ -181,32 +183,31 @@
     out[...] = nn(x[...], own) + SCALE * nn(wide[...], maps[...])
 
 
-def add_kernel(*refs):
-    total = refs[0][...]
-    for ref in refs[1:-1]:
-        total = total + ref[...].astype(F32)
-    refs[-1][...] = total.astype(BF16)
-
-
-def site_kernel(n_dp, feat, picks, _, *refs):
-    downs, ups, out = refs[:n_dp], refs[n_dp:2 * n_dp], refs[-1]
+def pick_sum(grads, picks, site):
+    total = jnp.zeros(grads[0].shape, F32)
+    for k, grad in enumerate(grads):
+        total = total + jnp.where(picks[k:k + 1, :1] == site, grad[...].astype(F32), 0.0)
+    return total
+
+
+def site_kernel(picks, _, *refs):
+    grads, out = refs[:-1], refs[-1]
     for site in range(out.shape[0]):
-        for grads, lo, hi in ((downs, 0, feat), (ups, feat, out.shape[2])):
-            total = jnp.zeros((out.shape[1], hi - lo), F32)
-            for s in range(n_dp):
-                use = picks[s:s + 1, :1] == site
-                total = total + jnp.where(use, grads[s][...].astype(F32), 0.0)
-            out[site, :, lo:hi] = total.astype(BF16)
-
-
-def last_kernel(feat, *refs):
-    parts, down, up = refs[:-2], refs[-2], refs[-1]
-    total = parts[0][...].astype(F32)
+        out[site] = pick_sum(grads, picks, site).astype(BF16)
+
+
+def last_kernel(n_pair, n_ups, n_mp, picks, *refs):
+    downs, ups, parts = refs[:n_pair], refs[n_pair:n_pair + n_ups], refs[n_pair + n_ups:n_pair + n_ups + n_mp]
+    down, up, y = refs[-3:]
+    total = downs[0][0].astype(F32)
+    for part in downs[1:]:
+        total = total + part[0].astype(F32)
+    down[0] = SCALE * total
+    up[0] = SCALE * pick_sum(ups, picks, pl.program_id(0))
+    total = parts[0][...]
     for part in parts[1:]:
         total = total + part[...].astype(F32)
-    total = SCALE * total
-    down[...] = total[:, :, :feat]
-    up[...] = total[:, :, feat:]
+    y[...] = total.astype(BF16)
 
 
 def shards(x, w, down, up, gy, owner, table):
@@ -267,10 +268,10 @@
     y_got = [shift(sent[s - 1], "mp", n_mp - s) for s in range(1, n_mp)]
     back, picks = call(
         functools.partial(back_kernel, n_dp, n_mp), "back",
-        [shape(tok, feat), shape(-(-n_dp // 8) * 8, 128, dtype=jnp.int32)],
+        [shape(tok, feat), shape(-(-n_dp * n_pair // 8) * 8, 128, dtype=jnp.int32)],
         [SMEM, whole(*w.shape)] + [row_block(cols)] * n_mp + [whole(feat, cols)] * n_other
         + [row_block(n_dp * rank), whole(*down.shape)] + [whole(rank, feat)] * away,
-        [row_block(feat), whole(-(-n_dp // 8) * 8, 128)],
+        [row_block(feat), whole(-(-n_dp * n_pair // 8) * 8, 128)],
         [pltpu.VMEM((feat, cols), BF16), pltpu.VMEM((n_dp * rank, feat), BF16)], grid=(TILES,),
     )(table, w, gy, *gy_got, *w_rows, h_wide, down, *downs)
     up_back, u_wide = gradient(gy, u_parts, [picks] + down_back[2:] + gy_got, "up", GRAD_COST)
@@ -279,23 +280,23 @@
         functools.partial(own_kernel, n_dp), "y_own", shape(tok, cols, dtype=F32),
         [SMEM, whole(*w.shape), row_block(feat), row_block(n_dp * rank), whole(*up.shape)]
         + [whole(rank, cols)] * away,
-        row_block(cols), [pltpu.VMEM((n_dp * rank, cols), BF16)], grid=(TILES,),
+        row_block(cols), [pltpu.VMEM((n_dp * rank, cols), BF16)], grid=(TILES,), flops=GRAD_COST,
     )(table, w, x, u_wide, up, *ups)
 
     summed = call(
-        functools.partial(site_kernel, n_dp, feat), "sites",
-        shape(sites, rank, feat + cols), [VMEM, ANY] + [VMEM] * (2 * n_dp), VMEM,
-    )(picks, y_own, *down_back, *up_back)
+        site_kernel, "sites", shape(sites, rank, feat), [VMEM, ANY] + [VMEM] * n_dp, VMEM,
+    )(picks, up_back[0], *down_back)
     both = [summed] + [shift(summed, "pair", q) for q in range(1, n_pair)]
-    down_grad, up_grad = call(
-        functools.partial(last_kernel, feat), "gradients",
-        [shape(sites, rank, feat, dtype=F32), shape(sites, rank, cols, dtype=F32)],
-        [VMEM] * n_pair, [VMEM] * 2,
-    )(*both)
-
-    y = call(
-        add_kernel, "y_add", shape(tok, cols), [row_block(cols)] * n_mp, row_block(cols), grid=(TILES,),
-    )(y_own, *y_got)
+    up_all = [shift(after(one, y_own), "pair", q) if q else one for q in range(n_pair) for one in up_back]
+    rows = tok // sites
+    of_site = lambda width: pl.BlockSpec((1, rank, width), lambda i: (i, 0, 0))
+    out_rows = pl.BlockSpec((rows, cols), lambda i: (i, 0))
+    down_grad, up_grad, y = call(
+        functools.partial(last_kernel, n_pair, n_pair * n_dp, n_mp), "last",
+        [shape(sites, rank, feat, dtype=F32), shape(sites, rank, cols, dtype=F32), shape(tok, cols)],
+        [whole(*picks.shape)] + [of_site(feat)] * n_pair + [whole(rank, cols)] * (n_pair * n_dp) + [out_rows] * n_mp,
+        [of_site(feat), of_site(cols), out_rows], grid=(sites,),
+    )(picks, *both, *up_all, y_own, *y_got)
     return y, back, down_grad.transpose(0, 2, 1), up_grad
 
 

time: 60.1 us -> 59.4 us (0.988)
  Pallas kernels: 18.7 us -> 17.6 us
  starting transfers between devices: 30.2 us -> 30.9 us
    pallas_call x3 -> x2, Pallas kernels: 2.94 us -> 1.81 us  [the longest x1 1.46 us: shards(): call(functools.partial(last_kernel, n_pair, n_pair * n_dp, n_mp), 'last',...]
    ppermute x19 -> x23, starting transfers between devices: 30.2 us -> 30.9 us  [shift(): lax.ppermute(value, axis, [(i, (i + by) % size) for i in range(size)])]
    ppermute x19 -> x23, waiting for transfers between devices: 10.2 us -> 9.87 us  [shift(): lax.ppermute(value, axis, [(i, (i + by) % size) for i in range(size)])]
  transfers between devices with their start and end apart: 19 -> 23, of which waited for: 5 -> 8; matrix products, arithmetic and copies ran while one was open for 0% -> 0% of each run, Pallas kernels for 23% -> 22%
where the time goes in v9:
time: 59.4 us; the launch traced here: 59.3 us
  starting transfers between devices  30.9 us (52%)
  Pallas kernels  17.6 us (30%)
  waiting for transfers between devices  9.87 us (17%)
  between operations  0.81 us (1%)
    ppermute x23, starting transfers between devices, shift(): lax.ppermute(value, axis, [(i, (i + by) % size) for i in range(size)])  30.9 us
    ppermute x23, waiting for transfers between devices, shift(): lax.ppermute(value, axis, [(i, (i + by) % size) for i in range(size)])  9.87 us
    pallas_call x1, Pallas kernels, shards(): call(functools.partial(back_kernel, n_dp, n_mp), 'back', [shape(tok, feat...  4.1 us
    pallas_call x1, Pallas kernels, shards(): call(functools.partial(pack_kernel, n_dp, n_mp, n_pair), 'pack', [shape(r...  3.23 us
    pallas_call x2, Pallas kernels, gradient(): call(functools.partial(grad_kernel, n_dp, n_mp, len(behind)), name + '_gr...  2.43 us
    pallas_call x2, Pallas kernels, low_rank(): call(functools.partial(reduce_kernel, n_dp), name + '_part', shape(tok //...  2.43 us
    pallas_call x1, Pallas kernels, shards(): call(functools.partial(own_kernel, n_dp), 'y_own', shape(tok, cols, dtype...  2.2 us
    pallas_call x1, Pallas kernels, shards(): call(functools.partial(last_kernel, n_pair, n_pair * n_dp, n_mp), 'last',...  1.46 us
  transfers between devices with their start and end apart: 23, of which 8 were waited for; matrix products, arithmetic and copies ran while one was open for 0% of the time, Pallas kernels for 22%

profile of v9, /device:TPU:0, one launch (start us, length us, event | category | flops | bytes accessed | tf_op | source)
XLA Modules:
  0.0 59.3 jit_solution(6031804103955788087)
XLA Ops:
  0.7 3.2 %pack.1 = (bf16[64,512]{1,0:T(8,128)(2,1)}, bf16[64,512]{1,0:T(8,128)(2,1)}, bf16[64,512]{1,0:T(8,128)(2,1)}, bf16[64,1024]{1,0:T(8,128)(2,1)}, bf16[64,1024]{1,...) custom-call(s32[1,2,4]{2,1,0:T(2,128)} %table.9, bf16[2,64,1024]{2,1,0:T(8,128)(2,1)} %bitcast.2, ...), custom_call_target="tpu_custom_call" | custom-call | flops 1 | bytes 1 | tf_op jit(solution)/shard_map/pack/pallas_call | solution.py:226
  3.9 3.0 %collective-permute-start = (bf16[512,512]{1,0:T(8,128)(2,1)}, bf16[512,512]{1,0:T(8,128)(2,1)S(1)}, u32[]{:S(2)}, u32[]{:S(2)}) collective-permute-start(bf16[512,512]{1,0:T(8,128)(2,1)} %get-tuple-element.37), channel_id=1, source_target_pairs={{0,2},{2,0},{1,3},{3,1},{4,6},{6,4},{5,7},{7,5},{8,10},{10,8},{9,1... | collective-permute-start | bytes 1572872 | tf_op jit(solution)/shard_map/ppermute | solution.py:35
  6.9 2.6 %collective-permute-start.2 = (bf16[64,512]{1,0:T(8,128)(2,1)}, bf16[64,512]{1,0:T(8,128)(2,1)S(1)}, u32[]{:S(2)}, u32[]{:S(2)}) collective-permute-start(bf16[64,512]{1,0:T(8,128)(2,1)} %get-tuple-element.40), channel_id=1, source_target_pairs={{0,8},{4,12},{8,0},{12,4},{1,9},{5,13},{9,1},{13,5},{2,10},{6,14},... | collective-permute-start | bytes 196616 | tf_op jit(solution)/shard_map/ppermute | solution.py:35
  9.5 1.6 %collective-permute-start.6 = (bf16[64,512]{1,0:T(8,128)(2,1)}, bf16[64,512]{1,0:T(8,128)(2,1)S(1)}, u32[]{:S(2)}, u32[]{:S(2)}) collective-permute-start(bf16[64,512]{1,0:T(8,128)(2,1)} %get-tuple-element.46), channel_id=1, source_target_pairs={{0,4},{4,8},{8,12},{12,0},{1,5},{5,9},{9,13},{13,1},{2,6},{6,10},{... | collective-permute-start | bytes 196616 | tf_op jit(solution)/shard_map/ppermute | solution.py:35
  11.1 2.2 %collective-permute-start.7 = (bf16[64,512]{1,0:T(8,128)(2,1)}, bf16[64,512]{1,0:T(8,128)(2,1)S(1)}, u32[]{:S(2)}, u32[]{:S(2)}) collective-permute-start(bf16[64,512]{1,0:T(8,128)(2,1)} %get-tuple-element.47), channel_id=1, source_target_pairs={{0,12},{4,0},{8,4},{12,8},{1,13},{5,1},{9,5},{13,9},{2,14},{6,2},{... | collective-permute-start | bytes 196616 | tf_op jit(solution)/shard_map/ppermute | solution.py:35
  13.3 1.2 %collective-permute-start.3 = (bf16[64,1024]{1,0:T(8,128)(2,1)}, bf16[64,1024]{1,0:T(8,128)(2,1)S(1)}, u32[]{:S(2)}, u32[]{:S(2)}) collective-permute-start(bf16[64,1024]{1,0:T(8,128)(2,1)} %get-tuple-element.41), channel_id=1, source_target_pairs={{0,4},{4,8},{8,12},{12,0},{1,5},{5,9},{9,13},{13,1},{2,6},{6,10},{... | collective-permute-start | bytes 393224 | tf_op jit(solution)/shard_map/ppermute | solution.py:35
  14.6 3.7 %collective-permute-start.4 = (bf16[64,1024]{1,0:T(8,128)(2,1)}, bf16[64,1024]{1,0:T(8,128)(2,1)S(1)}, u32[]{:S(2)}, u32[]{:S(2)}) collective-permute-start(bf16[64,1024]{1,0:T(8,128)(2,1)} %get-tuple-element.43), channel_id=1, source_target_pairs={{0,8},{4,12},{8,0},{12,4},{1,9},{5,13},{9,1},{13,5},{2,10},{6,14},... | collective-permute-start | bytes 393224 | tf_op jit(solution)/shard_map/ppermute | solution.py:35
  18.5 1.1 %h_part.1.refs_3_ = bf16[384,128]{1,0:T(8,128)(2,1)S(1)} custom-call(s32[12]{0:T(128)S(1)} %copy-done.6, s32[1,2,4]{2,1,0:T(2,128)S(1)} %copy-done.5, bf16[768,512]{1,0:T(8,128)(2,1)S(1)} %copy-done.2, bf16[64,512]{1,0:T(8,128)(2,1)S(1)} %collective-permute-done.6._.refs_0_, bf16[2,64,512]{2,1,0:T(8,128)(2,1)S(1)} %copy-done.4, ...), custom_call_target="tpu_custom_call" | custom-call | flops 1 | bytes 1 | tf_op jit(solution)/shard_map/h_part/pallas_call | solution.py:237
  19.7 0.6 %collective-permute-start.8 = (bf16[384,128]{1,0:T(8,128)(2,1)S(1)}, bf16[384,128]{1,0:T(8,128)(2,1)S(1)}, u32[]{:S(2)}, u32[]{:S(2)}) collective-permute-start(bf16[384,128]{1,0:T(8,128)(2,1)S(1)} %h_part.1.refs_3_), channel_id=1, source_target_pairs={{0,2},{2,0},{1,3},{3,1},{4,6},{6,4},{5,7},{7,5},{8,10},{10,8},{9,1... | collective-permute-start | bytes 294920 | tf_op jit(solution)/shard_map/ppermute | solution.py:35
  20.3 1.5 %collective-permute-start.1 = (bf16[768,512]{1,0:T(8,128)(2,1)S(1)}, bf16[768,512]{1,0:T(8,128)(2,1)S(1)}, u32[]{:S(2)}, u32[]{:S(2)}) collective-permute-start(bf16[768,512]{1,0:T(8,128)(2,1)S(1)} %copy-done.2), channel_id=1, source_target_pairs={{0,2},{2,0},{1,3},{3,1},{4,6},{6,4},{5,7},{7,5},{8,10},{10,8},{9,1... | collective-permute-start | bytes 2359304 | tf_op jit(solution)/shard_map/ppermute | solution.py:35
  21.8 3.7 %collective-permute-done.8.refs_4_ = bf16[384,128]{1,0:T(8,128)(2,1)S(1)} collective-permute-done((bf16[384,128]{1,0:T(8,128)(2,1)S(1)}, bf16[384,128]{1,0:T(8,128)(2,1)S(1)}, u32[]{:S(2)}, u32[]{:S(2)}) %collective-permute-start.8) | collective-permute-done | bytes 98336 | tf_op jit(solution)/shard_map/ppermute | solution.py:35
  25.5 1.3 %down_grad.1 = (bf16[64,1024]{1,0:T(8,128)(2,1)S(1)}, bf16[64,1024]{1,0:T(8,128)(2,1)S(1)}, bf16[64,1024]{1,0:T(8,128)(2,1)S(1)}, bf16[64,1024]{1,0:T(8,128)(2,1)S(1)}, bf16[768,256]{1,0:T(8,128)(2,1)S(1)}) custom-call(s32[12]{0:T(128)S(1)} %copy-done.6, bf16[768,1024]{1,0:T(8,128)(2,1)S(1)} %copy-done.1, ...), custom_call_target="tpu_custom_call" | custom-call | flops 15000000512 | bytes 1 | tf_op jit(solution)/shard_map/down_grad/pallas_call | solution.py:245
  26.9 5.1 %collective-permute-start.9 = (bf16[64,1024]{1,0:T(8,128)(2,1)S(1)}, bf16[64,1024]{1,0:T(8,128)(2,1)S(1)}, u32[]{:S(2)}, u32[]{:S(2)}) collective-permute-start(bf16[64,1024]{1,0:T(8,128)(2,1)S(1)} %get-tuple-element.49), channel_id=1, source_target_pairs={{0,12},{4,0},{8,4},{12,8},{1,13},{5,1},{9,5},{13,9},{2,14},{6,2},{... | collective-permute-start | bytes 393224 | tf_op jit(solution)/shard_map/ppermute | solution.py:35
  32.0 0.7 %collective-permute-start.12 = (bf16[64,1024]{1,0:T(8,128)(2,1)S(1)}, bf16[64,1024]{1,0:T(8,128)(2,1)S(1)}, u32[]{:S(2)}, u32[]{:S(2)}) collective-permute-start(bf16[64,1024]{1,0:T(8,128)(2,1)S(1)} %get-tuple-element.54), channel_id=1, source_target_pairs={{0,4},{4,8},{8,12},{12,0},{1,5},{5,9},{9,13},{13,1},{2,6},{6,10},{... | collective-permute-start | bytes 393224 | tf_op jit(solution)/shard_map/ppermute | solution.py:35
  32.7 1.3 %u_part.1._.refs_4_ = bf16[384,128]{1,0:T(8,128)(2,1)S(1)} custom-call(s32[12]{0:T(128)S(1)} %copy-done.6, s32[1,2,4]{2,1,0:T(2,128)S(1)} %copy-done.5, bf16[768,1024]{1,0:T(8,128)(2,1)S(1)} %copy-done.1, bf16[768,256]{1,0:T(8,128)(2,1)S(1)} %get-tuple-element.48._.refs_4_, bf16[2,64,1024]{2,1,0:T(8,128)(2,1)S(1)} %bitcast.3, ...), custom_call_target="tpu_custom_call" | custom-call | flops 1 | bytes 1 | tf_op jit(solution)/shard_map/u_part/pallas_call | solution.py:237
  34.0 1.9 %collective-permute-done.9.__.refs_1_ = bf16[64,1024]{1,0:T(8,128)(2,1)S(1)} collective-permute-done((bf16[64,1024]{1,0:T(8,128)(2,1)S(1)}, bf16[64,1024]{1,0:T(8,128)(2,1)S(1)}, u32[]{:S(2)}, u32[]{:S(2)}) %collective-permute-start.9) | collective-permute-done | bytes 131104 | tf_op jit(solution)/shard_map/ppermute | solution.py:35
  35.9 0.5 collective-permute-start.13
  36.4 1.4 %y_send.1 = (bf16[768,512]{1,0:T(8,128)(2,1)S(1)}, bf16[1024,512]{1,0:T(8,128)(2,1)S(1)}) custom-call(bf16[384,128]{1,0:T(8,128)(2,1)S(1)} %u_part.1._.refs_4_, bf16[64,1024]{1,0:T(8,128)(2,1)S(1)} %collective-permute-done.9.__.refs_1_, bf16[768,1024]{1,0:T(8,128)(2,1)S(1)} %copy-done.1, bf16[512,512]{1,0:T(8,128)(2,1)S(1)} %collective-permute-done.refs_0_, ...), custom_call_target="tpu_custom_call" | custom-call | flops 1 | bytes 1 | tf_op jit(solution)/shard_map/y_send/pallas_call | solution.py:260
  37.9 1.6 %collective-permute-start.22 = (bf16[768,512]{1,0:T(8,128)(2,1)S(1)}, bf16[768,512]{1,0:T(8,128)(2,1)S(1)}, u32[]{:S(2)}, u32[]{:S(2)}) collective-permute-start(bf16[768,512]{1,0:T(8,128)(2,1)S(1)} %get-tuple-element.65), channel_id=1, source_target_pairs={{0,2},{2,0},{1,3},{3,1},{4,6},{6,4},{5,7},{7,5},{8,10},{10,8},{9,1... | collective-permute-start | bytes 2359304 | tf_op jit(solution)/shard_map/ppermute | solution.py:35
  39.4 0.5 collective-permute-done.1.refs_2_.refs_3_
  39.9 4.1 %back.1 = (bf16[768,1024]{1,0:T(8,128)(2,1)}, s32[8,128]{1,0:T(8,128)S(1)}) custom-call(s32[1,2,4]{2,1,0:T(2,128)S(1)} %copy-done.5, bf16[2048,512]{1,0:T(8,128)(2,1)S(1)} %copy-done, bf16[768,512]{1,0:T(8,128)(2,1)S(1)} %copy-done.2, bf16[768,512]{1,0:T(8,128)(2,1)S(1)} %collective-permute-done.1.refs_2_.refs_3_, ...), custom_call_target="tpu_custom_call" | custom-call | flops 1 | bytes 1 | tf_op jit(solution)/shard_map/back/pallas_call | solution.py:269
  44.1 1.1 %up_grad.1 = (bf16[64,512]{1,0:T(8,128)(2,1)S(1)}, bf16[64,512]{1,0:T(8,128)(2,1)S(1)}, bf16[64,512]{1,0:T(8,128)(2,1)S(1)}, bf16[64,512]{1,0:T(8,128)(2,1)S(1)}, bf16[768,256]{1,0:T(8,128)(2,1)S(1)}) custom-call(s32[12]{0:T(128)S(1)} %copy-done.6, bf16[768,512]{1,0:T(8,128)(2,1)S(1)} %copy-done.2, s32[8,128]{1,0:T(8,128)S(1)} %get-tuple-element.52.refs_0_.picks, ...), custom_call_target="tpu_custom_call" | custom-call | flops 15000000512 | bytes 1 | tf_op jit(solution)/shard_map/up_grad/pallas_call | solution.py:245
  45.2 3.9 %collective-permute-start.15 = (bf16[64,512]{1,0:T(8,128)(2,1)S(1)}, bf16[64,512]{1,0:T(8,128)(2,1)S(1)}, u32[]{:S(2)}, u32[]{:S(2)}) collective-permute-start(bf16[64,512]{1,0:T(8,128)(2,1)S(1)} %get-tuple-element.57), channel_id=1, source_target_pairs={{0,12},{4,0},{8,4},{12,8},{1,13},{5,1},{9,5},{13,9},{2,14},{6,2},{... | collective-permute-start | bytes 196616 | tf_op jit(solution)/shard_map/ppermute | solution.py:35
  49.0 1.7 %collective-permute-start.17 = (bf16[64,512]{1,0:T(8,128)(2,1)S(1)}, bf16[64,512]{1,0:T(8,128)(2,1)S(1)}, u32[]{:S(2)}, u32[]{:S(2)}) collective-permute-start(bf16[64,512]{1,0:T(8,128)(2,1)S(1)} %get-tuple-element.59), channel_id=1, source_target_pairs={{0,4},{4,8},{8,12},{12,0},{1,5},{5,9},{9,13},{13,1},{2,6},{6,10},{... | collective-permute-start | bytes 196616 | tf_op jit(solution)/shard_map/ppermute | solution.py:35
  50.7 0.3 sites.1.refs_0_
  51.2 2.2 %y_own.1.refs_10_ = f32[768,512]{1,0:T(8,128)S(1)} custom-call(s32[1,2,4]{2,1,0:T(2,128)S(1)} %copy-done.5, bf16[2048,512]{1,0:T(8,128)(2,1)S(1)} %copy-done, bf16[768,1024]{1,0:T(8,128)(2,1)S(1)} %copy-done.1, bf16[768,256]{1,0:T(8,128)(2,1)S(1)} %get-tuple-element.60.wide, bf16[2,64,512]{2,1,0:T(8,128)(2,1)S(1)} %copy-done.4, ...), custom_call_target="tpu_custom_call" | custom-call | flops 15000000512 | bytes 1 | tf_op jit(solution)/shard_map/y_own/pallas_call | solution.py:279
  53.4 1.8 %collective-permute-done.17.refs_5_ = bf16[64,512]{1,0:T(8,128)(2,1)S(1)} collective-permute-done((bf16[64,512]{1,0:T(8,128)(2,1)S(1)}, bf16[64,512]{1,0:T(8,128)(2,1)S(1)}, u32[]{:S(2)}, u32[]{:S(2)}) %collective-permute-start.17) | collective-permute-done | bytes 65568 | tf_op jit(solution)/shard_map/ppermute | solution.py:35
  55.2 0.5 collective-permute-start.19
  55.8 0.7 %collective-permute-done.18.refs_6_ = bf16[64,512]{1,0:T(8,128)(2,1)S(1)} collective-permute-done((bf16[64,512]{1,0:T(8,128)(2,1)S(1)}, bf16[64,512]{1,0:T(8,128)(2,1)S(1)}, u32[]{:S(2)}, u32[]{:S(2)}) %collective-permute-start.18) | collective-permute-done | bytes 65568 | tf_op jit(solution)/shard_map/ppermute | solution.py:35
  56.6 0.4 collective-permute-done.20.refs_8_
  57.0 0.7 %collective-permute-done.21.refs_9_ = bf16[64,512]{1,0:T(8,128)(2,1)S(1)} collective-permute-done((bf16[64,512]{1,0:T(8,128)(2,1)S(1)}, bf16[64,512]{1,0:T(8,128)(2,1)S(1)}, u32[]{:S(2)}, u32[]{:S(2)}) %collective-permute-start.21) | collective-permute-done | bytes 65568 | tf_op jit(solution)/shard_map/ppermute | solution.py:35
  57.8 1.5 %last.1 = (f32[2,64,1024]{2,1,0:T(8,128)}, f32[2,64,512]{2,1,0:T(8,128)}, bf16[768,512]{1,0:T(8,128)(2,1)}) custom-call(s32[8,128]{1,0:T(8,128)S(1)} %get-tuple-element.52.refs_0_.picks, bf16[2,64,1024]{2,1,0:T(8,128)(2,1)S(1)} %sites.1.refs_0_, bf16[2,64,1024]{2,1,0:T(8,128)(2,1)S(1)} %collective-permute-done.14.refs_1_, ...), custom_call_target="tpu_custom_call" | custom-call | flops 1 | bytes 1 | tf_op jit(solution)/shard_map/last/pallas_call | solution.py:294
  (38 shorter events, 0.8 us)
Async XLA Ops:
  0.6 17.9 %copy-start.5 = (s32[1,2,4]{2,1,0:T(2,128)S(1)}, s32[1,2,4]{2,1,0:T(2,128)}, u32[]{:S(2)}) copy-start(s32[1,2,4]{2,1,0:T(2,128)} %table.9) | copy-start | bytes 100
  0.6 17.9 %copy-start.4 = (bf16[2,64,512]{2,1,0:T(8,128)(2,1)S(1)}, bf16[2,64,512]{2,1,0:T(8,128)(2,1)}, u32[]{:S(2)}) copy-start(bf16[2,64,512]{2,1,0:T(8,128)(2,1)} %own_up.1) | copy-start | bytes 393220
  0.7 17.9 %copy-start.6 = (s32[12]{0:T(128)S(1)}, s32[12]{0:T(128)}, u32[]{:S(2)}) copy-start(s32[12]{0:T(128)} %owner.7) | copy-start | bytes 148
  0.7 17.9 %copy-start.2 = (bf16[768,512]{1,0:T(8,128)(2,1)S(1)}, bf16[768,512]{1,0:T(8,128)(2,1)}, u32[]{:S(2)}) copy-start(bf16[768,512]{1,0:T(8,128)(2,1)} %act.7) | copy-start | bytes 2359300
  0.7 24.8 %copy-start.1 = (bf16[768,1024]{1,0:T(8,128)(2,1)S(1)}, bf16[768,1024]{1,0:T(8,128)(2,1)}, u32[]{:S(2)}) copy-start(bf16[768,1024]{1,0:T(8,128)(2,1)} %x.3) | copy-start | bytes 4718596
  3.9 16.3 %collective-permute-start = (bf16[512,512]{1,0:T(8,128)(2,1)}, bf16[512,512]{1,0:T(8,128)(2,1)S(1)}, u32[]{:S(2)}, u32[]{:S(2)}) collective-permute-start(bf16[512,512]{1,0:T(8,128)(2,1)} %get-tuple-element.37), channel_id=1, source_target_pairs={{0,2},{2,0},{1,3},{3,1},{4,6},{6,4},{5,7},{7,5},{8,10},{10,8},{9,1... | collective-permute-start | bytes 1572872 | tf_op jit(solution)/shard_map/ppermute | solution.py:35
  6.9 6.4 %collective-permute-start.2 = (bf16[64,512]{1,0:T(8,128)(2,1)}, bf16[64,512]{1,0:T(8,128)(2,1)S(1)}, u32[]{:S(2)}, u32[]{:S(2)}) collective-permute-start(bf16[64,512]{1,0:T(8,128)(2,1)} %get-tuple-element.40), channel_id=1, source_target_pairs={{0,8},{4,12},{8,0},{12,4},{1,9},{5,13},{9,1},{13,5},{2,10},{6,14},... | collective-permute-start | bytes 196616 | tf_op jit(solution)/shard_map/ppermute | solution.py:35
  9.5 8.7 %collective-permute-start.6 = (bf16[64,512]{1,0:T(8,128)(2,1)}, bf16[64,512]{1,0:T(8,128)(2,1)S(1)}, u32[]{:S(2)}, u32[]{:S(2)}) collective-permute-start(bf16[64,512]{1,0:T(8,128)(2,1)} %get-tuple-element.46), channel_id=1, source_target_pairs={{0,4},{4,8},{8,12},{12,0},{1,5},{5,9},{9,13},{13,1},{2,6},{6,10},{... | collective-permute-start | bytes 196616 | tf_op jit(solution)/shard_map/ppermute | solution.py:35
  11.1 7.4 %collective-permute-start.7 = (bf16[64,512]{1,0:T(8,128)(2,1)}, bf16[64,512]{1,0:T(8,128)(2,1)S(1)}, u32[]{:S(2)}, u32[]{:S(2)}) collective-permute-start(bf16[64,512]{1,0:T(8,128)(2,1)} %get-tuple-element.47), channel_id=1, source_target_pairs={{0,12},{4,0},{8,4},{12,8},{1,13},{5,1},{9,5},{13,9},{2,14},{6,2},{... | collective-permute-start | bytes 196616 | tf_op jit(solution)/shard_map/ppermute | solution.py:35
  13.3 12.1 %collective-permute-start.3 = (bf16[64,1024]{1,0:T(8,128)(2,1)}, bf16[64,1024]{1,0:T(8,128)(2,1)S(1)}, u32[]{:S(2)}, u32[]{:S(2)}) collective-permute-start(bf16[64,1024]{1,0:T(8,128)(2,1)} %get-tuple-element.41), channel_id=1, source_target_pairs={{0,4},{4,8},{8,12},{12,0},{1,5},{5,9},{9,13},{13,1},{2,6},{6,10},{... | collective-permute-start | bytes 393224 | tf_op jit(solution)/shard_map/ppermute | solution.py:35
  14.6 10.9 %collective-permute-start.4 = (bf16[64,1024]{1,0:T(8,128)(2,1)}, bf16[64,1024]{1,0:T(8,128)(2,1)S(1)}, u32[]{:S(2)}, u32[]{:S(2)}) collective-permute-start(bf16[64,1024]{1,0:T(8,128)(2,1)} %get-tuple-element.43), channel_id=1, source_target_pairs={{0,8},{4,12},{8,0},{12,4},{1,9},{5,13},{9,1},{13,5},{2,10},{6,14},... | collective-permute-start | bytes 393224 | tf_op jit(solution)/shard_map/ppermute | solution.py:35
  18.2 7.2 %collective-permute-start.5 = (bf16[64,1024]{1,0:T(8,128)(2,1)}, bf16[64,1024]{1,0:T(8,128)(2,1)S(1)}, u32[]{:S(2)}, u32[]{:S(2)}) collective-permute-start(bf16[64,1024]{1,0:T(8,128)(2,1)} %get-tuple-element.45), channel_id=1, source_target_pairs={{0,12},{4,0},{8,4},{12,8},{1,13},{5,1},{9,5},{13,9},{2,14},{6,2},{... | collective-permute-start | bytes 393224 | tf_op jit(solution)/shard_map/ppermute | solution.py:35
  19.6 13.0 %copy-start.3 = (bf16[2,1024,64]{1,2,0:T(8,128)(2,1)S(1)}, bf16[2,1024,64]{1,2,0:T(8,128)(2,1)}, u32[]{:S(2)}) copy-start(bf16[2,1024,64]{1,2,0:T(8,128)(2,1)} %param.9) | copy-start | bytes 786436
  19.7 5.8 %collective-permute-start.8 = (bf16[384,128]{1,0:T(8,128)(2,1)S(1)}, bf16[384,128]{1,0:T(8,128)(2,1)S(1)}, u32[]{:S(2)}, u32[]{:S(2)}) collective-permute-start(bf16[384,128]{1,0:T(8,128)(2,1)S(1)} %h_part.1.refs_3_), channel_id=1, source_target_pairs={{0,2},{2,0},{1,3},{3,1},{4,6},{6,4},{5,7},{7,5},{8,10},{10,8},{9,1... | collective-permute-start | bytes 294920 | tf_op jit(solution)/shard_map/ppermute | solution.py:35
  20.3 19.7 %collective-permute-start.1 = (bf16[768,512]{1,0:T(8,128)(2,1)S(1)}, bf16[768,512]{1,0:T(8,128)(2,1)S(1)}, u32[]{:S(2)}, u32[]{:S(2)}) collective-permute-start(bf16[768,512]{1,0:T(8,128)(2,1)S(1)} %copy-done.2), channel_id=1, source_target_pairs={{0,2},{2,0},{1,3},{3,1},{4,6},{6,4},{5,7},{7,5},{8,10},{10,8},{9,1... | collective-permute-start | bytes 2359304 | tf_op jit(solution)/shard_map/ppermute | solution.py:35
  26.8 9.6 %collective-permute-start.10 = (bf16[512,512]{1,0:T(8,128)(2,1)S(1)}, bf16[512,512]{1,0:T(8,128)(2,1)S(1)}, u32[]{:S(2)}, u32[]{:S(2)}) collective-permute-start(bf16[512,512]{1,0:T(8,128)(2,1)S(1)} %collective-permute-done.refs_0_), channel_id=1, source_target_pairs={{0,1},{1,0},{2,3},{3,2},{4,5},{5,4},{6,7},{7,6},{8,9},{9,8},{10,11... | collective-permute-start | bytes 1572872 | tf_op jit(solution)/shard_map/ppermute | solution.py:35
  26.9 9.0 %collective-permute-start.9 = (bf16[64,1024]{1,0:T(8,128)(2,1)S(1)}, bf16[64,1024]{1,0:T(8,128)(2,1)S(1)}, u32[]{:S(2)}, u32[]{:S(2)}) collective-permute-start(bf16[64,1024]{1,0:T(8,128)(2,1)S(1)} %get-tuple-element.49), channel_id=1, source_target_pairs={{0,12},{4,0},{8,4},{12,8},{1,13},{5,1},{9,5},{13,9},{2,14},{6,2},{... | collective-permute-start | bytes 393224 | tf_op jit(solution)/shard_map/ppermute | solution.py:35
  32.0 12.1 %collective-permute-start.11 = (bf16[64,1024]{1,0:T(8,128)(2,1)S(1)}, bf16[64,1024]{1,0:T(8,128)(2,1)S(1)}, u32[]{:S(2)}, u32[]{:S(2)}) collective-permute-start(bf16[64,1024]{1,0:T(8,128)(2,1)S(1)} %get-tuple-element.53), channel_id=1, source_target_pairs={{0,8},{4,12},{8,0},{12,4},{1,9},{5,13},{9,1},{13,5},{2,10},{6,14},... | collective-permute-start | bytes 393224 | tf_op jit(solution)/shard_map/ppermute | solution.py:35
  32.0 12.1 %collective-permute-start.12 = (bf16[64,1024]{1,0:T(8,128)(2,1)S(1)}, bf16[64,1024]{1,0:T(8,128)(2,1)S(1)}, u32[]{:S(2)}, u32[]{:S(2)}) collective-permute-start(bf16[64,1024]{1,0:T(8,128)(2,1)S(1)} %get-tuple-element.54), channel_id=1, source_target_pairs={{0,4},{4,8},{8,12},{12,0},{1,5},{5,9},{9,13},{13,1},{2,6},{6,10},{... | collective-permute-start | bytes 393224 | tf_op jit(solution)/shard_map/ppermute | solution.py:35
  34.0 6.0 %copy-start = (bf16[2048,512]{1,0:T(8,128)(2,1)S(1)}, bf16[2048,512]{1,0:T(8,128)(2,1)}, u32[]{:S(2)}) copy-start(bf16[2048,512]{1,0:T(8,128)(2,1)} %w.3) | copy-start | bytes 6291460
  35.9 8.1 %collective-permute-start.13 = (bf16[384,128]{1,0:T(8,128)(2,1)S(1)}, bf16[384,128]{1,0:T(8,128)(2,1)S(1)}, u32[]{:S(2)}, u32[]{:S(2)}) collective-permute-start(bf16[384,128]{1,0:T(8,128)(2,1)S(1)} %u_part.1._.refs_4_), channel_id=1, source_target_pairs={{0,2},{2,0},{1,3},{3,1},{4,6},{6,4},{5,7},{7,5},{8,10},{10,8},{9,1... | collective-permute-start | bytes 294920 | tf_op jit(solution)/shard_map/ppermute | solution.py:35
  37.9 19.9 %collective-permute-start.22 = (bf16[768,512]{1,0:T(8,128)(2,1)S(1)}, bf16[768,512]{1,0:T(8,128)(2,1)S(1)}, u32[]{:S(2)}, u32[]{:S(2)}) collective-permute-start(bf16[768,512]{1,0:T(8,128)(2,1)S(1)} %get-tuple-element.65), channel_id=1, source_target_pairs={{0,2},{2,0},{1,3},{3,1},{4,6},{6,4},{5,7},{7,5},{8,10},{10,8},{9,1... | collective-permute-start | bytes 2359304 | tf_op jit(solution)/shard_map/ppermute | solution.py:35
  45.2 10.0 %collective-permute-start.15 = (bf16[64,512]{1,0:T(8,128)(2,1)S(1)}, bf16[64,512]{1,0:T(8,128)(2,1)S(1)}, u32[]{:S(2)}, u32[]{:S(2)}) collective-permute-start(bf16[64,512]{1,0:T(8,128)(2,1)S(1)} %get-tuple-element.57), channel_id=1, source_target_pairs={{0,12},{4,0},{8,4},{12,8},{1,13},{5,1},{9,5},{13,9},{2,14},{6,2},{... | collective-permute-start | bytes 196616 | tf_op jit(solution)/shard_map/ppermute | solution.py:35
  49.0 6.2 %collective-permute-start.16 = (bf16[64,512]{1,0:T(8,128)(2,1)S(1)}, bf16[64,512]{1,0:T(8,128)(2,1)S(1)}, u32[]{:S(2)}, u32[]{:S(2)}) collective-permute-start(bf16[64,512]{1,0:T(8,128)(2,1)S(1)} %get-tuple-element.58), channel_id=1, source_target_pairs={{0,8},{4,12},{8,0},{12,4},{1,9},{5,13},{9,1},{13,5},{2,10},{6,14},... | collective-permute-start | bytes 196616 | tf_op jit(solution)/shard_map/ppermute | solution.py:35
  49.0 6.2 %collective-permute-start.17 = (bf16[64,512]{1,0:T(8,128)(2,1)S(1)}, bf16[64,512]{1,0:T(8,128)(2,1)S(1)}, u32[]{:S(2)}, u32[]{:S(2)}) collective-permute-start(bf16[64,512]{1,0:T(8,128)(2,1)S(1)} %get-tuple-element.59), channel_id=1, source_target_pairs={{0,4},{4,8},{8,12},{12,0},{1,5},{5,9},{9,13},{13,1},{2,6},{6,10},{... | collective-permute-start | bytes 196616 | tf_op jit(solution)/shard_map/ppermute | solution.py:35
  51.1 6.6 %collective-permute-start.14 = (bf16[2,64,1024]{2,1,0:T(8,128)(2,1)S(1)}, bf16[2,64,1024]{2,1,0:T(8,128)(2,1)S(1)}, u32[]{:S(2)}, u32[]{:S(2)}) collective-permute-start(bf16[2,64,1024]{2,1,0:T(8,128)(2,1)S(1)} %sites.1.refs_0_), channel_id=1, source_target_pairs={{0,1},{1,0},{2,3},{3,2},{4,5},{5,4},{6,7},{7,6},{8,9},{9,8},{10,11... | collective-permute-start | bytes 786440 | tf_op jit(solution)/shard_map/ppermute | solution.py:35
  55.2 1.3 %collective-permute-start.18 = (bf16[64,512]{1,0:T(8,128)(2,1)S(1)}, bf16[64,512]{1,0:T(8,128)(2,1)S(1)}, u32[]{:S(2)}, u32[]{:S(2)}) collective-permute-start(bf16[64,512]{1,0:T(8,128)(2,1)S(1)} %get-tuple-element.61._.refs_2_), channel_id=1, source_target_pairs={{0,1},{1,0},{2,3},{3,2},{4,5},{5,4},{6,7},{7,6},{8,9},{9,8},{10,11... | collective-permute-start | bytes 196616 | tf_op jit(solution)/shard_map/ppermute | solution.py:35
  55.2 1.4 %collective-permute-start.19 = (bf16[64,512]{1,0:T(8,128)(2,1)S(1)}, bf16[64,512]{1,0:T(8,128)(2,1)S(1)}, u32[]{:S(2)}, u32[]{:S(2)}) collective-permute-start(bf16[64,512]{1,0:T(8,128)(2,1)S(1)} %collective-permute-done.15.refs_3_), channel_id=1, source_target_pairs={{0,1},{1,0},{2,3},{3,2},{4,5},{5,4},{6,7},{7,6},{8,9},{9,8},{10,11... | collective-permute-start | bytes 196616 | tf_op jit(solution)/shard_map/ppermute | solution.py:35
  55.7 1.3 %collective-permute-start.20 = (bf16[64,512]{1,0:T(8,128)(2,1)S(1)}, bf16[64,512]{1,0:T(8,128)(2,1)S(1)}, u32[]{:S(2)}, u32[]{:S(2)}) collective-permute-start(bf16[64,512]{1,0:T(8,128)(2,1)S(1)} %collective-permute-done.16.refs_4_), channel_id=1, source_target_pairs={{0,1},{1,0},{2,3},{3,2},{4,5},{5,4},{6,7},{7,6},{8,9},{9,8},{10,11... | collective-permute-start | bytes 196616 | tf_op jit(solution)/shard_map/ppermute | solution.py:35
  56.5 1.3 %collective-permute-start.21 = (bf16[64,512]{1,0:T(8,128)(2,1)S(1)}, bf16[64,512]{1,0:T(8,128)(2,1)S(1)}, u32[]{:S(2)}, u32[]{:S(2)}) collective-permute-start(bf16[64,512]{1,0:T(8,128)(2,1)S(1)} %collective-permute-done.17.refs_5_), channel_id=1, source_target_pairs={{0,1},{1,0},{2,3},{3,2},{4,5},{5,4},{6,7},{7,6},{8,9},{9,8},{10,11... | collective-permute-start | bytes 196616 | tf_op jit(solution)/shard_map/ppermute | solution.py:35

commit v10 on v9

--- a/solution.py
+++ b/solution.py
@@ -35,6 +35,10 @@
     return lax.ppermute(value, axis, [(i, (i + by) % size) for i in range(size)])
 
 
+def swap(value, axis, mask):
+    return lax.ppermute(value, axis, [(i, i ^ mask) for i in range(lax.axis_size(axis))])
+
+
 def after(value, *others):
     return lax.optimization_barrier((value, *others))[0]
 
@@ -61,11 +65,11 @@
 def wanted_site(table, n_dp, s, q=0):
     n_pair = lax.axis_size("pair")
     core = lax.rem(lax.axis_index("pair") + n_pair - q, n_pair)
-    return table[0, core, lax.rem(lax.axis_index("dp") + s, n_dp)]
+    return table[0, core, lax.bitwise_xor(lax.axis_index("dp"), s)]
 
 
 def slot_of(owner, b, n_dp):
-    return lax.rem(lax.axis_index("dp") - owner[b] + n_dp, n_dp)
+    return lax.bitwise_xor(lax.axis_index("dp"), owner[b])
 
 
 def pack_kernel(n_dp, n_mp, n_pair, table, down, up, w, *refs):
@@ -230,8 +234,8 @@
         [pltpu.SemaphoreType.DMA((2 * away + n_other,))], mib=60,
     )(table, down, up, w)
     pieces = [shift(packed[2 * away + s - 1], "mp", s) for s in range(1, n_mp)]
-    ups = [shift(packed[s - 1], "dp", s) for s in range(1, n_dp)]
-    downs = [shift(after(packed[away + s - 1], ups[1 % away]), "dp", s) for s in range(1, n_dp)]
+    ups = [swap(packed[s - 1], "dp", s) for s in range(1, n_dp)]
+    downs = [swap(after(packed[away + s - 1], ups[1 % away]), "dp", s) for s in range(1, n_dp)]
 
     def low_rank(act, own, maps, behind, name):
         mine = call(
@@ -247,7 +251,7 @@
             [shape(rank, act.shape[1])] * n_dp + [shape(tok, n_dp * rank)],
             [SMEM, VMEM] + [ANY] * len(behind) + [VMEM] * n_mp, [VMEM] * (n_dp + 1), flops=flops,
         )(owner, act, *behind, *parts)
-        return [grads[0]] + [shift(grads[s], "dp", n_dp - s) for s in range(1, n_dp)], wide
+        return [grads[0]] + [swap(grads[s], "dp", s) for s in range(1, n_dp)], wide
 
     h_parts = low_rank(gy, up, ups, ups[0], "h")
     gy_got = [shift(after(gy, *pieces), "mp", s) for s in range(1, n_mp)]

time: 59.4 us -> 61.8 us (1.040)
  waiting for transfers between devices: 9.87 us -> 14 us
  starting transfers between devices: 30.9 us -> 29.1 us
    ppermute x23 -> x11, starting transfers between devices: 30.9 us -> 8.19 us  [shift(): lax.ppermute(value, axis, [(i, (i + by) % size) for i in range(size)])]
    ppermute x0 -> x12, starting transfers between devices: none -> 20.9 us  [swap(): lax.ppermute(value, axis, [(i, i ^ mask) for i in range(lax.axis_size(axi...]
    ppermute x0 -> x12, waiting for transfers between devices: none -> 8.68 us  [swap(): lax.ppermute(value, axis, [(i, i ^ mask) for i in range(lax.axis_size(axi...]
    ppermute x23 -> x11, waiting for transfers between devices: 9.87 us -> 5.36 us  [shift(): lax.ppermute(value, axis, [(i, (i + by) % size) for i in range(size)])]
  transfers between devices with their start and end apart: 23 -> 23, of which waited for: 8 -> 8; matrix products, arithmetic and copies ran while one was open for 0% -> 0% of each run, Pallas kernels for 22% -> 21%
where the time goes in v10:
time: 61.8 us; the launch traced here: 61.6 us
  starting transfers between devices  29.1 us (47%)
  Pallas kernels  17.6 us (28%)
  waiting for transfers between devices  14 us (23%)
  between operations  0.82 us (1%)
    ppermute x12, starting transfers between devices, swap(): lax.ppermute(value, axis, [(i, i ^ mask) for i in range(lax.axis_size(axi...  20.9 us
    ppermute x12, waiting for transfers between devices, swap(): lax.ppermute(value, axis, [(i, i ^ mask) for i in range(lax.axis_size(axi...  8.68 us
    ppermute x11, starting transfers between devices, shift(): lax.ppermute(value, axis, [(i, (i + by) % size) for i in range(size)])  8.19 us
    ppermute x11, waiting for transfers between devices, shift(): lax.ppermute(value, axis, [(i, (i + by) % size) for i in range(size)])  5.36 us
    pallas_call x1, Pallas kernels, shards(): call(functools.partial(back_kernel, n_dp, n_mp), 'back', [shape(tok, feat...  4.1 us
    pallas_call x1, Pallas kernels, shards(): call(functools.partial(pack_kernel, n_dp, n_mp, n_pair), 'pack', [shape(r...  3.23 us
    pallas_call x2, Pallas kernels, gradient(): call(functools.partial(grad_kernel, n_dp, n_mp, len(behind)), name + '_gr...  2.43 us
    pallas_call x2, Pallas kernels, low_rank(): call(functools.partial(reduce_kernel, n_dp), name + '_part', shape(tok //...  2.41 us
  transfers between devices with their start and end apart: 23, of which 8 were waited for; matrix products, arithmetic and copies ran while one was open for 0% of the time, Pallas kernels for 21%

profile of v10, /device:TPU:0, one launch (start us, length us, event | category | flops | bytes accessed | tf_op | source)
XLA Modules:
  0.0 61.6 jit_solution(7407022839805149117)
XLA Ops:
  0.7 3.2 %pack.1 = (bf16[64,512]{1,0:T(8,128)(2,1)}, bf16[64,512]{1,0:T(8,128)(2,1)}, bf16[64,512]{1,0:T(8,128)(2,1)}, bf16[64,1024]{1,0:T(8,128)(2,1)}, bf16[64,1024]{1,...) custom-call(s32[1,2,4]{2,1,0:T(2,128)} %table.9, bf16[2,64,1024]{2,1,0:T(8,128)(2,1)} %bitcast.2, ...), custom_call_target="tpu_custom_call" | custom-call | flops 1 | bytes 1 | tf_op jit(solution)/shard_map/pack/pallas_call | solution.py:230
  3.9 3.0 %collective-permute-start = (bf16[512,512]{1,0:T(8,128)(2,1)}, bf16[512,512]{1,0:T(8,128)(2,1)S(1)}, u32[]{:S(2)}, u32[]{:S(2)}) collective-permute-start(bf16[512,512]{1,0:T(8,128)(2,1)} %get-tuple-element.37), channel_id=1, source_target_pairs={{0,2},{2,0},{1,3},{3,1},{4,6},{6,4},{5,7},{7,5},{8,10},{10,8},{9,1... | collective-permute-start | bytes 1572872 | tf_op jit(solution)/shard_map/ppermute | solution.py:35
  6.9 2.6 %collective-permute-start.2 = (bf16[64,512]{1,0:T(8,128)(2,1)}, bf16[64,512]{1,0:T(8,128)(2,1)S(1)}, u32[]{:S(2)}, u32[]{:S(2)}) collective-permute-start(bf16[64,512]{1,0:T(8,128)(2,1)} %get-tuple-element.40), channel_id=1, source_target_pairs={{0,8},{4,12},{8,0},{12,4},{1,9},{5,13},{9,1},{13,5},{2,10},{6,14},... | collective-permute-start | bytes 196616 | tf_op jit(solution)/shard_map/ppermute | solution.py:39
  9.5 1.6 %collective-permute-start.6 = (bf16[64,512]{1,0:T(8,128)(2,1)}, bf16[64,512]{1,0:T(8,128)(2,1)S(1)}, u32[]{:S(2)}, u32[]{:S(2)}) collective-permute-start(bf16[64,512]{1,0:T(8,128)(2,1)} %get-tuple-element.46), channel_id=1, source_target_pairs={{0,4},{4,0},{8,12},{12,8},{1,5},{5,1},{9,13},{13,9},{2,6},{6,2},{1... | collective-permute-start | bytes 196616 | tf_op jit(solution)/shard_map/ppermute | solution.py:39
  11.3 1.4 %collective-permute-done.2.refs_1_ = bf16[64,512]{1,0:T(8,128)(2,1)S(1)} collective-permute-done((bf16[64,512]{1,0:T(8,128)(2,1)}, bf16[64,512]{1,0:T(8,128)(2,1)S(1)}, u32[]{:S(2)}, u32[]{:S(2)}) %collective-permute-start.2) | collective-permute-done | bytes 65568 | tf_op jit(solution)/shard_map/ppermute | solution.py:39
  12.7 2.5 %collective-permute-start.3 = (bf16[64,1024]{1,0:T(8,128)(2,1)}, bf16[64,1024]{1,0:T(8,128)(2,1)S(1)}, u32[]{:S(2)}, u32[]{:S(2)}) collective-permute-start(bf16[64,1024]{1,0:T(8,128)(2,1)} %get-tuple-element.41), channel_id=1, source_target_pairs={{0,4},{4,0},{8,12},{12,8},{1,5},{5,1},{9,13},{13,9},{2,6},{6,2},{1... | collective-permute-start | bytes 393224 | tf_op jit(solution)/shard_map/ppermute | solution.py:39
  15.2 3.3 %collective-permute-start.4 = (bf16[64,1024]{1,0:T(8,128)(2,1)}, bf16[64,1024]{1,0:T(8,128)(2,1)S(1)}, u32[]{:S(2)}, u32[]{:S(2)}) collective-permute-start(bf16[64,1024]{1,0:T(8,128)(2,1)} %get-tuple-element.43), channel_id=1, source_target_pairs={{0,8},{4,12},{8,0},{12,4},{1,9},{5,13},{9,1},{13,5},{2,10},{6,14},... | collective-permute-start | bytes 393224 | tf_op jit(solution)/shard_map/ppermute | solution.py:39
  18.5 1.1 %h_part.1.refs_3_ = bf16[384,128]{1,0:T(8,128)(2,1)S(1)} custom-call(s32[12]{0:T(128)S(1)} %copy-done.6, s32[1,2,4]{2,1,0:T(2,128)S(1)} %copy-done.5, bf16[768,512]{1,0:T(8,128)(2,1)S(1)} %copy-done.2, bf16[64,512]{1,0:T(8,128)(2,1)S(1)} %collective-permute-done.6._.refs_0_, bf16[2,64,512]{2,1,0:T(8,128)(2,1)S(1)} %copy-done.4, ...), custom_call_target="tpu_custom_call" | custom-call | flops 1 | bytes 1 | tf_op jit(solution)/shard_map/h_part/pallas_call | solution.py:241
  19.6 0.6 collective-permute-start.8
  20.2 1.6 %collective-permute-start.1 = (bf16[768,512]{1,0:T(8,128)(2,1)S(1)}, bf16[768,512]{1,0:T(8,128)(2,1)S(1)}, u32[]{:S(2)}, u32[]{:S(2)}) collective-permute-start(bf16[768,512]{1,0:T(8,128)(2,1)S(1)} %copy-done.2), channel_id=1, source_target_pairs={{0,2},{2,0},{1,3},{3,1},{4,6},{6,4},{5,7},{7,5},{8,10},{10,8},{9,1... | collective-permute-start | bytes 2359304 | tf_op jit(solution)/shard_map/ppermute | solution.py:35
  21.8 3.6 %collective-permute-done.8.refs_4_ = bf16[384,128]{1,0:T(8,128)(2,1)S(1)} collective-permute-done((bf16[384,128]{1,0:T(8,128)(2,1)S(1)}, bf16[384,128]{1,0:T(8,128)(2,1)S(1)}, u32[]{:S(2)}, u32[]{:S(2)}) %collective-permute-start.8) | collective-permute-done | bytes 98336 | tf_op jit(solution)/shard_map/ppermute | solution.py:35
  25.4 1.4 %collective-permute-done.4.refs_1_.refs_7_ = bf16[64,1024]{1,0:T(8,128)(2,1)S(1)} collective-permute-done((bf16[64,1024]{1,0:T(8,128)(2,1)}, bf16[64,1024]{1,0:T(8,128)(2,1)S(1)}, u32[]{:S(2)}, u32[]{:S(2)}) %collective-permute-start.4) | collective-permute-done | bytes 131104 | tf_op jit(solution)/shard_map/ppermute | solution.py:39
  26.8 1.3 %down_grad.1 = (bf16[64,1024]{1,0:T(8,128)(2,1)S(1)}, bf16[64,1024]{1,0:T(8,128)(2,1)S(1)}, bf16[64,1024]{1,0:T(8,128)(2,1)S(1)}, bf16[64,1024]{1,0:T(8,128)(2,1)S(1)}, bf16[768,256]{1,0:T(8,128)(2,1)S(1)}) custom-call(s32[12]{0:T(128)S(1)} %copy-done.6, bf16[768,1024]{1,0:T(8,128)(2,1)S(1)} %copy-done.1, ...), custom_call_target="tpu_custom_call" | custom-call | flops 15000000512 | bytes 1 | tf_op jit(solution)/shard_map/down_grad/pallas_call | solution.py:249
  28.2 2.0 %collective-permute-start.9 = (bf16[64,1024]{1,0:T(8,128)(2,1)S(1)}, bf16[64,1024]{1,0:T(8,128)(2,1)S(1)}, u32[]{:S(2)}, u32[]{:S(2)}) collective-permute-start(bf16[64,1024]{1,0:T(8,128)(2,1)S(1)} %get-tuple-element.49), channel_id=1, source_target_pairs={{0,4},{4,0},{8,12},{12,8},{1,5},{5,1},{9,13},{13,9},{2,6},{6,2},{1... | collective-permute-start | bytes 393224 | tf_op jit(solution)/shard_map/ppermute | solution.py:39
  30.3 1.0 %collective-permute-start.11 = (bf16[64,1024]{1,0:T(8,128)(2,1)S(1)}, bf16[64,1024]{1,0:T(8,128)(2,1)S(1)}, u32[]{:S(2)}, u32[]{:S(2)}) collective-permute-start(bf16[64,1024]{1,0:T(8,128)(2,1)S(1)} %get-tuple-element.53), channel_id=1, source_target_pairs={{0,8},{4,12},{8,0},{12,4},{1,9},{5,13},{9,1},{13,5},{2,10},{6,14},... | collective-permute-start | bytes 393224 | tf_op jit(solution)/shard_map/ppermute | solution.py:39
  31.3 1.4 %collective-permute-start.12 = (bf16[64,1024]{1,0:T(8,128)(2,1)S(1)}, bf16[64,1024]{1,0:T(8,128)(2,1)S(1)}, u32[]{:S(2)}, u32[]{:S(2)}) collective-permute-start(bf16[64,1024]{1,0:T(8,128)(2,1)S(1)} %get-tuple-element.54), channel_id=1, source_target_pairs={{0,12},{4,8},{8,4},{12,0},{1,13},{5,9},{9,5},{13,1},{2,14},{6,10},... | collective-permute-start | bytes 393224 | tf_op jit(solution)/shard_map/ppermute | solution.py:39
  32.7 1.3 %u_part.1._.refs_4_ = bf16[384,128]{1,0:T(8,128)(2,1)S(1)} custom-call(s32[12]{0:T(128)S(1)} %copy-done.6, s32[1,2,4]{2,1,0:T(2,128)S(1)} %copy-done.5, bf16[768,1024]{1,0:T(8,128)(2,1)S(1)} %copy-done.1, bf16[768,256]{1,0:T(8,128)(2,1)S(1)} %get-tuple-element.48._.refs_4_, bf16[2,64,1024]{2,1,0:T(8,128)(2,1)S(1)} %bitcast.3, ...), custom_call_target="tpu_custom_call" | custom-call | flops 1 | bytes 1 | tf_op jit(solution)/shard_map/u_part/pallas_call | solution.py:241
  34.0 2.5 %collective-permute-done.9.__.refs_1_ = bf16[64,1024]{1,0:T(8,128)(2,1)S(1)} collective-permute-done((bf16[64,1024]{1,0:T(8,128)(2,1)S(1)}, bf16[64,1024]{1,0:T(8,128)(2,1)S(1)}, u32[]{:S(2)}, u32[]{:S(2)}) %collective-permute-start.9) | collective-permute-done | bytes 131104 | tf_op jit(solution)/shard_map/ppermute | solution.py:39
  36.5 0.5 collective-permute-start.13
  37.0 1.4 %y_send.1 = (bf16[768,512]{1,0:T(8,128)(2,1)S(1)}, bf16[1024,512]{1,0:T(8,128)(2,1)S(1)}) custom-call(bf16[384,128]{1,0:T(8,128)(2,1)S(1)} %u_part.1._.refs_4_, bf16[64,1024]{1,0:T(8,128)(2,1)S(1)} %collective-permute-done.9.__.refs_1_, bf16[768,1024]{1,0:T(8,128)(2,1)S(1)} %copy-done.1, bf16[512,512]{1,0:T(8,128)(2,1)S(1)} %collective-permute-done.refs_0_, ...), custom_call_target="tpu_custom_call" | custom-call | flops 1 | bytes 1 | tf_op jit(solution)/shard_map/y_send/pallas_call | solution.py:264
  38.5 1.6 %collective-permute-start.22 = (bf16[768,512]{1,0:T(8,128)(2,1)S(1)}, bf16[768,512]{1,0:T(8,128)(2,1)S(1)}, u32[]{:S(2)}, u32[]{:S(2)}) collective-permute-start(bf16[768,512]{1,0:T(8,128)(2,1)S(1)} %get-tuple-element.65), channel_id=1, source_target_pairs={{0,2},{2,0},{1,3},{3,1},{4,6},{6,4},{5,7},{7,5},{8,10},{10,8},{9,1... | collective-permute-start | bytes 2359304 | tf_op jit(solution)/shard_map/ppermute | solution.py:35
  40.0 4.1 %back.1 = (bf16[768,1024]{1,0:T(8,128)(2,1)}, s32[8,128]{1,0:T(8,128)S(1)}) custom-call(s32[1,2,4]{2,1,0:T(2,128)S(1)} %copy-done.5, bf16[2048,512]{1,0:T(8,128)(2,1)S(1)} %copy-done, bf16[768,512]{1,0:T(8,128)(2,1)S(1)} %copy-done.2, bf16[768,512]{1,0:T(8,128)(2,1)S(1)} %collective-permute-done.1.refs_2_.refs_3_, ...), custom_call_target="tpu_custom_call" | custom-call | flops 1 | bytes 1 | tf_op jit(solution)/shard_map/back/pallas_call | solution.py:273
  44.1 1.1 %up_grad.1 = (bf16[64,512]{1,0:T(8,128)(2,1)S(1)}, bf16[64,512]{1,0:T(8,128)(2,1)S(1)}, bf16[64,512]{1,0:T(8,128)(2,1)S(1)}, bf16[64,512]{1,0:T(8,128)(2,1)S(1)}, bf16[768,256]{1,0:T(8,128)(2,1)S(1)}) custom-call(s32[12]{0:T(128)S(1)} %copy-done.6, bf16[768,512]{1,0:T(8,128)(2,1)S(1)} %copy-done.2, s32[8,128]{1,0:T(8,128)S(1)} %get-tuple-element.52.refs_0_.picks, ...), custom_call_target="tpu_custom_call" | custom-call | flops 15000000512 | bytes 1 | tf_op jit(solution)/shard_map/up_grad/pallas_call | solution.py:249
  45.2 2.3 %collective-permute-start.15 = (bf16[64,512]{1,0:T(8,128)(2,1)S(1)}, bf16[64,512]{1,0:T(8,128)(2,1)S(1)}, u32[]{:S(2)}, u32[]{:S(2)}) collective-permute-start(bf16[64,512]{1,0:T(8,128)(2,1)S(1)} %get-tuple-element.57), channel_id=1, source_target_pairs={{0,4},{4,0},{8,12},{12,8},{1,5},{5,1},{9,13},{13,9},{2,6},{6,2},{1... | collective-permute-start | bytes 196616 | tf_op jit(solution)/shard_map/ppermute | solution.py:39
  47.5 4.0 %collective-permute-start.16 = (bf16[64,512]{1,0:T(8,128)(2,1)S(1)}, bf16[64,512]{1,0:T(8,128)(2,1)S(1)}, u32[]{:S(2)}, u32[]{:S(2)}) collective-permute-start(bf16[64,512]{1,0:T(8,128)(2,1)S(1)} %get-tuple-element.58), channel_id=1, source_target_pairs={{0,8},{4,12},{8,0},{12,4},{1,9},{5,13},{9,1},{13,5},{2,10},{6,14},... | collective-permute-start | bytes 196616 | tf_op jit(solution)/shard_map/ppermute | solution.py:39
  52.0 2.2 %y_own.1.refs_10_ = f32[768,512]{1,0:T(8,128)S(1)} custom-call(s32[1,2,4]{2,1,0:T(2,128)S(1)} %copy-done.5, bf16[2048,512]{1,0:T(8,128)(2,1)S(1)} %copy-done, bf16[768,1024]{1,0:T(8,128)(2,1)S(1)} %copy-done.1, bf16[768,256]{1,0:T(8,128)(2,1)S(1)} %get-tuple-element.60.wide, bf16[2,64,512]{2,1,0:T(8,128)(2,1)S(1)} %copy-done.4, ...), custom_call_target="tpu_custom_call" | custom-call | flops 15000000512 | bytes 1 | tf_op jit(solution)/shard_map/y_own/pallas_call | solution.py:283
  54.2 3.4 %collective-permute-done.17.refs_5_ = bf16[64,512]{1,0:T(8,128)(2,1)S(1)} collective-permute-done((bf16[64,512]{1,0:T(8,128)(2,1)S(1)}, bf16[64,512]{1,0:T(8,128)(2,1)S(1)}, u32[]{:S(2)}, u32[]{:S(2)}) %collective-permute-start.17) | collective-permute-done | bytes 65568 | tf_op jit(solution)/shard_map/ppermute | solution.py:39
  57.6 0.5 collective-permute-start.19
  58.2 0.7 %collective-permute-done.18.refs_6_ = bf16[64,512]{1,0:T(8,128)(2,1)S(1)} collective-permute-done((bf16[64,512]{1,0:T(8,128)(2,1)S(1)}, bf16[64,512]{1,0:T(8,128)(2,1)S(1)}, u32[]{:S(2)}, u32[]{:S(2)}) %collective-permute-start.18) | collective-permute-done | bytes 65568 | tf_op jit(solution)/shard_map/ppermute | solution.py:35
  59.0 0.4 collective-permute-done.20.refs_8_
  59.4 0.7 %collective-permute-done.21.refs_9_ = bf16[64,512]{1,0:T(8,128)(2,1)S(1)} collective-permute-done((bf16[64,512]{1,0:T(8,128)(2,1)S(1)}, bf16[64,512]{1,0:T(8,128)(2,1)S(1)}, u32[]{:S(2)}, u32[]{:S(2)}) %collective-permute-start.21) | collective-permute-done | bytes 65568 | tf_op jit(solution)/shard_map/ppermute | solution.py:35
  60.1 1.5 %last.1 = (f32[2,64,1024]{2,1,0:T(8,128)}, f32[2,64,512]{2,1,0:T(8,128)}, bf16[768,512]{1,0:T(8,128)(2,1)}) custom-call(s32[8,128]{1,0:T(8,128)S(1)} %get-tuple-element.52.refs_0_.picks, bf16[2,64,1024]{2,1,0:T(8,128)(2,1)S(1)} %sites.1.refs_0_, bf16[2,64,1024]{2,1,0:T(8,128)(2,1)S(1)} %collective-permute-done.14.refs_1_, ...), custom_call_target="tpu_custom_call" | custom-call | flops 1 | bytes 1 | tf_op jit(solution)/shard_map/last/pallas_call | solution.py:298
  (38 shorter events, 1.0 us)
Async XLA Ops:
  0.6 17.8 %copy-start.5 = (s32[1,2,4]{2,1,0:T(2,128)S(1)}, s32[1,2,4]{2,1,0:T(2,128)}, u32[]{:S(2)}) copy-start(s32[1,2,4]{2,1,0:T(2,128)} %table.9) | copy-start | bytes 100
  0.6 17.8 %copy-start.4 = (bf16[2,64,512]{2,1,0:T(8,128)(2,1)S(1)}, bf16[2,64,512]{2,1,0:T(8,128)(2,1)}, u32[]{:S(2)}) copy-start(bf16[2,64,512]{2,1,0:T(8,128)(2,1)} %own_up.1) | copy-start | bytes 393220
  0.7 17.8 %copy-start.6 = (s32[12]{0:T(128)S(1)}, s32[12]{0:T(128)}, u32[]{:S(2)}) copy-start(s32[12]{0:T(128)} %owner.7) | copy-start | bytes 148
  0.7 17.8 %copy-start.2 = (bf16[768,512]{1,0:T(8,128)(2,1)S(1)}, bf16[768,512]{1,0:T(8,128)(2,1)}, u32[]{:S(2)}) copy-start(bf16[768,512]{1,0:T(8,128)(2,1)} %act.7) | copy-start | bytes 2359300
  0.7 26.1 %copy-start.1 = (bf16[768,1024]{1,0:T(8,128)(2,1)S(1)}, bf16[768,1024]{1,0:T(8,128)(2,1)}, u32[]{:S(2)}) copy-start(bf16[768,1024]{1,0:T(8,128)(2,1)} %x.3) | copy-start | bytes 4718596
  3.9 16.3 %collective-permute-start = (bf16[512,512]{1,0:T(8,128)(2,1)}, bf16[512,512]{1,0:T(8,128)(2,1)S(1)}, u32[]{:S(2)}, u32[]{:S(2)}) collective-permute-start(bf16[512,512]{1,0:T(8,128)(2,1)} %get-tuple-element.37), channel_id=1, source_target_pairs={{0,2},{2,0},{1,3},{3,1},{4,6},{6,4},{5,7},{7,5},{8,10},{10,8},{9,1... | collective-permute-start | bytes 1572872 | tf_op jit(solution)/shard_map/ppermute | solution.py:35
  6.9 5.8 %collective-permute-start.2 = (bf16[64,512]{1,0:T(8,128)(2,1)}, bf16[64,512]{1,0:T(8,128)(2,1)S(1)}, u32[]{:S(2)}, u32[]{:S(2)}) collective-permute-start(bf16[64,512]{1,0:T(8,128)(2,1)} %get-tuple-element.40), channel_id=1, source_target_pairs={{0,8},{4,12},{8,0},{12,4},{1,9},{5,13},{9,1},{13,5},{2,10},{6,14},... | collective-permute-start | bytes 196616 | tf_op jit(solution)/shard_map/ppermute | solution.py:39
  9.5 9.0 %collective-permute-start.6 = (bf16[64,512]{1,0:T(8,128)(2,1)}, bf16[64,512]{1,0:T(8,128)(2,1)S(1)}, u32[]{:S(2)}, u32[]{:S(2)}) collective-permute-start(bf16[64,512]{1,0:T(8,128)(2,1)} %get-tuple-element.46), channel_id=1, source_target_pairs={{0,4},{4,0},{8,12},{12,8},{1,5},{5,1},{9,13},{13,9},{2,6},{6,2},{1... | collective-permute-start | bytes 196616 | tf_op jit(solution)/shard_map/ppermute | solution.py:39
  11.1 7.4 %collective-permute-start.7 = (bf16[64,512]{1,0:T(8,128)(2,1)}, bf16[64,512]{1,0:T(8,128)(2,1)S(1)}, u32[]{:S(2)}, u32[]{:S(2)}) collective-permute-start(bf16[64,512]{1,0:T(8,128)(2,1)} %get-tuple-element.47), channel_id=1, source_target_pairs={{0,12},{4,8},{8,4},{12,0},{1,13},{5,9},{9,5},{13,1},{2,14},{6,10},... | collective-permute-start | bytes 196616 | tf_op jit(solution)/shard_map/ppermute | solution.py:39
  12.7 12.7 %collective-permute-start.3 = (bf16[64,1024]{1,0:T(8,128)(2,1)}, bf16[64,1024]{1,0:T(8,128)(2,1)S(1)}, u32[]{:S(2)}, u32[]{:S(2)}) collective-permute-start(bf16[64,1024]{1,0:T(8,128)(2,1)} %get-tuple-element.41), channel_id=1, source_target_pairs={{0,4},{4,0},{8,12},{12,8},{1,5},{5,1},{9,13},{13,9},{2,6},{6,2},{1... | collective-permute-start | bytes 393224 | tf_op jit(solution)/shard_map/ppermute | solution.py:39
  15.2 11.6 %collective-permute-start.4 = (bf16[64,1024]{1,0:T(8,128)(2,1)}, bf16[64,1024]{1,0:T(8,128)(2,1)S(1)}, u32[]{:S(2)}, u32[]{:S(2)}) collective-permute-start(bf16[64,1024]{1,0:T(8,128)(2,1)} %get-tuple-element.43), channel_id=1, source_target_pairs={{0,8},{4,12},{8,0},{12,4},{1,9},{5,13},{9,1},{13,5},{2,10},{6,14},... | collective-permute-start | bytes 393224 | tf_op jit(solution)/shard_map/ppermute | solution.py:39
  18.5 8.4 %collective-permute-start.5 = (bf16[64,1024]{1,0:T(8,128)(2,1)}, bf16[64,1024]{1,0:T(8,128)(2,1)S(1)}, u32[]{:S(2)}, u32[]{:S(2)}) collective-permute-start(bf16[64,1024]{1,0:T(8,128)(2,1)} %get-tuple-element.45), channel_id=1, source_target_pairs={{0,12},{4,8},{8,4},{12,0},{1,13},{5,9},{9,5},{13,1},{2,14},{6,10},... | collective-permute-start | bytes 393224 | tf_op jit(solution)/shard_map/ppermute | solution.py:39
  19.6 13.1 %copy-start.3 = (bf16[2,1024,64]{1,2,0:T(8,128)(2,1)S(1)}, bf16[2,1024,64]{1,2,0:T(8,128)(2,1)}, u32[]{:S(2)}) copy-start(bf16[2,1024,64]{1,2,0:T(8,128)(2,1)} %param.9) | copy-start | bytes 786436
  19.6 5.8 %collective-permute-start.8 = (bf16[384,128]{1,0:T(8,128)(2,1)S(1)}, bf16[384,128]{1,0:T(8,128)(2,1)S(1)}, u32[]{:S(2)}, u32[]{:S(2)}) collective-permute-start(bf16[384,128]{1,0:T(8,128)(2,1)S(1)} %h_part.1.refs_3_), channel_id=1, source_target_pairs={{0,2},{2,0},{1,3},{3,1},{4,6},{6,4},{5,7},{7,5},{8,10},{10,8},{9,1... | collective-permute-start | bytes 294920 | tf_op jit(solution)/shard_map/ppermute | solution.py:35
  20.2 19.8 %collective-permute-start.1 = (bf16[768,512]{1,0:T(8,128)(2,1)S(1)}, bf16[768,512]{1,0:T(8,128)(2,1)S(1)}, u32[]{:S(2)}, u32[]{:S(2)}) collective-permute-start(bf16[768,512]{1,0:T(8,128)(2,1)S(1)} %copy-done.2), channel_id=1, source_target_pairs={{0,2},{2,0},{1,3},{3,1},{4,6},{6,4},{5,7},{7,5},{8,10},{10,8},{9,1... | collective-permute-start | bytes 2359304 | tf_op jit(solution)/shard_map/ppermute | solution.py:35
  28.2 8.9 %collective-permute-start.10 = (bf16[512,512]{1,0:T(8,128)(2,1)S(1)}, bf16[512,512]{1,0:T(8,128)(2,1)S(1)}, u32[]{:S(2)}, u32[]{:S(2)}) collective-permute-start(bf16[512,512]{1,0:T(8,128)(2,1)S(1)} %collective-permute-done.refs_0_), channel_id=1, source_target_pairs={{0,1},{1,0},{2,3},{3,2},{4,5},{5,4},{6,7},{7,6},{8,9},{9,8},{10,11... | collective-permute-start | bytes 1572872 | tf_op jit(solution)/shard_map/ppermute | solution.py:35
  28.2 8.3 %collective-permute-start.9 = (bf16[64,1024]{1,0:T(8,128)(2,1)S(1)}, bf16[64,1024]{1,0:T(8,128)(2,1)S(1)}, u32[]{:S(2)}, u32[]{:S(2)}) collective-permute-start(bf16[64,1024]{1,0:T(8,128)(2,1)S(1)} %get-tuple-element.49), channel_id=1, source_target_pairs={{0,4},{4,0},{8,12},{12,8},{1,5},{5,1},{9,13},{13,9},{2,6},{6,2},{1... | collective-permute-start | bytes 393224 | tf_op jit(solution)/shard_map/ppermute | solution.py:39
  30.3 13.9 %collective-permute-start.11 = (bf16[64,1024]{1,0:T(8,128)(2,1)S(1)}, bf16[64,1024]{1,0:T(8,128)(2,1)S(1)}, u32[]{:S(2)}, u32[]{:S(2)}) collective-permute-start(bf16[64,1024]{1,0:T(8,128)(2,1)S(1)} %get-tuple-element.53), channel_id=1, source_target_pairs={{0,8},{4,12},{8,0},{12,4},{1,9},{5,13},{9,1},{13,5},{2,10},{6,14},... | collective-permute-start | bytes 393224 | tf_op jit(solution)/shard_map/ppermute | solution.py:39
  31.3 12.8 %collective-permute-start.12 = (bf16[64,1024]{1,0:T(8,128)(2,1)S(1)}, bf16[64,1024]{1,0:T(8,128)(2,1)S(1)}, u32[]{:S(2)}, u32[]{:S(2)}) collective-permute-start(bf16[64,1024]{1,0:T(8,128)(2,1)S(1)} %get-tuple-element.54), channel_id=1, source_target_pairs={{0,12},{4,8},{8,4},{12,0},{1,13},{5,9},{9,5},{13,1},{2,14},{6,10},... | collective-permute-start | bytes 393224 | tf_op jit(solution)/shard_map/ppermute | solution.py:39
  34.0 6.0 %copy-start = (bf16[2048,512]{1,0:T(8,128)(2,1)S(1)}, bf16[2048,512]{1,0:T(8,128)(2,1)}, u32[]{:S(2)}) copy-start(bf16[2048,512]{1,0:T(8,128)(2,1)} %w.3) | copy-start | bytes 6291460
  36.5 7.6 %collective-permute-start.13 = (bf16[384,128]{1,0:T(8,128)(2,1)S(1)}, bf16[384,128]{1,0:T(8,128)(2,1)S(1)}, u32[]{:S(2)}, u32[]{:S(2)}) collective-permute-start(bf16[384,128]{1,0:T(8,128)(2,1)S(1)} %u_part.1._.refs_4_), channel_id=1, source_target_pairs={{0,2},{2,0},{1,3},{3,1},{4,6},{6,4},{5,7},{7,5},{8,10},{10,8},{9,1... | collective-permute-start | bytes 294920 | tf_op jit(solution)/shard_map/ppermute | solution.py:35
  38.5 21.7 %collective-permute-start.22 = (bf16[768,512]{1,0:T(8,128)(2,1)S(1)}, bf16[768,512]{1,0:T(8,128)(2,1)S(1)}, u32[]{:S(2)}, u32[]{:S(2)}) collective-permute-start(bf16[768,512]{1,0:T(8,128)(2,1)S(1)} %get-tuple-element.65), channel_id=1, source_target_pairs={{0,2},{2,0},{1,3},{3,1},{4,6},{6,4},{5,7},{7,5},{8,10},{10,8},{9,1... | collective-permute-start | bytes 2359304 | tf_op jit(solution)/shard_map/ppermute | solution.py:35
  45.2 12.4 %collective-permute-start.15 = (bf16[64,512]{1,0:T(8,128)(2,1)S(1)}, bf16[64,512]{1,0:T(8,128)(2,1)S(1)}, u32[]{:S(2)}, u32[]{:S(2)}) collective-permute-start(bf16[64,512]{1,0:T(8,128)(2,1)S(1)} %get-tuple-element.57), channel_id=1, source_target_pairs={{0,4},{4,0},{8,12},{12,8},{1,5},{5,1},{9,13},{13,9},{2,6},{6,2},{1... | collective-permute-start | bytes 196616 | tf_op jit(solution)/shard_map/ppermute | solution.py:39
  47.5 10.1 %collective-permute-start.16 = (bf16[64,512]{1,0:T(8,128)(2,1)S(1)}, bf16[64,512]{1,0:T(8,128)(2,1)S(1)}, u32[]{:S(2)}, u32[]{:S(2)}) collective-permute-start(bf16[64,512]{1,0:T(8,128)(2,1)S(1)} %get-tuple-element.58), channel_id=1, source_target_pairs={{0,8},{4,12},{8,0},{12,4},{1,9},{5,13},{9,1},{13,5},{2,10},{6,14},... | collective-permute-start | bytes 196616 | tf_op jit(solution)/shard_map/ppermute | solution.py:39
  51.5 6.1 %collective-permute-start.17 = (bf16[64,512]{1,0:T(8,128)(2,1)S(1)}, bf16[64,512]{1,0:T(8,128)(2,1)S(1)}, u32[]{:S(2)}, u32[]{:S(2)}) collective-permute-start(bf16[64,512]{1,0:T(8,128)(2,1)S(1)} %get-tuple-element.59), channel_id=1, source_target_pairs={{0,12},{4,8},{8,4},{12,0},{1,13},{5,9},{9,5},{13,1},{2,14},{6,10},... | collective-permute-start | bytes 196616 | tf_op jit(solution)/shard_map/ppermute | solution.py:39
  51.9 8.2 %collective-permute-start.14 = (bf16[2,64,1024]{2,1,0:T(8,128)(2,1)S(1)}, bf16[2,64,1024]{2,1,0:T(8,128)(2,1)S(1)}, u32[]{:S(2)}, u32[]{:S(2)}) collective-permute-start(bf16[2,64,1024]{2,1,0:T(8,128)(2,1)S(1)} %sites.1.refs_0_), channel_id=1, source_target_pairs={{0,1},{1,0},{2,3},{3,2},{4,5},{5,4},{6,7},{7,6},{8,9},{9,8},{10,11... | collective-permute-start | bytes 786440 | tf_op jit(solution)/shard_map/ppermute | solution.py:35
  57.6 1.3 %collective-permute-start.18 = (bf16[64,512]{1,0:T(8,128)(2,1)S(1)}, bf16[64,512]{1,0:T(8,128)(2,1)S(1)}, u32[]{:S(2)}, u32[]{:S(2)}) collective-permute-start(bf16[64,512]{1,0:T(8,128)(2,1)S(1)} %get-tuple-element.61._.refs_2_), channel_id=1, source_target_pairs={{0,1},{1,0},{2,3},{3,2},{4,5},{5,4},{6,7},{7,6},{8,9},{9,8},{10,11... | collective-permute-start | bytes 196616 | tf_op jit(solution)/shard_map/ppermute | solution.py:35
  57.6 1.4 %collective-permute-start.19 = (bf16[64,512]{1,0:T(8,128)(2,1)S(1)}, bf16[64,512]{1,0:T(8,128)(2,1)S(1)}, u32[]{:S(2)}, u32[]{:S(2)}) collective-permute-start(bf16[64,512]{1,0:T(8,128)(2,1)S(1)} %collective-permute-done.15.refs_3_), channel_id=1, source_target_pairs={{0,1},{1,0},{2,3},{3,2},{4,5},{5,4},{6,7},{7,6},{8,9},{9,8},{10,11... | collective-permute-start | bytes 196616 | tf_op jit(solution)/shard_map/ppermute | solution.py:35
  58.1 1.3 %collective-permute-start.20 = (bf16[64,512]{1,0:T(8,128)(2,1)S(1)}, bf16[64,512]{1,0:T(8,128)(2,1)S(1)}, u32[]{:S(2)}, u32[]{:S(2)}) collective-permute-start(bf16[64,512]{1,0:T(8,128)(2,1)S(1)} %collective-permute-done.16.refs_4_), channel_id=1, source_target_pairs={{0,1},{1,0},{2,3},{3,2},{4,5},{5,4},{6,7},{7,6},{8,9},{9,8},{10,11... | collective-permute-start | bytes 196616 | tf_op jit(solution)/shard_map/ppermute | solution.py:35
  58.9 1.3 %collective-permute-start.21 = (bf16[64,512]{1,0:T(8,128)(2,1)S(1)}, bf16[64,512]{1,0:T(8,128)(2,1)S(1)}, u32[]{:S(2)}, u32[]{:S(2)}) collective-permute-start(bf16[64,512]{1,0:T(8,128)(2,1)S(1)} %collective-permute-done.17.refs_5_), channel_id=1, source_target_pairs={{0,1},{1,0},{2,3},{3,2},{4,5},{5,4},{6,7},{7,6},{8,9},{9,8},{10,11... | collective-permute-start | bytes 196616 | tf_op jit(solution)/shard_map/ppermute | solution.py:35

commit v11 on v10

--- a/solution.py
+++ b/solution.py
@@ -65,11 +65,11 @@
 def wanted_site(table, n_dp, s, q=0):
     n_pair = lax.axis_size("pair")
     core = lax.rem(lax.axis_index("pair") + n_pair - q, n_pair)
-    return table[0, core, lax.bitwise_xor(lax.axis_index("dp"), s)]
+    return table[0, core, lax.bitwise_xor(lax.axis_index("dp"), (n_dp - s) % n_dp)]
 
 
 def slot_of(owner, b, n_dp):
-    return lax.bitwise_xor(lax.axis_index("dp"), owner[b])
+    return lax.rem(n_dp - lax.bitwise_xor(lax.axis_index("dp"), owner[b]), n_dp)
 
 
 def pack_kernel(n_dp, n_mp, n_pair, table, down, up, w, *refs):
@@ -234,8 +234,8 @@
         [pltpu.SemaphoreType.DMA((2 * away + n_other,))], mib=60,
     )(table, down, up, w)
     pieces = [shift(packed[2 * away + s - 1], "mp", s) for s in range(1, n_mp)]
-    ups = [swap(packed[s - 1], "dp", s) for s in range(1, n_dp)]
-    downs = [swap(after(packed[away + s - 1], ups[1 % away]), "dp", s) for s in range(1, n_dp)]
+    ups = [swap(packed[s - 1], "dp", n_dp - s) for s in range(1, n_dp)]
+    downs = [swap(after(packed[away + s - 1], ups[0]), "dp", n_dp - s) for s in range(1, n_dp)]
 
     def low_rank(act, own, maps, behind, name):
         mine = call(
@@ -251,7 +251,7 @@
             [shape(rank, act.shape[1])] * n_dp + [shape(tok, n_dp * rank)],
             [SMEM, VMEM] + [ANY] * len(behind) + [VMEM] * n_mp, [VMEM] * (n_dp + 1), flops=flops,
         )(owner, act, *behind, *parts)
-        return [grads[0]] + [swap(grads[s], "dp", s) for s in range(1, n_dp)], wide
+        return [grads[0]] + [swap(grads[s], "dp", n_dp - s) for s in range(1, n_dp)], wide
 
     h_parts = low_rank(gy, up, ups, ups[0], "h")
     gy_got = [shift(after(gy, *pieces), "mp", s) for s in range(1, n_mp)]

time: 61.8 us -> 60 us (0.971)
  starting transfers between devices: 29.1 us -> 26.2 us
  waiting for transfers between devices: 14 us -> 15.2 us
    ppermute x12, starting transfers between devices: 20.9 us -> 18.1 us  [swap(): lax.ppermute(value, axis, [(i, i ^ mask) for i in range(lax.axis_size(axi...]
    ppermute x11, waiting for transfers between devices: 5.36 us -> 6.41 us  [shift(): lax.ppermute(value, axis, [(i, (i + by) % size) for i in range(size)])]
  transfers between devices with their start and end apart: 23 -> 23, of which waited for: 8 -> 9; matrix products, arithmetic and copies ran while one was open for 0% -> 0% of each run, Pallas kernels for 21% -> 22%
where the time goes in v11:
time: 60 us; the launch traced here: 59.8 us
  starting transfers between devices  26.2 us (44%)
  Pallas kernels  17.6 us (29%)
  waiting for transfers between devices  15.2 us (25%)
  between operations  0.8 us (1%)
    ppermute x12, starting transfers between devices, swap(): lax.ppermute(value, axis, [(i, i ^ mask) for i in range(lax.axis_size(axi...  18.1 us
    ppermute x12, waiting for transfers between devices, swap(): lax.ppermute(value, axis, [(i, i ^ mask) for i in range(lax.axis_size(axi...  8.81 us
    ppermute x11, starting transfers between devices, shift(): lax.ppermute(value, axis, [(i, (i + by) % size) for i in range(size)])  8.06 us
    ppermute x11, waiting for transfers between devices, shift(): lax.ppermute(value, axis, [(i, (i + by) % size) for i in range(size)])  6.41 us
    pallas_call x1, Pallas kernels, shards(): call(functools.partial(back_kernel, n_dp, n_mp), 'back', [shape(tok, feat...  4.1 us
    pallas_call x1, Pallas kernels, shards(): call(functools.partial(pack_kernel, n_dp, n_mp, n_pair), 'pack', [shape(r...  3.23 us
    pallas_call x2, Pallas kernels, gradient(): call(functools.partial(grad_kernel, n_dp, n_mp, len(behind)), name + '_gr...  2.43 us
    pallas_call x2, Pallas kernels, low_rank(): call(functools.partial(reduce_kernel, n_dp), name + '_part', shape(tok //...  2.41 us
  transfers between devices with their start and end apart: 23, of which 9 were waited for; matrix products, arithmetic and copies ran while one was open for 0% of the time, Pallas kernels for 22%

profile of v11, /device:TPU:0, one launch (start us, length us, event | category | flops | bytes accessed | tf_op | source)
XLA Modules:
  0.0 59.8 jit_solution(2466033930760140231)
XLA Ops:
  0.7 3.2 %pack.1 = (bf16[64,512]{1,0:T(8,128)(2,1)}, bf16[64,512]{1,0:T(8,128)(2,1)}, bf16[64,512]{1,0:T(8,128)(2,1)}, bf16[64,1024]{1,0:T(8,128)(2,1)}, bf16[64,1024]{1,...) custom-call(s32[1,2,4]{2,1,0:T(2,128)} %table.9, bf16[2,64,1024]{2,1,0:T(8,128)(2,1)} %bitcast.2, ...), custom_call_target="tpu_custom_call" | custom-call | flops 1 | bytes 1 | tf_op jit(solution)/shard_map/pack/pallas_call | solution.py:230
  3.9 3.0 %collective-permute-start = (bf16[512,512]{1,0:T(8,128)(2,1)}, bf16[512,512]{1,0:T(8,128)(2,1)S(1)}, u32[]{:S(2)}, u32[]{:S(2)}) collective-permute-start(bf16[512,512]{1,0:T(8,128)(2,1)} %get-tuple-element.37), channel_id=1, source_target_pairs={{0,2},{2,0},{1,3},{3,1},{4,6},{6,4},{5,7},{7,5},{8,10},{10,8},{9,1... | collective-permute-start | bytes 1572872 | tf_op jit(solution)/shard_map/ppermute | solution.py:35
  6.9 3.6 %collective-permute-start.2 = (bf16[64,512]{1,0:T(8,128)(2,1)}, bf16[64,512]{1,0:T(8,128)(2,1)S(1)}, u32[]{:S(2)}, u32[]{:S(2)}) collective-permute-start(bf16[64,512]{1,0:T(8,128)(2,1)} %get-tuple-element.40), channel_id=1, source_target_pairs={{0,12},{4,8},{8,4},{12,0},{1,13},{5,9},{9,5},{13,1},{2,14},{6,10},... | collective-permute-start | bytes 196616 | tf_op jit(solution)/shard_map/ppermute | solution.py:39
  10.5 0.8 %collective-permute-start.7 = (bf16[64,512]{1,0:T(8,128)(2,1)}, bf16[64,512]{1,0:T(8,128)(2,1)S(1)}, u32[]{:S(2)}, u32[]{:S(2)}) collective-permute-start(bf16[64,512]{1,0:T(8,128)(2,1)} %get-tuple-element.47), channel_id=1, source_target_pairs={{0,4},{4,0},{8,12},{12,8},{1,5},{5,1},{9,13},{13,9},{2,6},{6,2},{1... | collective-permute-start | bytes 196616 | tf_op jit(solution)/shard_map/ppermute | solution.py:39
  11.3 2.7 %collective-permute-done.2._.refs_0_ = bf16[64,512]{1,0:T(8,128)(2,1)S(1)} collective-permute-done((bf16[64,512]{1,0:T(8,128)(2,1)}, bf16[64,512]{1,0:T(8,128)(2,1)S(1)}, u32[]{:S(2)}, u32[]{:S(2)}) %collective-permute-start.2) | collective-permute-done | bytes 65568 | tf_op jit(solution)/shard_map/ppermute | solution.py:39
  14.0 3.6 %collective-permute-start.3 = (bf16[64,1024]{1,0:T(8,128)(2,1)}, bf16[64,1024]{1,0:T(8,128)(2,1)S(1)}, u32[]{:S(2)}, u32[]{:S(2)}) collective-permute-start(bf16[64,1024]{1,0:T(8,128)(2,1)} %get-tuple-element.41), channel_id=1, source_target_pairs={{0,12},{4,8},{8,4},{12,0},{1,13},{5,9},{9,5},{13,1},{2,14},{6,10},... | collective-permute-start | bytes 393224 | tf_op jit(solution)/shard_map/ppermute | solution.py:39
  17.6 0.7 %collective-permute-start.5 = (bf16[64,1024]{1,0:T(8,128)(2,1)}, bf16[64,1024]{1,0:T(8,128)(2,1)S(1)}, u32[]{:S(2)}, u32[]{:S(2)}) collective-permute-start(bf16[64,1024]{1,0:T(8,128)(2,1)} %get-tuple-element.45), channel_id=1, source_target_pairs={{0,4},{4,0},{8,12},{12,8},{1,5},{5,1},{9,13},{13,9},{2,6},{6,2},{1... | collective-permute-start | bytes 393224 | tf_op jit(solution)/shard_map/ppermute | solution.py:39
  18.4 1.1 %h_part.1.refs_3_ = bf16[384,128]{1,0:T(8,128)(2,1)S(1)} custom-call(s32[12]{0:T(128)S(1)} %copy-done.6, s32[1,2,4]{2,1,0:T(2,128)S(1)} %copy-done.5, bf16[768,512]{1,0:T(8,128)(2,1)S(1)} %copy-done.2, bf16[64,512]{1,0:T(8,128)(2,1)S(1)} %collective-permute-done.2._.refs_0_, bf16[2,64,512]{2,1,0:T(8,128)(2,1)S(1)} %copy-done.4, ...), custom_call_target="tpu_custom_call" | custom-call | flops 1 | bytes 1 | tf_op jit(solution)/shard_map/h_part/pallas_call | solution.py:241
  19.5 0.4 collective-permute-start.8
  20.0 1.7 %collective-permute-start.1 = (bf16[768,512]{1,0:T(8,128)(2,1)S(1)}, bf16[768,512]{1,0:T(8,128)(2,1)S(1)}, u32[]{:S(2)}, u32[]{:S(2)}) collective-permute-start(bf16[768,512]{1,0:T(8,128)(2,1)S(1)} %copy-done.2), channel_id=1, source_target_pairs={{0,2},{2,0},{1,3},{3,1},{4,6},{6,4},{5,7},{7,5},{8,10},{10,8},{9,1... | collective-permute-start | bytes 2359304 | tf_op jit(solution)/shard_map/ppermute | solution.py:35
  21.6 3.7 %collective-permute-done.8.refs_4_ = bf16[384,128]{1,0:T(8,128)(2,1)S(1)} collective-permute-done((bf16[384,128]{1,0:T(8,128)(2,1)S(1)}, bf16[384,128]{1,0:T(8,128)(2,1)S(1)}, u32[]{:S(2)}, u32[]{:S(2)}) %collective-permute-start.8) | collective-permute-done | bytes 98336 | tf_op jit(solution)/shard_map/ppermute | solution.py:35
  25.3 2.0 %collective-permute-done.4.refs_1_.refs_7_ = bf16[64,1024]{1,0:T(8,128)(2,1)S(1)} collective-permute-done((bf16[64,1024]{1,0:T(8,128)(2,1)}, bf16[64,1024]{1,0:T(8,128)(2,1)S(1)}, u32[]{:S(2)}, u32[]{:S(2)}) %collective-permute-start.4) | collective-permute-done | bytes 131104 | tf_op jit(solution)/shard_map/ppermute | solution.py:39
  27.3 1.3 %down_grad.1 = (bf16[64,1024]{1,0:T(8,128)(2,1)S(1)}, bf16[64,1024]{1,0:T(8,128)(2,1)S(1)}, bf16[64,1024]{1,0:T(8,128)(2,1)S(1)}, bf16[64,1024]{1,0:T(8,128)(2,1)S(1)}, bf16[768,256]{1,0:T(8,128)(2,1)S(1)}) custom-call(s32[12]{0:T(128)S(1)} %copy-done.6, bf16[768,1024]{1,0:T(8,128)(2,1)S(1)} %copy-done.1, ...), custom_call_target="tpu_custom_call" | custom-call | flops 15000000512 | bytes 1 | tf_op jit(solution)/shard_map/down_grad/pallas_call | solution.py:249
  28.7 2.7 %collective-permute-start.9 = (bf16[64,1024]{1,0:T(8,128)(2,1)S(1)}, bf16[64,1024]{1,0:T(8,128)(2,1)S(1)}, u32[]{:S(2)}, u32[]{:S(2)}) collective-permute-start(bf16[64,1024]{1,0:T(8,128)(2,1)S(1)} %get-tuple-element.49), channel_id=1, source_target_pairs={{0,12},{4,8},{8,4},{12,0},{1,13},{5,9},{9,5},{13,1},{2,14},{6,10},... | collective-permute-start | bytes 393224 | tf_op jit(solution)/shard_map/ppermute | solution.py:39
  31.4 1.7 %collective-permute-start.12 = (bf16[64,1024]{1,0:T(8,128)(2,1)S(1)}, bf16[64,1024]{1,0:T(8,128)(2,1)S(1)}, u32[]{:S(2)}, u32[]{:S(2)}) collective-permute-start(bf16[64,1024]{1,0:T(8,128)(2,1)S(1)} %get-tuple-element.54), channel_id=1, source_target_pairs={{0,4},{4,0},{8,12},{12,8},{1,5},{5,1},{9,13},{13,9},{2,6},{6,2},{1... | collective-permute-start | bytes 393224 | tf_op jit(solution)/shard_map/ppermute | solution.py:39
  33.2 1.3 %u_part.1._.refs_4_ = bf16[384,128]{1,0:T(8,128)(2,1)S(1)} custom-call(s32[12]{0:T(128)S(1)} %copy-done.6, s32[1,2,4]{2,1,0:T(2,128)S(1)} %copy-done.5, bf16[768,1024]{1,0:T(8,128)(2,1)S(1)} %copy-done.1, bf16[768,256]{1,0:T(8,128)(2,1)S(1)} %get-tuple-element.48._.refs_4_, bf16[2,64,1024]{2,1,0:T(8,128)(2,1)S(1)} %bitcast.3, ...), custom_call_target="tpu_custom_call" | custom-call | flops 1 | bytes 1 | tf_op jit(solution)/shard_map/u_part/pallas_call | solution.py:241
  34.5 2.5 %collective-permute-done.9.__.refs_1_ = bf16[64,1024]{1,0:T(8,128)(2,1)S(1)} collective-permute-done((bf16[64,1024]{1,0:T(8,128)(2,1)S(1)}, bf16[64,1024]{1,0:T(8,128)(2,1)S(1)}, u32[]{:S(2)}, u32[]{:S(2)}) %collective-permute-start.9) | collective-permute-done | bytes 131104 | tf_op jit(solution)/shard_map/ppermute | solution.py:39
  37.0 0.5 collective-permute-start.13
  37.6 1.4 %y_send.1 = (bf16[768,512]{1,0:T(8,128)(2,1)S(1)}, bf16[1024,512]{1,0:T(8,128)(2,1)S(1)}) custom-call(bf16[384,128]{1,0:T(8,128)(2,1)S(1)} %u_part.1._.refs_4_, bf16[64,1024]{1,0:T(8,128)(2,1)S(1)} %collective-permute-done.9.__.refs_1_, bf16[768,1024]{1,0:T(8,128)(2,1)S(1)} %copy-done.1, bf16[512,512]{1,0:T(8,128)(2,1)S(1)} %collective-permute-done.refs_0_, ...), custom_call_target="tpu_custom_call" | custom-call | flops 1 | bytes 1 | tf_op jit(solution)/shard_map/y_send/pallas_call | solution.py:264
  39.0 1.6 %collective-permute-start.22 = (bf16[768,512]{1,0:T(8,128)(2,1)S(1)}, bf16[768,512]{1,0:T(8,128)(2,1)S(1)}, u32[]{:S(2)}, u32[]{:S(2)}) collective-permute-start(bf16[768,512]{1,0:T(8,128)(2,1)S(1)} %get-tuple-element.65), channel_id=1, source_target_pairs={{0,2},{2,0},{1,3},{3,1},{4,6},{6,4},{5,7},{7,5},{8,10},{10,8},{9,1... | collective-permute-start | bytes 2359304 | tf_op jit(solution)/shard_map/ppermute | solution.py:35
  40.6 4.1 %back.1 = (bf16[768,1024]{1,0:T(8,128)(2,1)}, s32[8,128]{1,0:T(8,128)S(1)}) custom-call(s32[1,2,4]{2,1,0:T(2,128)S(1)} %copy-done.5, bf16[2048,512]{1,0:T(8,128)(2,1)S(1)} %copy-done, bf16[768,512]{1,0:T(8,128)(2,1)S(1)} %copy-done.2, bf16[768,512]{1,0:T(8,128)(2,1)S(1)} %collective-permute-done.1.refs_2_.refs_3_, ...), custom_call_target="tpu_custom_call" | custom-call | flops 1 | bytes 1 | tf_op jit(solution)/shard_map/back/pallas_call | solution.py:273
  44.7 1.1 %up_grad.1 = (bf16[64,512]{1,0:T(8,128)(2,1)S(1)}, bf16[64,512]{1,0:T(8,128)(2,1)S(1)}, bf16[64,512]{1,0:T(8,128)(2,1)S(1)}, bf16[64,512]{1,0:T(8,128)(2,1)S(1)}, bf16[768,256]{1,0:T(8,128)(2,1)S(1)}) custom-call(s32[12]{0:T(128)S(1)} %copy-done.6, bf16[768,512]{1,0:T(8,128)(2,1)S(1)} %copy-done.2, s32[8,128]{1,0:T(8,128)S(1)} %get-tuple-element.52.refs_0_.picks, ...), custom_call_target="tpu_custom_call" | custom-call | flops 15000000512 | bytes 1 | tf_op jit(solution)/shard_map/up_grad/pallas_call | solution.py:249
  45.8 2.8 %collective-permute-start.15 = (bf16[64,512]{1,0:T(8,128)(2,1)S(1)}, bf16[64,512]{1,0:T(8,128)(2,1)S(1)}, u32[]{:S(2)}, u32[]{:S(2)}) collective-permute-start(bf16[64,512]{1,0:T(8,128)(2,1)S(1)} %get-tuple-element.57), channel_id=1, source_target_pairs={{0,12},{4,8},{8,4},{12,0},{1,13},{5,9},{9,5},{13,1},{2,14},{6,10},... | collective-permute-start | bytes 196616 | tf_op jit(solution)/shard_map/ppermute | solution.py:39
  48.6 2.1 %collective-permute-start.16 = (bf16[64,512]{1,0:T(8,128)(2,1)S(1)}, bf16[64,512]{1,0:T(8,128)(2,1)S(1)}, u32[]{:S(2)}, u32[]{:S(2)}) collective-permute-start(bf16[64,512]{1,0:T(8,128)(2,1)S(1)} %get-tuple-element.58), channel_id=1, source_target_pairs={{0,8},{4,12},{8,0},{12,4},{1,9},{5,13},{9,1},{13,5},{2,10},{6,14},... | collective-permute-start | bytes 196616 | tf_op jit(solution)/shard_map/ppermute | solution.py:39
  51.1 2.2 %y_own.1.refs_10_ = f32[768,512]{1,0:T(8,128)S(1)} custom-call(s32[1,2,4]{2,1,0:T(2,128)S(1)} %copy-done.5, bf16[2048,512]{1,0:T(8,128)(2,1)S(1)} %copy-done, bf16[768,1024]{1,0:T(8,128)(2,1)S(1)} %copy-done.1, bf16[768,256]{1,0:T(8,128)(2,1)S(1)} %get-tuple-element.60.wide, bf16[2,64,512]{2,1,0:T(8,128)(2,1)S(1)} %copy-done.4, ...), custom_call_target="tpu_custom_call" | custom-call | flops 15000000512 | bytes 1 | tf_op jit(solution)/shard_map/y_own/pallas_call | solution.py:283
  53.3 1.6 %collective-permute-done.17.refs_5_ = bf16[64,512]{1,0:T(8,128)(2,1)S(1)} collective-permute-done((bf16[64,512]{1,0:T(8,128)(2,1)S(1)}, bf16[64,512]{1,0:T(8,128)(2,1)S(1)}, u32[]{:S(2)}, u32[]{:S(2)}) %collective-permute-start.17) | collective-permute-done | bytes 65568 | tf_op jit(solution)/shard_map/ppermute | solution.py:39
  54.9 0.5 collective-permute-start.19
  55.5 0.7 %collective-permute-done.18.refs_6_ = bf16[64,512]{1,0:T(8,128)(2,1)S(1)} collective-permute-done((bf16[64,512]{1,0:T(8,128)(2,1)S(1)}, bf16[64,512]{1,0:T(8,128)(2,1)S(1)}, u32[]{:S(2)}, u32[]{:S(2)}) %collective-permute-start.18) | collective-permute-done | bytes 65568 | tf_op jit(solution)/shard_map/ppermute | solution.py:35
  56.4 0.4 collective-permute-done.20.refs_8_
  56.7 0.7 %collective-permute-done.21.refs_9_ = bf16[64,512]{1,0:T(8,128)(2,1)S(1)} collective-permute-done((bf16[64,512]{1,0:T(8,128)(2,1)S(1)}, bf16[64,512]{1,0:T(8,128)(2,1)S(1)}, u32[]{:S(2)}, u32[]{:S(2)}) %collective-permute-start.21) | collective-permute-done | bytes 65568 | tf_op jit(solution)/shard_map/ppermute | solution.py:35
  57.4 0.9 %collective-permute-done.22.refs_11_ = bf16[768,512]{1,0:T(8,128)(2,1)S(1)} collective-permute-done((bf16[768,512]{1,0:T(8,128)(2,1)S(1)}, bf16[768,512]{1,0:T(8,128)(2,1)S(1)}, u32[]{:S(2)}, u32[]{:S(2)}) %collective-permute-start.22) | collective-permute-done | bytes 786464 | tf_op jit(solution)/shard_map/ppermute | solution.py:35
  58.4 1.5 %last.1 = (f32[2,64,1024]{2,1,0:T(8,128)}, f32[2,64,512]{2,1,0:T(8,128)}, bf16[768,512]{1,0:T(8,128)(2,1)}) custom-call(s32[8,128]{1,0:T(8,128)S(1)} %get-tuple-element.52.refs_0_.picks, bf16[2,64,1024]{2,1,0:T(8,128)(2,1)S(1)} %sites.1.refs_0_, bf16[2,64,1024]{2,1,0:T(8,128)(2,1)S(1)} %collective-permute-done.14.refs_1_, ...), custom_call_target="tpu_custom_call" | custom-call | flops 1 | bytes 1 | tf_op jit(solution)/shard_map/last/pallas_call | solution.py:298
  (38 shorter events, 0.8 us)
Async XLA Ops:
  0.6 17.8 %copy-start.5 = (s32[1,2,4]{2,1,0:T(2,128)S(1)}, s32[1,2,4]{2,1,0:T(2,128)}, u32[]{:S(2)}) copy-start(s32[1,2,4]{2,1,0:T(2,128)} %table.9) | copy-start | bytes 100
  0.6 17.8 %copy-start.4 = (bf16[2,64,512]{2,1,0:T(8,128)(2,1)S(1)}, bf16[2,64,512]{2,1,0:T(8,128)(2,1)}, u32[]{:S(2)}) copy-start(bf16[2,64,512]{2,1,0:T(8,128)(2,1)} %own_up.1) | copy-start | bytes 393220
  0.7 17.8 %copy-start.6 = (s32[12]{0:T(128)S(1)}, s32[12]{0:T(128)}, u32[]{:S(2)}) copy-start(s32[12]{0:T(128)} %owner.7) | copy-start | bytes 148
  0.7 17.8 %copy-start.2 = (bf16[768,512]{1,0:T(8,128)(2,1)S(1)}, bf16[768,512]{1,0:T(8,128)(2,1)}, u32[]{:S(2)}) copy-start(bf16[768,512]{1,0:T(8,128)(2,1)} %act.7) | copy-start | bytes 2359300
  0.7 26.6 %copy-start.1 = (bf16[768,1024]{1,0:T(8,128)(2,1)S(1)}, bf16[768,1024]{1,0:T(8,128)(2,1)}, u32[]{:S(2)}) copy-start(bf16[768,1024]{1,0:T(8,128)(2,1)} %x.3) | copy-start | bytes 4718596
  3.9 16.0 %collective-permute-start = (bf16[512,512]{1,0:T(8,128)(2,1)}, bf16[512,512]{1,0:T(8,128)(2,1)S(1)}, u32[]{:S(2)}, u32[]{:S(2)}) collective-permute-start(bf16[512,512]{1,0:T(8,128)(2,1)} %get-tuple-element.37), channel_id=1, source_target_pairs={{0,2},{2,0},{1,3},{3,1},{4,6},{6,4},{5,7},{7,5},{8,10},{10,8},{9,1... | collective-permute-start | bytes 1572872 | tf_op jit(solution)/shard_map/ppermute | solution.py:35
  6.9 7.1 %collective-permute-start.2 = (bf16[64,512]{1,0:T(8,128)(2,1)}, bf16[64,512]{1,0:T(8,128)(2,1)S(1)}, u32[]{:S(2)}, u32[]{:S(2)}) collective-permute-start(bf16[64,512]{1,0:T(8,128)(2,1)} %get-tuple-element.40), channel_id=1, source_target_pairs={{0,12},{4,8},{8,4},{12,0},{1,13},{5,9},{9,5},{13,1},{2,14},{6,10},... | collective-permute-start | bytes 196616 | tf_op jit(solution)/shard_map/ppermute | solution.py:39
  10.5 7.1 %collective-permute-start.6 = (bf16[64,512]{1,0:T(8,128)(2,1)}, bf16[64,512]{1,0:T(8,128)(2,1)S(1)}, u32[]{:S(2)}, u32[]{:S(2)}) collective-permute-start(bf16[64,512]{1,0:T(8,128)(2,1)} %get-tuple-element.46), channel_id=1, source_target_pairs={{0,8},{4,12},{8,0},{12,4},{1,9},{5,13},{9,1},{13,5},{2,10},{6,14},... | collective-permute-start | bytes 196616 | tf_op jit(solution)/shard_map/ppermute | solution.py:39
  10.5 7.9 %collective-permute-start.7 = (bf16[64,512]{1,0:T(8,128)(2,1)}, bf16[64,512]{1,0:T(8,128)(2,1)S(1)}, u32[]{:S(2)}, u32[]{:S(2)}) collective-permute-start(bf16[64,512]{1,0:T(8,128)(2,1)} %get-tuple-element.47), channel_id=1, source_target_pairs={{0,4},{4,0},{8,12},{12,8},{1,5},{5,1},{9,13},{13,9},{2,6},{6,2},{1... | collective-permute-start | bytes 196616 | tf_op jit(solution)/shard_map/ppermute | solution.py:39
  14.0 11.3 %collective-permute-start.3 = (bf16[64,1024]{1,0:T(8,128)(2,1)}, bf16[64,1024]{1,0:T(8,128)(2,1)S(1)}, u32[]{:S(2)}, u32[]{:S(2)}) collective-permute-start(bf16[64,1024]{1,0:T(8,128)(2,1)} %get-tuple-element.41), channel_id=1, source_target_pairs={{0,12},{4,8},{8,4},{12,0},{1,13},{5,9},{9,5},{13,1},{2,14},{6,10},... | collective-permute-start | bytes 393224 | tf_op jit(solution)/shard_map/ppermute | solution.py:39
  17.6 9.7 %collective-permute-start.4 = (bf16[64,1024]{1,0:T(8,128)(2,1)}, bf16[64,1024]{1,0:T(8,128)(2,1)S(1)}, u32[]{:S(2)}, u32[]{:S(2)}) collective-permute-start(bf16[64,1024]{1,0:T(8,128)(2,1)} %get-tuple-element.43), channel_id=1, source_target_pairs={{0,8},{4,12},{8,0},{12,4},{1,9},{5,13},{9,1},{13,5},{2,10},{6,14},... | collective-permute-start | bytes 393224 | tf_op jit(solution)/shard_map/ppermute | solution.py:39
  17.6 9.7 %collective-permute-start.5 = (bf16[64,1024]{1,0:T(8,128)(2,1)}, bf16[64,1024]{1,0:T(8,128)(2,1)S(1)}, u32[]{:S(2)}, u32[]{:S(2)}) collective-permute-start(bf16[64,1024]{1,0:T(8,128)(2,1)} %get-tuple-element.45), channel_id=1, source_target_pairs={{0,4},{4,0},{8,12},{12,8},{1,5},{5,1},{9,13},{13,9},{2,6},{6,2},{1... | collective-permute-start | bytes 393224 | tf_op jit(solution)/shard_map/ppermute | solution.py:39
  19.5 13.6 %copy-start.3 = (bf16[2,1024,64]{1,2,0:T(8,128)(2,1)S(1)}, bf16[2,1024,64]{1,2,0:T(8,128)(2,1)}, u32[]{:S(2)}) copy-start(bf16[2,1024,64]{1,2,0:T(8,128)(2,1)} %param.9) | copy-start | bytes 786436
  19.5 5.8 %collective-permute-start.8 = (bf16[384,128]{1,0:T(8,128)(2,1)S(1)}, bf16[384,128]{1,0:T(8,128)(2,1)S(1)}, u32[]{:S(2)}, u32[]{:S(2)}) collective-permute-start(bf16[384,128]{1,0:T(8,128)(2,1)S(1)} %h_part.1.refs_3_), channel_id=1, source_target_pairs={{0,2},{2,0},{1,3},{3,1},{4,6},{6,4},{5,7},{7,5},{8,10},{10,8},{9,1... | collective-permute-start | bytes 294920 | tf_op jit(solution)/shard_map/ppermute | solution.py:35
  20.0 20.6 %collective-permute-start.1 = (bf16[768,512]{1,0:T(8,128)(2,1)S(1)}, bf16[768,512]{1,0:T(8,128)(2,1)S(1)}, u32[]{:S(2)}, u32[]{:S(2)}) collective-permute-start(bf16[768,512]{1,0:T(8,128)(2,1)S(1)} %copy-done.2), channel_id=1, source_target_pairs={{0,2},{2,0},{1,3},{3,1},{4,6},{6,4},{5,7},{7,5},{8,10},{10,8},{9,1... | collective-permute-start | bytes 2359304 | tf_op jit(solution)/shard_map/ppermute | solution.py:35
  28.6 8.9 %collective-permute-start.10 = (bf16[512,512]{1,0:T(8,128)(2,1)S(1)}, bf16[512,512]{1,0:T(8,128)(2,1)S(1)}, u32[]{:S(2)}, u32[]{:S(2)}) collective-permute-start(bf16[512,512]{1,0:T(8,128)(2,1)S(1)} %collective-permute-done.refs_0_), channel_id=1, source_target_pairs={{0,1},{1,0},{2,3},{3,2},{4,5},{5,4},{6,7},{7,6},{8,9},{9,8},{10,11... | collective-permute-start | bytes 1572872 | tf_op jit(solution)/shard_map/ppermute | solution.py:35
  28.7 8.3 %collective-permute-start.9 = (bf16[64,1024]{1,0:T(8,128)(2,1)S(1)}, bf16[64,1024]{1,0:T(8,128)(2,1)S(1)}, u32[]{:S(2)}, u32[]{:S(2)}) collective-permute-start(bf16[64,1024]{1,0:T(8,128)(2,1)S(1)} %get-tuple-element.49), channel_id=1, source_target_pairs={{0,12},{4,8},{8,4},{12,0},{1,13},{5,9},{9,5},{13,1},{2,14},{6,10},... | collective-permute-start | bytes 393224 | tf_op jit(solution)/shard_map/ppermute | solution.py:39
  31.4 13.2 %collective-permute-start.11 = (bf16[64,1024]{1,0:T(8,128)(2,1)S(1)}, bf16[64,1024]{1,0:T(8,128)(2,1)S(1)}, u32[]{:S(2)}, u32[]{:S(2)}) collective-permute-start(bf16[64,1024]{1,0:T(8,128)(2,1)S(1)} %get-tuple-element.53), channel_id=1, source_target_pairs={{0,8},{4,12},{8,0},{12,4},{1,9},{5,13},{9,1},{13,5},{2,10},{6,14},... | collective-permute-start | bytes 393224 | tf_op jit(solution)/shard_map/ppermute | solution.py:39
  31.4 13.2 %collective-permute-start.12 = (bf16[64,1024]{1,0:T(8,128)(2,1)S(1)}, bf16[64,1024]{1,0:T(8,128)(2,1)S(1)}, u32[]{:S(2)}, u32[]{:S(2)}) collective-permute-start(bf16[64,1024]{1,0:T(8,128)(2,1)S(1)} %get-tuple-element.54), channel_id=1, source_target_pairs={{0,4},{4,0},{8,12},{12,8},{1,5},{5,1},{9,13},{13,9},{2,6},{6,2},{1... | collective-permute-start | bytes 393224 | tf_op jit(solution)/shard_map/ppermute | solution.py:39
  34.5 6.1 %copy-start = (bf16[2048,512]{1,0:T(8,128)(2,1)S(1)}, bf16[2048,512]{1,0:T(8,128)(2,1)}, u32[]{:S(2)}) copy-start(bf16[2048,512]{1,0:T(8,128)(2,1)} %w.3) | copy-start | bytes 6291460
  37.0 7.6 %collective-permute-start.13 = (bf16[384,128]{1,0:T(8,128)(2,1)S(1)}, bf16[384,128]{1,0:T(8,128)(2,1)S(1)}, u32[]{:S(2)}, u32[]{:S(2)}) collective-permute-start(bf16[384,128]{1,0:T(8,128)(2,1)S(1)} %u_part.1._.refs_4_), channel_id=1, source_target_pairs={{0,2},{2,0},{1,3},{3,1},{4,6},{6,4},{5,7},{7,5},{8,10},{10,8},{9,1... | collective-permute-start | bytes 294920 | tf_op jit(solution)/shard_map/ppermute | solution.py:35
  39.0 19.4 %collective-permute-start.22 = (bf16[768,512]{1,0:T(8,128)(2,1)S(1)}, bf16[768,512]{1,0:T(8,128)(2,1)S(1)}, u32[]{:S(2)}, u32[]{:S(2)}) collective-permute-start(bf16[768,512]{1,0:T(8,128)(2,1)S(1)} %get-tuple-element.65), channel_id=1, source_target_pairs={{0,2},{2,0},{1,3},{3,1},{4,6},{6,4},{5,7},{7,5},{8,10},{10,8},{9,1... | collective-permute-start | bytes 2359304 | tf_op jit(solution)/shard_map/ppermute | solution.py:35
  45.8 9.2 %collective-permute-start.15 = (bf16[64,512]{1,0:T(8,128)(2,1)S(1)}, bf16[64,512]{1,0:T(8,128)(2,1)S(1)}, u32[]{:S(2)}, u32[]{:S(2)}) collective-permute-start(bf16[64,512]{1,0:T(8,128)(2,1)S(1)} %get-tuple-element.57), channel_id=1, source_target_pairs={{0,12},{4,8},{8,4},{12,0},{1,13},{5,9},{9,5},{13,1},{2,14},{6,10},... | collective-permute-start | bytes 196616 | tf_op jit(solution)/shard_map/ppermute | solution.py:39
  48.6 6.3 %collective-permute-start.16 = (bf16[64,512]{1,0:T(8,128)(2,1)S(1)}, bf16[64,512]{1,0:T(8,128)(2,1)S(1)}, u32[]{:S(2)}, u32[]{:S(2)}) collective-permute-start(bf16[64,512]{1,0:T(8,128)(2,1)S(1)} %get-tuple-element.58), channel_id=1, source_target_pairs={{0,8},{4,12},{8,0},{12,4},{1,9},{5,13},{9,1},{13,5},{2,10},{6,14},... | collective-permute-start | bytes 196616 | tf_op jit(solution)/shard_map/ppermute | solution.py:39
  50.7 4.3 %collective-permute-start.17 = (bf16[64,512]{1,0:T(8,128)(2,1)S(1)}, bf16[64,512]{1,0:T(8,128)(2,1)S(1)}, u32[]{:S(2)}, u32[]{:S(2)}) collective-permute-start(bf16[64,512]{1,0:T(8,128)(2,1)S(1)} %get-tuple-element.59), channel_id=1, source_target_pairs={{0,4},{4,0},{8,12},{12,8},{1,5},{5,1},{9,13},{13,9},{2,6},{6,2},{1... | collective-permute-start | bytes 196616 | tf_op jit(solution)/shard_map/ppermute | solution.py:39
  51.0 6.4 %collective-permute-start.14 = (bf16[2,64,1024]{2,1,0:T(8,128)(2,1)S(1)}, bf16[2,64,1024]{2,1,0:T(8,128)(2,1)S(1)}, u32[]{:S(2)}, u32[]{:S(2)}) collective-permute-start(bf16[2,64,1024]{2,1,0:T(8,128)(2,1)S(1)} %sites.1.refs_0_), channel_id=1, source_target_pairs={{0,1},{1,0},{2,3},{3,2},{4,5},{5,4},{6,7},{7,6},{8,9},{9,8},{10,11... | collective-permute-start | bytes 786440 | tf_op jit(solution)/shard_map/ppermute | solution.py:35
  54.9 1.3 %collective-permute-start.18 = (bf16[64,512]{1,0:T(8,128)(2,1)S(1)}, bf16[64,512]{1,0:T(8,128)(2,1)S(1)}, u32[]{:S(2)}, u32[]{:S(2)}) collective-permute-start(bf16[64,512]{1,0:T(8,128)(2,1)S(1)} %get-tuple-element.61._.refs_2_), channel_id=1, source_target_pairs={{0,1},{1,0},{2,3},{3,2},{4,5},{5,4},{6,7},{7,6},{8,9},{9,8},{10,11... | collective-permute-start | bytes 196616 | tf_op jit(solution)/shard_map/ppermute | solution.py:35
  54.9 1.4 %collective-permute-start.19 = (bf16[64,512]{1,0:T(8,128)(2,1)S(1)}, bf16[64,512]{1,0:T(8,128)(2,1)S(1)}, u32[]{:S(2)}, u32[]{:S(2)}) collective-permute-start(bf16[64,512]{1,0:T(8,128)(2,1)S(1)} %collective-permute-done.15.refs_3_), channel_id=1, source_target_pairs={{0,1},{1,0},{2,3},{3,2},{4,5},{5,4},{6,7},{7,6},{8,9},{9,8},{10,11... | collective-permute-start | bytes 196616 | tf_op jit(solution)/shard_map/ppermute | solution.py:35
  55.5 1.3 %collective-permute-start.20 = (bf16[64,512]{1,0:T(8,128)(2,1)S(1)}, bf16[64,512]{1,0:T(8,128)(2,1)S(1)}, u32[]{:S(2)}, u32[]{:S(2)}) collective-permute-start(bf16[64,512]{1,0:T(8,128)(2,1)S(1)} %collective-permute-done.16.refs_4_), channel_id=1, source_target_pairs={{0,1},{1,0},{2,3},{3,2},{4,5},{5,4},{6,7},{7,6},{8,9},{9,8},{10,11... | collective-permute-start | bytes 196616 | tf_op jit(solution)/shard_map/ppermute | solution.py:35
  56.2 1.3 %collective-permute-start.21 = (bf16[64,512]{1,0:T(8,128)(2,1)S(1)}, bf16[64,512]{1,0:T(8,128)(2,1)S(1)}, u32[]{:S(2)}, u32[]{:S(2)}) collective-permute-start(bf16[64,512]{1,0:T(8,128)(2,1)S(1)} %collective-permute-done.17.refs_5_), channel_id=1, source_target_pairs={{0,1},{1,0},{2,3},{3,2},{4,5},{5,4},{6,7},{7,6},{8,9},{9,8},{10,11... | collective-permute-start | bytes 196616 | tf_op jit(solution)/shard_map/ppermute | solution.py:35

commit v12 on v11

--- a/solution.py
+++ b/solution.py
@@ -74,14 +74,19 @@
 
 def pack_kernel(n_dp, n_mp, n_pair, table, down, up, w, *refs):
     away = n_dp - 1
-    ups, downs, pieces, sem = refs[:away], refs[away:2 * away], refs[2 * away:-1], refs[-1]
+    ups, downs, near = refs[:away - 1], refs[away - 1:2 * away - 2], refs[2 * away - 2]
+    pieces, sem = refs[2 * away - 1:-1], refs[-1]
     feat = w.shape[0] // n_mp
     part = feat // n_pair
     copies = []
     for s in range(away):
         site = wanted_site(table, n_dp, s + 1)
-        copies.append(pltpu.make_async_copy(up.at[site], ups[s], sem.at[s]))
-        copies.append(pltpu.make_async_copy(down.at[site], downs[s], sem.at[away + s]))
+        if s < away - 1:
+            up_to, down_to = ups[s], downs[s]
+        else:
+            down_to, up_to = near.at[:, pl.ds(0, feat)], near.at[:, pl.ds(feat, up.shape[2])]
+        copies.append(pltpu.make_async_copy(up.at[site], up_to, sem.at[s]))
+        copies.append(pltpu.make_async_copy(down.at[site], down_to, sem.at[away + s]))
     for s in range(1, n_mp):
         row = lax.rem(lax.axis_index("mp") + s, n_mp) * feat + lax.axis_index("pair") * part
         row = pl.multiple_of(row, part)
@@ -89,19 +94,24 @@
     run(copies)
 
 
-def gather_maps(n_dp, table, own, gots, wide):
+def share(ref, width, tail):
+    start = ref.shape[1] - width if tail else 0
+    return ref[:, start:start + width]
+
+
+def gather_maps(n_dp, table, own, gots, wide, tail):
     rank = own.shape[1]
     wide[:rank, :] = own[wanted_site(table, n_dp, 0)]
     for s in range(1, n_dp):
-        wide[s * rank:(s + 1) * rank, :] = gots[s - 1][...]
-
-
-def reduce_kernel(n_dp, owner, table, act, _, own, *refs):
+        wide[s * rank:(s + 1) * rank, :] = share(gots[s - 1], wide.shape[1], tail)
+
+
+def reduce_kernel(n_dp, tail, owner, table, act, _, own, *refs):
     gots, out, wide = refs[:n_dp - 1], refs[n_dp - 1], refs[n_dp]
     rank = own.shape[1]
     blocks = owner.shape[0]
     rows = act.shape[0] // blocks
-    gather_maps(n_dp, table, own, gots, wide)
+    gather_maps(n_dp, table, own, gots, wide, tail)
     full = nt(act[...], wide[...])
     lane_slot = lax.broadcasted_iota(jnp.int32, (rows, n_dp * rank), 1) // rank
     folded = []
@@ -116,7 +126,7 @@
         out[j * rows:(j + 1) * rows, :] = pair.astype(BF16)
 
 
-def grad_kernel(n_dp, n_part, n_behind, owner, act, *refs):
+def grad_kernel(n_dp, n_part, n_behind, owner, act, near, *refs):
     refs = refs[n_behind:]
     parts, grads, wide = refs[:n_part], refs[n_part:n_part + n_dp], refs[n_part + n_dp]
     rank = wide.shape[1] // n_dp
@@ -132,11 +142,15 @@
         kept = jnp.where(lane_slot == slot_of(owner, b, n_dp), spread, 0.0)
         wide[b * rows:(b + 1) * rows, :] = kept.astype(BF16)
     full = tn(wide[...], act[...])
+    width = act.shape[1]
     for s in range(n_dp):
-        grads[s][...] = full[s * rank:(s + 1) * rank].astype(BF16)
-
-
-def send_kernel(n_pair, feat, n_mp, _, __, x, *refs):
+        grads[s][:, grads[s].shape[1] - width:] = full[s * rank:(s + 1) * rank].astype(BF16)
+    extra = grads[-1].shape[1] - width
+    if extra:
+        grads[-1][:, :extra] = near[...]
+
+
+def send_kernel(n_pair, feat, n_mp, _, x, *refs):
     n_other = n_mp - 1
     pieces, outs, rows = refs[:n_other * n_pair], refs[n_other * n_pair:n_other * n_pair + n_other], refs[-n_other:]
     part = feat // n_pair
@@ -167,7 +181,7 @@
             sites = jnp.where(row == k, wanted_site(table, n_dp, k % n_dp, k // n_dp), sites)
         picks[...] = sites
         own[...] = w[pl.ds(pl.multiple_of(lax.axis_index("mp") * feat, feat), feat), :]
-        gather_maps(n_dp, table, own_down, downs, maps)
+        gather_maps(n_dp, table, own_down, downs, maps, False)
 
     total = nt(gys[0][...], own[...]) + SCALE * nn(wide[...], maps[...])
     for gy, row in zip(gys[1:], rows):
@@ -181,23 +195,23 @@
 
     @pl.when(pl.program_id(0) == 0)
     def _():
-        gather_maps(n_dp, table, own_up, ups, maps)
+        gather_maps(n_dp, table, own_up, ups, maps, True)
 
     own = w[pl.ds(pl.multiple_of(lax.axis_index("mp") * feat, feat), feat), :]
     out[...] = nn(x[...], own) + SCALE * nn(wide[...], maps[...])
 
 
-def pick_sum(grads, picks, site):
-    total = jnp.zeros(grads[0].shape, F32)
+def pick_sum(grads, picks, site, width, tail):
+    total = jnp.zeros((grads[0].shape[0], width), F32)
     for k, grad in enumerate(grads):
-        total = total + jnp.where(picks[k:k + 1, :1] == site, grad[...].astype(F32), 0.0)
+        total = total + jnp.where(picks[k:k + 1, :1] == site, share(grad, width, tail).astype(F32), 0.0)
     return total
 
 
 def site_kernel(picks, _, *refs):
     grads, out = refs[:-1], refs[-1]
     for site in range(out.shape[0]):
-        out[site] = pick_sum(grads, picks, site).astype(BF16)
+        out[site] = pick_sum(grads, picks, site, out.shape[2], False).astype(BF16)
 
 
 def last_kernel(n_pair, n_ups, n_mp, picks, *refs):
@@ -207,7 +221,7 @@
     for part in downs[1:]:
         total = total + part[0].astype(F32)
     down[0] = SCALE * total
-    up[0] = SCALE * pick_sum(ups, picks, pl.program_id(0))
+    up[0] = SCALE * pick_sum(ups, picks, pl.program_id(0), up.shape[2], True)
     total = parts[0][...]
     for part in parts[1:]:
         total = total + part[...].astype(F32)
@@ -227,36 +241,38 @@
     whole = lambda *dims: pl.BlockSpec(dims, lambda i: (0,) * len(dims))
 
     away = n_dp - 1
+    far = away - 1
     packed = call(
         functools.partial(pack_kernel, n_dp, n_mp, n_pair), "pack",
-        [shape(rank, cols)] * away + [shape(rank, feat)] * away + [shape(part, cols)] * n_other,
-        [SMEM, ANY, ANY, ANY], [VMEM] * (2 * away + n_other),
+        [shape(rank, cols)] * far + [shape(rank, feat)] * far + [shape(rank, feat + cols)] + [shape(part, cols)] * n_other,
+        [SMEM, ANY, ANY, ANY], [VMEM] * (2 * far + 1 + n_other),
         [pltpu.SemaphoreType.DMA((2 * away + n_other,))], mib=60,
     )(table, down, up, w)
-    pieces = [shift(packed[2 * away + s - 1], "mp", s) for s in range(1, n_mp)]
-    ups = [swap(packed[s - 1], "dp", n_dp - s) for s in range(1, n_dp)]
-    downs = [swap(after(packed[away + s - 1], ups[0]), "dp", n_dp - s) for s in range(1, n_dp)]
-
-    def low_rank(act, own, maps, behind, name):
+    pieces = [shift(packed[2 * far + s], "mp", s) for s in range(1, n_mp)]
+    near = swap(packed[2 * far], "dp", 1)
+    ups = [swap(packed[s - 1], "dp", n_dp - s) for s in range(1, away)] + [near]
+    downs = [swap(after(packed[far + s - 1], ups[0]), "dp", n_dp - s) for s in range(1, away)] + [near]
+
+    def low_rank(act, own, maps, behind, tail, name):
         mine = call(
-            functools.partial(reduce_kernel, n_dp), name + "_part",
+            functools.partial(reduce_kernel, n_dp, tail), name + "_part",
             shape(tok // 2, 2 * rank), [SMEM, SMEM, VMEM, ANY] + [VMEM] * n_dp, VMEM,
             [pltpu.VMEM((n_dp * rank, act.shape[1]), BF16)],
         )(owner, table, act, behind, own, *maps)
         return [mine] + [shift(mine, "mp", s) for s in range(1, n_mp)]
 
-    def gradient(act, parts, behind, name, flops):
+    def gradient(act, parts, near, width, behind, name):
         *grads, wide = call(
             functools.partial(grad_kernel, n_dp, n_mp, len(behind)), name + "_grad",
-            [shape(rank, act.shape[1])] * n_dp + [shape(tok, n_dp * rank)],
-            [SMEM, VMEM] + [ANY] * len(behind) + [VMEM] * n_mp, [VMEM] * (n_dp + 1), flops=flops,
-        )(owner, act, *behind, *parts)
-        return [grads[0]] + [swap(grads[s], "dp", n_dp - s) for s in range(1, n_dp)], wide
-
-    h_parts = low_rank(gy, up, ups, ups[0], "h")
+            [shape(rank, act.shape[1])] * away + [shape(rank, width)] + [shape(tok, n_dp * rank)],
+            [SMEM, VMEM, VMEM] + [ANY] * len(behind) + [VMEM] * n_mp, [VMEM] * (n_dp + 1), flops=GRAD_COST,
+        )(owner, act, near, *behind, *parts)
+        return [grads[0]] + [swap(grads[s], "dp", n_dp - s) for s in range(1, away)], grads[-1], wide
+
+    h_parts = low_rank(gy, up, ups, ups[0], True, "h")
     gy_got = [shift(after(gy, *pieces), "mp", s) for s in range(1, n_mp)]
-    down_back, h_wide = gradient(x, h_parts, downs, "down", GRAD_COST)
-    u_parts = low_rank(x, down, downs, h_wide, "u")
+    down_back, down_near, h_wide = gradient(x, h_parts, h_parts[0], feat, downs, "down")
+    u_parts = low_rank(x, down, downs, h_wide, False, "u")
 
     parts = []
     for piece in pieces:
@@ -264,33 +280,37 @@
     sent = call(
         functools.partial(send_kernel, n_pair, feat, n_mp), "y_send",
         [shape(tok, cols)] * n_other + [shape(feat, cols)] * n_other,
-        [ANY, ANY, row_block(feat)] + [whole(part, cols)] * len(parts),
+        [ANY, row_block(feat)] + [whole(part, cols)] * len(parts),
         [row_block(cols)] * n_other + [whole(feat, cols)] * n_other,
         grid=(TILES,),
-    )(u_parts[0], down_back[1], x, *parts)
+    )(u_parts[0], x, *parts)
     w_rows = sent[n_other:]
     y_got = [shift(sent[s - 1], "mp", n_mp - s) for s in range(1, n_mp)]
     back, picks = call(
         functools.partial(back_kernel, n_dp, n_mp), "back",
         [shape(tok, feat), shape(-(-n_dp * n_pair // 8) * 8, 128, dtype=jnp.int32)],
         [SMEM, whole(*w.shape)] + [row_block(cols)] * n_mp + [whole(feat, cols)] * n_other
-        + [row_block(n_dp * rank), whole(*down.shape)] + [whole(rank, feat)] * away,
+        + [row_block(n_dp * rank), whole(*down.shape)] + [whole(*one.shape) for one in downs],
         [row_block(feat), whole(-(-n_dp * n_pair // 8) * 8, 128)],
         [pltpu.VMEM((feat, cols), BF16), pltpu.VMEM((n_dp * rank, feat), BF16)], grid=(TILES,),
     )(table, w, gy, *gy_got, *w_rows, h_wide, down, *downs)
-    up_back, u_wide = gradient(gy, u_parts, [picks] + down_back[2:] + gy_got, "up", GRAD_COST)
+    up_back, both_near, u_wide = gradient(
+        gy, u_parts, down_near, feat + cols, [picks] + down_back[1:] + gy_got, "up"
+    )
+    both_near = swap(both_near, "dp", 1)
+    down_back, up_back = down_back + [both_near], up_back + [both_near]
 
     y_own = call(
         functools.partial(own_kernel, n_dp), "y_own", shape(tok, cols, dtype=F32),
         [SMEM, whole(*w.shape), row_block(feat), row_block(n_dp * rank), whole(*up.shape)]
-        + [whole(rank, cols)] * away,
+        + [whole(*one.shape) for one in ups],
         row_block(cols), [pltpu.VMEM((n_dp * rank, cols), BF16)], grid=(TILES,), flops=GRAD_COST,
     )(table, w, x, u_wide, up, *ups)
 
     summed = call(
         site_kernel, "sites", shape(sites, rank, feat), [VMEM, ANY] + [VMEM] * n_dp, VMEM,
-    )(picks, up_back[0], *down_back)
-    both = [summed] + [shift(summed, "pair", q) for q in range(1, n_pair)]
+    )(picks, y_own, *down_back)
+    both = [summed] + [shift(after(summed, *up_back[1:away]), "pair", q) for q in range(1, n_pair)]
     up_all = [shift(after(one, y_own), "pair", q) if q else one for q in range(n_pair) for one in up_back]
     rows = tok // sites
     of_site = lambda width: pl.BlockSpec((1, rank, width), lambda i: (i, 0, 0))
@@ -298,7 +318,7 @@
     down_grad, up_grad, y = call(
         functools.partial(last_kernel, n_pair, n_pair * n_dp, n_mp), "last",
         [shape(sites, rank, feat, dtype=F32), shape(sites, rank, cols, dtype=F32), shape(tok, cols)],
-        [whole(*picks.shape)] + [of_site(feat)] * n_pair + [whole(rank, cols)] * (n_pair * n_dp) + [out_rows] * n_mp,
+        [whole(*picks.shape)] + [of_site(feat)] * n_pair + [whole(*one.shape) for one in up_all] + [out_rows] * n_mp,
         [of_site(feat), of_site(cols), out_rows], grid=(sites,),
     )(picks, *both, *up_all, y_own, *y_got)
     return y, back, down_grad.transpose(0, 2, 1), up_grad

time: 60 us -> 63.1 us (1.052)
  waiting for transfers between devices: 15.2 us -> 23.5 us
  starting transfers between devices: 26.2 us -> 20.9 us
    ppermute x12 -> x10, waiting for transfers between devices: 8.81 us -> 17.7 us  [swap(): lax.ppermute(value, axis, [(i, i ^ mask) for i in range(lax.axis_size(axi...]
    ppermute x12 -> x10, starting transfers between devices: 18.1 us -> 12.3 us  [swap(): lax.ppermute(value, axis, [(i, i ^ mask) for i in range(lax.axis_size(axi...]
  transfers between devices with their start and end apart: 23 -> 21, of which waited for: 9 -> 7; matrix products, arithmetic and copies ran while one was open for 0% -> 0% of each run, Pallas kernels for 22% -> 21%
where the time goes in v12:
time: 63.1 us; the launch traced here: 62.9 us
  waiting for transfers between devices  23.5 us (37%)
  starting transfers between devices  20.9 us (33%)
  Pallas kernels  17.6 us (28%)
  between operations  0.83 us (1%)
    ppermute x10, waiting for transfers between devices, swap(): lax.ppermute(value, axis, [(i, i ^ mask) for i in range(lax.axis_size(axi...  17.7 us
    ppermute x10, starting transfers between devices, swap(): lax.ppermute(value, axis, [(i, i ^ mask) for i in range(lax.axis_size(axi...  12.3 us
    ppermute x11, starting transfers between devices, shift(): lax.ppermute(value, axis, [(i, (i + by) % size) for i in range(size)])  8.53 us
    ppermute x11, waiting for transfers between devices, shift(): lax.ppermute(value, axis, [(i, (i + by) % size) for i in range(size)])  5.8 us
    pallas_call x1, Pallas kernels, shards(): call(functools.partial(back_kernel, n_dp, n_mp), 'back', [shape(tok, feat...  4.1 us
    pallas_call x1, Pallas kernels, shards(): call(functools.partial(pack_kernel, n_dp, n_mp, n_pair), 'pack', [shape(r...  3.22 us
    pallas_call x2, Pallas kernels, gradient(): call(functools.partial(grad_kernel, n_dp, n_mp, len(behind)), name + '_gr...  2.45 us
    pallas_call x2, Pallas kernels, low_rank(): call(functools.partial(reduce_kernel, n_dp, tail), name + '_part', shape(...  2.42 us
  transfers between devices with their start and end apart: 21, of which 7 were waited for; matrix products, arithmetic and copies ran while one was open for 0% of the time, Pallas kernels for 21%

profile of v12, /device:TPU:0, one launch (start us, length us, event | category | flops | bytes accessed | tf_op | source)
XLA Modules:
  0.0 62.9 jit_solution(1009286917845903439)
XLA Ops:
  0.7 3.2 %pack.1 = (bf16[64,512]{1,0:T(8,128)(2,1)}, bf16[64,512]{1,0:T(8,128)(2,1)}, bf16[64,1024]{1,0:T(8,128)(2,1)}, bf16[64,1024]{1,0:T(8,128)(2,1)}, bf16[64,1536]{1,0:T(8,128)(2,1)}, /*index=5*/bf16[512,512]{1,0:T(8,128)(2,1)}) custom-call(s32[1,2,4]{2,1,0:T(2,128)} %table.9, bf16[2,64,1024]{2,1,0:T(8,128)(2,1)} %bitcast.2, bf16[2,64,512]{2,1,0:T(8,128)(2,1)} %own_up.1, ...), custom_call_target="tpu_custom_call" | custom-call | flops 1 | bytes 1 | tf_op jit(solution)/shard_map/pack/pallas_call | solution.py:245
  3.9 3.0 %collective-permute-start = (bf16[512,512]{1,0:T(8,128)(2,1)}, bf16[512,512]{1,0:T(8,128)(2,1)S(1)}, u32[]{:S(2)}, u32[]{:S(2)}) collective-permute-start(bf16[512,512]{1,0:T(8,128)(2,1)} %get-tuple-element.36), channel_id=1, source_target_pairs={{0,2},{2,0},{1,3},{3,1},{4,6},{6,4},{5,7},{7,5},{8,10},{10,8},{9,1... | collective-permute-start | bytes 1572872 | tf_op jit(solution)/shard_map/ppermute | solution.py:35
  6.9 1.6 %collective-permute-start.4 = (bf16[64,1536]{1,0:T(8,128)(2,1)}, bf16[64,1536]{1,0:T(8,128)(2,1)S(1)}, u32[]{:S(2)}, u32[]{:S(2)}) collective-permute-start(bf16[64,1536]{1,0:T(8,128)(2,1)} %get-tuple-element.40), channel_id=1, source_target_pairs={{0,4},{4,0},{8,12},{12,8},{1,5},{5,1},{9,13},{13,9},{2,6},{6,2},{1... | collective-permute-start | bytes 589832 | tf_op jit(solution)/shard_map/ppermute | solution.py:39
  8.5 2.5 %collective-permute-start.2 = (bf16[64,512]{1,0:T(8,128)(2,1)}, bf16[64,512]{1,0:T(8,128)(2,1)S(1)}, u32[]{:S(2)}, u32[]{:S(2)}) collective-permute-start(bf16[64,512]{1,0:T(8,128)(2,1)} %get-tuple-element.38), channel_id=1, source_target_pairs={{0,12},{4,8},{8,4},{12,0},{1,13},{5,9},{9,5},{13,1},{2,14},{6,10},... | collective-permute-start | bytes 196616 | tf_op jit(solution)/shard_map/ppermute | solution.py:39
  11.0 0.1 collective-permute-start.3
  11.1 6.6 %collective-permute-done.2._.refs_0_ = bf16[64,512]{1,0:T(8,128)(2,1)S(1)} collective-permute-done((bf16[64,512]{1,0:T(8,128)(2,1)}, bf16[64,512]{1,0:T(8,128)(2,1)S(1)}, u32[]{:S(2)}, u32[]{:S(2)}) %collective-permute-start.2) | collective-permute-done | bytes 65568 | tf_op jit(solution)/shard_map/ppermute | solution.py:39
  17.7 1.4 %collective-permute-start.5 = (bf16[64,1024]{1,0:T(8,128)(2,1)}, bf16[64,1024]{1,0:T(8,128)(2,1)S(1)}, u32[]{:S(2)}, u32[]{:S(2)}) collective-permute-start(bf16[64,1024]{1,0:T(8,128)(2,1)} %get-tuple-element.42), channel_id=1, source_target_pairs={{0,12},{4,8},{8,4},{12,0},{1,13},{5,9},{9,5},{13,1},{2,14},{6,10},... | collective-permute-start | bytes 393224 | tf_op jit(solution)/shard_map/ppermute | solution.py:39
  19.2 1.1 %h_part.1.near.refs_3_ = bf16[384,128]{1,0:T(8,128)(2,1)S(1)} custom-call(s32[12]{0:T(128)S(1)} %copy-done.6, s32[1,2,4]{2,1,0:T(2,128)S(1)} %copy-done.5, bf16[768,512]{1,0:T(8,128)(2,1)S(1)} %copy-done.2, bf16[64,512]{1,0:T(8,128)(2,1)S(1)} %collective-permute-done.2._.refs_0_, bf16[2,64,512]{2,1,0:T(8,128)(2,1)S(1)} %copy-done.4, ...), custom_call_target="tpu_custom_call" | custom-call | flops 1 | bytes 1 | tf_op jit(solution)/shard_map/h_part/pallas_call | solution.py:257
  20.3 0.6 collective-permute-start.7
  20.9 1.5 %collective-permute-start.1 = (bf16[768,512]{1,0:T(8,128)(2,1)S(1)}, bf16[768,512]{1,0:T(8,128)(2,1)S(1)}, u32[]{:S(2)}, u32[]{:S(2)}) collective-permute-start(bf16[768,512]{1,0:T(8,128)(2,1)S(1)} %copy-done.2), channel_id=1, source_target_pairs={{0,2},{2,0},{1,3},{3,1},{4,6},{6,4},{5,7},{7,5},{8,10},{10,8},{9,1... | collective-permute-start | bytes 2359304 | tf_op jit(solution)/shard_map/ppermute | solution.py:35
  22.4 2.4 %collective-permute-done.5.refs_0_.refs_6_ = bf16[64,1024]{1,0:T(8,128)(2,1)S(1)} collective-permute-done((bf16[64,1024]{1,0:T(8,128)(2,1)}, bf16[64,1024]{1,0:T(8,128)(2,1)S(1)}, u32[]{:S(2)}, u32[]{:S(2)}) %collective-permute-start.5) | collective-permute-done | bytes 131104 | tf_op jit(solution)/shard_map/ppermute | solution.py:39
  24.8 4.5 %collective-permute-done.6.refs_1_.refs_7_ = bf16[64,1024]{1,0:T(8,128)(2,1)S(1)} collective-permute-done((bf16[64,1024]{1,0:T(8,128)(2,1)}, bf16[64,1024]{1,0:T(8,128)(2,1)S(1)}, u32[]{:S(2)}, u32[]{:S(2)}) %collective-permute-start.6) | collective-permute-done | bytes 131104 | tf_op jit(solution)/shard_map/ppermute | solution.py:39
  29.3 1.3 %down_grad.1 = (bf16[64,1024]{1,0:T(8,128)(2,1)S(1)}, bf16[64,1024]{1,0:T(8,128)(2,1)S(1)}, bf16[64,1024]{1,0:T(8,128)(2,1)S(1)}, bf16[64,1024]{1,0:T(8,128)(2,1)S(1)}, bf16[768,256]{1,0:T(8,128)(2,1)S(1)}) custom-call(s32[12]{0:T(128)S(1)} %copy-done.6, bf16[768,1024]{1,0:T(8,128)(2,1)S(1)} %copy-done.1, bf16[384,128]{1,0:T(8,128)(2,1)S(1)} %h_part.1.near.refs_3_, ...), custom_call_target="tpu_custom_call" | custom-call | flops 15000000512 | bytes 1 | tf_op jit(solution)/shard_map/down_grad/pallas_call | solution.py:265
  30.7 1.9 %collective-permute-start.9 = (bf16[64,1024]{1,0:T(8,128)(2,1)S(1)}, bf16[64,1024]{1,0:T(8,128)(2,1)S(1)}, u32[]{:S(2)}, u32[]{:S(2)}) collective-permute-start(bf16[64,1024]{1,0:T(8,128)(2,1)S(1)} %get-tuple-element.50), channel_id=1, source_target_pairs={{0,12},{4,8},{8,4},{12,0},{1,13},{5,9},{9,5},{13,1},{2,14},{6,10},... | collective-permute-start | bytes 393224 | tf_op jit(solution)/shard_map/ppermute | solution.py:39
  32.7 1.3 %u_part.1._.refs_4_ = bf16[384,128]{1,0:T(8,128)(2,1)S(1)} custom-call(s32[12]{0:T(128)S(1)} %copy-done.6, s32[1,2,4]{2,1,0:T(2,128)S(1)} %copy-done.5, bf16[768,1024]{1,0:T(8,128)(2,1)S(1)} %copy-done.1, bf16[768,256]{1,0:T(8,128)(2,1)S(1)} %get-tuple-element.45._.refs_4_, bf16[2,64,1024]{2,1,0:T(8,128)(2,1)S(1)} %bitcast.3, ...), custom_call_target="tpu_custom_call" | custom-call | flops 1 | bytes 1 | tf_op jit(solution)/shard_map/u_part/pallas_call | solution.py:257
  34.0 0.6 collective-permute-start.11
  34.6 1.4 %y_send.1 = (bf16[768,512]{1,0:T(8,128)(2,1)S(1)}, bf16[1024,512]{1,0:T(8,128)(2,1)S(1)}) custom-call(bf16[384,128]{1,0:T(8,128)(2,1)S(1)} %u_part.1._.refs_4_, bf16[768,1024]{1,0:T(8,128)(2,1)S(1)} %copy-done.1, bf16[512,512]{1,0:T(8,128)(2,1)S(1)} %collective-permute-done.refs_0_, bf16[512,512]{1,0:T(8,128)(2,1)S(1)} %collective-permute-done.8.refs_1_), custom_call_target="tpu_custom_call" | custom-call | flops 1 | bytes 1 | tf_op jit(solution)/shard_map/y_send/pallas_call | solution.py:280
  36.0 1.6 %collective-permute-start.20 = (bf16[768,512]{1,0:T(8,128)(2,1)S(1)}, bf16[768,512]{1,0:T(8,128)(2,1)S(1)}, u32[]{:S(2)}, u32[]{:S(2)}) collective-permute-start(bf16[768,512]{1,0:T(8,128)(2,1)S(1)} %get-tuple-element.63), channel_id=1, source_target_pairs={{0,2},{2,0},{1,3},{3,1},{4,6},{6,4},{5,7},{7,5},{8,10},{10,8},{9,1... | collective-permute-start | bytes 2359304 | tf_op jit(solution)/shard_map/ppermute | solution.py:35
  37.6 3.8 %collective-permute-done.1.refs_2_.refs_3_ = bf16[768,512]{1,0:T(8,128)(2,1)S(1)} collective-permute-done((bf16[768,512]{1,0:T(8,128)(2,1)S(1)}, bf16[768,512]{1,0:T(8,128)(2,1)S(1)}, u32[]{:S(2)}, u32[]{:S(2)}) %collective-permute-start.1) | collective-permute-done | bytes 786464 | tf_op jit(solution)/shard_map/ppermute | solution.py:35
  41.4 4.1 %back.1 = (bf16[768,1024]{1,0:T(8,128)(2,1)}, s32[8,128]{1,0:T(8,128)S(1)}) custom-call(s32[1,2,4]{2,1,0:T(2,128)S(1)} %copy-done.5, bf16[2048,512]{1,0:T(8,128)(2,1)S(1)} %copy-done, bf16[768,512]{1,0:T(8,128)(2,1)S(1)} %copy-done.2, bf16[768,512]{1,0:T(8,128)(2,1)S(1)} %collective-permute-done.1.refs_2_.refs_3_, ...), custom_call_target="tpu_custom_call" | custom-call | flops 1 | bytes 1 | tf_op jit(solution)/shard_map/back/pallas_call | solution.py:289
  45.5 1.1 %up_grad.1 = (bf16[64,512]{1,0:T(8,128)(2,1)S(1)}, bf16[64,512]{1,0:T(8,128)(2,1)S(1)}, bf16[64,512]{1,0:T(8,128)(2,1)S(1)}, bf16[64,1536]{1,0:T(8,128)(2,1)S(1)}, bf16[768,256]{1,0:T(8,128)(2,1)S(1)}) custom-call(s32[12]{0:T(128)S(1)} %copy-done.6, bf16[768,512]{1,0:T(8,128)(2,1)S(1)} %copy-done.2, bf16[64,1024]{1,0:T(8,128)(2,1)S(1)} %get-tuple-element.49.near, ...), custom_call_target="tpu_custom_call" | custom-call | flops 15000000512 | bytes 1 | tf_op jit(solution)/shard_map/up_grad/pallas_call | solution.py:265
  46.6 4.1 %collective-permute-start.13 = (bf16[64,512]{1,0:T(8,128)(2,1)S(1)}, bf16[64,512]{1,0:T(8,128)(2,1)S(1)}, u32[]{:S(2)}, u32[]{:S(2)}) collective-permute-start(bf16[64,512]{1,0:T(8,128)(2,1)S(1)} %get-tuple-element.55), channel_id=1, source_target_pairs={{0,12},{4,8},{8,4},{12,0},{1,13},{5,9},{9,5},{13,1},{2,14},{6,10},... | collective-permute-start | bytes 196616 | tf_op jit(solution)/shard_map/ppermute | solution.py:39
  50.7 0.7 %collective-permute-start.14 = (bf16[64,512]{1,0:T(8,128)(2,1)S(1)}, bf16[64,512]{1,0:T(8,128)(2,1)S(1)}, u32[]{:S(2)}, u32[]{:S(2)}) collective-permute-start(bf16[64,512]{1,0:T(8,128)(2,1)S(1)} %get-tuple-element.56), channel_id=1, source_target_pairs={{0,8},{4,12},{8,0},{12,4},{1,9},{5,13},{9,1},{13,5},{2,10},{6,14},... | collective-permute-start | bytes 196616 | tf_op jit(solution)/shard_map/ppermute | solution.py:39
  51.4 2.2 %y_own.1._.refs_10_ = f32[768,512]{1,0:T(8,128)S(1)} custom-call(s32[1,2,4]{2,1,0:T(2,128)S(1)} %copy-done.5, bf16[2048,512]{1,0:T(8,128)(2,1)S(1)} %copy-done, bf16[768,1024]{1,0:T(8,128)(2,1)S(1)} %copy-done.1, bf16[768,256]{1,0:T(8,128)(2,1)S(1)} %get-tuple-element.52.wide, bf16[2,64,512]{2,1,0:T(8,128)(2,1)S(1)} %copy-done.4, ...), custom_call_target="tpu_custom_call" | custom-call | flops 15000000512 | bytes 1 | tf_op jit(solution)/shard_map/y_own/pallas_call | solution.py:303
  53.6 4.2 %collective-permute-done.12.refs_3_.refs_5_ = bf16[64,1536]{1,0:T(8,128)(2,1)S(1)} collective-permute-done((bf16[64,1536]{1,0:T(8,128)(2,1)S(1)}, bf16[64,1536]{1,0:T(8,128)(2,1)S(1)}, u32[]{:S(2)}, u32[]{:S(2)}) %collective-permute-start.12) | collective-permute-done | bytes 196640 | tf_op jit(solution)/shard_map/ppermute | solution.py:39
  57.8 0.3 sites.1.refs_0_
  58.2 0.5 collective-permute-start.19
  58.8 0.4 collective-permute-start.17
  59.3 0.9 %collective-permute-done.16.refs_6_ = bf16[64,512]{1,0:T(8,128)(2,1)S(1)} collective-permute-done((bf16[64,512]{1,0:T(8,128)(2,1)S(1)}, bf16[64,512]{1,0:T(8,128)(2,1)S(1)}, u32[]{:S(2)}, u32[]{:S(2)}) %collective-permute-start.16) | collective-permute-done | bytes 65568 | tf_op jit(solution)/shard_map/ppermute | solution.py:35
  60.1 0.1 collective-permute-start.18
  60.3 1.1 %collective-permute-done.18.refs_8_ = bf16[64,512]{1,0:T(8,128)(2,1)S(1)} collective-permute-done((bf16[64,512]{1,0:T(8,128)(2,1)S(1)}, bf16[64,512]{1,0:T(8,128)(2,1)S(1)}, u32[]{:S(2)}, u32[]{:S(2)}) %collective-permute-start.18) | collective-permute-done | bytes 65568 | tf_op jit(solution)/shard_map/ppermute | solution.py:35
  61.4 1.5 %last.1 = (f32[2,64,1024]{2,1,0:T(8,128)}, f32[2,64,512]{2,1,0:T(8,128)}, bf16[768,512]{1,0:T(8,128)(2,1)}) custom-call(s32[8,128]{1,0:T(8,128)S(1)} %get-tuple-element.48.refs_0_.picks, bf16[2,64,1024]{2,1,0:T(8,128)(2,1)S(1)} %sites.1.refs_0_, bf16[2,64,1024]{2,1,0:T(8,128)(2,1)S(1)} %collective-permute-done.15.refs_1_, ...), custom_call_target="tpu_custom_call" | custom-call | flops 1 | bytes 1 | tf_op jit(solution)/shard_map/last/pallas_call | solution.py:318
  (34 shorter events, 0.3 us)
Async XLA Ops:
  0.6 18.5 %copy-start.5 = (s32[1,2,4]{2,1,0:T(2,128)S(1)}, s32[1,2,4]{2,1,0:T(2,128)}, u32[]{:S(2)}) copy-start(s32[1,2,4]{2,1,0:T(2,128)} %table.9) | copy-start | bytes 100
  0.6 18.5 %copy-start.4 = (bf16[2,64,512]{2,1,0:T(8,128)(2,1)S(1)}, bf16[2,64,512]{2,1,0:T(8,128)(2,1)}, u32[]{:S(2)}) copy-start(bf16[2,64,512]{2,1,0:T(8,128)(2,1)} %own_up.1) | copy-start | bytes 393220
  0.7 18.5 %copy-start.6 = (s32[12]{0:T(128)S(1)}, s32[12]{0:T(128)}, u32[]{:S(2)}) copy-start(s32[12]{0:T(128)} %owner.7) | copy-start | bytes 148
  0.7 18.5 %copy-start.2 = (bf16[768,512]{1,0:T(8,128)(2,1)S(1)}, bf16[768,512]{1,0:T(8,128)(2,1)}, u32[]{:S(2)}) copy-start(bf16[768,512]{1,0:T(8,128)(2,1)} %act.7) | copy-start | bytes 2359300
  0.7 28.6 %copy-start.1 = (bf16[768,1024]{1,0:T(8,128)(2,1)S(1)}, bf16[768,1024]{1,0:T(8,128)(2,1)}, u32[]{:S(2)}) copy-start(bf16[768,1024]{1,0:T(8,128)(2,1)} %x.3) | copy-start | bytes 4718596
  3.9 17.0 %collective-permute-start = (bf16[512,512]{1,0:T(8,128)(2,1)}, bf16[512,512]{1,0:T(8,128)(2,1)S(1)}, u32[]{:S(2)}, u32[]{:S(2)}) collective-permute-start(bf16[512,512]{1,0:T(8,128)(2,1)} %get-tuple-element.36), channel_id=1, source_target_pairs={{0,2},{2,0},{1,3},{3,1},{4,6},{6,4},{5,7},{7,5},{8,10},{10,8},{9,1... | collective-permute-start | bytes 1572872 | tf_op jit(solution)/shard_map/ppermute | solution.py:35
  6.9 12.2 %collective-permute-start.4 = (bf16[64,1536]{1,0:T(8,128)(2,1)}, bf16[64,1536]{1,0:T(8,128)(2,1)S(1)}, u32[]{:S(2)}, u32[]{:S(2)}) collective-permute-start(bf16[64,1536]{1,0:T(8,128)(2,1)} %get-tuple-element.40), channel_id=1, source_target_pairs={{0,4},{4,0},{8,12},{12,8},{1,5},{5,1},{9,13},{13,9},{2,6},{6,2},{1... | collective-permute-start | bytes 589832 | tf_op jit(solution)/shard_map/ppermute | solution.py:39
  8.5 9.2 %collective-permute-start.2 = (bf16[64,512]{1,0:T(8,128)(2,1)}, bf16[64,512]{1,0:T(8,128)(2,1)S(1)}, u32[]{:S(2)}, u32[]{:S(2)}) collective-permute-start(bf16[64,512]{1,0:T(8,128)(2,1)} %get-tuple-element.38), channel_id=1, source_target_pairs={{0,12},{4,8},{8,4},{12,0},{1,13},{5,9},{9,5},{13,1},{2,14},{6,10},... | collective-permute-start | bytes 196616 | tf_op jit(solution)/shard_map/ppermute | solution.py:39
  11.0 8.2 %collective-permute-start.3 = (bf16[64,512]{1,0:T(8,128)(2,1)}, bf16[64,512]{1,0:T(8,128)(2,1)S(1)}, u32[]{:S(2)}, u32[]{:S(2)}) collective-permute-start(bf16[64,512]{1,0:T(8,128)(2,1)} %get-tuple-element.39), channel_id=1, source_target_pairs={{0,8},{4,12},{8,0},{12,4},{1,9},{5,13},{9,1},{13,5},{2,10},{6,14},... | collective-permute-start | bytes 196616 | tf_op jit(solution)/shard_map/ppermute | solution.py:39
  17.7 7.1 %collective-permute-start.5 = (bf16[64,1024]{1,0:T(8,128)(2,1)}, bf16[64,1024]{1,0:T(8,128)(2,1)S(1)}, u32[]{:S(2)}, u32[]{:S(2)}) collective-permute-start(bf16[64,1024]{1,0:T(8,128)(2,1)} %get-tuple-element.42), channel_id=1, source_target_pairs={{0,12},{4,8},{8,4},{12,0},{1,13},{5,9},{9,5},{13,1},{2,14},{6,10},... | collective-permute-start | bytes 393224 | tf_op jit(solution)/shard_map/ppermute | solution.py:39
  19.1 10.2 %collective-permute-start.6 = (bf16[64,1024]{1,0:T(8,128)(2,1)}, bf16[64,1024]{1,0:T(8,128)(2,1)S(1)}, u32[]{:S(2)}, u32[]{:S(2)}) collective-permute-start(bf16[64,1024]{1,0:T(8,128)(2,1)} %get-tuple-element.44), channel_id=1, source_target_pairs={{0,8},{4,12},{8,0},{12,4},{1,9},{5,13},{9,1},{13,5},{2,10},{6,14},... | collective-permute-start | bytes 393224 | tf_op jit(solution)/shard_map/ppermute | solution.py:39
  20.3 12.4 %copy-start.3 = (bf16[2,1024,64]{1,2,0:T(8,128)(2,1)S(1)}, bf16[2,1024,64]{1,2,0:T(8,128)(2,1)}, u32[]{:S(2)}) copy-start(bf16[2,1024,64]{1,2,0:T(8,128)(2,1)} %param.9) | copy-start | bytes 786436
  20.3 9.0 %collective-permute-start.7 = (bf16[384,128]{1,0:T(8,128)(2,1)S(1)}, bf16[384,128]{1,0:T(8,128)(2,1)S(1)}, u32[]{:S(2)}, u32[]{:S(2)}) collective-permute-start(bf16[384,128]{1,0:T(8,128)(2,1)S(1)} %h_part.1.near.refs_3_), channel_id=1, source_target_pairs={{0,2},{2,0},{1,3},{3,1},{4,6},{6,4},{5,7},{7,5},{8,10},{10,8},{9,1... | collective-permute-start | bytes 294920 | tf_op jit(solution)/shard_map/ppermute | solution.py:35
  20.9 20.5 %collective-permute-start.1 = (bf16[768,512]{1,0:T(8,128)(2,1)S(1)}, bf16[768,512]{1,0:T(8,128)(2,1)S(1)}, u32[]{:S(2)}, u32[]{:S(2)}) collective-permute-start(bf16[768,512]{1,0:T(8,128)(2,1)S(1)} %copy-done.2), channel_id=1, source_target_pairs={{0,2},{2,0},{1,3},{3,1},{4,6},{6,4},{5,7},{7,5},{8,10},{10,8},{9,1... | collective-permute-start | bytes 2359304 | tf_op jit(solution)/shard_map/ppermute | solution.py:35
  30.6 4.0 %collective-permute-start.8 = (bf16[512,512]{1,0:T(8,128)(2,1)S(1)}, bf16[512,512]{1,0:T(8,128)(2,1)S(1)}, u32[]{:S(2)}, u32[]{:S(2)}) collective-permute-start(bf16[512,512]{1,0:T(8,128)(2,1)S(1)} %collective-permute-done.refs_0_), channel_id=1, source_target_pairs={{0,1},{1,0},{2,3},{3,2},{4,5},{5,4},{6,7},{7,6},{8,9},{9,8},{10,11... | collective-permute-start | bytes 1572872 | tf_op jit(solution)/shard_map/ppermute | solution.py:35
  30.7 14.8 %collective-permute-start.9 = (bf16[64,1024]{1,0:T(8,128)(2,1)S(1)}, bf16[64,1024]{1,0:T(8,128)(2,1)S(1)}, u32[]{:S(2)}, u32[]{:S(2)}) collective-permute-start(bf16[64,1024]{1,0:T(8,128)(2,1)S(1)} %get-tuple-element.50), channel_id=1, source_target_pairs={{0,12},{4,8},{8,4},{12,0},{1,13},{5,9},{9,5},{13,1},{2,14},{6,10},... | collective-permute-start | bytes 393224 | tf_op jit(solution)/shard_map/ppermute | solution.py:39
  32.7 12.8 %collective-permute-start.10 = (bf16[64,1024]{1,0:T(8,128)(2,1)S(1)}, bf16[64,1024]{1,0:T(8,128)(2,1)S(1)}, u32[]{:S(2)}, u32[]{:S(2)}) collective-permute-start(bf16[64,1024]{1,0:T(8,128)(2,1)S(1)} %get-tuple-element.51), channel_id=1, source_target_pairs={{0,8},{4,12},{8,0},{12,4},{1,9},{5,13},{9,1},{13,5},{2,10},{6,14},... | collective-permute-start | bytes 393224 | tf_op jit(solution)/shard_map/ppermute | solution.py:39
  34.0 7.4 %copy-start = (bf16[2048,512]{1,0:T(8,128)(2,1)S(1)}, bf16[2048,512]{1,0:T(8,128)(2,1)}, u32[]{:S(2)}) copy-start(bf16[2048,512]{1,0:T(8,128)(2,1)} %w.3) | copy-start | bytes 6291460
  34.0 11.5 %collective-permute-start.11 = (bf16[384,128]{1,0:T(8,128)(2,1)S(1)}, bf16[384,128]{1,0:T(8,128)(2,1)S(1)}, u32[]{:S(2)}, u32[]{:S(2)}) collective-permute-start(bf16[384,128]{1,0:T(8,128)(2,1)S(1)} %u_part.1._.refs_4_), channel_id=1, source_target_pairs={{0,2},{2,0},{1,3},{3,1},{4,6},{6,4},{5,7},{7,5},{8,10},{10,8},{9,1... | collective-permute-start | bytes 294920 | tf_op jit(solution)/shard_map/ppermute | solution.py:35
  36.0 25.4 %collective-permute-start.20 = (bf16[768,512]{1,0:T(8,128)(2,1)S(1)}, bf16[768,512]{1,0:T(8,128)(2,1)S(1)}, u32[]{:S(2)}, u32[]{:S(2)}) collective-permute-start(bf16[768,512]{1,0:T(8,128)(2,1)S(1)} %get-tuple-element.63), channel_id=1, source_target_pairs={{0,2},{2,0},{1,3},{3,1},{4,6},{6,4},{5,7},{7,5},{8,10},{10,8},{9,1... | collective-permute-start | bytes 2359304 | tf_op jit(solution)/shard_map/ppermute | solution.py:35
  46.6 11.5 %collective-permute-start.13 = (bf16[64,512]{1,0:T(8,128)(2,1)S(1)}, bf16[64,512]{1,0:T(8,128)(2,1)S(1)}, u32[]{:S(2)}, u32[]{:S(2)}) collective-permute-start(bf16[64,512]{1,0:T(8,128)(2,1)S(1)} %get-tuple-element.55), channel_id=1, source_target_pairs={{0,12},{4,8},{8,4},{12,0},{1,13},{5,9},{9,5},{13,1},{2,14},{6,10},... | collective-permute-start | bytes 196616 | tf_op jit(solution)/shard_map/ppermute | solution.py:39
  50.7 7.5 %collective-permute-start.14 = (bf16[64,512]{1,0:T(8,128)(2,1)S(1)}, bf16[64,512]{1,0:T(8,128)(2,1)S(1)}, u32[]{:S(2)}, u32[]{:S(2)}) collective-permute-start(bf16[64,512]{1,0:T(8,128)(2,1)S(1)} %get-tuple-element.56), channel_id=1, source_target_pairs={{0,8},{4,12},{8,0},{12,4},{1,9},{5,13},{9,1},{13,5},{2,10},{6,14},... | collective-permute-start | bytes 196616 | tf_op jit(solution)/shard_map/ppermute | solution.py:39
  51.4 6.4 %collective-permute-start.12 = (bf16[64,1536]{1,0:T(8,128)(2,1)S(1)}, bf16[64,1536]{1,0:T(8,128)(2,1)S(1)}, u32[]{:S(2)}, u32[]{:S(2)}) collective-permute-start(bf16[64,1536]{1,0:T(8,128)(2,1)S(1)} %get-tuple-element.54), channel_id=1, source_target_pairs={{0,4},{4,0},{8,12},{12,8},{1,5},{5,1},{9,13},{13,9},{2,6},{6,2},{1... | collective-permute-start | bytes 589832 | tf_op jit(solution)/shard_map/ppermute | solution.py:39
  58.2 3.2 %collective-permute-start.15 = (bf16[2,64,1024]{2,1,0:T(8,128)(2,1)S(1)}, bf16[2,64,1024]{2,1,0:T(8,128)(2,1)S(1)}, u32[]{:S(2)}, u32[]{:S(2)}) collective-permute-start(bf16[2,64,1024]{2,1,0:T(8,128)(2,1)S(1)} %sites.1.refs_0_), channel_id=1, source_target_pairs={{0,1},{1,0},{2,3},{3,2},{4,5},{5,4},{6,7},{7,6},{8,9},{9,8},{10,11... | collective-permute-start | bytes 786440 | tf_op jit(solution)/shard_map/ppermute | solution.py:35
  58.2 3.2 %collective-permute-start.19 = (bf16[64,1536]{1,0:T(8,128)(2,1)S(1)}, bf16[64,1536]{1,0:T(8,128)(2,1)S(1)}, u32[]{:S(2)}, u32[]{:S(2)}) collective-permute-start(bf16[64,1536]{1,0:T(8,128)(2,1)S(1)} %collective-permute-done.12.refs_3_.refs_5_), channel_id=1, source_target_pairs={{0,1},{1,0},{2,3},{3,2},{4,5},{5,4},{6,7},{7,6},{8,9},{9,8},{10,11... | collective-permute-start | bytes 589832 | tf_op jit(solution)/shard_map/ppermute | solution.py:35
  58.7 1.4 %collective-permute-start.16 = (bf16[64,512]{1,0:T(8,128)(2,1)S(1)}, bf16[64,512]{1,0:T(8,128)(2,1)S(1)}, u32[]{:S(2)}, u32[]{:S(2)}) collective-permute-start(bf16[64,512]{1,0:T(8,128)(2,1)S(1)} %get-tuple-element.59.refs_2_), channel_id=1, source_target_pairs={{0,1},{1,0},{2,3},{3,2},{4,5},{5,4},{6,7},{7,6},{8,9},{9,8},{10,11... | collective-permute-start | bytes 196616 | tf_op jit(solution)/shard_map/ppermute | solution.py:35
  58.8 1.5 %collective-permute-start.17 = (bf16[64,512]{1,0:T(8,128)(2,1)S(1)}, bf16[64,512]{1,0:T(8,128)(2,1)S(1)}, u32[]{:S(2)}, u32[]{:S(2)}) collective-permute-start(bf16[64,512]{1,0:T(8,128)(2,1)S(1)} %collective-permute-done.13.refs_3_), channel_id=1, source_target_pairs={{0,1},{1,0},{2,3},{3,2},{4,5},{5,4},{6,7},{7,6},{8,9},{9,8},{10,11... | collective-permute-start | bytes 196616 | tf_op jit(solution)/shard_map/ppermute | solution.py:35
  60.1 1.3 %collective-permute-start.18 = (bf16[64,512]{1,0:T(8,128)(2,1)S(1)}, bf16[64,512]{1,0:T(8,128)(2,1)S(1)}, u32[]{:S(2)}, u32[]{:S(2)}) collective-permute-start(bf16[64,512]{1,0:T(8,128)(2,1)S(1)} %collective-permute-done.14.refs_4_), channel_id=1, source_target_pairs={{0,1},{1,0},{2,3},{3,2},{4,5},{5,4},{6,7},{7,6},{8,9},{9,8},{10,11... | collective-permute-start | bytes 196616 | tf_op jit(solution)/shard_map/ppermute | solution.py:35

commit v13 on v11

--- a/solution.py
+++ b/solution.py
@@ -72,19 +72,19 @@
     return lax.rem(n_dp - lax.bitwise_xor(lax.axis_index("dp"), owner[b]), n_dp)
 
 
-def pack_kernel(n_dp, n_mp, n_pair, table, down, up, w, *refs):
+def pack_kernel(n_dp, n_mp, n_share, table, down, up, w, *refs):
     away = n_dp - 1
     ups, downs, pieces, sem = refs[:away], refs[away:2 * away], refs[2 * away:-1], refs[-1]
     feat = w.shape[0] // n_mp
-    part = feat // n_pair
+    part = feat // n_share
+    place = lax.axis_index("groups") * lax.axis_size("pair") + lax.axis_index("pair")
     copies = []
     for s in range(away):
         site = wanted_site(table, n_dp, s + 1)
         copies.append(pltpu.make_async_copy(up.at[site], ups[s], sem.at[s]))
         copies.append(pltpu.make_async_copy(down.at[site], downs[s], sem.at[away + s]))
     for s in range(1, n_mp):
-        row = lax.rem(lax.axis_index("mp") + s, n_mp) * feat + lax.axis_index("pair") * part
-        row = pl.multiple_of(row, part)
+        row = pl.multiple_of(lax.rem(lax.axis_index("mp") + s, n_mp) * feat + place * part, part)
         copies.append(pltpu.make_async_copy(w.at[pl.ds(row, part)], pieces[s - 1], sem.at[2 * away + s - 1]))
     run(copies)
 
@@ -97,10 +97,12 @@
 
 
 def reduce_kernel(n_dp, owner, table, act, _, own, *refs):
-    gots, out, wide = refs[:n_dp - 1], refs[n_dp - 1], refs[n_dp]
+    gots, out, again, wide = refs[:n_dp - 1], refs[n_dp - 1], refs[n_dp:-1], refs[-1]
     rank = own.shape[1]
     blocks = owner.shape[0]
     rows = act.shape[0] // blocks
+    for late in again:
+        late[...] = act[act.shape[0] - late.shape[0]:, :]
     gather_maps(n_dp, table, own, gots, wide)
     full = nt(act[...], wide[...])
     lane_slot = lax.broadcasted_iota(jnp.int32, (rows, n_dp * rank), 1) // rank
@@ -136,27 +138,28 @@
         grads[s][...] = full[s * rank:(s + 1) * rank].astype(BF16)
 
 
-def send_kernel(n_pair, feat, n_mp, _, __, x, *refs):
-    n_other = n_mp - 1
-    pieces, outs, rows = refs[:n_other * n_pair], refs[n_other * n_pair:n_other * n_pair + n_other], refs[-n_other:]
-    part = feat // n_pair
+def send_kernel(n_groups, n_pair, feat, n_mp, _, x, *refs):
+    n_other, n_share = n_mp - 1, n_groups * n_pair
+    pieces, outs, rows = refs[:n_other * n_share], refs[-2 * n_other:-n_other], refs[-n_other:]
+    part = feat // n_share
 
     @pl.when(pl.program_id(0) == 0)
     def _():
         for s in range(n_other):
-            for q in range(n_pair):
-                at = lax.rem(lax.axis_index("pair") + n_pair - q, n_pair) * part
-                rows[s][pl.ds(pl.multiple_of(at, part), part), :] = pieces[s * n_pair + q][...]
+            for k in range(n_share):
+                group = lax.rem(lax.axis_index("groups") + n_groups - k // n_pair, n_groups)
+                core = lax.rem(lax.axis_index("pair") + n_pair - k % n_pair, n_pair)
+                at = pl.multiple_of((group * n_pair + core) * part, part)
+                rows[s][pl.ds(at, part), :] = pieces[s * n_share + k][...]
 
     for s in range(n_other):
         outs[s][...] = nn(x[...], rows[s][...]).astype(BF16)
 
 
-def back_kernel(n_dp, n_mp, table, *refs):
-    w, gys, rows, wide, own_down, downs, out, picks, own, maps = (
-        refs[0], refs[1:1 + n_mp], refs[1 + n_mp:2 * n_mp], refs[2 * n_mp], refs[2 * n_mp + 1],
-        refs[2 * n_mp + 2:-4], refs[-4], refs[-3], refs[-2], refs[-1],
-    )
+def back_kernel(n_dp, n_mp, table, w, gy, wide, own_down, *refs):
+    n_other = n_mp - 1
+    early, late, rows = refs[:n_other], refs[n_other:2 * n_other], refs[2 * n_other:3 * n_other]
+    downs, out, picks, own, maps = refs[3 * n_other:-4], refs[-4], refs[-3], refs[-2], refs[-1]
     feat = out.shape[1]
 
     @pl.when(pl.program_id(0) == 0)
@@ -169,9 +172,10 @@
         own[...] = w[pl.ds(pl.multiple_of(lax.axis_index("mp") * feat, feat), feat), :]
         gather_maps(n_dp, table, own_down, downs, maps)
 
-    total = nt(gys[0][...], own[...]) + SCALE * nn(wide[...], maps[...])
-    for gy, row in zip(gys[1:], rows):
-        total = total + nt(gy[...], row[...])
+    total = nt(gy[...], own[...]) + SCALE * nn(wide[...], maps[...])
+    for first, second, row in zip(early, late, rows):
+        got = jnp.where(pl.program_id(0) == 0, first[...], second[...])
+        total = total + nt(got, row[...])
     out[...] = total.astype(BF16)
 
 
@@ -218,17 +222,18 @@
     tok, feat = x.shape
     cols = w.shape[1]
     sites, rank = up.shape[:2]
-    n_dp, n_mp, n_pair = (lax.axis_size(a) for a in ("dp", "mp", "pair"))
-    n_other = n_mp - 1
+    n_groups, n_dp, n_mp, n_pair = (lax.axis_size(a) for a in ("groups", "dp", "mp", "pair"))
+    n_other, n_share = n_mp - 1, n_groups * n_pair
     down = down.transpose(0, 2, 1)
-    part = feat // n_pair
+    part = feat // n_share
+    half = tok // 2
     tile = tok // TILES
     row_block = lambda width: pl.BlockSpec((tile, width), lambda i: (i, 0))
     whole = lambda *dims: pl.BlockSpec(dims, lambda i: (0,) * len(dims))
 
     away = n_dp - 1
     packed = call(
-        functools.partial(pack_kernel, n_dp, n_mp, n_pair), "pack",
+        functools.partial(pack_kernel, n_dp, n_mp, n_share), "pack",
         [shape(rank, cols)] * away + [shape(rank, feat)] * away + [shape(part, cols)] * n_other,
         [SMEM, ANY, ANY, ANY], [VMEM] * (2 * away + n_other),
         [pltpu.SemaphoreType.DMA((2 * away + n_other,))], mib=60,
@@ -237,13 +242,16 @@
     ups = [swap(packed[s - 1], "dp", n_dp - s) for s in range(1, n_dp)]
     downs = [swap(after(packed[away + s - 1], ups[0]), "dp", n_dp - s) for s in range(1, n_dp)]
 
-    def low_rank(act, own, maps, behind, name):
-        mine = call(
+    gy_early = [shift(after(gy[:half], packed[0]), "mp", s) for s in range(1, n_mp)]
+
+    def low_rank(act, own, maps, behind, again, name):
+        mine, *late = call(
             functools.partial(reduce_kernel, n_dp), name + "_part",
-            shape(tok // 2, 2 * rank), [SMEM, SMEM, VMEM, ANY] + [VMEM] * n_dp, VMEM,
+            [shape(tok // 2, 2 * rank)] + again,
+            [SMEM, SMEM, VMEM, ANY] + [VMEM] * n_dp, [VMEM] * (1 + len(again)),
             [pltpu.VMEM((n_dp * rank, act.shape[1]), BF16)],
         )(owner, table, act, behind, own, *maps)
-        return [mine] + [shift(mine, "mp", s) for s in range(1, n_mp)]
+        return [mine] + [shift(mine, "mp", s) for s in range(1, n_mp)], late
 
     def gradient(act, parts, behind, name, flops):
         *grads, wide = call(
@@ -253,32 +261,35 @@
         )(owner, act, *behind, *parts)
         return [grads[0]] + [swap(grads[s], "dp", n_dp - s) for s in range(1, n_dp)], wide
 
-    h_parts = low_rank(gy, up, ups, ups[0], "h")
-    gy_got = [shift(after(gy, *pieces), "mp", s) for s in range(1, n_mp)]
+    h_parts, late = low_rank(gy, up, ups, ups[0], [shape(tok - half, cols)], "h")
+    gy_late = [shift(after(late[0], *gy_early), "mp", s) for s in range(1, n_mp)]
     down_back, h_wide = gradient(x, h_parts, downs, "down", GRAD_COST)
-    u_parts = low_rank(x, down, downs, h_wide, "u")
+    u_parts, _ = low_rank(x, down, downs, h_wide, [], "u")
 
     parts = []
     for piece in pieces:
-        parts += [piece] + [shift(after(piece, h_wide), "pair", q) for q in range(1, n_pair)]
+        for j in range(n_groups):
+            one = shift(after(piece, h_parts[0]), "groups", j) if j else piece
+            parts += [shift(after(one, h_wide if j else h_parts[0]), "pair", q) if q else one for q in range(n_pair)]
     sent = call(
-        functools.partial(send_kernel, n_pair, feat, n_mp), "y_send",
+        functools.partial(send_kernel, n_groups, n_pair, feat, n_mp), "y_send",
         [shape(tok, cols)] * n_other + [shape(feat, cols)] * n_other,
-        [ANY, ANY, row_block(feat)] + [whole(part, cols)] * len(parts),
+        [ANY, row_block(feat)] + [whole(part, cols)] * len(parts),
         [row_block(cols)] * n_other + [whole(feat, cols)] * n_other,
         grid=(TILES,),
-    )(u_parts[0], down_back[1], x, *parts)
+    )(u_parts[0], x, *parts)
     w_rows = sent[n_other:]
     y_got = [shift(sent[s - 1], "mp", n_mp - s) for s in range(1, n_mp)]
+    half_rows = lambda width: pl.BlockSpec((half, width), lambda i: (i, 0))
     back, picks = call(
         functools.partial(back_kernel, n_dp, n_mp), "back",
         [shape(tok, feat), shape(-(-n_dp * n_pair // 8) * 8, 128, dtype=jnp.int32)],
-        [SMEM, whole(*w.shape)] + [row_block(cols)] * n_mp + [whole(feat, cols)] * n_other
-        + [row_block(n_dp * rank), whole(*down.shape)] + [whole(rank, feat)] * away,
-        [row_block(feat), whole(-(-n_dp * n_pair // 8) * 8, 128)],
-        [pltpu.VMEM((feat, cols), BF16), pltpu.VMEM((n_dp * rank, feat), BF16)], grid=(TILES,),
-    )(table, w, gy, *gy_got, *w_rows, h_wide, down, *downs)
-    up_back, u_wide = gradient(gy, u_parts, [picks] + down_back[2:] + gy_got, "up", GRAD_COST)
+        [SMEM, whole(*w.shape), half_rows(cols), half_rows(n_dp * rank), whole(*down.shape)]
+        + [whole(half, cols)] * (2 * n_other) + [whole(feat, cols)] * n_other + [whole(rank, feat)] * away,
+        [half_rows(feat), whole(-(-n_dp * n_pair // 8) * 8, 128)],
+        [pltpu.VMEM((feat, cols), BF16), pltpu.VMEM((n_dp * rank, feat), BF16)], grid=(2,),
+    )(table, w, gy, h_wide, down, *gy_early, *gy_late, *w_rows, *downs)
+    up_back, u_wide = gradient(gy, u_parts, [picks] + down_back[1:] + gy_late, "up", GRAD_COST)
 
     y_own = call(
         functools.partial(own_kernel, n_dp), "y_own", shape(tok, cols, dtype=F32),

time: 60 us -> 60.1 us (level)
  waiting for transfers between devices: 15.2 us -> 10.2 us
  starting transfers between devices: 26.2 us -> 30.6 us
  local copies, waits for them, and re-layouts: 0.03 us -> 1.13 us
    ppermute x11 -> x14, starting transfers between devices: 8.06 us -> 11.5 us  [shift(): lax.ppermute(value, axis, [(i, (i + by) % size) for i in range(size)])]
    ppermute x12, waiting for transfers between devices: 8.81 us -> 5.85 us  [swap(): lax.ppermute(value, axis, [(i, i ^ mask) for i in range(lax.axis_size(axi...]
    ppermute x11 -> x14, waiting for transfers between devices: 6.41 us -> 4.32 us  [shift(): lax.ppermute(value, axis, [(i, (i + by) % size) for i in range(size)])]
    slice x0 -> x1, local copies, waits for them, and re-layouts: none -> 1.1 us  [shards(): gy[:half]]
    ppermute x12, starting transfers between devices: 18.1 us -> 19.1 us  [swap(): lax.ppermute(value, axis, [(i, i ^ mask) for i in range(lax.axis_size(axi...]
  transfers between devices with their start and end apart: 23 -> 26, of which waited for: 9 -> 12; matrix products, arithmetic and copies ran while one was open for 0% -> 0% of each run, Pallas kernels for 22% -> 21%
where the time goes in v13:
time: 60.1 us; the launch traced here: 59.9 us
  starting transfers between devices  30.6 us (51%)
  Pallas kernels  17.3 us (29%)
  waiting for transfers between devices  10.2 us (17%)
  local copies, waits for them, and re-layouts  1.13 us (2%)
  between operations  0.79 us (1%)
    ppermute x12, starting transfers between devices, swap(): lax.ppermute(value, axis, [(i, i ^ mask) for i in range(lax.axis_size(axi...  19.1 us
    ppermute x14, starting transfers between devices, shift(): lax.ppermute(value, axis, [(i, (i + by) % size) for i in range(size)])  11.5 us
    ppermute x12, waiting for transfers between devices, swap(): lax.ppermute(value, axis, [(i, i ^ mask) for i in range(lax.axis_size(axi...  5.85 us
    ppermute x14, waiting for transfers between devices, shift(): lax.ppermute(value, axis, [(i, (i + by) % size) for i in range(size)])  4.32 us
    pallas_call x1, Pallas kernels, shards(): call(functools.partial(back_kernel, n_dp, n_mp), 'back', [shape(tok, feat...  3.96 us
    pallas_call x1, Pallas kernels, shards(): call(functools.partial(pack_kernel, n_dp, n_mp, n_share), 'pack', [shape(...  3.04 us
    pallas_call x2, Pallas kernels, gradient(): call(functools.partial(grad_kernel, n_dp, n_mp, len(behind)), name + '_gr...  2.45 us
    pallas_call x2, Pallas kernels, low_rank(): call(functools.partial(reduce_kernel, n_dp), name + '_part', [shape(tok /...  2.43 us
  transfers between devices with their start and end apart: 26, of which 12 were waited for; matrix products, arithmetic and copies ran while one was open for 0% of the time, Pallas kernels for 21%

profile of v13, /device:TPU:0, one launch (start us, length us, event | category | flops | bytes accessed | tf_op | source)
XLA Modules:
  0.0 59.9 jit_solution(12038653094119669339)
XLA Ops:
  0.7 1.1 %slice.3 = bf16[384,512]{1,0:T(8,128)(2,1)S(1)} slice(bf16[768,512]{1,0:T(8,128)(2,1)} %act.7), slice={[0:384], [0:512]} | slice | bytes 786432 | tf_op jit(solution)/shard_map/slice | solution.py:245
  1.8 3.0 %pack.1 = (bf16[64,512]{1,0:T(8,128)(2,1)}, bf16[64,512]{1,0:T(8,128)(2,1)}, bf16[64,512]{1,0:T(8,128)(2,1)}, bf16[64,1024]{1,0:T(8,128)(2,1)}, bf16[64,1024]{1,...) custom-call(s32[1,2,4]{2,1,0:T(2,128)} %table.9, bf16[2,64,1024]{2,1,0:T(8,128)(2,1)} %bitcast.2, ...), custom_call_target="tpu_custom_call" | custom-call | flops 1 | bytes 1 | tf_op jit(solution)/shard_map/pack/pallas_call | solution.py:235
  4.8 3.0 %collective-permute-start.7 = (bf16[384,512]{1,0:T(8,128)(2,1)S(1)}, bf16[384,512]{1,0:T(8,128)(2,1)S(1)}, u32[]{:S(2)}, u32[]{:S(2)}) collective-permute-start(bf16[384,512]{1,0:T(8,128)(2,1)S(1)} %slice.3), channel_id=1, source_target_pairs={{0,2},{2,0},{1,3},{3,1},{4,6},{6,4},{5,7},{7,5},{8,10},{10,8},{9,1... | collective-permute-start | bytes 1179656 | tf_op jit(solution)/shard_map/ppermute | solution.py:35
  7.9 4.1 %collective-permute-start = (bf16[64,512]{1,0:T(8,128)(2,1)}, bf16[64,512]{1,0:T(8,128)(2,1)S(1)}, u32[]{:S(2)}, u32[]{:S(2)}) collective-permute-start(bf16[64,512]{1,0:T(8,128)(2,1)} %get-tuple-element.42), channel_id=1, source_target_pairs={{0,12},{4,8},{8,4},{12,0},{1,13},{5,9},{9,5},{13,1},{2,14},{6,10},... | collective-permute-start | bytes 196616 | tf_op jit(solution)/shard_map/ppermute | solution.py:39
  12.0 0.6 collective-permute-start.5
  12.5 2.6 %collective-permute-done._.refs_0_ = bf16[64,512]{1,0:T(8,128)(2,1)S(1)} collective-permute-done((bf16[64,512]{1,0:T(8,128)(2,1)}, bf16[64,512]{1,0:T(8,128)(2,1)S(1)}, u32[]{:S(2)}, u32[]{:S(2)}) %collective-permute-start) | collective-permute-done | bytes 65568 | tf_op jit(solution)/shard_map/ppermute | solution.py:39
  15.2 3.6 %collective-permute-start.1 = (bf16[64,1024]{1,0:T(8,128)(2,1)}, bf16[64,1024]{1,0:T(8,128)(2,1)S(1)}, u32[]{:S(2)}, u32[]{:S(2)}) collective-permute-start(bf16[64,1024]{1,0:T(8,128)(2,1)} %get-tuple-element.43), channel_id=1, source_target_pairs={{0,12},{4,8},{8,4},{12,0},{1,13},{5,9},{9,5},{13,1},{2,14},{6,10},... | collective-permute-start | bytes 393224 | tf_op jit(solution)/shard_map/ppermute | solution.py:39
  19.3 2.0 %collective-permute-start.3 = (bf16[64,1024]{1,0:T(8,128)(2,1)}, bf16[64,1024]{1,0:T(8,128)(2,1)S(1)}, u32[]{:S(2)}, u32[]{:S(2)}) collective-permute-start(bf16[64,1024]{1,0:T(8,128)(2,1)} %get-tuple-element.47), channel_id=1, source_target_pairs={{0,4},{4,0},{8,12},{12,8},{1,5},{5,1},{9,13},{13,9},{2,6},{6,2},{1... | collective-permute-start | bytes 393224 | tf_op jit(solution)/shard_map/ppermute | solution.py:39
  21.3 1.1 %h_part.1 = (bf16[384,128]{1,0:T(8,128)(2,1)S(1)}, bf16[384,512]{1,0:T(8,128)(2,1)S(1)}) custom-call(s32[12]{0:T(128)S(1)} %copy-done.6, s32[1,2,4]{2,1,0:T(2,128)S(1)} %copy-done.5, bf16[768,512]{1,0:T(8,128)(2,1)S(1)} %copy-done.2, bf16[64,512]{1,0:T(8,128)(2,1)S(1)} %collective-permute-done._.refs_0_, bf16[2,64,512]{2,1,0:T(8,128)(2,1)S(1)} %copy-done.4, ...), custom_call_target="tpu_custom_call" | custom-call | flops 1 | bytes 1 | tf_op jit(solution)/shard_map/h_part/pallas_call | solution.py:248
  22.6 1.7 %collective-permute-start.6 = (bf16[384,128]{1,0:T(8,128)(2,1)S(1)}, bf16[384,128]{1,0:T(8,128)(2,1)S(1)}, u32[]{:S(2)}, u32[]{:S(2)}) collective-permute-start(bf16[384,128]{1,0:T(8,128)(2,1)S(1)} %get-tuple-element.50.refs_3_), channel_id=1, source_target_pairs={{0,2},{2,0},{1,3},{3,1},{4,6},{6,4},{5,7},{7,5},{8,10},{10,8},{9,1... | collective-permute-start | bytes 294920 | tf_op jit(solution)/shard_map/ppermute | solution.py:35
  24.3 1.5 %collective-permute-start.11 = (bf16[256,512]{1,0:T(8,128)(2,1)S(1)}, bf16[256,512]{1,0:T(8,128)(2,1)S(1)}, u32[]{:S(2)}, u32[]{:S(2)}) collective-permute-start(bf16[256,512]{1,0:T(8,128)(2,1)S(1)} %collective-permute-done.9.refs_0_), channel_id=1, source_target_pairs={{0,16},{16,0},{1,17},{17,1},{2,18},{18,2},{3,19},{19,3},{4,20},{20... | collective-permute-start | bytes 786440 | tf_op jit(solution)/shard_map/ppermute | solution.py:35
  25.8 1.4 %collective-permute-done.6.refs_4_ = bf16[384,128]{1,0:T(8,128)(2,1)S(1)} collective-permute-done((bf16[384,128]{1,0:T(8,128)(2,1)S(1)}, bf16[384,128]{1,0:T(8,128)(2,1)S(1)}, u32[]{:S(2)}, u32[]{:S(2)}) %collective-permute-start.6) | collective-permute-done | bytes 98336 | tf_op jit(solution)/shard_map/ppermute | solution.py:35
  27.2 1.7 %collective-permute-start.8 = (bf16[384,512]{1,0:T(8,128)(2,1)S(1)}, bf16[384,512]{1,0:T(8,128)(2,1)S(1)}, u32[]{:S(2)}, u32[]{:S(2)}) collective-permute-start(bf16[384,512]{1,0:T(8,128)(2,1)S(1)} %get-tuple-element.54), channel_id=1, source_target_pairs={{0,2},{2,0},{1,3},{3,1},{4,6},{6,4},{5,7},{7,5},{8,10},{10,8},{9,1... | collective-permute-start | bytes 1179656 | tf_op jit(solution)/shard_map/ppermute | solution.py:35
  29.0 1.3 %down_grad.1 = (bf16[64,1024]{1,0:T(8,128)(2,1)S(1)}, bf16[64,1024]{1,0:T(8,128)(2,1)S(1)}, bf16[64,1024]{1,0:T(8,128)(2,1)S(1)}, bf16[64,1024]{1,0:T(8,128)(2,1)S(1)}, bf16[768,256]{1,0:T(8,128)(2,1)S(1)}) custom-call(s32[12]{0:T(128)S(1)} %copy-done.6, bf16[768,1024]{1,0:T(8,128)(2,1)S(1)} %copy-done.1, ...), custom_call_target="tpu_custom_call" | custom-call | flops 15000000512 | bytes 1 | tf_op jit(solution)/shard_map/down_grad/pallas_call | solution.py:257
  30.3 0.9 %collective-permute-done.11.refs_2_ = bf16[256,512]{1,0:T(8,128)(2,1)S(1)} collective-permute-done((bf16[256,512]{1,0:T(8,128)(2,1)S(1)}, bf16[256,512]{1,0:T(8,128)(2,1)S(1)}, u32[]{:S(2)}, u32[]{:S(2)}) %collective-permute-start.11) | collective-permute-done | bytes 262176 | tf_op jit(solution)/shard_map/ppermute | solution.py:35
  31.2 3.6 %collective-permute-start.13 = (bf16[64,1024]{1,0:T(8,128)(2,1)S(1)}, bf16[64,1024]{1,0:T(8,128)(2,1)S(1)}, u32[]{:S(2)}, u32[]{:S(2)}) collective-permute-start(bf16[64,1024]{1,0:T(8,128)(2,1)S(1)} %get-tuple-element.60), channel_id=1, source_target_pairs={{0,12},{4,8},{8,4},{12,0},{1,13},{5,9},{9,5},{13,1},{2,14},{6,10},... | collective-permute-start | bytes 393224 | tf_op jit(solution)/shard_map/ppermute | solution.py:39
  34.8 0.8 %collective-permute-start.15 = (bf16[64,1024]{1,0:T(8,128)(2,1)S(1)}, bf16[64,1024]{1,0:T(8,128)(2,1)S(1)}, u32[]{:S(2)}, u32[]{:S(2)}) collective-permute-start(bf16[64,1024]{1,0:T(8,128)(2,1)S(1)} %get-tuple-element.62), channel_id=1, source_target_pairs={{0,4},{4,0},{8,12},{12,8},{1,5},{5,1},{9,13},{13,9},{2,6},{6,2},{1... | collective-permute-start | bytes 393224 | tf_op jit(solution)/shard_map/ppermute | solution.py:39
  35.6 1.3 %u_part.1._.refs_5_ = bf16[384,128]{1,0:T(8,128)(2,1)S(1)} custom-call(s32[12]{0:T(128)S(1)} %copy-done.6, s32[1,2,4]{2,1,0:T(2,128)S(1)} %copy-done.5, bf16[768,1024]{1,0:T(8,128)(2,1)S(1)} %copy-done.1, bf16[768,256]{1,0:T(8,128)(2,1)S(1)} %get-tuple-element.51._.wide, bf16[2,64,1024]{2,1,0:T(8,128)(2,1)S(1)} %bitcast.3, ...), custom_call_target="tpu_custom_call" | custom-call | flops 1 | bytes 1 | tf_op jit(solution)/shard_map/u_part/pallas_call | solution.py:248
  36.9 0.7 %collective-permute-start.16 = (bf16[384,128]{1,0:T(8,128)(2,1)S(1)}, bf16[384,128]{1,0:T(8,128)(2,1)S(1)}, u32[]{:S(2)}, u32[]{:S(2)}) collective-permute-start(bf16[384,128]{1,0:T(8,128)(2,1)S(1)} %u_part.1._.refs_5_), channel_id=1, source_target_pairs={{0,2},{2,0},{1,3},{3,1},{4,6},{6,4},{5,7},{7,5},{8,10},{10,8},{9,1... | collective-permute-start | bytes 294920 | tf_op jit(solution)/shard_map/ppermute | solution.py:35
  37.6 1.4 %y_send.1 = (bf16[768,512]{1,0:T(8,128)(2,1)S(1)}, bf16[1024,512]{1,0:T(8,128)(2,1)S(1)}) custom-call(bf16[384,128]{1,0:T(8,128)(2,1)S(1)} %u_part.1._.refs_5_, bf16[768,1024]{1,0:T(8,128)(2,1)S(1)} %copy-done.1, bf16[256,512]{1,0:T(8,128)(2,1)S(1)} %collective-permute-done.9.refs_0_, bf16[256,512]{1,0:T(8,128)(2,1)S(1)} %collective-permute-done.10.refs_1_, ...), custom_call_target="tpu_custom_call" | custom-call | flops 1 | bytes 1 | tf_op jit(solution)/shard_map/y_send/pallas_call | solution.py:274
  39.1 1.8 %collective-permute-start.25 = (bf16[768,512]{1,0:T(8,128)(2,1)S(1)}, bf16[768,512]{1,0:T(8,128)(2,1)S(1)}, u32[]{:S(2)}, u32[]{:S(2)}) collective-permute-start(bf16[768,512]{1,0:T(8,128)(2,1)S(1)} %get-tuple-element.73), channel_id=1, source_target_pairs={{0,2},{2,0},{1,3},{3,1},{4,6},{6,4},{5,7},{7,5},{8,10},{10,8},{9,1... | collective-permute-start | bytes 2359304 | tf_op jit(solution)/shard_map/ppermute | solution.py:35
  40.9 4.0 %back.1 = (bf16[768,1024]{1,0:T(8,128)(2,1)}, s32[8,128]{1,0:T(8,128)S(1)}) custom-call(s32[1,2,4]{2,1,0:T(2,128)S(1)} %copy-done.5, bf16[2048,512]{1,0:T(8,128)(2,1)S(1)} %copy-done, bf16[768,512]{1,0:T(8,128)(2,1)S(1)} %copy-done.2, bf16[768,256]{1,0:T(8,128)(2,1)S(1)} %get-tuple-element.51._.wide, bf16[2,64,1024]{2,1,0:T(8,128)(2,1)S(1)} %bitcast.4, ...), custom_call_target="tpu_custom_call" | custom-call | flops 1 | bytes 1 | tf_op jit(solution)/shard_map/back/pallas_call | solution.py:284
  44.8 1.7 %collective-permute-done.14.refs_2_ = bf16[64,1024]{1,0:T(8,128)(2,1)S(1)} collective-permute-done((bf16[64,1024]{1,0:T(8,128)(2,1)S(1)}, bf16[64,1024]{1,0:T(8,128)(2,1)S(1)}, u32[]{:S(2)}, u32[]{:S(2)}) %collective-permute-start.14) | collective-permute-done | bytes 131104 | tf_op jit(solution)/shard_map/ppermute | solution.py:39
  46.6 1.1 %up_grad.1 = (bf16[64,512]{1,0:T(8,128)(2,1)S(1)}, bf16[64,512]{1,0:T(8,128)(2,1)S(1)}, bf16[64,512]{1,0:T(8,128)(2,1)S(1)}, bf16[64,512]{1,0:T(8,128)(2,1)S(1)}, bf16[768,256]{1,0:T(8,128)(2,1)S(1)}) custom-call(s32[12]{0:T(128)S(1)} %copy-done.6, bf16[768,512]{1,0:T(8,128)(2,1)S(1)} %copy-done.2, s32[8,128]{1,0:T(8,128)S(1)} %get-tuple-element.59.refs_0_.picks, ...), custom_call_target="tpu_custom_call" | custom-call | flops 15000000512 | bytes 1 | tf_op jit(solution)/shard_map/up_grad/pallas_call | solution.py:257
  47.7 2.5 %collective-permute-start.18 = (bf16[64,512]{1,0:T(8,128)(2,1)S(1)}, bf16[64,512]{1,0:T(8,128)(2,1)S(1)}, u32[]{:S(2)}, u32[]{:S(2)}) collective-permute-start(bf16[64,512]{1,0:T(8,128)(2,1)S(1)} %get-tuple-element.65), channel_id=1, source_target_pairs={{0,12},{4,8},{8,4},{12,0},{1,13},{5,9},{9,5},{13,1},{2,14},{6,10},... | collective-permute-start | bytes 196616 | tf_op jit(solution)/shard_map/ppermute | solution.py:39
  50.2 1.9 %collective-permute-start.20 = (bf16[64,512]{1,0:T(8,128)(2,1)S(1)}, bf16[64,512]{1,0:T(8,128)(2,1)S(1)}, u32[]{:S(2)}, u32[]{:S(2)}) collective-permute-start(bf16[64,512]{1,0:T(8,128)(2,1)S(1)} %get-tuple-element.67), channel_id=1, source_target_pairs={{0,4},{4,0},{8,12},{12,8},{1,5},{5,1},{9,13},{13,9},{2,6},{6,2},{1... | collective-permute-start | bytes 196616 | tf_op jit(solution)/shard_map/ppermute | solution.py:39
  52.6 2.2 %y_own.1.refs_10_ = f32[768,512]{1,0:T(8,128)S(1)} custom-call(s32[1,2,4]{2,1,0:T(2,128)S(1)} %copy-done.5, bf16[2048,512]{1,0:T(8,128)(2,1)S(1)} %copy-done, bf16[768,1024]{1,0:T(8,128)(2,1)S(1)} %copy-done.1, bf16[768,256]{1,0:T(8,128)(2,1)S(1)} %get-tuple-element.68.wide, bf16[2,64,512]{2,1,0:T(8,128)(2,1)S(1)} %copy-done.4, ...), custom_call_target="tpu_custom_call" | custom-call | flops 15000000512 | bytes 1 | tf_op jit(solution)/shard_map/y_own/pallas_call | solution.py:294
  55.3 0.8 %collective-permute-done.19.refs_4_ = bf16[64,512]{1,0:T(8,128)(2,1)S(1)} collective-permute-done((bf16[64,512]{1,0:T(8,128)(2,1)S(1)}, bf16[64,512]{1,0:T(8,128)(2,1)S(1)}, u32[]{:S(2)}, u32[]{:S(2)}) %collective-permute-start.19) | collective-permute-done | bytes 65568 | tf_op jit(solution)/shard_map/ppermute | solution.py:39
  56.1 0.5 collective-permute-start.23
  56.6 0.7 %collective-permute-done.22.refs_7_ = bf16[64,512]{1,0:T(8,128)(2,1)S(1)} collective-permute-done((bf16[64,512]{1,0:T(8,128)(2,1)S(1)}, bf16[64,512]{1,0:T(8,128)(2,1)S(1)}, u32[]{:S(2)}, u32[]{:S(2)}) %collective-permute-start.22) | collective-permute-done | bytes 65568 | tf_op jit(solution)/shard_map/ppermute | solution.py:35
  57.9 0.6 %collective-permute-done.25.refs_11_ = bf16[768,512]{1,0:T(8,128)(2,1)S(1)} collective-permute-done((bf16[768,512]{1,0:T(8,128)(2,1)S(1)}, bf16[768,512]{1,0:T(8,128)(2,1)S(1)}, u32[]{:S(2)}, u32[]{:S(2)}) %collective-permute-start.25) | collective-permute-done | bytes 786464 | tf_op jit(solution)/shard_map/ppermute | solution.py:35
  58.5 1.5 %last.1 = (f32[2,64,1024]{2,1,0:T(8,128)}, f32[2,64,512]{2,1,0:T(8,128)}, bf16[768,512]{1,0:T(8,128)(2,1)}) custom-call(s32[8,128]{1,0:T(8,128)S(1)} %get-tuple-element.59.refs_0_.picks, bf16[2,64,1024]{2,1,0:T(8,128)(2,1)S(1)} %sites.1.refs_0_, bf16[2,64,1024]{2,1,0:T(8,128)(2,1)S(1)} %collective-permute-done.17.refs_1_, ...), custom_call_target="tpu_custom_call" | custom-call | flops 1 | bytes 1 | tf_op jit(solution)/shard_map/last/pallas_call | solution.py:309
  (45 shorter events, 2.3 us)
Async XLA Ops:
  0.6 20.6 %copy-start.2 = (bf16[768,512]{1,0:T(8,128)(2,1)S(1)}, bf16[768,512]{1,0:T(8,128)(2,1)}, u32[]{:S(2)}) copy-start(bf16[768,512]{1,0:T(8,128)(2,1)} %act.7) | copy-start | bytes 2359300
  0.6 20.6 %copy-start.5 = (s32[1,2,4]{2,1,0:T(2,128)S(1)}, s32[1,2,4]{2,1,0:T(2,128)}, u32[]{:S(2)}) copy-start(s32[1,2,4]{2,1,0:T(2,128)} %table.9) | copy-start | bytes 100
  0.7 20.6 %copy-start.4 = (bf16[2,64,512]{2,1,0:T(8,128)(2,1)S(1)}, bf16[2,64,512]{2,1,0:T(8,128)(2,1)}, u32[]{:S(2)}) copy-start(bf16[2,64,512]{2,1,0:T(8,128)(2,1)} %own_up.1) | copy-start | bytes 393220
  0.7 20.6 %copy-start.6 = (s32[12]{0:T(128)S(1)}, s32[12]{0:T(128)}, u32[]{:S(2)}) copy-start(s32[12]{0:T(128)} %owner.7) | copy-start | bytes 148
  1.8 27.2 %copy-start.1 = (bf16[768,1024]{1,0:T(8,128)(2,1)S(1)}, bf16[768,1024]{1,0:T(8,128)(2,1)}, u32[]{:S(2)}) copy-start(bf16[768,1024]{1,0:T(8,128)(2,1)} %x.3) | copy-start | bytes 4718596
  4.8 19.5 %collective-permute-start.7 = (bf16[384,512]{1,0:T(8,128)(2,1)S(1)}, bf16[384,512]{1,0:T(8,128)(2,1)S(1)}, u32[]{:S(2)}, u32[]{:S(2)}) collective-permute-start(bf16[384,512]{1,0:T(8,128)(2,1)S(1)} %slice.3), channel_id=1, source_target_pairs={{0,2},{2,0},{1,3},{3,1},{4,6},{6,4},{5,7},{7,5},{8,10},{10,8},{9,1... | collective-permute-start | bytes 1179656 | tf_op jit(solution)/shard_map/ppermute | solution.py:35
  7.8 14.7 %collective-permute-start.9 = (bf16[256,512]{1,0:T(8,128)(2,1)}, bf16[256,512]{1,0:T(8,128)(2,1)S(1)}, u32[]{:S(2)}, u32[]{:S(2)}) collective-permute-start(bf16[256,512]{1,0:T(8,128)(2,1)} %get-tuple-element.55), channel_id=1, source_target_pairs={{0,2},{2,0},{1,3},{3,1},{4,6},{6,4},{5,7},{7,5},{8,10},{10,8},{9,1... | collective-permute-start | bytes 786440 | tf_op jit(solution)/shard_map/ppermute | solution.py:35
  7.9 7.3 %collective-permute-start = (bf16[64,512]{1,0:T(8,128)(2,1)}, bf16[64,512]{1,0:T(8,128)(2,1)S(1)}, u32[]{:S(2)}, u32[]{:S(2)}) collective-permute-start(bf16[64,512]{1,0:T(8,128)(2,1)} %get-tuple-element.42), channel_id=1, source_target_pairs={{0,12},{4,8},{8,4},{12,0},{1,13},{5,9},{9,5},{13,1},{2,14},{6,10},... | collective-permute-start | bytes 196616 | tf_op jit(solution)/shard_map/ppermute | solution.py:39
  12.0 7.3 %collective-permute-start.4 = (bf16[64,512]{1,0:T(8,128)(2,1)}, bf16[64,512]{1,0:T(8,128)(2,1)S(1)}, u32[]{:S(2)}, u32[]{:S(2)}) collective-permute-start(bf16[64,512]{1,0:T(8,128)(2,1)} %get-tuple-element.48), channel_id=1, source_target_pairs={{0,8},{4,12},{8,0},{12,4},{1,9},{5,13},{9,1},{13,5},{2,10},{6,14},... | collective-permute-start | bytes 196616 | tf_op jit(solution)/shard_map/ppermute | solution.py:39
  12.0 7.3 %collective-permute-start.5 = (bf16[64,512]{1,0:T(8,128)(2,1)}, bf16[64,512]{1,0:T(8,128)(2,1)S(1)}, u32[]{:S(2)}, u32[]{:S(2)}) collective-permute-start(bf16[64,512]{1,0:T(8,128)(2,1)} %get-tuple-element.49), channel_id=1, source_target_pairs={{0,4},{4,0},{8,12},{12,8},{1,5},{5,1},{9,13},{13,9},{2,6},{6,2},{1... | collective-permute-start | bytes 196616 | tf_op jit(solution)/shard_map/ppermute | solution.py:39
  15.2 12.0 %collective-permute-start.1 = (bf16[64,1024]{1,0:T(8,128)(2,1)}, bf16[64,1024]{1,0:T(8,128)(2,1)S(1)}, u32[]{:S(2)}, u32[]{:S(2)}) collective-permute-start(bf16[64,1024]{1,0:T(8,128)(2,1)} %get-tuple-element.43), channel_id=1, source_target_pairs={{0,12},{4,8},{8,4},{12,0},{1,13},{5,9},{9,5},{13,1},{2,14},{6,10},... | collective-permute-start | bytes 393224 | tf_op jit(solution)/shard_map/ppermute | solution.py:39
  19.3 9.7 %collective-permute-start.2 = (bf16[64,1024]{1,0:T(8,128)(2,1)}, bf16[64,1024]{1,0:T(8,128)(2,1)S(1)}, u32[]{:S(2)}, u32[]{:S(2)}) collective-permute-start(bf16[64,1024]{1,0:T(8,128)(2,1)} %get-tuple-element.45), channel_id=1, source_target_pairs={{0,8},{4,12},{8,0},{12,4},{1,9},{5,13},{9,1},{13,5},{2,10},{6,14},... | collective-permute-start | bytes 393224 | tf_op jit(solution)/shard_map/ppermute | solution.py:39
  19.3 9.7 %collective-permute-start.3 = (bf16[64,1024]{1,0:T(8,128)(2,1)}, bf16[64,1024]{1,0:T(8,128)(2,1)S(1)}, u32[]{:S(2)}, u32[]{:S(2)}) collective-permute-start(bf16[64,1024]{1,0:T(8,128)(2,1)} %get-tuple-element.47), channel_id=1, source_target_pairs={{0,4},{4,0},{8,12},{12,8},{1,5},{5,1},{9,13},{13,9},{2,6},{6,2},{1... | collective-permute-start | bytes 393224 | tf_op jit(solution)/shard_map/ppermute | solution.py:39
  22.6 4.6 %collective-permute-start.6 = (bf16[384,128]{1,0:T(8,128)(2,1)S(1)}, bf16[384,128]{1,0:T(8,128)(2,1)S(1)}, u32[]{:S(2)}, u32[]{:S(2)}) collective-permute-start(bf16[384,128]{1,0:T(8,128)(2,1)S(1)} %get-tuple-element.50.refs_3_), channel_id=1, source_target_pairs={{0,2},{2,0},{1,3},{3,1},{4,6},{6,4},{5,7},{7,5},{8,10},{10,8},{9,1... | collective-permute-start | bytes 294920 | tf_op jit(solution)/shard_map/ppermute | solution.py:35
  24.3 6.9 %collective-permute-start.11 = (bf16[256,512]{1,0:T(8,128)(2,1)S(1)}, bf16[256,512]{1,0:T(8,128)(2,1)S(1)}, u32[]{:S(2)}, u32[]{:S(2)}) collective-permute-start(bf16[256,512]{1,0:T(8,128)(2,1)S(1)} %collective-permute-done.9.refs_0_), channel_id=1, source_target_pairs={{0,16},{16,0},{1,17},{17,1},{2,18},{18,2},{3,19},{19,3},{4,20},{20... | collective-permute-start | bytes 786440 | tf_op jit(solution)/shard_map/ppermute | solution.py:35
  25.8 9.8 %copy-start.3 = (bf16[2,1024,64]{1,2,0:T(8,128)(2,1)S(1)}, bf16[2,1024,64]{1,2,0:T(8,128)(2,1)}, u32[]{:S(2)}) copy-start(bf16[2,1024,64]{1,2,0:T(8,128)(2,1)} %param.9) | copy-start | bytes 786436
  27.2 7.6 %collective-permute-start.10 = (bf16[256,512]{1,0:T(8,128)(2,1)S(1)}, bf16[256,512]{1,0:T(8,128)(2,1)S(1)}, u32[]{:S(2)}, u32[]{:S(2)}) collective-permute-start(bf16[256,512]{1,0:T(8,128)(2,1)S(1)} %collective-permute-done.9.refs_0_), channel_id=1, source_target_pairs={{0,1},{1,0},{2,3},{3,2},{4,5},{5,4},{6,7},{7,6},{8,9},{9,8},{10,11... | collective-permute-start | bytes 786440 | tf_op jit(solution)/shard_map/ppermute | solution.py:35
  27.2 11.9 %collective-permute-start.8 = (bf16[384,512]{1,0:T(8,128)(2,1)S(1)}, bf16[384,512]{1,0:T(8,128)(2,1)S(1)}, u32[]{:S(2)}, u32[]{:S(2)}) collective-permute-start(bf16[384,512]{1,0:T(8,128)(2,1)S(1)} %get-tuple-element.54), channel_id=1, source_target_pairs={{0,2},{2,0},{1,3},{3,1},{4,6},{6,4},{5,7},{7,5},{8,10},{10,8},{9,1... | collective-permute-start | bytes 1179656 | tf_op jit(solution)/shard_map/ppermute | solution.py:35
  31.2 5.7 %collective-permute-start.12 = (bf16[256,512]{1,0:T(8,128)(2,1)S(1)}, bf16[256,512]{1,0:T(8,128)(2,1)S(1)}, u32[]{:S(2)}, u32[]{:S(2)}) collective-permute-start(bf16[256,512]{1,0:T(8,128)(2,1)S(1)} %collective-permute-done.11.refs_2_), channel_id=1, source_target_pairs={{0,1},{1,0},{2,3},{3,2},{4,5},{5,4},{6,7},{7,6},{8,9},{9,8},{10,11... | collective-permute-start | bytes 786440 | tf_op jit(solution)/shard_map/ppermute | solution.py:35
  31.2 13.6 %collective-permute-start.13 = (bf16[64,1024]{1,0:T(8,128)(2,1)S(1)}, bf16[64,1024]{1,0:T(8,128)(2,1)S(1)}, u32[]{:S(2)}, u32[]{:S(2)}) collective-permute-start(bf16[64,1024]{1,0:T(8,128)(2,1)S(1)} %get-tuple-element.60), channel_id=1, source_target_pairs={{0,12},{4,8},{8,4},{12,0},{1,13},{5,9},{9,5},{13,1},{2,14},{6,10},... | collective-permute-start | bytes 393224 | tf_op jit(solution)/shard_map/ppermute | solution.py:39
  34.8 11.7 %collective-permute-start.14 = (bf16[64,1024]{1,0:T(8,128)(2,1)S(1)}, bf16[64,1024]{1,0:T(8,128)(2,1)S(1)}, u32[]{:S(2)}, u32[]{:S(2)}) collective-permute-start(bf16[64,1024]{1,0:T(8,128)(2,1)S(1)} %get-tuple-element.61), channel_id=1, source_target_pairs={{0,8},{4,12},{8,0},{12,4},{1,9},{5,13},{9,1},{13,5},{2,10},{6,14},... | collective-permute-start | bytes 393224 | tf_op jit(solution)/shard_map/ppermute | solution.py:39
  34.8 11.7 %collective-permute-start.15 = (bf16[64,1024]{1,0:T(8,128)(2,1)S(1)}, bf16[64,1024]{1,0:T(8,128)(2,1)S(1)}, u32[]{:S(2)}, u32[]{:S(2)}) collective-permute-start(bf16[64,1024]{1,0:T(8,128)(2,1)S(1)} %get-tuple-element.62), channel_id=1, source_target_pairs={{0,4},{4,0},{8,12},{12,8},{1,5},{5,1},{9,13},{13,9},{2,6},{6,2},{1... | collective-permute-start | bytes 393224 | tf_op jit(solution)/shard_map/ppermute | solution.py:39
  36.9 7.9 %collective-permute-start.16 = (bf16[384,128]{1,0:T(8,128)(2,1)S(1)}, bf16[384,128]{1,0:T(8,128)(2,1)S(1)}, u32[]{:S(2)}, u32[]{:S(2)}) collective-permute-start(bf16[384,128]{1,0:T(8,128)(2,1)S(1)} %u_part.1._.refs_5_), channel_id=1, source_target_pairs={{0,2},{2,0},{1,3},{3,1},{4,6},{6,4},{5,7},{7,5},{8,10},{10,8},{9,1... | collective-permute-start | bytes 294920 | tf_op jit(solution)/shard_map/ppermute | solution.py:35
  39.1 19.4 %collective-permute-start.25 = (bf16[768,512]{1,0:T(8,128)(2,1)S(1)}, bf16[768,512]{1,0:T(8,128)(2,1)S(1)}, u32[]{:S(2)}, u32[]{:S(2)}) collective-permute-start(bf16[768,512]{1,0:T(8,128)(2,1)S(1)} %get-tuple-element.73), channel_id=1, source_target_pairs={{0,2},{2,0},{1,3},{3,1},{4,6},{6,4},{5,7},{7,5},{8,10},{10,8},{9,1... | collective-permute-start | bytes 2359304 | tf_op jit(solution)/shard_map/ppermute | solution.py:35
  47.7 8.4 %collective-permute-start.18 = (bf16[64,512]{1,0:T(8,128)(2,1)S(1)}, bf16[64,512]{1,0:T(8,128)(2,1)S(1)}, u32[]{:S(2)}, u32[]{:S(2)}) collective-permute-start(bf16[64,512]{1,0:T(8,128)(2,1)S(1)} %get-tuple-element.65), channel_id=1, source_target_pairs={{0,12},{4,8},{8,4},{12,0},{1,13},{5,9},{9,5},{13,1},{2,14},{6,10},... | collective-permute-start | bytes 196616 | tf_op jit(solution)/shard_map/ppermute | solution.py:39
  50.2 5.9 %collective-permute-start.19 = (bf16[64,512]{1,0:T(8,128)(2,1)S(1)}, bf16[64,512]{1,0:T(8,128)(2,1)S(1)}, u32[]{:S(2)}, u32[]{:S(2)}) collective-permute-start(bf16[64,512]{1,0:T(8,128)(2,1)S(1)} %get-tuple-element.66), channel_id=1, source_target_pairs={{0,8},{4,12},{8,0},{12,4},{1,9},{5,13},{9,1},{13,5},{2,10},{6,14},... | collective-permute-start | bytes 196616 | tf_op jit(solution)/shard_map/ppermute | solution.py:39
  50.2 4.7 %collective-permute-start.20 = (bf16[64,512]{1,0:T(8,128)(2,1)S(1)}, bf16[64,512]{1,0:T(8,128)(2,1)S(1)}, u32[]{:S(2)}, u32[]{:S(2)}) collective-permute-start(bf16[64,512]{1,0:T(8,128)(2,1)S(1)} %get-tuple-element.67), channel_id=1, source_target_pairs={{0,4},{4,0},{8,12},{12,8},{1,5},{5,1},{9,13},{13,9},{2,6},{6,2},{1... | collective-permute-start | bytes 196616 | tf_op jit(solution)/shard_map/ppermute | solution.py:39
  52.5 5.4 %collective-permute-start.17 = (bf16[2,64,1024]{2,1,0:T(8,128)(2,1)S(1)}, bf16[2,64,1024]{2,1,0:T(8,128)(2,1)S(1)}, u32[]{:S(2)}, u32[]{:S(2)}) collective-permute-start(bf16[2,64,1024]{2,1,0:T(8,128)(2,1)S(1)} %sites.1.refs_0_), channel_id=1, source_target_pairs={{0,1},{1,0},{2,3},{3,2},{4,5},{5,4},{6,7},{7,6},{8,9},{9,8},{10,11... | collective-permute-start | bytes 786440 | tf_op jit(solution)/shard_map/ppermute | solution.py:35
  55.0 1.6 %collective-permute-start.21 = (bf16[64,512]{1,0:T(8,128)(2,1)S(1)}, bf16[64,512]{1,0:T(8,128)(2,1)S(1)}, u32[]{:S(2)}, u32[]{:S(2)}) collective-permute-start(bf16[64,512]{1,0:T(8,128)(2,1)S(1)} %get-tuple-element.69._.refs_2_), channel_id=1, source_target_pairs={{0,1},{1,0},{2,3},{3,2},{4,5},{5,4},{6,7},{7,6},{8,9},{9,8},{10,11... | collective-permute-start | bytes 196616 | tf_op jit(solution)/shard_map/ppermute | solution.py:35
  56.1 1.3 %collective-permute-start.22 = (bf16[64,512]{1,0:T(8,128)(2,1)S(1)}, bf16[64,512]{1,0:T(8,128)(2,1)S(1)}, u32[]{:S(2)}, u32[]{:S(2)}) collective-permute-start(bf16[64,512]{1,0:T(8,128)(2,1)S(1)} %collective-permute-done.18.refs_3_), channel_id=1, source_target_pairs={{0,1},{1,0},{2,3},{3,2},{4,5},{5,4},{6,7},{7,6},{8,9},{9,8},{10,11... | collective-permute-start | bytes 196616 | tf_op jit(solution)/shard_map/ppermute | solution.py:35
  56.1 1.4 %collective-permute-start.23 = (bf16[64,512]{1,0:T(8,128)(2,1)S(1)}, bf16[64,512]{1,0:T(8,128)(2,1)S(1)}, u32[]{:S(2)}, u32[]{:S(2)}) collective-permute-start(bf16[64,512]{1,0:T(8,128)(2,1)S(1)} %collective-permute-done.19.refs_4_), channel_id=1, source_target_pairs={{0,1},{1,0},{2,3},{3,2},{4,5},{5,4},{6,7},{7,6},{8,9},{9,8},{10,11... | collective-permute-start | bytes 196616 | tf_op jit(solution)/shard_map/ppermute | solution.py:35
  56.6 1.3 %collective-permute-start.24 = (bf16[64,512]{1,0:T(8,128)(2,1)S(1)}, bf16[64,512]{1,0:T(8,128)(2,1)S(1)}, u32[]{:S(2)}, u32[]{:S(2)}) collective-permute-start(bf16[64,512]{1,0:T(8,128)(2,1)S(1)} %collective-permute-done.20.refs_5_), channel_id=1, source_target_pairs={{0,1},{1,0},{2,3},{3,2},{4,5},{5,4},{6,7},{7,6},{8,9},{9,8},{10,11... | collective-permute-start | bytes 196616 | tf_op jit(solution)/shard_map/ppermute | solution.py:35
  (1 other events, 3.9 us)

commit v14 on v11

--- a/solution.py
+++ b/solution.py
@@ -55,13 +55,6 @@
     return lax.dot_general(a, b, (((0,), (0,)), ((), ())), preferred_element_type=F32)
 
 
-def run(copies):
-    for copy in copies:
-        copy.start()
-    for copy in copies:
-        copy.wait()
-
-
 def wanted_site(table, n_dp, s, q=0):
     n_pair = lax.axis_size("pair")
     core = lax.rem(lax.axis_index("pair") + n_pair - q, n_pair)
@@ -74,19 +67,27 @@
 
 def pack_kernel(n_dp, n_mp, n_pair, table, down, up, w, *refs):
     away = n_dp - 1
-    ups, downs, pieces, sem = refs[:away], refs[away:2 * away], refs[2 * away:-1], refs[-1]
+    ups, downs, pieces, rows, sem = refs[:away], refs[away:2 * away], refs[2 * away:-2], refs[-2], refs[-1]
     feat = w.shape[0] // n_mp
     part = feat // n_pair
-    copies = []
-    for s in range(away):
-        site = wanted_site(table, n_dp, s + 1)
-        copies.append(pltpu.make_async_copy(up.at[site], ups[s], sem.at[s]))
-        copies.append(pltpu.make_async_copy(down.at[site], downs[s], sem.at[away + s]))
+    fetches, copies = [], []
     for s in range(1, n_mp):
         row = lax.rem(lax.axis_index("mp") + s, n_mp) * feat + lax.axis_index("pair") * part
         row = pl.multiple_of(row, part)
-        copies.append(pltpu.make_async_copy(w.at[pl.ds(row, part)], pieces[s - 1], sem.at[2 * away + s - 1]))
-    run(copies)
+        fetches.append(pltpu.make_async_copy(w.at[pl.ds(row, part)], rows.at[s - 1], sem.at[s - 1]))
+        fetches[-1].start()
+    for s in range(away):
+        site = wanted_site(table, n_dp, s + 1)
+        copies.append(pltpu.make_async_copy(up.at[site], ups[s], sem.at[n_mp - 1 + s]))
+        copies.append(pltpu.make_async_copy(down.at[site], downs[s], sem.at[n_mp - 1 + away + s]))
+    for copy in copies:
+        copy.start()
+    for s, fetch in enumerate(fetches):
+        fetch.wait()
+        copies.append(pltpu.make_async_copy(rows.at[s], pieces[s], sem.at[n_mp - 1 + 2 * away + s]))
+        copies[-1].start()
+    for copy in copies:
+        copy.wait()
 
 
 def gather_maps(n_dp, table, own, gots, wide):
@@ -184,7 +185,7 @@
         gather_maps(n_dp, table, own_up, ups, maps)
 
     own = w[pl.ds(pl.multiple_of(lax.axis_index("mp") * feat, feat), feat), :]
-    out[...] = nn(x[...], own) + SCALE * nn(wide[...], maps[...])
+    out[...] = (nn(x[...], own) + SCALE * nn(wide[...], maps[...])).astype(BF16)
 
 
 def pick_sum(grads, picks, site):
@@ -208,7 +209,7 @@
         total = total + part[0].astype(F32)
     down[0] = SCALE * total
     up[0] = SCALE * pick_sum(ups, picks, pl.program_id(0))
-    total = parts[0][...]
+    total = parts[0][...].astype(F32)
     for part in parts[1:]:
         total = total + part[...].astype(F32)
     y[...] = total.astype(BF16)
@@ -230,8 +231,8 @@
     packed = call(
         functools.partial(pack_kernel, n_dp, n_mp, n_pair), "pack",
         [shape(rank, cols)] * away + [shape(rank, feat)] * away + [shape(part, cols)] * n_other,
-        [SMEM, ANY, ANY, ANY], [VMEM] * (2 * away + n_other),
-        [pltpu.SemaphoreType.DMA((2 * away + n_other,))], mib=60,
+        [SMEM, VMEM, VMEM, ANY], [ANY] * (2 * away + n_other),
+        [pltpu.VMEM((n_other, part, cols), BF16), pltpu.SemaphoreType.DMA((2 * away + 2 * n_other,))], mib=60,
     )(table, down, up, w)
     pieces = [shift(packed[2 * away + s - 1], "mp", s) for s in range(1, n_mp)]
     ups = [swap(packed[s - 1], "dp", n_dp - s) for s in range(1, n_dp)]
@@ -267,7 +268,7 @@
         [ANY, ANY, row_block(feat)] + [whole(part, cols)] * len(parts),
         [row_block(cols)] * n_other + [whole(feat, cols)] * n_other,
         grid=(TILES,),
-    )(u_parts[0], down_back[1], x, *parts)
+    )(u_parts[0], down_back[away], x, *parts)
     w_rows = sent[n_other:]
     y_got = [shift(sent[s - 1], "mp", n_mp - s) for s in range(1, n_mp)]
     back, picks = call(
@@ -278,10 +279,10 @@
         [row_block(feat), whole(-(-n_dp * n_pair // 8) * 8, 128)],
         [pltpu.VMEM((feat, cols), BF16), pltpu.VMEM((n_dp * rank, feat), BF16)], grid=(TILES,),
     )(table, w, gy, *gy_got, *w_rows, h_wide, down, *downs)
-    up_back, u_wide = gradient(gy, u_parts, [picks] + down_back[2:] + gy_got, "up", GRAD_COST)
+    up_back, u_wide = gradient(gy, u_parts, [picks] + down_back[1:] + gy_got, "up", GRAD_COST)
 
     y_own = call(
-        functools.partial(own_kernel, n_dp), "y_own", shape(tok, cols, dtype=F32),
+        functools.partial(own_kernel, n_dp), "y_own", shape(tok, cols),
         [SMEM, whole(*w.shape), row_block(feat), row_block(n_dp * rank), whole(*up.shape)]
         + [whole(rank, cols)] * away,
         row_block(cols), [pltpu.VMEM((n_dp * rank, cols), BF16)], grid=(TILES,), flops=GRAD_COST,

time: 60 us -> 59.8 us (level)
    ppermute x11, waiting for transfers between devices: 6.41 us -> 7.18 us  [shift(): lax.ppermute(value, axis, [(i, (i + by) % size) for i in range(size)])]
    ppermute x12, starting transfers between devices: 18.1 us -> 17.4 us  [swap(): lax.ppermute(value, axis, [(i, i ^ mask) for i in range(lax.axis_size(axi...]
    ppermute x12, waiting for transfers between devices: 8.81 us -> 8.13 us  [swap(): lax.ppermute(value, axis, [(i, i ^ mask) for i in range(lax.axis_size(axi...]
where the time goes in v14:
time: 59.8 us; the launch traced here: 59.6 us
  starting transfers between devices  25.8 us (43%)
  Pallas kernels  17.7 us (30%)
  waiting for transfers between devices  15.3 us (26%)
  between operations  0.81 us (1%)
    ppermute x12, starting transfers between devices, swap(): lax.ppermute(value, axis, [(i, i ^ mask) for i in range(lax.axis_size(axi...  17.4 us
    ppermute x11, starting transfers between devices, shift(): lax.ppermute(value, axis, [(i, (i + by) % size) for i in range(size)])  8.39 us
    ppermute x12, waiting for transfers between devices, swap(): lax.ppermute(value, axis, [(i, i ^ mask) for i in range(lax.axis_size(axi...  8.13 us
    ppermute x11, waiting for transfers between devices, shift(): lax.ppermute(value, axis, [(i, (i + by) % size) for i in range(size)])  7.18 us
    pallas_call x1, Pallas kernels, shards(): call(functools.partial(back_kernel, n_dp, n_mp), 'back', [shape(tok, feat...  4.07 us
    pallas_call x1, Pallas kernels, shards(): call(functools.partial(pack_kernel, n_dp, n_mp, n_pair), 'pack', [shape(r...  3.28 us
    pallas_call x2, Pallas kernels, gradient(): call(functools.partial(grad_kernel, n_dp, n_mp, len(behind)), name + '_gr...  2.45 us
    pallas_call x2, Pallas kernels, low_rank(): call(functools.partial(reduce_kernel, n_dp), name + '_part', shape(tok //...  2.42 us
  transfers between devices with their start and end apart: 23, of which 9 were waited for; matrix products, arithmetic and copies ran while one was open for 0% of the time, Pallas kernels for 22%

profile of v14, /device:TPU:0, one launch (start us, length us, event | category | flops | bytes accessed | tf_op | source)
XLA Modules:
  0.0 59.6 jit_solution(8643150544529101265)
XLA Ops:
  0.7 3.3 %pack.1 = (bf16[64,512]{1,0:T(8,128)(2,1)}, bf16[64,512]{1,0:T(8,128)(2,1)}, bf16[64,512]{1,0:T(8,128)(2,1)}, bf16[64,1024]{1,0:T(8,128)(2,1)}, bf16[64,1024]{1,...) custom-call(s32[1,2,4]{2,1,0:T(2,128)} %table.9, bf16[2,64,1024]{2,1,0:T(8,128)(2,1)} %bitcast.2, ...), custom_call_target="tpu_custom_call" | custom-call | flops 1 | bytes 1 | tf_op jit(solution)/shard_map/pack/pallas_call | solution.py:231
  4.0 3.0 %collective-permute-start = (bf16[512,512]{1,0:T(8,128)(2,1)}, bf16[512,512]{1,0:T(8,128)(2,1)S(1)}, u32[]{:S(2)}, u32[]{:S(2)}) collective-permute-start(bf16[512,512]{1,0:T(8,128)(2,1)} %get-tuple-element.37), channel_id=1, source_target_pairs={{0,2},{2,0},{1,3},{3,1},{4,6},{6,4},{5,7},{7,5},{8,10},{10,8},{9,1... | collective-permute-start | bytes 1572872 | tf_op jit(solution)/shard_map/ppermute | solution.py:35
  7.0 3.6 %collective-permute-start.2 = (bf16[64,512]{1,0:T(8,128)(2,1)}, bf16[64,512]{1,0:T(8,128)(2,1)S(1)}, u32[]{:S(2)}, u32[]{:S(2)}) collective-permute-start(bf16[64,512]{1,0:T(8,128)(2,1)} %get-tuple-element.40), channel_id=1, source_target_pairs={{0,12},{4,8},{8,4},{12,0},{1,13},{5,9},{9,5},{13,1},{2,14},{6,10},... | collective-permute-start | bytes 196616 | tf_op jit(solution)/shard_map/ppermute | solution.py:39
  10.6 0.8 %collective-permute-start.7 = (bf16[64,512]{1,0:T(8,128)(2,1)}, bf16[64,512]{1,0:T(8,128)(2,1)S(1)}, u32[]{:S(2)}, u32[]{:S(2)}) collective-permute-start(bf16[64,512]{1,0:T(8,128)(2,1)} %get-tuple-element.47), channel_id=1, source_target_pairs={{0,4},{4,0},{8,12},{12,8},{1,5},{5,1},{9,13},{13,9},{2,6},{6,2},{1... | collective-permute-start | bytes 196616 | tf_op jit(solution)/shard_map/ppermute | solution.py:39
  11.4 2.7 %collective-permute-done.2._.refs_0_ = bf16[64,512]{1,0:T(8,128)(2,1)S(1)} collective-permute-done((bf16[64,512]{1,0:T(8,128)(2,1)}, bf16[64,512]{1,0:T(8,128)(2,1)S(1)}, u32[]{:S(2)}, u32[]{:S(2)}) %collective-permute-start.2) | collective-permute-done | bytes 65568 | tf_op jit(solution)/shard_map/ppermute | solution.py:39
  14.0 3.6 %collective-permute-start.3 = (bf16[64,1024]{1,0:T(8,128)(2,1)}, bf16[64,1024]{1,0:T(8,128)(2,1)S(1)}, u32[]{:S(2)}, u32[]{:S(2)}) collective-permute-start(bf16[64,1024]{1,0:T(8,128)(2,1)} %get-tuple-element.41), channel_id=1, source_target_pairs={{0,12},{4,8},{8,4},{12,0},{1,13},{5,9},{9,5},{13,1},{2,14},{6,10},... | collective-permute-start | bytes 393224 | tf_op jit(solution)/shard_map/ppermute | solution.py:39
  17.7 0.7 %collective-permute-start.5 = (bf16[64,1024]{1,0:T(8,128)(2,1)}, bf16[64,1024]{1,0:T(8,128)(2,1)S(1)}, u32[]{:S(2)}, u32[]{:S(2)}) collective-permute-start(bf16[64,1024]{1,0:T(8,128)(2,1)} %get-tuple-element.45), channel_id=1, source_target_pairs={{0,4},{4,0},{8,12},{12,8},{1,5},{5,1},{9,13},{13,9},{2,6},{6,2},{1... | collective-permute-start | bytes 393224 | tf_op jit(solution)/shard_map/ppermute | solution.py:39
  18.5 1.1 %h_part.1.refs_3_ = bf16[384,128]{1,0:T(8,128)(2,1)S(1)} custom-call(s32[12]{0:T(128)S(1)} %copy-done.6, s32[1,2,4]{2,1,0:T(2,128)S(1)} %copy-done.5, bf16[768,512]{1,0:T(8,128)(2,1)S(1)} %copy-done.2, bf16[64,512]{1,0:T(8,128)(2,1)S(1)} %collective-permute-done.2._.refs_0_, bf16[2,64,512]{2,1,0:T(8,128)(2,1)S(1)} %copy-done.4, ...), custom_call_target="tpu_custom_call" | custom-call | flops 1 | bytes 1 | tf_op jit(solution)/shard_map/h_part/pallas_call | solution.py:242
  19.6 0.4 collective-permute-start.8
  20.0 1.7 %collective-permute-start.1 = (bf16[768,512]{1,0:T(8,128)(2,1)S(1)}, bf16[768,512]{1,0:T(8,128)(2,1)S(1)}, u32[]{:S(2)}, u32[]{:S(2)}) collective-permute-start(bf16[768,512]{1,0:T(8,128)(2,1)S(1)} %copy-done.2), channel_id=1, source_target_pairs={{0,2},{2,0},{1,3},{3,1},{4,6},{6,4},{5,7},{7,5},{8,10},{10,8},{9,1... | collective-permute-start | bytes 2359304 | tf_op jit(solution)/shard_map/ppermute | solution.py:35
  21.7 3.7 %collective-permute-done.8.refs_4_ = bf16[384,128]{1,0:T(8,128)(2,1)S(1)} collective-permute-done((bf16[384,128]{1,0:T(8,128)(2,1)S(1)}, bf16[384,128]{1,0:T(8,128)(2,1)S(1)}, u32[]{:S(2)}, u32[]{:S(2)}) %collective-permute-start.8) | collective-permute-done | bytes 98336 | tf_op jit(solution)/shard_map/ppermute | solution.py:35
  25.4 1.9 %collective-permute-done.4.refs_1_.refs_7_ = bf16[64,1024]{1,0:T(8,128)(2,1)S(1)} collective-permute-done((bf16[64,1024]{1,0:T(8,128)(2,1)}, bf16[64,1024]{1,0:T(8,128)(2,1)S(1)}, u32[]{:S(2)}, u32[]{:S(2)}) %collective-permute-start.4) | collective-permute-done | bytes 131104 | tf_op jit(solution)/shard_map/ppermute | solution.py:39
  27.3 1.3 %down_grad.1 = (bf16[64,1024]{1,0:T(8,128)(2,1)S(1)}, bf16[64,1024]{1,0:T(8,128)(2,1)S(1)}, bf16[64,1024]{1,0:T(8,128)(2,1)S(1)}, bf16[64,1024]{1,0:T(8,128)(2,1)S(1)}, bf16[768,256]{1,0:T(8,128)(2,1)S(1)}) custom-call(s32[12]{0:T(128)S(1)} %copy-done.6, bf16[768,1024]{1,0:T(8,128)(2,1)S(1)} %copy-done.1, ...), custom_call_target="tpu_custom_call" | custom-call | flops 15000000512 | bytes 1 | tf_op jit(solution)/shard_map/down_grad/pallas_call | solution.py:250
  28.8 2.7 %collective-permute-start.11 = (bf16[64,1024]{1,0:T(8,128)(2,1)S(1)}, bf16[64,1024]{1,0:T(8,128)(2,1)S(1)}, u32[]{:S(2)}, u32[]{:S(2)}) collective-permute-start(bf16[64,1024]{1,0:T(8,128)(2,1)S(1)} %get-tuple-element.53), channel_id=1, source_target_pairs={{0,12},{4,8},{8,4},{12,0},{1,13},{5,9},{9,5},{13,1},{2,14},{6,10},... | collective-permute-start | bytes 393224 | tf_op jit(solution)/shard_map/ppermute | solution.py:39
  31.6 0.8 %collective-permute-start.12 = (bf16[64,1024]{1,0:T(8,128)(2,1)S(1)}, bf16[64,1024]{1,0:T(8,128)(2,1)S(1)}, u32[]{:S(2)}, u32[]{:S(2)}) collective-permute-start(bf16[64,1024]{1,0:T(8,128)(2,1)S(1)} %get-tuple-element.54), channel_id=1, source_target_pairs={{0,8},{4,12},{8,0},{12,4},{1,9},{5,13},{9,1},{13,5},{2,10},{6,14},... | collective-permute-start | bytes 393224 | tf_op jit(solution)/shard_map/ppermute | solution.py:39
  32.3 1.3 %u_part.1._.refs_5_ = bf16[384,128]{1,0:T(8,128)(2,1)S(1)} custom-call(s32[12]{0:T(128)S(1)} %copy-done.6, s32[1,2,4]{2,1,0:T(2,128)S(1)} %copy-done.5, bf16[768,1024]{1,0:T(8,128)(2,1)S(1)} %copy-done.1, bf16[768,256]{1,0:T(8,128)(2,1)S(1)} %get-tuple-element.48._.refs_4_, bf16[2,64,1024]{2,1,0:T(8,128)(2,1)S(1)} %bitcast.3, ...), custom_call_target="tpu_custom_call" | custom-call | flops 1 | bytes 1 | tf_op jit(solution)/shard_map/u_part/pallas_call | solution.py:242
  33.6 1.0 %collective-permute-done.9.__.refs_3_ = bf16[64,1024]{1,0:T(8,128)(2,1)S(1)} collective-permute-done((bf16[64,1024]{1,0:T(8,128)(2,1)S(1)}, bf16[64,1024]{1,0:T(8,128)(2,1)S(1)}, u32[]{:S(2)}, u32[]{:S(2)}) %collective-permute-start.9) | collective-permute-done | bytes 131104 | tf_op jit(solution)/shard_map/ppermute | solution.py:39
  34.7 0.5 collective-permute-start.13
  35.2 1.4 %y_send.1 = (bf16[768,512]{1,0:T(8,128)(2,1)S(1)}, bf16[1024,512]{1,0:T(8,128)(2,1)S(1)}) custom-call(bf16[384,128]{1,0:T(8,128)(2,1)S(1)} %u_part.1._.refs_5_, bf16[64,1024]{1,0:T(8,128)(2,1)S(1)} %collective-permute-done.9.__.refs_3_, bf16[768,1024]{1,0:T(8,128)(2,1)S(1)} %copy-done.1, bf16[512,512]{1,0:T(8,128)(2,1)S(1)} %collective-permute-done.refs_0_, ...), custom_call_target="tpu_custom_call" | custom-call | flops 1 | bytes 1 | tf_op jit(solution)/shard_map/y_send/pallas_call | solution.py:265
  36.6 1.6 %collective-permute-start.22 = (bf16[768,512]{1,0:T(8,128)(2,1)S(1)}, bf16[768,512]{1,0:T(8,128)(2,1)S(1)}, u32[]{:S(2)}, u32[]{:S(2)}) collective-permute-start(bf16[768,512]{1,0:T(8,128)(2,1)S(1)} %get-tuple-element.65), channel_id=1, source_target_pairs={{0,2},{2,0},{1,3},{3,1},{4,6},{6,4},{5,7},{7,5},{8,10},{10,8},{9,1... | collective-permute-start | bytes 2359304 | tf_op jit(solution)/shard_map/ppermute | solution.py:35
  38.2 2.6 %collective-permute-done.1.refs_2_.refs_4_ = bf16[768,512]{1,0:T(8,128)(2,1)S(1)} collective-permute-done((bf16[768,512]{1,0:T(8,128)(2,1)S(1)}, bf16[768,512]{1,0:T(8,128)(2,1)S(1)}, u32[]{:S(2)}, u32[]{:S(2)}) %collective-permute-start.1) | collective-permute-done | bytes 786464 | tf_op jit(solution)/shard_map/ppermute | solution.py:35
  40.8 4.1 %back.1 = (bf16[768,1024]{1,0:T(8,128)(2,1)}, s32[8,128]{1,0:T(8,128)S(1)}) custom-call(s32[1,2,4]{2,1,0:T(2,128)S(1)} %copy-done.5, bf16[2048,512]{1,0:T(8,128)(2,1)S(1)} %copy-done, bf16[768,512]{1,0:T(8,128)(2,1)S(1)} %copy-done.2, bf16[768,512]{1,0:T(8,128)(2,1)S(1)} %collective-permute-done.1.refs_2_.refs_4_, ...), custom_call_target="tpu_custom_call" | custom-call | flops 1 | bytes 1 | tf_op jit(solution)/shard_map/back/pallas_call | solution.py:274
  44.9 1.1 %up_grad.1 = (bf16[64,512]{1,0:T(8,128)(2,1)S(1)}, bf16[64,512]{1,0:T(8,128)(2,1)S(1)}, bf16[64,512]{1,0:T(8,128)(2,1)S(1)}, bf16[64,512]{1,0:T(8,128)(2,1)S(1)}, bf16[768,256]{1,0:T(8,128)(2,1)S(1)}) custom-call(s32[12]{0:T(128)S(1)} %copy-done.6, bf16[768,512]{1,0:T(8,128)(2,1)S(1)} %copy-done.2, s32[8,128]{1,0:T(8,128)S(1)} %get-tuple-element.52.refs_0_.picks, ...), custom_call_target="tpu_custom_call" | custom-call | flops 15000000512 | bytes 1 | tf_op jit(solution)/shard_map/up_grad/pallas_call | solution.py:250
  46.0 2.6 %collective-permute-start.17 = (bf16[64,512]{1,0:T(8,128)(2,1)S(1)}, bf16[64,512]{1,0:T(8,128)(2,1)S(1)}, u32[]{:S(2)}, u32[]{:S(2)}) collective-permute-start(bf16[64,512]{1,0:T(8,128)(2,1)S(1)} %get-tuple-element.59), channel_id=1, source_target_pairs={{0,4},{4,0},{8,12},{12,8},{1,5},{5,1},{9,13},{13,9},{2,6},{6,2},{1... | collective-permute-start | bytes 196616 | tf_op jit(solution)/shard_map/ppermute | solution.py:39
  48.6 2.0 %collective-permute-start.16 = (bf16[64,512]{1,0:T(8,128)(2,1)S(1)}, bf16[64,512]{1,0:T(8,128)(2,1)S(1)}, u32[]{:S(2)}, u32[]{:S(2)}) collective-permute-start(bf16[64,512]{1,0:T(8,128)(2,1)S(1)} %get-tuple-element.58), channel_id=1, source_target_pairs={{0,8},{4,12},{8,0},{12,4},{1,9},{5,13},{9,1},{13,5},{2,10},{6,14},... | collective-permute-start | bytes 196616 | tf_op jit(solution)/shard_map/ppermute | solution.py:39
  50.6 0.5 collective-permute-start.15
  51.5 2.2 %y_own.1.refs_10_ = bf16[768,512]{1,0:T(8,128)(2,1)S(1)} custom-call(s32[1,2,4]{2,1,0:T(2,128)S(1)} %copy-done.5, bf16[2048,512]{1,0:T(8,128)(2,1)S(1)} %copy-done, bf16[768,1024]{1,0:T(8,128)(2,1)S(1)} %copy-done.1, bf16[768,256]{1,0:T(8,128)(2,1)S(1)} %get-tuple-element.60.wide, bf16[2,64,512]{2,1,0:T(8,128)(2,1)S(1)} %copy-done.4, ...), custom_call_target="tpu_custom_call" | custom-call | flops 15000000512 | bytes 1 | tf_op jit(solution)/shard_map/y_own/pallas_call | solution.py:284
  53.6 0.5 collective-permute-start.18
  54.5 2.2 %collective-permute-done.15.refs_3_ = bf16[64,512]{1,0:T(8,128)(2,1)S(1)} collective-permute-done((bf16[64,512]{1,0:T(8,128)(2,1)S(1)}, bf16[64,512]{1,0:T(8,128)(2,1)S(1)}, u32[]{:S(2)}, u32[]{:S(2)}) %collective-permute-start.15) | collective-permute-done | bytes 65568 | tf_op jit(solution)/shard_map/ppermute | solution.py:39
  56.6 0.5 collective-permute-start.19
  57.2 0.7 %collective-permute-done.20.refs_8_ = bf16[64,512]{1,0:T(8,128)(2,1)S(1)} collective-permute-done((bf16[64,512]{1,0:T(8,128)(2,1)S(1)}, bf16[64,512]{1,0:T(8,128)(2,1)S(1)}, u32[]{:S(2)}, u32[]{:S(2)}) %collective-permute-start.20) | collective-permute-done | bytes 65568 | tf_op jit(solution)/shard_map/ppermute | solution.py:35
  58.1 1.6 %last.1 = (f32[2,64,1024]{2,1,0:T(8,128)}, f32[2,64,512]{2,1,0:T(8,128)}, bf16[768,512]{1,0:T(8,128)(2,1)}) custom-call(s32[8,128]{1,0:T(8,128)S(1)} %get-tuple-element.52.refs_0_.picks, bf16[2,64,1024]{2,1,0:T(8,128)(2,1)S(1)} %sites.1.refs_0_, bf16[2,64,1024]{2,1,0:T(8,128)(2,1)S(1)} %collective-permute-done.14.refs_1_, ...), custom_call_target="tpu_custom_call" | custom-call | flops 1 | bytes 1 | tf_op jit(solution)/shard_map/last/pallas_call | solution.py:299
  (38 shorter events, 1.1 us)
Async XLA Ops:
  0.6 17.8 %copy-start.4 = (bf16[2,64,512]{2,1,0:T(8,128)(2,1)S(1)}, bf16[2,64,512]{2,1,0:T(8,128)(2,1)}, u32[]{:S(2)}) copy-start(bf16[2,64,512]{2,1,0:T(8,128)(2,1)} %own_up.1) | copy-start | bytes 393220
  0.6 17.8 %copy-start.5 = (s32[1,2,4]{2,1,0:T(2,128)S(1)}, s32[1,2,4]{2,1,0:T(2,128)}, u32[]{:S(2)}) copy-start(s32[1,2,4]{2,1,0:T(2,128)} %table.9) | copy-start | bytes 100
  0.7 17.8 %copy-start.2 = (bf16[768,512]{1,0:T(8,128)(2,1)S(1)}, bf16[768,512]{1,0:T(8,128)(2,1)}, u32[]{:S(2)}) copy-start(bf16[768,512]{1,0:T(8,128)(2,1)} %act.7) | copy-start | bytes 2359300
  0.7 17.8 %copy-start.6 = (s32[12]{0:T(128)S(1)}, s32[12]{0:T(128)}, u32[]{:S(2)}) copy-start(s32[12]{0:T(128)} %owner.7) | copy-start | bytes 148
  0.7 26.7 %copy-start.1 = (bf16[768,1024]{1,0:T(8,128)(2,1)S(1)}, bf16[768,1024]{1,0:T(8,128)(2,1)}, u32[]{:S(2)}) copy-start(bf16[768,1024]{1,0:T(8,128)(2,1)} %x.3) | copy-start | bytes 4718596
  4.0 16.0 %collective-permute-start = (bf16[512,512]{1,0:T(8,128)(2,1)}, bf16[512,512]{1,0:T(8,128)(2,1)S(1)}, u32[]{:S(2)}, u32[]{:S(2)}) collective-permute-start(bf16[512,512]{1,0:T(8,128)(2,1)} %get-tuple-element.37), channel_id=1, source_target_pairs={{0,2},{2,0},{1,3},{3,1},{4,6},{6,4},{5,7},{7,5},{8,10},{10,8},{9,1... | collective-permute-start | bytes 1572872 | tf_op jit(solution)/shard_map/ppermute | solution.py:35
  7.0 7.1 %collective-permute-start.2 = (bf16[64,512]{1,0:T(8,128)(2,1)}, bf16[64,512]{1,0:T(8,128)(2,1)S(1)}, u32[]{:S(2)}, u32[]{:S(2)}) collective-permute-start(bf16[64,512]{1,0:T(8,128)(2,1)} %get-tuple-element.40), channel_id=1, source_target_pairs={{0,12},{4,8},{8,4},{12,0},{1,13},{5,9},{9,5},{13,1},{2,14},{6,10},... | collective-permute-start | bytes 196616 | tf_op jit(solution)/shard_map/ppermute | solution.py:39
  10.6 7.1 %collective-permute-start.6 = (bf16[64,512]{1,0:T(8,128)(2,1)}, bf16[64,512]{1,0:T(8,128)(2,1)S(1)}, u32[]{:S(2)}, u32[]{:S(2)}) collective-permute-start(bf16[64,512]{1,0:T(8,128)(2,1)} %get-tuple-element.46), channel_id=1, source_target_pairs={{0,8},{4,12},{8,0},{12,4},{1,9},{5,13},{9,1},{13,5},{2,10},{6,14},... | collective-permute-start | bytes 196616 | tf_op jit(solution)/shard_map/ppermute | solution.py:39
  10.6 7.9 %collective-permute-start.7 = (bf16[64,512]{1,0:T(8,128)(2,1)}, bf16[64,512]{1,0:T(8,128)(2,1)S(1)}, u32[]{:S(2)}, u32[]{:S(2)}) collective-permute-start(bf16[64,512]{1,0:T(8,128)(2,1)} %get-tuple-element.47), channel_id=1, source_target_pairs={{0,4},{4,0},{8,12},{12,8},{1,5},{5,1},{9,13},{13,9},{2,6},{6,2},{1... | collective-permute-start | bytes 196616 | tf_op jit(solution)/shard_map/ppermute | solution.py:39
  14.0 11.3 %collective-permute-start.3 = (bf16[64,1024]{1,0:T(8,128)(2,1)}, bf16[64,1024]{1,0:T(8,128)(2,1)S(1)}, u32[]{:S(2)}, u32[]{:S(2)}) collective-permute-start(bf16[64,1024]{1,0:T(8,128)(2,1)} %get-tuple-element.41), channel_id=1, source_target_pairs={{0,12},{4,8},{8,4},{12,0},{1,13},{5,9},{9,5},{13,1},{2,14},{6,10},... | collective-permute-start | bytes 393224 | tf_op jit(solution)/shard_map/ppermute | solution.py:39
  17.7 9.7 %collective-permute-start.4 = (bf16[64,1024]{1,0:T(8,128)(2,1)}, bf16[64,1024]{1,0:T(8,128)(2,1)S(1)}, u32[]{:S(2)}, u32[]{:S(2)}) collective-permute-start(bf16[64,1024]{1,0:T(8,128)(2,1)} %get-tuple-element.43), channel_id=1, source_target_pairs={{0,8},{4,12},{8,0},{12,4},{1,9},{5,13},{9,1},{13,5},{2,10},{6,14},... | collective-permute-start | bytes 393224 | tf_op jit(solution)/shard_map/ppermute | solution.py:39
  17.7 9.7 %collective-permute-start.5 = (bf16[64,1024]{1,0:T(8,128)(2,1)}, bf16[64,1024]{1,0:T(8,128)(2,1)S(1)}, u32[]{:S(2)}, u32[]{:S(2)}) collective-permute-start(bf16[64,1024]{1,0:T(8,128)(2,1)} %get-tuple-element.45), channel_id=1, source_target_pairs={{0,4},{4,0},{8,12},{12,8},{1,5},{5,1},{9,13},{13,9},{2,6},{6,2},{1... | collective-permute-start | bytes 393224 | tf_op jit(solution)/shard_map/ppermute | solution.py:39
  19.6 12.7 %copy-start.3 = (bf16[2,1024,64]{1,2,0:T(8,128)(2,1)S(1)}, bf16[2,1024,64]{1,2,0:T(8,128)(2,1)}, u32[]{:S(2)}) copy-start(bf16[2,1024,64]{1,2,0:T(8,128)(2,1)} %param.9) | copy-start | bytes 786436
  19.6 5.8 %collective-permute-start.8 = (bf16[384,128]{1,0:T(8,128)(2,1)S(1)}, bf16[384,128]{1,0:T(8,128)(2,1)S(1)}, u32[]{:S(2)}, u32[]{:S(2)}) collective-permute-start(bf16[384,128]{1,0:T(8,128)(2,1)S(1)} %h_part.1.refs_3_), channel_id=1, source_target_pairs={{0,2},{2,0},{1,3},{3,1},{4,6},{6,4},{5,7},{7,5},{8,10},{10,8},{9,1... | collective-permute-start | bytes 294920 | tf_op jit(solution)/shard_map/ppermute | solution.py:35
  20.0 20.8 %collective-permute-start.1 = (bf16[768,512]{1,0:T(8,128)(2,1)S(1)}, bf16[768,512]{1,0:T(8,128)(2,1)S(1)}, u32[]{:S(2)}, u32[]{:S(2)}) collective-permute-start(bf16[768,512]{1,0:T(8,128)(2,1)S(1)} %copy-done.2), channel_id=1, source_target_pairs={{0,2},{2,0},{1,3},{3,1},{4,6},{6,4},{5,7},{7,5},{8,10},{10,8},{9,1... | collective-permute-start | bytes 2359304 | tf_op jit(solution)/shard_map/ppermute | solution.py:35
  28.7 6.5 %collective-permute-start.10 = (bf16[512,512]{1,0:T(8,128)(2,1)S(1)}, bf16[512,512]{1,0:T(8,128)(2,1)S(1)}, u32[]{:S(2)}, u32[]{:S(2)}) collective-permute-start(bf16[512,512]{1,0:T(8,128)(2,1)S(1)} %collective-permute-done.refs_0_), channel_id=1, source_target_pairs={{0,1},{1,0},{2,3},{3,2},{4,5},{5,4},{6,7},{7,6},{8,9},{9,8},{10,11... | collective-permute-start | bytes 1572872 | tf_op jit(solution)/shard_map/ppermute | solution.py:35
  28.8 5.9 %collective-permute-start.9 = (bf16[64,1024]{1,0:T(8,128)(2,1)S(1)}, bf16[64,1024]{1,0:T(8,128)(2,1)S(1)}, u32[]{:S(2)}, u32[]{:S(2)}) collective-permute-start(bf16[64,1024]{1,0:T(8,128)(2,1)S(1)} %get-tuple-element.49), channel_id=1, source_target_pairs={{0,4},{4,0},{8,12},{12,8},{1,5},{5,1},{9,13},{13,9},{2,6},{6,2},{1... | collective-permute-start | bytes 393224 | tf_op jit(solution)/shard_map/ppermute | solution.py:39
  28.8 16.0 %collective-permute-start.11 = (bf16[64,1024]{1,0:T(8,128)(2,1)S(1)}, bf16[64,1024]{1,0:T(8,128)(2,1)S(1)}, u32[]{:S(2)}, u32[]{:S(2)}) collective-permute-start(bf16[64,1024]{1,0:T(8,128)(2,1)S(1)} %get-tuple-element.53), channel_id=1, source_target_pairs={{0,12},{4,8},{8,4},{12,0},{1,13},{5,9},{9,5},{13,1},{2,14},{6,10},... | collective-permute-start | bytes 393224 | tf_op jit(solution)/shard_map/ppermute | solution.py:39
  31.6 13.3 %collective-permute-start.12 = (bf16[64,1024]{1,0:T(8,128)(2,1)S(1)}, bf16[64,1024]{1,0:T(8,128)(2,1)S(1)}, u32[]{:S(2)}, u32[]{:S(2)}) collective-permute-start(bf16[64,1024]{1,0:T(8,128)(2,1)S(1)} %get-tuple-element.54), channel_id=1, source_target_pairs={{0,8},{4,12},{8,0},{12,4},{1,9},{5,13},{9,1},{13,5},{2,10},{6,14},... | collective-permute-start | bytes 393224 | tf_op jit(solution)/shard_map/ppermute | solution.py:39
  33.6 7.1 %copy-start = (bf16[2048,512]{1,0:T(8,128)(2,1)S(1)}, bf16[2048,512]{1,0:T(8,128)(2,1)}, u32[]{:S(2)}) copy-start(bf16[2048,512]{1,0:T(8,128)(2,1)} %w.3) | copy-start | bytes 6291460
  34.7 10.2 %collective-permute-start.13 = (bf16[384,128]{1,0:T(8,128)(2,1)S(1)}, bf16[384,128]{1,0:T(8,128)(2,1)S(1)}, u32[]{:S(2)}, u32[]{:S(2)}) collective-permute-start(bf16[384,128]{1,0:T(8,128)(2,1)S(1)} %u_part.1._.refs_5_), channel_id=1, source_target_pairs={{0,2},{2,0},{1,3},{3,1},{4,6},{6,4},{5,7},{7,5},{8,10},{10,8},{9,1... | collective-permute-start | bytes 294920 | tf_op jit(solution)/shard_map/ppermute | solution.py:35
  36.6 21.4 %collective-permute-start.22 = (bf16[768,512]{1,0:T(8,128)(2,1)S(1)}, bf16[768,512]{1,0:T(8,128)(2,1)S(1)}, u32[]{:S(2)}, u32[]{:S(2)}) collective-permute-start(bf16[768,512]{1,0:T(8,128)(2,1)S(1)} %get-tuple-element.65), channel_id=1, source_target_pairs={{0,2},{2,0},{1,3},{3,1},{4,6},{6,4},{5,7},{7,5},{8,10},{10,8},{9,1... | collective-permute-start | bytes 2359304 | tf_op jit(solution)/shard_map/ppermute | solution.py:35
  46.0 7.7 %collective-permute-start.17 = (bf16[64,512]{1,0:T(8,128)(2,1)S(1)}, bf16[64,512]{1,0:T(8,128)(2,1)S(1)}, u32[]{:S(2)}, u32[]{:S(2)}) collective-permute-start(bf16[64,512]{1,0:T(8,128)(2,1)S(1)} %get-tuple-element.59), channel_id=1, source_target_pairs={{0,4},{4,0},{8,12},{12,8},{1,5},{5,1},{9,13},{13,9},{2,6},{6,2},{1... | collective-permute-start | bytes 196616 | tf_op jit(solution)/shard_map/ppermute | solution.py:39
  48.6 5.9 %collective-permute-start.16 = (bf16[64,512]{1,0:T(8,128)(2,1)S(1)}, bf16[64,512]{1,0:T(8,128)(2,1)S(1)}, u32[]{:S(2)}, u32[]{:S(2)}) collective-permute-start(bf16[64,512]{1,0:T(8,128)(2,1)S(1)} %get-tuple-element.58), channel_id=1, source_target_pairs={{0,8},{4,12},{8,0},{12,4},{1,9},{5,13},{9,1},{13,5},{2,10},{6,14},... | collective-permute-start | bytes 196616 | tf_op jit(solution)/shard_map/ppermute | solution.py:39
  50.6 6.1 %collective-permute-start.15 = (bf16[64,512]{1,0:T(8,128)(2,1)S(1)}, bf16[64,512]{1,0:T(8,128)(2,1)S(1)}, u32[]{:S(2)}, u32[]{:S(2)}) collective-permute-start(bf16[64,512]{1,0:T(8,128)(2,1)S(1)} %get-tuple-element.57), channel_id=1, source_target_pairs={{0,12},{4,8},{8,4},{12,0},{1,13},{5,9},{9,5},{13,1},{2,14},{6,10},... | collective-permute-start | bytes 196616 | tf_op jit(solution)/shard_map/ppermute | solution.py:39
  51.4 6.7 %collective-permute-start.14 = (bf16[2,64,1024]{2,1,0:T(8,128)(2,1)S(1)}, bf16[2,64,1024]{2,1,0:T(8,128)(2,1)S(1)}, u32[]{:S(2)}, u32[]{:S(2)}) collective-permute-start(bf16[2,64,1024]{2,1,0:T(8,128)(2,1)S(1)} %sites.1.refs_0_), channel_id=1, source_target_pairs={{0,1},{1,0},{2,3},{3,2},{4,5},{5,4},{6,7},{7,6},{8,9},{9,8},{10,11... | collective-permute-start | bytes 786440 | tf_op jit(solution)/shard_map/ppermute | solution.py:35
  53.6 3.0 %collective-permute-start.18 = (bf16[64,512]{1,0:T(8,128)(2,1)S(1)}, bf16[64,512]{1,0:T(8,128)(2,1)S(1)}, u32[]{:S(2)}, u32[]{:S(2)}) collective-permute-start(bf16[64,512]{1,0:T(8,128)(2,1)S(1)} %get-tuple-element.61._.refs_2_), channel_id=1, source_target_pairs={{0,1},{1,0},{2,3},{3,2},{4,5},{5,4},{6,7},{7,6},{8,9},{9,8},{10,11... | collective-permute-start | bytes 196616 | tf_op jit(solution)/shard_map/ppermute | solution.py:35
  54.5 2.7 %collective-permute-start.21 = (bf16[64,512]{1,0:T(8,128)(2,1)S(1)}, bf16[64,512]{1,0:T(8,128)(2,1)S(1)}, u32[]{:S(2)}, u32[]{:S(2)}) collective-permute-start(bf16[64,512]{1,0:T(8,128)(2,1)S(1)} %collective-permute-done.17.refs_5_), channel_id=1, source_target_pairs={{0,1},{1,0},{2,3},{3,2},{4,5},{5,4},{6,7},{7,6},{8,9},{9,8},{10,11... | collective-permute-start | bytes 196616 | tf_op jit(solution)/shard_map/ppermute | solution.py:35
  56.6 1.3 %collective-permute-start.20 = (bf16[64,512]{1,0:T(8,128)(2,1)S(1)}, bf16[64,512]{1,0:T(8,128)(2,1)S(1)}, u32[]{:S(2)}, u32[]{:S(2)}) collective-permute-start(bf16[64,512]{1,0:T(8,128)(2,1)S(1)} %collective-permute-done.16.refs_4_), channel_id=1, source_target_pairs={{0,1},{1,0},{2,3},{3,2},{4,5},{5,4},{6,7},{7,6},{8,9},{9,8},{10,11... | collective-permute-start | bytes 196616 | tf_op jit(solution)/shard_map/ppermute | solution.py:35
  56.6 1.4 %collective-permute-start.19 = (bf16[64,512]{1,0:T(8,128)(2,1)S(1)}, bf16[64,512]{1,0:T(8,128)(2,1)S(1)}, u32[]{:S(2)}, u32[]{:S(2)}) collective-permute-start(bf16[64,512]{1,0:T(8,128)(2,1)S(1)} %collective-permute-done.15.refs_3_), channel_id=1, source_target_pairs={{0,1},{1,0},{2,3},{3,2},{4,5},{5,4},{6,7},{7,6},{8,9},{9,8},{10,11... | collective-permute-start | bytes 196616 | tf_op jit(solution)/shard_map/ppermute | solution.py:35

commit v15 on v14

--- a/solution.py
+++ b/solution.py
@@ -58,11 +58,11 @@
 def wanted_site(table, n_dp, s, q=0):
     n_pair = lax.axis_size("pair")
     core = lax.rem(lax.axis_index("pair") + n_pair - q, n_pair)
-    return table[0, core, lax.bitwise_xor(lax.axis_index("dp"), (n_dp - s) % n_dp)]
+    return table[0, core, lax.bitwise_xor(lax.axis_index("dp"), s)]
 
 
 def slot_of(owner, b, n_dp):
-    return lax.rem(n_dp - lax.bitwise_xor(lax.axis_index("dp"), owner[b]), n_dp)
+    return lax.bitwise_xor(lax.axis_index("dp"), owner[b])
 
 
 def pack_kernel(n_dp, n_mp, n_pair, table, down, up, w, *refs):
@@ -235,8 +235,8 @@
         [pltpu.VMEM((n_other, part, cols), BF16), pltpu.SemaphoreType.DMA((2 * away + 2 * n_other,))], mib=60,
     )(table, down, up, w)
     pieces = [shift(packed[2 * away + s - 1], "mp", s) for s in range(1, n_mp)]
-    ups = [swap(packed[s - 1], "dp", n_dp - s) for s in range(1, n_dp)]
-    downs = [swap(after(packed[away + s - 1], ups[0]), "dp", n_dp - s) for s in range(1, n_dp)]
+    ups = [swap(packed[s - 1], "dp", s) for s in range(1, n_dp)]
+    downs = [swap(after(packed[away + s - 1], ups[away - 1]), "dp", s) for s in range(1, n_dp)]
 
     def low_rank(act, own, maps, behind, name):
         mine = call(
@@ -252,7 +252,7 @@
             [shape(rank, act.shape[1])] * n_dp + [shape(tok, n_dp * rank)],
             [SMEM, VMEM] + [ANY] * len(behind) + [VMEM] * n_mp, [VMEM] * (n_dp + 1), flops=flops,
         )(owner, act, *behind, *parts)
-        return [grads[0]] + [swap(grads[s], "dp", n_dp - s) for s in range(1, n_dp)], wide
+        return [grads[0]] + [swap(grads[s], "dp", s) for s in range(1, n_dp)], wide
 
     h_parts = low_rank(gy, up, ups, ups[0], "h")
     gy_got = [shift(after(gy, *pieces), "mp", s) for s in range(1, n_mp)]
@@ -268,7 +268,7 @@
         [ANY, ANY, row_block(feat)] + [whole(part, cols)] * len(parts),
         [row_block(cols)] * n_other + [whole(feat, cols)] * n_other,
         grid=(TILES,),
-    )(u_parts[0], down_back[away], x, *parts)
+    )(u_parts[0], down_back[1], x, *parts)
     w_rows = sent[n_other:]
     y_got = [shift(sent[s - 1], "mp", n_mp - s) for s in range(1, n_mp)]
     back, picks = call(

time: 59.8 us -> 60.1 us (level)
  starting transfers between devices: 25.8 us -> 26.9 us
  waiting for transfers between devices: 15.3 us -> 14.6 us
    ppermute x12, starting transfers between devices: 17.4 us -> 18 us  [swap(): lax.ppermute(value, axis, [(i, i ^ mask) for i in range(lax.axis_size(axi...]
  transfers between devices with their start and end apart: 23 -> 23, of which waited for: 9 -> 9; matrix products, arithmetic and copies ran while one was open for 0% -> 0% of each run, Pallas kernels for 22% -> 21%
where the time goes in v15:
time: 60.1 us; the launch traced here: 60 us
  starting transfers between devices  26.9 us (45%)
  Pallas kernels  17.7 us (29%)
  waiting for transfers between devices  14.6 us (24%)
  between operations  0.82 us (1%)
    ppermute x12, starting transfers between devices, swap(): lax.ppermute(value, axis, [(i, i ^ mask) for i in range(lax.axis_size(axi...  18 us
    ppermute x11, starting transfers between devices, shift(): lax.ppermute(value, axis, [(i, (i + by) % size) for i in range(size)])  8.81 us
    ppermute x12, waiting for transfers between devices, swap(): lax.ppermute(value, axis, [(i, i ^ mask) for i in range(lax.axis_size(axi...  7.84 us
    ppermute x11, waiting for transfers between devices, shift(): lax.ppermute(value, axis, [(i, (i + by) % size) for i in range(size)])  6.74 us
    pallas_call x1, Pallas kernels, shards(): call(functools.partial(back_kernel, n_dp, n_mp), 'back', [shape(tok, feat...  4.07 us
    pallas_call x1, Pallas kernels, shards(): call(functools.partial(pack_kernel, n_dp, n_mp, n_pair), 'pack', [shape(r...  3.28 us
    pallas_call x2, Pallas kernels, gradient(): call(functools.partial(grad_kernel, n_dp, n_mp, len(behind)), name + '_gr...  2.45 us
    pallas_call x2, Pallas kernels, low_rank(): call(functools.partial(reduce_kernel, n_dp), name + '_part', shape(tok //...  2.42 us
  transfers between devices with their start and end apart: 23, of which 9 were waited for; matrix products, arithmetic and copies ran while one was open for 0% of the time, Pallas kernels for 21%

profile of v15, /device:TPU:0, one launch (start us, length us, event | category | flops | bytes accessed | tf_op | source)
XLA Modules:
  0.0 60.0 jit_solution(10891074929388365623)
XLA Ops:
  0.7 3.3 %pack.1 = (bf16[64,512]{1,0:T(8,128)(2,1)}, bf16[64,512]{1,0:T(8,128)(2,1)}, bf16[64,512]{1,0:T(8,128)(2,1)}, bf16[64,1024]{1,0:T(8,128)(2,1)}, bf16[64,1024]{1,...) custom-call(s32[1,2,4]{2,1,0:T(2,128)} %table.9, bf16[2,64,1024]{2,1,0:T(8,128)(2,1)} %bitcast.2, ...), custom_call_target="tpu_custom_call" | custom-call | flops 1 | bytes 1 | tf_op jit(solution)/shard_map/pack/pallas_call | solution.py:231
  4.0 3.0 %collective-permute-start = (bf16[512,512]{1,0:T(8,128)(2,1)}, bf16[512,512]{1,0:T(8,128)(2,1)S(1)}, u32[]{:S(2)}, u32[]{:S(2)}) collective-permute-start(bf16[512,512]{1,0:T(8,128)(2,1)} %get-tuple-element.37), channel_id=1, source_target_pairs={{0,2},{2,0},{1,3},{3,1},{4,6},{6,4},{5,7},{7,5},{8,10},{10,8},{9,1... | collective-permute-start | bytes 1572872 | tf_op jit(solution)/shard_map/ppermute | solution.py:35
  7.0 3.6 %collective-permute-start.2 = (bf16[64,512]{1,0:T(8,128)(2,1)}, bf16[64,512]{1,0:T(8,128)(2,1)S(1)}, u32[]{:S(2)}, u32[]{:S(2)}) collective-permute-start(bf16[64,512]{1,0:T(8,128)(2,1)} %get-tuple-element.40), channel_id=1, source_target_pairs={{0,12},{4,8},{8,4},{12,0},{1,13},{5,9},{9,5},{13,1},{2,14},{6,10},... | collective-permute-start | bytes 196616 | tf_op jit(solution)/shard_map/ppermute | solution.py:39
  10.6 0.8 %collective-permute-start.7 = (bf16[64,512]{1,0:T(8,128)(2,1)}, bf16[64,512]{1,0:T(8,128)(2,1)S(1)}, u32[]{:S(2)}, u32[]{:S(2)}) collective-permute-start(bf16[64,512]{1,0:T(8,128)(2,1)} %get-tuple-element.47), channel_id=1, source_target_pairs={{0,8},{4,12},{8,0},{12,4},{1,9},{5,13},{9,1},{13,5},{2,10},{6,14},... | collective-permute-start | bytes 196616 | tf_op jit(solution)/shard_map/ppermute | solution.py:39
  11.4 2.1 %collective-permute-done.2.refs_2_ = bf16[64,512]{1,0:T(8,128)(2,1)S(1)} collective-permute-done((bf16[64,512]{1,0:T(8,128)(2,1)}, bf16[64,512]{1,0:T(8,128)(2,1)S(1)}, u32[]{:S(2)}, u32[]{:S(2)}) %collective-permute-start.2) | collective-permute-done | bytes 65568 | tf_op jit(solution)/shard_map/ppermute | solution.py:39
  13.5 4.7 %collective-permute-start.4 = (bf16[64,1024]{1,0:T(8,128)(2,1)}, bf16[64,1024]{1,0:T(8,128)(2,1)S(1)}, u32[]{:S(2)}, u32[]{:S(2)}) collective-permute-start(bf16[64,1024]{1,0:T(8,128)(2,1)} %get-tuple-element.43), channel_id=1, source_target_pairs={{0,8},{4,12},{8,0},{12,4},{1,9},{5,13},{9,1},{13,5},{2,10},{6,14},... | collective-permute-start | bytes 393224 | tf_op jit(solution)/shard_map/ppermute | solution.py:39
  18.3 1.1 %h_part.1.refs_3_ = bf16[384,128]{1,0:T(8,128)(2,1)S(1)} custom-call(s32[12]{0:T(128)S(1)} %copy-done.6, s32[1,2,4]{2,1,0:T(2,128)S(1)} %copy-done.5, bf16[768,512]{1,0:T(8,128)(2,1)S(1)} %copy-done.2, bf16[64,512]{1,0:T(8,128)(2,1)S(1)} %collective-permute-done.6._.refs_0_, bf16[2,64,512]{2,1,0:T(8,128)(2,1)S(1)} %copy-done.4, ...), custom_call_target="tpu_custom_call" | custom-call | flops 1 | bytes 1 | tf_op jit(solution)/shard_map/h_part/pallas_call | solution.py:242
  19.4 0.6 %collective-permute-start.8 = (bf16[384,128]{1,0:T(8,128)(2,1)S(1)}, bf16[384,128]{1,0:T(8,128)(2,1)S(1)}, u32[]{:S(2)}, u32[]{:S(2)}) collective-permute-start(bf16[384,128]{1,0:T(8,128)(2,1)S(1)} %h_part.1.refs_3_), channel_id=1, source_target_pairs={{0,2},{2,0},{1,3},{3,1},{4,6},{6,4},{5,7},{7,5},{8,10},{10,8},{9,1... | collective-permute-start | bytes 294920 | tf_op jit(solution)/shard_map/ppermute | solution.py:35
  20.0 1.8 %collective-permute-start.1 = (bf16[768,512]{1,0:T(8,128)(2,1)S(1)}, bf16[768,512]{1,0:T(8,128)(2,1)S(1)}, u32[]{:S(2)}, u32[]{:S(2)}) collective-permute-start(bf16[768,512]{1,0:T(8,128)(2,1)S(1)} %copy-done.2), channel_id=1, source_target_pairs={{0,2},{2,0},{1,3},{3,1},{4,6},{6,4},{5,7},{7,5},{8,10},{10,8},{9,1... | collective-permute-start | bytes 2359304 | tf_op jit(solution)/shard_map/ppermute | solution.py:35
  21.8 3.3 %collective-permute-done.8.refs_4_ = bf16[384,128]{1,0:T(8,128)(2,1)S(1)} collective-permute-done((bf16[384,128]{1,0:T(8,128)(2,1)S(1)}, bf16[384,128]{1,0:T(8,128)(2,1)S(1)}, u32[]{:S(2)}, u32[]{:S(2)}) %collective-permute-start.8) | collective-permute-done | bytes 98336 | tf_op jit(solution)/shard_map/ppermute | solution.py:35
  25.2 2.1 %collective-permute-done.4.refs_1_.refs_7_ = bf16[64,1024]{1,0:T(8,128)(2,1)S(1)} collective-permute-done((bf16[64,1024]{1,0:T(8,128)(2,1)}, bf16[64,1024]{1,0:T(8,128)(2,1)S(1)}, u32[]{:S(2)}, u32[]{:S(2)}) %collective-permute-start.4) | collective-permute-done | bytes 131104 | tf_op jit(solution)/shard_map/ppermute | solution.py:39
  27.3 1.3 %down_grad.1 = (bf16[64,1024]{1,0:T(8,128)(2,1)S(1)}, bf16[64,1024]{1,0:T(8,128)(2,1)S(1)}, bf16[64,1024]{1,0:T(8,128)(2,1)S(1)}, bf16[64,1024]{1,0:T(8,128)(2,1)S(1)}, bf16[768,256]{1,0:T(8,128)(2,1)S(1)}) custom-call(s32[12]{0:T(128)S(1)} %copy-done.6, bf16[768,1024]{1,0:T(8,128)(2,1)S(1)} %copy-done.1, ...), custom_call_target="tpu_custom_call" | custom-call | flops 15000000512 | bytes 1 | tf_op jit(solution)/shard_map/down_grad/pallas_call | solution.py:250
  28.7 2.0 %collective-permute-start.9 = (bf16[64,1024]{1,0:T(8,128)(2,1)S(1)}, bf16[64,1024]{1,0:T(8,128)(2,1)S(1)}, u32[]{:S(2)}, u32[]{:S(2)}) collective-permute-start(bf16[64,1024]{1,0:T(8,128)(2,1)S(1)} %get-tuple-element.49), channel_id=1, source_target_pairs={{0,4},{4,0},{8,12},{12,8},{1,5},{5,1},{9,13},{13,9},{2,6},{6,2},{1... | collective-permute-start | bytes 393224 | tf_op jit(solution)/shard_map/ppermute | solution.py:39
  30.7 1.0 %collective-permute-start.11 = (bf16[64,1024]{1,0:T(8,128)(2,1)S(1)}, bf16[64,1024]{1,0:T(8,128)(2,1)S(1)}, u32[]{:S(2)}, u32[]{:S(2)}) collective-permute-start(bf16[64,1024]{1,0:T(8,128)(2,1)S(1)} %get-tuple-element.53), channel_id=1, source_target_pairs={{0,8},{4,12},{8,0},{12,4},{1,9},{5,13},{9,1},{13,5},{2,10},{6,14},... | collective-permute-start | bytes 393224 | tf_op jit(solution)/shard_map/ppermute | solution.py:39
  31.7 1.5 %collective-permute-start.12 = (bf16[64,1024]{1,0:T(8,128)(2,1)S(1)}, bf16[64,1024]{1,0:T(8,128)(2,1)S(1)}, u32[]{:S(2)}, u32[]{:S(2)}) collective-permute-start(bf16[64,1024]{1,0:T(8,128)(2,1)S(1)} %get-tuple-element.54), channel_id=1, source_target_pairs={{0,12},{4,8},{8,4},{12,0},{1,13},{5,9},{9,5},{13,1},{2,14},{6,10},... | collective-permute-start | bytes 393224 | tf_op jit(solution)/shard_map/ppermute | solution.py:39
  33.2 1.3 %u_part.1._.refs_5_ = bf16[384,128]{1,0:T(8,128)(2,1)S(1)} custom-call(s32[12]{0:T(128)S(1)} %copy-done.6, s32[1,2,4]{2,1,0:T(2,128)S(1)} %copy-done.5, bf16[768,1024]{1,0:T(8,128)(2,1)S(1)} %copy-done.1, bf16[768,256]{1,0:T(8,128)(2,1)S(1)} %get-tuple-element.48._.refs_4_, bf16[2,64,1024]{2,1,0:T(8,128)(2,1)S(1)} %bitcast.3, ...), custom_call_target="tpu_custom_call" | custom-call | flops 1 | bytes 1 | tf_op jit(solution)/shard_map/u_part/pallas_call | solution.py:242
  34.5 2.5 %collective-permute-done.9.__.refs_1_ = bf16[64,1024]{1,0:T(8,128)(2,1)S(1)} collective-permute-done((bf16[64,1024]{1,0:T(8,128)(2,1)S(1)}, bf16[64,1024]{1,0:T(8,128)(2,1)S(1)}, u32[]{:S(2)}, u32[]{:S(2)}) %collective-permute-start.9) | collective-permute-done | bytes 131104 | tf_op jit(solution)/shard_map/ppermute | solution.py:39
  37.0 0.5 collective-permute-start.13
  37.5 1.4 %y_send.1 = (bf16[768,512]{1,0:T(8,128)(2,1)S(1)}, bf16[1024,512]{1,0:T(8,128)(2,1)S(1)}) custom-call(bf16[384,128]{1,0:T(8,128)(2,1)S(1)} %u_part.1._.refs_5_, bf16[64,1024]{1,0:T(8,128)(2,1)S(1)} %collective-permute-done.9.__.refs_1_, bf16[768,1024]{1,0:T(8,128)(2,1)S(1)} %copy-done.1, bf16[512,512]{1,0:T(8,128)(2,1)S(1)} %collective-permute-done.refs_0_, ...), custom_call_target="tpu_custom_call" | custom-call | flops 1 | bytes 1 | tf_op jit(solution)/shard_map/y_send/pallas_call | solution.py:265
  38.9 1.6 %collective-permute-start.22 = (bf16[768,512]{1,0:T(8,128)(2,1)S(1)}, bf16[768,512]{1,0:T(8,128)(2,1)S(1)}, u32[]{:S(2)}, u32[]{:S(2)}) collective-permute-start(bf16[768,512]{1,0:T(8,128)(2,1)S(1)} %get-tuple-element.65), channel_id=1, source_target_pairs={{0,2},{2,0},{1,3},{3,1},{4,6},{6,4},{5,7},{7,5},{8,10},{10,8},{9,1... | collective-permute-start | bytes 2359304 | tf_op jit(solution)/shard_map/ppermute | solution.py:35
  40.5 4.1 %back.1 = (bf16[768,1024]{1,0:T(8,128)(2,1)}, s32[8,128]{1,0:T(8,128)S(1)}) custom-call(s32[1,2,4]{2,1,0:T(2,128)S(1)} %copy-done.5, bf16[2048,512]{1,0:T(8,128)(2,1)S(1)} %copy-done, bf16[768,512]{1,0:T(8,128)(2,1)S(1)} %copy-done.2, bf16[768,512]{1,0:T(8,128)(2,1)S(1)} %collective-permute-done.1.refs_2_.refs_4_, ...), custom_call_target="tpu_custom_call" | custom-call | flops 1 | bytes 1 | tf_op jit(solution)/shard_map/back/pallas_call | solution.py:274
  44.6 1.1 %up_grad.1 = (bf16[64,512]{1,0:T(8,128)(2,1)S(1)}, bf16[64,512]{1,0:T(8,128)(2,1)S(1)}, bf16[64,512]{1,0:T(8,128)(2,1)S(1)}, bf16[64,512]{1,0:T(8,128)(2,1)S(1)}, bf16[768,256]{1,0:T(8,128)(2,1)S(1)}) custom-call(s32[12]{0:T(128)S(1)} %copy-done.6, bf16[768,512]{1,0:T(8,128)(2,1)S(1)} %copy-done.2, s32[8,128]{1,0:T(8,128)S(1)} %get-tuple-element.52.refs_0_.picks, ...), custom_call_target="tpu_custom_call" | custom-call | flops 15000000512 | bytes 1 | tf_op jit(solution)/shard_map/up_grad/pallas_call | solution.py:250
  45.7 3.6 %collective-permute-start.17 = (bf16[64,512]{1,0:T(8,128)(2,1)S(1)}, bf16[64,512]{1,0:T(8,128)(2,1)S(1)}, u32[]{:S(2)}, u32[]{:S(2)}) collective-permute-start(bf16[64,512]{1,0:T(8,128)(2,1)S(1)} %get-tuple-element.59), channel_id=1, source_target_pairs={{0,12},{4,8},{8,4},{12,0},{1,13},{5,9},{9,5},{13,1},{2,14},{6,10},... | collective-permute-start | bytes 196616 | tf_op jit(solution)/shard_map/ppermute | solution.py:39
  49.3 0.9 %collective-permute-start.15 = (bf16[64,512]{1,0:T(8,128)(2,1)S(1)}, bf16[64,512]{1,0:T(8,128)(2,1)S(1)}, u32[]{:S(2)}, u32[]{:S(2)}) collective-permute-start(bf16[64,512]{1,0:T(8,128)(2,1)S(1)} %get-tuple-element.57), channel_id=1, source_target_pairs={{0,4},{4,0},{8,12},{12,8},{1,5},{5,1},{9,13},{13,9},{2,6},{6,2},{1... | collective-permute-start | bytes 196616 | tf_op jit(solution)/shard_map/ppermute | solution.py:39
  50.6 2.2 %y_own.1.refs_10_ = bf16[768,512]{1,0:T(8,128)(2,1)S(1)} custom-call(s32[1,2,4]{2,1,0:T(2,128)S(1)} %copy-done.5, bf16[2048,512]{1,0:T(8,128)(2,1)S(1)} %copy-done, bf16[768,1024]{1,0:T(8,128)(2,1)S(1)} %copy-done.1, bf16[768,256]{1,0:T(8,128)(2,1)S(1)} %get-tuple-element.60.wide, bf16[2,64,512]{2,1,0:T(8,128)(2,1)S(1)} %copy-done.4, ...), custom_call_target="tpu_custom_call" | custom-call | flops 15000000512 | bytes 1 | tf_op jit(solution)/shard_map/y_own/pallas_call | solution.py:284
  52.8 0.5 collective-permute-start.18
  53.3 1.2 %collective-permute-done.16.refs_4_ = bf16[64,512]{1,0:T(8,128)(2,1)S(1)} collective-permute-done((bf16[64,512]{1,0:T(8,128)(2,1)S(1)}, bf16[64,512]{1,0:T(8,128)(2,1)S(1)}, u32[]{:S(2)}, u32[]{:S(2)}) %collective-permute-start.16) | collective-permute-done | bytes 65568 | tf_op jit(solution)/shard_map/ppermute | solution.py:39
  54.5 0.5 collective-permute-start.20
  55.0 0.7 %collective-permute-done.21.refs_9_ = bf16[64,512]{1,0:T(8,128)(2,1)S(1)} collective-permute-done((bf16[64,512]{1,0:T(8,128)(2,1)S(1)}, bf16[64,512]{1,0:T(8,128)(2,1)S(1)}, u32[]{:S(2)}, u32[]{:S(2)}) %collective-permute-start.21) | collective-permute-done | bytes 65568 | tf_op jit(solution)/shard_map/ppermute | solution.py:35
  55.9 0.4 collective-permute-done.19.refs_7_
  56.2 2.2 %collective-permute-done.22.refs_11_ = bf16[768,512]{1,0:T(8,128)(2,1)S(1)} collective-permute-done((bf16[768,512]{1,0:T(8,128)(2,1)S(1)}, bf16[768,512]{1,0:T(8,128)(2,1)S(1)}, u32[]{:S(2)}, u32[]{:S(2)}) %collective-permute-start.22) | collective-permute-done | bytes 786464 | tf_op jit(solution)/shard_map/ppermute | solution.py:35
  58.4 1.5 %last.1 = (f32[2,64,1024]{2,1,0:T(8,128)}, f32[2,64,512]{2,1,0:T(8,128)}, bf16[768,512]{1,0:T(8,128)(2,1)}) custom-call(s32[8,128]{1,0:T(8,128)S(1)} %get-tuple-element.52.refs_0_.picks, bf16[2,64,1024]{2,1,0:T(8,128)(2,1)S(1)} %sites.1.refs_0_, bf16[2,64,1024]{2,1,0:T(8,128)(2,1)S(1)} %collective-permute-done.14.refs_1_, ...), custom_call_target="tpu_custom_call" | custom-call | flops 1 | bytes 1 | tf_op jit(solution)/shard_map/last/pallas_call | solution.py:299
  (38 shorter events, 0.8 us)
Async XLA Ops:
  0.6 17.6 %copy-start.4 = (bf16[2,64,512]{2,1,0:T(8,128)(2,1)S(1)}, bf16[2,64,512]{2,1,0:T(8,128)(2,1)}, u32[]{:S(2)}) copy-start(bf16[2,64,512]{2,1,0:T(8,128)(2,1)} %own_up.1) | copy-start | bytes 393220
  0.6 17.6 %copy-start.5 = (s32[1,2,4]{2,1,0:T(2,128)S(1)}, s32[1,2,4]{2,1,0:T(2,128)}, u32[]{:S(2)}) copy-start(s32[1,2,4]{2,1,0:T(2,128)} %table.9) | copy-start | bytes 100
  0.7 17.6 %copy-start.2 = (bf16[768,512]{1,0:T(8,128)(2,1)S(1)}, bf16[768,512]{1,0:T(8,128)(2,1)}, u32[]{:S(2)}) copy-start(bf16[768,512]{1,0:T(8,128)(2,1)} %act.7) | copy-start | bytes 2359300
  0.7 17.6 %copy-start.6 = (s32[12]{0:T(128)S(1)}, s32[12]{0:T(128)}, u32[]{:S(2)}) copy-start(s32[12]{0:T(128)} %owner.7) | copy-start | bytes 148
  0.7 26.6 %copy-start.1 = (bf16[768,1024]{1,0:T(8,128)(2,1)S(1)}, bf16[768,1024]{1,0:T(8,128)(2,1)}, u32[]{:S(2)}) copy-start(bf16[768,1024]{1,0:T(8,128)(2,1)} %x.3) | copy-start | bytes 4718596
  4.0 16.0 %collective-permute-start = (bf16[512,512]{1,0:T(8,128)(2,1)}, bf16[512,512]{1,0:T(8,128)(2,1)S(1)}, u32[]{:S(2)}, u32[]{:S(2)}) collective-permute-start(bf16[512,512]{1,0:T(8,128)(2,1)} %get-tuple-element.37), channel_id=1, source_target_pairs={{0,2},{2,0},{1,3},{3,1},{4,6},{6,4},{5,7},{7,5},{8,10},{10,8},{9,1... | collective-permute-start | bytes 1572872 | tf_op jit(solution)/shard_map/ppermute | solution.py:35
  7.0 6.5 %collective-permute-start.2 = (bf16[64,512]{1,0:T(8,128)(2,1)}, bf16[64,512]{1,0:T(8,128)(2,1)S(1)}, u32[]{:S(2)}, u32[]{:S(2)}) collective-permute-start(bf16[64,512]{1,0:T(8,128)(2,1)} %get-tuple-element.40), channel_id=1, source_target_pairs={{0,12},{4,8},{8,4},{12,0},{1,13},{5,9},{9,5},{13,1},{2,14},{6,10},... | collective-permute-start | bytes 196616 | tf_op jit(solution)/shard_map/ppermute | solution.py:39
  10.6 7.6 %collective-permute-start.6 = (bf16[64,512]{1,0:T(8,128)(2,1)}, bf16[64,512]{1,0:T(8,128)(2,1)S(1)}, u32[]{:S(2)}, u32[]{:S(2)}) collective-permute-start(bf16[64,512]{1,0:T(8,128)(2,1)} %get-tuple-element.46), channel_id=1, source_target_pairs={{0,4},{4,0},{8,12},{12,8},{1,5},{5,1},{9,13},{13,9},{2,6},{6,2},{1... | collective-permute-start | bytes 196616 | tf_op jit(solution)/shard_map/ppermute | solution.py:39
  10.6 7.6 %collective-permute-start.7 = (bf16[64,512]{1,0:T(8,128)(2,1)}, bf16[64,512]{1,0:T(8,128)(2,1)S(1)}, u32[]{:S(2)}, u32[]{:S(2)}) collective-permute-start(bf16[64,512]{1,0:T(8,128)(2,1)} %get-tuple-element.47), channel_id=1, source_target_pairs={{0,8},{4,12},{8,0},{12,4},{1,9},{5,13},{9,1},{13,5},{2,10},{6,14},... | collective-permute-start | bytes 196616 | tf_op jit(solution)/shard_map/ppermute | solution.py:39
  13.5 11.7 %collective-permute-start.3 = (bf16[64,1024]{1,0:T(8,128)(2,1)}, bf16[64,1024]{1,0:T(8,128)(2,1)S(1)}, u32[]{:S(2)}, u32[]{:S(2)}) collective-permute-start(bf16[64,1024]{1,0:T(8,128)(2,1)} %get-tuple-element.41), channel_id=1, source_target_pairs={{0,4},{4,0},{8,12},{12,8},{1,5},{5,1},{9,13},{13,9},{2,6},{6,2},{1... | collective-permute-start | bytes 393224 | tf_op jit(solution)/shard_map/ppermute | solution.py:39
  13.5 13.8 %collective-permute-start.4 = (bf16[64,1024]{1,0:T(8,128)(2,1)}, bf16[64,1024]{1,0:T(8,128)(2,1)S(1)}, u32[]{:S(2)}, u32[]{:S(2)}) collective-permute-start(bf16[64,1024]{1,0:T(8,128)(2,1)} %get-tuple-element.43), channel_id=1, source_target_pairs={{0,8},{4,12},{8,0},{12,4},{1,9},{5,13},{9,1},{13,5},{2,10},{6,14},... | collective-permute-start | bytes 393224 | tf_op jit(solution)/shard_map/ppermute | solution.py:39
  18.2 9.1 %collective-permute-start.5 = (bf16[64,1024]{1,0:T(8,128)(2,1)}, bf16[64,1024]{1,0:T(8,128)(2,1)S(1)}, u32[]{:S(2)}, u32[]{:S(2)}) collective-permute-start(bf16[64,1024]{1,0:T(8,128)(2,1)} %get-tuple-element.45), channel_id=1, source_target_pairs={{0,12},{4,8},{8,4},{12,0},{1,13},{5,9},{9,5},{13,1},{2,14},{6,10},... | collective-permute-start | bytes 393224 | tf_op jit(solution)/shard_map/ppermute | solution.py:39
  19.4 13.8 %copy-start.3 = (bf16[2,1024,64]{1,2,0:T(8,128)(2,1)S(1)}, bf16[2,1024,64]{1,2,0:T(8,128)(2,1)}, u32[]{:S(2)}) copy-start(bf16[2,1024,64]{1,2,0:T(8,128)(2,1)} %param.9) | copy-start | bytes 786436
  19.4 5.8 %collective-permute-start.8 = (bf16[384,128]{1,0:T(8,128)(2,1)S(1)}, bf16[384,128]{1,0:T(8,128)(2,1)S(1)}, u32[]{:S(2)}, u32[]{:S(2)}) collective-permute-start(bf16[384,128]{1,0:T(8,128)(2,1)S(1)} %h_part.1.refs_3_), channel_id=1, source_target_pairs={{0,2},{2,0},{1,3},{3,1},{4,6},{6,4},{5,7},{7,5},{8,10},{10,8},{9,1... | collective-permute-start | bytes 294920 | tf_op jit(solution)/shard_map/ppermute | solution.py:35
  20.0 20.5 %collective-permute-start.1 = (bf16[768,512]{1,0:T(8,128)(2,1)S(1)}, bf16[768,512]{1,0:T(8,128)(2,1)S(1)}, u32[]{:S(2)}, u32[]{:S(2)}) collective-permute-start(bf16[768,512]{1,0:T(8,128)(2,1)S(1)} %copy-done.2), channel_id=1, source_target_pairs={{0,2},{2,0},{1,3},{3,1},{4,6},{6,4},{5,7},{7,5},{8,10},{10,8},{9,1... | collective-permute-start | bytes 2359304 | tf_op jit(solution)/shard_map/ppermute | solution.py:35
  28.6 8.9 %collective-permute-start.10 = (bf16[512,512]{1,0:T(8,128)(2,1)S(1)}, bf16[512,512]{1,0:T(8,128)(2,1)S(1)}, u32[]{:S(2)}, u32[]{:S(2)}) collective-permute-start(bf16[512,512]{1,0:T(8,128)(2,1)S(1)} %collective-permute-done.refs_0_), channel_id=1, source_target_pairs={{0,1},{1,0},{2,3},{3,2},{4,5},{5,4},{6,7},{7,6},{8,9},{9,8},{10,11... | collective-permute-start | bytes 1572872 | tf_op jit(solution)/shard_map/ppermute | solution.py:35
  28.7 8.3 %collective-permute-start.9 = (bf16[64,1024]{1,0:T(8,128)(2,1)S(1)}, bf16[64,1024]{1,0:T(8,128)(2,1)S(1)}, u32[]{:S(2)}, u32[]{:S(2)}) collective-permute-start(bf16[64,1024]{1,0:T(8,128)(2,1)S(1)} %get-tuple-element.49), channel_id=1, source_target_pairs={{0,4},{4,0},{8,12},{12,8},{1,5},{5,1},{9,13},{13,9},{2,6},{6,2},{1... | collective-permute-start | bytes 393224 | tf_op jit(solution)/shard_map/ppermute | solution.py:39
  30.7 13.9 %collective-permute-start.11 = (bf16[64,1024]{1,0:T(8,128)(2,1)S(1)}, bf16[64,1024]{1,0:T(8,128)(2,1)S(1)}, u32[]{:S(2)}, u32[]{:S(2)}) collective-permute-start(bf16[64,1024]{1,0:T(8,128)(2,1)S(1)} %get-tuple-element.53), channel_id=1, source_target_pairs={{0,8},{4,12},{8,0},{12,4},{1,9},{5,13},{9,1},{13,5},{2,10},{6,14},... | collective-permute-start | bytes 393224 | tf_op jit(solution)/shard_map/ppermute | solution.py:39
  31.7 12.9 %collective-permute-start.12 = (bf16[64,1024]{1,0:T(8,128)(2,1)S(1)}, bf16[64,1024]{1,0:T(8,128)(2,1)S(1)}, u32[]{:S(2)}, u32[]{:S(2)}) collective-permute-start(bf16[64,1024]{1,0:T(8,128)(2,1)S(1)} %get-tuple-element.54), channel_id=1, source_target_pairs={{0,12},{4,8},{8,4},{12,0},{1,13},{5,9},{9,5},{13,1},{2,14},{6,10},... | collective-permute-start | bytes 393224 | tf_op jit(solution)/shard_map/ppermute | solution.py:39
  34.5 6.0 %copy-start = (bf16[2048,512]{1,0:T(8,128)(2,1)S(1)}, bf16[2048,512]{1,0:T(8,128)(2,1)}, u32[]{:S(2)}) copy-start(bf16[2048,512]{1,0:T(8,128)(2,1)} %w.3) | copy-start | bytes 6291460
  37.0 7.6 %collective-permute-start.13 = (bf16[384,128]{1,0:T(8,128)(2,1)S(1)}, bf16[384,128]{1,0:T(8,128)(2,1)S(1)}, u32[]{:S(2)}, u32[]{:S(2)}) collective-permute-start(bf16[384,128]{1,0:T(8,128)(2,1)S(1)} %u_part.1._.refs_5_), channel_id=1, source_target_pairs={{0,2},{2,0},{1,3},{3,1},{4,6},{6,4},{5,7},{7,5},{8,10},{10,8},{9,1... | collective-permute-start | bytes 294920 | tf_op jit(solution)/shard_map/ppermute | solution.py:35
  38.9 19.5 %collective-permute-start.22 = (bf16[768,512]{1,0:T(8,128)(2,1)S(1)}, bf16[768,512]{1,0:T(8,128)(2,1)S(1)}, u32[]{:S(2)}, u32[]{:S(2)}) collective-permute-start(bf16[768,512]{1,0:T(8,128)(2,1)S(1)} %get-tuple-element.65), channel_id=1, source_target_pairs={{0,2},{2,0},{1,3},{3,1},{4,6},{6,4},{5,7},{7,5},{8,10},{10,8},{9,1... | collective-permute-start | bytes 2359304 | tf_op jit(solution)/shard_map/ppermute | solution.py:35
  45.7 7.1 %collective-permute-start.17 = (bf16[64,512]{1,0:T(8,128)(2,1)S(1)}, bf16[64,512]{1,0:T(8,128)(2,1)S(1)}, u32[]{:S(2)}, u32[]{:S(2)}) collective-permute-start(bf16[64,512]{1,0:T(8,128)(2,1)S(1)} %get-tuple-element.59), channel_id=1, source_target_pairs={{0,12},{4,8},{8,4},{12,0},{1,13},{5,9},{9,5},{13,1},{2,14},{6,10},... | collective-permute-start | bytes 196616 | tf_op jit(solution)/shard_map/ppermute | solution.py:39
  49.3 5.2 %collective-permute-start.16 = (bf16[64,512]{1,0:T(8,128)(2,1)S(1)}, bf16[64,512]{1,0:T(8,128)(2,1)S(1)}, u32[]{:S(2)}, u32[]{:S(2)}) collective-permute-start(bf16[64,512]{1,0:T(8,128)(2,1)S(1)} %get-tuple-element.58), channel_id=1, source_target_pairs={{0,8},{4,12},{8,0},{12,4},{1,9},{5,13},{9,1},{13,5},{2,10},{6,14},... | collective-permute-start | bytes 196616 | tf_op jit(solution)/shard_map/ppermute | solution.py:39
  49.3 5.2 %collective-permute-start.15 = (bf16[64,512]{1,0:T(8,128)(2,1)S(1)}, bf16[64,512]{1,0:T(8,128)(2,1)S(1)}, u32[]{:S(2)}, u32[]{:S(2)}) collective-permute-start(bf16[64,512]{1,0:T(8,128)(2,1)S(1)} %get-tuple-element.57), channel_id=1, source_target_pairs={{0,4},{4,0},{8,12},{12,8},{1,5},{5,1},{9,13},{13,9},{2,6},{6,2},{1... | collective-permute-start | bytes 196616 | tf_op jit(solution)/shard_map/ppermute | solution.py:39
  50.5 5.7 %collective-permute-start.14 = (bf16[2,64,1024]{2,1,0:T(8,128)(2,1)S(1)}, bf16[2,64,1024]{2,1,0:T(8,128)(2,1)S(1)}, u32[]{:S(2)}, u32[]{:S(2)}) collective-permute-start(bf16[2,64,1024]{2,1,0:T(8,128)(2,1)S(1)} %sites.1.refs_0_), channel_id=1, source_target_pairs={{0,1},{1,0},{2,3},{3,2},{4,5},{5,4},{6,7},{7,6},{8,9},{9,8},{10,11... | collective-permute-start | bytes 786440 | tf_op jit(solution)/shard_map/ppermute | solution.py:35
  52.8 2.2 %collective-permute-start.18 = (bf16[64,512]{1,0:T(8,128)(2,1)S(1)}, bf16[64,512]{1,0:T(8,128)(2,1)S(1)}, u32[]{:S(2)}, u32[]{:S(2)}) collective-permute-start(bf16[64,512]{1,0:T(8,128)(2,1)S(1)} %get-tuple-element.61._.refs_2_), channel_id=1, source_target_pairs={{0,1},{1,0},{2,3},{3,2},{4,5},{5,4},{6,7},{7,6},{8,9},{9,8},{10,11... | collective-permute-start | bytes 196616 | tf_op jit(solution)/shard_map/ppermute | solution.py:35
  54.5 1.3 %collective-permute-start.21 = (bf16[64,512]{1,0:T(8,128)(2,1)S(1)}, bf16[64,512]{1,0:T(8,128)(2,1)S(1)}, u32[]{:S(2)}, u32[]{:S(2)}) collective-permute-start(bf16[64,512]{1,0:T(8,128)(2,1)S(1)} %collective-permute-done.17.refs_5_), channel_id=1, source_target_pairs={{0,1},{1,0},{2,3},{3,2},{4,5},{5,4},{6,7},{7,6},{8,9},{9,8},{10,11... | collective-permute-start | bytes 196616 | tf_op jit(solution)/shard_map/ppermute | solution.py:35
  54.5 1.4 %collective-permute-start.20 = (bf16[64,512]{1,0:T(8,128)(2,1)S(1)}, bf16[64,512]{1,0:T(8,128)(2,1)S(1)}, u32[]{:S(2)}, u32[]{:S(2)}) collective-permute-start(bf16[64,512]{1,0:T(8,128)(2,1)S(1)} %collective-permute-done.16.refs_4_), channel_id=1, source_target_pairs={{0,1},{1,0},{2,3},{3,2},{4,5},{5,4},{6,7},{7,6},{8,9},{9,8},{10,11... | collective-permute-start | bytes 196616 | tf_op jit(solution)/shard_map/ppermute | solution.py:35
  55.0 1.3 %collective-permute-start.19 = (bf16[64,512]{1,0:T(8,128)(2,1)S(1)}, bf16[64,512]{1,0:T(8,128)(2,1)S(1)}, u32[]{:S(2)}, u32[]{:S(2)}) collective-permute-start(bf16[64,512]{1,0:T(8,128)(2,1)S(1)} %collective-permute-done.15.refs_3_), channel_id=1, source_target_pairs={{0,1},{1,0},{2,3},{3,2},{4,5},{5,4},{6,7},{7,6},{8,9},{9,8},{10,11... | collective-permute-start | bytes 196616 | tf_op jit(solution)/shard_map/ppermute | solution.py:35

commit v16 on v15

--- a/solution.py
+++ b/solution.py
@@ -257,20 +257,21 @@
     h_parts = low_rank(gy, up, ups, ups[0], "h")
     gy_got = [shift(after(gy, *pieces), "mp", s) for s in range(1, n_mp)]
     down_back, h_wide = gradient(x, h_parts, downs, "down", GRAD_COST)
-    u_parts = low_rank(x, down, downs, h_wide, "u")
-
     parts = []
     for piece in pieces:
         parts += [piece] + [shift(after(piece, h_wide), "pair", q) for q in range(1, n_pair)]
+    u_parts = low_rank(x, down, downs, parts[-1], "u")
+
+
     sent = call(
         functools.partial(send_kernel, n_pair, feat, n_mp), "y_send",
         [shape(tok, cols)] * n_other + [shape(feat, cols)] * n_other,
         [ANY, ANY, row_block(feat)] + [whole(part, cols)] * len(parts),
         [row_block(cols)] * n_other + [whole(feat, cols)] * n_other,
         grid=(TILES,),
-    )(u_parts[0], down_back[1], x, *parts)
+    )(u_parts[0], h_wide, x, *parts)
     w_rows = sent[n_other:]
-    y_got = [shift(sent[s - 1], "mp", n_mp - s) for s in range(1, n_mp)]
+    y_got = [shift(after(sent[s - 1], down_back[1]), "mp", n_mp - s) for s in range(1, n_mp)]
     back, picks = call(
         functools.partial(back_kernel, n_dp, n_mp), "back",
         [shape(tok, feat), shape(-(-n_dp * n_pair // 8) * 8, 128, dtype=jnp.int32)],

time: 60.1 us -> 59.6 us (level)
  waiting for transfers between devices: 14.6 us -> 13.2 us
  starting transfers between devices: 26.9 us -> 27.6 us
    ppermute x12, waiting for transfers between devices: 7.84 us -> 6.03 us  [swap(): lax.ppermute(value, axis, [(i, i ^ mask) for i in range(lax.axis_size(axi...]
    ppermute x12, starting transfers between devices: 18 us -> 19.2 us  [swap(): lax.ppermute(value, axis, [(i, i ^ mask) for i in range(lax.axis_size(axi...]
  transfers between devices with their start and end apart: 23 -> 23, of which waited for: 9 -> 10; matrix products, arithmetic and copies ran while one was open for 0% -> 0% of each run, Pallas kernels for 21% -> 22%
where the time goes in v16:
time: 59.6 us; the launch traced here: 59.4 us
  starting transfers between devices  27.6 us (46%)
  Pallas kernels  17.7 us (30%)
  waiting for transfers between devices  13.2 us (22%)
  between operations  0.82 us (1%)
    ppermute x12, starting transfers between devices, swap(): lax.ppermute(value, axis, [(i, i ^ mask) for i in range(lax.axis_size(axi...  19.2 us
    ppermute x11, starting transfers between devices, shift(): lax.ppermute(value, axis, [(i, (i + by) % size) for i in range(size)])  8.45 us
    ppermute x11, waiting for transfers between devices, shift(): lax.ppermute(value, axis, [(i, (i + by) % size) for i in range(size)])  7.19 us
    ppermute x12, waiting for transfers between devices, swap(): lax.ppermute(value, axis, [(i, i ^ mask) for i in range(lax.axis_size(axi...  6.03 us
    pallas_call x1, Pallas kernels, shards(): call(functools.partial(back_kernel, n_dp, n_mp), 'back', [shape(tok, feat...  4.07 us
    pallas_call x1, Pallas kernels, shards(): call(functools.partial(pack_kernel, n_dp, n_mp, n_pair), 'pack', [shape(r...  3.28 us
    pallas_call x2, Pallas kernels, gradient(): call(functools.partial(grad_kernel, n_dp, n_mp, len(behind)), name + '_gr...  2.44 us
    pallas_call x2, Pallas kernels, low_rank(): call(functools.partial(reduce_kernel, n_dp), name + '_part', shape(tok //...  2.42 us
  transfers between devices with their start and end apart: 23, of which 10 were waited for; matrix products, arithmetic and copies ran while one was open for 0% of the time, Pallas kernels for 22%

profile of v16, /device:TPU:0, one launch (start us, length us, event | category | flops | bytes accessed | tf_op | source)
XLA Modules:
  0.0 59.4 jit_solution(620641415243658623)
XLA Ops:
  0.7 3.3 %pack.1 = (bf16[64,512]{1,0:T(8,128)(2,1)}, bf16[64,512]{1,0:T(8,128)(2,1)}, bf16[64,512]{1,0:T(8,128)(2,1)}, bf16[64,1024]{1,0:T(8,128)(2,1)}, bf16[64,1024]{1,...) custom-call(s32[1,2,4]{2,1,0:T(2,128)} %table.9, bf16[2,64,1024]{2,1,0:T(8,128)(2,1)} %bitcast.2, ...), custom_call_target="tpu_custom_call" | custom-call | flops 1 | bytes 1 | tf_op jit(solution)/shard_map/pack/pallas_call | solution.py:231
  4.0 3.0 %collective-permute-start = (bf16[512,512]{1,0:T(8,128)(2,1)}, bf16[512,512]{1,0:T(8,128)(2,1)S(1)}, u32[]{:S(2)}, u32[]{:S(2)}) collective-permute-start(bf16[512,512]{1,0:T(8,128)(2,1)} %get-tuple-element.38), channel_id=1, source_target_pairs={{0,2},{2,0},{1,3},{3,1},{4,6},{6,4},{5,7},{7,5},{8,10},{10,8},{9,1... | collective-permute-start | bytes 1572872 | tf_op jit(solution)/shard_map/ppermute | solution.py:35
  7.0 3.6 %collective-permute-start.2 = (bf16[64,512]{1,0:T(8,128)(2,1)}, bf16[64,512]{1,0:T(8,128)(2,1)S(1)}, u32[]{:S(2)}, u32[]{:S(2)}) collective-permute-start(bf16[64,512]{1,0:T(8,128)(2,1)} %get-tuple-element.41), channel_id=1, source_target_pairs={{0,12},{4,8},{8,4},{12,0},{1,13},{5,9},{9,5},{13,1},{2,14},{6,10},... | collective-permute-start | bytes 196616 | tf_op jit(solution)/shard_map/ppermute | solution.py:39
  10.6 0.8 %collective-permute-start.7 = (bf16[64,512]{1,0:T(8,128)(2,1)}, bf16[64,512]{1,0:T(8,128)(2,1)S(1)}, u32[]{:S(2)}, u32[]{:S(2)}) collective-permute-start(bf16[64,512]{1,0:T(8,128)(2,1)} %get-tuple-element.48), channel_id=1, source_target_pairs={{0,8},{4,12},{8,0},{12,4},{1,9},{5,13},{9,1},{13,5},{2,10},{6,14},... | collective-permute-start | bytes 196616 | tf_op jit(solution)/shard_map/ppermute | solution.py:39
  11.4 2.1 %collective-permute-done.2.refs_2_ = bf16[64,512]{1,0:T(8,128)(2,1)S(1)} collective-permute-done((bf16[64,512]{1,0:T(8,128)(2,1)}, bf16[64,512]{1,0:T(8,128)(2,1)S(1)}, u32[]{:S(2)}, u32[]{:S(2)}) %collective-permute-start.2) | collective-permute-done | bytes 65568 | tf_op jit(solution)/shard_map/ppermute | solution.py:39
  13.5 4.7 %collective-permute-start.4 = (bf16[64,1024]{1,0:T(8,128)(2,1)}, bf16[64,1024]{1,0:T(8,128)(2,1)S(1)}, u32[]{:S(2)}, u32[]{:S(2)}) collective-permute-start(bf16[64,1024]{1,0:T(8,128)(2,1)} %get-tuple-element.44), channel_id=1, source_target_pairs={{0,8},{4,12},{8,0},{12,4},{1,9},{5,13},{9,1},{13,5},{2,10},{6,14},... | collective-permute-start | bytes 393224 | tf_op jit(solution)/shard_map/ppermute | solution.py:39
  18.3 1.1 %h_part.1.refs_3_ = bf16[384,128]{1,0:T(8,128)(2,1)S(1)} custom-call(s32[12]{0:T(128)S(1)} %copy-done.6, s32[1,2,4]{2,1,0:T(2,128)S(1)} %copy-done.5, bf16[768,512]{1,0:T(8,128)(2,1)S(1)} %copy-done.2, bf16[64,512]{1,0:T(8,128)(2,1)S(1)} %collective-permute-done.6._.refs_0_, bf16[2,64,512]{2,1,0:T(8,128)(2,1)S(1)} %copy-done.4, ...), custom_call_target="tpu_custom_call" | custom-call | flops 1 | bytes 1 | tf_op jit(solution)/shard_map/h_part/pallas_call | solution.py:242
  19.4 0.6 %collective-permute-start.8 = (bf16[384,128]{1,0:T(8,128)(2,1)S(1)}, bf16[384,128]{1,0:T(8,128)(2,1)S(1)}, u32[]{:S(2)}, u32[]{:S(2)}) collective-permute-start(bf16[384,128]{1,0:T(8,128)(2,1)S(1)} %h_part.1.refs_3_), channel_id=1, source_target_pairs={{0,2},{2,0},{1,3},{3,1},{4,6},{6,4},{5,7},{7,5},{8,10},{10,8},{9,1... | collective-permute-start | bytes 294920 | tf_op jit(solution)/shard_map/ppermute | solution.py:35
  20.0 1.8 %collective-permute-start.1 = (bf16[768,512]{1,0:T(8,128)(2,1)S(1)}, bf16[768,512]{1,0:T(8,128)(2,1)S(1)}, u32[]{:S(2)}, u32[]{:S(2)}) collective-permute-start(bf16[768,512]{1,0:T(8,128)(2,1)S(1)} %copy-done.2), channel_id=1, source_target_pairs={{0,2},{2,0},{1,3},{3,1},{4,6},{6,4},{5,7},{7,5},{8,10},{10,8},{9,1... | collective-permute-start | bytes 2359304 | tf_op jit(solution)/shard_map/ppermute | solution.py:35
  21.8 3.3 %collective-permute-done.8.refs_4_ = bf16[384,128]{1,0:T(8,128)(2,1)S(1)} collective-permute-done((bf16[384,128]{1,0:T(8,128)(2,1)S(1)}, bf16[384,128]{1,0:T(8,128)(2,1)S(1)}, u32[]{:S(2)}, u32[]{:S(2)}) %collective-permute-start.8) | collective-permute-done | bytes 98336 | tf_op jit(solution)/shard_map/ppermute | solution.py:35
  25.2 2.1 %collective-permute-done.4.refs_1_.refs_7_ = bf16[64,1024]{1,0:T(8,128)(2,1)S(1)} collective-permute-done((bf16[64,1024]{1,0:T(8,128)(2,1)}, bf16[64,1024]{1,0:T(8,128)(2,1)S(1)}, u32[]{:S(2)}, u32[]{:S(2)}) %collective-permute-start.4) | collective-permute-done | bytes 131104 | tf_op jit(solution)/shard_map/ppermute | solution.py:39
  27.3 1.3 %down_grad.1 = (bf16[64,1024]{1,0:T(8,128)(2,1)S(1)}, bf16[64,1024]{1,0:T(8,128)(2,1)S(1)}, bf16[64,1024]{1,0:T(8,128)(2,1)S(1)}, bf16[64,1024]{1,0:T(8,128)(2,1)S(1)}, bf16[768,256]{1,0:T(8,128)(2,1)S(1)}) custom-call(s32[12]{0:T(128)S(1)} %copy-done.6, bf16[768,1024]{1,0:T(8,128)(2,1)S(1)} %copy-done.1, ...), custom_call_target="tpu_custom_call" | custom-call | flops 15000000512 | bytes 1 | tf_op jit(solution)/shard_map/down_grad/pallas_call | solution.py:250
  28.7 2.0 %collective-permute-start.10 = (bf16[64,1024]{1,0:T(8,128)(2,1)S(1)}, bf16[64,1024]{1,0:T(8,128)(2,1)S(1)}, u32[]{:S(2)}, u32[]{:S(2)}) collective-permute-start(bf16[64,1024]{1,0:T(8,128)(2,1)S(1)} %get-tuple-element.53), channel_id=1, source_target_pairs={{0,4},{4,0},{8,12},{12,8},{1,5},{5,1},{9,13},{13,9},{2,6},{6,2},{1... | collective-permute-start | bytes 393224 | tf_op jit(solution)/shard_map/ppermute | solution.py:39
  30.7 1.0 %collective-permute-start.11 = (bf16[64,1024]{1,0:T(8,128)(2,1)S(1)}, bf16[64,1024]{1,0:T(8,128)(2,1)S(1)}, u32[]{:S(2)}, u32[]{:S(2)}) collective-permute-start(bf16[64,1024]{1,0:T(8,128)(2,1)S(1)} %get-tuple-element.54), channel_id=1, source_target_pairs={{0,8},{4,12},{8,0},{12,4},{1,9},{5,13},{9,1},{13,5},{2,10},{6,14},... | collective-permute-start | bytes 393224 | tf_op jit(solution)/shard_map/ppermute | solution.py:39
  31.7 1.5 %collective-permute-start.12 = (bf16[64,1024]{1,0:T(8,128)(2,1)S(1)}, bf16[64,1024]{1,0:T(8,128)(2,1)S(1)}, u32[]{:S(2)}, u32[]{:S(2)}) collective-permute-start(bf16[64,1024]{1,0:T(8,128)(2,1)S(1)} %get-tuple-element.55), channel_id=1, source_target_pairs={{0,12},{4,8},{8,4},{12,0},{1,13},{5,9},{9,5},{13,1},{2,14},{6,10},... | collective-permute-start | bytes 393224 | tf_op jit(solution)/shard_map/ppermute | solution.py:39
  33.2 1.3 %u_part.1._.refs_5_ = bf16[384,128]{1,0:T(8,128)(2,1)S(1)} custom-call(s32[12]{0:T(128)S(1)} %copy-done.6, s32[1,2,4]{2,1,0:T(2,128)S(1)} %copy-done.5, bf16[768,1024]{1,0:T(8,128)(2,1)S(1)} %copy-done.1, bf16[512,512]{1,0:T(8,128)(2,1)S(1)} %collective-permute-done.9._.refs_1_, bf16[2,64,1024]{2,1,0:T(8,128)(2,1)S(1)} %bitcast.3, ...), custom_call_target="tpu_custom_call" | custom-call | flops 1 | bytes 1 | tf_op jit(solution)/shard_map/u_part/pallas_call | solution.py:242
  34.5 0.6 %collective-permute-start.13 = (bf16[384,128]{1,0:T(8,128)(2,1)S(1)}, bf16[384,128]{1,0:T(8,128)(2,1)S(1)}, u32[]{:S(2)}, u32[]{:S(2)}) collective-permute-start(bf16[384,128]{1,0:T(8,128)(2,1)S(1)} %u_part.1._.refs_5_), channel_id=1, source_target_pairs={{0,2},{2,0},{1,3},{3,1},{4,6},{6,4},{5,7},{7,5},{8,10},{10,8},{9,1... | collective-permute-start | bytes 294920 | tf_op jit(solution)/shard_map/ppermute | solution.py:35
  35.1 1.4 %y_send.1 = (bf16[768,512]{1,0:T(8,128)(2,1)S(1)}, bf16[1024,512]{1,0:T(8,128)(2,1)S(1)}) custom-call(bf16[384,128]{1,0:T(8,128)(2,1)S(1)} %u_part.1._.refs_5_, bf16[768,256]{1,0:T(8,128)(2,1)S(1)} %get-tuple-element.49.__.refs_4_, bf16[768,1024]{1,0:T(8,128)(2,1)S(1)} %copy-done.1, bf16[512,512]{1,0:T(8,128)(2,1)S(1)} %collective-permute-done.refs_0_, ...), custom_call_target="tpu_custom_call" | custom-call | flops 1 | bytes 1 | tf_op jit(solution)/shard_map/y_send/pallas_call | solution.py:266
  36.5 0.4 collective-permute-done.10.refs_1_
  37.0 1.1 %collective-permute-start.22 = (bf16[768,512]{1,0:T(8,128)(2,1)S(1)}, bf16[768,512]{1,0:T(8,128)(2,1)S(1)}, u32[]{:S(2)}, u32[]{:S(2)}) collective-permute-start(bf16[768,512]{1,0:T(8,128)(2,1)S(1)} %get-tuple-element.67), channel_id=1, source_target_pairs={{0,2},{2,0},{1,3},{3,1},{4,6},{6,4},{5,7},{7,5},{8,10},{10,8},{9,1... | collective-permute-start | bytes 2359304 | tf_op jit(solution)/shard_map/ppermute | solution.py:35
  38.1 2.5 %collective-permute-done.1.refs_2_.refs_4_ = bf16[768,512]{1,0:T(8,128)(2,1)S(1)} collective-permute-done((bf16[768,512]{1,0:T(8,128)(2,1)S(1)}, bf16[768,512]{1,0:T(8,128)(2,1)S(1)}, u32[]{:S(2)}, u32[]{:S(2)}) %collective-permute-start.1) | collective-permute-done | bytes 786464 | tf_op jit(solution)/shard_map/ppermute | solution.py:35
  40.6 4.1 %back.1 = (bf16[768,1024]{1,0:T(8,128)(2,1)}, s32[8,128]{1,0:T(8,128)S(1)}) custom-call(s32[1,2,4]{2,1,0:T(2,128)S(1)} %copy-done.5, bf16[2048,512]{1,0:T(8,128)(2,1)S(1)} %copy-done, bf16[768,512]{1,0:T(8,128)(2,1)S(1)} %copy-done.2, bf16[768,512]{1,0:T(8,128)(2,1)S(1)} %collective-permute-done.1.refs_2_.refs_4_, ...), custom_call_target="tpu_custom_call" | custom-call | flops 1 | bytes 1 | tf_op jit(solution)/shard_map/back/pallas_call | solution.py:275
  44.7 1.1 %up_grad.1 = (bf16[64,512]{1,0:T(8,128)(2,1)S(1)}, bf16[64,512]{1,0:T(8,128)(2,1)S(1)}, bf16[64,512]{1,0:T(8,128)(2,1)S(1)}, bf16[64,512]{1,0:T(8,128)(2,1)S(1)}, bf16[768,256]{1,0:T(8,128)(2,1)S(1)}) custom-call(s32[12]{0:T(128)S(1)} %copy-done.6, bf16[768,512]{1,0:T(8,128)(2,1)S(1)} %copy-done.2, s32[8,128]{1,0:T(8,128)S(1)} %get-tuple-element.52.refs_0_.picks, ...), custom_call_target="tpu_custom_call" | custom-call | flops 15000000512 | bytes 1 | tf_op jit(solution)/shard_map/up_grad/pallas_call | solution.py:250
  45.8 5.0 %collective-permute-start.17 = (bf16[64,512]{1,0:T(8,128)(2,1)S(1)}, bf16[64,512]{1,0:T(8,128)(2,1)S(1)}, u32[]{:S(2)}, u32[]{:S(2)}) collective-permute-start(bf16[64,512]{1,0:T(8,128)(2,1)S(1)} %get-tuple-element.60), channel_id=1, source_target_pairs={{0,12},{4,8},{8,4},{12,0},{1,13},{5,9},{9,5},{13,1},{2,14},{6,10},... | collective-permute-start | bytes 196616 | tf_op jit(solution)/shard_map/ppermute | solution.py:39
  50.7 0.6 %collective-permute-start.15 = (bf16[64,512]{1,0:T(8,128)(2,1)S(1)}, bf16[64,512]{1,0:T(8,128)(2,1)S(1)}, u32[]{:S(2)}, u32[]{:S(2)}) collective-permute-start(bf16[64,512]{1,0:T(8,128)(2,1)S(1)} %get-tuple-element.58), channel_id=1, source_target_pairs={{0,4},{4,0},{8,12},{12,8},{1,5},{5,1},{9,13},{13,9},{2,6},{6,2},{1... | collective-permute-start | bytes 196616 | tf_op jit(solution)/shard_map/ppermute | solution.py:39
  51.8 2.2 %y_own.1.refs_10_ = bf16[768,512]{1,0:T(8,128)(2,1)S(1)} custom-call(s32[1,2,4]{2,1,0:T(2,128)S(1)} %copy-done.5, bf16[2048,512]{1,0:T(8,128)(2,1)S(1)} %copy-done, bf16[768,1024]{1,0:T(8,128)(2,1)S(1)} %copy-done.1, bf16[768,256]{1,0:T(8,128)(2,1)S(1)} %get-tuple-element.61.wide, bf16[2,64,512]{2,1,0:T(8,128)(2,1)S(1)} %copy-done.4, ...), custom_call_target="tpu_custom_call" | custom-call | flops 15000000512 | bytes 1 | tf_op jit(solution)/shard_map/y_own/pallas_call | solution.py:285
  54.0 0.5 collective-permute-start.18
  54.5 1.4 %collective-permute-done.16.refs_4_ = bf16[64,512]{1,0:T(8,128)(2,1)S(1)} collective-permute-done((bf16[64,512]{1,0:T(8,128)(2,1)S(1)}, bf16[64,512]{1,0:T(8,128)(2,1)S(1)}, u32[]{:S(2)}, u32[]{:S(2)}) %collective-permute-start.16) | collective-permute-done | bytes 65568 | tf_op jit(solution)/shard_map/ppermute | solution.py:39
  55.9 0.5 collective-permute-start.20
  56.5 0.7 %collective-permute-done.21.refs_9_ = bf16[64,512]{1,0:T(8,128)(2,1)S(1)} collective-permute-done((bf16[64,512]{1,0:T(8,128)(2,1)S(1)}, bf16[64,512]{1,0:T(8,128)(2,1)S(1)}, u32[]{:S(2)}, u32[]{:S(2)}) %collective-permute-start.21) | collective-permute-done | bytes 65568 | tf_op jit(solution)/shard_map/ppermute | solution.py:35
  57.3 0.4 collective-permute-done.19.refs_7_
  57.8 1.5 %last.1 = (f32[2,64,1024]{2,1,0:T(8,128)}, f32[2,64,512]{2,1,0:T(8,128)}, bf16[768,512]{1,0:T(8,128)(2,1)}) custom-call(s32[8,128]{1,0:T(8,128)S(1)} %get-tuple-element.52.refs_0_.picks, bf16[2,64,1024]{2,1,0:T(8,128)(2,1)S(1)} %sites.1.refs_0_, bf16[2,64,1024]{2,1,0:T(8,128)(2,1)S(1)} %collective-permute-done.14.refs_1_, ...), custom_call_target="tpu_custom_call" | custom-call | flops 1 | bytes 1 | tf_op jit(solution)/shard_map/last/pallas_call | solution.py:300
  (38 shorter events, 1.0 us)
Async XLA Ops:
  0.6 17.6 %copy-start.4 = (bf16[2,64,512]{2,1,0:T(8,128)(2,1)S(1)}, bf16[2,64,512]{2,1,0:T(8,128)(2,1)}, u32[]{:S(2)}) copy-start(bf16[2,64,512]{2,1,0:T(8,128)(2,1)} %own_up.1) | copy-start | bytes 393220
  0.6 17.6 %copy-start.5 = (s32[1,2,4]{2,1,0:T(2,128)S(1)}, s32[1,2,4]{2,1,0:T(2,128)}, u32[]{:S(2)}) copy-start(s32[1,2,4]{2,1,0:T(2,128)} %table.9) | copy-start | bytes 100
  0.7 17.6 %copy-start.2 = (bf16[768,512]{1,0:T(8,128)(2,1)S(1)}, bf16[768,512]{1,0:T(8,128)(2,1)}, u32[]{:S(2)}) copy-start(bf16[768,512]{1,0:T(8,128)(2,1)} %act.7) | copy-start | bytes 2359300
  0.7 17.6 %copy-start.6 = (s32[12]{0:T(128)S(1)}, s32[12]{0:T(128)}, u32[]{:S(2)}) copy-start(s32[12]{0:T(128)} %owner.7) | copy-start | bytes 148
  0.7 26.6 %copy-start.1 = (bf16[768,1024]{1,0:T(8,128)(2,1)S(1)}, bf16[768,1024]{1,0:T(8,128)(2,1)}, u32[]{:S(2)}) copy-start(bf16[768,1024]{1,0:T(8,128)(2,1)} %x.3) | copy-start | bytes 4718596
  4.0 16.0 %collective-permute-start = (bf16[512,512]{1,0:T(8,128)(2,1)}, bf16[512,512]{1,0:T(8,128)(2,1)S(1)}, u32[]{:S(2)}, u32[]{:S(2)}) collective-permute-start(bf16[512,512]{1,0:T(8,128)(2,1)} %get-tuple-element.38), channel_id=1, source_target_pairs={{0,2},{2,0},{1,3},{3,1},{4,6},{6,4},{5,7},{7,5},{8,10},{10,8},{9,1... | collective-permute-start | bytes 1572872 | tf_op jit(solution)/shard_map/ppermute | solution.py:35
  7.0 6.5 %collective-permute-start.2 = (bf16[64,512]{1,0:T(8,128)(2,1)}, bf16[64,512]{1,0:T(8,128)(2,1)S(1)}, u32[]{:S(2)}, u32[]{:S(2)}) collective-permute-start(bf16[64,512]{1,0:T(8,128)(2,1)} %get-tuple-element.41), channel_id=1, source_target_pairs={{0,12},{4,8},{8,4},{12,0},{1,13},{5,9},{9,5},{13,1},{2,14},{6,10},... | collective-permute-start | bytes 196616 | tf_op jit(solution)/shard_map/ppermute | solution.py:39
  10.6 7.6 %collective-permute-start.6 = (bf16[64,512]{1,0:T(8,128)(2,1)}, bf16[64,512]{1,0:T(8,128)(2,1)S(1)}, u32[]{:S(2)}, u32[]{:S(2)}) collective-permute-start(bf16[64,512]{1,0:T(8,128)(2,1)} %get-tuple-element.47), channel_id=1, source_target_pairs={{0,4},{4,0},{8,12},{12,8},{1,5},{5,1},{9,13},{13,9},{2,6},{6,2},{1... | collective-permute-start | bytes 196616 | tf_op jit(solution)/shard_map/ppermute | solution.py:39
  10.6 7.6 %collective-permute-start.7 = (bf16[64,512]{1,0:T(8,128)(2,1)}, bf16[64,512]{1,0:T(8,128)(2,1)S(1)}, u32[]{:S(2)}, u32[]{:S(2)}) collective-permute-start(bf16[64,512]{1,0:T(8,128)(2,1)} %get-tuple-element.48), channel_id=1, source_target_pairs={{0,8},{4,12},{8,0},{12,4},{1,9},{5,13},{9,1},{13,5},{2,10},{6,14},... | collective-permute-start | bytes 196616 | tf_op jit(solution)/shard_map/ppermute | solution.py:39
  13.5 11.7 %collective-permute-start.3 = (bf16[64,1024]{1,0:T(8,128)(2,1)}, bf16[64,1024]{1,0:T(8,128)(2,1)S(1)}, u32[]{:S(2)}, u32[]{:S(2)}) collective-permute-start(bf16[64,1024]{1,0:T(8,128)(2,1)} %get-tuple-element.42), channel_id=1, source_target_pairs={{0,4},{4,0},{8,12},{12,8},{1,5},{5,1},{9,13},{13,9},{2,6},{6,2},{1... | collective-permute-start | bytes 393224 | tf_op jit(solution)/shard_map/ppermute | solution.py:39
  13.5 13.8 %collective-permute-start.4 = (bf16[64,1024]{1,0:T(8,128)(2,1)}, bf16[64,1024]{1,0:T(8,128)(2,1)S(1)}, u32[]{:S(2)}, u32[]{:S(2)}) collective-permute-start(bf16[64,1024]{1,0:T(8,128)(2,1)} %get-tuple-element.44), channel_id=1, source_target_pairs={{0,8},{4,12},{8,0},{12,4},{1,9},{5,13},{9,1},{13,5},{2,10},{6,14},... | collective-permute-start | bytes 393224 | tf_op jit(solution)/shard_map/ppermute | solution.py:39
  18.2 9.1 %collective-permute-start.5 = (bf16[64,1024]{1,0:T(8,128)(2,1)}, bf16[64,1024]{1,0:T(8,128)(2,1)S(1)}, u32[]{:S(2)}, u32[]{:S(2)}) collective-permute-start(bf16[64,1024]{1,0:T(8,128)(2,1)} %get-tuple-element.46), channel_id=1, source_target_pairs={{0,12},{4,8},{8,4},{12,0},{1,13},{5,9},{9,5},{13,1},{2,14},{6,10},... | collective-permute-start | bytes 393224 | tf_op jit(solution)/shard_map/ppermute | solution.py:39
  19.4 13.8 %copy-start.3 = (bf16[2,1024,64]{1,2,0:T(8,128)(2,1)S(1)}, bf16[2,1024,64]{1,2,0:T(8,128)(2,1)}, u32[]{:S(2)}) copy-start(bf16[2,1024,64]{1,2,0:T(8,128)(2,1)} %param.9) | copy-start | bytes 786436
  19.4 5.8 %collective-permute-start.8 = (bf16[384,128]{1,0:T(8,128)(2,1)S(1)}, bf16[384,128]{1,0:T(8,128)(2,1)S(1)}, u32[]{:S(2)}, u32[]{:S(2)}) collective-permute-start(bf16[384,128]{1,0:T(8,128)(2,1)S(1)} %h_part.1.refs_3_), channel_id=1, source_target_pairs={{0,2},{2,0},{1,3},{3,1},{4,6},{6,4},{5,7},{7,5},{8,10},{10,8},{9,1... | collective-permute-start | bytes 294920 | tf_op jit(solution)/shard_map/ppermute | solution.py:35
  20.0 20.6 %collective-permute-start.1 = (bf16[768,512]{1,0:T(8,128)(2,1)S(1)}, bf16[768,512]{1,0:T(8,128)(2,1)S(1)}, u32[]{:S(2)}, u32[]{:S(2)}) collective-permute-start(bf16[768,512]{1,0:T(8,128)(2,1)S(1)} %copy-done.2), channel_id=1, source_target_pairs={{0,2},{2,0},{1,3},{3,1},{4,6},{6,4},{5,7},{7,5},{8,10},{10,8},{9,1... | collective-permute-start | bytes 2359304 | tf_op jit(solution)/shard_map/ppermute | solution.py:35
  28.6 4.5 %collective-permute-start.9 = (bf16[512,512]{1,0:T(8,128)(2,1)S(1)}, bf16[512,512]{1,0:T(8,128)(2,1)S(1)}, u32[]{:S(2)}, u32[]{:S(2)}) collective-permute-start(bf16[512,512]{1,0:T(8,128)(2,1)S(1)} %collective-permute-done.refs_0_), channel_id=1, source_target_pairs={{0,1},{1,0},{2,3},{3,2},{4,5},{5,4},{6,7},{7,6},{8,9},{9,8},{10,11... | collective-permute-start | bytes 1572872 | tf_op jit(solution)/shard_map/ppermute | solution.py:35
  28.7 8.3 %collective-permute-start.10 = (bf16[64,1024]{1,0:T(8,128)(2,1)S(1)}, bf16[64,1024]{1,0:T(8,128)(2,1)S(1)}, u32[]{:S(2)}, u32[]{:S(2)}) collective-permute-start(bf16[64,1024]{1,0:T(8,128)(2,1)S(1)} %get-tuple-element.53), channel_id=1, source_target_pairs={{0,4},{4,0},{8,12},{12,8},{1,5},{5,1},{9,13},{13,9},{2,6},{6,2},{1... | collective-permute-start | bytes 393224 | tf_op jit(solution)/shard_map/ppermute | solution.py:39
  30.7 13.9 %collective-permute-start.11 = (bf16[64,1024]{1,0:T(8,128)(2,1)S(1)}, bf16[64,1024]{1,0:T(8,128)(2,1)S(1)}, u32[]{:S(2)}, u32[]{:S(2)}) collective-permute-start(bf16[64,1024]{1,0:T(8,128)(2,1)S(1)} %get-tuple-element.54), channel_id=1, source_target_pairs={{0,8},{4,12},{8,0},{12,4},{1,9},{5,13},{9,1},{13,5},{2,10},{6,14},... | collective-permute-start | bytes 393224 | tf_op jit(solution)/shard_map/ppermute | solution.py:39
  31.7 13.0 %collective-permute-start.12 = (bf16[64,1024]{1,0:T(8,128)(2,1)S(1)}, bf16[64,1024]{1,0:T(8,128)(2,1)S(1)}, u32[]{:S(2)}, u32[]{:S(2)}) collective-permute-start(bf16[64,1024]{1,0:T(8,128)(2,1)S(1)} %get-tuple-element.55), channel_id=1, source_target_pairs={{0,12},{4,8},{8,4},{12,0},{1,13},{5,9},{9,5},{13,1},{2,14},{6,10},... | collective-permute-start | bytes 393224 | tf_op jit(solution)/shard_map/ppermute | solution.py:39
  34.5 6.1 %copy-start = (bf16[2048,512]{1,0:T(8,128)(2,1)S(1)}, bf16[2048,512]{1,0:T(8,128)(2,1)}, u32[]{:S(2)}) copy-start(bf16[2048,512]{1,0:T(8,128)(2,1)} %w.3) | copy-start | bytes 6291460
  34.5 10.2 %collective-permute-start.13 = (bf16[384,128]{1,0:T(8,128)(2,1)S(1)}, bf16[384,128]{1,0:T(8,128)(2,1)S(1)}, u32[]{:S(2)}, u32[]{:S(2)}) collective-permute-start(bf16[384,128]{1,0:T(8,128)(2,1)S(1)} %u_part.1._.refs_5_), channel_id=1, source_target_pairs={{0,2},{2,0},{1,3},{3,1},{4,6},{6,4},{5,7},{7,5},{8,10},{10,8},{9,1... | collective-permute-start | bytes 294920 | tf_op jit(solution)/shard_map/ppermute | solution.py:35
  37.0 20.9 %collective-permute-start.22 = (bf16[768,512]{1,0:T(8,128)(2,1)S(1)}, bf16[768,512]{1,0:T(8,128)(2,1)S(1)}, u32[]{:S(2)}, u32[]{:S(2)}) collective-permute-start(bf16[768,512]{1,0:T(8,128)(2,1)S(1)} %get-tuple-element.67), channel_id=1, source_target_pairs={{0,2},{2,0},{1,3},{3,1},{4,6},{6,4},{5,7},{7,5},{8,10},{10,8},{9,1... | collective-permute-start | bytes 2359304 | tf_op jit(solution)/shard_map/ppermute | solution.py:35
  45.8 8.2 %collective-permute-start.17 = (bf16[64,512]{1,0:T(8,128)(2,1)S(1)}, bf16[64,512]{1,0:T(8,128)(2,1)S(1)}, u32[]{:S(2)}, u32[]{:S(2)}) collective-permute-start(bf16[64,512]{1,0:T(8,128)(2,1)S(1)} %get-tuple-element.60), channel_id=1, source_target_pairs={{0,12},{4,8},{8,4},{12,0},{1,13},{5,9},{9,5},{13,1},{2,14},{6,10},... | collective-permute-start | bytes 196616 | tf_op jit(solution)/shard_map/ppermute | solution.py:39
  50.7 5.2 %collective-permute-start.16 = (bf16[64,512]{1,0:T(8,128)(2,1)S(1)}, bf16[64,512]{1,0:T(8,128)(2,1)S(1)}, u32[]{:S(2)}, u32[]{:S(2)}) collective-permute-start(bf16[64,512]{1,0:T(8,128)(2,1)S(1)} %get-tuple-element.59), channel_id=1, source_target_pairs={{0,8},{4,12},{8,0},{12,4},{1,9},{5,13},{9,1},{13,5},{2,10},{6,14},... | collective-permute-start | bytes 196616 | tf_op jit(solution)/shard_map/ppermute | solution.py:39
  50.7 5.2 %collective-permute-start.15 = (bf16[64,512]{1,0:T(8,128)(2,1)S(1)}, bf16[64,512]{1,0:T(8,128)(2,1)S(1)}, u32[]{:S(2)}, u32[]{:S(2)}) collective-permute-start(bf16[64,512]{1,0:T(8,128)(2,1)S(1)} %get-tuple-element.58), channel_id=1, source_target_pairs={{0,4},{4,0},{8,12},{12,8},{1,5},{5,1},{9,13},{13,9},{2,6},{6,2},{1... | collective-permute-start | bytes 196616 | tf_op jit(solution)/shard_map/ppermute | solution.py:39
  51.7 6.0 %collective-permute-start.14 = (bf16[2,64,1024]{2,1,0:T(8,128)(2,1)S(1)}, bf16[2,64,1024]{2,1,0:T(8,128)(2,1)S(1)}, u32[]{:S(2)}, u32[]{:S(2)}) collective-permute-start(bf16[2,64,1024]{2,1,0:T(8,128)(2,1)S(1)} %sites.1.refs_0_), channel_id=1, source_target_pairs={{0,1},{1,0},{2,3},{3,2},{4,5},{5,4},{6,7},{7,6},{8,9},{9,8},{10,11... | collective-permute-start | bytes 786440 | tf_op jit(solution)/shard_map/ppermute | solution.py:35
  54.0 2.4 %collective-permute-start.18 = (bf16[64,512]{1,0:T(8,128)(2,1)S(1)}, bf16[64,512]{1,0:T(8,128)(2,1)S(1)}, u32[]{:S(2)}, u32[]{:S(2)}) collective-permute-start(bf16[64,512]{1,0:T(8,128)(2,1)S(1)} %get-tuple-element.62._.refs_2_), channel_id=1, source_target_pairs={{0,1},{1,0},{2,3},{3,2},{4,5},{5,4},{6,7},{7,6},{8,9},{9,8},{10,11... | collective-permute-start | bytes 196616 | tf_op jit(solution)/shard_map/ppermute | solution.py:35
  55.9 1.3 %collective-permute-start.21 = (bf16[64,512]{1,0:T(8,128)(2,1)S(1)}, bf16[64,512]{1,0:T(8,128)(2,1)S(1)}, u32[]{:S(2)}, u32[]{:S(2)}) collective-permute-start(bf16[64,512]{1,0:T(8,128)(2,1)S(1)} %collective-permute-done.17.refs_5_), channel_id=1, source_target_pairs={{0,1},{1,0},{2,3},{3,2},{4,5},{5,4},{6,7},{7,6},{8,9},{9,8},{10,11... | collective-permute-start | bytes 196616 | tf_op jit(solution)/shard_map/ppermute | solution.py:35
  55.9 1.4 %collective-permute-start.20 = (bf16[64,512]{1,0:T(8,128)(2,1)S(1)}, bf16[64,512]{1,0:T(8,128)(2,1)S(1)}, u32[]{:S(2)}, u32[]{:S(2)}) collective-permute-start(bf16[64,512]{1,0:T(8,128)(2,1)S(1)} %collective-permute-done.16.refs_4_), channel_id=1, source_target_pairs={{0,1},{1,0},{2,3},{3,2},{4,5},{5,4},{6,7},{7,6},{8,9},{9,8},{10,11... | collective-permute-start | bytes 196616 | tf_op jit(solution)/shard_map/ppermute | solution.py:35
  56.4 1.3 %collective-permute-start.19 = (bf16[64,512]{1,0:T(8,128)(2,1)S(1)}, bf16[64,512]{1,0:T(8,128)(2,1)S(1)}, u32[]{:S(2)}, u32[]{:S(2)}) collective-permute-start(bf16[64,512]{1,0:T(8,128)(2,1)S(1)} %collective-permute-done.15.refs_3_), channel_id=1, source_target_pairs={{0,1},{1,0},{2,3},{3,2},{4,5},{5,4},{6,7},{7,6},{8,9},{9,8},{10,11... | collective-permute-start | bytes 196616 | tf_op jit(solution)/shard_map/ppermute | solution.py:35

commit v17 on v16

--- a/solution.py
+++ b/solution.py
@@ -65,27 +65,17 @@
     return lax.bitwise_xor(lax.axis_index("dp"), owner[b])
 
 
-def pack_kernel(n_dp, n_mp, n_pair, table, down, up, w, *refs):
-    away = n_dp - 1
-    ups, downs, pieces, rows, sem = refs[:away], refs[away:2 * away], refs[2 * away:-2], refs[-2], refs[-1]
-    feat = w.shape[0] // n_mp
-    part = feat // n_pair
-    fetches, copies = [], []
-    for s in range(1, n_mp):
-        row = lax.rem(lax.axis_index("mp") + s, n_mp) * feat + lax.axis_index("pair") * part
-        row = pl.multiple_of(row, part)
-        fetches.append(pltpu.make_async_copy(w.at[pl.ds(row, part)], rows.at[s - 1], sem.at[s - 1]))
-        fetches[-1].start()
+def pack_kernel(n_dp, n_mp, table, down, up, *refs):
+    away, n_other = n_dp - 1, n_mp - 1
+    rows, refs, sem = refs[:n_other], refs[n_other:-1], refs[-1]
+    ups, downs, pieces = refs[:away], refs[away:2 * away], refs[2 * away:]
+    copies = [pltpu.make_async_copy(rows[s], pieces[s], sem.at[s]) for s in range(n_other)]
     for s in range(away):
         site = wanted_site(table, n_dp, s + 1)
-        copies.append(pltpu.make_async_copy(up.at[site], ups[s], sem.at[n_mp - 1 + s]))
-        copies.append(pltpu.make_async_copy(down.at[site], downs[s], sem.at[n_mp - 1 + away + s]))
+        copies.append(pltpu.make_async_copy(up.at[site], ups[s], sem.at[n_other + s]))
+        copies.append(pltpu.make_async_copy(down.at[site], downs[s], sem.at[n_other + away + s]))
     for copy in copies:
         copy.start()
-    for s, fetch in enumerate(fetches):
-        fetch.wait()
-        copies.append(pltpu.make_async_copy(rows.at[s], pieces[s], sem.at[n_mp - 1 + 2 * away + s]))
-        copies[-1].start()
     for copy in copies:
         copy.wait()
 
@@ -228,12 +218,16 @@
     whole = lambda *dims: pl.BlockSpec(dims, lambda i: (0,) * len(dims))
 
     away = n_dp - 1
+    def sent_rows(s):
+        return lambda i: (lax.rem(lax.axis_index("mp") + s, n_mp) * n_pair + lax.axis_index("pair"), 0)
+
     packed = call(
-        functools.partial(pack_kernel, n_dp, n_mp, n_pair), "pack",
+        functools.partial(pack_kernel, n_dp, n_mp), "pack",
         [shape(rank, cols)] * away + [shape(rank, feat)] * away + [shape(part, cols)] * n_other,
-        [SMEM, VMEM, VMEM, ANY], [ANY] * (2 * away + n_other),
-        [pltpu.VMEM((n_other, part, cols), BF16), pltpu.SemaphoreType.DMA((2 * away + 2 * n_other,))], mib=60,
-    )(table, down, up, w)
+        [SMEM, whole(*down.shape), whole(*up.shape)] + [pl.BlockSpec((part, cols), sent_rows(s)) for s in range(1, n_mp)],
+        [ANY] * (2 * away + n_other),
+        [pltpu.SemaphoreType.DMA((2 * away + n_other,))], mib=60, grid=(1,),
+    )(table, down, up, *[w] * n_other)
     pieces = [shift(packed[2 * away + s - 1], "mp", s) for s in range(1, n_mp)]
     ups = [swap(packed[s - 1], "dp", s) for s in range(1, n_dp)]
     downs = [swap(after(packed[away + s - 1], ups[away - 1]), "dp", s) for s in range(1, n_dp)]

time: 59.6 us -> 58.6 us (0.983)
  Pallas kernels: 17.7 us -> 16.8 us
    pallas_call x1, Pallas kernels: 3.28 us -> 2.38 us  [shards(): call(functools.partial(pack_kernel, n_dp, n_mp), 'pack', [shape(rank, col...]
where the time goes in v17:
time: 58.6 us; the launch traced here: 58.5 us
  starting transfers between devices  27.6 us (47%)
  Pallas kernels  16.8 us (29%)
  waiting for transfers between devices  13.2 us (23%)
  between operations  0.82 us (1%)
    ppermute x12, starting transfers between devices, swap(): lax.ppermute(value, axis, [(i, i ^ mask) for i in range(lax.axis_size(axi...  19.2 us
    ppermute x11, starting transfers between devices, shift(): lax.ppermute(value, axis, [(i, (i + by) % size) for i in range(size)])  8.45 us
    ppermute x11, waiting for transfers between devices, shift(): lax.ppermute(value, axis, [(i, (i + by) % size) for i in range(size)])  7.18 us
    ppermute x12, waiting for transfers between devices, swap(): lax.ppermute(value, axis, [(i, i ^ mask) for i in range(lax.axis_size(axi...  6.03 us
    pallas_call x1, Pallas kernels, shards(): call(functools.partial(back_kernel, n_dp, n_mp), 'back', [shape(tok, feat...  4.07 us
    pallas_call x2, Pallas kernels, gradient(): call(functools.partial(grad_kernel, n_dp, n_mp, len(behind)), name + '_gr...  2.45 us
    pallas_call x2, Pallas kernels, low_rank(): call(functools.partial(reduce_kernel, n_dp), name + '_part', shape(tok //...  2.42 us
    pallas_call x1, Pallas kernels, shards(): call(functools.partial(pack_kernel, n_dp, n_mp), 'pack', [shape(rank, col...  2.38 us
  transfers between devices with their start and end apart: 23, of which 10 were waited for; matrix products, arithmetic and copies ran while one was open for 0% of the time, Pallas kernels for 22%

profile of v17, /device:TPU:0, one launch (start us, length us, event | category | flops | bytes accessed | tf_op | source)
XLA Modules:
  0.0 58.5 jit_solution(640118180093136262)
XLA Ops:
  0.7 2.4 %pack.1 = (bf16[64,512]{1,0:T(8,128)(2,1)}, bf16[64,512]{1,0:T(8,128)(2,1)}, bf16[64,512]{1,0:T(8,128)(2,1)}, bf16[64,1024]{1,0:T(8,128)(2,1)}, bf16[64,1024]{1,...) custom-call(s32[1,2,4]{2,1,0:T(2,128)} %table.9, bf16[2,64,1024]{2,1,0:T(8,128)(2,1)} %bitcast.2, ...), custom_call_target="tpu_custom_call" | custom-call | flops 1 | bytes 1 | tf_op jit(solution)/shard_map/pack/pallas_call | solution.py:224
  3.1 3.0 %collective-permute-start = (bf16[512,512]{1,0:T(8,128)(2,1)}, bf16[512,512]{1,0:T(8,128)(2,1)S(1)}, u32[]{:S(2)}, u32[]{:S(2)}) collective-permute-start(bf16[512,512]{1,0:T(8,128)(2,1)} %get-tuple-element.38), channel_id=1, source_target_pairs={{0,2},{2,0},{1,3},{3,1},{4,6},{6,4},{5,7},{7,5},{8,10},{10,8},{9,1... | collective-permute-start | bytes 1572872 | tf_op jit(solution)/shard_map/ppermute | solution.py:35
  6.1 3.6 %collective-permute-start.2 = (bf16[64,512]{1,0:T(8,128)(2,1)}, bf16[64,512]{1,0:T(8,128)(2,1)S(1)}, u32[]{:S(2)}, u32[]{:S(2)}) collective-permute-start(bf16[64,512]{1,0:T(8,128)(2,1)} %get-tuple-element.41), channel_id=1, source_target_pairs={{0,12},{4,8},{8,4},{12,0},{1,13},{5,9},{9,5},{13,1},{2,14},{6,10},... | collective-permute-start | bytes 196616 | tf_op jit(solution)/shard_map/ppermute | solution.py:39
  9.7 0.8 %collective-permute-start.7 = (bf16[64,512]{1,0:T(8,128)(2,1)}, bf16[64,512]{1,0:T(8,128)(2,1)S(1)}, u32[]{:S(2)}, u32[]{:S(2)}) collective-permute-start(bf16[64,512]{1,0:T(8,128)(2,1)} %get-tuple-element.48), channel_id=1, source_target_pairs={{0,8},{4,12},{8,0},{12,4},{1,9},{5,13},{9,1},{13,5},{2,10},{6,14},... | collective-permute-start | bytes 196616 | tf_op jit(solution)/shard_map/ppermute | solution.py:39
  10.5 2.1 %collective-permute-done.2.refs_2_ = bf16[64,512]{1,0:T(8,128)(2,1)S(1)} collective-permute-done((bf16[64,512]{1,0:T(8,128)(2,1)}, bf16[64,512]{1,0:T(8,128)(2,1)S(1)}, u32[]{:S(2)}, u32[]{:S(2)}) %collective-permute-start.2) | collective-permute-done | bytes 65568 | tf_op jit(solution)/shard_map/ppermute | solution.py:39
  12.6 4.7 %collective-permute-start.4 = (bf16[64,1024]{1,0:T(8,128)(2,1)}, bf16[64,1024]{1,0:T(8,128)(2,1)S(1)}, u32[]{:S(2)}, u32[]{:S(2)}) collective-permute-start(bf16[64,1024]{1,0:T(8,128)(2,1)} %get-tuple-element.44), channel_id=1, source_target_pairs={{0,8},{4,12},{8,0},{12,4},{1,9},{5,13},{9,1},{13,5},{2,10},{6,14},... | collective-permute-start | bytes 393224 | tf_op jit(solution)/shard_map/ppermute | solution.py:39
  17.4 1.1 %h_part.1.refs_3_ = bf16[384,128]{1,0:T(8,128)(2,1)S(1)} custom-call(s32[12]{0:T(128)S(1)} %copy-done.6, s32[1,2,4]{2,1,0:T(2,128)S(1)} %copy-done.5, bf16[768,512]{1,0:T(8,128)(2,1)S(1)} %copy-done.2, bf16[64,512]{1,0:T(8,128)(2,1)S(1)} %collective-permute-done.6._.refs_0_, bf16[2,64,512]{2,1,0:T(8,128)(2,1)S(1)} %copy-done.4, ...), custom_call_target="tpu_custom_call" | custom-call | flops 1 | bytes 1 | tf_op jit(solution)/shard_map/h_part/pallas_call | solution.py:236
  18.5 0.6 %collective-permute-start.8 = (bf16[384,128]{1,0:T(8,128)(2,1)S(1)}, bf16[384,128]{1,0:T(8,128)(2,1)S(1)}, u32[]{:S(2)}, u32[]{:S(2)}) collective-permute-start(bf16[384,128]{1,0:T(8,128)(2,1)S(1)} %h_part.1.refs_3_), channel_id=1, source_target_pairs={{0,2},{2,0},{1,3},{3,1},{4,6},{6,4},{5,7},{7,5},{8,10},{10,8},{9,1... | collective-permute-start | bytes 294920 | tf_op jit(solution)/shard_map/ppermute | solution.py:35
  19.1 1.9 %collective-permute-start.1 = (bf16[768,512]{1,0:T(8,128)(2,1)S(1)}, bf16[768,512]{1,0:T(8,128)(2,1)S(1)}, u32[]{:S(2)}, u32[]{:S(2)}) collective-permute-start(bf16[768,512]{1,0:T(8,128)(2,1)S(1)} %copy-done.2), channel_id=1, source_target_pairs={{0,2},{2,0},{1,3},{3,1},{4,6},{6,4},{5,7},{7,5},{8,10},{10,8},{9,1... | collective-permute-start | bytes 2359304 | tf_op jit(solution)/shard_map/ppermute | solution.py:35
  20.9 3.3 %collective-permute-done.8.refs_4_ = bf16[384,128]{1,0:T(8,128)(2,1)S(1)} collective-permute-done((bf16[384,128]{1,0:T(8,128)(2,1)S(1)}, bf16[384,128]{1,0:T(8,128)(2,1)S(1)}, u32[]{:S(2)}, u32[]{:S(2)}) %collective-permute-start.8) | collective-permute-done | bytes 98336 | tf_op jit(solution)/shard_map/ppermute | solution.py:35
  24.3 2.1 %collective-permute-done.4.refs_1_.refs_7_ = bf16[64,1024]{1,0:T(8,128)(2,1)S(1)} collective-permute-done((bf16[64,1024]{1,0:T(8,128)(2,1)}, bf16[64,1024]{1,0:T(8,128)(2,1)S(1)}, u32[]{:S(2)}, u32[]{:S(2)}) %collective-permute-start.4) | collective-permute-done | bytes 131104 | tf_op jit(solution)/shard_map/ppermute | solution.py:39
  26.4 1.3 %down_grad.1 = (bf16[64,1024]{1,0:T(8,128)(2,1)S(1)}, bf16[64,1024]{1,0:T(8,128)(2,1)S(1)}, bf16[64,1024]{1,0:T(8,128)(2,1)S(1)}, bf16[64,1024]{1,0:T(8,128)(2,1)S(1)}, bf16[768,256]{1,0:T(8,128)(2,1)S(1)}) custom-call(s32[12]{0:T(128)S(1)} %copy-done.6, bf16[768,1024]{1,0:T(8,128)(2,1)S(1)} %copy-done.1, ...), custom_call_target="tpu_custom_call" | custom-call | flops 15000000512 | bytes 1 | tf_op jit(solution)/shard_map/down_grad/pallas_call | solution.py:244
  27.8 2.0 %collective-permute-start.10 = (bf16[64,1024]{1,0:T(8,128)(2,1)S(1)}, bf16[64,1024]{1,0:T(8,128)(2,1)S(1)}, u32[]{:S(2)}, u32[]{:S(2)}) collective-permute-start(bf16[64,1024]{1,0:T(8,128)(2,1)S(1)} %get-tuple-element.53), channel_id=1, source_target_pairs={{0,4},{4,0},{8,12},{12,8},{1,5},{5,1},{9,13},{13,9},{2,6},{6,2},{1... | collective-permute-start | bytes 393224 | tf_op jit(solution)/shard_map/ppermute | solution.py:39
  29.8 1.0 %collective-permute-start.11 = (bf16[64,1024]{1,0:T(8,128)(2,1)S(1)}, bf16[64,1024]{1,0:T(8,128)(2,1)S(1)}, u32[]{:S(2)}, u32[]{:S(2)}) collective-permute-start(bf16[64,1024]{1,0:T(8,128)(2,1)S(1)} %get-tuple-element.54), channel_id=1, source_target_pairs={{0,8},{4,12},{8,0},{12,4},{1,9},{5,13},{9,1},{13,5},{2,10},{6,14},... | collective-permute-start | bytes 393224 | tf_op jit(solution)/shard_map/ppermute | solution.py:39
  30.8 1.5 %collective-permute-start.12 = (bf16[64,1024]{1,0:T(8,128)(2,1)S(1)}, bf16[64,1024]{1,0:T(8,128)(2,1)S(1)}, u32[]{:S(2)}, u32[]{:S(2)}) collective-permute-start(bf16[64,1024]{1,0:T(8,128)(2,1)S(1)} %get-tuple-element.55), channel_id=1, source_target_pairs={{0,12},{4,8},{8,4},{12,0},{1,13},{5,9},{9,5},{13,1},{2,14},{6,10},... | collective-permute-start | bytes 393224 | tf_op jit(solution)/shard_map/ppermute | solution.py:39
  32.3 1.3 %u_part.1._.refs_5_ = bf16[384,128]{1,0:T(8,128)(2,1)S(1)} custom-call(s32[12]{0:T(128)S(1)} %copy-done.6, s32[1,2,4]{2,1,0:T(2,128)S(1)} %copy-done.5, bf16[768,1024]{1,0:T(8,128)(2,1)S(1)} %copy-done.1, bf16[512,512]{1,0:T(8,128)(2,1)S(1)} %collective-permute-done.9._.refs_1_, bf16[2,64,1024]{2,1,0:T(8,128)(2,1)S(1)} %bitcast.3, ...), custom_call_target="tpu_custom_call" | custom-call | flops 1 | bytes 1 | tf_op jit(solution)/shard_map/u_part/pallas_call | solution.py:236
  33.6 0.6 %collective-permute-start.13 = (bf16[384,128]{1,0:T(8,128)(2,1)S(1)}, bf16[384,128]{1,0:T(8,128)(2,1)S(1)}, u32[]{:S(2)}, u32[]{:S(2)}) collective-permute-start(bf16[384,128]{1,0:T(8,128)(2,1)S(1)} %u_part.1._.refs_5_), channel_id=1, source_target_pairs={{0,2},{2,0},{1,3},{3,1},{4,6},{6,4},{5,7},{7,5},{8,10},{10,8},{9,1... | collective-permute-start | bytes 294920 | tf_op jit(solution)/shard_map/ppermute | solution.py:35
  34.2 1.4 %y_send.1 = (bf16[768,512]{1,0:T(8,128)(2,1)S(1)}, bf16[1024,512]{1,0:T(8,128)(2,1)S(1)}) custom-call(bf16[384,128]{1,0:T(8,128)(2,1)S(1)} %u_part.1._.refs_5_, bf16[768,256]{1,0:T(8,128)(2,1)S(1)} %get-tuple-element.49.__.refs_4_, bf16[768,1024]{1,0:T(8,128)(2,1)S(1)} %copy-done.1, bf16[512,512]{1,0:T(8,128)(2,1)S(1)} %collective-permute-done.refs_0_, ...), custom_call_target="tpu_custom_call" | custom-call | flops 1 | bytes 1 | tf_op jit(solution)/shard_map/y_send/pallas_call | solution.py:260
  35.6 0.4 collective-permute-done.10.refs_1_
  36.1 1.1 %collective-permute-start.22 = (bf16[768,512]{1,0:T(8,128)(2,1)S(1)}, bf16[768,512]{1,0:T(8,128)(2,1)S(1)}, u32[]{:S(2)}, u32[]{:S(2)}) collective-permute-start(bf16[768,512]{1,0:T(8,128)(2,1)S(1)} %get-tuple-element.67), channel_id=1, source_target_pairs={{0,2},{2,0},{1,3},{3,1},{4,6},{6,4},{5,7},{7,5},{8,10},{10,8},{9,1... | collective-permute-start | bytes 2359304 | tf_op jit(solution)/shard_map/ppermute | solution.py:35
  37.2 2.5 %collective-permute-done.1.refs_2_.refs_4_ = bf16[768,512]{1,0:T(8,128)(2,1)S(1)} collective-permute-done((bf16[768,512]{1,0:T(8,128)(2,1)S(1)}, bf16[768,512]{1,0:T(8,128)(2,1)S(1)}, u32[]{:S(2)}, u32[]{:S(2)}) %collective-permute-start.1) | collective-permute-done | bytes 786464 | tf_op jit(solution)/shard_map/ppermute | solution.py:35
  39.7 4.1 %back.1 = (bf16[768,1024]{1,0:T(8,128)(2,1)}, s32[8,128]{1,0:T(8,128)S(1)}) custom-call(s32[1,2,4]{2,1,0:T(2,128)S(1)} %copy-done.5, bf16[2048,512]{1,0:T(8,128)(2,1)S(1)} %copy-done, bf16[768,512]{1,0:T(8,128)(2,1)S(1)} %copy-done.2, bf16[768,512]{1,0:T(8,128)(2,1)S(1)} %collective-permute-done.1.refs_2_.refs_4_, ...), custom_call_target="tpu_custom_call" | custom-call | flops 1 | bytes 1 | tf_op jit(solution)/shard_map/back/pallas_call | solution.py:269
  43.8 1.1 %up_grad.1 = (bf16[64,512]{1,0:T(8,128)(2,1)S(1)}, bf16[64,512]{1,0:T(8,128)(2,1)S(1)}, bf16[64,512]{1,0:T(8,128)(2,1)S(1)}, bf16[64,512]{1,0:T(8,128)(2,1)S(1)}, bf16[768,256]{1,0:T(8,128)(2,1)S(1)}) custom-call(s32[12]{0:T(128)S(1)} %copy-done.6, bf16[768,512]{1,0:T(8,128)(2,1)S(1)} %copy-done.2, s32[8,128]{1,0:T(8,128)S(1)} %get-tuple-element.52.refs_0_.picks, ...), custom_call_target="tpu_custom_call" | custom-call | flops 15000000512 | bytes 1 | tf_op jit(solution)/shard_map/up_grad/pallas_call | solution.py:244
  44.9 4.9 %collective-permute-start.17 = (bf16[64,512]{1,0:T(8,128)(2,1)S(1)}, bf16[64,512]{1,0:T(8,128)(2,1)S(1)}, u32[]{:S(2)}, u32[]{:S(2)}) collective-permute-start(bf16[64,512]{1,0:T(8,128)(2,1)S(1)} %get-tuple-element.60), channel_id=1, source_target_pairs={{0,12},{4,8},{8,4},{12,0},{1,13},{5,9},{9,5},{13,1},{2,14},{6,10},... | collective-permute-start | bytes 196616 | tf_op jit(solution)/shard_map/ppermute | solution.py:39
  49.9 0.6 %collective-permute-start.15 = (bf16[64,512]{1,0:T(8,128)(2,1)S(1)}, bf16[64,512]{1,0:T(8,128)(2,1)S(1)}, u32[]{:S(2)}, u32[]{:S(2)}) collective-permute-start(bf16[64,512]{1,0:T(8,128)(2,1)S(1)} %get-tuple-element.58), channel_id=1, source_target_pairs={{0,4},{4,0},{8,12},{12,8},{1,5},{5,1},{9,13},{13,9},{2,6},{6,2},{1... | collective-permute-start | bytes 196616 | tf_op jit(solution)/shard_map/ppermute | solution.py:39
  50.9 2.2 %y_own.1.refs_10_ = bf16[768,512]{1,0:T(8,128)(2,1)S(1)} custom-call(s32[1,2,4]{2,1,0:T(2,128)S(1)} %copy-done.5, bf16[2048,512]{1,0:T(8,128)(2,1)S(1)} %copy-done, bf16[768,1024]{1,0:T(8,128)(2,1)S(1)} %copy-done.1, bf16[768,256]{1,0:T(8,128)(2,1)S(1)} %get-tuple-element.61.wide, bf16[2,64,512]{2,1,0:T(8,128)(2,1)S(1)} %copy-done.4, ...), custom_call_target="tpu_custom_call" | custom-call | flops 15000000512 | bytes 1 | tf_op jit(solution)/shard_map/y_own/pallas_call | solution.py:279
  53.1 0.5 collective-permute-start.18
  53.6 1.4 %collective-permute-done.16.refs_4_ = bf16[64,512]{1,0:T(8,128)(2,1)S(1)} collective-permute-done((bf16[64,512]{1,0:T(8,128)(2,1)S(1)}, bf16[64,512]{1,0:T(8,128)(2,1)S(1)}, u32[]{:S(2)}, u32[]{:S(2)}) %collective-permute-start.16) | collective-permute-done | bytes 65568 | tf_op jit(solution)/shard_map/ppermute | solution.py:39
  55.0 0.5 collective-permute-start.20
  55.6 0.7 %collective-permute-done.21.refs_9_ = bf16[64,512]{1,0:T(8,128)(2,1)S(1)} collective-permute-done((bf16[64,512]{1,0:T(8,128)(2,1)S(1)}, bf16[64,512]{1,0:T(8,128)(2,1)S(1)}, u32[]{:S(2)}, u32[]{:S(2)}) %collective-permute-start.21) | collective-permute-done | bytes 65568 | tf_op jit(solution)/shard_map/ppermute | solution.py:35
  56.4 0.4 collective-permute-done.19.refs_7_
  57.0 1.5 %last.1 = (f32[2,64,1024]{2,1,0:T(8,128)}, f32[2,64,512]{2,1,0:T(8,128)}, bf16[768,512]{1,0:T(8,128)(2,1)}) custom-call(s32[8,128]{1,0:T(8,128)S(1)} %get-tuple-element.52.refs_0_.picks, bf16[2,64,1024]{2,1,0:T(8,128)(2,1)S(1)} %sites.1.refs_0_, bf16[2,64,1024]{2,1,0:T(8,128)(2,1)S(1)} %collective-permute-done.14.refs_1_, ...), custom_call_target="tpu_custom_call" | custom-call | flops 1 | bytes 1 | tf_op jit(solution)/shard_map/last/pallas_call | solution.py:294
  (38 shorter events, 1.0 us)
Async XLA Ops:
  0.6 16.7 %copy-start.4 = (bf16[2,64,512]{2,1,0:T(8,128)(2,1)S(1)}, bf16[2,64,512]{2,1,0:T(8,128)(2,1)}, u32[]{:S(2)}) copy-start(bf16[2,64,512]{2,1,0:T(8,128)(2,1)} %own_up.1) | copy-start | bytes 393220
  0.6 16.7 %copy-start.5 = (s32[1,2,4]{2,1,0:T(2,128)S(1)}, s32[1,2,4]{2,1,0:T(2,128)}, u32[]{:S(2)}) copy-start(s32[1,2,4]{2,1,0:T(2,128)} %table.9) | copy-start | bytes 100
  0.7 16.7 %copy-start.2 = (bf16[768,512]{1,0:T(8,128)(2,1)S(1)}, bf16[768,512]{1,0:T(8,128)(2,1)}, u32[]{:S(2)}) copy-start(bf16[768,512]{1,0:T(8,128)(2,1)} %act.7) | copy-start | bytes 2359300
  0.7 16.7 %copy-start.6 = (s32[12]{0:T(128)S(1)}, s32[12]{0:T(128)}, u32[]{:S(2)}) copy-start(s32[12]{0:T(128)} %owner.7) | copy-start | bytes 148
  0.7 25.7 %copy-start.1 = (bf16[768,1024]{1,0:T(8,128)(2,1)S(1)}, bf16[768,1024]{1,0:T(8,128)(2,1)}, u32[]{:S(2)}) copy-start(bf16[768,1024]{1,0:T(8,128)(2,1)} %x.3) | copy-start | bytes 4718596
  3.1 16.0 %collective-permute-start = (bf16[512,512]{1,0:T(8,128)(2,1)}, bf16[512,512]{1,0:T(8,128)(2,1)S(1)}, u32[]{:S(2)}, u32[]{:S(2)}) collective-permute-start(bf16[512,512]{1,0:T(8,128)(2,1)} %get-tuple-element.38), channel_id=1, source_target_pairs={{0,2},{2,0},{1,3},{3,1},{4,6},{6,4},{5,7},{7,5},{8,10},{10,8},{9,1... | collective-permute-start | bytes 1572872 | tf_op jit(solution)/shard_map/ppermute | solution.py:35
  6.1 6.5 %collective-permute-start.2 = (bf16[64,512]{1,0:T(8,128)(2,1)}, bf16[64,512]{1,0:T(8,128)(2,1)S(1)}, u32[]{:S(2)}, u32[]{:S(2)}) collective-permute-start(bf16[64,512]{1,0:T(8,128)(2,1)} %get-tuple-element.41), channel_id=1, source_target_pairs={{0,12},{4,8},{8,4},{12,0},{1,13},{5,9},{9,5},{13,1},{2,14},{6,10},... | collective-permute-start | bytes 196616 | tf_op jit(solution)/shard_map/ppermute | solution.py:39
  9.7 7.6 %collective-permute-start.6 = (bf16[64,512]{1,0:T(8,128)(2,1)}, bf16[64,512]{1,0:T(8,128)(2,1)S(1)}, u32[]{:S(2)}, u32[]{:S(2)}) collective-permute-start(bf16[64,512]{1,0:T(8,128)(2,1)} %get-tuple-element.47), channel_id=1, source_target_pairs={{0,4},{4,0},{8,12},{12,8},{1,5},{5,1},{9,13},{13,9},{2,6},{6,2},{1... | collective-permute-start | bytes 196616 | tf_op jit(solution)/shard_map/ppermute | solution.py:39
  9.7 7.6 %collective-permute-start.7 = (bf16[64,512]{1,0:T(8,128)(2,1)}, bf16[64,512]{1,0:T(8,128)(2,1)S(1)}, u32[]{:S(2)}, u32[]{:S(2)}) collective-permute-start(bf16[64,512]{1,0:T(8,128)(2,1)} %get-tuple-element.48), channel_id=1, source_target_pairs={{0,8},{4,12},{8,0},{12,4},{1,9},{5,13},{9,1},{13,5},{2,10},{6,14},... | collective-permute-start | bytes 196616 | tf_op jit(solution)/shard_map/ppermute | solution.py:39
  12.6 11.7 %collective-permute-start.3 = (bf16[64,1024]{1,0:T(8,128)(2,1)}, bf16[64,1024]{1,0:T(8,128)(2,1)S(1)}, u32[]{:S(2)}, u32[]{:S(2)}) collective-permute-start(bf16[64,1024]{1,0:T(8,128)(2,1)} %get-tuple-element.42), channel_id=1, source_target_pairs={{0,4},{4,0},{8,12},{12,8},{1,5},{5,1},{9,13},{13,9},{2,6},{6,2},{1... | collective-permute-start | bytes 393224 | tf_op jit(solution)/shard_map/ppermute | solution.py:39
  12.6 13.8 %collective-permute-start.4 = (bf16[64,1024]{1,0:T(8,128)(2,1)}, bf16[64,1024]{1,0:T(8,128)(2,1)S(1)}, u32[]{:S(2)}, u32[]{:S(2)}) collective-permute-start(bf16[64,1024]{1,0:T(8,128)(2,1)} %get-tuple-element.44), channel_id=1, source_target_pairs={{0,8},{4,12},{8,0},{12,4},{1,9},{5,13},{9,1},{13,5},{2,10},{6,14},... | collective-permute-start | bytes 393224 | tf_op jit(solution)/shard_map/ppermute | solution.py:39
  17.3 9.1 %collective-permute-start.5 = (bf16[64,1024]{1,0:T(8,128)(2,1)}, bf16[64,1024]{1,0:T(8,128)(2,1)S(1)}, u32[]{:S(2)}, u32[]{:S(2)}) collective-permute-start(bf16[64,1024]{1,0:T(8,128)(2,1)} %get-tuple-element.46), channel_id=1, source_target_pairs={{0,12},{4,8},{8,4},{12,0},{1,13},{5,9},{9,5},{13,1},{2,14},{6,10},... | collective-permute-start | bytes 393224 | tf_op jit(solution)/shard_map/ppermute | solution.py:39
  18.5 13.8 %copy-start.3 = (bf16[2,1024,64]{1,2,0:T(8,128)(2,1)S(1)}, bf16[2,1024,64]{1,2,0:T(8,128)(2,1)}, u32[]{:S(2)}) copy-start(bf16[2,1024,64]{1,2,0:T(8,128)(2,1)} %param.9) | copy-start | bytes 786436
  18.5 5.8 %collective-permute-start.8 = (bf16[384,128]{1,0:T(8,128)(2,1)S(1)}, bf16[384,128]{1,0:T(8,128)(2,1)S(1)}, u32[]{:S(2)}, u32[]{:S(2)}) collective-permute-start(bf16[384,128]{1,0:T(8,128)(2,1)S(1)} %h_part.1.refs_3_), channel_id=1, source_target_pairs={{0,2},{2,0},{1,3},{3,1},{4,6},{6,4},{5,7},{7,5},{8,10},{10,8},{9,1... | collective-permute-start | bytes 294920 | tf_op jit(solution)/shard_map/ppermute | solution.py:35
  19.1 20.6 %collective-permute-start.1 = (bf16[768,512]{1,0:T(8,128)(2,1)S(1)}, bf16[768,512]{1,0:T(8,128)(2,1)S(1)}, u32[]{:S(2)}, u32[]{:S(2)}) collective-permute-start(bf16[768,512]{1,0:T(8,128)(2,1)S(1)} %copy-done.2), channel_id=1, source_target_pairs={{0,2},{2,0},{1,3},{3,1},{4,6},{6,4},{5,7},{7,5},{8,10},{10,8},{9,1... | collective-permute-start | bytes 2359304 | tf_op jit(solution)/shard_map/ppermute | solution.py:35
  27.7 4.5 %collective-permute-start.9 = (bf16[512,512]{1,0:T(8,128)(2,1)S(1)}, bf16[512,512]{1,0:T(8,128)(2,1)S(1)}, u32[]{:S(2)}, u32[]{:S(2)}) collective-permute-start(bf16[512,512]{1,0:T(8,128)(2,1)S(1)} %collective-permute-done.refs_0_), channel_id=1, source_target_pairs={{0,1},{1,0},{2,3},{3,2},{4,5},{5,4},{6,7},{7,6},{8,9},{9,8},{10,11... | collective-permute-start | bytes 1572872 | tf_op jit(solution)/shard_map/ppermute | solution.py:35
  27.8 8.3 %collective-permute-start.10 = (bf16[64,1024]{1,0:T(8,128)(2,1)S(1)}, bf16[64,1024]{1,0:T(8,128)(2,1)S(1)}, u32[]{:S(2)}, u32[]{:S(2)}) collective-permute-start(bf16[64,1024]{1,0:T(8,128)(2,1)S(1)} %get-tuple-element.53), channel_id=1, source_target_pairs={{0,4},{4,0},{8,12},{12,8},{1,5},{5,1},{9,13},{13,9},{2,6},{6,2},{1... | collective-permute-start | bytes 393224 | tf_op jit(solution)/shard_map/ppermute | solution.py:39
  29.8 13.9 %collective-permute-start.11 = (bf16[64,1024]{1,0:T(8,128)(2,1)S(1)}, bf16[64,1024]{1,0:T(8,128)(2,1)S(1)}, u32[]{:S(2)}, u32[]{:S(2)}) collective-permute-start(bf16[64,1024]{1,0:T(8,128)(2,1)S(1)} %get-tuple-element.54), channel_id=1, source_target_pairs={{0,8},{4,12},{8,0},{12,4},{1,9},{5,13},{9,1},{13,5},{2,10},{6,14},... | collective-permute-start | bytes 393224 | tf_op jit(solution)/shard_map/ppermute | solution.py:39
  30.8 13.0 %collective-permute-start.12 = (bf16[64,1024]{1,0:T(8,128)(2,1)S(1)}, bf16[64,1024]{1,0:T(8,128)(2,1)S(1)}, u32[]{:S(2)}, u32[]{:S(2)}) collective-permute-start(bf16[64,1024]{1,0:T(8,128)(2,1)S(1)} %get-tuple-element.55), channel_id=1, source_target_pairs={{0,12},{4,8},{8,4},{12,0},{1,13},{5,9},{9,5},{13,1},{2,14},{6,10},... | collective-permute-start | bytes 393224 | tf_op jit(solution)/shard_map/ppermute | solution.py:39
  33.6 6.1 %copy-start = (bf16[2048,512]{1,0:T(8,128)(2,1)S(1)}, bf16[2048,512]{1,0:T(8,128)(2,1)}, u32[]{:S(2)}) copy-start(bf16[2048,512]{1,0:T(8,128)(2,1)} %w.1) | copy-start | bytes 6291460
  33.6 10.2 %collective-permute-start.13 = (bf16[384,128]{1,0:T(8,128)(2,1)S(1)}, bf16[384,128]{1,0:T(8,128)(2,1)S(1)}, u32[]{:S(2)}, u32[]{:S(2)}) collective-permute-start(bf16[384,128]{1,0:T(8,128)(2,1)S(1)} %u_part.1._.refs_5_), channel_id=1, source_target_pairs={{0,2},{2,0},{1,3},{3,1},{4,6},{6,4},{5,7},{7,5},{8,10},{10,8},{9,1... | collective-permute-start | bytes 294920 | tf_op jit(solution)/shard_map/ppermute | solution.py:35
  36.1 20.9 %collective-permute-start.22 = (bf16[768,512]{1,0:T(8,128)(2,1)S(1)}, bf16[768,512]{1,0:T(8,128)(2,1)S(1)}, u32[]{:S(2)}, u32[]{:S(2)}) collective-permute-start(bf16[768,512]{1,0:T(8,128)(2,1)S(1)} %get-tuple-element.67), channel_id=1, source_target_pairs={{0,2},{2,0},{1,3},{3,1},{4,6},{6,4},{5,7},{7,5},{8,10},{10,8},{9,1... | collective-permute-start | bytes 2359304 | tf_op jit(solution)/shard_map/ppermute | solution.py:35
  44.9 8.2 %collective-permute-start.17 = (bf16[64,512]{1,0:T(8,128)(2,1)S(1)}, bf16[64,512]{1,0:T(8,128)(2,1)S(1)}, u32[]{:S(2)}, u32[]{:S(2)}) collective-permute-start(bf16[64,512]{1,0:T(8,128)(2,1)S(1)} %get-tuple-element.60), channel_id=1, source_target_pairs={{0,12},{4,8},{8,4},{12,0},{1,13},{5,9},{9,5},{13,1},{2,14},{6,10},... | collective-permute-start | bytes 196616 | tf_op jit(solution)/shard_map/ppermute | solution.py:39
  49.9 5.2 %collective-permute-start.16 = (bf16[64,512]{1,0:T(8,128)(2,1)S(1)}, bf16[64,512]{1,0:T(8,128)(2,1)S(1)}, u32[]{:S(2)}, u32[]{:S(2)}) collective-permute-start(bf16[64,512]{1,0:T(8,128)(2,1)S(1)} %get-tuple-element.59), channel_id=1, source_target_pairs={{0,8},{4,12},{8,0},{12,4},{1,9},{5,13},{9,1},{13,5},{2,10},{6,14},... | collective-permute-start | bytes 196616 | tf_op jit(solution)/shard_map/ppermute | solution.py:39
  49.9 5.2 %collective-permute-start.15 = (bf16[64,512]{1,0:T(8,128)(2,1)S(1)}, bf16[64,512]{1,0:T(8,128)(2,1)S(1)}, u32[]{:S(2)}, u32[]{:S(2)}) collective-permute-start(bf16[64,512]{1,0:T(8,128)(2,1)S(1)} %get-tuple-element.58), channel_id=1, source_target_pairs={{0,4},{4,0},{8,12},{12,8},{1,5},{5,1},{9,13},{13,9},{2,6},{6,2},{1... | collective-permute-start | bytes 196616 | tf_op jit(solution)/shard_map/ppermute | solution.py:39
  50.8 6.0 %collective-permute-start.14 = (bf16[2,64,1024]{2,1,0:T(8,128)(2,1)S(1)}, bf16[2,64,1024]{2,1,0:T(8,128)(2,1)S(1)}, u32[]{:S(2)}, u32[]{:S(2)}) collective-permute-start(bf16[2,64,1024]{2,1,0:T(8,128)(2,1)S(1)} %sites.1.refs_0_), channel_id=1, source_target_pairs={{0,1},{1,0},{2,3},{3,2},{4,5},{5,4},{6,7},{7,6},{8,9},{9,8},{10,11... | collective-permute-start | bytes 786440 | tf_op jit(solution)/shard_map/ppermute | solution.py:35
  53.1 2.4 %collective-permute-start.18 = (bf16[64,512]{1,0:T(8,128)(2,1)S(1)}, bf16[64,512]{1,0:T(8,128)(2,1)S(1)}, u32[]{:S(2)}, u32[]{:S(2)}) collective-permute-start(bf16[64,512]{1,0:T(8,128)(2,1)S(1)} %get-tuple-element.62._.refs_2_), channel_id=1, source_target_pairs={{0,1},{1,0},{2,3},{3,2},{4,5},{5,4},{6,7},{7,6},{8,9},{9,8},{10,11... | collective-permute-start | bytes 196616 | tf_op jit(solution)/shard_map/ppermute | solution.py:35
  55.0 1.3 %collective-permute-start.21 = (bf16[64,512]{1,0:T(8,128)(2,1)S(1)}, bf16[64,512]{1,0:T(8,128)(2,1)S(1)}, u32[]{:S(2)}, u32[]{:S(2)}) collective-permute-start(bf16[64,512]{1,0:T(8,128)(2,1)S(1)} %collective-permute-done.17.refs_5_), channel_id=1, source_target_pairs={{0,1},{1,0},{2,3},{3,2},{4,5},{5,4},{6,7},{7,6},{8,9},{9,8},{10,11... | collective-permute-start | bytes 196616 | tf_op jit(solution)/shard_map/ppermute | solution.py:35
  55.0 1.4 %collective-permute-start.20 = (bf16[64,512]{1,0:T(8,128)(2,1)S(1)}, bf16[64,512]{1,0:T(8,128)(2,1)S(1)}, u32[]{:S(2)}, u32[]{:S(2)}) collective-permute-start(bf16[64,512]{1,0:T(8,128)(2,1)S(1)} %collective-permute-done.16.refs_4_), channel_id=1, source_target_pairs={{0,1},{1,0},{2,3},{3,2},{4,5},{5,4},{6,7},{7,6},{8,9},{9,8},{10,11... | collective-permute-start | bytes 196616 | tf_op jit(solution)/shard_map/ppermute | solution.py:35
  55.5 1.3 %collective-permute-start.19 = (bf16[64,512]{1,0:T(8,128)(2,1)S(1)}, bf16[64,512]{1,0:T(8,128)(2,1)S(1)}, u32[]{:S(2)}, u32[]{:S(2)}) collective-permute-start(bf16[64,512]{1,0:T(8,128)(2,1)S(1)} %collective-permute-done.15.refs_3_), channel_id=1, source_target_pairs={{0,1},{1,0},{2,3},{3,2},{4,5},{5,4},{6,7},{7,6},{8,9},{9,8},{10,11... | collective-permute-start | bytes 196616 | tf_op jit(solution)/shard_map/ppermute | solution.py:35

commit v18 on v17

--- a/solution.py
+++ b/solution.py
@@ -191,14 +191,14 @@
         out[site] = pick_sum(grads, picks, site).astype(BF16)
 
 
-def last_kernel(n_pair, n_ups, n_mp, picks, *refs):
+def last_kernel(cuts, n_pair, n_ups, n_mp, picks, *refs):
     downs, ups, parts = refs[:n_pair], refs[n_pair:n_pair + n_ups], refs[n_pair + n_ups:n_pair + n_ups + n_mp]
     down, up, y = refs[-3:]
     total = downs[0][0].astype(F32)
     for part in downs[1:]:
         total = total + part[0].astype(F32)
     down[0] = SCALE * total
-    up[0] = SCALE * pick_sum(ups, picks, pl.program_id(0))
+    up[0] = SCALE * pick_sum(ups, picks, pl.program_id(0) // cuts)
     total = parts[0][...].astype(F32)
     for part in parts[1:]:
         total = total + part[...].astype(F32)
@@ -288,14 +288,16 @@
     )(picks, up_back[0], *down_back)
     both = [summed] + [shift(summed, "pair", q) for q in range(1, n_pair)]
     up_all = [shift(after(one, y_own), "pair", q) if q else one for q in range(n_pair) for one in up_back]
-    rows = tok // sites
-    of_site = lambda width: pl.BlockSpec((1, rank, width), lambda i: (i, 0, 0))
+    cuts = 2
+    rows = tok // (sites * cuts)
+    of_site = lambda width: pl.BlockSpec((1, rank // cuts, width), lambda i: (i // cuts, i % cuts, 0))
+    of_slot = pl.BlockSpec((rank // cuts, cols), lambda i: (i % cuts, 0))
     out_rows = pl.BlockSpec((rows, cols), lambda i: (i, 0))
     down_grad, up_grad, y = call(
-        functools.partial(last_kernel, n_pair, n_pair * n_dp, n_mp), "last",
+        functools.partial(last_kernel, cuts, n_pair, n_pair * n_dp, n_mp), "last",
         [shape(sites, rank, feat, dtype=F32), shape(sites, rank, cols, dtype=F32), shape(tok, cols)],
-        [whole(*picks.shape)] + [of_site(feat)] * n_pair + [whole(rank, cols)] * (n_pair * n_dp) + [out_rows] * n_mp,
-        [of_site(feat), of_site(cols), out_rows], grid=(sites,),
+        [whole(*picks.shape)] + [of_site(feat)] * n_pair + [of_slot] * (n_pair * n_dp) + [out_rows] * n_mp,
+        [of_site(feat), of_site(cols), out_rows], grid=(sites * cuts,),
     )(picks, *both, *up_all, y_own, *y_got)
     return y, back, down_grad.transpose(0, 2, 1), up_grad
 

time: 58.6 us -> 59 us (level)
  no operation moved by 1% of the time
where the time goes in v18:
time: 59 us; the launch traced here: 58.8 us
  starting transfers between devices  27.6 us (47%)
  Pallas kernels  17.1 us (29%)
  waiting for transfers between devices  13.2 us (22%)
  between operations  0.82 us (1%)
    ppermute x12, starting transfers between devices, swap(): lax.ppermute(value, axis, [(i, i ^ mask) for i in range(lax.axis_size(axi...  19.2 us
    ppermute x11, starting transfers between devices, shift(): lax.ppermute(value, axis, [(i, (i + by) % size) for i in range(size)])  8.45 us
    ppermute x11, waiting for transfers between devices, shift(): lax.ppermute(value, axis, [(i, (i + by) % size) for i in range(size)])  7.18 us
    ppermute x12, waiting for transfers between devices, swap(): lax.ppermute(value, axis, [(i, i ^ mask) for i in range(lax.axis_size(axi...  6.03 us
    pallas_call x1, Pallas kernels, shards(): call(functools.partial(back_kernel, n_dp, n_mp), 'back', [shape(tok, feat...  4.07 us
    pallas_call x2, Pallas kernels, gradient(): call(functools.partial(grad_kernel, n_dp, n_mp, len(behind)), name + '_gr...  2.45 us
    pallas_call x2, Pallas kernels, low_rank(): call(functools.partial(reduce_kernel, n_dp), name + '_part', shape(tok //...  2.42 us
    pallas_call x1, Pallas kernels, shards(): call(functools.partial(pack_kernel, n_dp, n_mp), 'pack', [shape(rank, col...  2.38 us
  transfers between devices with their start and end apart: 23, of which 10 were waited for; matrix products, arithmetic and copies ran while one was open for 0% of the time, Pallas kernels for 22%

profile of v18, /device:TPU:0, one launch (start us, length us, event | category | flops | bytes accessed | tf_op | source)
XLA Modules:
  0.0 58.8 jit_solution(16909513274668136129)
XLA Ops:
  0.7 2.4 %pack.1 = (bf16[64,512]{1,0:T(8,128)(2,1)}, bf16[64,512]{1,0:T(8,128)(2,1)}, bf16[64,512]{1,0:T(8,128)(2,1)}, bf16[64,1024]{1,0:T(8,128)(2,1)}, bf16[64,1024]{1,...) custom-call(s32[1,2,4]{2,1,0:T(2,128)} %table.9, bf16[2,64,1024]{2,1,0:T(8,128)(2,1)} %bitcast.2, ...), custom_call_target="tpu_custom_call" | custom-call | flops 1 | bytes 1 | tf_op jit(solution)/shard_map/pack/pallas_call | solution.py:224
  3.1 3.0 %collective-permute-start = (bf16[512,512]{1,0:T(8,128)(2,1)}, bf16[512,512]{1,0:T(8,128)(2,1)S(1)}, u32[]{:S(2)}, u32[]{:S(2)}) collective-permute-start(bf16[512,512]{1,0:T(8,128)(2,1)} %get-tuple-element.38), channel_id=1, source_target_pairs={{0,2},{2,0},{1,3},{3,1},{4,6},{6,4},{5,7},{7,5},{8,10},{10,8},{9,1... | collective-permute-start | bytes 1572872 | tf_op jit(solution)/shard_map/ppermute | solution.py:35
  6.1 3.6 %collective-permute-start.2 = (bf16[64,512]{1,0:T(8,128)(2,1)}, bf16[64,512]{1,0:T(8,128)(2,1)S(1)}, u32[]{:S(2)}, u32[]{:S(2)}) collective-permute-start(bf16[64,512]{1,0:T(8,128)(2,1)} %get-tuple-element.41), channel_id=1, source_target_pairs={{0,12},{4,8},{8,4},{12,0},{1,13},{5,9},{9,5},{13,1},{2,14},{6,10},... | collective-permute-start | bytes 196616 | tf_op jit(solution)/shard_map/ppermute | solution.py:39
  9.7 0.8 %collective-permute-start.7 = (bf16[64,512]{1,0:T(8,128)(2,1)}, bf16[64,512]{1,0:T(8,128)(2,1)S(1)}, u32[]{:S(2)}, u32[]{:S(2)}) collective-permute-start(bf16[64,512]{1,0:T(8,128)(2,1)} %get-tuple-element.48), channel_id=1, source_target_pairs={{0,8},{4,12},{8,0},{12,4},{1,9},{5,13},{9,1},{13,5},{2,10},{6,14},... | collective-permute-start | bytes 196616 | tf_op jit(solution)/shard_map/ppermute | solution.py:39
  10.5 2.1 %collective-permute-done.2.refs_2_ = bf16[64,512]{1,0:T(8,128)(2,1)S(1)} collective-permute-done((bf16[64,512]{1,0:T(8,128)(2,1)}, bf16[64,512]{1,0:T(8,128)(2,1)S(1)}, u32[]{:S(2)}, u32[]{:S(2)}) %collective-permute-start.2) | collective-permute-done | bytes 65568 | tf_op jit(solution)/shard_map/ppermute | solution.py:39
  12.6 4.7 %collective-permute-start.4 = (bf16[64,1024]{1,0:T(8,128)(2,1)}, bf16[64,1024]{1,0:T(8,128)(2,1)S(1)}, u32[]{:S(2)}, u32[]{:S(2)}) collective-permute-start(bf16[64,1024]{1,0:T(8,128)(2,1)} %get-tuple-element.44), channel_id=1, source_target_pairs={{0,8},{4,12},{8,0},{12,4},{1,9},{5,13},{9,1},{13,5},{2,10},{6,14},... | collective-permute-start | bytes 393224 | tf_op jit(solution)/shard_map/ppermute | solution.py:39
  17.4 1.1 %h_part.1.refs_3_ = bf16[384,128]{1,0:T(8,128)(2,1)S(1)} custom-call(s32[12]{0:T(128)S(1)} %copy-done.6, s32[1,2,4]{2,1,0:T(2,128)S(1)} %copy-done.5, bf16[768,512]{1,0:T(8,128)(2,1)S(1)} %copy-done.2, bf16[64,512]{1,0:T(8,128)(2,1)S(1)} %collective-permute-done.6._.refs_0_, bf16[2,64,512]{2,1,0:T(8,128)(2,1)S(1)} %copy-done.4, ...), custom_call_target="tpu_custom_call" | custom-call | flops 1 | bytes 1 | tf_op jit(solution)/shard_map/h_part/pallas_call | solution.py:236
  18.5 0.6 %collective-permute-start.8 = (bf16[384,128]{1,0:T(8,128)(2,1)S(1)}, bf16[384,128]{1,0:T(8,128)(2,1)S(1)}, u32[]{:S(2)}, u32[]{:S(2)}) collective-permute-start(bf16[384,128]{1,0:T(8,128)(2,1)S(1)} %h_part.1.refs_3_), channel_id=1, source_target_pairs={{0,2},{2,0},{1,3},{3,1},{4,6},{6,4},{5,7},{7,5},{8,10},{10,8},{9,1... | collective-permute-start | bytes 294920 | tf_op jit(solution)/shard_map/ppermute | solution.py:35
  19.1 1.9 %collective-permute-start.1 = (bf16[768,512]{1,0:T(8,128)(2,1)S(1)}, bf16[768,512]{1,0:T(8,128)(2,1)S(1)}, u32[]{:S(2)}, u32[]{:S(2)}) collective-permute-start(bf16[768,512]{1,0:T(8,128)(2,1)S(1)} %copy-done.2), channel_id=1, source_target_pairs={{0,2},{2,0},{1,3},{3,1},{4,6},{6,4},{5,7},{7,5},{8,10},{10,8},{9,1... | collective-permute-start | bytes 2359304 | tf_op jit(solution)/shard_map/ppermute | solution.py:35
  20.9 3.3 %collective-permute-done.8.refs_4_ = bf16[384,128]{1,0:T(8,128)(2,1)S(1)} collective-permute-done((bf16[384,128]{1,0:T(8,128)(2,1)S(1)}, bf16[384,128]{1,0:T(8,128)(2,1)S(1)}, u32[]{:S(2)}, u32[]{:S(2)}) %collective-permute-start.8) | collective-permute-done | bytes 98336 | tf_op jit(solution)/shard_map/ppermute | solution.py:35
  24.3 2.1 %collective-permute-done.4.refs_1_.refs_7_ = bf16[64,1024]{1,0:T(8,128)(2,1)S(1)} collective-permute-done((bf16[64,1024]{1,0:T(8,128)(2,1)}, bf16[64,1024]{1,0:T(8,128)(2,1)S(1)}, u32[]{:S(2)}, u32[]{:S(2)}) %collective-permute-start.4) | collective-permute-done | bytes 131104 | tf_op jit(solution)/shard_map/ppermute | solution.py:39
  26.4 1.3 %down_grad.1 = (bf16[64,1024]{1,0:T(8,128)(2,1)S(1)}, bf16[64,1024]{1,0:T(8,128)(2,1)S(1)}, bf16[64,1024]{1,0:T(8,128)(2,1)S(1)}, bf16[64,1024]{1,0:T(8,128)(2,1)S(1)}, bf16[768,256]{1,0:T(8,128)(2,1)S(1)}) custom-call(s32[12]{0:T(128)S(1)} %copy-done.6, bf16[768,1024]{1,0:T(8,128)(2,1)S(1)} %copy-done.1, ...), custom_call_target="tpu_custom_call" | custom-call | flops 15000000512 | bytes 1 | tf_op jit(solution)/shard_map/down_grad/pallas_call | solution.py:244
  27.8 2.0 %collective-permute-start.10 = (bf16[64,1024]{1,0:T(8,128)(2,1)S(1)}, bf16[64,1024]{1,0:T(8,128)(2,1)S(1)}, u32[]{:S(2)}, u32[]{:S(2)}) collective-permute-start(bf16[64,1024]{1,0:T(8,128)(2,1)S(1)} %get-tuple-element.53), channel_id=1, source_target_pairs={{0,4},{4,0},{8,12},{12,8},{1,5},{5,1},{9,13},{13,9},{2,6},{6,2},{1... | collective-permute-start | bytes 393224 | tf_op jit(solution)/shard_map/ppermute | solution.py:39
  29.8 1.0 %collective-permute-start.11 = (bf16[64,1024]{1,0:T(8,128)(2,1)S(1)}, bf16[64,1024]{1,0:T(8,128)(2,1)S(1)}, u32[]{:S(2)}, u32[]{:S(2)}) collective-permute-start(bf16[64,1024]{1,0:T(8,128)(2,1)S(1)} %get-tuple-element.54), channel_id=1, source_target_pairs={{0,8},{4,12},{8,0},{12,4},{1,9},{5,13},{9,1},{13,5},{2,10},{6,14},... | collective-permute-start | bytes 393224 | tf_op jit(solution)/shard_map/ppermute | solution.py:39
  30.8 1.5 %collective-permute-start.12 = (bf16[64,1024]{1,0:T(8,128)(2,1)S(1)}, bf16[64,1024]{1,0:T(8,128)(2,1)S(1)}, u32[]{:S(2)}, u32[]{:S(2)}) collective-permute-start(bf16[64,1024]{1,0:T(8,128)(2,1)S(1)} %get-tuple-element.55), channel_id=1, source_target_pairs={{0,12},{4,8},{8,4},{12,0},{1,13},{5,9},{9,5},{13,1},{2,14},{6,10},... | collective-permute-start | bytes 393224 | tf_op jit(solution)/shard_map/ppermute | solution.py:39
  32.3 1.3 %u_part.1._.refs_5_ = bf16[384,128]{1,0:T(8,128)(2,1)S(1)} custom-call(s32[12]{0:T(128)S(1)} %copy-done.6, s32[1,2,4]{2,1,0:T(2,128)S(1)} %copy-done.5, bf16[768,1024]{1,0:T(8,128)(2,1)S(1)} %copy-done.1, bf16[512,512]{1,0:T(8,128)(2,1)S(1)} %collective-permute-done.9._.refs_1_, bf16[2,64,1024]{2,1,0:T(8,128)(2,1)S(1)} %bitcast.3, ...), custom_call_target="tpu_custom_call" | custom-call | flops 1 | bytes 1 | tf_op jit(solution)/shard_map/u_part/pallas_call | solution.py:236
  33.6 0.6 %collective-permute-start.13 = (bf16[384,128]{1,0:T(8,128)(2,1)S(1)}, bf16[384,128]{1,0:T(8,128)(2,1)S(1)}, u32[]{:S(2)}, u32[]{:S(2)}) collective-permute-start(bf16[384,128]{1,0:T(8,128)(2,1)S(1)} %u_part.1._.refs_5_), channel_id=1, source_target_pairs={{0,2},{2,0},{1,3},{3,1},{4,6},{6,4},{5,7},{7,5},{8,10},{10,8},{9,1... | collective-permute-start | bytes 294920 | tf_op jit(solution)/shard_map/ppermute | solution.py:35
  34.2 1.4 %y_send.1 = (bf16[768,512]{1,0:T(8,128)(2,1)S(1)}, bf16[1024,512]{1,0:T(8,128)(2,1)S(1)}) custom-call(bf16[384,128]{1,0:T(8,128)(2,1)S(1)} %u_part.1._.refs_5_, bf16[768,256]{1,0:T(8,128)(2,1)S(1)} %get-tuple-element.49.__.refs_4_, bf16[768,1024]{1,0:T(8,128)(2,1)S(1)} %copy-done.1, bf16[512,512]{1,0:T(8,128)(2,1)S(1)} %collective-permute-done.refs_0_, ...), custom_call_target="tpu_custom_call" | custom-call | flops 1 | bytes 1 | tf_op jit(solution)/shard_map/y_send/pallas_call | solution.py:260
  35.6 0.4 collective-permute-done.10.refs_1_
  36.1 1.1 %collective-permute-start.22 = (bf16[768,512]{1,0:T(8,128)(2,1)S(1)}, bf16[768,512]{1,0:T(8,128)(2,1)S(1)}, u32[]{:S(2)}, u32[]{:S(2)}) collective-permute-start(bf16[768,512]{1,0:T(8,128)(2,1)S(1)} %get-tuple-element.67), channel_id=1, source_target_pairs={{0,2},{2,0},{1,3},{3,1},{4,6},{6,4},{5,7},{7,5},{8,10},{10,8},{9,1... | collective-permute-start | bytes 2359304 | tf_op jit(solution)/shard_map/ppermute | solution.py:35
  37.2 2.5 %collective-permute-done.1.refs_2_.refs_4_ = bf16[768,512]{1,0:T(8,128)(2,1)S(1)} collective-permute-done((bf16[768,512]{1,0:T(8,128)(2,1)S(1)}, bf16[768,512]{1,0:T(8,128)(2,1)S(1)}, u32[]{:S(2)}, u32[]{:S(2)}) %collective-permute-start.1) | collective-permute-done | bytes 786464 | tf_op jit(solution)/shard_map/ppermute | solution.py:35
  39.7 4.1 %back.1 = (bf16[768,1024]{1,0:T(8,128)(2,1)}, s32[8,128]{1,0:T(8,128)S(1)}) custom-call(s32[1,2,4]{2,1,0:T(2,128)S(1)} %copy-done.5, bf16[2048,512]{1,0:T(8,128)(2,1)S(1)} %copy-done, bf16[768,512]{1,0:T(8,128)(2,1)S(1)} %copy-done.2, bf16[768,512]{1,0:T(8,128)(2,1)S(1)} %collective-permute-done.1.refs_2_.refs_4_, ...), custom_call_target="tpu_custom_call" | custom-call | flops 1 | bytes 1 | tf_op jit(solution)/shard_map/back/pallas_call | solution.py:269
  43.8 1.1 %up_grad.1 = (bf16[64,512]{1,0:T(8,128)(2,1)S(1)}, bf16[64,512]{1,0:T(8,128)(2,1)S(1)}, bf16[64,512]{1,0:T(8,128)(2,1)S(1)}, bf16[64,512]{1,0:T(8,128)(2,1)S(1)}, bf16[768,256]{1,0:T(8,128)(2,1)S(1)}) custom-call(s32[12]{0:T(128)S(1)} %copy-done.6, bf16[768,512]{1,0:T(8,128)(2,1)S(1)} %copy-done.2, s32[8,128]{1,0:T(8,128)S(1)} %get-tuple-element.52.refs_0_.picks, ...), custom_call_target="tpu_custom_call" | custom-call | flops 15000000512 | bytes 1 | tf_op jit(solution)/shard_map/up_grad/pallas_call | solution.py:244
  44.9 4.9 %collective-permute-start.17 = (bf16[64,512]{1,0:T(8,128)(2,1)S(1)}, bf16[64,512]{1,0:T(8,128)(2,1)S(1)}, u32[]{:S(2)}, u32[]{:S(2)}) collective-permute-start(bf16[64,512]{1,0:T(8,128)(2,1)S(1)} %get-tuple-element.60), channel_id=1, source_target_pairs={{0,12},{4,8},{8,4},{12,0},{1,13},{5,9},{9,5},{13,1},{2,14},{6,10},... | collective-permute-start | bytes 196616 | tf_op jit(solution)/shard_map/ppermute | solution.py:39
  49.9 0.6 %collective-permute-start.15 = (bf16[64,512]{1,0:T(8,128)(2,1)S(1)}, bf16[64,512]{1,0:T(8,128)(2,1)S(1)}, u32[]{:S(2)}, u32[]{:S(2)}) collective-permute-start(bf16[64,512]{1,0:T(8,128)(2,1)S(1)} %get-tuple-element.58), channel_id=1, source_target_pairs={{0,4},{4,0},{8,12},{12,8},{1,5},{5,1},{9,13},{13,9},{2,6},{6,2},{1... | collective-permute-start | bytes 196616 | tf_op jit(solution)/shard_map/ppermute | solution.py:39
  50.9 2.2 %y_own.1.refs_10_ = bf16[768,512]{1,0:T(8,128)(2,1)S(1)} custom-call(s32[1,2,4]{2,1,0:T(2,128)S(1)} %copy-done.5, bf16[2048,512]{1,0:T(8,128)(2,1)S(1)} %copy-done, bf16[768,1024]{1,0:T(8,128)(2,1)S(1)} %copy-done.1, bf16[768,256]{1,0:T(8,128)(2,1)S(1)} %get-tuple-element.61.wide, bf16[2,64,512]{2,1,0:T(8,128)(2,1)S(1)} %copy-done.4, ...), custom_call_target="tpu_custom_call" | custom-call | flops 15000000512 | bytes 1 | tf_op jit(solution)/shard_map/y_own/pallas_call | solution.py:279
  53.1 0.5 collective-permute-start.18
  53.6 1.4 %collective-permute-done.16.refs_4_ = bf16[64,512]{1,0:T(8,128)(2,1)S(1)} collective-permute-done((bf16[64,512]{1,0:T(8,128)(2,1)S(1)}, bf16[64,512]{1,0:T(8,128)(2,1)S(1)}, u32[]{:S(2)}, u32[]{:S(2)}) %collective-permute-start.16) | collective-permute-done | bytes 65568 | tf_op jit(solution)/shard_map/ppermute | solution.py:39
  55.0 0.5 collective-permute-start.20
  55.6 0.7 %collective-permute-done.21.refs_9_ = bf16[64,512]{1,0:T(8,128)(2,1)S(1)} collective-permute-done((bf16[64,512]{1,0:T(8,128)(2,1)S(1)}, bf16[64,512]{1,0:T(8,128)(2,1)S(1)}, u32[]{:S(2)}, u32[]{:S(2)}) %collective-permute-start.21) | collective-permute-done | bytes 65568 | tf_op jit(solution)/shard_map/ppermute | solution.py:35
  56.4 0.4 collective-permute-done.19.refs_7_
  57.0 1.9 %last.1 = (f32[2,64,1024]{2,1,0:T(8,128)}, f32[2,64,512]{2,1,0:T(8,128)}, bf16[768,512]{1,0:T(8,128)(2,1)}) custom-call(s32[8,128]{1,0:T(8,128)S(1)} %get-tuple-element.52.refs_0_.picks, bf16[2,64,1024]{2,1,0:T(8,128)(2,1)S(1)} %sites.1.refs_0_, bf16[2,64,1024]{2,1,0:T(8,128)(2,1)S(1)} %collective-permute-done.14.refs_1_, ...), custom_call_target="tpu_custom_call" | custom-call | flops 1 | bytes 1 | tf_op jit(solution)/shard_map/last/pallas_call | solution.py:296
  (38 shorter events, 1.0 us)
Async XLA Ops:
  0.6 16.7 %copy-start.4 = (bf16[2,64,512]{2,1,0:T(8,128)(2,1)S(1)}, bf16[2,64,512]{2,1,0:T(8,128)(2,1)}, u32[]{:S(2)}) copy-start(bf16[2,64,512]{2,1,0:T(8,128)(2,1)} %own_up.1) | copy-start | bytes 393220
  0.6 16.7 %copy-start.5 = (s32[1,2,4]{2,1,0:T(2,128)S(1)}, s32[1,2,4]{2,1,0:T(2,128)}, u32[]{:S(2)}) copy-start(s32[1,2,4]{2,1,0:T(2,128)} %table.9) | copy-start | bytes 100
  0.7 16.7 %copy-start.2 = (bf16[768,512]{1,0:T(8,128)(2,1)S(1)}, bf16[768,512]{1,0:T(8,128)(2,1)}, u32[]{:S(2)}) copy-start(bf16[768,512]{1,0:T(8,128)(2,1)} %act.7) | copy-start | bytes 2359300
  0.7 16.7 %copy-start.6 = (s32[12]{0:T(128)S(1)}, s32[12]{0:T(128)}, u32[]{:S(2)}) copy-start(s32[12]{0:T(128)} %owner.7) | copy-start | bytes 148
  0.7 25.7 %copy-start.1 = (bf16[768,1024]{1,0:T(8,128)(2,1)S(1)}, bf16[768,1024]{1,0:T(8,128)(2,1)}, u32[]{:S(2)}) copy-start(bf16[768,1024]{1,0:T(8,128)(2,1)} %x.3) | copy-start | bytes 4718596
  3.1 16.0 %collective-permute-start = (bf16[512,512]{1,0:T(8,128)(2,1)}, bf16[512,512]{1,0:T(8,128)(2,1)S(1)}, u32[]{:S(2)}, u32[]{:S(2)}) collective-permute-start(bf16[512,512]{1,0:T(8,128)(2,1)} %get-tuple-element.38), channel_id=1, source_target_pairs={{0,2},{2,0},{1,3},{3,1},{4,6},{6,4},{5,7},{7,5},{8,10},{10,8},{9,1... | collective-permute-start | bytes 1572872 | tf_op jit(solution)/shard_map/ppermute | solution.py:35
  6.1 6.5 %collective-permute-start.2 = (bf16[64,512]{1,0:T(8,128)(2,1)}, bf16[64,512]{1,0:T(8,128)(2,1)S(1)}, u32[]{:S(2)}, u32[]{:S(2)}) collective-permute-start(bf16[64,512]{1,0:T(8,128)(2,1)} %get-tuple-element.41), channel_id=1, source_target_pairs={{0,12},{4,8},{8,4},{12,0},{1,13},{5,9},{9,5},{13,1},{2,14},{6,10},... | collective-permute-start | bytes 196616 | tf_op jit(solution)/shard_map/ppermute | solution.py:39
  9.7 7.6 %collective-permute-start.6 = (bf16[64,512]{1,0:T(8,128)(2,1)}, bf16[64,512]{1,0:T(8,128)(2,1)S(1)}, u32[]{:S(2)}, u32[]{:S(2)}) collective-permute-start(bf16[64,512]{1,0:T(8,128)(2,1)} %get-tuple-element.47), channel_id=1, source_target_pairs={{0,4},{4,0},{8,12},{12,8},{1,5},{5,1},{9,13},{13,9},{2,6},{6,2},{1... | collective-permute-start | bytes 196616 | tf_op jit(solution)/shard_map/ppermute | solution.py:39
  9.7 7.6 %collective-permute-start.7 = (bf16[64,512]{1,0:T(8,128)(2,1)}, bf16[64,512]{1,0:T(8,128)(2,1)S(1)}, u32[]{:S(2)}, u32[]{:S(2)}) collective-permute-start(bf16[64,512]{1,0:T(8,128)(2,1)} %get-tuple-element.48), channel_id=1, source_target_pairs={{0,8},{4,12},{8,0},{12,4},{1,9},{5,13},{9,1},{13,5},{2,10},{6,14},... | collective-permute-start | bytes 196616 | tf_op jit(solution)/shard_map/ppermute | solution.py:39
  12.6 11.7 %collective-permute-start.3 = (bf16[64,1024]{1,0:T(8,128)(2,1)}, bf16[64,1024]{1,0:T(8,128)(2,1)S(1)}, u32[]{:S(2)}, u32[]{:S(2)}) collective-permute-start(bf16[64,1024]{1,0:T(8,128)(2,1)} %get-tuple-element.42), channel_id=1, source_target_pairs={{0,4},{4,0},{8,12},{12,8},{1,5},{5,1},{9,13},{13,9},{2,6},{6,2},{1... | collective-permute-start | bytes 393224 | tf_op jit(solution)/shard_map/ppermute | solution.py:39
  12.6 13.8 %collective-permute-start.4 = (bf16[64,1024]{1,0:T(8,128)(2,1)}, bf16[64,1024]{1,0:T(8,128)(2,1)S(1)}, u32[]{:S(2)}, u32[]{:S(2)}) collective-permute-start(bf16[64,1024]{1,0:T(8,128)(2,1)} %get-tuple-element.44), channel_id=1, source_target_pairs={{0,8},{4,12},{8,0},{12,4},{1,9},{5,13},{9,1},{13,5},{2,10},{6,14},... | collective-permute-start | bytes 393224 | tf_op jit(solution)/shard_map/ppermute | solution.py:39
  17.3 9.1 %collective-permute-start.5 = (bf16[64,1024]{1,0:T(8,128)(2,1)}, bf16[64,1024]{1,0:T(8,128)(2,1)S(1)}, u32[]{:S(2)}, u32[]{:S(2)}) collective-permute-start(bf16[64,1024]{1,0:T(8,128)(2,1)} %get-tuple-element.46), channel_id=1, source_target_pairs={{0,12},{4,8},{8,4},{12,0},{1,13},{5,9},{9,5},{13,1},{2,14},{6,10},... | collective-permute-start | bytes 393224 | tf_op jit(solution)/shard_map/ppermute | solution.py:39
  18.5 13.8 %copy-start.3 = (bf16[2,1024,64]{1,2,0:T(8,128)(2,1)S(1)}, bf16[2,1024,64]{1,2,0:T(8,128)(2,1)}, u32[]{:S(2)}) copy-start(bf16[2,1024,64]{1,2,0:T(8,128)(2,1)} %param.9) | copy-start | bytes 786436
  18.5 5.8 %collective-permute-start.8 = (bf16[384,128]{1,0:T(8,128)(2,1)S(1)}, bf16[384,128]{1,0:T(8,128)(2,1)S(1)}, u32[]{:S(2)}, u32[]{:S(2)}) collective-permute-start(bf16[384,128]{1,0:T(8,128)(2,1)S(1)} %h_part.1.refs_3_), channel_id=1, source_target_pairs={{0,2},{2,0},{1,3},{3,1},{4,6},{6,4},{5,7},{7,5},{8,10},{10,8},{9,1... | collective-permute-start | bytes 294920 | tf_op jit(solution)/shard_map/ppermute | solution.py:35
  19.1 20.6 %collective-permute-start.1 = (bf16[768,512]{1,0:T(8,128)(2,1)S(1)}, bf16[768,512]{1,0:T(8,128)(2,1)S(1)}, u32[]{:S(2)}, u32[]{:S(2)}) collective-permute-start(bf16[768,512]{1,0:T(8,128)(2,1)S(1)} %copy-done.2), channel_id=1, source_target_pairs={{0,2},{2,0},{1,3},{3,1},{4,6},{6,4},{5,7},{7,5},{8,10},{10,8},{9,1... | collective-permute-start | bytes 2359304 | tf_op jit(solution)/shard_map/ppermute | solution.py:35
  27.7 4.5 %collective-permute-start.9 = (bf16[512,512]{1,0:T(8,128)(2,1)S(1)}, bf16[512,512]{1,0:T(8,128)(2,1)S(1)}, u32[]{:S(2)}, u32[]{:S(2)}) collective-permute-start(bf16[512,512]{1,0:T(8,128)(2,1)S(1)} %collective-permute-done.refs_0_), channel_id=1, source_target_pairs={{0,1},{1,0},{2,3},{3,2},{4,5},{5,4},{6,7},{7,6},{8,9},{9,8},{10,11... | collective-permute-start | bytes 1572872 | tf_op jit(solution)/shard_map/ppermute | solution.py:35
  27.8 8.3 %collective-permute-start.10 = (bf16[64,1024]{1,0:T(8,128)(2,1)S(1)}, bf16[64,1024]{1,0:T(8,128)(2,1)S(1)}, u32[]{:S(2)}, u32[]{:S(2)}) collective-permute-start(bf16[64,1024]{1,0:T(8,128)(2,1)S(1)} %get-tuple-element.53), channel_id=1, source_target_pairs={{0,4},{4,0},{8,12},{12,8},{1,5},{5,1},{9,13},{13,9},{2,6},{6,2},{1... | collective-permute-start | bytes 393224 | tf_op jit(solution)/shard_map/ppermute | solution.py:39
  29.8 13.9 %collective-permute-start.11 = (bf16[64,1024]{1,0:T(8,128)(2,1)S(1)}, bf16[64,1024]{1,0:T(8,128)(2,1)S(1)}, u32[]{:S(2)}, u32[]{:S(2)}) collective-permute-start(bf16[64,1024]{1,0:T(8,128)(2,1)S(1)} %get-tuple-element.54), channel_id=1, source_target_pairs={{0,8},{4,12},{8,0},{12,4},{1,9},{5,13},{9,1},{13,5},{2,10},{6,14},... | collective-permute-start | bytes 393224 | tf_op jit(solution)/shard_map/ppermute | solution.py:39
  30.8 13.0 %collective-permute-start.12 = (bf16[64,1024]{1,0:T(8,128)(2,1)S(1)}, bf16[64,1024]{1,0:T(8,128)(2,1)S(1)}, u32[]{:S(2)}, u32[]{:S(2)}) collective-permute-start(bf16[64,1024]{1,0:T(8,128)(2,1)S(1)} %get-tuple-element.55), channel_id=1, source_target_pairs={{0,12},{4,8},{8,4},{12,0},{1,13},{5,9},{9,5},{13,1},{2,14},{6,10},... | collective-permute-start | bytes 393224 | tf_op jit(solution)/shard_map/ppermute | solution.py:39
  33.6 6.1 %copy-start = (bf16[2048,512]{1,0:T(8,128)(2,1)S(1)}, bf16[2048,512]{1,0:T(8,128)(2,1)}, u32[]{:S(2)}) copy-start(bf16[2048,512]{1,0:T(8,128)(2,1)} %w.1) | copy-start | bytes 6291460
  33.6 10.2 %collective-permute-start.13 = (bf16[384,128]{1,0:T(8,128)(2,1)S(1)}, bf16[384,128]{1,0:T(8,128)(2,1)S(1)}, u32[]{:S(2)}, u32[]{:S(2)}) collective-permute-start(bf16[384,128]{1,0:T(8,128)(2,1)S(1)} %u_part.1._.refs_5_), channel_id=1, source_target_pairs={{0,2},{2,0},{1,3},{3,1},{4,6},{6,4},{5,7},{7,5},{8,10},{10,8},{9,1... | collective-permute-start | bytes 294920 | tf_op jit(solution)/shard_map/ppermute | solution.py:35
  36.1 20.9 %collective-permute-start.22 = (bf16[768,512]{1,0:T(8,128)(2,1)S(1)}, bf16[768,512]{1,0:T(8,128)(2,1)S(1)}, u32[]{:S(2)}, u32[]{:S(2)}) collective-permute-start(bf16[768,512]{1,0:T(8,128)(2,1)S(1)} %get-tuple-element.67), channel_id=1, source_target_pairs={{0,2},{2,0},{1,3},{3,1},{4,6},{6,4},{5,7},{7,5},{8,10},{10,8},{9,1... | collective-permute-start | bytes 2359304 | tf_op jit(solution)/shard_map/ppermute | solution.py:35
  44.9 8.2 %collective-permute-start.17 = (bf16[64,512]{1,0:T(8,128)(2,1)S(1)}, bf16[64,512]{1,0:T(8,128)(2,1)S(1)}, u32[]{:S(2)}, u32[]{:S(2)}) collective-permute-start(bf16[64,512]{1,0:T(8,128)(2,1)S(1)} %get-tuple-element.60), channel_id=1, source_target_pairs={{0,12},{4,8},{8,4},{12,0},{1,13},{5,9},{9,5},{13,1},{2,14},{6,10},... | collective-permute-start | bytes 196616 | tf_op jit(solution)/shard_map/ppermute | solution.py:39
  49.9 5.2 %collective-permute-start.16 = (bf16[64,512]{1,0:T(8,128)(2,1)S(1)}, bf16[64,512]{1,0:T(8,128)(2,1)S(1)}, u32[]{:S(2)}, u32[]{:S(2)}) collective-permute-start(bf16[64,512]{1,0:T(8,128)(2,1)S(1)} %get-tuple-element.59), channel_id=1, source_target_pairs={{0,8},{4,12},{8,0},{12,4},{1,9},{5,13},{9,1},{13,5},{2,10},{6,14},... | collective-permute-start | bytes 196616 | tf_op jit(solution)/shard_map/ppermute | solution.py:39
  49.9 5.2 %collective-permute-start.15 = (bf16[64,512]{1,0:T(8,128)(2,1)S(1)}, bf16[64,512]{1,0:T(8,128)(2,1)S(1)}, u32[]{:S(2)}, u32[]{:S(2)}) collective-permute-start(bf16[64,512]{1,0:T(8,128)(2,1)S(1)} %get-tuple-element.58), channel_id=1, source_target_pairs={{0,4},{4,0},{8,12},{12,8},{1,5},{5,1},{9,13},{13,9},{2,6},{6,2},{1... | collective-permute-start | bytes 196616 | tf_op jit(solution)/shard_map/ppermute | solution.py:39
  50.8 6.0 %collective-permute-start.14 = (bf16[2,64,1024]{2,1,0:T(8,128)(2,1)S(1)}, bf16[2,64,1024]{2,1,0:T(8,128)(2,1)S(1)}, u32[]{:S(2)}, u32[]{:S(2)}) collective-permute-start(bf16[2,64,1024]{2,1,0:T(8,128)(2,1)S(1)} %sites.1.refs_0_), channel_id=1, source_target_pairs={{0,1},{1,0},{2,3},{3,2},{4,5},{5,4},{6,7},{7,6},{8,9},{9,8},{10,11... | collective-permute-start | bytes 786440 | tf_op jit(solution)/shard_map/ppermute | solution.py:35
  53.1 2.4 %collective-permute-start.18 = (bf16[64,512]{1,0:T(8,128)(2,1)S(1)}, bf16[64,512]{1,0:T(8,128)(2,1)S(1)}, u32[]{:S(2)}, u32[]{:S(2)}) collective-permute-start(bf16[64,512]{1,0:T(8,128)(2,1)S(1)} %get-tuple-element.62._.refs_2_), channel_id=1, source_target_pairs={{0,1},{1,0},{2,3},{3,2},{4,5},{5,4},{6,7},{7,6},{8,9},{9,8},{10,11... | collective-permute-start | bytes 196616 | tf_op jit(solution)/shard_map/ppermute | solution.py:35
  55.0 1.3 %collective-permute-start.21 = (bf16[64,512]{1,0:T(8,128)(2,1)S(1)}, bf16[64,512]{1,0:T(8,128)(2,1)S(1)}, u32[]{:S(2)}, u32[]{:S(2)}) collective-permute-start(bf16[64,512]{1,0:T(8,128)(2,1)S(1)} %collective-permute-done.17.refs_5_), channel_id=1, source_target_pairs={{0,1},{1,0},{2,3},{3,2},{4,5},{5,4},{6,7},{7,6},{8,9},{9,8},{10,11... | collective-permute-start | bytes 196616 | tf_op jit(solution)/shard_map/ppermute | solution.py:35
  55.0 1.4 %collective-permute-start.20 = (bf16[64,512]{1,0:T(8,128)(2,1)S(1)}, bf16[64,512]{1,0:T(8,128)(2,1)S(1)}, u32[]{:S(2)}, u32[]{:S(2)}) collective-permute-start(bf16[64,512]{1,0:T(8,128)(2,1)S(1)} %collective-permute-done.16.refs_4_), channel_id=1, source_target_pairs={{0,1},{1,0},{2,3},{3,2},{4,5},{5,4},{6,7},{7,6},{8,9},{9,8},{10,11... | collective-permute-start | bytes 196616 | tf_op jit(solution)/shard_map/ppermute | solution.py:35
  55.5 1.3 %collective-permute-start.19 = (bf16[64,512]{1,0:T(8,128)(2,1)S(1)}, bf16[64,512]{1,0:T(8,128)(2,1)S(1)}, u32[]{:S(2)}, u32[]{:S(2)}) collective-permute-start(bf16[64,512]{1,0:T(8,128)(2,1)S(1)} %collective-permute-done.15.refs_3_), channel_id=1, source_target_pairs={{0,1},{1,0},{2,3},{3,2},{4,5},{5,4},{6,7},{7,6},{8,9},{9,8},{10,11... | collective-permute-start | bytes 196616 | tf_op jit(solution)/shard_map/ppermute | solution.py:35

commit v19 on v17

--- a/solution.py
+++ b/solution.py
@@ -194,11 +194,12 @@
 def last_kernel(n_pair, n_ups, n_mp, picks, *refs):
     downs, ups, parts = refs[:n_pair], refs[n_pair:n_pair + n_ups], refs[n_pair + n_ups:n_pair + n_ups + n_mp]
     down, up, y = refs[-3:]
-    total = downs[0][0].astype(F32)
-    for part in downs[1:]:
-        total = total + part[0].astype(F32)
-    down[0] = SCALE * total
-    up[0] = SCALE * pick_sum(ups, picks, pl.program_id(0))
+    for site in range(up.shape[0]):
+        total = downs[0][site].astype(F32)
+        for part in downs[1:]:
+            total = total + part[site].astype(F32)
+        down[site] = SCALE * total
+        up[site] = SCALE * pick_sum(ups, picks, site)
     total = parts[0][...].astype(F32)
     for part in parts[1:]:
         total = total + part[...].astype(F32)
@@ -288,14 +289,10 @@
     )(picks, up_back[0], *down_back)
     both = [summed] + [shift(summed, "pair", q) for q in range(1, n_pair)]
     up_all = [shift(after(one, y_own), "pair", q) if q else one for q in range(n_pair) for one in up_back]
-    rows = tok // sites
-    of_site = lambda width: pl.BlockSpec((1, rank, width), lambda i: (i, 0, 0))
-    out_rows = pl.BlockSpec((rows, cols), lambda i: (i, 0))
     down_grad, up_grad, y = call(
         functools.partial(last_kernel, n_pair, n_pair * n_dp, n_mp), "last",
         [shape(sites, rank, feat, dtype=F32), shape(sites, rank, cols, dtype=F32), shape(tok, cols)],
-        [whole(*picks.shape)] + [of_site(feat)] * n_pair + [whole(rank, cols)] * (n_pair * n_dp) + [out_rows] * n_mp,
-        [of_site(feat), of_site(cols), out_rows], grid=(sites,),
+        [VMEM] * (1 + n_pair + n_pair * n_dp + n_mp), [VMEM] * 3,
     )(picks, *both, *up_all, y_own, *y_got)
     return y, back, down_grad.transpose(0, 2, 1), up_grad
 

time: 58.6 us -> 58.8 us (level)
  no operation moved by 1% of the time
where the time goes in v19:
time: 58.8 us; the launch traced here: 58.6 us
  starting transfers between devices  27.6 us (47%)
  Pallas kernels  16.9 us (29%)
  waiting for transfers between devices  13.2 us (22%)
  between operations  0.82 us (1%)
    ppermute x12, starting transfers between devices, swap(): lax.ppermute(value, axis, [(i, i ^ mask) for i in range(lax.axis_size(axi...  19.2 us
    ppermute x11, starting transfers between devices, shift(): lax.ppermute(value, axis, [(i, (i + by) % size) for i in range(size)])  8.45 us
    ppermute x11, waiting for transfers between devices, shift(): lax.ppermute(value, axis, [(i, (i + by) % size) for i in range(size)])  7.18 us
    ppermute x12, waiting for transfers between devices, swap(): lax.ppermute(value, axis, [(i, i ^ mask) for i in range(lax.axis_size(axi...  6.03 us
    pallas_call x1, Pallas kernels, shards(): call(functools.partial(back_kernel, n_dp, n_mp), 'back', [shape(tok, feat...  4.07 us
    pallas_call x2, Pallas kernels, gradient(): call(functools.partial(grad_kernel, n_dp, n_mp, len(behind)), name + '_gr...  2.45 us
    pallas_call x2, Pallas kernels, low_rank(): call(functools.partial(reduce_kernel, n_dp), name + '_part', shape(tok //...  2.42 us
    pallas_call x1, Pallas kernels, shards(): call(functools.partial(pack_kernel, n_dp, n_mp), 'pack', [shape(rank, col...  2.38 us
  transfers between devices with their start and end apart: 23, of which 10 were waited for; matrix products, arithmetic and copies ran while one was open for 0% of the time, Pallas kernels for 22%

profile of v19, /device:TPU:0, one launch (start us, length us, event | category | flops | bytes accessed | tf_op | source)
XLA Modules:
  0.0 58.6 jit_solution(2514879473724589752)
XLA Ops:
  0.7 2.4 %pack.1 = (bf16[64,512]{1,0:T(8,128)(2,1)}, bf16[64,512]{1,0:T(8,128)(2,1)}, bf16[64,512]{1,0:T(8,128)(2,1)}, bf16[64,1024]{1,0:T(8,128)(2,1)}, bf16[64,1024]{1,...) custom-call(s32[1,2,4]{2,1,0:T(2,128)} %table.9, bf16[2,64,1024]{2,1,0:T(8,128)(2,1)} %bitcast.2, ...), custom_call_target="tpu_custom_call" | custom-call | flops 1 | bytes 1 | tf_op jit(solution)/shard_map/pack/pallas_call | solution.py:225
  3.1 3.0 %collective-permute-start = (bf16[512,512]{1,0:T(8,128)(2,1)}, bf16[512,512]{1,0:T(8,128)(2,1)S(1)}, u32[]{:S(2)}, u32[]{:S(2)}) collective-permute-start(bf16[512,512]{1,0:T(8,128)(2,1)} %get-tuple-element.38), channel_id=1, source_target_pairs={{0,2},{2,0},{1,3},{3,1},{4,6},{6,4},{5,7},{7,5},{8,10},{10,8},{9,1... | collective-permute-start | bytes 1572872 | tf_op jit(solution)/shard_map/ppermute | solution.py:35
  6.1 3.6 %collective-permute-start.2 = (bf16[64,512]{1,0:T(8,128)(2,1)}, bf16[64,512]{1,0:T(8,128)(2,1)S(1)}, u32[]{:S(2)}, u32[]{:S(2)}) collective-permute-start(bf16[64,512]{1,0:T(8,128)(2,1)} %get-tuple-element.41), channel_id=1, source_target_pairs={{0,12},{4,8},{8,4},{12,0},{1,13},{5,9},{9,5},{13,1},{2,14},{6,10},... | collective-permute-start | bytes 196616 | tf_op jit(solution)/shard_map/ppermute | solution.py:39
  9.7 0.8 %collective-permute-start.7 = (bf16[64,512]{1,0:T(8,128)(2,1)}, bf16[64,512]{1,0:T(8,128)(2,1)S(1)}, u32[]{:S(2)}, u32[]{:S(2)}) collective-permute-start(bf16[64,512]{1,0:T(8,128)(2,1)} %get-tuple-element.48), channel_id=1, source_target_pairs={{0,8},{4,12},{8,0},{12,4},{1,9},{5,13},{9,1},{13,5},{2,10},{6,14},... | collective-permute-start | bytes 196616 | tf_op jit(solution)/shard_map/ppermute | solution.py:39
  10.5 2.1 %collective-permute-done.2.refs_2_ = bf16[64,512]{1,0:T(8,128)(2,1)S(1)} collective-permute-done((bf16[64,512]{1,0:T(8,128)(2,1)}, bf16[64,512]{1,0:T(8,128)(2,1)S(1)}, u32[]{:S(2)}, u32[]{:S(2)}) %collective-permute-start.2) | collective-permute-done | bytes 65568 | tf_op jit(solution)/shard_map/ppermute | solution.py:39
  12.6 4.7 %collective-permute-start.4 = (bf16[64,1024]{1,0:T(8,128)(2,1)}, bf16[64,1024]{1,0:T(8,128)(2,1)S(1)}, u32[]{:S(2)}, u32[]{:S(2)}) collective-permute-start(bf16[64,1024]{1,0:T(8,128)(2,1)} %get-tuple-element.44), channel_id=1, source_target_pairs={{0,8},{4,12},{8,0},{12,4},{1,9},{5,13},{9,1},{13,5},{2,10},{6,14},... | collective-permute-start | bytes 393224 | tf_op jit(solution)/shard_map/ppermute | solution.py:39
  17.4 1.1 %h_part.1.refs_3_ = bf16[384,128]{1,0:T(8,128)(2,1)S(1)} custom-call(s32[12]{0:T(128)S(1)} %copy-done.6, s32[1,2,4]{2,1,0:T(2,128)S(1)} %copy-done.5, bf16[768,512]{1,0:T(8,128)(2,1)S(1)} %copy-done.2, bf16[64,512]{1,0:T(8,128)(2,1)S(1)} %collective-permute-done.6._.refs_0_, bf16[2,64,512]{2,1,0:T(8,128)(2,1)S(1)} %copy-done.4, ...), custom_call_target="tpu_custom_call" | custom-call | flops 1 | bytes 1 | tf_op jit(solution)/shard_map/h_part/pallas_call | solution.py:237
  18.5 0.6 %collective-permute-start.8 = (bf16[384,128]{1,0:T(8,128)(2,1)S(1)}, bf16[384,128]{1,0:T(8,128)(2,1)S(1)}, u32[]{:S(2)}, u32[]{:S(2)}) collective-permute-start(bf16[384,128]{1,0:T(8,128)(2,1)S(1)} %h_part.1.refs_3_), channel_id=1, source_target_pairs={{0,2},{2,0},{1,3},{3,1},{4,6},{6,4},{5,7},{7,5},{8,10},{10,8},{9,1... | collective-permute-start | bytes 294920 | tf_op jit(solution)/shard_map/ppermute | solution.py:35
  19.1 1.9 %collective-permute-start.1 = (bf16[768,512]{1,0:T(8,128)(2,1)S(1)}, bf16[768,512]{1,0:T(8,128)(2,1)S(1)}, u32[]{:S(2)}, u32[]{:S(2)}) collective-permute-start(bf16[768,512]{1,0:T(8,128)(2,1)S(1)} %copy-done.2), channel_id=1, source_target_pairs={{0,2},{2,0},{1,3},{3,1},{4,6},{6,4},{5,7},{7,5},{8,10},{10,8},{9,1... | collective-permute-start | bytes 2359304 | tf_op jit(solution)/shard_map/ppermute | solution.py:35
  20.9 3.3 %collective-permute-done.8.refs_4_ = bf16[384,128]{1,0:T(8,128)(2,1)S(1)} collective-permute-done((bf16[384,128]{1,0:T(8,128)(2,1)S(1)}, bf16[384,128]{1,0:T(8,128)(2,1)S(1)}, u32[]{:S(2)}, u32[]{:S(2)}) %collective-permute-start.8) | collective-permute-done | bytes 98336 | tf_op jit(solution)/shard_map/ppermute | solution.py:35
  24.3 2.1 %collective-permute-done.4.refs_1_.refs_7_ = bf16[64,1024]{1,0:T(8,128)(2,1)S(1)} collective-permute-done((bf16[64,1024]{1,0:T(8,128)(2,1)}, bf16[64,1024]{1,0:T(8,128)(2,1)S(1)}, u32[]{:S(2)}, u32[]{:S(2)}) %collective-permute-start.4) | collective-permute-done | bytes 131104 | tf_op jit(solution)/shard_map/ppermute | solution.py:39
  26.4 1.3 %down_grad.1 = (bf16[64,1024]{1,0:T(8,128)(2,1)S(1)}, bf16[64,1024]{1,0:T(8,128)(2,1)S(1)}, bf16[64,1024]{1,0:T(8,128)(2,1)S(1)}, bf16[64,1024]{1,0:T(8,128)(2,1)S(1)}, bf16[768,256]{1,0:T(8,128)(2,1)S(1)}) custom-call(s32[12]{0:T(128)S(1)} %copy-done.6, bf16[768,1024]{1,0:T(8,128)(2,1)S(1)} %copy-done.1, ...), custom_call_target="tpu_custom_call" | custom-call | flops 15000000512 | bytes 1 | tf_op jit(solution)/shard_map/down_grad/pallas_call | solution.py:245
  27.8 2.0 %collective-permute-start.10 = (bf16[64,1024]{1,0:T(8,128)(2,1)S(1)}, bf16[64,1024]{1,0:T(8,128)(2,1)S(1)}, u32[]{:S(2)}, u32[]{:S(2)}) collective-permute-start(bf16[64,1024]{1,0:T(8,128)(2,1)S(1)} %get-tuple-element.53), channel_id=1, source_target_pairs={{0,4},{4,0},{8,12},{12,8},{1,5},{5,1},{9,13},{13,9},{2,6},{6,2},{1... | collective-permute-start | bytes 393224 | tf_op jit(solution)/shard_map/ppermute | solution.py:39
  29.8 1.0 %collective-permute-start.11 = (bf16[64,1024]{1,0:T(8,128)(2,1)S(1)}, bf16[64,1024]{1,0:T(8,128)(2,1)S(1)}, u32[]{:S(2)}, u32[]{:S(2)}) collective-permute-start(bf16[64,1024]{1,0:T(8,128)(2,1)S(1)} %get-tuple-element.54), channel_id=1, source_target_pairs={{0,8},{4,12},{8,0},{12,4},{1,9},{5,13},{9,1},{13,5},{2,10},{6,14},... | collective-permute-start | bytes 393224 | tf_op jit(solution)/shard_map/ppermute | solution.py:39
  30.8 1.5 %collective-permute-start.12 = (bf16[64,1024]{1,0:T(8,128)(2,1)S(1)}, bf16[64,1024]{1,0:T(8,128)(2,1)S(1)}, u32[]{:S(2)}, u32[]{:S(2)}) collective-permute-start(bf16[64,1024]{1,0:T(8,128)(2,1)S(1)} %get-tuple-element.55), channel_id=1, source_target_pairs={{0,12},{4,8},{8,4},{12,0},{1,13},{5,9},{9,5},{13,1},{2,14},{6,10},... | collective-permute-start | bytes 393224 | tf_op jit(solution)/shard_map/ppermute | solution.py:39
  32.3 1.3 %u_part.1._.refs_5_ = bf16[384,128]{1,0:T(8,128)(2,1)S(1)} custom-call(s32[12]{0:T(128)S(1)} %copy-done.6, s32[1,2,4]{2,1,0:T(2,128)S(1)} %copy-done.5, bf16[768,1024]{1,0:T(8,128)(2,1)S(1)} %copy-done.1, bf16[512,512]{1,0:T(8,128)(2,1)S(1)} %collective-permute-done.9._.refs_1_, bf16[2,64,1024]{2,1,0:T(8,128)(2,1)S(1)} %bitcast.3, ...), custom_call_target="tpu_custom_call" | custom-call | flops 1 | bytes 1 | tf_op jit(solution)/shard_map/u_part/pallas_call | solution.py:237
  33.6 0.6 %collective-permute-start.13 = (bf16[384,128]{1,0:T(8,128)(2,1)S(1)}, bf16[384,128]{1,0:T(8,128)(2,1)S(1)}, u32[]{:S(2)}, u32[]{:S(2)}) collective-permute-start(bf16[384,128]{1,0:T(8,128)(2,1)S(1)} %u_part.1._.refs_5_), channel_id=1, source_target_pairs={{0,2},{2,0},{1,3},{3,1},{4,6},{6,4},{5,7},{7,5},{8,10},{10,8},{9,1... | collective-permute-start | bytes 294920 | tf_op jit(solution)/shard_map/ppermute | solution.py:35
  34.2 1.4 %y_send.1 = (bf16[768,512]{1,0:T(8,128)(2,1)S(1)}, bf16[1024,512]{1,0:T(8,128)(2,1)S(1)}) custom-call(bf16[384,128]{1,0:T(8,128)(2,1)S(1)} %u_part.1._.refs_5_, bf16[768,256]{1,0:T(8,128)(2,1)S(1)} %get-tuple-element.49.__.refs_4_, bf16[768,1024]{1,0:T(8,128)(2,1)S(1)} %copy-done.1, bf16[512,512]{1,0:T(8,128)(2,1)S(1)} %collective-permute-done.refs_0_, ...), custom_call_target="tpu_custom_call" | custom-call | flops 1 | bytes 1 | tf_op jit(solution)/shard_map/y_send/pallas_call | solution.py:261
  35.6 0.4 collective-permute-done.10.refs_1_
  36.1 1.1 %collective-permute-start.22 = (bf16[768,512]{1,0:T(8,128)(2,1)S(1)}, bf16[768,512]{1,0:T(8,128)(2,1)S(1)}, u32[]{:S(2)}, u32[]{:S(2)}) collective-permute-start(bf16[768,512]{1,0:T(8,128)(2,1)S(1)} %get-tuple-element.67), channel_id=1, source_target_pairs={{0,2},{2,0},{1,3},{3,1},{4,6},{6,4},{5,7},{7,5},{8,10},{10,8},{9,1... | collective-permute-start | bytes 2359304 | tf_op jit(solution)/shard_map/ppermute | solution.py:35
  37.2 2.5 %collective-permute-done.1.refs_2_.refs_4_ = bf16[768,512]{1,0:T(8,128)(2,1)S(1)} collective-permute-done((bf16[768,512]{1,0:T(8,128)(2,1)S(1)}, bf16[768,512]{1,0:T(8,128)(2,1)S(1)}, u32[]{:S(2)}, u32[]{:S(2)}) %collective-permute-start.1) | collective-permute-done | bytes 786464 | tf_op jit(solution)/shard_map/ppermute | solution.py:35
  39.7 4.1 %back.1 = (bf16[768,1024]{1,0:T(8,128)(2,1)}, s32[8,128]{1,0:T(8,128)S(1)}) custom-call(s32[1,2,4]{2,1,0:T(2,128)S(1)} %copy-done.5, bf16[2048,512]{1,0:T(8,128)(2,1)S(1)} %copy-done, bf16[768,512]{1,0:T(8,128)(2,1)S(1)} %copy-done.2, bf16[768,512]{1,0:T(8,128)(2,1)S(1)} %collective-permute-done.1.refs_2_.refs_4_, ...), custom_call_target="tpu_custom_call" | custom-call | flops 1 | bytes 1 | tf_op jit(solution)/shard_map/back/pallas_call | solution.py:270
  43.8 1.1 %up_grad.1 = (bf16[64,512]{1,0:T(8,128)(2,1)S(1)}, bf16[64,512]{1,0:T(8,128)(2,1)S(1)}, bf16[64,512]{1,0:T(8,128)(2,1)S(1)}, bf16[64,512]{1,0:T(8,128)(2,1)S(1)}, bf16[768,256]{1,0:T(8,128)(2,1)S(1)}) custom-call(s32[12]{0:T(128)S(1)} %copy-done.6, bf16[768,512]{1,0:T(8,128)(2,1)S(1)} %copy-done.2, s32[8,128]{1,0:T(8,128)S(1)} %get-tuple-element.52.refs_0_.picks, ...), custom_call_target="tpu_custom_call" | custom-call | flops 15000000512 | bytes 1 | tf_op jit(solution)/shard_map/up_grad/pallas_call | solution.py:245
  44.9 4.9 %collective-permute-start.17 = (bf16[64,512]{1,0:T(8,128)(2,1)S(1)}, bf16[64,512]{1,0:T(8,128)(2,1)S(1)}, u32[]{:S(2)}, u32[]{:S(2)}) collective-permute-start(bf16[64,512]{1,0:T(8,128)(2,1)S(1)} %get-tuple-element.60), channel_id=1, source_target_pairs={{0,12},{4,8},{8,4},{12,0},{1,13},{5,9},{9,5},{13,1},{2,14},{6,10},... | collective-permute-start | bytes 196616 | tf_op jit(solution)/shard_map/ppermute | solution.py:39
  49.9 0.6 %collective-permute-start.15 = (bf16[64,512]{1,0:T(8,128)(2,1)S(1)}, bf16[64,512]{1,0:T(8,128)(2,1)S(1)}, u32[]{:S(2)}, u32[]{:S(2)}) collective-permute-start(bf16[64,512]{1,0:T(8,128)(2,1)S(1)} %get-tuple-element.58), channel_id=1, source_target_pairs={{0,4},{4,0},{8,12},{12,8},{1,5},{5,1},{9,13},{13,9},{2,6},{6,2},{1... | collective-permute-start | bytes 196616 | tf_op jit(solution)/shard_map/ppermute | solution.py:39
  50.9 2.2 %y_own.1.refs_10_ = bf16[768,512]{1,0:T(8,128)(2,1)S(1)} custom-call(s32[1,2,4]{2,1,0:T(2,128)S(1)} %copy-done.5, bf16[2048,512]{1,0:T(8,128)(2,1)S(1)} %copy-done, bf16[768,1024]{1,0:T(8,128)(2,1)S(1)} %copy-done.1, bf16[768,256]{1,0:T(8,128)(2,1)S(1)} %get-tuple-element.61.wide, bf16[2,64,512]{2,1,0:T(8,128)(2,1)S(1)} %copy-done.4, ...), custom_call_target="tpu_custom_call" | custom-call | flops 15000000512 | bytes 1 | tf_op jit(solution)/shard_map/y_own/pallas_call | solution.py:280
  53.1 0.5 collective-permute-start.18
  53.6 1.4 %collective-permute-done.16.refs_4_ = bf16[64,512]{1,0:T(8,128)(2,1)S(1)} collective-permute-done((bf16[64,512]{1,0:T(8,128)(2,1)S(1)}, bf16[64,512]{1,0:T(8,128)(2,1)S(1)}, u32[]{:S(2)}, u32[]{:S(2)}) %collective-permute-start.16) | collective-permute-done | bytes 65568 | tf_op jit(solution)/shard_map/ppermute | solution.py:39
  55.0 0.5 collective-permute-start.20
  55.6 0.7 %collective-permute-done.21.refs_9_ = bf16[64,512]{1,0:T(8,128)(2,1)S(1)} collective-permute-done((bf16[64,512]{1,0:T(8,128)(2,1)S(1)}, bf16[64,512]{1,0:T(8,128)(2,1)S(1)}, u32[]{:S(2)}, u32[]{:S(2)}) %collective-permute-start.21) | collective-permute-done | bytes 65568 | tf_op jit(solution)/shard_map/ppermute | solution.py:35
  56.4 0.4 collective-permute-done.19.refs_7_
  57.0 1.7 %last.1 = (f32[2,64,1024]{2,1,0:T(8,128)}, f32[2,64,512]{2,1,0:T(8,128)}, bf16[768,512]{1,0:T(8,128)(2,1)}) custom-call(s32[8,128]{1,0:T(8,128)S(1)} %get-tuple-element.52.refs_0_.picks, bf16[2,64,1024]{2,1,0:T(8,128)(2,1)S(1)} %sites.1.refs_0_, bf16[2,64,1024]{2,1,0:T(8,128)(2,1)S(1)} %collective-permute-done.14.refs_1_, ...), custom_call_target="tpu_custom_call" | custom-call | flops 1 | bytes 1 | tf_op jit(solution)/shard_map/last/pallas_call | solution.py:292
  (38 shorter events, 1.0 us)
Async XLA Ops:
  0.6 16.7 %copy-start.4 = (bf16[2,64,512]{2,1,0:T(8,128)(2,1)S(1)}, bf16[2,64,512]{2,1,0:T(8,128)(2,1)}, u32[]{:S(2)}) copy-start(bf16[2,64,512]{2,1,0:T(8,128)(2,1)} %own_up.1) | copy-start | bytes 393220
  0.6 16.7 %copy-start.5 = (s32[1,2,4]{2,1,0:T(2,128)S(1)}, s32[1,2,4]{2,1,0:T(2,128)}, u32[]{:S(2)}) copy-start(s32[1,2,4]{2,1,0:T(2,128)} %table.9) | copy-start | bytes 100
  0.7 16.7 %copy-start.2 = (bf16[768,512]{1,0:T(8,128)(2,1)S(1)}, bf16[768,512]{1,0:T(8,128)(2,1)}, u32[]{:S(2)}) copy-start(bf16[768,512]{1,0:T(8,128)(2,1)} %act.7) | copy-start | bytes 2359300
  0.7 16.7 %copy-start.6 = (s32[12]{0:T(128)S(1)}, s32[12]{0:T(128)}, u32[]{:S(2)}) copy-start(s32[12]{0:T(128)} %owner.7) | copy-start | bytes 148
  0.7 25.7 %copy-start.1 = (bf16[768,1024]{1,0:T(8,128)(2,1)S(1)}, bf16[768,1024]{1,0:T(8,128)(2,1)}, u32[]{:S(2)}) copy-start(bf16[768,1024]{1,0:T(8,128)(2,1)} %x.3) | copy-start | bytes 4718596
  3.1 16.0 %collective-permute-start = (bf16[512,512]{1,0:T(8,128)(2,1)}, bf16[512,512]{1,0:T(8,128)(2,1)S(1)}, u32[]{:S(2)}, u32[]{:S(2)}) collective-permute-start(bf16[512,512]{1,0:T(8,128)(2,1)} %get-tuple-element.38), channel_id=1, source_target_pairs={{0,2},{2,0},{1,3},{3,1},{4,6},{6,4},{5,7},{7,5},{8,10},{10,8},{9,1... | collective-permute-start | bytes 1572872 | tf_op jit(solution)/shard_map/ppermute | solution.py:35
  6.1 6.5 %collective-permute-start.2 = (bf16[64,512]{1,0:T(8,128)(2,1)}, bf16[64,512]{1,0:T(8,128)(2,1)S(1)}, u32[]{:S(2)}, u32[]{:S(2)}) collective-permute-start(bf16[64,512]{1,0:T(8,128)(2,1)} %get-tuple-element.41), channel_id=1, source_target_pairs={{0,12},{4,8},{8,4},{12,0},{1,13},{5,9},{9,5},{13,1},{2,14},{6,10},... | collective-permute-start | bytes 196616 | tf_op jit(solution)/shard_map/ppermute | solution.py:39
  9.7 7.6 %collective-permute-start.6 = (bf16[64,512]{1,0:T(8,128)(2,1)}, bf16[64,512]{1,0:T(8,128)(2,1)S(1)}, u32[]{:S(2)}, u32[]{:S(2)}) collective-permute-start(bf16[64,512]{1,0:T(8,128)(2,1)} %get-tuple-element.47), channel_id=1, source_target_pairs={{0,4},{4,0},{8,12},{12,8},{1,5},{5,1},{9,13},{13,9},{2,6},{6,2},{1... | collective-permute-start | bytes 196616 | tf_op jit(solution)/shard_map/ppermute | solution.py:39
  9.7 7.6 %collective-permute-start.7 = (bf16[64,512]{1,0:T(8,128)(2,1)}, bf16[64,512]{1,0:T(8,128)(2,1)S(1)}, u32[]{:S(2)}, u32[]{:S(2)}) collective-permute-start(bf16[64,512]{1,0:T(8,128)(2,1)} %get-tuple-element.48), channel_id=1, source_target_pairs={{0,8},{4,12},{8,0},{12,4},{1,9},{5,13},{9,1},{13,5},{2,10},{6,14},... | collective-permute-start | bytes 196616 | tf_op jit(solution)/shard_map/ppermute | solution.py:39
  12.6 11.7 %collective-permute-start.3 = (bf16[64,1024]{1,0:T(8,128)(2,1)}, bf16[64,1024]{1,0:T(8,128)(2,1)S(1)}, u32[]{:S(2)}, u32[]{:S(2)}) collective-permute-start(bf16[64,1024]{1,0:T(8,128)(2,1)} %get-tuple-element.42), channel_id=1, source_target_pairs={{0,4},{4,0},{8,12},{12,8},{1,5},{5,1},{9,13},{13,9},{2,6},{6,2},{1... | collective-permute-start | bytes 393224 | tf_op jit(solution)/shard_map/ppermute | solution.py:39
  12.6 13.8 %collective-permute-start.4 = (bf16[64,1024]{1,0:T(8,128)(2,1)}, bf16[64,1024]{1,0:T(8,128)(2,1)S(1)}, u32[]{:S(2)}, u32[]{:S(2)}) collective-permute-start(bf16[64,1024]{1,0:T(8,128)(2,1)} %get-tuple-element.44), channel_id=1, source_target_pairs={{0,8},{4,12},{8,0},{12,4},{1,9},{5,13},{9,1},{13,5},{2,10},{6,14},... | collective-permute-start | bytes 393224 | tf_op jit(solution)/shard_map/ppermute | solution.py:39
  17.3 9.1 %collective-permute-start.5 = (bf16[64,1024]{1,0:T(8,128)(2,1)}, bf16[64,1024]{1,0:T(8,128)(2,1)S(1)}, u32[]{:S(2)}, u32[]{:S(2)}) collective-permute-start(bf16[64,1024]{1,0:T(8,128)(2,1)} %get-tuple-element.46), channel_id=1, source_target_pairs={{0,12},{4,8},{8,4},{12,0},{1,13},{5,9},{9,5},{13,1},{2,14},{6,10},... | collective-permute-start | bytes 393224 | tf_op jit(solution)/shard_map/ppermute | solution.py:39
  18.5 13.8 %copy-start.3 = (bf16[2,1024,64]{1,2,0:T(8,128)(2,1)S(1)}, bf16[2,1024,64]{1,2,0:T(8,128)(2,1)}, u32[]{:S(2)}) copy-start(bf16[2,1024,64]{1,2,0:T(8,128)(2,1)} %param.9) | copy-start | bytes 786436
  18.5 5.8 %collective-permute-start.8 = (bf16[384,128]{1,0:T(8,128)(2,1)S(1)}, bf16[384,128]{1,0:T(8,128)(2,1)S(1)}, u32[]{:S(2)}, u32[]{:S(2)}) collective-permute-start(bf16[384,128]{1,0:T(8,128)(2,1)S(1)} %h_part.1.refs_3_), channel_id=1, source_target_pairs={{0,2},{2,0},{1,3},{3,1},{4,6},{6,4},{5,7},{7,5},{8,10},{10,8},{9,1... | collective-permute-start | bytes 294920 | tf_op jit(solution)/shard_map/ppermute | solution.py:35
  19.1 20.6 %collective-permute-start.1 = (bf16[768,512]{1,0:T(8,128)(2,1)S(1)}, bf16[768,512]{1,0:T(8,128)(2,1)S(1)}, u32[]{:S(2)}, u32[]{:S(2)}) collective-permute-start(bf16[768,512]{1,0:T(8,128)(2,1)S(1)} %copy-done.2), channel_id=1, source_target_pairs={{0,2},{2,0},{1,3},{3,1},{4,6},{6,4},{5,7},{7,5},{8,10},{10,8},{9,1... | collective-permute-start | bytes 2359304 | tf_op jit(solution)/shard_map/ppermute | solution.py:35
  27.7 4.5 %collective-permute-start.9 = (bf16[512,512]{1,0:T(8,128)(2,1)S(1)}, bf16[512,512]{1,0:T(8,128)(2,1)S(1)}, u32[]{:S(2)}, u32[]{:S(2)}) collective-permute-start(bf16[512,512]{1,0:T(8,128)(2,1)S(1)} %collective-permute-done.refs_0_), channel_id=1, source_target_pairs={{0,1},{1,0},{2,3},{3,2},{4,5},{5,4},{6,7},{7,6},{8,9},{9,8},{10,11... | collective-permute-start | bytes 1572872 | tf_op jit(solution)/shard_map/ppermute | solution.py:35
  27.8 8.3 %collective-permute-start.10 = (bf16[64,1024]{1,0:T(8,128)(2,1)S(1)}, bf16[64,1024]{1,0:T(8,128)(2,1)S(1)}, u32[]{:S(2)}, u32[]{:S(2)}) collective-permute-start(bf16[64,1024]{1,0:T(8,128)(2,1)S(1)} %get-tuple-element.53), channel_id=1, source_target_pairs={{0,4},{4,0},{8,12},{12,8},{1,5},{5,1},{9,13},{13,9},{2,6},{6,2},{1... | collective-permute-start | bytes 393224 | tf_op jit(solution)/shard_map/ppermute | solution.py:39
  29.8 13.9 %collective-permute-start.11 = (bf16[64,1024]{1,0:T(8,128)(2,1)S(1)}, bf16[64,1024]{1,0:T(8,128)(2,1)S(1)}, u32[]{:S(2)}, u32[]{:S(2)}) collective-permute-start(bf16[64,1024]{1,0:T(8,128)(2,1)S(1)} %get-tuple-element.54), channel_id=1, source_target_pairs={{0,8},{4,12},{8,0},{12,4},{1,9},{5,13},{9,1},{13,5},{2,10},{6,14},... | collective-permute-start | bytes 393224 | tf_op jit(solution)/shard_map/ppermute | solution.py:39
  30.8 13.0 %collective-permute-start.12 = (bf16[64,1024]{1,0:T(8,128)(2,1)S(1)}, bf16[64,1024]{1,0:T(8,128)(2,1)S(1)}, u32[]{:S(2)}, u32[]{:S(2)}) collective-permute-start(bf16[64,1024]{1,0:T(8,128)(2,1)S(1)} %get-tuple-element.55), channel_id=1, source_target_pairs={{0,12},{4,8},{8,4},{12,0},{1,13},{5,9},{9,5},{13,1},{2,14},{6,10},... | collective-permute-start | bytes 393224 | tf_op jit(solution)/shard_map/ppermute | solution.py:39
  33.6 6.1 %copy-start = (bf16[2048,512]{1,0:T(8,128)(2,1)S(1)}, bf16[2048,512]{1,0:T(8,128)(2,1)}, u32[]{:S(2)}) copy-start(bf16[2048,512]{1,0:T(8,128)(2,1)} %w.1) | copy-start | bytes 6291460
  33.6 10.2 %collective-permute-start.13 = (bf16[384,128]{1,0:T(8,128)(2,1)S(1)}, bf16[384,128]{1,0:T(8,128)(2,1)S(1)}, u32[]{:S(2)}, u32[]{:S(2)}) collective-permute-start(bf16[384,128]{1,0:T(8,128)(2,1)S(1)} %u_part.1._.refs_5_), channel_id=1, source_target_pairs={{0,2},{2,0},{1,3},{3,1},{4,6},{6,4},{5,7},{7,5},{8,10},{10,8},{9,1... | collective-permute-start | bytes 294920 | tf_op jit(solution)/shard_map/ppermute | solution.py:35
  36.1 20.9 %collective-permute-start.22 = (bf16[768,512]{1,0:T(8,128)(2,1)S(1)}, bf16[768,512]{1,0:T(8,128)(2,1)S(1)}, u32[]{:S(2)}, u32[]{:S(2)}) collective-permute-start(bf16[768,512]{1,0:T(8,128)(2,1)S(1)} %get-tuple-element.67), channel_id=1, source_target_pairs={{0,2},{2,0},{1,3},{3,1},{4,6},{6,4},{5,7},{7,5},{8,10},{10,8},{9,1... | collective-permute-start | bytes 2359304 | tf_op jit(solution)/shard_map/ppermute | solution.py:35
  44.9 8.2 %collective-permute-start.17 = (bf16[64,512]{1,0:T(8,128)(2,1)S(1)}, bf16[64,512]{1,0:T(8,128)(2,1)S(1)}, u32[]{:S(2)}, u32[]{:S(2)}) collective-permute-start(bf16[64,512]{1,0:T(8,128)(2,1)S(1)} %get-tuple-element.60), channel_id=1, source_target_pairs={{0,12},{4,8},{8,4},{12,0},{1,13},{5,9},{9,5},{13,1},{2,14},{6,10},... | collective-permute-start | bytes 196616 | tf_op jit(solution)/shard_map/ppermute | solution.py:39
  49.9 5.2 %collective-permute-start.16 = (bf16[64,512]{1,0:T(8,128)(2,1)S(1)}, bf16[64,512]{1,0:T(8,128)(2,1)S(1)}, u32[]{:S(2)}, u32[]{:S(2)}) collective-permute-start(bf16[64,512]{1,0:T(8,128)(2,1)S(1)} %get-tuple-element.59), channel_id=1, source_target_pairs={{0,8},{4,12},{8,0},{12,4},{1,9},{5,13},{9,1},{13,5},{2,10},{6,14},... | collective-permute-start | bytes 196616 | tf_op jit(solution)/shard_map/ppermute | solution.py:39
  49.9 5.2 %collective-permute-start.15 = (bf16[64,512]{1,0:T(8,128)(2,1)S(1)}, bf16[64,512]{1,0:T(8,128)(2,1)S(1)}, u32[]{:S(2)}, u32[]{:S(2)}) collective-permute-start(bf16[64,512]{1,0:T(8,128)(2,1)S(1)} %get-tuple-element.58), channel_id=1, source_target_pairs={{0,4},{4,0},{8,12},{12,8},{1,5},{5,1},{9,13},{13,9},{2,6},{6,2},{1... | collective-permute-start | bytes 196616 | tf_op jit(solution)/shard_map/ppermute | solution.py:39
  50.8 6.0 %collective-permute-start.14 = (bf16[2,64,1024]{2,1,0:T(8,128)(2,1)S(1)}, bf16[2,64,1024]{2,1,0:T(8,128)(2,1)S(1)}, u32[]{:S(2)}, u32[]{:S(2)}) collective-permute-start(bf16[2,64,1024]{2,1,0:T(8,128)(2,1)S(1)} %sites.1.refs_0_), channel_id=1, source_target_pairs={{0,1},{1,0},{2,3},{3,2},{4,5},{5,4},{6,7},{7,6},{8,9},{9,8},{10,11... | collective-permute-start | bytes 786440 | tf_op jit(solution)/shard_map/ppermute | solution.py:35
  53.1 2.4 %collective-permute-start.18 = (bf16[64,512]{1,0:T(8,128)(2,1)S(1)}, bf16[64,512]{1,0:T(8,128)(2,1)S(1)}, u32[]{:S(2)}, u32[]{:S(2)}) collective-permute-start(bf16[64,512]{1,0:T(8,128)(2,1)S(1)} %get-tuple-element.62._.refs_2_), channel_id=1, source_target_pairs={{0,1},{1,0},{2,3},{3,2},{4,5},{5,4},{6,7},{7,6},{8,9},{9,8},{10,11... | collective-permute-start | bytes 196616 | tf_op jit(solution)/shard_map/ppermute | solution.py:35
  55.0 1.3 %collective-permute-start.21 = (bf16[64,512]{1,0:T(8,128)(2,1)S(1)}, bf16[64,512]{1,0:T(8,128)(2,1)S(1)}, u32[]{:S(2)}, u32[]{:S(2)}) collective-permute-start(bf16[64,512]{1,0:T(8,128)(2,1)S(1)} %collective-permute-done.17.refs_5_), channel_id=1, source_target_pairs={{0,1},{1,0},{2,3},{3,2},{4,5},{5,4},{6,7},{7,6},{8,9},{9,8},{10,11... | collective-permute-start | bytes 196616 | tf_op jit(solution)/shard_map/ppermute | solution.py:35
  55.0 1.4 %collective-permute-start.20 = (bf16[64,512]{1,0:T(8,128)(2,1)S(1)}, bf16[64,512]{1,0:T(8,128)(2,1)S(1)}, u32[]{:S(2)}, u32[]{:S(2)}) collective-permute-start(bf16[64,512]{1,0:T(8,128)(2,1)S(1)} %collective-permute-done.16.refs_4_), channel_id=1, source_target_pairs={{0,1},{1,0},{2,3},{3,2},{4,5},{5,4},{6,7},{7,6},{8,9},{9,8},{10,11... | collective-permute-start | bytes 196616 | tf_op jit(solution)/shard_map/ppermute | solution.py:35
  55.5 1.3 %collective-permute-start.19 = (bf16[64,512]{1,0:T(8,128)(2,1)S(1)}, bf16[64,512]{1,0:T(8,128)(2,1)S(1)}, u32[]{:S(2)}, u32[]{:S(2)}) collective-permute-start(bf16[64,512]{1,0:T(8,128)(2,1)S(1)} %collective-permute-done.15.refs_3_), channel_id=1, source_target_pairs={{0,1},{1,0},{2,3},{3,2},{4,5},{5,4},{6,7},{7,6},{8,9},{9,8},{10,11... | collective-permute-start | bytes 196616 | tf_op jit(solution)/shard_map/ppermute | solution.py:35

commit v20 on v17

--- a/solution.py
+++ b/solution.py
@@ -8,7 +8,7 @@
 from jax.sharding import PartitionSpec as P
 
 SCALE = 2.0
-TILES = 3
+TILES = 2
 GRAD_COST = 15_000_000_000
 F32 = jnp.float32
 BF16 = jnp.bfloat16

time: 58.6 us -> 58.6 us (level)
  waiting for transfers between devices: 13.2 us -> 13.9 us
  transfers between devices with their start and end apart: 23 -> 23, of which waited for: 10 -> 10; matrix products, arithmetic and copies ran while one was open for 0% -> 0% of each run, Pallas kernels for 22% -> 21%
where the time goes in v20:
time: 58.6 us; the launch traced here: 58.5 us
  starting transfers between devices  27.5 us (47%)
  Pallas kernels  16.3 us (28%)
  waiting for transfers between devices  13.9 us (24%)
  between operations  0.82 us (1%)
    ppermute x12, starting transfers between devices, swap(): lax.ppermute(value, axis, [(i, i ^ mask) for i in range(lax.axis_size(axi...  19.2 us
    ppermute x11, starting transfers between devices, shift(): lax.ppermute(value, axis, [(i, (i + by) % size) for i in range(size)])  8.28 us
    ppermute x11, waiting for transfers between devices, shift(): lax.ppermute(value, axis, [(i, (i + by) % size) for i in range(size)])  7.47 us
    ppermute x12, waiting for transfers between devices, swap(): lax.ppermute(value, axis, [(i, i ^ mask) for i in range(lax.axis_size(axi...  6.4 us
    pallas_call x1, Pallas kernels, shards(): call(functools.partial(back_kernel, n_dp, n_mp), 'back', [shape(tok, feat...  3.95 us
    pallas_call x2, Pallas kernels, gradient(): call(functools.partial(grad_kernel, n_dp, n_mp, len(behind)), name + '_gr...  2.45 us
    pallas_call x2, Pallas kernels, low_rank(): call(functools.partial(reduce_kernel, n_dp), name + '_part', shape(tok //...  2.42 us
    pallas_call x1, Pallas kernels, shards(): call(functools.partial(pack_kernel, n_dp, n_mp), 'pack', [shape(rank, col...  2.38 us
  transfers between devices with their start and end apart: 23, of which 10 were waited for; matrix products, arithmetic and copies ran while one was open for 0% of the time, Pallas kernels for 21%

profile of v20, /device:TPU:0, one launch (start us, length us, event | category | flops | bytes accessed | tf_op | source)
XLA Modules:
  0.0 58.5 jit_solution(14985639445795325964)
XLA Ops:
  0.7 2.4 %pack.1 = (bf16[64,512]{1,0:T(8,128)(2,1)}, bf16[64,512]{1,0:T(8,128)(2,1)}, bf16[64,512]{1,0:T(8,128)(2,1)}, bf16[64,1024]{1,0:T(8,128)(2,1)}, bf16[64,1024]{1,...) custom-call(s32[1,2,4]{2,1,0:T(2,128)} %table.9, bf16[2,64,1024]{2,1,0:T(8,128)(2,1)} %bitcast.2, ...), custom_call_target="tpu_custom_call" | custom-call | flops 1 | bytes 1 | tf_op jit(solution)/shard_map/pack/pallas_call | solution.py:224
  3.1 3.0 %collective-permute-start = (bf16[512,512]{1,0:T(8,128)(2,1)}, bf16[512,512]{1,0:T(8,128)(2,1)S(1)}, u32[]{:S(2)}, u32[]{:S(2)}) collective-permute-start(bf16[512,512]{1,0:T(8,128)(2,1)} %get-tuple-element.38), channel_id=1, source_target_pairs={{0,2},{2,0},{1,3},{3,1},{4,6},{6,4},{5,7},{7,5},{8,10},{10,8},{9,1... | collective-permute-start | bytes 1572872 | tf_op jit(solution)/shard_map/ppermute | solution.py:35
  6.1 3.6 %collective-permute-start.2 = (bf16[64,512]{1,0:T(8,128)(2,1)}, bf16[64,512]{1,0:T(8,128)(2,1)S(1)}, u32[]{:S(2)}, u32[]{:S(2)}) collective-permute-start(bf16[64,512]{1,0:T(8,128)(2,1)} %get-tuple-element.41), channel_id=1, source_target_pairs={{0,12},{4,8},{8,4},{12,0},{1,13},{5,9},{9,5},{13,1},{2,14},{6,10},... | collective-permute-start | bytes 196616 | tf_op jit(solution)/shard_map/ppermute | solution.py:39
  9.7 0.8 %collective-permute-start.7 = (bf16[64,512]{1,0:T(8,128)(2,1)}, bf16[64,512]{1,0:T(8,128)(2,1)S(1)}, u32[]{:S(2)}, u32[]{:S(2)}) collective-permute-start(bf16[64,512]{1,0:T(8,128)(2,1)} %get-tuple-element.48), channel_id=1, source_target_pairs={{0,8},{4,12},{8,0},{12,4},{1,9},{5,13},{9,1},{13,5},{2,10},{6,14},... | collective-permute-start | bytes 196616 | tf_op jit(solution)/shard_map/ppermute | solution.py:39
  10.5 2.1 %collective-permute-done.2.refs_2_ = bf16[64,512]{1,0:T(8,128)(2,1)S(1)} collective-permute-done((bf16[64,512]{1,0:T(8,128)(2,1)}, bf16[64,512]{1,0:T(8,128)(2,1)S(1)}, u32[]{:S(2)}, u32[]{:S(2)}) %collective-permute-start.2) | collective-permute-done | bytes 65568 | tf_op jit(solution)/shard_map/ppermute | solution.py:39
  12.6 4.7 %collective-permute-start.4 = (bf16[64,1024]{1,0:T(8,128)(2,1)}, bf16[64,1024]{1,0:T(8,128)(2,1)S(1)}, u32[]{:S(2)}, u32[]{:S(2)}) collective-permute-start(bf16[64,1024]{1,0:T(8,128)(2,1)} %get-tuple-element.44), channel_id=1, source_target_pairs={{0,8},{4,12},{8,0},{12,4},{1,9},{5,13},{9,1},{13,5},{2,10},{6,14},... | collective-permute-start | bytes 393224 | tf_op jit(solution)/shard_map/ppermute | solution.py:39
  17.4 1.1 %h_part.1.refs_3_ = bf16[384,128]{1,0:T(8,128)(2,1)S(1)} custom-call(s32[12]{0:T(128)S(1)} %copy-done.6, s32[1,2,4]{2,1,0:T(2,128)S(1)} %copy-done.5, bf16[768,512]{1,0:T(8,128)(2,1)S(1)} %copy-done.2, bf16[64,512]{1,0:T(8,128)(2,1)S(1)} %collective-permute-done.6._.refs_0_, bf16[2,64,512]{2,1,0:T(8,128)(2,1)S(1)} %copy-done.4, ...), custom_call_target="tpu_custom_call" | custom-call | flops 1 | bytes 1 | tf_op jit(solution)/shard_map/h_part/pallas_call | solution.py:236
  18.5 0.6 %collective-permute-start.8 = (bf16[384,128]{1,0:T(8,128)(2,1)S(1)}, bf16[384,128]{1,0:T(8,128)(2,1)S(1)}, u32[]{:S(2)}, u32[]{:S(2)}) collective-permute-start(bf16[384,128]{1,0:T(8,128)(2,1)S(1)} %h_part.1.refs_3_), channel_id=1, source_target_pairs={{0,2},{2,0},{1,3},{3,1},{4,6},{6,4},{5,7},{7,5},{8,10},{10,8},{9,1... | collective-permute-start | bytes 294920 | tf_op jit(solution)/shard_map/ppermute | solution.py:35
  19.1 1.9 %collective-permute-start.1 = (bf16[768,512]{1,0:T(8,128)(2,1)S(1)}, bf16[768,512]{1,0:T(8,128)(2,1)S(1)}, u32[]{:S(2)}, u32[]{:S(2)}) collective-permute-start(bf16[768,512]{1,0:T(8,128)(2,1)S(1)} %copy-done.2), channel_id=1, source_target_pairs={{0,2},{2,0},{1,3},{3,1},{4,6},{6,4},{5,7},{7,5},{8,10},{10,8},{9,1... | collective-permute-start | bytes 2359304 | tf_op jit(solution)/shard_map/ppermute | solution.py:35
  20.9 3.3 %collective-permute-done.8.refs_4_ = bf16[384,128]{1,0:T(8,128)(2,1)S(1)} collective-permute-done((bf16[384,128]{1,0:T(8,128)(2,1)S(1)}, bf16[384,128]{1,0:T(8,128)(2,1)S(1)}, u32[]{:S(2)}, u32[]{:S(2)}) %collective-permute-start.8) | collective-permute-done | bytes 98336 | tf_op jit(solution)/shard_map/ppermute | solution.py:35
  24.3 2.1 %collective-permute-done.4.refs_1_.refs_7_ = bf16[64,1024]{1,0:T(8,128)(2,1)S(1)} collective-permute-done((bf16[64,1024]{1,0:T(8,128)(2,1)}, bf16[64,1024]{1,0:T(8,128)(2,1)S(1)}, u32[]{:S(2)}, u32[]{:S(2)}) %collective-permute-start.4) | collective-permute-done | bytes 131104 | tf_op jit(solution)/shard_map/ppermute | solution.py:39
  26.4 1.3 %down_grad.1 = (bf16[64,1024]{1,0:T(8,128)(2,1)S(1)}, bf16[64,1024]{1,0:T(8,128)(2,1)S(1)}, bf16[64,1024]{1,0:T(8,128)(2,1)S(1)}, bf16[64,1024]{1,0:T(8,128)(2,1)S(1)}, bf16[768,256]{1,0:T(8,128)(2,1)S(1)}) custom-call(s32[12]{0:T(128)S(1)} %copy-done.6, bf16[768,1024]{1,0:T(8,128)(2,1)S(1)} %copy-done.1, ...), custom_call_target="tpu_custom_call" | custom-call | flops 15000000512 | bytes 1 | tf_op jit(solution)/shard_map/down_grad/pallas_call | solution.py:244
  27.8 2.0 %collective-permute-start.10 = (bf16[64,1024]{1,0:T(8,128)(2,1)S(1)}, bf16[64,1024]{1,0:T(8,128)(2,1)S(1)}, u32[]{:S(2)}, u32[]{:S(2)}) collective-permute-start(bf16[64,1024]{1,0:T(8,128)(2,1)S(1)} %get-tuple-element.53), channel_id=1, source_target_pairs={{0,4},{4,0},{8,12},{12,8},{1,5},{5,1},{9,13},{13,9},{2,6},{6,2},{1... | collective-permute-start | bytes 393224 | tf_op jit(solution)/shard_map/ppermute | solution.py:39
  29.8 1.0 %collective-permute-start.11 = (bf16[64,1024]{1,0:T(8,128)(2,1)S(1)}, bf16[64,1024]{1,0:T(8,128)(2,1)S(1)}, u32[]{:S(2)}, u32[]{:S(2)}) collective-permute-start(bf16[64,1024]{1,0:T(8,128)(2,1)S(1)} %get-tuple-element.54), channel_id=1, source_target_pairs={{0,8},{4,12},{8,0},{12,4},{1,9},{5,13},{9,1},{13,5},{2,10},{6,14},... | collective-permute-start | bytes 393224 | tf_op jit(solution)/shard_map/ppermute | solution.py:39
  30.8 1.5 %collective-permute-start.12 = (bf16[64,1024]{1,0:T(8,128)(2,1)S(1)}, bf16[64,1024]{1,0:T(8,128)(2,1)S(1)}, u32[]{:S(2)}, u32[]{:S(2)}) collective-permute-start(bf16[64,1024]{1,0:T(8,128)(2,1)S(1)} %get-tuple-element.55), channel_id=1, source_target_pairs={{0,12},{4,8},{8,4},{12,0},{1,13},{5,9},{9,5},{13,1},{2,14},{6,10},... | collective-permute-start | bytes 393224 | tf_op jit(solution)/shard_map/ppermute | solution.py:39
  32.3 1.3 %u_part.1._.refs_5_ = bf16[384,128]{1,0:T(8,128)(2,1)S(1)} custom-call(s32[12]{0:T(128)S(1)} %copy-done.6, s32[1,2,4]{2,1,0:T(2,128)S(1)} %copy-done.5, bf16[768,1024]{1,0:T(8,128)(2,1)S(1)} %copy-done.1, bf16[512,512]{1,0:T(8,128)(2,1)S(1)} %collective-permute-done.9._.refs_1_, bf16[2,64,1024]{2,1,0:T(8,128)(2,1)S(1)} %bitcast.3, ...), custom_call_target="tpu_custom_call" | custom-call | flops 1 | bytes 1 | tf_op jit(solution)/shard_map/u_part/pallas_call | solution.py:236
  33.6 0.6 %collective-permute-start.13 = (bf16[384,128]{1,0:T(8,128)(2,1)S(1)}, bf16[384,128]{1,0:T(8,128)(2,1)S(1)}, u32[]{:S(2)}, u32[]{:S(2)}) collective-permute-start(bf16[384,128]{1,0:T(8,128)(2,1)S(1)} %u_part.1._.refs_5_), channel_id=1, source_target_pairs={{0,2},{2,0},{1,3},{3,1},{4,6},{6,4},{5,7},{7,5},{8,10},{10,8},{9,1... | collective-permute-start | bytes 294920 | tf_op jit(solution)/shard_map/ppermute | solution.py:35
  34.2 1.2 %y_send.1 = (bf16[768,512]{1,0:T(8,128)(2,1)S(1)}, bf16[1024,512]{1,0:T(8,128)(2,1)S(1)}) custom-call(bf16[384,128]{1,0:T(8,128)(2,1)S(1)} %u_part.1._.refs_5_, bf16[768,256]{1,0:T(8,128)(2,1)S(1)} %get-tuple-element.49.__.refs_4_, bf16[768,1024]{1,0:T(8,128)(2,1)S(1)} %copy-done.1, bf16[512,512]{1,0:T(8,128)(2,1)S(1)} %collective-permute-done.refs_0_, ...), custom_call_target="tpu_custom_call" | custom-call | flops 1 | bytes 1 | tf_op jit(solution)/shard_map/y_send/pallas_call | solution.py:260
  35.5 0.6 %collective-permute-done.10.refs_1_ = bf16[64,1024]{1,0:T(8,128)(2,1)S(1)} collective-permute-done((bf16[64,1024]{1,0:T(8,128)(2,1)S(1)}, bf16[64,1024]{1,0:T(8,128)(2,1)S(1)}, u32[]{:S(2)}, u32[]{:S(2)}) %collective-permute-start.10) | collective-permute-done | bytes 131104 | tf_op jit(solution)/shard_map/ppermute | solution.py:39
  36.1 1.0 %collective-permute-start.22 = (bf16[768,512]{1,0:T(8,128)(2,1)S(1)}, bf16[768,512]{1,0:T(8,128)(2,1)S(1)}, u32[]{:S(2)}, u32[]{:S(2)}) collective-permute-start(bf16[768,512]{1,0:T(8,128)(2,1)S(1)} %get-tuple-element.67), channel_id=1, source_target_pairs={{0,2},{2,0},{1,3},{3,1},{4,6},{6,4},{5,7},{7,5},{8,10},{10,8},{9,1... | collective-permute-start | bytes 2359304 | tf_op jit(solution)/shard_map/ppermute | solution.py:35
  37.0 2.7 %collective-permute-done.1.refs_2_.refs_4_ = bf16[768,512]{1,0:T(8,128)(2,1)S(1)} collective-permute-done((bf16[768,512]{1,0:T(8,128)(2,1)S(1)}, bf16[768,512]{1,0:T(8,128)(2,1)S(1)}, u32[]{:S(2)}, u32[]{:S(2)}) %collective-permute-start.1) | collective-permute-done | bytes 786464 | tf_op jit(solution)/shard_map/ppermute | solution.py:35
  39.7 4.0 %back.1 = (bf16[768,1024]{1,0:T(8,128)(2,1)}, s32[8,128]{1,0:T(8,128)S(1)}) custom-call(s32[1,2,4]{2,1,0:T(2,128)S(1)} %copy-done.5, bf16[2048,512]{1,0:T(8,128)(2,1)S(1)} %copy-done, bf16[768,512]{1,0:T(8,128)(2,1)S(1)} %copy-done.2, bf16[768,512]{1,0:T(8,128)(2,1)S(1)} %collective-permute-done.1.refs_2_.refs_4_, ...), custom_call_target="tpu_custom_call" | custom-call | flops 1 | bytes 1 | tf_op jit(solution)/shard_map/back/pallas_call | solution.py:269
  43.7 1.1 %up_grad.1 = (bf16[64,512]{1,0:T(8,128)(2,1)S(1)}, bf16[64,512]{1,0:T(8,128)(2,1)S(1)}, bf16[64,512]{1,0:T(8,128)(2,1)S(1)}, bf16[64,512]{1,0:T(8,128)(2,1)S(1)}, bf16[768,256]{1,0:T(8,128)(2,1)S(1)}) custom-call(s32[12]{0:T(128)S(1)} %copy-done.6, bf16[768,512]{1,0:T(8,128)(2,1)S(1)} %copy-done.2, s32[8,128]{1,0:T(8,128)S(1)} %get-tuple-element.52.refs_0_.picks, ...), custom_call_target="tpu_custom_call" | custom-call | flops 15000000512 | bytes 1 | tf_op jit(solution)/shard_map/up_grad/pallas_call | solution.py:244
  44.8 4.9 %collective-permute-start.17 = (bf16[64,512]{1,0:T(8,128)(2,1)S(1)}, bf16[64,512]{1,0:T(8,128)(2,1)S(1)}, u32[]{:S(2)}, u32[]{:S(2)}) collective-permute-start(bf16[64,512]{1,0:T(8,128)(2,1)S(1)} %get-tuple-element.60), channel_id=1, source_target_pairs={{0,12},{4,8},{8,4},{12,0},{1,13},{5,9},{9,5},{13,1},{2,14},{6,10},... | collective-permute-start | bytes 196616 | tf_op jit(solution)/shard_map/ppermute | solution.py:39
  49.7 0.6 %collective-permute-start.15 = (bf16[64,512]{1,0:T(8,128)(2,1)S(1)}, bf16[64,512]{1,0:T(8,128)(2,1)S(1)}, u32[]{:S(2)}, u32[]{:S(2)}) collective-permute-start(bf16[64,512]{1,0:T(8,128)(2,1)S(1)} %get-tuple-element.58), channel_id=1, source_target_pairs={{0,4},{4,0},{8,12},{12,8},{1,5},{5,1},{9,13},{13,9},{2,6},{6,2},{1... | collective-permute-start | bytes 196616 | tf_op jit(solution)/shard_map/ppermute | solution.py:39
  50.8 2.0 %y_own.1.refs_10_ = bf16[768,512]{1,0:T(8,128)(2,1)S(1)} custom-call(s32[1,2,4]{2,1,0:T(2,128)S(1)} %copy-done.5, bf16[2048,512]{1,0:T(8,128)(2,1)S(1)} %copy-done, bf16[768,1024]{1,0:T(8,128)(2,1)S(1)} %copy-done.1, bf16[768,256]{1,0:T(8,128)(2,1)S(1)} %get-tuple-element.61.wide, bf16[2,64,512]{2,1,0:T(8,128)(2,1)S(1)} %copy-done.4, ...), custom_call_target="tpu_custom_call" | custom-call | flops 15000000512 | bytes 1 | tf_op jit(solution)/shard_map/y_own/pallas_call | solution.py:279
  52.8 0.5 collective-permute-start.18
  53.3 1.6 %collective-permute-done.16.refs_4_ = bf16[64,512]{1,0:T(8,128)(2,1)S(1)} collective-permute-done((bf16[64,512]{1,0:T(8,128)(2,1)S(1)}, bf16[64,512]{1,0:T(8,128)(2,1)S(1)}, u32[]{:S(2)}, u32[]{:S(2)}) %collective-permute-start.16) | collective-permute-done | bytes 65568 | tf_op jit(solution)/shard_map/ppermute | solution.py:39
  54.9 0.5 collective-permute-start.20
  55.5 0.7 %collective-permute-done.21.refs_9_ = bf16[64,512]{1,0:T(8,128)(2,1)S(1)} collective-permute-done((bf16[64,512]{1,0:T(8,128)(2,1)S(1)}, bf16[64,512]{1,0:T(8,128)(2,1)S(1)}, u32[]{:S(2)}, u32[]{:S(2)}) %collective-permute-start.21) | collective-permute-done | bytes 65568 | tf_op jit(solution)/shard_map/ppermute | solution.py:35
  56.3 0.4 collective-permute-done.19.refs_7_
  57.0 1.5 %last.1 = (f32[2,64,1024]{2,1,0:T(8,128)}, f32[2,64,512]{2,1,0:T(8,128)}, bf16[768,512]{1,0:T(8,128)(2,1)}) custom-call(s32[8,128]{1,0:T(8,128)S(1)} %get-tuple-element.52.refs_0_.picks, bf16[2,64,1024]{2,1,0:T(8,128)(2,1)S(1)} %sites.1.refs_0_, bf16[2,64,1024]{2,1,0:T(8,128)(2,1)S(1)} %collective-permute-done.14.refs_1_, ...), custom_call_target="tpu_custom_call" | custom-call | flops 1 | bytes 1 | tf_op jit(solution)/shard_map/last/pallas_call | solution.py:294
  (38 shorter events, 1.1 us)
Async XLA Ops:
  0.6 16.7 %copy-start.4 = (bf16[2,64,512]{2,1,0:T(8,128)(2,1)S(1)}, bf16[2,64,512]{2,1,0:T(8,128)(2,1)}, u32[]{:S(2)}) copy-start(bf16[2,64,512]{2,1,0:T(8,128)(2,1)} %own_up.1) | copy-start | bytes 393220
  0.6 16.7 %copy-start.5 = (s32[1,2,4]{2,1,0:T(2,128)S(1)}, s32[1,2,4]{2,1,0:T(2,128)}, u32[]{:S(2)}) copy-start(s32[1,2,4]{2,1,0:T(2,128)} %table.9) | copy-start | bytes 100
  0.7 16.7 %copy-start.2 = (bf16[768,512]{1,0:T(8,128)(2,1)S(1)}, bf16[768,512]{1,0:T(8,128)(2,1)}, u32[]{:S(2)}) copy-start(bf16[768,512]{1,0:T(8,128)(2,1)} %act.7) | copy-start | bytes 2359300
  0.7 16.7 %copy-start.6 = (s32[12]{0:T(128)S(1)}, s32[12]{0:T(128)}, u32[]{:S(2)}) copy-start(s32[12]{0:T(128)} %owner.7) | copy-start | bytes 148
  0.7 25.7 %copy-start.1 = (bf16[768,1024]{1,0:T(8,128)(2,1)S(1)}, bf16[768,1024]{1,0:T(8,128)(2,1)}, u32[]{:S(2)}) copy-start(bf16[768,1024]{1,0:T(8,128)(2,1)} %x.3) | copy-start | bytes 4718596
  3.1 16.0 %collective-permute-start = (bf16[512,512]{1,0:T(8,128)(2,1)}, bf16[512,512]{1,0:T(8,128)(2,1)S(1)}, u32[]{:S(2)}, u32[]{:S(2)}) collective-permute-start(bf16[512,512]{1,0:T(8,128)(2,1)} %get-tuple-element.38), channel_id=1, source_target_pairs={{0,2},{2,0},{1,3},{3,1},{4,6},{6,4},{5,7},{7,5},{8,10},{10,8},{9,1... | collective-permute-start | bytes 1572872 | tf_op jit(solution)/shard_map/ppermute | solution.py:35
  6.1 6.5 %collective-permute-start.2 = (bf16[64,512]{1,0:T(8,128)(2,1)}, bf16[64,512]{1,0:T(8,128)(2,1)S(1)}, u32[]{:S(2)}, u32[]{:S(2)}) collective-permute-start(bf16[64,512]{1,0:T(8,128)(2,1)} %get-tuple-element.41), channel_id=1, source_target_pairs={{0,12},{4,8},{8,4},{12,0},{1,13},{5,9},{9,5},{13,1},{2,14},{6,10},... | collective-permute-start | bytes 196616 | tf_op jit(solution)/shard_map/ppermute | solution.py:39
  9.7 7.6 %collective-permute-start.6 = (bf16[64,512]{1,0:T(8,128)(2,1)}, bf16[64,512]{1,0:T(8,128)(2,1)S(1)}, u32[]{:S(2)}, u32[]{:S(2)}) collective-permute-start(bf16[64,512]{1,0:T(8,128)(2,1)} %get-tuple-element.47), channel_id=1, source_target_pairs={{0,4},{4,0},{8,12},{12,8},{1,5},{5,1},{9,13},{13,9},{2,6},{6,2},{1... | collective-permute-start | bytes 196616 | tf_op jit(solution)/shard_map/ppermute | solution.py:39
  9.7 7.6 %collective-permute-start.7 = (bf16[64,512]{1,0:T(8,128)(2,1)}, bf16[64,512]{1,0:T(8,128)(2,1)S(1)}, u32[]{:S(2)}, u32[]{:S(2)}) collective-permute-start(bf16[64,512]{1,0:T(8,128)(2,1)} %get-tuple-element.48), channel_id=1, source_target_pairs={{0,8},{4,12},{8,0},{12,4},{1,9},{5,13},{9,1},{13,5},{2,10},{6,14},... | collective-permute-start | bytes 196616 | tf_op jit(solution)/shard_map/ppermute | solution.py:39
  12.6 11.7 %collective-permute-start.3 = (bf16[64,1024]{1,0:T(8,128)(2,1)}, bf16[64,1024]{1,0:T(8,128)(2,1)S(1)}, u32[]{:S(2)}, u32[]{:S(2)}) collective-permute-start(bf16[64,1024]{1,0:T(8,128)(2,1)} %get-tuple-element.42), channel_id=1, source_target_pairs={{0,4},{4,0},{8,12},{12,8},{1,5},{5,1},{9,13},{13,9},{2,6},{6,2},{1... | collective-permute-start | bytes 393224 | tf_op jit(solution)/shard_map/ppermute | solution.py:39
  12.6 13.8 %collective-permute-start.4 = (bf16[64,1024]{1,0:T(8,128)(2,1)}, bf16[64,1024]{1,0:T(8,128)(2,1)S(1)}, u32[]{:S(2)}, u32[]{:S(2)}) collective-permute-start(bf16[64,1024]{1,0:T(8,128)(2,1)} %get-tuple-element.44), channel_id=1, source_target_pairs={{0,8},{4,12},{8,0},{12,4},{1,9},{5,13},{9,1},{13,5},{2,10},{6,14},... | collective-permute-start | bytes 393224 | tf_op jit(solution)/shard_map/ppermute | solution.py:39
  17.3 9.1 %collective-permute-start.5 = (bf16[64,1024]{1,0:T(8,128)(2,1)}, bf16[64,1024]{1,0:T(8,128)(2,1)S(1)}, u32[]{:S(2)}, u32[]{:S(2)}) collective-permute-start(bf16[64,1024]{1,0:T(8,128)(2,1)} %get-tuple-element.46), channel_id=1, source_target_pairs={{0,12},{4,8},{8,4},{12,0},{1,13},{5,9},{9,5},{13,1},{2,14},{6,10},... | collective-permute-start | bytes 393224 | tf_op jit(solution)/shard_map/ppermute | solution.py:39
  18.5 13.8 %copy-start.3 = (bf16[2,1024,64]{1,2,0:T(8,128)(2,1)S(1)}, bf16[2,1024,64]{1,2,0:T(8,128)(2,1)}, u32[]{:S(2)}) copy-start(bf16[2,1024,64]{1,2,0:T(8,128)(2,1)} %param.9) | copy-start | bytes 786436
  18.5 5.8 %collective-permute-start.8 = (bf16[384,128]{1,0:T(8,128)(2,1)S(1)}, bf16[384,128]{1,0:T(8,128)(2,1)S(1)}, u32[]{:S(2)}, u32[]{:S(2)}) collective-permute-start(bf16[384,128]{1,0:T(8,128)(2,1)S(1)} %h_part.1.refs_3_), channel_id=1, source_target_pairs={{0,2},{2,0},{1,3},{3,1},{4,6},{6,4},{5,7},{7,5},{8,10},{10,8},{9,1... | collective-permute-start | bytes 294920 | tf_op jit(solution)/shard_map/ppermute | solution.py:35
  19.1 20.6 %collective-permute-start.1 = (bf16[768,512]{1,0:T(8,128)(2,1)S(1)}, bf16[768,512]{1,0:T(8,128)(2,1)S(1)}, u32[]{:S(2)}, u32[]{:S(2)}) collective-permute-start(bf16[768,512]{1,0:T(8,128)(2,1)S(1)} %copy-done.2), channel_id=1, source_target_pairs={{0,2},{2,0},{1,3},{3,1},{4,6},{6,4},{5,7},{7,5},{8,10},{10,8},{9,1... | collective-permute-start | bytes 2359304 | tf_op jit(solution)/shard_map/ppermute | solution.py:35
  27.7 4.5 %collective-permute-start.9 = (bf16[512,512]{1,0:T(8,128)(2,1)S(1)}, bf16[512,512]{1,0:T(8,128)(2,1)S(1)}, u32[]{:S(2)}, u32[]{:S(2)}) collective-permute-start(bf16[512,512]{1,0:T(8,128)(2,1)S(1)} %collective-permute-done.refs_0_), channel_id=1, source_target_pairs={{0,1},{1,0},{2,3},{3,2},{4,5},{5,4},{6,7},{7,6},{8,9},{9,8},{10,11... | collective-permute-start | bytes 1572872 | tf_op jit(solution)/shard_map/ppermute | solution.py:35
  27.8 8.3 %collective-permute-start.10 = (bf16[64,1024]{1,0:T(8,128)(2,1)S(1)}, bf16[64,1024]{1,0:T(8,128)(2,1)S(1)}, u32[]{:S(2)}, u32[]{:S(2)}) collective-permute-start(bf16[64,1024]{1,0:T(8,128)(2,1)S(1)} %get-tuple-element.53), channel_id=1, source_target_pairs={{0,4},{4,0},{8,12},{12,8},{1,5},{5,1},{9,13},{13,9},{2,6},{6,2},{1... | collective-permute-start | bytes 393224 | tf_op jit(solution)/shard_map/ppermute | solution.py:39
  29.8 13.8 %collective-permute-start.11 = (bf16[64,1024]{1,0:T(8,128)(2,1)S(1)}, bf16[64,1024]{1,0:T(8,128)(2,1)S(1)}, u32[]{:S(2)}, u32[]{:S(2)}) collective-permute-start(bf16[64,1024]{1,0:T(8,128)(2,1)S(1)} %get-tuple-element.54), channel_id=1, source_target_pairs={{0,8},{4,12},{8,0},{12,4},{1,9},{5,13},{9,1},{13,5},{2,10},{6,14},... | collective-permute-start | bytes 393224 | tf_op jit(solution)/shard_map/ppermute | solution.py:39
  30.8 12.9 %collective-permute-start.12 = (bf16[64,1024]{1,0:T(8,128)(2,1)S(1)}, bf16[64,1024]{1,0:T(8,128)(2,1)S(1)}, u32[]{:S(2)}, u32[]{:S(2)}) collective-permute-start(bf16[64,1024]{1,0:T(8,128)(2,1)S(1)} %get-tuple-element.55), channel_id=1, source_target_pairs={{0,12},{4,8},{8,4},{12,0},{1,13},{5,9},{9,5},{13,1},{2,14},{6,10},... | collective-permute-start | bytes 393224 | tf_op jit(solution)/shard_map/ppermute | solution.py:39
  33.6 6.1 %copy-start = (bf16[2048,512]{1,0:T(8,128)(2,1)S(1)}, bf16[2048,512]{1,0:T(8,128)(2,1)}, u32[]{:S(2)}) copy-start(bf16[2048,512]{1,0:T(8,128)(2,1)} %w.1) | copy-start | bytes 6291460
  33.6 10.1 %collective-permute-start.13 = (bf16[384,128]{1,0:T(8,128)(2,1)S(1)}, bf16[384,128]{1,0:T(8,128)(2,1)S(1)}, u32[]{:S(2)}, u32[]{:S(2)}) collective-permute-start(bf16[384,128]{1,0:T(8,128)(2,1)S(1)} %u_part.1._.refs_5_), channel_id=1, source_target_pairs={{0,2},{2,0},{1,3},{3,1},{4,6},{6,4},{5,7},{7,5},{8,10},{10,8},{9,1... | collective-permute-start | bytes 294920 | tf_op jit(solution)/shard_map/ppermute | solution.py:35
  36.1 20.9 %collective-permute-start.22 = (bf16[768,512]{1,0:T(8,128)(2,1)S(1)}, bf16[768,512]{1,0:T(8,128)(2,1)S(1)}, u32[]{:S(2)}, u32[]{:S(2)}) collective-permute-start(bf16[768,512]{1,0:T(8,128)(2,1)S(1)} %get-tuple-element.67), channel_id=1, source_target_pairs={{0,2},{2,0},{1,3},{3,1},{4,6},{6,4},{5,7},{7,5},{8,10},{10,8},{9,1... | collective-permute-start | bytes 2359304 | tf_op jit(solution)/shard_map/ppermute | solution.py:35
  44.8 8.0 %collective-permute-start.17 = (bf16[64,512]{1,0:T(8,128)(2,1)S(1)}, bf16[64,512]{1,0:T(8,128)(2,1)S(1)}, u32[]{:S(2)}, u32[]{:S(2)}) collective-permute-start(bf16[64,512]{1,0:T(8,128)(2,1)S(1)} %get-tuple-element.60), channel_id=1, source_target_pairs={{0,12},{4,8},{8,4},{12,0},{1,13},{5,9},{9,5},{13,1},{2,14},{6,10},... | collective-permute-start | bytes 196616 | tf_op jit(solution)/shard_map/ppermute | solution.py:39
  49.7 5.2 %collective-permute-start.16 = (bf16[64,512]{1,0:T(8,128)(2,1)S(1)}, bf16[64,512]{1,0:T(8,128)(2,1)S(1)}, u32[]{:S(2)}, u32[]{:S(2)}) collective-permute-start(bf16[64,512]{1,0:T(8,128)(2,1)S(1)} %get-tuple-element.59), channel_id=1, source_target_pairs={{0,8},{4,12},{8,0},{12,4},{1,9},{5,13},{9,1},{13,5},{2,10},{6,14},... | collective-permute-start | bytes 196616 | tf_op jit(solution)/shard_map/ppermute | solution.py:39
  49.7 5.2 %collective-permute-start.15 = (bf16[64,512]{1,0:T(8,128)(2,1)S(1)}, bf16[64,512]{1,0:T(8,128)(2,1)S(1)}, u32[]{:S(2)}, u32[]{:S(2)}) collective-permute-start(bf16[64,512]{1,0:T(8,128)(2,1)S(1)} %get-tuple-element.58), channel_id=1, source_target_pairs={{0,4},{4,0},{8,12},{12,8},{1,5},{5,1},{9,13},{13,9},{2,6},{6,2},{1... | collective-permute-start | bytes 196616 | tf_op jit(solution)/shard_map/ppermute | solution.py:39
  50.7 6.0 %collective-permute-start.14 = (bf16[2,64,1024]{2,1,0:T(8,128)(2,1)S(1)}, bf16[2,64,1024]{2,1,0:T(8,128)(2,1)S(1)}, u32[]{:S(2)}, u32[]{:S(2)}) collective-permute-start(bf16[2,64,1024]{2,1,0:T(8,128)(2,1)S(1)} %sites.1.refs_0_), channel_id=1, source_target_pairs={{0,1},{1,0},{2,3},{3,2},{4,5},{5,4},{6,7},{7,6},{8,9},{9,8},{10,11... | collective-permute-start | bytes 786440 | tf_op jit(solution)/shard_map/ppermute | solution.py:35
  52.8 2.6 %collective-permute-start.18 = (bf16[64,512]{1,0:T(8,128)(2,1)S(1)}, bf16[64,512]{1,0:T(8,128)(2,1)S(1)}, u32[]{:S(2)}, u32[]{:S(2)}) collective-permute-start(bf16[64,512]{1,0:T(8,128)(2,1)S(1)} %get-tuple-element.62._.refs_2_), channel_id=1, source_target_pairs={{0,1},{1,0},{2,3},{3,2},{4,5},{5,4},{6,7},{7,6},{8,9},{9,8},{10,11... | collective-permute-start | bytes 196616 | tf_op jit(solution)/shard_map/ppermute | solution.py:35
  54.9 1.3 %collective-permute-start.21 = (bf16[64,512]{1,0:T(8,128)(2,1)S(1)}, bf16[64,512]{1,0:T(8,128)(2,1)S(1)}, u32[]{:S(2)}, u32[]{:S(2)}) collective-permute-start(bf16[64,512]{1,0:T(8,128)(2,1)S(1)} %collective-permute-done.17.refs_5_), channel_id=1, source_target_pairs={{0,1},{1,0},{2,3},{3,2},{4,5},{5,4},{6,7},{7,6},{8,9},{9,8},{10,11... | collective-permute-start | bytes 196616 | tf_op jit(solution)/shard_map/ppermute | solution.py:35
  54.9 1.4 %collective-permute-start.20 = (bf16[64,512]{1,0:T(8,128)(2,1)S(1)}, bf16[64,512]{1,0:T(8,128)(2,1)S(1)}, u32[]{:S(2)}, u32[]{:S(2)}) collective-permute-start(bf16[64,512]{1,0:T(8,128)(2,1)S(1)} %collective-permute-done.16.refs_4_), channel_id=1, source_target_pairs={{0,1},{1,0},{2,3},{3,2},{4,5},{5,4},{6,7},{7,6},{8,9},{9,8},{10,11... | collective-permute-start | bytes 196616 | tf_op jit(solution)/shard_map/ppermute | solution.py:35
  55.4 1.3 %collective-permute-start.19 = (bf16[64,512]{1,0:T(8,128)(2,1)S(1)}, bf16[64,512]{1,0:T(8,128)(2,1)S(1)}, u32[]{:S(2)}, u32[]{:S(2)}) collective-permute-start(bf16[64,512]{1,0:T(8,128)(2,1)S(1)} %collective-permute-done.15.refs_3_), channel_id=1, source_target_pairs={{0,1},{1,0},{2,3},{3,2},{4,5},{5,4},{6,7},{7,6},{8,9},{9,8},{10,11... | collective-permute-start | bytes 196616 | tf_op jit(solution)/shard_map/ppermute | solution.py:35
